TPU v7x, 32 devices: a whole 2x2x4 slice. The times are simulated.
32 devices in a mesh: domain: 8 (over y, x, core), band: 4 (over z).
Axes of the slice: x: 2, y: 2, z: 4, core: 2. Of those that a mesh axis runs over, the one named last changes fastest.
Arguments:
- wavefunctions: bfloat16 [3072, 16384], P('domain', 'band'), may hold values from -6 to 6
- rotation: bfloat16 [16384, 1024], P('band', 'domain'), may hold values from -0.0625 to 0.0625
- cell_matrices: bfloat16 [8, 512, 512], P('domain'), may hold values from -0.25 to 0.25
- cell_nodes: int32 [8, 512], P('domain'), may hold values from 0 to 511, as said below
- face_map: int32 [1024], P('domain'), may hold values from 0 to 383, as said below
Outputs:
- applied: float32 [3072, 1024], P('domain', 'band')
Inputs may be any that keep to these rules, and one draw needn't show every extreme that they name: `cell_nodes`: each cell names 512 distinct positions of its device's extended list (the 384 own nodes, then the 128 shared nodes of the next device); consecutive cells of a device share 128 positions; only the last cell of each device names shared nodes, and it names all of them. `face_map`: each device's block holds 128 distinct own nodes, all of them nodes of its first cell that no other of its cells names.
All inputs are finite; a program needn't handle non-finite values.
Results may differ from a plain program's by a relative error of at most 0.0029.
Values may be sent and summed in bfloat16 or wider, within the bound.
No kernel may reach another device: no remote copies, remote signals or barrier semaphores. Data moves between devices by JAX's collectives and lax.ppermute only.
A program may use at most 64 MiB of HBM per device.

v0:
```python
import jax
import jax.numpy as jnp
from jax import lax
from jax.sharding import PartitionSpec as P


def shifted(value, axis, steps):
    count = lax.axis_size(axis)
    leading, last = (max(0, -steps), min(count, count - steps))
    return lax.ppermute(value, axis, [(source, source + steps) for source in range(leading, last)])


def cell_terms(source, matrices, index_list, segment_count):
    gathered = jnp.take(source, index_list, axis=0)
    products = jnp.einsum("cij,cjo->cio", matrices, gathered, preferred_element_type=jnp.float32)
    width = products.shape[2]
    return jax.ops.segment_sum(
        products.reshape(-1, width), index_list.reshape(-1), num_segments=segment_count
    )


def local(wavefunctions, rotation, cell_matrices, cell_nodes, face_map):
    partial_sum = jnp.dot(
        wavefunctions,
        lax.all_gather(rotation, "domain", axis=1, tiled=True),
        preferred_element_type=jnp.float32,
    )
    rotated = lax.psum_scatter(partial_sum, "band", scatter_dimension=1, tiled=True).astype(
        jnp.bfloat16
    )
    node_count = rotated.shape[0]
    shared_count = face_map.shape[0]
    segment_count = node_count + shared_count
    face_rows = jnp.take(rotated, face_map, axis=0)
    incoming = shifted(face_rows, "domain", -1)
    extended = jnp.concatenate([rotated, incoming], axis=0)
    accumulated = cell_terms(extended, cell_matrices, cell_nodes, segment_count)
    outgoing = accumulated[node_count:]
    returned = shifted(outgoing, "domain", 1)
    return accumulated[:node_count].at[face_map].add(returned)


def solution(mesh):
    in_specs = (
        P("domain", "band"),
        P("band", "domain"),
        P("domain", None, None),
        P("domain", None),
        P("domain"),
    )
    out_specs = P("domain", "band")
    return jax.shard_map(local, mesh=mesh, in_specs=in_specs, out_specs=out_specs, check_vma=False)
```

profile of v0, /device:TPU:1, one launch (start us, length us, event | category | flops | bytes accessed | tf_op | source)
XLA Modules:
  0.0 144.4 jit_solution(1709257170258178313)
XLA Ops:
  6.5 0.0 copy-start
  6.5 0.0 all-gather.2.cloned.1.call-start
  6.5 0.7 all-gather.2.cloned.1.call-update
  7.3 0.0 copy-start.3
  7.3 0.0 copy-start.2
  7.3 0.0 reduce-scatter.2.cloned.1.call-start
  7.3 60.4 %all-gather.2.cloned.1.call-done = bf16[4096,1024]{1,0:T(8,128)(2,1)} async-done(((bf16[4096,128]{1,0:T(8,128)(2,1)}), bf16[4096,1024]{1,0:T(8,128)(2,1)}) %all-gather.2.cloned.1.call-update) | async-done | bytes 8388624 | tf_op jit(solution)/shard_map/all_gather | solution.py:25
  67.7 0.0 copy-done
  67.7 7.0 %fusion.7 = f32[384,1024]{1,0:T(8,128)} fusion(bf16[384,4096]{1,0:T(8,128)(2,1)S(1)} %copy-done, bf16[4096,1024]{1,0:T(8,128)(2,1)} %all-gather.2.cloned.1.call-done), kind=kOutput, calls=%fused_computation.21 | convolution fusion | flops 3221225472 | bytes 13107200 | tf_op jit(solution)/shard_map/dot_general | solution.py:23
  74.7 0.0 reduce-scatter.2.cloned.1.call-update
  74.8 0.0 copy-done.3
  74.8 0.0 copy-done.2
  74.9 34.8 %reduce-scatter.2.cloned.1.call-done = f32[384,256]{1,0:T(8,128)} async-done(((f32[384,1024]{1,0:T(8,128)}), f32[384,256]{1,0:T(8,128)}) %reduce-scatter.2.cloned.1.call-update) | async-done | bytes 393232 | tf_op jit(solution)/shard_map/reduce_scatter | solution.py:28
  109.6 1.0 convert_element_type.3
  110.6 0.0 copy-start.1
  110.7 0.8 gather_fusion
  111.5 0.1 broadcast_select_fusion
  111.6 2.7 %collective-permute-start = (bf16[128,256]{1,0:T(8,128)(2,1)S(1)}, bf16[128,256]{1,0:T(8,128)(2,1)S(1)}, u32[]{:S(2)}, u32[]{:S(2)}) collective-permute-start(bf16[128,256]{1,0:T(8,128)(2,1)S(1)} %broadcast_select_fusion), channel_id=1, source_target_pairs={{4,0},{8,4},{12,8},{16,12},{20,16},{24,20},{28,24},{5,1},{9,5},{13... | collective-permute-start | bytes 196616 | tf_op jit(solution)/shard_map/ppermute | solution.py:10
  114.4 0.0 copy-done.1
  114.4 3.0 %collective-permute-done = bf16[128,256]{1,0:T(8,128)(2,1)S(1)} collective-permute-done((bf16[128,256]{1,0:T(8,128)(2,1)S(1)}, bf16[128,256]{1,0:T(8,128)(2,1)S(1)}, u32[]{:S(2)}, u32[]{:S(2)}) %collective-permute-start) | collective-permute-done | bytes 65568 | tf_op jit(solution)/shard_map/ppermute | solution.py:10
  117.4 0.9 pad_maximum_fusion
  118.3 2.6 %gather_fusion.1 = bf16[512,256]{1,0:T(8,128)(2,1)} fusion(bf16[512,256]{1,0:T(8,128)(2,1)S(1)} %pad_maximum_fusion, s32[1024]{0:T(1024)S(1)} %pad_clamp_fusion), kind=kCustom, calls=%fused_computation.1 | custom fusion | bytes 526336 | tf_op jit(solution)/shard_map/jit(_take)/gather | solution.py:14
  120.9 2.4 %convolution_bitcast_fusion = f32[512,256]{0,1:T(8,128)} fusion(bf16[1,512,512]{2,1,0:T(8,128)(2,1)} %param.7, bf16[512,256]{1,0:T(8,128)(2,1)} %gather_fusion.1, pred[512]{0:T(512)(128)(4,1)S(1)} %get-tuple-element.5), kind=kOutput, calls=%fused_computation.4 | convolution fusion | flops 134348800 | bytes 1311232 | tf_op jit(solution)/shard_map/cij,cjo->cio/dot_general | solution.py:15
  123.3 2.0 %copy.7 = f32[512,256]{1,0:T(8,128)} copy(f32[512,256]{0,1:T(8,128)} %convolution_bitcast_fusion) | data formatting | bytes 1048576 | tf_op jit(solution)/shard_map/cij,cjo->cio/dot_general | solution.py:15
  125.3 4.6 %scatter_custom_fusion = f32[512,256]{1,0:T(8,128)} fusion(s32[512]{0:T(512)S(1)} %bitcast.18, f32[512,256]{1,0:T(8,128)} %copy.7, f32[]{:T(128)} %constant.18.clone.1), kind=kCustom, calls=%fused_computation.9 | custom fusion | flops 131072 | bytes 524800 | tf_op jit(solution)/shard_map/scatter-add | solution.py:17
  129.9 0.9 slice.13
  130.8 1.9 %collective-permute-start.1 = (f32[128,256]{1,0:T(8,128)S(1)}, f32[128,256]{1,0:T(8,128)S(1)}, u32[]{:S(2)}, u32[]{:S(2)}) collective-permute-start(f32[128,256]{1,0:T(8,128)S(1)} %slice.13), channel_id=1, source_target_pairs={{0,4},{4,8},{8,12},{12,16},{16,20},{20,24},{24,28},{1,5},{5,9},{9,... | collective-permute-start | bytes 393224 | tf_op jit(solution)/shard_map/ppermute | solution.py:10
  132.7 1.8 %slice.12 = f32[384,256]{1,0:T(8,128)} slice(f32[512,256]{1,0:T(8,128)} %scatter_custom_fusion), slice={[0:384], [0:256]} | slice | bytes 786432 | tf_op jit(solution)/shard_map/slice | solution.py:40
  134.5 0.2 collective-permute-done.1
  134.6 2.9 %scatter_fusion = f32[384,256]{1,0:T(8,128)} fusion(f32[384,256]{1,0:T(8,128)} %slice.12, s32[128]{0:T(128)S(1)} %compare_select_fusion.1, f32[128,256]{1,0:T(8,128)S(1)} %collective-permute-done.1), kind=kCustom, calls=%fused_computation.3 | custom fusion | flops 32768 | bytes 393728 | tf_op jit(solution)/shard_map/scatter-add | solution.py:40
  (5 shorter events, 0.0 us)
Async XLA Ops:
  6.5 61.2 %copy-start = (bf16[384,4096]{1,0:T(8,128)(2,1)S(1)}, bf16[384,4096]{1,0:T(8,128)(2,1)}, u32[]{:S(2)}) copy-start(bf16[384,4096]{1,0:T(8,128)(2,1)} %param.5) | copy-start | bytes 9437188
  6.5 61.2 %all-gather.2.cloned.1.call-start = ((), (), s32[]{:S(2)}) async-start(), calls=%async_computation.1 | async-start | bytes 9437184 | tf_op jit(solution)/shard_map/all_gather | solution.py:25
  7.3 67.5 %copy-start.3 = (s32[128]{0:T(128)S(1)}, s32[128]{0:T(128)}, u32[]{:S(2)}) copy-start(s32[128]{0:T(128)} %param.9) | copy-start | bytes 1540
  7.3 67.6 %copy-start.2 = (s32[1,512]{1,0:T(1,128)S(1)}, s32[1,512]{1,0:T(1,128)}, u32[]{:S(2)}) copy-start(s32[1,512]{1,0:T(1,128)} %param.8) | copy-start | bytes 6148
  7.3 102.3 %reduce-scatter.2.cloned.1.call-start = ((), (), s32[]{:S(2)}) async-start(), calls=%async_computation.2 | async-start | bytes 1966080 | tf_op jit(solution)/shard_map/reduce_scatter | solution.py:28
  110.6 3.7 %copy-start.1 = (bf16[384,256]{1,0:T(8,128)(2,1)}, bf16[384,256]{1,0:T(8,128)(2,1)S(1)}, u32[]{:S(2)}) copy-start(bf16[384,256]{1,0:T(8,128)(2,1)S(1)} %convert_element_type.3) | copy-start | bytes 589828
  111.6 5.8 %collective-permute-start = (bf16[128,256]{1,0:T(8,128)(2,1)S(1)}, bf16[128,256]{1,0:T(8,128)(2,1)S(1)}, u32[]{:S(2)}, u32[]{:S(2)}) collective-permute-start(bf16[128,256]{1,0:T(8,128)(2,1)S(1)} %broadcast_select_fusion), channel_id=1, source_target_pairs={{4,0},{8,4},{12,8},{16,12},{20,16},{24,20},{28,24},{5,1},{9,5},{13... | collective-permute-start | bytes 196616 | tf_op jit(solution)/shard_map/ppermute | solution.py:10
  130.8 3.9 %collective-permute-start.1 = (f32[128,256]{1,0:T(8,128)S(1)}, f32[128,256]{1,0:T(8,128)S(1)}, u32[]{:S(2)}, u32[]{:S(2)}) collective-permute-start(f32[128,256]{1,0:T(8,128)S(1)} %slice.13), channel_id=1, source_target_pairs={{0,4},{4,8},{8,12},{12,16},{16,20},{20,24},{24,28},{1,5},{5,9},{9,... | collective-permute-start | bytes 393224 | tf_op jit(solution)/shard_map/ppermute | solution.py:10
Sparse Core Ops, SparseCore 0:
  9.2 58.4 all-gather.1
  74.9 34.6 reduce-scatter.1
where the time goes:
time: 146 us; the launch traced here: 144 us
  waiting for transfers between devices  99 us (68%)
  between operations  13.5 us (9%)
  other arithmetic  9.55 us (7%)
  matrix products  9.4 us (6%)
  local copies, waits for them, and re-layouts  8.15 us (6%)
  starting transfers between devices  4.71 us (3%)
    all_gather x1, waiting for transfers between devices, local(): lax.all_gather(rotation, 'domain', axis=1, tiled=True)  60.4 us
    reduce_scatter x1, waiting for transfers between devices, local(): lax.psum_scatter(partial_sum, 'band', scatter_dimension=1, tiled=True)  34.8 us
    dot_general x1, matrix products, local(): jnp.dot(wavefunctions, lax.all_gather(rotation, 'domain', axis=1, tiled=T...  7.01 us
    ppermute x2, starting transfers between devices, shifted(): lax.ppermute(value, axis, [(source, source + steps) for source in range(l...  4.67 us
    scatter-add x1, other arithmetic, cell_terms(): jax.ops.segment_sum(products.reshape(-1, width), index_list.reshape(-1),...  4.56 us
    ppermute x2, waiting for transfers between devices, shifted(): lax.ppermute(value, axis, [(source, source + steps) for source in range(l...  3.14 us
  transfers between devices with their start and end apart: 4, of which 4 were waited for; matrix products, arithmetic and copies ran while one was open for 1% of the time, Pallas kernels for 0%

commit v1 on v0

v1 whole, which is shorter than its diff:
```python
import jax
import jax.numpy as jnp
from jax import lax
from jax.sharding import PartitionSpec as P

CORE, NEAR, FAR = 1, 2, 4


def dot(left, right):
    precision = lax.Precision.HIGHEST if left.dtype == jnp.float32 else None
    return jnp.dot(left, right, precision=precision, preferred_element_type=jnp.float32)


def split(value):
    high = lax.reduce_precision(value, 8, 7)
    return high.astype(jnp.bfloat16), (value - high).astype(jnp.bfloat16)


def shifted(value, axis, steps):
    count = lax.axis_size(axis)
    leading, last = (max(0, -steps), min(count, count - steps))
    return lax.ppermute(value, axis, [(source, source + steps) for source in range(leading, last)])


def exchanged(value, axis, mask):
    return lax.ppermute(value, axis, [(source, source ^ mask) for source in range(lax.axis_size(axis))])


def rotate_square(wavefunctions, rotation):
    domain, band = lax.axis_index("domain"), lax.axis_index("band")
    chip, core = domain // 2, domain % 2
    half = rotation.shape[0] // 2
    top, bottom = rotation[:half], rotation[half:]
    near_top = exchanged(top, "domain", NEAR)
    far_bottom = exchanged(bottom, "domain", FAR)
    near_bottom = exchanged(bottom, "domain", NEAR)
    far_top = exchanged(top, "domain", FAR)
    both_top = exchanged(near_top, "domain", FAR)
    both_bottom = exchanged(far_bottom, "domain", NEAR)
    pieces = [(top, bottom), (near_top, near_bottom), (far_top, far_bottom), (both_top, both_bottom)]
    w_top, w_bottom = wavefunctions[:, :half], wavefunctions[:, half:]
    blocks = []
    for upper, lower in pieces:
        other_upper = exchanged(upper, "domain", CORE)
        other_lower = exchanged(lower, "domain", CORE)
        mine = dot(w_top, upper) + dot(w_bottom, lower)
        other = dot(w_top, other_upper) + dot(w_bottom, other_lower)
        blocks.append(jnp.where(core == 0, jnp.concatenate([mine, other], 1), jnp.concatenate([other, mine], 1)))
    partial = jnp.stack(blocks)
    rounded = partial.astype(jnp.bfloat16)
    place = chip ^ band
    total = lax.dynamic_index_in_dim(partial, place, 0, keepdims=False)
    for mask in range(1, lax.axis_size("band")):
        sent = lax.dynamic_index_in_dim(rounded, place ^ mask, 0, keepdims=False)
        total = total + exchanged(sent, "band", mask).astype(jnp.float32)
    return total


def rotate_any(wavefunctions, rotation):
    columns = lax.all_gather(rotation, "domain", axis=1, tiled=True)
    return lax.psum_scatter(dot(wavefunctions, columns), "band", scatter_dimension=1, tiled=True)


def local(wavefunctions, rotation, cell_matrices, cell_nodes, face_map):
    cells = cell_nodes.shape[0]
    own = wavefunctions.shape[0]
    extent = own + face_map.shape[0]
    held = jnp.bfloat16 if cells == 1 else jnp.float32

    places = jax.nn.one_hot(cell_nodes, extent, dtype=held)
    assembled = jnp.zeros((extent, extent), jnp.float32)
    for cell in range(cells):
        rows = dot(places[cell].T, cell_matrices[cell].astype(held)).astype(held)
        assembled = assembled + dot(rows, places[cell])
    assembled = assembled.astype(held)
    pick = jax.nn.one_hot(face_map, own, dtype=held)
    corner = shifted(assembled[own:, own:], "domain", 1)
    returned = dot(dot(pick.T, corner).astype(held), pick).astype(held)

    chips = lax.axis_size("domain") // 2
    square = chips == FAR and chips == lax.axis_size("band")
    rotated = (rotate_square if square else rotate_any)(wavefunctions, rotation)

    high, low = split(rotated)
    if cells == 1:
        def apply(matrix):
            return dot(matrix, high) + dot(matrix, low)
    else:
        def apply(matrix):
            return dot(matrix, rotated)

    faces = dot(pick, high.astype(held)).astype(jnp.bfloat16)
    incoming = shifted(faces, "domain", -1)
    back = shifted(apply(assembled[own:, :own]), "domain", 1)
    result = apply(assembled[:own, :own]) + apply(returned) + dot(assembled[:own, own:], incoming.astype(held))
    if cells == 1:
        back_high, back_low = split(back)
        return result + dot(pick.T, back_high) + dot(pick.T, back_low)
    return result + dot(pick.T, back)


def solution(mesh):
    in_specs = (
        P("domain", "band"),
        P("band", "domain"),
        P("domain", None, None),
        P("domain", None),
        P("domain"),
    )
    out_specs = P("domain", "band")
    return jax.shard_map(local, mesh=mesh, in_specs=in_specs, out_specs=out_specs, check_vma=False)
```

time: 146 us -> 89.1 us (0.61)
  waiting for transfers between devices: 99 us -> 39.4 us
  starting transfers between devices: 4.71 us -> 22.6 us
  between operations: 13.5 us -> 0.47 us
  matrix products: 9.4 us -> 21.5 us
  other arithmetic: 9.55 us -> 1.61 us
  local copies, waits for them, and re-layouts: 8.15 us -> 3.18 us
    all_gather x1 -> x0, waiting for transfers between devices: 60.4 us -> none  [local(): lax.all_gather(rotation, 'domain', axis=1, tiled=True)]
    ppermute x0 -> x17, waiting for transfers between devices: none -> 36.7 us  [exchanged(): lax.ppermute(value, axis, [(source, source ^ mask) for source in range(la...]
    reduce_scatter x1 -> x0, waiting for transfers between devices: 34.8 us -> none  [local(): lax.psum_scatter(partial_sum, 'band', scatter_dimension=1, tiled=True)]
    ppermute x0 -> x17, starting transfers between devices: none -> 13.6 us  [exchanged(): lax.ppermute(value, axis, [(source, source ^ mask) for source in range(la...]
    dot_general x2 -> x28, matrix products: 9.4 us -> 21.5 us  [dot(): jnp.dot(left, right, precision=precision, preferred_element_type=jnp.floa...]
    scatter-add x2 -> x0, other arithmetic: 7.45 us -> none  [the longest x1 4.56 us: cell_terms(): jax.ops.segment_sum(products.reshape(-1, width), index_list.reshape(-1),...]
    ppermute x2 -> x3, starting transfers between devices: 4.67 us -> 8.97 us  [shifted(): lax.ppermute(value, axis, [(source, source + steps) for source in range(l...]
    gather x2 -> x0, local copies, waits for them, and re-layouts: 3.43 us -> none  [the longest x1 2.58 us: cell_terms(): gathered = jnp.take(source, index_list, axis=0)]
  transfers between devices with their start and end apart: 4 -> 20, of which waited for: 4 -> 6; matrix products, arithmetic and copies ran while one was open for 1% -> 23% of each run, Pallas kernels for 0% -> 0%
where the time goes in v1:
time: 89.1 us; the launch traced here: 88.7 us
  waiting for transfers between devices  39.4 us (44%)
  starting transfers between devices  22.6 us (25%)
  matrix products  21.5 us (24%)
  local copies, waits for them, and re-layouts  3.18 us (4%)
  other arithmetic  1.61 us (2%)
    ppermute x17, waiting for transfers between devices, exchanged(): lax.ppermute(value, axis, [(source, source ^ mask) for source in range(la...  36.7 us
    dot_general x28, matrix products, dot(): jnp.dot(left, right, precision=precision, preferred_element_type=jnp.floa...  21.5 us
    ppermute x17, starting transfers between devices, exchanged(): lax.ppermute(value, axis, [(source, source ^ mask) for source in range(la...  13.6 us
    ppermute x3, starting transfers between devices, shifted(): lax.ppermute(value, axis, [(source, source + steps) for source in range(l...  8.97 us
    ppermute x3, waiting for transfers between devices, shifted(): lax.ppermute(value, axis, [(source, source + steps) for source in range(l...  2.68 us
    slice x1, local copies, waits for them, and re-layouts, rotate_square(): top, bottom = (rotation[:half], rotation[half:])  2.41 us
  transfers between devices with their start and end apart: 20, of which 6 were waited for; matrix products, arithmetic and copies ran while one was open for 23% of the time, Pallas kernels for 0%

profile of v1, /device:TPU:1, one launch (start us, length us, event | category | flops | bytes accessed | tf_op | source)
XLA Modules:
  0.0 88.7 jit_solution(2802298123163350346)
XLA Ops:
  0.0 2.4 %fusion.65 = (bf16[2048,128]{1,0:T(8,128)(2,1)}, bf16[2048,128]{1,0:T(8,128)(2,1)}) fusion(bf16[4096,128]{1,0:T(8,128)(2,1)} %param.6), kind=kLoop, calls=%fused_computation.92 | loop fusion | bytes 2097152 | tf_op jit(solution)/shard_map/slice | solution.py:33
  2.4 2.0 %collective-permute-start.2 = (bf16[2048,128]{1,0:T(8,128)(2,1)}, bf16[2048,128]{1,0:T(8,128)(2,1)S(1)}, u32[]{:S(2)}, u32[]{:S(2)}) collective-permute-start(bf16[2048,128]{1,0:T(8,128)(2,1)} %get-tuple-element.7), channel_id=1, source_target_pairs={{0,8},{4,12},{8,0},{12,4},{16,24},{20,28},{24,16},{28,20},{1,9},{5... | collective-permute-start | bytes 1572872 | tf_op jit(solution)/shard_map/ppermute | solution.py:26
  4.5 1.2 %collective-permute-start.6 = (bf16[2048,128]{1,0:T(8,128)(2,1)}, bf16[2048,128]{1,0:T(8,128)(2,1)}, u32[]{:S(2)}, u32[]{:S(2)}) collective-permute-start(bf16[2048,128]{1,0:T(8,128)(2,1)} %get-tuple-element.7), channel_id=1, source_target_pairs={{0,16},{4,20},{8,24},{12,28},{16,0},{20,4},{24,8},{28,12},{1,17},{... | collective-permute-start | bytes 1572872 | tf_op jit(solution)/shard_map/ppermute | solution.py:26
  5.7 0.2 collective-permute-start.7
  5.9 1.5 %collective-permute-start.1 = (bf16[2048,128]{1,0:T(8,128)(2,1)}, bf16[2048,128]{1,0:T(8,128)(2,1)}, u32[]{:S(2)}, u32[]{:S(2)}) collective-permute-start(bf16[2048,128]{1,0:T(8,128)(2,1)} %get-tuple-element.8), channel_id=1, source_target_pairs={{0,4},{4,0},{8,12},{12,8},{16,20},{20,16},{24,28},{28,24},{1,5},{5... | collective-permute-start | bytes 1572872 | tf_op jit(solution)/shard_map/ppermute | solution.py:26
  7.4 0.0 collective-permute-start
  7.4 2.7 %fusion.44 = f32[384,128]{0,1:T(8,128)} fusion(bf16[384,4096]{1,0:T(8,128)(2,1)} %param.5, bf16[4096,128]{1,0:T(8,128)(2,1)S(1)} %copy-done.2), kind=kOutput, calls=%fused_computation.67 | convolution fusion | flops 201326592 | bytes 2293760 | tf_op jit(solution)/shard_map/dot_general | solution.py:11
  10.1 1.0 %convolution_convert_fusion = bf16[512,512]{1,0:T(8,128)(2,1)S(1)} fusion(bf16[1,512,512]{2,1,0:T(8,128)(2,1)S(1)} %copy-done, s32[512]{0:T(512)S(1)} %bitcast.66), kind=kOutput, calls=%fused_computation.1 | convolution fusion | flops 537919488 | bytes 1050624 | tf_op jit(solution)/shard_map/dot_general | solution.py:11
  11.2 0.0 copy-start.1
  11.2 2.1 %fusion.10 = f32[1,384,128]{1,2,0:T(8,128)S(1)} fusion(f32[384,128]{0,1:T(8,128)} %fusion.44, bf16[384,4096]{1,0:T(8,128)(2,1)} %param.5, bf16[4096,128]{1,0:T(8,128)(2,1)S(1)} %copy-done.2), kind=kOutput, calls=%fused_computation.25 | convolution fusion | flops 201375744 | bytes 2490368 | tf_op jit(solution)/shard_map/dot_general | solution.py:11
  13.4 0.1 collective-permute-start.3
  13.4 2.1 %fusion.34 = f32[384,128]{0,1:T(8,128)S(1)} fusion(bf16[2048,128]{1,0:T(8,128)(2,1)} %collective-permute-done.1, bf16[384,4096]{1,0:T(8,128)(2,1)} %param.5), kind=kOutput, calls=%fused_computation.57 | convolution fusion | flops 201326592 | bytes 2293760 | tf_op jit(solution)/shard_map/dot_general | solution.py:11
  15.5 13.0 %collective-permute-done.7 = bf16[2048,128]{1,0:T(8,128)(2,1)} collective-permute-done((bf16[2048,128]{1,0:T(8,128)(2,1)}, bf16[2048,128]{1,0:T(8,128)(2,1)}, u32[]{:S(2)}, u32[]{:S(2)}) %collective-permute-start.7) | collective-permute-done | bytes 524320 | tf_op jit(solution)/shard_map/ppermute | solution.py:26
  28.5 3.9 %collective-permute-start.17 = (bf16[128,128]{1,0:T(8,128)(2,1)S(1)}, bf16[128,128]{1,0:T(8,128)(2,1)S(1)}, u32[]{:S(2)}, u32[]{:S(2)}) collective-permute-start(bf16[128,128]{1,0:T(8,128)(2,1)S(1)} %slice.33), channel_id=1, source_target_pairs={{0,4},{4,8},{8,12},{12,16},{16,20},{20,24},{24,28},{1,5},{5,9},{9,... | collective-permute-start | bytes 98312 | tf_op jit(solution)/shard_map/ppermute | solution.py:22
  32.4 0.0 collective-permute-done
  32.4 2.4 %collective-permute-start.11 = (bf16[2048,128]{1,0:T(8,128)(2,1)}, bf16[2048,128]{1,0:T(8,128)(2,1)S(1)}, u32[]{:S(2)}, u32[]{:S(2)}) collective-permute-start(bf16[2048,128]{1,0:T(8,128)(2,1)} %collective-permute-done.7), channel_id=1, source_target_pairs={{0,8},{4,12},{8,0},{12,4},{16,24},{20,28},{24,16},{28,20},{1,9},{5... | collective-permute-start | bytes 1572872 | tf_op jit(solution)/shard_map/ppermute | solution.py:26
  34.8 0.6 fusion.9
  35.5 1.6 %fusion.28 = f32[384,128]{0,1:T(8,128)S(1)} fusion(bf16[2048,128]{1,0:T(8,128)(2,1)} %collective-permute-done.7, bf16[384,4096]{1,0:T(8,128)(2,1)S(1)} %copy-done.1), kind=kOutput, calls=%fused_computation.51 | convolution fusion | flops 201326592 | bytes 2293760 | tf_op jit(solution)/shard_map/dot_general | solution.py:11
  37.1 0.1 collective-permute-start.9
  37.2 0.0 collective-permute-done.6
  37.2 0.1 collective-permute-start.10
  37.3 0.5 collective-permute-start.8
  37.8 0.6 fusion.32
  38.4 1.6 %fusion.6 = f32[1,384,128]{1,2,0:T(8,128)S(1)} fusion(f32[384,128]{0,1:T(8,128)S(1)} %fusion.28, bf16[2048,128]{1,0:T(8,128)(2,1)} %collective-permute-done.6, bf16[384,4096]{1,0:T(8,128)(2,1)S(1)} %copy-done.1), kind=kOutput, calls=%fused_computation.17 | convolution fusion | flops 201375744 | bytes 2490368 | tf_op jit(solution)/shard_map/dot_general | solution.py:11
  40.0 0.6 fusion.8
  40.6 6.2 %collective-permute-done.11 = bf16[2048,128]{1,0:T(8,128)(2,1)S(1)} collective-permute-done((bf16[2048,128]{1,0:T(8,128)(2,1)}, bf16[2048,128]{1,0:T(8,128)(2,1)S(1)}, u32[]{:S(2)}, u32[]{:S(2)}) %collective-permute-start.11) | collective-permute-done | bytes 524320 | tf_op jit(solution)/shard_map/ppermute | solution.py:26
  46.9 0.0 collective-permute-start.5
  46.9 0.6 fusion.24
  47.4 0.0 collective-permute-done.9
  47.5 0.6 collective-permute-start.4
  48.0 0.6 fusion.26
  48.6 1.7 %collective-permute-done.10 = bf16[2048,128]{1,0:T(8,128)(2,1)S(1)} collective-permute-done((bf16[2048,128]{1,0:T(8,128)(2,1)S(1)}, bf16[2048,128]{1,0:T(8,128)(2,1)S(1)}, u32[]{:S(2)}, u32[]{:S(2)}) %collective-permute-start.10) | collective-permute-done | bytes 524320 | tf_op jit(solution)/shard_map/ppermute | solution.py:26
  50.3 1.3 %collective-permute-start.13 = (bf16[2048,128]{1,0:T(8,128)(2,1)S(1)}, bf16[2048,128]{1,0:T(8,128)(2,1)S(1)}, u32[]{:S(2)}, u32[]{:S(2)}) collective-permute-start(bf16[2048,128]{1,0:T(8,128)(2,1)S(1)} %collective-permute-done.11), channel_id=1, source_target_pairs={{0,4},{4,0},{8,12},{12,8},{16,20},{20,16},{24,28},{28,24},{1,5},{5... | collective-permute-start | bytes 1572872 | tf_op jit(solution)/shard_map/ppermute | solution.py:26
  51.6 0.0 collective-permute-start.12
  51.6 0.6 fusion.5
  52.2 0.0 collective-permute-done.5
  52.2 0.6 fusion.30
  52.8 0.0 collective-permute-done.4
  52.8 0.6 fusion.7
  53.5 0.6 fusion.4
  54.1 0.6 fusion.22
  54.7 0.6 fusion.3
  55.4 0.2 fusion.64
  55.6 0.7 dynamic-slice_bitcast_fusion.2
  56.3 3.3 %collective-permute-start.16 = (bf16[384,256]{0,1:T(8,128)(2,1)}, bf16[384,256]{0,1:T(8,128)(2,1)S(1)}, u32[]{:S(2)}, u32[]{:S(2)}) collective-permute-start(bf16[384,256]{0,1:T(8,128)(2,1)} %get-tuple-element.10), channel_id=1, source_target_pairs={{0,3},{1,2},{2,1},{3,0},{4,7},{5,6},{6,5},{7,4},{8,11},{9,10},{10,... | collective-permute-start | bytes 589832 | tf_op jit(solution)/shard_map/ppermute | solution.py:26
  59.7 0.3 collective-permute-start.14
  59.9 0.5 convolution_convert_fusion.2
  60.4 0.1 pad_maximum_fusion
  60.6 3.9 %collective-permute-done.16 = bf16[384,256]{0,1:T(8,128)(2,1)S(1)} collective-permute-done((bf16[384,256]{0,1:T(8,128)(2,1)}, bf16[384,256]{0,1:T(8,128)(2,1)S(1)}, u32[]{:S(2)}, u32[]{:S(2)}) %collective-permute-start.16) | collective-permute-done | bytes 196640 | tf_op jit(solution)/shard_map/ppermute | solution.py:26
  64.5 11.8 %collective-permute-done.15 = bf16[384,256]{0,1:T(8,128)(2,1)} collective-permute-done((bf16[384,256]{0,1:T(8,128)(2,1)S(1)}, bf16[384,256]{0,1:T(8,128)(2,1)}, u32[]{:S(2)}, u32[]{:S(2)}) %collective-permute-start.15) | collective-permute-done | bytes 196640 | tf_op jit(solution)/shard_map/ppermute | solution.py:26
  76.3 1.1 %reduce-precision_convert_fusion = (bf16[384,256]{0,1:T(8,128)(2,1)S(1)}, bf16[384,256]{0,1:T(8,128)(2,1)S(1)}) fusion(bf16[384,256]{0,1:T(8,128)(2,1)S(1)} %collective-permute-done.16, bf16[384,256]{0,1:T(8,128)(2,1)} %collective-permute-done.15, bf16[384,256]{0,1:T(8,128)(2,1)} %collective-permute-done.14, f32[4,384,256]{1,2,0:T(8,128)S(1)} %pad_maximum_fusion, ...), kind=kLoop, calls=%fused_computation.33 | loop fusion | flops 983040 | bytes 1376260 | tf_op jit(solution)/shard_map/convert_element_type | solution.py:16
  77.4 0.2 fusion.58
  77.6 0.3 fusion.46
  77.9 0.2 convolution_convert_fusion.4
  78.2 0.2 convolution_add_fusion.11
  78.4 3.2 %collective-permute-start.19 = (f32[128,256]{1,0:T(8,128)S(1)}, f32[128,256]{1,0:T(8,128)S(1)}, u32[]{:S(2)}, u32[]{:S(2)}) collective-permute-start(f32[128,256]{1,0:T(8,128)S(1)} %convolution_add_fusion.11), channel_id=1, source_target_pairs={{0,4},{4,8},{8,12},{12,16},{16,20},{20,24},{24,28},{1,5},{5,9},{9,... | collective-permute-start | bytes 393224 | tf_op jit(solution)/shard_map/ppermute | solution.py:22
  81.6 0.3 fusion.66
  81.9 0.3 convolution_add_fusion.1
  82.2 1.9 %collective-permute-start.18 = (bf16[128,256]{1,0:T(8,128)(2,1)S(1)}, bf16[128,256]{1,0:T(8,128)(2,1)S(1)}, u32[]{:S(2)}, u32[]{:S(2)}) collective-permute-start(bf16[128,256]{1,0:T(8,128)(2,1)S(1)} %convolution_convert_fusion.4), channel_id=1, source_target_pairs={{4,0},{8,4},{12,8},{16,12},{20,16},{24,20},{28,24},{5,1},{9,5},{13... | collective-permute-start | bytes 196616 | tf_op jit(solution)/shard_map/ppermute | solution.py:22
  84.1 0.3 fusion.1
  84.4 0.3 fusion.50
  84.7 0.3 fusion.49
  85.1 2.7 %collective-permute-done.18 = bf16[128,256]{1,0:T(8,128)(2,1)S(1)} collective-permute-done((bf16[128,256]{1,0:T(8,128)(2,1)S(1)}, bf16[128,256]{1,0:T(8,128)(2,1)S(1)}, u32[]{:S(2)}, u32[]{:S(2)}) %collective-permute-start.18) | collective-permute-done | bytes 65568 | tf_op jit(solution)/shard_map/ppermute | solution.py:22
  87.7 0.9 %fusion.2 = f32[384,256]{1,0:T(8,128)} fusion(f32[384,256]{1,0:T(8,128)S(1)} %fusion.50, f32[384,256]{1,0:T(8,128)S(1)} %fusion.49, f32[384,256]{1,0:T(8,128)S(1)} %fusion.1, bf16[128,256]{1,0:T(8,128)(2,1)S(1)} %collective-permute-done.18, bf16[512,512]{1,0:T(8,128)(2,1)S(1)} %convolution_convert_fusion), kind=kOutput, calls=%fused_computation.9 | convolution fusion | flops 25460736 | bytes 1736704 | tf_op jit(solution)/shard_map/dot_general | solution.py:11
  (24 shorter events, 0.2 us)
Async XLA Ops:
  0.0 10.1 %copy-start = (bf16[1,512,512]{2,1,0:T(8,128)(2,1)S(1)}, bf16[1,512,512]{2,1,0:T(8,128)(2,1)}, u32[]{:S(2)}) copy-start(bf16[1,512,512]{2,1,0:T(8,128)(2,1)} %param.7) | copy-start | bytes 1572868
  0.0 7.4 %copy-start.2 = (bf16[4096,128]{1,0:T(8,128)(2,1)S(1)}, bf16[4096,128]{1,0:T(8,128)(2,1)}, u32[]{:S(2)}) copy-start(bf16[4096,128]{1,0:T(8,128)(2,1)} %param.6) | copy-start | bytes 3145732
  2.4 7.7 %copy-start.4 = (s32[1,512]{1,0:T(1,128)S(1)}, s32[1,512]{1,0:T(1,128)}, u32[]{:S(2)}) copy-start(s32[1,512]{1,0:T(1,128)} %param.8) | copy-start | bytes 6148
  2.4 34.7 %collective-permute-start.2 = (bf16[2048,128]{1,0:T(8,128)(2,1)}, bf16[2048,128]{1,0:T(8,128)(2,1)S(1)}, u32[]{:S(2)}, u32[]{:S(2)}) collective-permute-start(bf16[2048,128]{1,0:T(8,128)(2,1)} %get-tuple-element.7), channel_id=1, source_target_pairs={{0,8},{4,12},{8,0},{12,4},{16,24},{20,28},{24,16},{28,20},{1,9},{5... | collective-permute-start | bytes 1572872 | tf_op jit(solution)/shard_map/ppermute | solution.py:26
  4.5 32.7 %collective-permute-start.6 = (bf16[2048,128]{1,0:T(8,128)(2,1)}, bf16[2048,128]{1,0:T(8,128)(2,1)}, u32[]{:S(2)}, u32[]{:S(2)}) collective-permute-start(bf16[2048,128]{1,0:T(8,128)(2,1)} %get-tuple-element.7), channel_id=1, source_target_pairs={{0,16},{4,20},{8,24},{12,28},{16,0},{20,4},{24,8},{28,12},{1,17},{... | collective-permute-start | bytes 1572872 | tf_op jit(solution)/shard_map/ppermute | solution.py:26
  5.7 22.8 %collective-permute-start.7 = (bf16[2048,128]{1,0:T(8,128)(2,1)}, bf16[2048,128]{1,0:T(8,128)(2,1)}, u32[]{:S(2)}, u32[]{:S(2)}) collective-permute-start(bf16[2048,128]{1,0:T(8,128)(2,1)} %get-tuple-element.8), channel_id=1, source_target_pairs={{0,16},{4,20},{8,24},{12,28},{16,0},{20,4},{24,8},{28,12},{1,17},{... | collective-permute-start | bytes 1572872 | tf_op jit(solution)/shard_map/ppermute | solution.py:26
  5.9 7.4 %collective-permute-start.1 = (bf16[2048,128]{1,0:T(8,128)(2,1)}, bf16[2048,128]{1,0:T(8,128)(2,1)}, u32[]{:S(2)}, u32[]{:S(2)}) collective-permute-start(bf16[2048,128]{1,0:T(8,128)(2,1)} %get-tuple-element.8), channel_id=1, source_target_pairs={{0,4},{4,0},{8,12},{12,8},{16,20},{20,16},{24,28},{28,24},{1,5},{5... | collective-permute-start | bytes 1572872 | tf_op jit(solution)/shard_map/ppermute | solution.py:26
  7.4 24.9 %collective-permute-start = (bf16[2048,128]{1,0:T(8,128)(2,1)}, bf16[2048,128]{1,0:T(8,128)(2,1)S(1)}, u32[]{:S(2)}, u32[]{:S(2)}) collective-permute-start(bf16[2048,128]{1,0:T(8,128)(2,1)} %get-tuple-element.7), channel_id=1, source_target_pairs={{0,4},{4,0},{8,12},{12,8},{16,20},{20,16},{24,28},{28,24},{1,5},{5... | collective-permute-start | bytes 1572872 | tf_op jit(solution)/shard_map/ppermute | solution.py:26
  11.2 23.6 %copy-start.1 = (bf16[384,4096]{1,0:T(8,128)(2,1)S(1)}, bf16[384,4096]{1,0:T(8,128)(2,1)}, u32[]{:S(2)}) copy-start(bf16[384,4096]{1,0:T(8,128)(2,1)} %param.5) | copy-start | bytes 9437188
  13.4 23.9 %collective-permute-start.3 = (bf16[2048,128]{1,0:T(8,128)(2,1)}, bf16[2048,128]{1,0:T(8,128)(2,1)S(1)}, u32[]{:S(2)}, u32[]{:S(2)}) collective-permute-start(bf16[2048,128]{1,0:T(8,128)(2,1)} %get-tuple-element.8), channel_id=1, source_target_pairs={{0,8},{4,12},{8,0},{12,4},{16,24},{20,28},{24,16},{28,20},{1,9},{5... | collective-permute-start | bytes 1572872 | tf_op jit(solution)/shard_map/ppermute | solution.py:26
  28.5 31.5 %collective-permute-start.17 = (bf16[128,128]{1,0:T(8,128)(2,1)S(1)}, bf16[128,128]{1,0:T(8,128)(2,1)S(1)}, u32[]{:S(2)}, u32[]{:S(2)}) collective-permute-start(bf16[128,128]{1,0:T(8,128)(2,1)S(1)} %slice.33), channel_id=1, source_target_pairs={{0,4},{4,8},{8,12},{12,16},{16,20},{20,24},{24,28},{1,5},{5,9},{9,... | collective-permute-start | bytes 98312 | tf_op jit(solution)/shard_map/ppermute | solution.py:22
  32.4 14.5 %collective-permute-start.11 = (bf16[2048,128]{1,0:T(8,128)(2,1)}, bf16[2048,128]{1,0:T(8,128)(2,1)S(1)}, u32[]{:S(2)}, u32[]{:S(2)}) collective-permute-start(bf16[2048,128]{1,0:T(8,128)(2,1)} %collective-permute-done.7), channel_id=1, source_target_pairs={{0,8},{4,12},{8,0},{12,4},{16,24},{20,28},{24,16},{28,20},{1,9},{5... | collective-permute-start | bytes 1572872 | tf_op jit(solution)/shard_map/ppermute | solution.py:26
  37.1 10.3 %collective-permute-start.9 = (bf16[2048,128]{1,0:T(8,128)(2,1)}, bf16[2048,128]{1,0:T(8,128)(2,1)S(1)}, u32[]{:S(2)}, u32[]{:S(2)}) collective-permute-start(bf16[2048,128]{1,0:T(8,128)(2,1)} %collective-permute-done.7), channel_id=1, source_target_pairs={{0,4},{4,0},{8,12},{12,8},{16,20},{20,16},{24,28},{28,24},{1,5},{5... | collective-permute-start | bytes 1572872 | tf_op jit(solution)/shard_map/ppermute | solution.py:26
  37.2 13.1 %collective-permute-start.10 = (bf16[2048,128]{1,0:T(8,128)(2,1)S(1)}, bf16[2048,128]{1,0:T(8,128)(2,1)S(1)}, u32[]{:S(2)}, u32[]{:S(2)}) collective-permute-start(bf16[2048,128]{1,0:T(8,128)(2,1)S(1)} %collective-permute-done.2), channel_id=1, source_target_pairs={{0,16},{4,20},{8,24},{12,28},{16,0},{20,4},{24,8},{28,12},{1,17},{... | collective-permute-start | bytes 1572872 | tf_op jit(solution)/shard_map/ppermute | solution.py:26
  37.3 14.3 %collective-permute-start.8 = (bf16[2048,128]{1,0:T(8,128)(2,1)}, bf16[2048,128]{1,0:T(8,128)(2,1)S(1)}, u32[]{:S(2)}, u32[]{:S(2)}) collective-permute-start(bf16[2048,128]{1,0:T(8,128)(2,1)} %collective-permute-done.6), channel_id=1, source_target_pairs={{0,4},{4,0},{8,12},{12,8},{16,20},{20,16},{24,28},{28,24},{1,5},{5... | collective-permute-start | bytes 1572872 | tf_op jit(solution)/shard_map/ppermute | solution.py:26
  46.9 5.4 %collective-permute-start.5 = (bf16[2048,128]{1,0:T(8,128)(2,1)S(1)}, bf16[2048,128]{1,0:T(8,128)(2,1)S(1)}, u32[]{:S(2)}, u32[]{:S(2)}) collective-permute-start(bf16[2048,128]{1,0:T(8,128)(2,1)S(1)} %collective-permute-done.3), channel_id=1, source_target_pairs={{0,4},{4,0},{8,12},{12,8},{16,20},{20,16},{24,28},{28,24},{1,5},{5... | collective-permute-start | bytes 1572872 | tf_op jit(solution)/shard_map/ppermute | solution.py:26
  47.5 5.4 %collective-permute-start.4 = (bf16[2048,128]{1,0:T(8,128)(2,1)S(1)}, bf16[2048,128]{1,0:T(8,128)(2,1)S(1)}, u32[]{:S(2)}, u32[]{:S(2)}) collective-permute-start(bf16[2048,128]{1,0:T(8,128)(2,1)S(1)} %collective-permute-done.2), channel_id=1, source_target_pairs={{0,4},{4,0},{8,12},{12,8},{16,20},{20,16},{24,28},{28,24},{1,5},{5... | collective-permute-start | bytes 1572872 | tf_op jit(solution)/shard_map/ppermute | solution.py:26
  50.3 3.8 %collective-permute-start.13 = (bf16[2048,128]{1,0:T(8,128)(2,1)S(1)}, bf16[2048,128]{1,0:T(8,128)(2,1)S(1)}, u32[]{:S(2)}, u32[]{:S(2)}) collective-permute-start(bf16[2048,128]{1,0:T(8,128)(2,1)S(1)} %collective-permute-done.11), channel_id=1, source_target_pairs={{0,4},{4,0},{8,12},{12,8},{16,20},{20,16},{24,28},{28,24},{1,5},{5... | collective-permute-start | bytes 1572872 | tf_op jit(solution)/shard_map/ppermute | solution.py:26
  51.6 3.1 %collective-permute-start.12 = (bf16[2048,128]{1,0:T(8,128)(2,1)S(1)}, bf16[2048,128]{1,0:T(8,128)(2,1)S(1)}, u32[]{:S(2)}, u32[]{:S(2)}) collective-permute-start(bf16[2048,128]{1,0:T(8,128)(2,1)S(1)} %collective-permute-done.10), channel_id=1, source_target_pairs={{0,4},{4,0},{8,12},{12,8},{16,20},{20,16},{24,28},{28,24},{1,5},{5... | collective-permute-start | bytes 1572872 | tf_op jit(solution)/shard_map/ppermute | solution.py:26
  55.3 4.6 %copy-start.3 = (s32[128]{0:T(128)S(1)}, s32[128]{0:T(128)}, u32[]{:S(2)}) copy-start(s32[128]{0:T(128)} %param.9) | copy-start | bytes 1540
  56.3 8.1 %collective-permute-start.16 = (bf16[384,256]{0,1:T(8,128)(2,1)}, bf16[384,256]{0,1:T(8,128)(2,1)S(1)}, u32[]{:S(2)}, u32[]{:S(2)}) collective-permute-start(bf16[384,256]{0,1:T(8,128)(2,1)} %get-tuple-element.10), channel_id=1, source_target_pairs={{0,3},{1,2},{2,1},{3,0},{4,7},{5,6},{6,5},{7,4},{8,11},{9,10},{10,... | collective-permute-start | bytes 589832 | tf_op jit(solution)/shard_map/ppermute | solution.py:26
  59.7 16.6 %collective-permute-start.15 = (bf16[384,256]{0,1:T(8,128)(2,1)S(1)}, bf16[384,256]{0,1:T(8,128)(2,1)}, u32[]{:S(2)}, u32[]{:S(2)}) collective-permute-start(bf16[384,256]{0,1:T(8,128)(2,1)S(1)} %get-tuple-element.11), channel_id=1, source_target_pairs={{0,2},{1,3},{2,0},{3,1},{4,6},{5,7},{6,4},{7,5},{8,10},{9,11},{10,... | collective-permute-start | bytes 589832 | tf_op jit(solution)/shard_map/ppermute | solution.py:26
  59.7 16.6 %collective-permute-start.14 = (bf16[384,256]{0,1:T(8,128)(2,1)S(1)}, bf16[384,256]{0,1:T(8,128)(2,1)}, u32[]{:S(2)}, u32[]{:S(2)}) collective-permute-start(bf16[384,256]{0,1:T(8,128)(2,1)S(1)} %get-tuple-element.9), channel_id=1, source_target_pairs={{0,1},{1,0},{2,3},{3,2},{4,5},{5,4},{6,7},{7,6},{8,9},{9,8},{10,11... | collective-permute-start | bytes 589832 | tf_op jit(solution)/shard_map/ppermute | solution.py:26
  78.4 6.0 %collective-permute-start.19 = (f32[128,256]{1,0:T(8,128)S(1)}, f32[128,256]{1,0:T(8,128)S(1)}, u32[]{:S(2)}, u32[]{:S(2)}) collective-permute-start(f32[128,256]{1,0:T(8,128)S(1)} %convolution_add_fusion.11), channel_id=1, source_target_pairs={{0,4},{4,8},{8,12},{12,16},{16,20},{20,24},{24,28},{1,5},{5,9},{9,... | collective-permute-start | bytes 393224 | tf_op jit(solution)/shard_map/ppermute | solution.py:22
  82.2 5.6 %collective-permute-start.18 = (bf16[128,256]{1,0:T(8,128)(2,1)S(1)}, bf16[128,256]{1,0:T(8,128)(2,1)S(1)}, u32[]{:S(2)}, u32[]{:S(2)}) collective-permute-start(bf16[128,256]{1,0:T(8,128)(2,1)S(1)} %convolution_convert_fusion.4), channel_id=1, source_target_pairs={{4,0},{8,4},{12,8},{16,12},{20,16},{24,20},{28,24},{5,1},{9,5},{13... | collective-permute-start | bytes 196616 | tf_op jit(solution)/shard_map/ppermute | solution.py:22

commit v2 on v1

--- a/solution.py
+++ b/solution.py
@@ -27,33 +27,35 @@
 
 
 def rotate_square(wavefunctions, rotation):
-    domain, band = lax.axis_index("domain"), lax.axis_index("band")
-    chip, core = domain // 2, domain % 2
+    chip, core, band = lax.axis_index("domain") // 2, lax.axis_index("domain") % 2, lax.axis_index("band")
+    first = core == 0
     half = rotation.shape[0] // 2
-    top, bottom = rotation[:half], rotation[half:]
-    near_top = exchanged(top, "domain", NEAR)
-    far_bottom = exchanged(bottom, "domain", FAR)
-    near_bottom = exchanged(bottom, "domain", NEAR)
-    far_top = exchanged(top, "domain", FAR)
-    both_top = exchanged(near_top, "domain", FAR)
-    both_bottom = exchanged(far_bottom, "domain", NEAR)
-    pieces = [(top, bottom), (near_top, near_bottom), (far_top, far_bottom), (both_top, both_bottom)]
-    w_top, w_bottom = wavefunctions[:, :half], wavefunctions[:, half:]
-    blocks = []
-    for upper, lower in pieces:
-        other_upper = exchanged(upper, "domain", CORE)
-        other_lower = exchanged(lower, "domain", CORE)
-        mine = dot(w_top, upper) + dot(w_bottom, lower)
-        other = dot(w_top, other_upper) + dot(w_bottom, other_lower)
-        blocks.append(jnp.where(core == 0, jnp.concatenate([mine, other], 1), jnp.concatenate([other, mine], 1)))
-    partial = jnp.stack(blocks)
-    rounded = partial.astype(jnp.bfloat16)
-    place = chip ^ band
-    total = lax.dynamic_index_in_dim(partial, place, 0, keepdims=False)
-    for mask in range(1, lax.axis_size("band")):
-        sent = lax.dynamic_index_in_dim(rounded, place ^ mask, 0, keepdims=False)
-        total = total + exchanged(sent, "band", mask).astype(jnp.float32)
-    return total
+    start, other_start = core * half, (1 - core) * half
+    keep = lax.dynamic_slice_in_dim(rotation, start, half, 0)
+    received = exchanged(lax.dynamic_slice_in_dim(rotation, other_start, half, 0), "domain", CORE)
+    mine = lax.dynamic_slice_in_dim(wavefunctions, start, half, 1)
+    theirs = exchanged(lax.dynamic_slice_in_dim(wavefunctions, other_start, half, 1), "domain", CORE)
+    onward = [(source, source ^ (NEAR if source & CORE else FAR)) for source in range(lax.axis_size("domain"))]
+
+    def unit(shard):
+        near, far = exchanged(shard, "domain", NEAR), exchanged(shard, "domain", FAR)
+        both = lax.ppermute(jnp.where(first, near, far), "domain", onward)
+        return shard, near, far, both
+
+    def reduced(shards):
+        swapped = [exchanged(dot(theirs, shard), "domain", CORE) for shard in shards]
+        partial = jnp.stack([dot(mine, shard) + other for shard, other in zip(shards, swapped)])
+        rounded = partial.astype(jnp.bfloat16)
+        place = chip ^ band
+        total = lax.dynamic_index_in_dim(partial, place, 0, keepdims=False)
+        for mask in range(1, lax.axis_size("band")):
+            sent = lax.dynamic_index_in_dim(rounded, place ^ mask, 0, keepdims=False)
+            total = total + exchanged(sent, "band", mask).astype(jnp.float32)
+        return total
+
+    left = unit(jnp.where(first, keep, received))
+    right = unit(jnp.where(first, received, keep))
+    return jnp.concatenate([reduced(left), reduced(right)], 1)
 
 
 def rotate_any(wavefunctions, rotation):

time: 89.1 us -> 100 us (1.12)
  waiting for transfers between devices: 39.4 us -> 25.1 us
  matrix products: 21.5 us -> 34.2 us
  starting transfers between devices: 22.6 us -> 29.4 us
  other arithmetic: 1.61 us -> 5.8 us
  local copies, waits for them, and re-layouts: 3.18 us -> 4.23 us
    ppermute x17 -> x20, waiting for transfers between devices: 36.7 us -> 19 us  [exchanged(): lax.ppermute(value, axis, [(source, source ^ mask) for source in range(la...]
    dot_general x28, matrix products: 21.5 us -> 34.2 us  [dot(): jnp.dot(left, right, precision=precision, preferred_element_type=jnp.floa...]
    ppermute x17 -> x20, starting transfers between devices: 13.6 us -> 19 us  [exchanged(): lax.ppermute(value, axis, [(source, source ^ mask) for source in range(la...]
    select_n x4 -> x3, other arithmetic: 0.14 us -> 5.42 us  [the longest x2 3.02 us: unit(): both = lax.ppermute(jnp.where(first, near, far), 'domain', onward)]
    ppermute x0 -> x2, waiting for transfers between devices: none -> 3.44 us  [unit(): both = lax.ppermute(jnp.where(first, near, far), 'domain', onward)]
    dynamic_slice x0 -> x2, local copies, waits for them, and re-layouts: none -> 3.36 us  [the longest x1 2.03 us: rotate_square(): lax.dynamic_slice_in_dim(rotation, other_start, half, 0)]
    slice x1 -> x0, local copies, waits for them, and re-layouts: 2.41 us -> none  [rotate_square(): top, bottom = (rotation[:half], rotation[half:])]
    ppermute x0 -> x2, starting transfers between devices: none -> 2.07 us  [unit(): both = lax.ppermute(jnp.where(first, near, far), 'domain', onward)]
  transfers between devices with their start and end apart: 20 -> 25, of which waited for: 6 -> 8; matrix products, arithmetic and copies ran while one was open for 23% -> 38% of each run, Pallas kernels for 0% -> 0%
where the time goes in v2:
time: 100 us; the launch traced here: 99.3 us
  matrix products  34.2 us (34%)
  starting transfers between devices  29.4 us (29%)
  waiting for transfers between devices  25.1 us (25%)
  other arithmetic  5.8 us (6%)
  local copies, waits for them, and re-layouts  4.23 us (4%)
    dot_general x28, matrix products, dot(): jnp.dot(left, right, precision=precision, preferred_element_type=jnp.floa...  34.2 us
    ppermute x20, starting transfers between devices, exchanged(): lax.ppermute(value, axis, [(source, source ^ mask) for source in range(la...  19 us
    ppermute x20, waiting for transfers between devices, exchanged(): lax.ppermute(value, axis, [(source, source ^ mask) for source in range(la...  19 us
    ppermute x3, starting transfers between devices, shifted(): lax.ppermute(value, axis, [(source, source + steps) for source in range(l...  8.33 us
    ppermute x2, waiting for transfers between devices, unit(): both = lax.ppermute(jnp.where(first, near, far), 'domain', onward)  3.44 us
    select_n x2, other arithmetic, unit(): both = lax.ppermute(jnp.where(first, near, far), 'domain', onward)  3.02 us
    ppermute x3, waiting for transfers between devices, shifted(): lax.ppermute(value, axis, [(source, source + steps) for source in range(l...  2.68 us
    select_n x1, other arithmetic, rotate_square(): left = unit(jnp.where(first, keep, received))  2.4 us
  transfers between devices with their start and end apart: 25, of which 8 were waited for; matrix products, arithmetic and copies ran while one was open for 38% of the time, Pallas kernels for 0%

profile of v2, /device:TPU:1, one launch (start us, length us, event | category | flops | bytes accessed | tf_op | source)
XLA Modules:
  0.0 99.3 jit_solution(7336194925662375198)
XLA Ops:
  0.0 2.0 %constant_dynamic-slice_fusion.1 = bf16[2048,128]{1,0:T(8,128)(2,1)} fusion(bf16[4096,128]{1,0:T(8,128)(2,1)} %param.6, s32[]{:T(128)S(6)} %select_n.60), kind=kLoop, calls=%fused_computation.89 | loop fusion | bytes 1048580 | tf_op jit(solution)/shard_map/dynamic_slice | solution.py:35
  2.1 2.2 %collective-permute-done = bf16[2048,128]{1,0:T(8,128)(2,1)} collective-permute-done((bf16[2048,128]{1,0:T(8,128)(2,1)}, bf16[2048,128]{1,0:T(8,128)(2,1)}, u32[]{:S(2)}, u32[]{:S(2)}) %collective-permute-start) | collective-permute-done | bytes 524320 | tf_op jit(solution)/shard_map/ppermute | solution.py:26
  4.3 2.4 %broadcast_select_fusion.3 = (bf16[2048,128]{1,0:T(8,128)(2,1)}, bf16[2048,128]{1,0:T(8,128)(2,1)}) fusion(bf16[2048,128]{1,0:T(8,128)(2,1)} %collective-permute-done, pred[]{:T(512)S(6)} %eq.76, bf16[4096,128]{1,0:T(8,128)(2,1)} %param.6, s32[]{:T(128)S(6)} %select_n.58), kind=kLoop, calls=%fused_computation.41 | loop fusion | flops 524288 | bytes 2097157 | tf_op jit(solution)/shard_map/jit(_where)/select_n | solution.py:56
  6.7 2.3 %collective-permute-start.13 = (bf16[2048,128]{1,0:T(8,128)(2,1)}, bf16[2048,128]{1,0:T(8,128)(2,1)}, u32[]{:S(2)}, u32[]{:S(2)}) collective-permute-start(bf16[2048,128]{1,0:T(8,128)(2,1)} %get-tuple-element.6), channel_id=1, source_target_pairs={{0,8},{4,12},{8,0},{12,4},{16,24},{20,28},{24,16},{28,20},{1,9},{5... | collective-permute-start | bytes 1572872 | tf_op jit(solution)/shard_map/ppermute | solution.py:26
  9.0 1.2 %collective-permute-start.15 = (bf16[2048,128]{1,0:T(8,128)(2,1)}, bf16[2048,128]{1,0:T(8,128)(2,1)}, u32[]{:S(2)}, u32[]{:S(2)}) collective-permute-start(bf16[2048,128]{1,0:T(8,128)(2,1)} %get-tuple-element.6), channel_id=1, source_target_pairs={{0,16},{4,20},{8,24},{12,28},{16,0},{20,4},{24,8},{28,12},{1,17},{... | collective-permute-start | bytes 1572872 | tf_op jit(solution)/shard_map/ppermute | solution.py:26
  10.3 1.3 %constant_dynamic-slice_fusion = bf16[384,2048]{1,0:T(8,128)(2,1)} fusion(bf16[384,4096]{1,0:T(8,128)(2,1)S(1)} %copy-done, s32[]{:T(128)S(6)} %select_n.60), kind=kLoop, calls=%fused_computation.88 | loop fusion | bytes 3145732 | tf_op jit(solution)/shard_map/dynamic_slice | solution.py:37
  11.6 0.9 collective-permute-start.1
  12.5 2.8 %convolution_convert_fusion = bf16[512,512]{1,0:T(8,128)(2,1)} fusion(bf16[1,512,512]{2,1,0:T(8,128)(2,1)} %param.7, s32[512]{0:T(512)S(1)} %bitcast.81), kind=kOutput, calls=%fused_computation | convolution fusion | flops 537919488 | bytes 1050624 | tf_op jit(solution)/shard_map/dot_general | solution.py:11
  15.4 0.8 slice.17
  16.1 2.0 %collective-permute-start.22 = (bf16[128,128]{1,0:T(8,128)(2,1)S(1)}, bf16[128,128]{1,0:T(8,128)(2,1)S(1)}, u32[]{:S(2)}, u32[]{:S(2)}) collective-permute-start(bf16[128,128]{1,0:T(8,128)(2,1)S(1)} %slice.17), channel_id=1, source_target_pairs={{0,4},{4,8},{8,12},{12,16},{16,20},{20,24},{24,28},{1,5},{5,9},{9,... | collective-permute-start | bytes 98312 | tf_op jit(solution)/shard_map/ppermute | solution.py:22
  18.2 1.2 %collective-permute-start.3 = (bf16[2048,128]{1,0:T(8,128)(2,1)}, bf16[2048,128]{1,0:T(8,128)(2,1)}, u32[]{:S(2)}, u32[]{:S(2)}) collective-permute-start(bf16[2048,128]{1,0:T(8,128)(2,1)} %get-tuple-element.5), channel_id=1, source_target_pairs={{0,8},{4,12},{8,0},{12,4},{16,24},{20,28},{24,16},{28,20},{1,9},{5... | collective-permute-start | bytes 1572872 | tf_op jit(solution)/shard_map/ppermute | solution.py:26
  19.5 1.9 %collective-permute-done.13 = bf16[2048,128]{1,0:T(8,128)(2,1)} collective-permute-done((bf16[2048,128]{1,0:T(8,128)(2,1)}, bf16[2048,128]{1,0:T(8,128)(2,1)}, u32[]{:S(2)}, u32[]{:S(2)}) %collective-permute-start.13) | collective-permute-done | bytes 524320 | tf_op jit(solution)/shard_map/ppermute | solution.py:26
  21.3 1.2 %collective-permute-start.5 = (bf16[2048,128]{1,0:T(8,128)(2,1)}, bf16[2048,128]{1,0:T(8,128)(2,1)}, u32[]{:S(2)}, u32[]{:S(2)}) collective-permute-start(bf16[2048,128]{1,0:T(8,128)(2,1)} %get-tuple-element.5), channel_id=1, source_target_pairs={{0,16},{4,20},{8,24},{12,28},{16,0},{20,4},{24,8},{28,12},{1,17},{... | collective-permute-start | bytes 1572872 | tf_op jit(solution)/shard_map/ppermute | solution.py:26
  22.5 1.9 %broadcast_select_fusion = bf16[2048,128]{1,0:T(8,128)(2,1)} fusion(bf16[2048,128]{1,0:T(8,128)(2,1)} %collective-permute-done.13, bf16[2048,128]{1,0:T(8,128)(2,1)} %collective-permute-done.15, pred[]{:T(512)S(6)} %eq.76), kind=kLoop, calls=%fused_computation.38 | loop fusion | flops 262144 | bytes 1572865 | tf_op jit(solution)/shard_map/jit(_where)/select_n | solution.py:42
  24.4 1.2 %collective-permute-start.17 = (bf16[2048,128]{1,0:T(8,128)(2,1)}, bf16[2048,128]{1,0:T(8,128)(2,1)}, u32[]{:S(2)}, u32[]{:S(2)}) collective-permute-start(bf16[2048,128]{1,0:T(8,128)(2,1)} %broadcast_select_fusion), channel_id=1, source_target_pairs={{0,16},{4,12},{8,24},{12,4},{16,0},{20,28},{24,8},{28,20},{1,17},{... | collective-permute-start | bytes 1572872 | tf_op jit(solution)/shard_map/ppermute | solution.py:42
  25.7 0.5 convolution_convert_fusion.2
  26.2 7.1 %collective-permute-done.3 = bf16[2048,128]{1,0:T(8,128)(2,1)} collective-permute-done((bf16[2048,128]{1,0:T(8,128)(2,1)}, bf16[2048,128]{1,0:T(8,128)(2,1)}, u32[]{:S(2)}, u32[]{:S(2)}) %collective-permute-start.3) | collective-permute-done | bytes 524320 | tf_op jit(solution)/shard_map/ppermute | solution.py:26
  33.3 0.4 collective-permute-done.5
  33.6 1.1 %broadcast_select_fusion.2 = bf16[2048,128]{1,0:T(8,128)(2,1)S(1)} fusion(bf16[2048,128]{1,0:T(8,128)(2,1)} %collective-permute-done.3, bf16[2048,128]{1,0:T(8,128)(2,1)} %collective-permute-done.5, pred[]{:T(512)S(6)} %eq.76), kind=kLoop, calls=%fused_computation.40 | loop fusion | flops 262144 | bytes 1572865 | tf_op jit(solution)/shard_map/jit(_where)/select_n | solution.py:42
  34.7 0.9 collective-permute-start.7
  35.6 3.4 %collective-permute-done.17 = bf16[2048,128]{1,0:T(8,128)(2,1)} collective-permute-done((bf16[2048,128]{1,0:T(8,128)(2,1)}, bf16[2048,128]{1,0:T(8,128)(2,1)}, u32[]{:S(2)}, u32[]{:S(2)}) %collective-permute-start.17) | collective-permute-done | bytes 524320 | tf_op jit(solution)/shard_map/ppermute | solution.py:42
  39.0 2.1 %fusion.68 = f32[384,128]{0,1:T(8,128)S(1)} fusion(bf16[384,2048]{1,0:T(8,128)(2,1)} %collective-permute-done.1, bf16[2048,128]{1,0:T(8,128)(2,1)} %collective-permute-done.17), kind=kOutput, calls=%fused_computation.100 | convolution fusion | flops 201326592 | bytes 2293760 | tf_op jit(solution)/shard_map/dot_general | solution.py:11
  41.1 2.6 %collective-permute-start.18 = (f32[384,128]{0,1:T(8,128)S(1)}, f32[384,128]{0,1:T(8,128)S(1)}, u32[]{:S(2)}, u32[]{:S(2)}) collective-permute-start(f32[384,128]{0,1:T(8,128)S(1)} %fusion.68), channel_id=1, source_target_pairs={{0,4},{4,0},{8,12},{12,8},{16,20},{20,16},{24,28},{28,24},{1,5},{5... | collective-permute-start | bytes 589832 | tf_op jit(solution)/shard_map/ppermute | solution.py:26
  43.8 2.1 %fusion.67 = f32[384,128]{0,1:T(8,128)S(1)} fusion(bf16[384,2048]{1,0:T(8,128)(2,1)} %collective-permute-done.1, bf16[2048,128]{1,0:T(8,128)(2,1)} %collective-permute-done.15), kind=kOutput, calls=%fused_computation.99 | convolution fusion | flops 201326592 | bytes 2293760 | tf_op jit(solution)/shard_map/dot_general | solution.py:11
  45.9 0.1 collective-permute-start.16
  46.0 2.1 %fusion.66 = f32[384,128]{0,1:T(8,128)S(1)} fusion(bf16[384,2048]{1,0:T(8,128)(2,1)} %collective-permute-done.1, bf16[2048,128]{1,0:T(8,128)(2,1)} %collective-permute-done.13), kind=kOutput, calls=%fused_computation.98 | convolution fusion | flops 201326592 | bytes 2293760 | tf_op jit(solution)/shard_map/dot_general | solution.py:11
  48.1 0.6 collective-permute-start.14
  48.6 2.1 %fusion.65 = f32[384,128]{0,1:T(8,128)S(1)} fusion(bf16[384,2048]{1,0:T(8,128)(2,1)} %collective-permute-done.1, bf16[2048,128]{1,0:T(8,128)(2,1)} %get-tuple-element.6), kind=kOutput, calls=%fused_computation.97 | convolution fusion | flops 201326592 | bytes 2293760 | tf_op jit(solution)/shard_map/dot_general | solution.py:11
  50.7 0.1 collective-permute-start.12
  50.8 2.0 %fusion.64 = f32[384,128]{0,1:T(8,128)S(1)} fusion(bf16[384,2048]{1,0:T(8,128)(2,1)} %collective-permute-done.1, bf16[2048,128]{1,0:T(8,128)(2,1)S(1)} %collective-permute-done.7), kind=kOutput, calls=%fused_computation.96 | convolution fusion | flops 201326592 | bytes 2293760 | tf_op jit(solution)/shard_map/dot_general | solution.py:11
  52.8 0.6 collective-permute-start.8
  53.3 2.1 %fusion.63 = f32[384,128]{0,1:T(8,128)S(1)} fusion(bf16[384,2048]{1,0:T(8,128)(2,1)} %collective-permute-done.1, bf16[2048,128]{1,0:T(8,128)(2,1)} %collective-permute-done.5), kind=kOutput, calls=%fused_computation.95 | convolution fusion | flops 201326592 | bytes 2293760 | tf_op jit(solution)/shard_map/dot_general | solution.py:11
  55.5 2.1 %fusion.62 = f32[384,128]{0,1:T(8,128)S(1)} fusion(bf16[384,2048]{1,0:T(8,128)(2,1)} %collective-permute-done.1, bf16[2048,128]{1,0:T(8,128)(2,1)} %collective-permute-done.3), kind=kOutput, calls=%fused_computation.94 | convolution fusion | flops 201326592 | bytes 2293760 | tf_op jit(solution)/shard_map/dot_general | solution.py:11
  57.6 2.0 %fusion.61 = f32[384,128]{0,1:T(8,128)S(1)} fusion(bf16[384,2048]{1,0:T(8,128)(2,1)} %collective-permute-done.1, bf16[2048,128]{1,0:T(8,128)(2,1)S(1)} %copy-done.1), kind=kOutput, calls=%fused_computation.93 | convolution fusion | flops 201326592 | bytes 2293760 | tf_op jit(solution)/shard_map/dot_general | solution.py:11
  59.6 0.1 collective-permute-start.6
  59.7 1.6 %fusion.3 = f32[1,384,128]{1,2,0:T(8,128)S(1)} fusion(f32[384,128]{0,1:T(8,128)S(1)} %collective-permute-done.18, bf16[2048,128]{1,0:T(8,128)(2,1)} %collective-permute-done.17, bf16[384,4096]{1,0:T(8,128)(2,1)S(1)} %copy-done, s32[]{:T(128)S(6)} %select_n.58), kind=kOutput, calls=%fused_computation.10 | convolution fusion | flops 201375744 | bytes 2490372 | tf_op jit(solution)/shard_map/dot_general | solution.py:11
  61.4 0.6 collective-permute-start.4
  61.9 1.6 %fusion.4 = f32[1,384,128]{1,2,0:T(8,128)S(1)} fusion(f32[384,128]{0,1:T(8,128)S(1)} %collective-permute-done.16, bf16[2048,128]{1,0:T(8,128)(2,1)} %collective-permute-done.15, bf16[384,4096]{1,0:T(8,128)(2,1)S(1)} %copy-done, s32[]{:T(128)S(6)} %select_n.58), kind=kOutput, calls=%fused_computation.12 | convolution fusion | flops 201375744 | bytes 2490372 | tf_op jit(solution)/shard_map/dot_general | solution.py:11
  63.5 0.1 collective-permute-start.2
  63.6 1.6 %fusion.5 = f32[1,384,128]{1,2,0:T(8,128)S(1)} fusion(f32[384,128]{0,1:T(8,128)S(1)} %collective-permute-done.14, bf16[2048,128]{1,0:T(8,128)(2,1)} %collective-permute-done.13, bf16[384,4096]{1,0:T(8,128)(2,1)S(1)} %copy-done, s32[]{:T(128)S(6)} %select_n.58), kind=kOutput, calls=%fused_computation.14 | convolution fusion | flops 201375744 | bytes 2490372 | tf_op jit(solution)/shard_map/dot_general | solution.py:11
  65.3 1.6 %fusion.6 = f32[1,384,128]{1,2,0:T(8,128)S(1)} fusion(f32[384,128]{0,1:T(8,128)S(1)} %collective-permute-done.12, bf16[2048,128]{1,0:T(8,128)(2,1)} %get-tuple-element.6, bf16[384,4096]{1,0:T(8,128)(2,1)S(1)} %copy-done, s32[]{:T(128)S(6)} %select_n.58), kind=kOutput, calls=%fused_computation.16 | convolution fusion | flops 201375744 | bytes 2490372 | tf_op jit(solution)/shard_map/dot_general | solution.py:11
  67.1 3.3 %collective-permute-start.21 = (bf16[384,128]{0,1:T(8,128)(2,1)S(1)}, bf16[384,128]{0,1:T(8,128)(2,1)S(1)}, u32[]{:S(2)}, u32[]{:S(2)}) collective-permute-start(bf16[384,128]{0,1:T(8,128)(2,1)S(1)} %get-tuple-element.11), channel_id=1, source_target_pairs={{0,3},{1,2},{2,1},{3,0},{4,7},{5,6},{6,5},{7,4},{8,11},{9,10},{10,... | collective-permute-start | bytes 294920 | tf_op jit(solution)/shard_map/ppermute | solution.py:26
  70.4 0.6 fusion.7
  71.0 0.4 collective-permute-start.19
  71.5 1.6 %fusion.8 = f32[1,384,128]{1,2,0:T(8,128)S(1)} fusion(f32[384,128]{0,1:T(8,128)S(1)} %collective-permute-done.6, bf16[2048,128]{1,0:T(8,128)(2,1)} %collective-permute-done.5, bf16[384,4096]{1,0:T(8,128)(2,1)S(1)} %copy-done, s32[]{:T(128)S(6)} %select_n.58), kind=kOutput, calls=%fused_computation.20 | convolution fusion | flops 201375744 | bytes 2490372 | tf_op jit(solution)/shard_map/dot_general | solution.py:11
  73.1 1.6 %fusion.9 = f32[1,384,128]{1,2,0:T(8,128)S(1)} fusion(f32[384,128]{0,1:T(8,128)S(1)} %collective-permute-done.4, bf16[2048,128]{1,0:T(8,128)(2,1)} %collective-permute-done.3, bf16[384,4096]{1,0:T(8,128)(2,1)S(1)} %copy-done, s32[]{:T(128)S(6)} %select_n.58), kind=kOutput, calls=%fused_computation.22 | convolution fusion | flops 201375744 | bytes 2490372 | tf_op jit(solution)/shard_map/dot_general | solution.py:11
  74.8 0.6 fusion.10
  75.5 3.2 %collective-permute-start.11 = (bf16[384,128]{0,1:T(8,128)(2,1)S(1)}, bf16[384,128]{0,1:T(8,128)(2,1)S(1)}, u32[]{:S(2)}, u32[]{:S(2)}) collective-permute-start(bf16[384,128]{0,1:T(8,128)(2,1)S(1)} %get-tuple-element.8), channel_id=1, source_target_pairs={{0,3},{1,2},{2,1},{3,0},{4,7},{5,6},{6,5},{7,4},{8,11},{9,10},{10,... | collective-permute-start | bytes 294920 | tf_op jit(solution)/shard_map/ppermute | solution.py:26
  78.8 0.4 collective-permute-start.9
  79.3 1.6 %collective-permute-done.11 = bf16[384,128]{0,1:T(8,128)(2,1)S(1)} collective-permute-done((bf16[384,128]{0,1:T(8,128)(2,1)S(1)}, bf16[384,128]{0,1:T(8,128)(2,1)S(1)}, u32[]{:S(2)}, u32[]{:S(2)}) %collective-permute-start.11) | collective-permute-done | bytes 98336 | tf_op jit(solution)/shard_map/ppermute | solution.py:26
  80.9 5.8 %collective-permute-done.10 = bf16[384,128]{0,1:T(8,128)(2,1)S(1)} collective-permute-done((bf16[384,128]{0,1:T(8,128)(2,1)S(1)}, bf16[384,128]{0,1:T(8,128)(2,1)S(1)}, u32[]{:S(2)}, u32[]{:S(2)}) %collective-permute-start.10) | collective-permute-done | bytes 98336 | tf_op jit(solution)/shard_map/ppermute | solution.py:26
  86.8 0.2 fusion.45
  87.0 0.3 fusion.29
  87.3 0.2 convolution_convert_fusion.4
  87.5 0.2 convolution_add_fusion.11
  87.8 4.4 %collective-permute-start.24 = (f32[128,256]{1,0:T(8,128)S(1)}, f32[128,256]{1,0:T(8,128)S(1)}, u32[]{:S(2)}, u32[]{:S(2)}) collective-permute-start(f32[128,256]{1,0:T(8,128)S(1)} %convolution_add_fusion.11), channel_id=1, source_target_pairs={{0,4},{4,8},{8,12},{12,16},{16,20},{20,24},{24,28},{1,5},{5,9},{9,... | collective-permute-start | bytes 393224 | tf_op jit(solution)/shard_map/ppermute | solution.py:22
  92.1 0.3 fusion.69
  92.4 0.3 convolution_add_fusion.1
  92.7 1.9 %collective-permute-start.23 = (bf16[128,256]{1,0:T(8,128)(2,1)S(1)}, bf16[128,256]{1,0:T(8,128)(2,1)S(1)}, u32[]{:S(2)}, u32[]{:S(2)}) collective-permute-start(bf16[128,256]{1,0:T(8,128)(2,1)S(1)} %convolution_convert_fusion.4), channel_id=1, source_target_pairs={{4,0},{8,4},{12,8},{16,12},{20,16},{24,20},{28,24},{5,1},{9,5},{13... | collective-permute-start | bytes 196616 | tf_op jit(solution)/shard_map/ppermute | solution.py:22
  94.7 0.3 fusion.1
  95.0 0.3 fusion.36
  95.3 0.3 fusion.35
  95.7 2.7 %collective-permute-done.23 = bf16[128,256]{1,0:T(8,128)(2,1)S(1)} collective-permute-done((bf16[128,256]{1,0:T(8,128)(2,1)S(1)}, bf16[128,256]{1,0:T(8,128)(2,1)S(1)}, u32[]{:S(2)}, u32[]{:S(2)}) %collective-permute-start.23) | collective-permute-done | bytes 65568 | tf_op jit(solution)/shard_map/ppermute | solution.py:22
  98.3 0.9 fusion.2
  (39 shorter events, 0.6 us)
Async XLA Ops:
  0.0 10.3 %copy-start = (bf16[384,4096]{1,0:T(8,128)(2,1)S(1)}, bf16[384,4096]{1,0:T(8,128)(2,1)}, u32[]{:S(2)}) copy-start(bf16[384,4096]{1,0:T(8,128)(2,1)} %param.5) | copy-start | bytes 9437188
  2.0 2.3 %collective-permute-start = (bf16[2048,128]{1,0:T(8,128)(2,1)}, bf16[2048,128]{1,0:T(8,128)(2,1)}, u32[]{:S(2)}, u32[]{:S(2)}) collective-permute-start(bf16[2048,128]{1,0:T(8,128)(2,1)} %constant_dynamic-slice_fusion.1), channel_id=1, source_target_pairs={{0,4},{4,0},{8,12},{12,8},{16,20},{20,16},{24,28},{28,24},{1,5},{5... | collective-permute-start | bytes 1572872 | tf_op jit(solution)/shard_map/ppermute | solution.py:26
  6.7 5.8 %copy-start.4 = (s32[1,512]{1,0:T(1,128)S(1)}, s32[1,512]{1,0:T(1,128)}, u32[]{:S(2)}) copy-start(s32[1,512]{1,0:T(1,128)} %param.8) | copy-start | bytes 6148
  6.7 14.7 %collective-permute-start.13 = (bf16[2048,128]{1,0:T(8,128)(2,1)}, bf16[2048,128]{1,0:T(8,128)(2,1)}, u32[]{:S(2)}, u32[]{:S(2)}) collective-permute-start(bf16[2048,128]{1,0:T(8,128)(2,1)} %get-tuple-element.6), channel_id=1, source_target_pairs={{0,8},{4,12},{8,0},{12,4},{16,24},{20,28},{24,16},{28,20},{1,9},{5... | collective-permute-start | bytes 1572872 | tf_op jit(solution)/shard_map/ppermute | solution.py:26
  9.0 13.5 %collective-permute-start.15 = (bf16[2048,128]{1,0:T(8,128)(2,1)}, bf16[2048,128]{1,0:T(8,128)(2,1)}, u32[]{:S(2)}, u32[]{:S(2)}) collective-permute-start(bf16[2048,128]{1,0:T(8,128)(2,1)} %get-tuple-element.6), channel_id=1, source_target_pairs={{0,16},{4,20},{8,24},{12,28},{16,0},{20,4},{24,8},{28,12},{1,17},{... | collective-permute-start | bytes 1572872 | tf_op jit(solution)/shard_map/ppermute | solution.py:26
  11.6 27.4 %collective-permute-start.1 = (bf16[384,2048]{1,0:T(8,128)(2,1)}, bf16[384,2048]{1,0:T(8,128)(2,1)}, u32[]{:S(2)}, u32[]{:S(2)}) collective-permute-start(bf16[384,2048]{1,0:T(8,128)(2,1)} %constant_dynamic-slice_fusion), channel_id=1, source_target_pairs={{0,4},{4,0},{8,12},{12,8},{16,20},{20,16},{24,28},{28,24},{1,5},{5... | collective-permute-start | bytes 4718600 | tf_op jit(solution)/shard_map/ppermute | solution.py:26
  15.4 10.3 %copy-start.3 = (s32[128]{0:T(128)S(1)}, s32[128]{0:T(128)}, u32[]{:S(2)}) copy-start(s32[128]{0:T(128)} %param.9) | copy-start | bytes 1540
  16.1 9.5 %collective-permute-start.22 = (bf16[128,128]{1,0:T(8,128)(2,1)S(1)}, bf16[128,128]{1,0:T(8,128)(2,1)S(1)}, u32[]{:S(2)}, u32[]{:S(2)}) collective-permute-start(bf16[128,128]{1,0:T(8,128)(2,1)S(1)} %slice.17), channel_id=1, source_target_pairs={{0,4},{4,8},{8,12},{12,16},{16,20},{20,24},{24,28},{1,5},{5,9},{9,... | collective-permute-start | bytes 98312 | tf_op jit(solution)/shard_map/ppermute | solution.py:22
  18.2 15.0 %collective-permute-start.3 = (bf16[2048,128]{1,0:T(8,128)(2,1)}, bf16[2048,128]{1,0:T(8,128)(2,1)}, u32[]{:S(2)}, u32[]{:S(2)}) collective-permute-start(bf16[2048,128]{1,0:T(8,128)(2,1)} %get-tuple-element.5), channel_id=1, source_target_pairs={{0,8},{4,12},{8,0},{12,4},{16,24},{20,28},{24,16},{28,20},{1,9},{5... | collective-permute-start | bytes 1572872 | tf_op jit(solution)/shard_map/ppermute | solution.py:26
  21.3 12.3 %collective-permute-start.5 = (bf16[2048,128]{1,0:T(8,128)(2,1)}, bf16[2048,128]{1,0:T(8,128)(2,1)}, u32[]{:S(2)}, u32[]{:S(2)}) collective-permute-start(bf16[2048,128]{1,0:T(8,128)(2,1)} %get-tuple-element.5), channel_id=1, source_target_pairs={{0,16},{4,20},{8,24},{12,28},{16,0},{20,4},{24,8},{28,12},{1,17},{... | collective-permute-start | bytes 1572872 | tf_op jit(solution)/shard_map/ppermute | solution.py:26
  24.4 14.6 %collective-permute-start.17 = (bf16[2048,128]{1,0:T(8,128)(2,1)}, bf16[2048,128]{1,0:T(8,128)(2,1)}, u32[]{:S(2)}, u32[]{:S(2)}) collective-permute-start(bf16[2048,128]{1,0:T(8,128)(2,1)} %broadcast_select_fusion), channel_id=1, source_target_pairs={{0,16},{4,12},{8,24},{12,4},{16,0},{20,28},{24,8},{28,20},{1,17},{... | collective-permute-start | bytes 1572872 | tf_op jit(solution)/shard_map/ppermute | solution.py:42
  34.7 16.1 %collective-permute-start.7 = (bf16[2048,128]{1,0:T(8,128)(2,1)S(1)}, bf16[2048,128]{1,0:T(8,128)(2,1)S(1)}, u32[]{:S(2)}, u32[]{:S(2)}) collective-permute-start(bf16[2048,128]{1,0:T(8,128)(2,1)S(1)} %broadcast_select_fusion.2), channel_id=1, source_target_pairs={{0,16},{4,12},{8,24},{12,4},{16,0},{20,28},{24,8},{28,20},{1,17},{... | collective-permute-start | bytes 1572872 | tf_op jit(solution)/shard_map/ppermute | solution.py:42
  41.1 18.5 %collective-permute-start.18 = (f32[384,128]{0,1:T(8,128)S(1)}, f32[384,128]{0,1:T(8,128)S(1)}, u32[]{:S(2)}, u32[]{:S(2)}) collective-permute-start(f32[384,128]{0,1:T(8,128)S(1)} %fusion.68), channel_id=1, source_target_pairs={{0,4},{4,0},{8,12},{12,8},{16,20},{20,16},{24,28},{28,24},{1,5},{5... | collective-permute-start | bytes 589832 | tf_op jit(solution)/shard_map/ppermute | solution.py:26
  45.9 15.5 %collective-permute-start.16 = (f32[384,128]{0,1:T(8,128)S(1)}, f32[384,128]{0,1:T(8,128)S(1)}, u32[]{:S(2)}, u32[]{:S(2)}) collective-permute-start(f32[384,128]{0,1:T(8,128)S(1)} %fusion.67), channel_id=1, source_target_pairs={{0,4},{4,0},{8,12},{12,8},{16,20},{20,16},{24,28},{28,24},{1,5},{5... | collective-permute-start | bytes 589832 | tf_op jit(solution)/shard_map/ppermute | solution.py:26
  48.1 15.5 %collective-permute-start.14 = (f32[384,128]{0,1:T(8,128)S(1)}, f32[384,128]{0,1:T(8,128)S(1)}, u32[]{:S(2)}, u32[]{:S(2)}) collective-permute-start(f32[384,128]{0,1:T(8,128)S(1)} %fusion.66), channel_id=1, source_target_pairs={{0,4},{4,0},{8,12},{12,8},{16,20},{20,16},{24,28},{28,24},{1,5},{5... | collective-permute-start | bytes 589832 | tf_op jit(solution)/shard_map/ppermute | solution.py:26
  50.7 14.6 %collective-permute-start.12 = (f32[384,128]{0,1:T(8,128)S(1)}, f32[384,128]{0,1:T(8,128)S(1)}, u32[]{:S(2)}, u32[]{:S(2)}) collective-permute-start(f32[384,128]{0,1:T(8,128)S(1)} %fusion.65), channel_id=1, source_target_pairs={{0,4},{4,0},{8,12},{12,8},{16,20},{20,16},{24,28},{28,24},{1,5},{5... | collective-permute-start | bytes 589832 | tf_op jit(solution)/shard_map/ppermute | solution.py:26
  52.8 17.6 %collective-permute-start.8 = (f32[384,128]{0,1:T(8,128)S(1)}, f32[384,128]{0,1:T(8,128)S(1)}, u32[]{:S(2)}, u32[]{:S(2)}) collective-permute-start(f32[384,128]{0,1:T(8,128)S(1)} %fusion.64), channel_id=1, source_target_pairs={{0,4},{4,0},{8,12},{12,8},{16,20},{20,16},{24,28},{28,24},{1,5},{5... | collective-permute-start | bytes 589832 | tf_op jit(solution)/shard_map/ppermute | solution.py:26
  55.4 2.2 %copy-start.1 = (bf16[2048,128]{1,0:T(8,128)(2,1)S(1)}, bf16[2048,128]{1,0:T(8,128)(2,1)}, u32[]{:S(2)}) copy-start(bf16[2048,128]{1,0:T(8,128)(2,1)} %get-tuple-element.5) | copy-start | bytes 1572868
  59.6 11.4 %collective-permute-start.6 = (f32[384,128]{0,1:T(8,128)S(1)}, f32[384,128]{0,1:T(8,128)S(1)}, u32[]{:S(2)}, u32[]{:S(2)}) collective-permute-start(f32[384,128]{0,1:T(8,128)S(1)} %fusion.63), channel_id=1, source_target_pairs={{0,4},{4,0},{8,12},{12,8},{16,20},{20,16},{24,28},{28,24},{1,5},{5... | collective-permute-start | bytes 589832 | tf_op jit(solution)/shard_map/ppermute | solution.py:26
  61.4 11.8 %collective-permute-start.4 = (f32[384,128]{0,1:T(8,128)S(1)}, f32[384,128]{0,1:T(8,128)S(1)}, u32[]{:S(2)}, u32[]{:S(2)}) collective-permute-start(f32[384,128]{0,1:T(8,128)S(1)} %fusion.62), channel_id=1, source_target_pairs={{0,4},{4,0},{8,12},{12,8},{16,20},{20,16},{24,28},{28,24},{1,5},{5... | collective-permute-start | bytes 589832 | tf_op jit(solution)/shard_map/ppermute | solution.py:26
  63.5 11.2 %collective-permute-start.2 = (f32[384,128]{0,1:T(8,128)S(1)}, f32[384,128]{0,1:T(8,128)S(1)}, u32[]{:S(2)}, u32[]{:S(2)}) collective-permute-start(f32[384,128]{0,1:T(8,128)S(1)} %fusion.61), channel_id=1, source_target_pairs={{0,4},{4,0},{8,12},{12,8},{16,20},{20,16},{24,28},{28,24},{1,5},{5... | collective-permute-start | bytes 589832 | tf_op jit(solution)/shard_map/ppermute | solution.py:26
  67.1 11.7 %collective-permute-start.21 = (bf16[384,128]{0,1:T(8,128)(2,1)S(1)}, bf16[384,128]{0,1:T(8,128)(2,1)S(1)}, u32[]{:S(2)}, u32[]{:S(2)}) collective-permute-start(bf16[384,128]{0,1:T(8,128)(2,1)S(1)} %get-tuple-element.11), channel_id=1, source_target_pairs={{0,3},{1,2},{2,1},{3,0},{4,7},{5,6},{6,5},{7,4},{8,11},{9,10},{10,... | collective-permute-start | bytes 294920 | tf_op jit(solution)/shard_map/ppermute | solution.py:26
  70.4 8.8 %collective-permute-start.20 = (bf16[384,128]{0,1:T(8,128)(2,1)S(1)}, bf16[384,128]{0,1:T(8,128)(2,1)S(1)}, u32[]{:S(2)}, u32[]{:S(2)}) collective-permute-start(bf16[384,128]{0,1:T(8,128)(2,1)S(1)} %get-tuple-element.12), channel_id=1, source_target_pairs={{0,2},{1,3},{2,0},{3,1},{4,6},{5,7},{6,4},{7,5},{8,10},{9,11},{10,... | collective-permute-start | bytes 294920 | tf_op jit(solution)/shard_map/ppermute | solution.py:26
  71.0 8.2 %collective-permute-start.19 = (bf16[384,128]{0,1:T(8,128)(2,1)S(1)}, bf16[384,128]{0,1:T(8,128)(2,1)S(1)}, u32[]{:S(2)}, u32[]{:S(2)}) collective-permute-start(bf16[384,128]{0,1:T(8,128)(2,1)S(1)} %get-tuple-element.10), channel_id=1, source_target_pairs={{0,1},{1,0},{2,3},{3,2},{4,5},{5,4},{6,7},{7,6},{8,9},{9,8},{10,11... | collective-permute-start | bytes 294920 | tf_op jit(solution)/shard_map/ppermute | solution.py:26
  75.5 5.4 %collective-permute-start.11 = (bf16[384,128]{0,1:T(8,128)(2,1)S(1)}, bf16[384,128]{0,1:T(8,128)(2,1)S(1)}, u32[]{:S(2)}, u32[]{:S(2)}) collective-permute-start(bf16[384,128]{0,1:T(8,128)(2,1)S(1)} %get-tuple-element.8), channel_id=1, source_target_pairs={{0,3},{1,2},{2,1},{3,0},{4,7},{5,6},{6,5},{7,4},{8,11},{9,10},{10,... | collective-permute-start | bytes 294920 | tf_op jit(solution)/shard_map/ppermute | solution.py:26
  78.7 8.1 %copy-start.2 = (bf16[512,512]{1,0:T(8,128)(2,1)S(1)}, bf16[512,512]{1,0:T(8,128)(2,1)}, u32[]{:S(2)}) copy-start(bf16[512,512]{1,0:T(8,128)(2,1)} %convolution_convert_fusion) | copy-start | bytes 1572868
  78.7 8.0 %collective-permute-start.10 = (bf16[384,128]{0,1:T(8,128)(2,1)S(1)}, bf16[384,128]{0,1:T(8,128)(2,1)S(1)}, u32[]{:S(2)}, u32[]{:S(2)}) collective-permute-start(bf16[384,128]{0,1:T(8,128)(2,1)S(1)} %get-tuple-element.9), channel_id=1, source_target_pairs={{0,2},{1,3},{2,0},{3,1},{4,6},{5,7},{6,4},{7,5},{8,10},{9,11},{10,... | collective-permute-start | bytes 294920 | tf_op jit(solution)/shard_map/ppermute | solution.py:26
  78.8 7.9 %collective-permute-start.9 = (bf16[384,128]{0,1:T(8,128)(2,1)S(1)}, bf16[384,128]{0,1:T(8,128)(2,1)S(1)}, u32[]{:S(2)}, u32[]{:S(2)}) collective-permute-start(bf16[384,128]{0,1:T(8,128)(2,1)S(1)} %get-tuple-element.7), channel_id=1, source_target_pairs={{0,1},{1,0},{2,3},{3,2},{4,5},{5,4},{6,7},{7,6},{8,9},{9,8},{10,11... | collective-permute-start | bytes 294920 | tf_op jit(solution)/shard_map/ppermute | solution.py:26
  87.8 7.2 %collective-permute-start.24 = (f32[128,256]{1,0:T(8,128)S(1)}, f32[128,256]{1,0:T(8,128)S(1)}, u32[]{:S(2)}, u32[]{:S(2)}) collective-permute-start(f32[128,256]{1,0:T(8,128)S(1)} %convolution_add_fusion.11), channel_id=1, source_target_pairs={{0,4},{4,8},{8,12},{12,16},{16,20},{20,24},{24,28},{1,5},{5,9},{9,... | collective-permute-start | bytes 393224 | tf_op jit(solution)/shard_map/ppermute | solution.py:22
  92.7 5.6 %collective-permute-start.23 = (bf16[128,256]{1,0:T(8,128)(2,1)S(1)}, bf16[128,256]{1,0:T(8,128)(2,1)S(1)}, u32[]{:S(2)}, u32[]{:S(2)}) collective-permute-start(bf16[128,256]{1,0:T(8,128)(2,1)S(1)} %convolution_convert_fusion.4), channel_id=1, source_target_pairs={{4,0},{8,4},{12,8},{16,12},{20,16},{24,20},{28,24},{5,1},{9,5},{13... | collective-permute-start | bytes 196616 | tf_op jit(solution)/shard_map/ppermute | solution.py:22

commit v3 on v0

v3 whole, which is shorter than its diff:
```python
import functools

import jax
import jax.numpy as jnp
from jax import lax
from jax.experimental import pallas as pl
from jax.experimental.pallas import tpu as pltpu
from jax.sharding import PartitionSpec as P

CORE, NEAR, FAR = 1, 2, 4
VMEM = pl.BlockSpec(memory_space=pltpu.VMEM)
ANY = pl.BlockSpec(memory_space=pl.ANY)
SMEM = pl.BlockSpec(memory_space=pltpu.SMEM)
F32, BF16 = jnp.float32, jnp.bfloat16


def dot(left, right):
    precision = lax.Precision.HIGHEST if left.dtype == F32 else None
    return jnp.dot(left, right, precision=precision, preferred_element_type=F32)


def split(value):
    high = value.astype(BF16)
    return high, (value - high.astype(F32)).astype(BF16)


def shifted(value, axis, steps):
    count = lax.axis_size(axis)
    leading, last = (max(0, -steps), min(count, count - steps))
    return lax.ppermute(value, axis, [(source, source + steps) for source in range(leading, last)])


def exchanged(value, axis, mask, core=None):
    sources = range(lax.axis_size(axis))
    return lax.ppermute(value, axis, [(source, source ^ mask) for source in sources if core in (None, source & CORE)])


def call(kernel, outs, operands, flops=0, scalars=1, after=(), space=VMEM, scratch=()):
    size = sum(value.size * value.dtype.itemsize for value in (*operands, *outs))
    count = len(operands)

    def body(*refs):
        kernel(*refs[:count], *refs[count + len(after) :])

    return pl.pallas_call(
        body,
        out_shape=outs,
        in_specs=[SMEM] * scalars + [space] * (count - scalars) + [ANY] * len(after),
        out_specs=[VMEM] * len(outs),
        scratch_shapes=list(scratch),
        cost_estimate=pl.CostEstimate(flops=flops, bytes_accessed=size, transcendentals=0),
        compiler_params=pltpu.CompilerParams(vmem_limit_bytes=48 * 2**20),
    )(*operands, *after)


def shape(*dims, dtype=F32):
    return jax.ShapeDtypeStruct(dims, dtype)


def shard_kernel(side, place, own, other, out, done):
    half = out.shape[0]

    def fill(source):
        start = pl.multiple_of(place[0] * half, half)
        copy = pltpu.make_async_copy(source.at[pl.ds(start, half)], out, done)
        copy.start()
        copy.wait()

    pl.when(place[0] == side)(lambda: fill(own))
    pl.when(place[0] != side)(lambda: fill(other))


def product(states, place, piece):
    half = piece.shape[0]
    start = pl.multiple_of(place[0] * half, half)
    return jnp.dot(states[:, pl.ds(start, half)], piece[...], preferred_element_type=F32)


def early_kernel(count, place, states, *refs):
    pieces, out = refs[:count], refs[count]
    for slot, piece in enumerate(pieces):
        out[slot] = product(states, place, piece)


def late_kernel(place, states, even, odd, out):
    @pl.when(place[0] == 0)
    def _():
        out[...] = product(states, place, even)

    @pl.when(place[0] == 1)
    def _():
        out[...] = product(states, place, odd)


def pick_kernel(count, place, early, late, early_other, late_other, kept, *sent):
    where = place[1]
    last = early.shape[0]

    def store(slot, out):
        @pl.when(slot < last)
        def _():
            out[...] = (early[jnp.minimum(slot, last - 1)] + early_other[jnp.minimum(slot, last - 1)]).astype(out.dtype)

        @pl.when(slot == last)
        def _():
            out[...] = (late[...] + late_other[...]).astype(out.dtype)

    store(where, kept)
    for mask, out in zip(range(1, count), sent):
        store(where ^ mask, out)


def rotate_square(wavefunctions, rotation, operator):
    domain, band = lax.axis_index("domain"), lax.axis_index("band")
    bands = lax.axis_size("band")
    place = jnp.stack([domain % 2, (domain // 2) ^ band])
    rows, states = wavefunctions.shape
    width = rotation.shape[1]
    half = states // 2
    flops = 2 * rows * half * width
    swapped = exchanged(rotation, "domain", CORE)

    def shard(side, after):
        kernel, outs = functools.partial(shard_kernel, side), [shape(half, width, dtype=BF16)]
        scratch = (pltpu.SemaphoreType.DMA,)
        return call(kernel, outs, (place, rotation, swapped), after=after, space=ANY, scratch=scratch)[0]

    def early(who, pieces, after=()):
        count = len(pieces)
        kernel = functools.partial(early_kernel, count)
        return call(kernel, [shape(count, rows, width)], (place, who, *pieces), count * flops, after=after)[0]

    def late(who, even, odd, after=()):
        return call(late_kernel, [shape(rows, width)], (place, who, even, odd), flops, after=after)[0]

    def picked(early_mine, late_mine, early_other, late_other):
        outs = [shape(rows, width)] + [shape(rows, width, dtype=BF16)] * (bands - 1)
        return call(
            functools.partial(pick_kernel, bands), outs, (place, early_mine, late_mine, early_other, late_other)
        )

    def spread(kept, *sent):
        return [kept] + [exchanged(value, "band", mask) for mask, value in zip(range(1, bands), sent)]

    def gathered(piece):
        return exchanged(piece, "domain", NEAR), exchanged(piece, "domain", FAR)

    def forwarded(near, far):
        return exchanged(near, "domain", FAR, 0), exchanged(far, "domain", NEAR, CORE)

    left = shard(0, ())
    near, far = gathered(left)
    other, left = lax.optimization_barrier((wavefunctions, left))
    theirs = exchanged(other, "domain", CORE)
    assembled, pick, returned = operator()
    near, far, returned = lax.optimization_barrier((near, far, returned))
    even, odd = forwarded(near, far)
    early_theirs = early(theirs, (left, near, far))
    early_other = exchanged(early_theirs, "domain", CORE)
    right = shard(1, (early_theirs,))
    right_near, right_far = gathered(right)
    early_mine = early(wavefunctions, (left, near, far), (right,))
    late_theirs = late(theirs, even, odd)
    late_other = exchanged(late_theirs, "domain", CORE)
    late_mine = late(wavefunctions, even, odd, (late_theirs,))
    left_out = picked(early_mine, late_mine, early_other, late_other)
    left_parts = spread(*left_out)

    right_near, right_far, sent = lax.optimization_barrier((right_near, right_far, left_out[1]))
    even, odd = forwarded(right_near, right_far)
    early_theirs = early(theirs, (right, right_near, right_far), (sent,))
    early_other = exchanged(early_theirs, "domain", CORE)
    early_mine = early(wavefunctions, (right, right_near, right_far), (early_theirs,))
    late_theirs = late(theirs, even, odd)
    late_other = exchanged(late_theirs, "domain", CORE)
    late_mine = late(wavefunctions, even, odd, (late_theirs,))
    right_parts = spread(*picked(early_mine, late_mine, early_other, late_other))
    return (left_parts, right_parts), (assembled, pick, returned)


def rotate_any(wavefunctions, rotation):
    columns = lax.all_gather(rotation, "domain", axis=1, tiled=True)
    return lax.psum_scatter(dot(wavefunctions, columns), "band", scatter_dimension=1, tiled=True)


def faces_kernel(count, width, *refs):
    parts, (assembled, pick, total, faces, back) = refs[: 2 * count], refs[2 * count :]
    own = total.shape[0]
    for side in range(2):
        some = parts[side * count : (side + 1) * count]
        value = some[0][...]
        for part in some[1:]:
            value = value + part[...].astype(F32)
        columns = slice(side * width, (side + 1) * width)
        total[:, columns] = value
        high, low = split(value)
        faces[:, columns] = dot(pick[...], high).astype(BF16)
        outward = assembled[own:, :own]
        back[:, columns] = dot(outward, high) + dot(outward, low)


def inner_kernel(total, assembled, returned, out):
    own = total.shape[0]
    high, low = split(total[...])
    inner = assembled[:own, :own]
    out[...] = dot(inner, high) + dot(inner, low) + dot(returned[...], high) + dot(returned[...], low)


def final_kernel(inner, assembled, spread, incoming, back, out):
    own = inner.shape[0]
    high, low = split(back[...])
    out[...] = inner[...] + dot(assembled[:own, own:], incoming[...]) + dot(spread[...], high) + dot(spread[...], low)


def finish_square(parts, operator):
    (left, right), (assembled, pick, returned) = parts, operator
    rows, width = left[0].shape
    faces_count = pick.shape[0]
    columns = 2 * width
    total, faces, back = call(
        functools.partial(faces_kernel, len(left), width),
        [shape(rows, columns), shape(faces_count, columns, dtype=BF16), shape(faces_count, columns)],
        (*left, *right, assembled, pick),
        scalars=0,
    )
    incoming, back = shifted(faces, "domain", -1), shifted(back, "domain", 1)
    inner = call(inner_kernel, [shape(rows, columns)], (total, assembled, returned), 8 * rows * rows * columns, scalars=0)[0]
    return call(final_kernel, [shape(rows, columns)], (inner, assembled, pick.T, incoming, back), scalars=0)[0]


def finish_any(rotated, assembled, pick, returned):
    own = rotated.shape[0]
    rotated = rotated.astype(BF16).astype(assembled.dtype)
    incoming = shifted(dot(pick, rotated).astype(BF16), "domain", -1).astype(assembled.dtype)
    back = shifted(dot(assembled[own:, :own], rotated), "domain", 1)
    inner = dot(assembled[:own, :own], rotated) + dot(returned, rotated) + dot(assembled[:own, own:], incoming)
    return inner + dot(pick.T.astype(F32), back)


def assemble(cell_matrices, cell_nodes, face_map, own):
    cells = cell_nodes.shape[0]
    extent = own + face_map.shape[0]
    held = BF16 if cells == 1 else F32
    places = jax.nn.one_hot(cell_nodes, extent, dtype=held)
    assembled = jnp.zeros((extent, extent), F32)
    for cell in range(cells):
        rows = dot(places[cell].T, cell_matrices[cell].astype(held)).astype(held)
        assembled = assembled + dot(rows, places[cell])
    assembled = assembled.astype(held)
    pick = jax.nn.one_hot(face_map, own, dtype=held)
    corner = shifted(assembled[own:, own:], "domain", 1)
    returned = dot(dot(pick.T, corner).astype(held), pick).astype(held)
    return assembled, pick, returned


def local(wavefunctions, rotation, cell_matrices, cell_nodes, face_map):
    operator = functools.partial(assemble, cell_matrices, cell_nodes, face_map, wavefunctions.shape[0])
    chips = lax.axis_size("domain") // 2
    if chips == FAR and chips == lax.axis_size("band") and cell_nodes.shape[0] == 1:
        return finish_square(*rotate_square(wavefunctions, rotation, operator))
    return finish_any(rotate_any(wavefunctions, rotation), *operator())


def solution(mesh):
    in_specs = (
        P("domain", "band"),
        P("band", "domain"),
        P("domain", None, None),
        P("domain", None),
        P("domain"),
    )
    out_specs = P("domain", "band")
    return jax.shard_map(local, mesh=mesh, in_specs=in_specs, out_specs=out_specs, check_vma=False)
```

time: 146 us -> 89.8 us (0.62)
  the two profiles are of different devices: /device:TPU:1 before, /device:TPU:20 now
where the time goes in v3:
time: 89.8 us; the launch traced here: 89.4 us
  waiting for transfers between devices  36.5 us (41%)
  starting transfers between devices  26.1 us (29%)
  Pallas kernels  22.7 us (25%)
  matrix products  2.23 us (2%)
  local copies, waits for them, and re-layouts  1.26 us (1%)
    ppermute x20, waiting for transfers between devices, exchanged(): lax.ppermute(value, axis, [(source, source ^ mask) for source in sources...  23.4 us
    pallas_call x15, Pallas kernels, call(): pl.pallas_call(body, out_shape=outs, in_specs=[SMEM] * scalars + [space]...  22.7 us
    ppermute x20, starting transfers between devices, exchanged(): lax.ppermute(value, axis, [(source, source ^ mask) for source in sources...  19.2 us
    ppermute x3, waiting for transfers between devices, shifted(): lax.ppermute(value, axis, [(source, source + steps) for source in range(l...  13.1 us
    ppermute x3, starting transfers between devices, shifted(): lax.ppermute(value, axis, [(source, source + steps) for source in range(l...  6.83 us
    dot_general x2, matrix products, dot(): return jnp.dot(left, right, precision=precision, preferred_element_type=F32)  2.23 us
  transfers between devices with their start and end apart: 23, of which 10 were waited for; matrix products, arithmetic and copies ran while one was open for 3% of the time, Pallas kernels for 23%

profile of v3, /device:TPU:20, one launch (start us, length us, event | category | flops | bytes accessed | tf_op | source)
XLA Modules:
  0.0 89.4 jit_solution(12044014227250760705)
XLA Ops:
  0.0 0.0 collective-permute-start
  0.0 0.1 pad_add_fusion.refs_0_
  0.1 2.8 %collective-permute-done.refs_2_ = bf16[4096,128]{1,0:T(8,128)(2,1)S(1)} collective-permute-done((bf16[4096,128]{1,0:T(8,128)(2,1)}, bf16[4096,128]{1,0:T(8,128)(2,1)S(1)}, u32[]{:S(2)}, u32[]{:S(2)}) %collective-permute-start) | collective-permute-done | bytes 1048608 | tf_op jit(solution)/shard_map/ppermute | solution.py:35
  2.9 1.2 %copy-done.2 = bf16[4096,128]{1,0:T(8,128)(2,1)S(1)} copy-done((bf16[4096,128]{1,0:T(8,128)(2,1)S(1)}, bf16[4096,128]{1,0:T(8,128)(2,1)}, u32[]{:S(2)}) %copy-start.2) | copy-done | bytes 1048600
  4.1 0.6 shard_map.58.refs_2_
  4.7 0.2 collective-permute-start.4
  4.9 1.5 %collective-permute-start.1 = (bf16[2048,128]{1,0:T(8,128)(2,1)S(1)}, bf16[2048,128]{1,0:T(8,128)(2,1)S(1)}, u32[]{:S(2)}, u32[]{:S(2)}) collective-permute-start(bf16[2048,128]{1,0:T(8,128)(2,1)S(1)} %shard_map.58.refs_2_), channel_id=1, source_target_pairs={{0,8},{4,12},{8,0},{12,4},{16,24},{20,28},{24,16},{28,20},{1,9},{5... | collective-permute-start | bytes 1572872 | tf_op jit(solution)/shard_map/ppermute | solution.py:35
  6.4 0.5 collective-permute-start.2
  6.9 1.7 %convolution_convert_fusion.refs_8_.refs_1_ = bf16[512,512]{1,0:T(8,128)(2,1)S(1)} fusion(bf16[1,512,512]{2,1,0:T(8,128)(2,1)S(1)} %copy-done, s32[512]{0:T(512)} %bitcast.12), kind=kOutput, calls=%fused_computation | convolution fusion | flops 537919488 | bytes 1050624 | tf_op jit(solution)/shard_map/dot_general | solution.py:19
  8.7 0.0 copy-start.3
  8.7 2.1 %collective-permute-start.3 = (bf16[128,128]{1,0:T(8,128)(2,1)S(1)}, bf16[128,128]{1,0:T(8,128)(2,1)S(1)}, u32[]{:S(2)}, u32[]{:S(2)}) collective-permute-start(bf16[128,128]{1,0:T(8,128)(2,1)S(1)} %slice.4), channel_id=1, source_target_pairs={{0,4},{4,8},{8,12},{12,16},{16,20},{20,24},{24,28},{1,5},{5,9},{9,... | collective-permute-start | bytes 98312 | tf_op jit(solution)/shard_map/ppermute | solution.py:30
  10.8 8.4 %collective-permute-done.3 = bf16[128,128]{1,0:T(8,128)(2,1)S(1)} collective-permute-done((bf16[128,128]{1,0:T(8,128)(2,1)S(1)}, bf16[128,128]{1,0:T(8,128)(2,1)S(1)}, u32[]{:S(2)}, u32[]{:S(2)}) %collective-permute-start.3) | collective-permute-done | bytes 32800 | tf_op jit(solution)/shard_map/ppermute | solution.py:30
  19.2 0.5 convolution_convert_fusion.2.refs_2_
  19.7 1.1 %collective-permute-done.2.refs_4_ = bf16[2048,128]{1,0:T(8,128)(2,1)} collective-permute-done((bf16[2048,128]{1,0:T(8,128)(2,1)S(1)}, bf16[2048,128]{1,0:T(8,128)(2,1)}, u32[]{:S(2)}, u32[]{:S(2)}) %collective-permute-start.2) | collective-permute-done | bytes 524320 | tf_op jit(solution)/shard_map/ppermute | solution.py:35
  20.8 2.1 %collective-permute-start.5 = (bf16[2048,128]{1,0:T(8,128)(2,1)S(1)}, bf16[2048,128]{1,0:T(8,128)(2,1)S(1)}, u32[]{:S(2)}, u32[]{:S(2)}) collective-permute-start(bf16[2048,128]{1,0:T(8,128)(2,1)S(1)} %collective-permute-done.1.refs_3_), channel_id=1, source_target_pairs={{0,16},{8,24},{16,0},{24,8},{1,17},{9,25},{17,1},{25,9},{2,18},{10... | collective-permute-start | bytes 1572872 | tf_op jit(solution)/shard_map/ppermute | solution.py:35
  22.8 0.7 collective-permute-start.6
  23.6 3.4 %shard_map.59.refs_3_ = f32[3,384,128]{2,1,0:T(8,128)S(1)} custom-call(s32[2]{0:T(128)S(1)} %pad_add_fusion.refs_0_, bf16[384,4096]{1,0:T(8,128)(2,1)} %collective-permute-done.4.refs_1_, bf16[2048,128]{1,0:T(8,128)(2,1)S(1)} %shard_map.58.refs_2_, bf16[2048,128]{1,0:T(8,128)(2,1)S(1)} %collective-permute-done.1.refs_3_, ...), custom_call_target="tpu_custom_call" | custom-call | flops 603979776 | bytes 5308424 | tf_op jit(solution)/shard_map/pallas_call | solution.py:45
  26.9 0.0 copy-start.1
  27.0 0.1 collective-permute-start.7
  27.0 0.6 shard_map.60.refs_5_.refs_2_
  27.7 1.1 %collective-permute-start.12 = (bf16[2048,128]{1,0:T(8,128)(2,1)S(1)}, bf16[2048,128]{1,0:T(8,128)(2,1)S(1)}, u32[]{:S(2)}, u32[]{:S(2)}) collective-permute-start(bf16[2048,128]{1,0:T(8,128)(2,1)S(1)} %shard_map.60.refs_5_.refs_2_), channel_id=1, source_target_pairs={{0,8},{4,12},{8,0},{12,4},{16,24},{20,28},{24,16},{28,20},{1,9},{5... | collective-permute-start | bytes 1572872 | tf_op jit(solution)/shard_map/ppermute | solution.py:35
  28.7 1.5 %collective-permute-start.13 = (bf16[2048,128]{1,0:T(8,128)(2,1)S(1)}, bf16[2048,128]{1,0:T(8,128)(2,1)S(1)}, u32[]{:S(2)}, u32[]{:S(2)}) collective-permute-start(bf16[2048,128]{1,0:T(8,128)(2,1)S(1)} %shard_map.60.refs_5_.refs_2_), channel_id=1, source_target_pairs={{0,16},{4,20},{8,24},{12,28},{16,0},{20,4},{24,8},{28,12},{1,17},{... | collective-permute-start | bytes 1572872 | tf_op jit(solution)/shard_map/ppermute | solution.py:35
  30.2 1.9 %collective-permute-done.5.refs_2_ = bf16[2048,128]{1,0:T(8,128)(2,1)S(1)} collective-permute-done((bf16[2048,128]{1,0:T(8,128)(2,1)S(1)}, bf16[2048,128]{1,0:T(8,128)(2,1)S(1)}, u32[]{:S(2)}, u32[]{:S(2)}) %collective-permute-start.5) | collective-permute-done | bytes 524320 | tf_op jit(solution)/shard_map/ppermute | solution.py:35
  32.1 0.0 collective-permute-done.6.refs_3_
  32.1 2.5 %shard_map.62.refs_4_ = f32[384,128]{1,0:T(8,128)S(1)} custom-call(s32[2]{0:T(128)S(1)} %pad_add_fusion.refs_0_, bf16[384,4096]{1,0:T(8,128)(2,1)} %collective-permute-done.4.refs_1_, bf16[2048,128]{1,0:T(8,128)(2,1)S(1)} %collective-permute-done.5.refs_2_, bf16[2048,128]{1,0:T(8,128)(2,1)S(1)} %collective-permute-done.6.refs_3_), custom_call_target="tpu_custom_call" | custom-call | flops 201326592 | bytes 4390920 | tf_op jit(solution)/shard_map/pallas_call | solution.py:45
  34.6 0.1 collective-permute-start.8
  34.7 1.1 %shard_map.63.refs_2_ = f32[384,128]{1,0:T(8,128)S(1)} custom-call(s32[2]{0:T(128)S(1)} %pad_add_fusion.refs_0_, bf16[384,4096]{1,0:T(8,128)(2,1)S(1)} %copy-done.1, bf16[2048,128]{1,0:T(8,128)(2,1)S(1)} %collective-permute-done.5.refs_2_, bf16[2048,128]{1,0:T(8,128)(2,1)S(1)} %collective-permute-done.6.refs_3_, f32[384,128]{1,0:T(8,128)S(1)} %shard_map.62.refs_4_), custom_call_target="tpu_custom_call" | custom-call | flops 201326592 | bytes 4390920 | tf_op jit(solution)/shard_map/pallas_call | solution.py:45
  35.8 2.4 %shard_map.61.refs_1_ = f32[3,384,128]{2,1,0:T(8,128)S(1)} custom-call(s32[2]{0:T(128)S(1)} %pad_add_fusion.refs_0_, bf16[384,4096]{1,0:T(8,128)(2,1)S(1)} %copy-done.1, bf16[2048,128]{1,0:T(8,128)(2,1)S(1)} %shard_map.58.refs_2_, bf16[2048,128]{1,0:T(8,128)(2,1)S(1)} %collective-permute-done.1.refs_3_, bf16[2048,128]{1,0:T(8,128)(2,1)} %collective-permute-done.2.refs_4_, ...), custom_call_target="tpu_custom_call" | custom-call | flops 603979776 | bytes 5308424 | tf_op jit(solution)/shard_map/pallas_call | solution.py:45
  38.3 0.0 collective-permute-done.8.refs_4_
  38.3 0.0 collective-permute-done.7.refs_3_
  38.3 0.7 shard_map.64
  39.0 3.3 %collective-permute-done.12.refs_3_ = bf16[2048,128]{1,0:T(8,128)(2,1)S(1)} collective-permute-done((bf16[2048,128]{1,0:T(8,128)(2,1)S(1)}, bf16[2048,128]{1,0:T(8,128)(2,1)S(1)}, u32[]{:S(2)}, u32[]{:S(2)}) %collective-permute-start.12) | collective-permute-done | bytes 524320 | tf_op jit(solution)/shard_map/ppermute | solution.py:35
  42.3 0.8 collective-permute-done.13.refs_4_
  43.1 3.1 %collective-permute-start.14 = (bf16[2048,128]{1,0:T(8,128)(2,1)S(1)}, bf16[2048,128]{1,0:T(8,128)(2,1)S(1)}, u32[]{:S(2)}, u32[]{:S(2)}) collective-permute-start(bf16[2048,128]{1,0:T(8,128)(2,1)S(1)} %collective-permute-done.12.refs_3_), channel_id=1, source_target_pairs={{0,16},{8,24},{16,0},{24,8},{1,17},{9,25},{17,1},{25,9},{2,18},{10... | collective-permute-start | bytes 1572872 | tf_op jit(solution)/shard_map/ppermute | solution.py:35
  46.2 0.7 collective-permute-start.15
  46.9 3.3 %shard_map.65.refs_5_ = f32[3,384,128]{2,1,0:T(8,128)S(1)} custom-call(s32[2]{0:T(128)S(1)} %pad_add_fusion.refs_0_, bf16[384,4096]{1,0:T(8,128)(2,1)} %collective-permute-done.4.refs_1_, bf16[2048,128]{1,0:T(8,128)(2,1)S(1)} %shard_map.60.refs_5_.refs_2_, bf16[2048,128]{1,0:T(8,128)(2,1)S(1)} %collective-permute-done.12.refs_3_, ...), custom_call_target="tpu_custom_call" | custom-call | flops 603979776 | bytes 5308424 | tf_op jit(solution)/shard_map/pallas_call | solution.py:45
  50.2 0.1 collective-permute-start.16
  50.2 3.9 %collective-permute-done.14.refs_2_ = bf16[2048,128]{1,0:T(8,128)(2,1)S(1)} collective-permute-done((bf16[2048,128]{1,0:T(8,128)(2,1)S(1)}, bf16[2048,128]{1,0:T(8,128)(2,1)S(1)}, u32[]{:S(2)}, u32[]{:S(2)}) %collective-permute-start.14) | collective-permute-done | bytes 524320 | tf_op jit(solution)/shard_map/ppermute | solution.py:35
  54.2 0.0 collective-permute-done.15.refs_3_
  54.2 2.5 %shard_map.67.refs_4_ = f32[384,128]{1,0:T(8,128)S(1)} custom-call(s32[2]{0:T(128)S(1)} %pad_add_fusion.refs_0_, bf16[384,4096]{1,0:T(8,128)(2,1)} %collective-permute-done.4.refs_1_, bf16[2048,128]{1,0:T(8,128)(2,1)S(1)} %collective-permute-done.14.refs_2_, bf16[2048,128]{1,0:T(8,128)(2,1)S(1)} %collective-permute-done.15.refs_3_), custom_call_target="tpu_custom_call" | custom-call | flops 201326592 | bytes 4390920 | tf_op jit(solution)/shard_map/pallas_call | solution.py:45
  56.6 0.1 collective-permute-start.17
  56.7 1.6 %collective-permute-start.9 = (bf16[384,128]{1,0:T(8,128)(2,1)S(1)}, bf16[384,128]{1,0:T(8,128)(2,1)S(1)}, u32[]{:S(2)}, u32[]{:S(2)}) collective-permute-start(bf16[384,128]{1,0:T(8,128)(2,1)S(1)} %get-tuple-element.34.refs_5_), channel_id=1, source_target_pairs={{0,1},{1,0},{2,3},{3,2},{4,5},{5,4},{6,7},{7,6},{8,9},{9,8},{10,11... | collective-permute-start | bytes 294920 | tf_op jit(solution)/shard_map/ppermute | solution.py:35
  58.4 0.3 collective-permute-start.10
  58.7 1.6 %collective-permute-start.11 = (bf16[384,128]{1,0:T(8,128)(2,1)S(1)}, bf16[384,128]{1,0:T(8,128)(2,1)S(1)}, u32[]{:S(2)}, u32[]{:S(2)}) collective-permute-start(bf16[384,128]{1,0:T(8,128)(2,1)S(1)} %get-tuple-element.31), channel_id=1, source_target_pairs={{0,3},{1,2},{2,1},{3,0},{4,7},{5,6},{6,5},{7,4},{8,11},{9,10},{10,... | collective-permute-start | bytes 294920 | tf_op jit(solution)/shard_map/ppermute | solution.py:35
  60.3 1.9 %shard_map.66.refs_1_ = f32[3,384,128]{2,1,0:T(8,128)S(1)} custom-call(s32[2]{0:T(128)S(1)} %pad_add_fusion.refs_0_, bf16[384,4096]{1,0:T(8,128)(2,1)S(1)} %copy-done.1, bf16[2048,128]{1,0:T(8,128)(2,1)S(1)} %shard_map.60.refs_5_.refs_2_, bf16[2048,128]{1,0:T(8,128)(2,1)S(1)} %collective-permute-done.12.refs_3_, ...), custom_call_target="tpu_custom_call" | custom-call | flops 603979776 | bytes 5308424 | tf_op jit(solution)/shard_map/pallas_call | solution.py:45
  62.2 1.1 %shard_map.68.refs_2_ = f32[384,128]{1,0:T(8,128)S(1)} custom-call(s32[2]{0:T(128)S(1)} %pad_add_fusion.refs_0_, bf16[384,4096]{1,0:T(8,128)(2,1)S(1)} %copy-done.1, bf16[2048,128]{1,0:T(8,128)(2,1)S(1)} %collective-permute-done.14.refs_2_, bf16[2048,128]{1,0:T(8,128)(2,1)S(1)} %collective-permute-done.15.refs_3_, f32[384,128]{1,0:T(8,128)S(1)} %shard_map.67.refs_4_), custom_call_target="tpu_custom_call" | custom-call | flops 201326592 | bytes 4390920 | tf_op jit(solution)/shard_map/pallas_call | solution.py:45
  63.3 0.0 collective-permute-done.16.refs_3_
  63.3 0.7 shard_map.69
  64.0 2.5 %collective-permute-start.18 = (bf16[384,128]{1,0:T(8,128)(2,1)S(1)}, bf16[384,128]{1,0:T(8,128)(2,1)S(1)}, u32[]{:S(2)}, u32[]{:S(2)}) collective-permute-start(bf16[384,128]{1,0:T(8,128)(2,1)S(1)} %get-tuple-element.36), channel_id=1, source_target_pairs={{0,1},{1,0},{2,3},{3,2},{4,5},{5,4},{6,7},{7,6},{8,9},{9,8},{10,11... | collective-permute-start | bytes 294920 | tf_op jit(solution)/shard_map/ppermute | solution.py:35
  66.6 0.0 collective-permute-start.19
  66.6 0.0 collective-permute-done.9.refs_1_
  66.6 1.5 %collective-permute-start.20 = (bf16[384,128]{1,0:T(8,128)(2,1)S(1)}, bf16[384,128]{1,0:T(8,128)(2,1)S(1)}, u32[]{:S(2)}, u32[]{:S(2)}) collective-permute-start(bf16[384,128]{1,0:T(8,128)(2,1)S(1)} %get-tuple-element.38), channel_id=1, source_target_pairs={{0,3},{1,2},{2,1},{3,0},{4,7},{5,6},{6,5},{7,4},{8,11},{9,10},{10,... | collective-permute-start | bytes 294920 | tf_op jit(solution)/shard_map/ppermute | solution.py:35
  68.1 0.1 fusion.8.refs_9_
  68.2 6.3 %collective-permute-done.11.refs_3_ = bf16[384,128]{1,0:T(8,128)(2,1)S(1)} collective-permute-done((bf16[384,128]{1,0:T(8,128)(2,1)S(1)}, bf16[384,128]{1,0:T(8,128)(2,1)S(1)}, u32[]{:S(2)}, u32[]{:S(2)}) %collective-permute-start.11) | collective-permute-done | bytes 98336 | tf_op jit(solution)/shard_map/ppermute | solution.py:35
  74.5 0.0 collective-permute-done.18.refs_5_
  74.5 0.0 collective-permute-done.19.refs_6_
  74.5 3.4 %collective-permute-done.20.refs_7_ = bf16[384,128]{1,0:T(8,128)(2,1)S(1)} collective-permute-done((bf16[384,128]{1,0:T(8,128)(2,1)S(1)}, bf16[384,128]{1,0:T(8,128)(2,1)S(1)}, u32[]{:S(2)}, u32[]{:S(2)}) %collective-permute-start.20) | collective-permute-done | bytes 98336 | tf_op jit(solution)/shard_map/ppermute | solution.py:35
  77.9 0.3 shard_map.70
  78.3 2.9 %collective-permute-start.21 = (bf16[128,256]{1,0:T(8,128)(2,1)S(1)}, bf16[128,256]{1,0:T(8,128)(2,1)S(1)}, u32[]{:S(2)}, u32[]{:S(2)}) collective-permute-start(bf16[128,256]{1,0:T(8,128)(2,1)S(1)} %get-tuple-element.41), channel_id=1, source_target_pairs={{4,0},{8,4},{12,8},{16,12},{20,16},{24,20},{28,24},{5,1},{9,5},{13... | collective-permute-start | bytes 196616 | tf_op jit(solution)/shard_map/ppermute | solution.py:30
  81.1 1.9 %collective-permute-start.22 = (f32[128,256]{1,0:T(8,128)S(1)}, f32[128,256]{1,0:T(8,128)S(1)}, u32[]{:S(2)}, u32[]{:S(2)}) collective-permute-start(f32[128,256]{1,0:T(8,128)S(1)} %get-tuple-element.42), channel_id=1, source_target_pairs={{0,4},{4,8},{8,12},{12,16},{16,20},{20,24},{24,28},{1,5},{5,9},{9,... | collective-permute-start | bytes 393224 | tf_op jit(solution)/shard_map/ppermute | solution.py:30
  83.1 0.6 shard_map.71.refs_0_
  83.7 0.0 collective-permute-done.21.refs_3_
  83.7 4.6 %collective-permute-done.22.refs_4_ = f32[128,256]{1,0:T(8,128)S(1)} collective-permute-done((f32[128,256]{1,0:T(8,128)S(1)}, f32[128,256]{1,0:T(8,128)S(1)}, u32[]{:S(2)}, u32[]{:S(2)}) %collective-permute-start.22) | collective-permute-done | bytes 131104 | tf_op jit(solution)/shard_map/ppermute | solution.py:30
  88.3 1.0 %shard_map.72 = f32[384,256]{1,0:T(8,128)} custom-call(f32[384,256]{1,0:T(8,128)S(1)} %shard_map.71.refs_0_, bf16[512,512]{1,0:T(8,128)(2,1)S(1)} %convolution_convert_fusion.refs_8_.refs_1_, bf16[384,128]{1,0:T(8,128)(2,1)S(1)} %fusion.9.refs_2_, bf16[128,256]{1,0:T(8,128)(2,1)S(1)} %collective-permute-done.21.refs_3_, ...), custom_call_target="tpu_custom_call" | custom-call | bytes 1605632 | tf_op jit(solution)/shard_map/pallas_call | solution.py:45
  (17 shorter events, 0.1 us)
Async XLA Ops:
  0.0 6.9 %copy-start = (bf16[1,512,512]{2,1,0:T(8,128)(2,1)S(1)}, bf16[1,512,512]{2,1,0:T(8,128)(2,1)}, u32[]{:S(2)}) copy-start(bf16[1,512,512]{2,1,0:T(8,128)(2,1)} %param.7) | copy-start | bytes 1572868
  0.0 19.2 %copy-start.6 = (s32[128]{0:T(128)S(1)}, s32[128]{0:T(128)}, u32[]{:S(2)}) copy-start(s32[128]{0:T(128)} %param.9) | copy-start | bytes 1540
  0.0 2.9 %collective-permute-start = (bf16[4096,128]{1,0:T(8,128)(2,1)}, bf16[4096,128]{1,0:T(8,128)(2,1)S(1)}, u32[]{:S(2)}, u32[]{:S(2)}) collective-permute-start(bf16[4096,128]{1,0:T(8,128)(2,1)} %refs_1_.7), channel_id=1, source_target_pairs={{0,4},{4,0},{8,12},{12,8},{16,20},{20,16},{24,28},{28,24},{1,5},{5... | collective-permute-start | bytes 3145736 | tf_op jit(solution)/shard_map/ppermute | solution.py:35
  2.9 1.2 %copy-start.2 = (bf16[4096,128]{1,0:T(8,128)(2,1)S(1)}, bf16[4096,128]{1,0:T(8,128)(2,1)}, u32[]{:S(2)}) copy-start(bf16[4096,128]{1,0:T(8,128)(2,1)} %refs_1_.7) | copy-start | bytes 3145732
  4.1 2.8 %copy-start.4 = (bf16[4096,128]{1,0:T(8,128)(2,1)}, bf16[4096,128]{1,0:T(8,128)(2,1)S(1)}, u32[]{:S(2)}) copy-start(bf16[4096,128]{1,0:T(8,128)(2,1)S(1)} %collective-permute-done.refs_2_) | copy-start | bytes 3145732
  4.7 18.8 %collective-permute-start.4 = (bf16[384,4096]{1,0:T(8,128)(2,1)}, bf16[384,4096]{1,0:T(8,128)(2,1)}, u32[]{:S(2)}, u32[]{:S(2)}) collective-permute-start(bf16[384,4096]{1,0:T(8,128)(2,1)} %refs_1_.11), channel_id=1, source_target_pairs={{0,4},{4,0},{8,12},{12,8},{16,20},{20,16},{24,28},{28,24},{1,5},{5... | collective-permute-start | bytes 9437192 | tf_op jit(solution)/shard_map/ppermute | solution.py:35
  4.9 14.8 %collective-permute-start.1 = (bf16[2048,128]{1,0:T(8,128)(2,1)S(1)}, bf16[2048,128]{1,0:T(8,128)(2,1)S(1)}, u32[]{:S(2)}, u32[]{:S(2)}) collective-permute-start(bf16[2048,128]{1,0:T(8,128)(2,1)S(1)} %shard_map.58.refs_2_), channel_id=1, source_target_pairs={{0,8},{4,12},{8,0},{12,4},{16,24},{20,28},{24,16},{28,20},{1,9},{5... | collective-permute-start | bytes 1572872 | tf_op jit(solution)/shard_map/ppermute | solution.py:35
  6.4 14.4 %collective-permute-start.2 = (bf16[2048,128]{1,0:T(8,128)(2,1)S(1)}, bf16[2048,128]{1,0:T(8,128)(2,1)}, u32[]{:S(2)}, u32[]{:S(2)}) collective-permute-start(bf16[2048,128]{1,0:T(8,128)(2,1)S(1)} %shard_map.58.refs_2_), channel_id=1, source_target_pairs={{0,16},{4,20},{8,24},{12,28},{16,0},{20,4},{24,8},{28,12},{1,17},{... | collective-permute-start | bytes 1572872 | tf_op jit(solution)/shard_map/ppermute | solution.py:35
  8.7 18.3 %copy-start.3 = (bf16[4096,128]{1,0:T(8,128)(2,1)S(1)}, bf16[4096,128]{1,0:T(8,128)(2,1)}, u32[]{:S(2)}) copy-start(bf16[4096,128]{1,0:T(8,128)(2,1)} %refs_1_.7) | copy-start | bytes 3145732
  8.7 10.5 %collective-permute-start.3 = (bf16[128,128]{1,0:T(8,128)(2,1)S(1)}, bf16[128,128]{1,0:T(8,128)(2,1)S(1)}, u32[]{:S(2)}, u32[]{:S(2)}) collective-permute-start(bf16[128,128]{1,0:T(8,128)(2,1)S(1)} %slice.4), channel_id=1, source_target_pairs={{0,4},{4,8},{8,12},{12,16},{16,20},{20,24},{24,28},{1,5},{5,9},{9,... | collective-permute-start | bytes 98312 | tf_op jit(solution)/shard_map/ppermute | solution.py:30
  19.7 7.3 %copy-start.5 = (bf16[4096,128]{1,0:T(8,128)(2,1)S(1)}, bf16[4096,128]{1,0:T(8,128)(2,1)}, u32[]{:S(2)}) copy-start(bf16[4096,128]{1,0:T(8,128)(2,1)} %copy-done.4) | copy-start | bytes 3145732
  20.8 11.3 %collective-permute-start.5 = (bf16[2048,128]{1,0:T(8,128)(2,1)S(1)}, bf16[2048,128]{1,0:T(8,128)(2,1)S(1)}, u32[]{:S(2)}, u32[]{:S(2)}) collective-permute-start(bf16[2048,128]{1,0:T(8,128)(2,1)S(1)} %collective-permute-done.1.refs_3_), channel_id=1, source_target_pairs={{0,16},{8,24},{16,0},{24,8},{1,17},{9,25},{17,1},{25,9},{2,18},{10... | collective-permute-start | bytes 1572872 | tf_op jit(solution)/shard_map/ppermute | solution.py:35
  22.8 9.3 %collective-permute-start.6 = (bf16[2048,128]{1,0:T(8,128)(2,1)}, bf16[2048,128]{1,0:T(8,128)(2,1)S(1)}, u32[]{:S(2)}, u32[]{:S(2)}) collective-permute-start(bf16[2048,128]{1,0:T(8,128)(2,1)} %collective-permute-done.2.refs_4_), channel_id=1, source_target_pairs={{4,12},{12,4},{20,28},{28,20},{5,13},{13,5},{21,29},{29,21},{6,14}... | collective-permute-start | bytes 1572872 | tf_op jit(solution)/shard_map/ppermute | solution.py:35
  26.9 7.8 %copy-start.1 = (bf16[384,4096]{1,0:T(8,128)(2,1)S(1)}, bf16[384,4096]{1,0:T(8,128)(2,1)}, u32[]{:S(2)}) copy-start(bf16[384,4096]{1,0:T(8,128)(2,1)} %refs_1_.11) | copy-start | bytes 9437188
  27.0 11.3 %collective-permute-start.7 = (f32[3,384,128]{2,1,0:T(8,128)S(1)}, f32[3,384,128]{2,1,0:T(8,128)S(1)}, u32[]{:S(2)}, u32[]{:S(2)}) collective-permute-start(f32[3,384,128]{2,1,0:T(8,128)S(1)} %shard_map.59.refs_3_), channel_id=1, source_target_pairs={{0,4},{4,0},{8,12},{12,8},{16,20},{20,16},{24,28},{28,24},{1,5},{5... | collective-permute-start | bytes 1769480 | tf_op jit(solution)/shard_map/ppermute | solution.py:35
  27.7 14.6 %collective-permute-start.12 = (bf16[2048,128]{1,0:T(8,128)(2,1)S(1)}, bf16[2048,128]{1,0:T(8,128)(2,1)S(1)}, u32[]{:S(2)}, u32[]{:S(2)}) collective-permute-start(bf16[2048,128]{1,0:T(8,128)(2,1)S(1)} %shard_map.60.refs_5_.refs_2_), channel_id=1, source_target_pairs={{0,8},{4,12},{8,0},{12,4},{16,24},{20,28},{24,16},{28,20},{1,9},{5... | collective-permute-start | bytes 1572872 | tf_op jit(solution)/shard_map/ppermute | solution.py:35
  28.7 14.4 %collective-permute-start.13 = (bf16[2048,128]{1,0:T(8,128)(2,1)S(1)}, bf16[2048,128]{1,0:T(8,128)(2,1)S(1)}, u32[]{:S(2)}, u32[]{:S(2)}) collective-permute-start(bf16[2048,128]{1,0:T(8,128)(2,1)S(1)} %shard_map.60.refs_5_.refs_2_), channel_id=1, source_target_pairs={{0,16},{4,20},{8,24},{12,28},{16,0},{20,4},{24,8},{28,12},{1,17},{... | collective-permute-start | bytes 1572872 | tf_op jit(solution)/shard_map/ppermute | solution.py:35
  34.6 3.7 %collective-permute-start.8 = (f32[384,128]{1,0:T(8,128)S(1)}, f32[384,128]{1,0:T(8,128)S(1)}, u32[]{:S(2)}, u32[]{:S(2)}) collective-permute-start(f32[384,128]{1,0:T(8,128)S(1)} %shard_map.62.refs_4_), channel_id=1, source_target_pairs={{0,4},{4,0},{8,12},{12,8},{16,20},{20,16},{24,28},{28,24},{1,5},{5... | collective-permute-start | bytes 589832 | tf_op jit(solution)/shard_map/ppermute | solution.py:35
  43.1 11.1 %collective-permute-start.14 = (bf16[2048,128]{1,0:T(8,128)(2,1)S(1)}, bf16[2048,128]{1,0:T(8,128)(2,1)S(1)}, u32[]{:S(2)}, u32[]{:S(2)}) collective-permute-start(bf16[2048,128]{1,0:T(8,128)(2,1)S(1)} %collective-permute-done.12.refs_3_), channel_id=1, source_target_pairs={{0,16},{8,24},{16,0},{24,8},{1,17},{9,25},{17,1},{25,9},{2,18},{10... | collective-permute-start | bytes 1572872 | tf_op jit(solution)/shard_map/ppermute | solution.py:35
  46.2 8.0 %collective-permute-start.15 = (bf16[2048,128]{1,0:T(8,128)(2,1)S(1)}, bf16[2048,128]{1,0:T(8,128)(2,1)S(1)}, u32[]{:S(2)}, u32[]{:S(2)}) collective-permute-start(bf16[2048,128]{1,0:T(8,128)(2,1)S(1)} %collective-permute-done.13.refs_4_), channel_id=1, source_target_pairs={{4,12},{12,4},{20,28},{28,20},{5,13},{13,5},{21,29},{29,21},{6,14}... | collective-permute-start | bytes 1572872 | tf_op jit(solution)/shard_map/ppermute | solution.py:35
  50.2 13.2 %collective-permute-start.16 = (f32[3,384,128]{2,1,0:T(8,128)S(1)}, f32[3,384,128]{2,1,0:T(8,128)S(1)}, u32[]{:S(2)}, u32[]{:S(2)}) collective-permute-start(f32[3,384,128]{2,1,0:T(8,128)S(1)} %shard_map.65.refs_5_), channel_id=1, source_target_pairs={{0,4},{4,0},{8,12},{12,8},{16,20},{20,16},{24,28},{28,24},{1,5},{5... | collective-permute-start | bytes 1769480 | tf_op jit(solution)/shard_map/ppermute | solution.py:35
  56.6 6.7 %collective-permute-start.17 = (f32[384,128]{1,0:T(8,128)S(1)}, f32[384,128]{1,0:T(8,128)S(1)}, u32[]{:S(2)}, u32[]{:S(2)}) collective-permute-start(f32[384,128]{1,0:T(8,128)S(1)} %shard_map.67.refs_4_), channel_id=1, source_target_pairs={{0,4},{4,0},{8,12},{12,8},{16,20},{20,16},{24,28},{28,24},{1,5},{5... | collective-permute-start | bytes 589832 | tf_op jit(solution)/shard_map/ppermute | solution.py:35
  56.7 9.9 %collective-permute-start.9 = (bf16[384,128]{1,0:T(8,128)(2,1)S(1)}, bf16[384,128]{1,0:T(8,128)(2,1)S(1)}, u32[]{:S(2)}, u32[]{:S(2)}) collective-permute-start(bf16[384,128]{1,0:T(8,128)(2,1)S(1)} %get-tuple-element.34.refs_5_), channel_id=1, source_target_pairs={{0,1},{1,0},{2,3},{3,2},{4,5},{5,4},{6,7},{7,6},{8,9},{9,8},{10,11... | collective-permute-start | bytes 294920 | tf_op jit(solution)/shard_map/ppermute | solution.py:35
  58.4 9.8 %collective-permute-start.10 = (bf16[384,128]{1,0:T(8,128)(2,1)S(1)}, bf16[384,128]{1,0:T(8,128)(2,1)S(1)}, u32[]{:S(2)}, u32[]{:S(2)}) collective-permute-start(bf16[384,128]{1,0:T(8,128)(2,1)S(1)} %get-tuple-element.30), channel_id=1, source_target_pairs={{0,2},{1,3},{2,0},{3,1},{4,6},{5,7},{6,4},{7,5},{8,10},{9,11},{10,... | collective-permute-start | bytes 294920 | tf_op jit(solution)/shard_map/ppermute | solution.py:35
  58.7 15.8 %collective-permute-start.11 = (bf16[384,128]{1,0:T(8,128)(2,1)S(1)}, bf16[384,128]{1,0:T(8,128)(2,1)S(1)}, u32[]{:S(2)}, u32[]{:S(2)}) collective-permute-start(bf16[384,128]{1,0:T(8,128)(2,1)S(1)} %get-tuple-element.31), channel_id=1, source_target_pairs={{0,3},{1,2},{2,1},{3,0},{4,7},{5,6},{6,5},{7,4},{8,11},{9,10},{10,... | collective-permute-start | bytes 294920 | tf_op jit(solution)/shard_map/ppermute | solution.py:35
  64.0 10.4 %collective-permute-start.18 = (bf16[384,128]{1,0:T(8,128)(2,1)S(1)}, bf16[384,128]{1,0:T(8,128)(2,1)S(1)}, u32[]{:S(2)}, u32[]{:S(2)}) collective-permute-start(bf16[384,128]{1,0:T(8,128)(2,1)S(1)} %get-tuple-element.36), channel_id=1, source_target_pairs={{0,1},{1,0},{2,3},{3,2},{4,5},{5,4},{6,7},{7,6},{8,9},{9,8},{10,11... | collective-permute-start | bytes 294920 | tf_op jit(solution)/shard_map/ppermute | solution.py:35
  66.6 7.9 %collective-permute-start.19 = (bf16[384,128]{1,0:T(8,128)(2,1)S(1)}, bf16[384,128]{1,0:T(8,128)(2,1)S(1)}, u32[]{:S(2)}, u32[]{:S(2)}) collective-permute-start(bf16[384,128]{1,0:T(8,128)(2,1)S(1)} %get-tuple-element.37), channel_id=1, source_target_pairs={{0,2},{1,3},{2,0},{3,1},{4,6},{5,7},{6,4},{7,5},{8,10},{9,11},{10,... | collective-permute-start | bytes 294920 | tf_op jit(solution)/shard_map/ppermute | solution.py:35
  66.6 11.3 %collective-permute-start.20 = (bf16[384,128]{1,0:T(8,128)(2,1)S(1)}, bf16[384,128]{1,0:T(8,128)(2,1)S(1)}, u32[]{:S(2)}, u32[]{:S(2)}) collective-permute-start(bf16[384,128]{1,0:T(8,128)(2,1)S(1)} %get-tuple-element.38), channel_id=1, source_target_pairs={{0,3},{1,2},{2,1},{3,0},{4,7},{5,6},{6,5},{7,4},{8,11},{9,10},{10,... | collective-permute-start | bytes 294920 | tf_op jit(solution)/shard_map/ppermute | solution.py:35
  78.3 5.4 %collective-permute-start.21 = (bf16[128,256]{1,0:T(8,128)(2,1)S(1)}, bf16[128,256]{1,0:T(8,128)(2,1)S(1)}, u32[]{:S(2)}, u32[]{:S(2)}) collective-permute-start(bf16[128,256]{1,0:T(8,128)(2,1)S(1)} %get-tuple-element.41), channel_id=1, source_target_pairs={{4,0},{8,4},{12,8},{16,12},{20,16},{24,20},{28,24},{5,1},{9,5},{13... | collective-permute-start | bytes 196616 | tf_op jit(solution)/shard_map/ppermute | solution.py:30
  81.1 7.2 %collective-permute-start.22 = (f32[128,256]{1,0:T(8,128)S(1)}, f32[128,256]{1,0:T(8,128)S(1)}, u32[]{:S(2)}, u32[]{:S(2)}) collective-permute-start(f32[128,256]{1,0:T(8,128)S(1)} %get-tuple-element.42), channel_id=1, source_target_pairs={{0,4},{4,8},{8,12},{12,16},{16,20},{20,24},{24,28},{1,5},{5,9},{9,... | collective-permute-start | bytes 393224 | tf_op jit(solution)/shard_map/ppermute | solution.py:30

commit v4 on v3

v4 whole, which is shorter than its diff:
```python
import functools

import jax
import jax.numpy as jnp
from jax import lax
from jax.experimental import pallas as pl
from jax.experimental.pallas import tpu as pltpu
from jax.sharding import PartitionSpec as P

CORE, NEAR, FAR = 1, 2, 4
VMEM = pl.BlockSpec(memory_space=pltpu.VMEM)
ANY = pl.BlockSpec(memory_space=pl.ANY)
F32, BF16 = jnp.float32, jnp.bfloat16


def dot(left, right):
    precision = lax.Precision.HIGHEST if left.dtype == F32 else None
    return jnp.dot(left, right, precision=precision, preferred_element_type=F32)


def split(value):
    high = value.astype(BF16)
    return high, (value - high.astype(F32)).astype(BF16)


def shifted(value, axis, steps):
    count = lax.axis_size(axis)
    leading, last = (max(0, -steps), min(count, count - steps))
    return lax.ppermute(value, axis, [(source, source + steps) for source in range(leading, last)])


def exchanged(value, axis, mask, core=None):
    sources = range(lax.axis_size(axis))
    return lax.ppermute(value, axis, [(source, source ^ mask) for source in sources if core in (None, source & CORE)])


def call(kernel, outs, operands, after=(), spaces=None, scratch=()):
    count = len(operands)

    def body(*refs):
        kernel(*refs[:count], *refs[count + len(after) :])

    return pl.pallas_call(
        body,
        out_shape=outs,
        in_specs=[pl.BlockSpec(memory_space=space) for space in spaces or [pltpu.VMEM] * count] + [ANY] * len(after),
        out_specs=[VMEM] * len(outs),
        scratch_shapes=list(scratch),
        cost_estimate=pl.CostEstimate(flops=0, bytes_accessed=1024, transcendentals=0),
        compiler_params=pltpu.CompilerParams(vmem_limit_bytes=24 * 2**20),
    )(*operands, *after)


def shape(*dims, dtype=F32):
    return jax.ShapeDtypeStruct(dims, dtype)


def core():
    return lax.rem(lax.axis_index("domain"), 2)


def half_kernel(source, out, done):
    half = out.shape[0]
    copy = pltpu.make_async_copy(source.at[pl.ds(pl.multiple_of(core() * half, half), half)], out, done)
    copy.start()
    copy.wait()


def choose_kernel(even, odd, out):
    first = core() == 0

    @pl.when(first)
    def _():
        out[...] = even[...]

    @pl.when(jnp.logical_not(first))
    def _():
        out[...] = odd[...]


def products(states, pieces):
    half = pieces.shape[0]
    start = pl.multiple_of(core() * half, half)
    return jnp.dot(states[:, pl.ds(start, half)], pieces, preferred_element_type=F32)


def early_kernel(counts, mine, theirs, *refs):
    pieces = []
    for slot, count in enumerate(counts):
        value = refs[0][...]
        for other in refs[1:count]:
            value = jnp.where(core() == 0, value, other[...]) if slot == 0 else value + other[...]
        refs = refs[count:]
        pieces.append(value)
    own, others = refs
    width = pieces[0].shape[1]
    for first in range(0, len(pieces), 2):
        group = pieces[first : first + 2]
        wide = group[0] if len(group) == 1 else jnp.concatenate(group, 1)
        for states, out in ((theirs, others), (mine, own)):
            result = products(states, wide)
            for slot in range(len(group)):
                out[first + slot] = result[:, slot * width : (slot + 1) * width]


def late_kernel(states, even, odd, out):
    out[...] = products(states, even[...] + odd[...])


def pick_kernel(count, early, late, early_other, late_other, kept, *sent):
    where = lax.bitwise_xor(lax.div(lax.axis_index("domain"), 2), lax.axis_index("band"))
    last = early.shape[0]

    def store(slot, out):
        @pl.when(slot < last)
        def _():
            out[...] = (early[jnp.minimum(slot, last - 1)] + early_other[jnp.minimum(slot, last - 1)]).astype(out.dtype)

        @pl.when(slot == last)
        def _():
            out[...] = (late[...] + late_other[...]).astype(out.dtype)

    store(where, kept)
    for mask, out in zip(range(1, count), sent):
        store(lax.bitwise_xor(where, mask), out)


def sum_kernel(*refs):
    value = refs[0][...]
    for part in refs[1:-1]:
        value = value + part[...].astype(F32)
    refs[-1][...] = value


def rotate_square(wavefunctions, rotation, operator):
    bands = lax.axis_size("band")
    rows, states = wavefunctions.shape
    width = rotation.shape[1]
    half = states // 2
    piece = [shape(half, width, dtype=BF16)]

    def halved(value, space, after=()):
        return call(half_kernel, piece, (value,), after=after, spaces=[space], scratch=[pltpu.SemaphoreType.DMA])[0]

    def early(counts, pieces, after=()):
        outs = [shape(len(counts), rows, width)] * 2
        kernel = functools.partial(early_kernel, counts)
        own, others = call(kernel, outs, (wavefunctions, theirs, *pieces), after)
        return own, exchanged(others, "domain", CORE), others

    def late(even, odd, after=()):
        others = call(late_kernel, [shape(rows, width)], (theirs, even, odd), after)[0]
        own = call(late_kernel, [shape(rows, width)], (wavefunctions, even, odd), (others,))[0]
        return own, exchanged(others, "domain", CORE)

    def spread(early_own, early_other, late_own, late_other, after=()):
        outs = [shape(rows, width)] + [shape(rows, width, dtype=BF16)] * (bands - 1)
        kernel = functools.partial(pick_kernel, bands)
        kept, *sent = call(kernel, outs, (early_own, late_own, early_other, late_other), after=after)
        return [kept] + [exchanged(value, "band", mask) for mask, value in zip(range(1, bands), sent)], sent[0]

    swapped = exchanged(rotation, "domain", CORE)
    keep = halved(rotation, pltpu.HBM)
    near_even, far_even = exchanged(keep, "domain", NEAR, 0), exchanged(keep, "domain", FAR, 0)
    received = halved(swapped, pl.ANY, (keep,))
    near_odd, far_odd = exchanged(received, "domain", NEAR, CORE), exchanged(received, "domain", FAR, CORE)
    other, received = lax.optimization_barrier((wavefunctions, received))
    theirs = exchanged(other, "domain", CORE)
    operator = operator()
    right = call(choose_kernel, piece, (received, keep), after=operator[:1])[0]
    near, far = exchanged(right, "domain", NEAR), exchanged(right, "domain", FAR)

    near_even, far_odd, right = lax.optimization_barrier((near_even, far_odd, right))
    even, odd = exchanged(near_even, "domain", FAR, 0), exchanged(far_odd, "domain", NEAR, CORE)
    early_own, early_other, token = early((2, 2, 2), (keep, received, near_even, near_odd, far_even, far_odd))

    near, far, token = lax.optimization_barrier((near, far, token))
    right_even, right_odd = exchanged(near, "domain", FAR, 0), exchanged(far, "domain", NEAR, CORE)

    late_own, late_other = late(even, odd, (token, near, far))
    left_parts, token = spread(early_own, early_other, late_own, late_other)
    left_total = call(sum_kernel, [shape(rows, width)], left_parts)[0]

    early_own, early_other, token = early((1, 1, 1), (right, near, far), (token,))
    late_own, late_other = late(right_even, right_odd, (token,))
    right_parts, _ = spread(early_own, early_other, late_own, late_other, (left_total,))
    return left_total, right_parts, operator


def rotate_any(wavefunctions, rotation):
    columns = lax.all_gather(rotation, "domain", axis=1, tiled=True)
    return lax.psum_scatter(dot(wavefunctions, columns), "band", scatter_dimension=1, tiled=True)


def faces_kernel(width, *refs):
    left, *parts, assembled, pick, total, faces, back = refs
    own = total.shape[0]
    value = parts[0][...]
    for part in parts[1:]:
        value = value + part[...].astype(F32)
    for side, half in enumerate((left[...], value)):
        columns = slice(side * width, (side + 1) * width)
        total[:, columns] = half
        high, low = split(half)
        faces[:, columns] = dot(pick[...], high).astype(BF16)
        outward = assembled[own:, :own]
        back[:, columns] = dot(outward, high) + dot(outward, low)


def inner_kernel(total, assembled, corner, pick, spread, out):
    own = total.shape[0]
    high, low = split(total[...])
    inner = assembled[:own, :own]
    face_high, face_low = dot(pick[...], high).astype(BF16), dot(pick[...], low).astype(BF16)
    back_high, back_low = split(dot(corner[...], face_high) + dot(corner[...], face_low))
    out[...] = dot(inner, high) + dot(inner, low) + dot(spread[...], back_high) + dot(spread[...], back_low)


def final_kernel(inner, assembled, spread, incoming, back, out):
    own = inner.shape[0]
    high, low = split(back[...])
    out[...] = inner[...] + dot(assembled[:own, own:], incoming[...]) + dot(spread[...], high) + dot(spread[...], low)


def finish_square(left, parts, operator):
    assembled, corner, pick, spread = operator
    rows, width = left.shape
    faces_count = pick.shape[0]
    columns = 2 * width
    total, faces, back = call(
        functools.partial(faces_kernel, width),
        [shape(rows, columns), shape(faces_count, columns, dtype=BF16), shape(faces_count, columns)],
        (left, *parts, assembled, pick),
    )
    incoming, back = shifted(faces, "domain", -1), shifted(back, "domain", 1)
    inner = call(inner_kernel, [shape(rows, columns)], (total, assembled, corner, pick, spread))[0]
    return call(final_kernel, [shape(rows, columns)], (inner, assembled, spread, incoming, back))[0]


def finish_any(rotated, cell_matrices, cell_nodes, face_map):
    own = rotated.shape[0]
    assembled, pick, returned = assemble_any(cell_matrices, cell_nodes, face_map, own)
    rotated = rotated.astype(BF16).astype(assembled.dtype)
    incoming = shifted(dot(pick, rotated).astype(BF16), "domain", -1).astype(assembled.dtype)
    back = shifted(dot(assembled[own:, :own], rotated), "domain", 1)
    inner = dot(assembled[:own, :own], rotated) + dot(returned, rotated) + dot(assembled[:own, own:], incoming)
    return inner + dot(pick.T.astype(F32), back)


def assemble_any(cell_matrices, cell_nodes, face_map, own):
    cells = cell_nodes.shape[0]
    extent = own + face_map.shape[0]
    held = BF16 if cells == 1 else F32
    places = jax.nn.one_hot(cell_nodes, extent, dtype=held)
    assembled = jnp.zeros((extent, extent), F32)
    for cell in range(cells):
        rows = dot(places[cell].T, cell_matrices[cell].astype(held)).astype(held)
        assembled = assembled + dot(rows, places[cell])
    assembled = assembled.astype(held)
    pick = jax.nn.one_hot(face_map, own, dtype=held)
    corner = shifted(assembled[own:, own:], "domain", 1)
    returned = dot(dot(pick.T, corner).astype(held), pick).astype(held)
    return assembled, pick, returned


def assemble_kernel(matrix, nodes, faces, assembled, corner, pick, spread):
    own, extent = spread.shape[0], assembled.shape[0]
    places = jnp.where(lax.broadcasted_iota(jnp.int32, (extent, extent), 0) == nodes[...], 1.0, 0.0).astype(BF16)
    rows = dot(places, matrix[0]).astype(BF16)
    whole = lax.dot_general(rows, places, (((1,), (1,)), ((), ())), preferred_element_type=F32).astype(BF16)
    assembled[...] = whole
    corner[...] = whole[own:, own:]
    chosen = jnp.where(lax.broadcasted_iota(jnp.int32, spread.shape, 0) == faces[...], 1.0, 0.0)
    spread[...] = chosen.astype(BF16)
    pick[...] = chosen.T.astype(BF16)


def assemble(cell_matrices, cell_nodes, face_map, own):
    shared = face_map.shape[0]
    outs = [(own + shared, own + shared), (shared, shared), (shared, own), (own, shared)]
    operands = (cell_matrices, cell_nodes, face_map.reshape(1, shared))
    assembled, corner, pick, spread = call(assemble_kernel, [shape(*dims, dtype=BF16) for dims in outs], operands)
    return assembled, shifted(corner, "domain", 1), pick, spread


def local(wavefunctions, rotation, cell_matrices, cell_nodes, face_map):
    chips = lax.axis_size("domain") // 2
    if chips == FAR and chips == lax.axis_size("band") and cell_nodes.shape[0] == 1:
        operator = functools.partial(assemble, cell_matrices, cell_nodes, face_map, wavefunctions.shape[0])
        return finish_square(*rotate_square(wavefunctions, rotation, operator))
    return finish_any(rotate_any(wavefunctions, rotation), cell_matrices, cell_nodes, face_map)


def solution(mesh):
    in_specs = (
        P("domain", "band"),
        P("band", "domain"),
        P("domain", None, None),
        P("domain", None),
        P("domain"),
    )
    out_specs = P("domain", "band")
    return jax.shard_map(local, mesh=mesh, in_specs=in_specs, out_specs=out_specs, check_vma=False)
```

time: 89.8 us -> 88.8 us (0.989)
  the two profiles are of different devices: /device:TPU:20 before, /device:TPU:12 now
where the time goes in v4:
time: 88.8 us; the launch traced here: 88.5 us
  waiting for transfers between devices  44.8 us (50%)
  starting transfers between devices  32.1 us (36%)
  Pallas kernels  9.15 us (10%)
  local copies, waits for them, and re-layouts  2.06 us (2%)
    ppermute x22, waiting for transfers between devices, exchanged(): lax.ppermute(value, axis, [(source, source ^ mask) for source in sources...  40.6 us
    ppermute x22, starting transfers between devices, exchanged(): lax.ppermute(value, axis, [(source, source ^ mask) for source in sources...  23.7 us
    pallas_call x16, Pallas kernels, call(): pl.pallas_call(body, out_shape=outs, in_specs=[pl.BlockSpec(memory_space=...  9.15 us
    ppermute x3, starting transfers between devices, shifted(): lax.ppermute(value, axis, [(source, source + steps) for source in range(l...  8.38 us
    ppermute x3, waiting for transfers between devices, shifted(): lax.ppermute(value, axis, [(source, source + steps) for source in range(l...  4.21 us
    unnamed x10, local copies, waits for them, and re-layouts  2.06 us
  transfers between devices with their start and end apart: 25, of which 13 were waited for; matrix products, arithmetic and copies ran while one was open for 0% of the time, Pallas kernels for 9%

profile of v4, /device:TPU:12, one launch (start us, length us, event | category | flops | bytes accessed | tf_op | source)
XLA Modules:
  0.0 88.5 jit_solution(13745462414887433630)
XLA Ops:
  0.0 0.0 collective-permute-start
  0.0 1.4 %copy-done.1 = bf16[4096,128]{1,0:T(8,128)(2,1)S(1)} copy-done((bf16[4096,128]{1,0:T(8,128)(2,1)S(1)}, bf16[4096,128]{1,0:T(8,128)(2,1)}, u32[]{:S(2)}) %copy-start.1) | copy-done | bytes 1048600
  1.4 1.4 %collective-permute-done.refs_0_ = bf16[4096,128]{1,0:T(8,128)(2,1)S(1)} collective-permute-done((bf16[4096,128]{1,0:T(8,128)(2,1)}, bf16[4096,128]{1,0:T(8,128)(2,1)S(1)}, u32[]{:S(2)}, u32[]{:S(2)}) %collective-permute-start) | collective-permute-done | bytes 1048608 | tf_op jit(solution)/shard_map/ppermute | solution.py:34
  2.9 0.2 collective-permute-start.1
  3.1 3.4 %collective-permute-start.2 = (bf16[2048,128]{1,0:T(8,128)(2,1)S(1)}, bf16[2048,128]{1,0:T(8,128)(2,1)S(1)}, u32[]{:S(2)}, u32[]{:S(2)}) collective-permute-start(bf16[2048,128]{1,0:T(8,128)(2,1)S(1)} %shard_map.55.refs_1_.refs_2_), channel_id=1, source_target_pairs={{0,8},{8,0},{16,24},{24,16},{1,9},{9,1},{17,25},{25,17},{2,10},{10... | collective-permute-start | bytes 1572872 | tf_op jit(solution)/shard_map/ppermute | solution.py:34
  6.5 0.7 collective-permute-start.3
  7.2 2.4 %collective-permute-start.5 = (bf16[2048,128]{1,0:T(8,128)(2,1)S(1)}, bf16[2048,128]{1,0:T(8,128)(2,1)S(1)}, u32[]{:S(2)}, u32[]{:S(2)}) collective-permute-start(bf16[2048,128]{1,0:T(8,128)(2,1)S(1)} %shard_map.55.refs_1_.refs_2_), channel_id=1, source_target_pairs={{0,16},{8,24},{16,0},{24,8},{1,17},{9,25},{17,1},{25,9},{2,18},{10... | collective-permute-start | bytes 1572872 | tf_op jit(solution)/shard_map/ppermute | solution.py:34
  9.7 0.7 collective-permute-start.4
  10.4 0.0 copy-start.3
  10.4 0.7 copy-done.3
  11.1 0.7 shard_map.57
  11.8 0.1 shard_map.58.refs_2_
  11.8 5.0 %collective-permute-done.2.refs_4_ = bf16[2048,128]{1,0:T(8,128)(2,1)S(1)} collective-permute-done((bf16[2048,128]{1,0:T(8,128)(2,1)S(1)}, bf16[2048,128]{1,0:T(8,128)(2,1)S(1)}, u32[]{:S(2)}, u32[]{:S(2)}) %collective-permute-start.2) | collective-permute-done | bytes 524320 | tf_op jit(solution)/shard_map/ppermute | solution.py:34
  16.8 1.5 %collective-permute-start.8 = (bf16[2048,128]{1,0:T(8,128)(2,1)S(1)}, bf16[2048,128]{1,0:T(8,128)(2,1)S(1)}, u32[]{:S(2)}, u32[]{:S(2)}) collective-permute-start(bf16[2048,128]{1,0:T(8,128)(2,1)S(1)} %shard_map.58.refs_2_), channel_id=1, source_target_pairs={{0,8},{4,12},{8,0},{12,4},{16,24},{20,28},{24,16},{28,20},{1,9},{5... | collective-permute-start | bytes 1572872 | tf_op jit(solution)/shard_map/ppermute | solution.py:34
  18.3 0.0 collective-permute-done.3.refs_7_
  18.3 0.0 collective-permute-start.9
  18.3 2.9 %collective-permute-done.5.refs_6_ = bf16[2048,128]{1,0:T(8,128)(2,1)S(1)} collective-permute-done((bf16[2048,128]{1,0:T(8,128)(2,1)S(1)}, bf16[2048,128]{1,0:T(8,128)(2,1)S(1)}, u32[]{:S(2)}, u32[]{:S(2)}) %collective-permute-start.5) | collective-permute-done | bytes 524320 | tf_op jit(solution)/shard_map/ppermute | solution.py:34
  21.2 2.4 %collective-permute-start.6 = (bf16[2048,128]{1,0:T(8,128)(2,1)S(1)}, bf16[2048,128]{1,0:T(8,128)(2,1)S(1)}, u32[]{:S(2)}, u32[]{:S(2)}) collective-permute-start(bf16[2048,128]{1,0:T(8,128)(2,1)S(1)} %collective-permute-done.2.refs_4_), channel_id=1, source_target_pairs={{0,16},{8,24},{16,0},{24,8},{1,17},{9,25},{17,1},{25,9},{2,18},{10... | collective-permute-start | bytes 1572872 | tf_op jit(solution)/shard_map/ppermute | solution.py:34
  23.6 0.0 collective-permute-done.4.refs_5_
  23.6 0.7 collective-permute-start.7
  24.3 0.0 collective-permute-done.1.refs_1_.refs_0_
  24.4 1.8 %shard_map.59 = (f32[3,384,128]{2,1,0:T(8,128)S(1)}, f32[3,384,128]{2,1,0:T(8,128)S(1)}) custom-call(bf16[384,4096]{1,0:T(8,128)(2,1)S(1)} %copy-done, bf16[384,4096]{1,0:T(8,128)(2,1)S(1)} %collective-permute-done.1.refs_1_.refs_0_, bf16[2048,128]{1,0:T(8,128)(2,1)S(1)} %shard_map.55.refs_1_.refs_2_, bf16[2048,128]{1,0:T(8,128)(2,1)S(1)} %shard_map.56.refs_0_.refs_3_, ...), custom_call_target="tpu_custom_call" | custom-call | bytes 1024 | tf_op jit(solution)/shard_map/pallas_call | solution.py:43
  26.2 0.1 collective-permute-start.10
  26.3 5.4 %collective-permute-done.8.refs_4_.refs_3_ = bf16[2048,128]{1,0:T(8,128)(2,1)S(1)} collective-permute-done((bf16[2048,128]{1,0:T(8,128)(2,1)S(1)}, bf16[2048,128]{1,0:T(8,128)(2,1)S(1)}, u32[]{:S(2)}, u32[]{:S(2)}) %collective-permute-start.8) | collective-permute-done | bytes 524320 | tf_op jit(solution)/shard_map/ppermute | solution.py:34
  31.7 0.0 collective-permute-done.9.refs_5_.refs_4_
  31.7 5.1 %collective-permute-done.6.refs_1_ = bf16[2048,128]{1,0:T(8,128)(2,1)S(1)} collective-permute-done((bf16[2048,128]{1,0:T(8,128)(2,1)S(1)}, bf16[2048,128]{1,0:T(8,128)(2,1)S(1)}, u32[]{:S(2)}, u32[]{:S(2)}) %collective-permute-start.6) | collective-permute-done | bytes 524320 | tf_op jit(solution)/shard_map/ppermute | solution.py:34
  36.8 0.0 collective-permute-done.7.refs_2_
  36.8 0.6 shard_map.60.refs_3_
  37.4 0.1 collective-permute-start.11
  37.4 2.4 %collective-permute-start.15 = (bf16[2048,128]{1,0:T(8,128)(2,1)S(1)}, bf16[2048,128]{1,0:T(8,128)(2,1)S(1)}, u32[]{:S(2)}, u32[]{:S(2)}) collective-permute-start(bf16[2048,128]{1,0:T(8,128)(2,1)S(1)} %collective-permute-done.8.refs_4_.refs_3_), channel_id=1, source_target_pairs={{0,16},{8,24},{16,0},{24,8},{1,17},{9,25},{17,1},{25,9},{2,18},{10... | collective-permute-start | bytes 1572872 | tf_op jit(solution)/shard_map/ppermute | solution.py:34
  39.9 0.7 collective-permute-start.16
  40.6 0.6 shard_map.61.refs_1_
  41.2 0.0 collective-permute-done.10.refs_2_
  41.2 0.1 shard_map.62
  41.3 1.8 %shard_map.64 = (f32[3,384,128]{2,1,0:T(8,128)S(1)}, f32[3,384,128]{2,1,0:T(8,128)S(1)}) custom-call(bf16[384,4096]{1,0:T(8,128)(2,1)S(1)} %copy-done, bf16[384,4096]{1,0:T(8,128)(2,1)S(1)} %collective-permute-done.1.refs_1_.refs_0_, bf16[2048,128]{1,0:T(8,128)(2,1)S(1)} %shard_map.58.refs_2_, bf16[2048,128]{1,0:T(8,128)(2,1)S(1)} %collective-permute-done.8.refs_4_.refs_3_, ...), custom_call_target="tpu_custom_call" | custom-call | bytes 1024 | tf_op jit(solution)/shard_map/pallas_call | solution.py:43
  43.1 1.3 %collective-permute-start.17 = (f32[3,384,128]{2,1,0:T(8,128)S(1)}, f32[3,384,128]{2,1,0:T(8,128)S(1)}, u32[]{:S(2)}, u32[]{:S(2)}) collective-permute-start(f32[3,384,128]{2,1,0:T(8,128)S(1)} %get-tuple-element.48.refs_3_), channel_id=1, source_target_pairs={{0,4},{4,0},{8,12},{12,8},{16,20},{20,16},{24,28},{28,24},{1,5},{5... | collective-permute-start | bytes 1769480 | tf_op jit(solution)/shard_map/ppermute | solution.py:34
  44.3 4.2 %collective-permute-done.15.refs_1_ = bf16[2048,128]{1,0:T(8,128)(2,1)S(1)} collective-permute-done((bf16[2048,128]{1,0:T(8,128)(2,1)S(1)}, bf16[2048,128]{1,0:T(8,128)(2,1)S(1)}, u32[]{:S(2)}, u32[]{:S(2)}) %collective-permute-start.15) | collective-permute-done | bytes 524320 | tf_op jit(solution)/shard_map/ppermute | solution.py:34
  48.5 0.0 collective-permute-done.16.refs_2_
  48.5 0.6 shard_map.65.refs_3_
  49.1 0.2 collective-permute-start.18
  49.3 0.4 collective-permute-start.12
  49.7 2.6 %collective-permute-start.13 = (bf16[384,128]{1,0:T(8,128)(2,1)S(1)}, bf16[384,128]{1,0:T(8,128)(2,1)S(1)}, u32[]{:S(2)}, u32[]{:S(2)}) collective-permute-start(bf16[384,128]{1,0:T(8,128)(2,1)S(1)} %get-tuple-element.44), channel_id=1, source_target_pairs={{0,2},{1,3},{2,0},{3,1},{4,6},{5,7},{6,4},{7,5},{8,10},{9,11},{10,... | collective-permute-start | bytes 294920 | tf_op jit(solution)/shard_map/ppermute | solution.py:34
  52.3 0.5 collective-permute-start.14
  52.8 0.6 shard_map.66.refs_1_
  53.4 1.1 %collective-permute-done.12.refs_1_ = bf16[384,128]{1,0:T(8,128)(2,1)S(1)} collective-permute-done((bf16[384,128]{1,0:T(8,128)(2,1)S(1)}, bf16[384,128]{1,0:T(8,128)(2,1)S(1)}, u32[]{:S(2)}, u32[]{:S(2)}) %collective-permute-start.12) | collective-permute-done | bytes 98336 | tf_op jit(solution)/shard_map/ppermute | solution.py:34
  54.4 5.3 %collective-permute-done.13.refs_2_ = bf16[384,128]{1,0:T(8,128)(2,1)S(1)} collective-permute-done((bf16[384,128]{1,0:T(8,128)(2,1)S(1)}, bf16[384,128]{1,0:T(8,128)(2,1)S(1)}, u32[]{:S(2)}, u32[]{:S(2)}) %collective-permute-start.13) | collective-permute-done | bytes 98336 | tf_op jit(solution)/shard_map/ppermute | solution.py:34
  59.7 2.2 %collective-permute-done.14.refs_3_ = bf16[384,128]{1,0:T(8,128)(2,1)S(1)} collective-permute-done((bf16[384,128]{1,0:T(8,128)(2,1)S(1)}, bf16[384,128]{1,0:T(8,128)(2,1)S(1)}, u32[]{:S(2)}, u32[]{:S(2)}) %collective-permute-start.14) | collective-permute-done | bytes 98336 | tf_op jit(solution)/shard_map/ppermute | solution.py:34
  62.0 0.0 collective-permute-done.17.refs_2_
  62.0 0.1 shard_map.67
  62.1 0.2 collective-permute-start.19
  62.3 2.9 %collective-permute-start.20 = (bf16[384,128]{1,0:T(8,128)(2,1)S(1)}, bf16[384,128]{1,0:T(8,128)(2,1)S(1)}, u32[]{:S(2)}, u32[]{:S(2)}) collective-permute-start(bf16[384,128]{1,0:T(8,128)(2,1)S(1)} %get-tuple-element.51), channel_id=1, source_target_pairs={{0,2},{1,3},{2,0},{3,1},{4,6},{5,7},{6,4},{7,5},{8,10},{9,11},{10,... | collective-permute-start | bytes 294920 | tf_op jit(solution)/shard_map/ppermute | solution.py:34
  65.3 0.4 collective-permute-start.21
  65.7 2.1 %collective-permute-done.19.refs_2_ = bf16[384,128]{1,0:T(8,128)(2,1)S(1)} collective-permute-done((bf16[384,128]{1,0:T(8,128)(2,1)S(1)}, bf16[384,128]{1,0:T(8,128)(2,1)S(1)}, u32[]{:S(2)}, u32[]{:S(2)}) %collective-permute-start.19) | collective-permute-done | bytes 98336 | tf_op jit(solution)/shard_map/ppermute | solution.py:34
  67.8 3.7 %collective-permute-done.20.refs_3_ = bf16[384,128]{1,0:T(8,128)(2,1)S(1)} collective-permute-done((bf16[384,128]{1,0:T(8,128)(2,1)S(1)}, bf16[384,128]{1,0:T(8,128)(2,1)S(1)}, u32[]{:S(2)}, u32[]{:S(2)}) %collective-permute-start.20) | collective-permute-done | bytes 98336 | tf_op jit(solution)/shard_map/ppermute | solution.py:34
  71.4 2.3 %collective-permute-done.21.refs_4_ = bf16[384,128]{1,0:T(8,128)(2,1)S(1)} collective-permute-done((bf16[384,128]{1,0:T(8,128)(2,1)S(1)}, bf16[384,128]{1,0:T(8,128)(2,1)S(1)}, u32[]{:S(2)}, u32[]{:S(2)}) %collective-permute-start.21) | collective-permute-done | bytes 98336 | tf_op jit(solution)/shard_map/ppermute | solution.py:34
  73.7 0.3 shard_map.68
  74.0 1.9 %collective-permute-start.24 = (f32[128,256]{1,0:T(8,128)S(1)}, f32[128,256]{1,0:T(8,128)S(1)}, u32[]{:S(2)}, u32[]{:S(2)}) collective-permute-start(f32[128,256]{1,0:T(8,128)S(1)} %get-tuple-element.58), channel_id=1, source_target_pairs={{0,4},{4,8},{8,12},{12,16},{16,20},{20,24},{24,28},{1,5},{5,9},{9,... | collective-permute-start | bytes 393224 | tf_op jit(solution)/shard_map/ppermute | solution.py:29
  76.0 4.5 %collective-permute-start.23 = (bf16[128,256]{1,0:T(8,128)(2,1)S(1)}, bf16[128,256]{1,0:T(8,128)(2,1)S(1)}, u32[]{:S(2)}, u32[]{:S(2)}) collective-permute-start(bf16[128,256]{1,0:T(8,128)(2,1)S(1)} %get-tuple-element.57), channel_id=1, source_target_pairs={{4,0},{8,4},{12,8},{16,12},{20,16},{24,20},{28,24},{5,1},{9,5},{13... | collective-permute-start | bytes 196616 | tf_op jit(solution)/shard_map/ppermute | solution.py:29
  80.5 1.9 %collective-permute-start.22 = (bf16[128,128]{1,0:T(8,128)(2,1)S(1)}, bf16[128,128]{1,0:T(8,128)(2,1)S(1)}, u32[]{:S(2)}, u32[]{:S(2)}) collective-permute-start(bf16[128,128]{1,0:T(8,128)(2,1)S(1)} %get-tuple-element.55), channel_id=1, source_target_pairs={{0,4},{4,8},{8,12},{12,16},{16,20},{20,24},{24,28},{1,5},{5,9},{9,... | collective-permute-start | bytes 98312 | tf_op jit(solution)/shard_map/ppermute | solution.py:29
  82.4 4.2 %collective-permute-done.22.refs_2_ = bf16[128,128]{1,0:T(8,128)(2,1)S(1)} collective-permute-done((bf16[128,128]{1,0:T(8,128)(2,1)S(1)}, bf16[128,128]{1,0:T(8,128)(2,1)S(1)}, u32[]{:S(2)}, u32[]{:S(2)}) %collective-permute-start.22) | collective-permute-done | bytes 32800 | tf_op jit(solution)/shard_map/ppermute | solution.py:29
  86.7 0.7 shard_map.69.refs_0_
  87.4 0.0 collective-permute-done.23.refs_3_
  87.4 0.0 collective-permute-done.24.refs_4_
  87.4 1.0 %shard_map.70 = f32[384,256]{1,0:T(8,128)} custom-call(f32[384,256]{1,0:T(8,128)S(1)} %shard_map.69.refs_0_, bf16[512,512]{1,0:T(8,128)(2,1)S(1)} %get-tuple-element.34.refs_2_.refs_5_.refs_1_, bf16[384,128]{1,0:T(8,128)(2,1)S(1)} %get-tuple-element.56.refs_4_.refs_2_, bf16[128,256]{1,0:T(8,128)(2,1)S(1)} %collective-permute-done.23.refs_3_, ...), custom_call_target="tpu_custom_call" | custom-call | bytes 1024 | tf_op jit(solution)/shard_map/pallas_call | solution.py:43
  (12 shorter events, 0.2 us)
Async XLA Ops:
  0.0 2.9 %copy-start = (bf16[384,4096]{1,0:T(8,128)(2,1)S(1)}, bf16[384,4096]{1,0:T(8,128)(2,1)}, u32[]{:S(2)}) copy-start(bf16[384,4096]{1,0:T(8,128)(2,1)} %refs_0_.11) | copy-start | bytes 9437188
  0.0 2.9 %collective-permute-start = (bf16[4096,128]{1,0:T(8,128)(2,1)}, bf16[4096,128]{1,0:T(8,128)(2,1)S(1)}, u32[]{:S(2)}, u32[]{:S(2)}) collective-permute-start(bf16[4096,128]{1,0:T(8,128)(2,1)} %refs_0_.6), channel_id=1, source_target_pairs={{0,4},{4,0},{8,12},{12,8},{16,20},{20,16},{24,28},{28,24},{1,5},{5... | collective-permute-start | bytes 3145736 | tf_op jit(solution)/shard_map/ppermute | solution.py:34
  0.0 1.4 %copy-start.1 = (bf16[4096,128]{1,0:T(8,128)(2,1)S(1)}, bf16[4096,128]{1,0:T(8,128)(2,1)}, u32[]{:S(2)}) copy-start(bf16[4096,128]{1,0:T(8,128)(2,1)} %refs_0_.6) | copy-start | bytes 3145732
  1.4 9.0 %copy-start.2 = (bf16[1,512,512]{2,1,0:T(8,128)(2,1)S(1)}, bf16[1,512,512]{2,1,0:T(8,128)(2,1)}, u32[]{:S(2)}) copy-start(bf16[1,512,512]{2,1,0:T(8,128)(2,1)} %refs_0_.7) | copy-start | bytes 1572868
  1.4 9.0 %copy-start.4 = (s32[128]{0:T(128)S(1)}, s32[128]{0:T(128)}, u32[]{:S(2)}) copy-start(s32[128]{0:T(128)} %param.9) | copy-start | bytes 1540
  2.9 21.4 %collective-permute-start.1 = (bf16[384,4096]{1,0:T(8,128)(2,1)S(1)}, bf16[384,4096]{1,0:T(8,128)(2,1)S(1)}, u32[]{:S(2)}, u32[]{:S(2)}) collective-permute-start(bf16[384,4096]{1,0:T(8,128)(2,1)S(1)} %copy-done), channel_id=1, source_target_pairs={{0,4},{4,0},{8,12},{12,8},{16,20},{20,16},{24,28},{28,24},{1,5},{5... | collective-permute-start | bytes 9437192 | tf_op jit(solution)/shard_map/ppermute | solution.py:34
  3.1 13.7 %collective-permute-start.2 = (bf16[2048,128]{1,0:T(8,128)(2,1)S(1)}, bf16[2048,128]{1,0:T(8,128)(2,1)S(1)}, u32[]{:S(2)}, u32[]{:S(2)}) collective-permute-start(bf16[2048,128]{1,0:T(8,128)(2,1)S(1)} %shard_map.55.refs_1_.refs_2_), channel_id=1, source_target_pairs={{0,8},{8,0},{16,24},{24,16},{1,9},{9,1},{17,25},{25,17},{2,10},{10... | collective-permute-start | bytes 1572872 | tf_op jit(solution)/shard_map/ppermute | solution.py:34
  6.5 11.8 %collective-permute-start.3 = (bf16[2048,128]{1,0:T(8,128)(2,1)S(1)}, bf16[2048,128]{1,0:T(8,128)(2,1)S(1)}, u32[]{:S(2)}, u32[]{:S(2)}) collective-permute-start(bf16[2048,128]{1,0:T(8,128)(2,1)S(1)} %shard_map.56.refs_0_.refs_3_), channel_id=1, source_target_pairs={{4,20},{12,28},{20,4},{28,12},{5,21},{13,29},{21,5},{29,13},{6,22}... | collective-permute-start | bytes 1572872 | tf_op jit(solution)/shard_map/ppermute | solution.py:34
  7.2 14.0 %collective-permute-start.5 = (bf16[2048,128]{1,0:T(8,128)(2,1)S(1)}, bf16[2048,128]{1,0:T(8,128)(2,1)S(1)}, u32[]{:S(2)}, u32[]{:S(2)}) collective-permute-start(bf16[2048,128]{1,0:T(8,128)(2,1)S(1)} %shard_map.55.refs_1_.refs_2_), channel_id=1, source_target_pairs={{0,16},{8,24},{16,0},{24,8},{1,17},{9,25},{17,1},{25,9},{2,18},{10... | collective-permute-start | bytes 1572872 | tf_op jit(solution)/shard_map/ppermute | solution.py:34
  9.7 14.0 %collective-permute-start.4 = (bf16[2048,128]{1,0:T(8,128)(2,1)S(1)}, bf16[2048,128]{1,0:T(8,128)(2,1)S(1)}, u32[]{:S(2)}, u32[]{:S(2)}) collective-permute-start(bf16[2048,128]{1,0:T(8,128)(2,1)S(1)} %shard_map.56.refs_0_.refs_3_), channel_id=1, source_target_pairs={{4,12},{12,4},{20,28},{28,20},{5,13},{13,5},{21,29},{29,21},{6,14}... | collective-permute-start | bytes 1572872 | tf_op jit(solution)/shard_map/ppermute | solution.py:34
  10.4 0.7 copy-start.3
  16.8 14.9 %collective-permute-start.8 = (bf16[2048,128]{1,0:T(8,128)(2,1)S(1)}, bf16[2048,128]{1,0:T(8,128)(2,1)S(1)}, u32[]{:S(2)}, u32[]{:S(2)}) collective-permute-start(bf16[2048,128]{1,0:T(8,128)(2,1)S(1)} %shard_map.58.refs_2_), channel_id=1, source_target_pairs={{0,8},{4,12},{8,0},{12,4},{16,24},{20,28},{24,16},{28,20},{1,9},{5... | collective-permute-start | bytes 1572872 | tf_op jit(solution)/shard_map/ppermute | solution.py:34
  18.3 13.4 %collective-permute-start.9 = (bf16[2048,128]{1,0:T(8,128)(2,1)S(1)}, bf16[2048,128]{1,0:T(8,128)(2,1)S(1)}, u32[]{:S(2)}, u32[]{:S(2)}) collective-permute-start(bf16[2048,128]{1,0:T(8,128)(2,1)S(1)} %shard_map.58.refs_2_), channel_id=1, source_target_pairs={{0,16},{4,20},{8,24},{12,28},{16,0},{20,4},{24,8},{28,12},{1,17},{... | collective-permute-start | bytes 1572872 | tf_op jit(solution)/shard_map/ppermute | solution.py:34
  21.2 15.6 %collective-permute-start.6 = (bf16[2048,128]{1,0:T(8,128)(2,1)S(1)}, bf16[2048,128]{1,0:T(8,128)(2,1)S(1)}, u32[]{:S(2)}, u32[]{:S(2)}) collective-permute-start(bf16[2048,128]{1,0:T(8,128)(2,1)S(1)} %collective-permute-done.2.refs_4_), channel_id=1, source_target_pairs={{0,16},{8,24},{16,0},{24,8},{1,17},{9,25},{17,1},{25,9},{2,18},{10... | collective-permute-start | bytes 1572872 | tf_op jit(solution)/shard_map/ppermute | solution.py:34
  23.6 13.1 %collective-permute-start.7 = (bf16[2048,128]{1,0:T(8,128)(2,1)S(1)}, bf16[2048,128]{1,0:T(8,128)(2,1)S(1)}, u32[]{:S(2)}, u32[]{:S(2)}) collective-permute-start(bf16[2048,128]{1,0:T(8,128)(2,1)S(1)} %collective-permute-done.3.refs_7_), channel_id=1, source_target_pairs={{4,12},{12,4},{20,28},{28,20},{5,13},{13,5},{21,29},{29,21},{6,14}... | collective-permute-start | bytes 1572872 | tf_op jit(solution)/shard_map/ppermute | solution.py:34
  26.2 15.0 %collective-permute-start.10 = (f32[3,384,128]{2,1,0:T(8,128)S(1)}, f32[3,384,128]{2,1,0:T(8,128)S(1)}, u32[]{:S(2)}, u32[]{:S(2)}) collective-permute-start(f32[3,384,128]{2,1,0:T(8,128)S(1)} %get-tuple-element.39.refs_3_), channel_id=1, source_target_pairs={{0,4},{4,0},{8,12},{12,8},{16,20},{20,16},{24,28},{28,24},{1,5},{5... | collective-permute-start | bytes 1769480 | tf_op jit(solution)/shard_map/ppermute | solution.py:34
  37.4 3.8 %collective-permute-start.11 = (f32[384,128]{1,0:T(8,128)S(1)}, f32[384,128]{1,0:T(8,128)S(1)}, u32[]{:S(2)}, u32[]{:S(2)}) collective-permute-start(f32[384,128]{1,0:T(8,128)S(1)} %shard_map.60.refs_3_), channel_id=1, source_target_pairs={{0,4},{4,0},{8,12},{12,8},{16,20},{20,16},{24,28},{28,24},{1,5},{5... | collective-permute-start | bytes 589832 | tf_op jit(solution)/shard_map/ppermute | solution.py:34
  37.4 11.1 %collective-permute-start.15 = (bf16[2048,128]{1,0:T(8,128)(2,1)S(1)}, bf16[2048,128]{1,0:T(8,128)(2,1)S(1)}, u32[]{:S(2)}, u32[]{:S(2)}) collective-permute-start(bf16[2048,128]{1,0:T(8,128)(2,1)S(1)} %collective-permute-done.8.refs_4_.refs_3_), channel_id=1, source_target_pairs={{0,16},{8,24},{16,0},{24,8},{1,17},{9,25},{17,1},{25,9},{2,18},{10... | collective-permute-start | bytes 1572872 | tf_op jit(solution)/shard_map/ppermute | solution.py:34
  39.9 8.7 %collective-permute-start.16 = (bf16[2048,128]{1,0:T(8,128)(2,1)S(1)}, bf16[2048,128]{1,0:T(8,128)(2,1)S(1)}, u32[]{:S(2)}, u32[]{:S(2)}) collective-permute-start(bf16[2048,128]{1,0:T(8,128)(2,1)S(1)} %collective-permute-done.9.refs_5_.refs_4_), channel_id=1, source_target_pairs={{4,12},{12,4},{20,28},{28,20},{5,13},{13,5},{21,29},{29,21},{6,14}... | collective-permute-start | bytes 1572872 | tf_op jit(solution)/shard_map/ppermute | solution.py:34
  43.1 18.9 %collective-permute-start.17 = (f32[3,384,128]{2,1,0:T(8,128)S(1)}, f32[3,384,128]{2,1,0:T(8,128)S(1)}, u32[]{:S(2)}, u32[]{:S(2)}) collective-permute-start(f32[3,384,128]{2,1,0:T(8,128)S(1)} %get-tuple-element.48.refs_3_), channel_id=1, source_target_pairs={{0,4},{4,0},{8,12},{12,8},{16,20},{20,16},{24,28},{28,24},{1,5},{5... | collective-permute-start | bytes 1769480 | tf_op jit(solution)/shard_map/ppermute | solution.py:34
  49.1 12.9 %collective-permute-start.18 = (f32[384,128]{1,0:T(8,128)S(1)}, f32[384,128]{1,0:T(8,128)S(1)}, u32[]{:S(2)}, u32[]{:S(2)}) collective-permute-start(f32[384,128]{1,0:T(8,128)S(1)} %shard_map.65.refs_3_), channel_id=1, source_target_pairs={{0,4},{4,0},{8,12},{12,8},{16,20},{20,16},{24,28},{28,24},{1,5},{5... | collective-permute-start | bytes 589832 | tf_op jit(solution)/shard_map/ppermute | solution.py:34
  49.3 5.1 %collective-permute-start.12 = (bf16[384,128]{1,0:T(8,128)(2,1)S(1)}, bf16[384,128]{1,0:T(8,128)(2,1)S(1)}, u32[]{:S(2)}, u32[]{:S(2)}) collective-permute-start(bf16[384,128]{1,0:T(8,128)(2,1)S(1)} %get-tuple-element.43.refs_5_), channel_id=1, source_target_pairs={{0,1},{1,0},{2,3},{3,2},{4,5},{5,4},{6,7},{7,6},{8,9},{9,8},{10,11... | collective-permute-start | bytes 294920 | tf_op jit(solution)/shard_map/ppermute | solution.py:34
  49.7 10.0 %collective-permute-start.13 = (bf16[384,128]{1,0:T(8,128)(2,1)S(1)}, bf16[384,128]{1,0:T(8,128)(2,1)S(1)}, u32[]{:S(2)}, u32[]{:S(2)}) collective-permute-start(bf16[384,128]{1,0:T(8,128)(2,1)S(1)} %get-tuple-element.44), channel_id=1, source_target_pairs={{0,2},{1,3},{2,0},{3,1},{4,6},{5,7},{6,4},{7,5},{8,10},{9,11},{10,... | collective-permute-start | bytes 294920 | tf_op jit(solution)/shard_map/ppermute | solution.py:34
  52.3 9.6 %collective-permute-start.14 = (bf16[384,128]{1,0:T(8,128)(2,1)S(1)}, bf16[384,128]{1,0:T(8,128)(2,1)S(1)}, u32[]{:S(2)}, u32[]{:S(2)}) collective-permute-start(bf16[384,128]{1,0:T(8,128)(2,1)S(1)} %get-tuple-element.45), channel_id=1, source_target_pairs={{0,3},{1,2},{2,1},{3,0},{4,7},{5,6},{6,5},{7,4},{8,11},{9,10},{10,... | collective-permute-start | bytes 294920 | tf_op jit(solution)/shard_map/ppermute | solution.py:34
  62.1 5.7 %collective-permute-start.19 = (bf16[384,128]{1,0:T(8,128)(2,1)S(1)}, bf16[384,128]{1,0:T(8,128)(2,1)S(1)}, u32[]{:S(2)}, u32[]{:S(2)}) collective-permute-start(bf16[384,128]{1,0:T(8,128)(2,1)S(1)} %get-tuple-element.50), channel_id=1, source_target_pairs={{0,1},{1,0},{2,3},{3,2},{4,5},{5,4},{6,7},{7,6},{8,9},{9,8},{10,11... | collective-permute-start | bytes 294920 | tf_op jit(solution)/shard_map/ppermute | solution.py:34
  62.3 9.1 %collective-permute-start.20 = (bf16[384,128]{1,0:T(8,128)(2,1)S(1)}, bf16[384,128]{1,0:T(8,128)(2,1)S(1)}, u32[]{:S(2)}, u32[]{:S(2)}) collective-permute-start(bf16[384,128]{1,0:T(8,128)(2,1)S(1)} %get-tuple-element.51), channel_id=1, source_target_pairs={{0,2},{1,3},{2,0},{3,1},{4,6},{5,7},{6,4},{7,5},{8,10},{9,11},{10,... | collective-permute-start | bytes 294920 | tf_op jit(solution)/shard_map/ppermute | solution.py:34
  65.3 8.4 %collective-permute-start.21 = (bf16[384,128]{1,0:T(8,128)(2,1)S(1)}, bf16[384,128]{1,0:T(8,128)(2,1)S(1)}, u32[]{:S(2)}, u32[]{:S(2)}) collective-permute-start(bf16[384,128]{1,0:T(8,128)(2,1)S(1)} %get-tuple-element.52), channel_id=1, source_target_pairs={{0,3},{1,2},{2,1},{3,0},{4,7},{5,6},{6,5},{7,4},{8,11},{9,10},{10,... | collective-permute-start | bytes 294920 | tf_op jit(solution)/shard_map/ppermute | solution.py:34
  74.0 13.4 %collective-permute-start.24 = (f32[128,256]{1,0:T(8,128)S(1)}, f32[128,256]{1,0:T(8,128)S(1)}, u32[]{:S(2)}, u32[]{:S(2)}) collective-permute-start(f32[128,256]{1,0:T(8,128)S(1)} %get-tuple-element.58), channel_id=1, source_target_pairs={{0,4},{4,8},{8,12},{12,16},{16,20},{20,24},{24,28},{1,5},{5,9},{9,... | collective-permute-start | bytes 393224 | tf_op jit(solution)/shard_map/ppermute | solution.py:29
  76.0 11.4 %collective-permute-start.23 = (bf16[128,256]{1,0:T(8,128)(2,1)S(1)}, bf16[128,256]{1,0:T(8,128)(2,1)S(1)}, u32[]{:S(2)}, u32[]{:S(2)}) collective-permute-start(bf16[128,256]{1,0:T(8,128)(2,1)S(1)} %get-tuple-element.57), channel_id=1, source_target_pairs={{4,0},{8,4},{12,8},{16,12},{20,16},{24,20},{28,24},{5,1},{9,5},{13... | collective-permute-start | bytes 196616 | tf_op jit(solution)/shard_map/ppermute | solution.py:29
  80.5 6.1 %collective-permute-start.22 = (bf16[128,128]{1,0:T(8,128)(2,1)S(1)}, bf16[128,128]{1,0:T(8,128)(2,1)S(1)}, u32[]{:S(2)}, u32[]{:S(2)}) collective-permute-start(bf16[128,128]{1,0:T(8,128)(2,1)S(1)} %get-tuple-element.55), channel_id=1, source_target_pairs={{0,4},{4,8},{8,12},{12,16},{16,20},{20,24},{24,28},{1,5},{5,9},{9,... | collective-permute-start | bytes 98312 | tf_op jit(solution)/shard_map/ppermute | solution.py:29

commit v5 on v4

v5 whole, which is shorter than its diff:
```python
import functools

import jax
import jax.numpy as jnp
from jax import lax
from jax.experimental import pallas as pl
from jax.experimental.pallas import tpu as pltpu
from jax.sharding import PartitionSpec as P

CORE, NEAR, FAR = 1, 2, 4
VMEM = pl.BlockSpec(memory_space=pltpu.VMEM)
ANY = pl.BlockSpec(memory_space=pl.ANY)
F32, BF16 = jnp.float32, jnp.bfloat16


def dot(left, right):
    precision = lax.Precision.HIGHEST if left.dtype == F32 else None
    return jnp.dot(left, right, precision=precision, preferred_element_type=F32)


def split(value):
    high = value.astype(BF16)
    return high, (value - high.astype(F32)).astype(BF16)


def shifted(value, axis, steps):
    count = lax.axis_size(axis)
    leading, last = (max(0, -steps), min(count, count - steps))
    return lax.ppermute(value, axis, [(source, source + steps) for source in range(leading, last)])


def exchanged(value, axis, mask, core=None):
    sources = range(lax.axis_size(axis))
    return lax.ppermute(value, axis, [(source, source ^ mask) for source in sources if core in (None, source & CORE)])


def call(kernel, outs, operands, after=(), spaces=None, scratch=()):
    count = len(operands)

    def body(*refs):
        kernel(*refs[:count], *refs[count + len(after) :])

    return pl.pallas_call(
        body,
        out_shape=outs,
        in_specs=[pl.BlockSpec(memory_space=space) for space in spaces or [pltpu.VMEM] * count] + [ANY] * len(after),
        out_specs=[VMEM] * len(outs),
        scratch_shapes=list(scratch),
        cost_estimate=pl.CostEstimate(flops=0, bytes_accessed=1024, transcendentals=0),
        compiler_params=pltpu.CompilerParams(vmem_limit_bytes=24 * 2**20),
    )(*operands, *after)


def shape(*dims, dtype=F32):
    return jax.ShapeDtypeStruct(dims, dtype)


def core():
    return lax.rem(lax.axis_index("domain"), 2)


def block_of_band():
    return lax.bitwise_xor(lax.div(lax.axis_index("domain"), 2), lax.axis_index("band"))


def multiply(mine, theirs, pieces, store):
    rows, width = mine.shape[0], pieces[0].shape[1]
    for first in range(0, len(pieces), 2):
        group = pieces[first : first + 2]
        wide = group[0] if len(group) == 1 else jnp.concatenate(group, 1)
        for side, states in enumerate((mine, theirs)):
            result = jnp.dot(states[...], wide, preferred_element_type=F32)
            for slot in range(len(group)):
                store(first + slot, slice(side * rows, (side + 1) * rows), result[:, slot * width : (slot + 1) * width])


def halves_kernel(near_even, far_even, near_odd, far_odd, top, bottom, done):
    half = top.shape[0]

    def fill(near, far):
        copies = [
            pltpu.make_async_copy(near.at[pl.ds(0, half)], top, done.at[0]),
            pltpu.make_async_copy(far.at[pl.ds(half, half)], bottom, done.at[1]),
        ]
        for copy in copies:
            copy.start()
        for copy in copies:
            copy.wait()

    pl.when(core() == 0)(lambda: fill(near_even, far_even))
    pl.when(core() != 0)(lambda: fill(near_odd, far_odd))


def early_kernel(mine, theirs, own, near_even, far_even, near_odd, far_odd, blocks):
    def store(slot, rows, value):
        blocks[slot, rows] = value

    first = core() == 0
    near, far = jnp.where(first, near_even[...], near_odd[...]), jnp.where(first, far_even[...], far_odd[...])
    multiply(mine, theirs, [own[...], near, far], store)


def late_kernel(mine, theirs, top, bottom, early, kept, *refs):
    sent, last = refs[:-1], refs[-1]
    half = top.shape[0]
    rows = mine.shape[0]
    for side, states in enumerate((mine, theirs)):
        result = jnp.dot(states[:, :half], top[...], preferred_element_type=F32)
        last[side * rows : (side + 1) * rows] = result + jnp.dot(states[:, half:], bottom[...], preferred_element_type=F32)
    count = early.shape[0]
    where = block_of_band()
    for mask, out in enumerate((kept, *sent)):
        slot = lax.bitwise_xor(where, mask)

        @pl.when(slot < count)
        def _():
            out[...] = early[jnp.minimum(slot, count - 1)].astype(out.dtype)

        @pl.when(slot == count)
        def _():
            out[...] = last[...].astype(out.dtype)


def sum_kernel(kept, *refs):
    parts, (mine, theirs) = refs[:-2], refs[-2:]
    value = kept[...]
    for part in parts:
        value = value + part[...].astype(F32)
    rows = mine.shape[0]
    mine[...] = value[:rows]
    theirs[...] = value[rows:]


def rotate_square(wavefunctions, rotation, operator):
    bands, chips = lax.axis_size("band"), lax.axis_size("domain") // 2
    rows, states = wavefunctions.shape
    width = rotation.shape[1]
    half = states // 2
    received = [exchanged(rotation, "domain", NEAR, 0), exchanged(rotation, "domain", FAR, 0)]
    theirs = exchanged(wavefunctions, "domain", CORE)
    operator = operator()
    later, _, _ = lax.optimization_barrier((rotation, theirs, operator[1]))
    received += [exchanged(later, "domain", NEAR, CORE), exchanged(later, "domain", FAR, CORE)]
    halves = [shape(half, width, dtype=BF16)] * 2
    top, bottom = call(halves_kernel, halves, received, scratch=[pltpu.SemaphoreType.DMA((2,))])
    top, bottom = exchanged(top, "domain", FAR), exchanged(bottom, "domain", NEAR)
    early = call(early_kernel, [shape(chips - 1, 2 * rows, width)], (wavefunctions, theirs, rotation, *received))[0]
    outs = [shape(2 * rows, width)] + [shape(2 * rows, width, dtype=BF16)] * (bands - 1)
    scratch = [pltpu.VMEM((2 * rows, width), F32)]
    kept, *sent = call(late_kernel, outs, (wavefunctions, theirs, top, bottom, early), scratch=scratch)
    parts = [exchanged(value, "band", mask) for mask, value in enumerate(sent, 1)]
    mine, others = call(sum_kernel, [shape(rows, width)] * 2, (kept, *parts))
    return mine, exchanged(others, "domain", CORE), operator


def rotate_any(wavefunctions, rotation):
    columns = lax.all_gather(rotation, "domain", axis=1, tiled=True)
    return lax.psum_scatter(dot(wavefunctions, columns), "band", scatter_dimension=1, tiled=True)


def faces_kernel(mine, other, assembled, pick, total, faces, back):
    own, width = mine.shape
    first = core() == 0
    for side, half in enumerate((jnp.where(first, mine[...], other[...]), jnp.where(first, other[...], mine[...]))):
        columns = slice(side * width, (side + 1) * width)
        total[:, columns] = half
        high, low = split(half)
        faces[:, columns] = dot(pick[...], high).astype(BF16)
        outward = assembled[own:, :own]
        back[:, columns] = dot(outward, high) + dot(outward, low)


def inner_kernel(total, assembled, corner, pick, spread, out):
    own = total.shape[0]
    high, low = split(total[...])
    inner = assembled[:own, :own]
    face_high, face_low = dot(pick[...], high).astype(BF16), dot(pick[...], low).astype(BF16)
    back_high, back_low = split(dot(corner[...], face_high) + dot(corner[...], face_low))
    out[...] = dot(inner, high) + dot(inner, low) + dot(spread[...], back_high) + dot(spread[...], back_low)


def final_kernel(inner, assembled, spread, incoming, back, out):
    own = inner.shape[0]
    high, low = split(back[...])
    out[...] = inner[...] + dot(assembled[:own, own:], incoming[...]) + dot(spread[...], high) + dot(spread[...], low)


def finish_square(mine, other, operator):
    assembled, corner, pick, spread = operator
    rows, width = mine.shape
    shared, columns = pick.shape[0], 2 * width
    outs = [shape(rows, columns), shape(shared, columns, dtype=BF16), shape(shared, columns)]
    total, faces, back = call(faces_kernel, outs, (mine, other, assembled, pick))
    incoming, back = shifted(faces, "domain", -1), shifted(back, "domain", 1)
    inner = call(inner_kernel, [shape(rows, columns)], (total, assembled, corner, pick, spread))[0]
    return call(final_kernel, [shape(rows, columns)], (inner, assembled, spread, incoming, back))[0]


def finish_any(rotated, cell_matrices, cell_nodes, face_map):
    own = rotated.shape[0]
    assembled, pick, returned = assemble_any(cell_matrices, cell_nodes, face_map, own)
    rotated = rotated.astype(BF16).astype(assembled.dtype)
    incoming = shifted(dot(pick, rotated).astype(BF16), "domain", -1).astype(assembled.dtype)
    back = shifted(dot(assembled[own:, :own], rotated), "domain", 1)
    inner = dot(assembled[:own, :own], rotated) + dot(returned, rotated) + dot(assembled[:own, own:], incoming)
    return inner + dot(pick.T.astype(F32), back)


def assemble_any(cell_matrices, cell_nodes, face_map, own):
    cells = cell_nodes.shape[0]
    extent = own + face_map.shape[0]
    held = BF16 if cells == 1 else F32
    places = jax.nn.one_hot(cell_nodes, extent, dtype=held)
    assembled = jnp.zeros((extent, extent), F32)
    for cell in range(cells):
        rows = dot(places[cell].T, cell_matrices[cell].astype(held)).astype(held)
        assembled = assembled + dot(rows, places[cell])
    assembled = assembled.astype(held)
    pick = jax.nn.one_hot(face_map, own, dtype=held)
    corner = shifted(assembled[own:, own:], "domain", 1)
    returned = dot(dot(pick.T, corner).astype(held), pick).astype(held)
    return assembled, pick, returned


def assemble_kernel(matrix, nodes, faces, assembled, corner, pick, spread):
    own, extent = spread.shape[0], assembled.shape[0]
    places = jnp.where(lax.broadcasted_iota(jnp.int32, (extent, extent), 0) == nodes[...], 1.0, 0.0).astype(BF16)
    rows = dot(places, matrix[0]).astype(BF16)
    whole = lax.dot_general(rows, places, (((1,), (1,)), ((), ())), preferred_element_type=F32).astype(BF16)
    assembled[...] = whole
    corner[...] = whole[own:, own:]
    chosen = jnp.where(lax.broadcasted_iota(jnp.int32, spread.shape, 0) == faces[...], 1.0, 0.0)
    spread[...] = chosen.astype(BF16)
    pick[...] = chosen.T.astype(BF16)


def assemble(cell_matrices, cell_nodes, face_map, own):
    shared = face_map.shape[0]
    outs = [(own + shared, own + shared), (shared, shared), (shared, own), (own, shared)]
    operands = (cell_matrices, cell_nodes, face_map.reshape(1, shared))
    assembled, corner, pick, spread = call(assemble_kernel, [shape(*dims, dtype=BF16) for dims in outs], operands)
    return assembled, shifted(corner, "domain", 1), pick, spread


def local(wavefunctions, rotation, cell_matrices, cell_nodes, face_map):
    chips = lax.axis_size("domain") // 2
    if chips == FAR and chips == lax.axis_size("band") and cell_nodes.shape[0] == 1:
        operator = functools.partial(assemble, cell_matrices, cell_nodes, face_map, wavefunctions.shape[0])
        return finish_square(*rotate_square(wavefunctions, rotation, operator))
    return finish_any(rotate_any(wavefunctions, rotation), cell_matrices, cell_nodes, face_map)


def solution(mesh):
    in_specs = (
        P("domain", "band"),
        P("band", "domain"),
        P("domain", None, None),
        P("domain", None),
        P("domain"),
    )
    out_specs = P("domain", "band")
    return jax.shard_map(local, mesh=mesh, in_specs=in_specs, out_specs=out_specs, check_vma=False)
```

time: 88.8 us -> 87 us (0.980)
  the two profiles are of different devices: /device:TPU:12 before, /device:TPU:1 now
where the time goes in v5:
time: 87 us; the launch traced here: 85.3 us
  waiting for transfers between devices  49.3 us (57%)
  starting transfers between devices  24.8 us (29%)
  Pallas kernels  8.29 us (10%)
  local copies, waits for them, and re-layouts  2.7 us (3%)
    ppermute x11, waiting for transfers between devices, exchanged(): lax.ppermute(value, axis, [(source, source ^ mask) for source in sources...  46.4 us
    ppermute x11, starting transfers between devices, exchanged(): lax.ppermute(value, axis, [(source, source ^ mask) for source in sources...  15 us
    ppermute x3, starting transfers between devices, shifted(): lax.ppermute(value, axis, [(source, source + steps) for source in range(l...  9.81 us
    pallas_call x8, Pallas kernels, call(): pl.pallas_call(body, out_shape=outs, in_specs=[pl.BlockSpec(memory_space=...  8.29 us
    ppermute x3, waiting for transfers between devices, shifted(): lax.ppermute(value, axis, [(source, source + steps) for source in range(l...  2.91 us
    unnamed x10, local copies, waits for them, and re-layouts  2.7 us
  transfers between devices with their start and end apart: 14, of which 8 were waited for; matrix products, arithmetic and copies ran while one was open for 0% of the time, Pallas kernels for 6%

profile of v5, /device:TPU:1, one launch (start us, length us, event | category | flops | bytes accessed | tf_op | source)
XLA Modules:
  0.0 85.3 jit_solution(8396142236376971020)
XLA Ops:
  0.0 0.0 copy-start
  0.0 0.0 copy-start.1
  0.0 0.1 collective-permute-start
  0.1 0.0 copy-start.2
  0.1 1.2 %copy-done.2 = bf16[1,512,512]{2,1,0:T(8,128)(2,1)S(1)} copy-done((bf16[1,512,512]{2,1,0:T(8,128)(2,1)S(1)}, bf16[1,512,512]{2,1,0:T(8,128)(2,1)}, u32[]{:S(2)}) %copy-start.2) | copy-done | bytes 524312
  1.3 0.0 copy-start.3
  1.3 0.8 copy-done.3
  2.1 0.0 copy-start.4
  2.1 0.7 copy-done.4
  2.8 0.7 shard_map.55
  3.5 4.5 %collective-permute-start.3 = (bf16[128,128]{1,0:T(8,128)(2,1)S(1)}, bf16[128,128]{1,0:T(8,128)(2,1)S(1)}, u32[]{:S(2)}, u32[]{:S(2)}) collective-permute-start(bf16[128,128]{1,0:T(8,128)(2,1)S(1)} %get-tuple-element.21), channel_id=1, source_target_pairs={{0,4},{4,8},{8,12},{12,16},{16,20},{20,24},{24,28},{1,5},{5,9},{9,... | collective-permute-start | bytes 98312 | tf_op jit(solution)/shard_map/ppermute | solution.py:29
  8.0 0.7 collective-permute-start.2
  8.7 0.7 collective-permute-start.1
  9.5 0.0 collective-permute-done.3.refs_2_
  9.5 0.0 collective-permute-done.refs_1_
  9.5 3.1 %collective-permute-start.5 = (bf16[4096,128]{1,0:T(8,128)(2,1)}, bf16[4096,128]{1,0:T(8,128)(2,1)S(1)}, u32[]{:S(2)}, u32[]{:S(2)}) collective-permute-start(bf16[4096,128]{1,0:T(8,128)(2,1)} %refs_2_.1), channel_id=1, source_target_pairs={{4,20},{12,28},{20,4},{28,12},{5,21},{13,29},{21,5},{29,13},{6,22}... | collective-permute-start | bytes 3145736 | tf_op jit(solution)/shard_map/ppermute | solution.py:34
  12.6 1.9 %collective-permute-start.4 = (bf16[4096,128]{1,0:T(8,128)(2,1)}, bf16[4096,128]{1,0:T(8,128)(2,1)S(1)}, u32[]{:S(2)}, u32[]{:S(2)}) collective-permute-start(bf16[4096,128]{1,0:T(8,128)(2,1)} %refs_2_.1), channel_id=1, source_target_pairs={{4,12},{12,4},{20,28},{28,20},{5,13},{13,5},{21,29},{29,21},{6,14}... | collective-permute-start | bytes 3145736 | tf_op jit(solution)/shard_map/ppermute | solution.py:34
  14.6 0.0 collective-permute-done.2.refs_1_.refs_4_
  14.6 0.0 collective-permute-done.1.refs_0_.refs_3_
  14.6 20.0 %collective-permute-done.5.refs_3_.refs_6_ = bf16[4096,128]{1,0:T(8,128)(2,1)S(1)} collective-permute-done((bf16[4096,128]{1,0:T(8,128)(2,1)}, bf16[4096,128]{1,0:T(8,128)(2,1)S(1)}, u32[]{:S(2)}, u32[]{:S(2)}) %collective-permute-start.5) | collective-permute-done | bytes 1048608 | tf_op jit(solution)/shard_map/ppermute | solution.py:34
  34.6 3.6 %collective-permute-done.4.refs_2_.refs_5_ = bf16[4096,128]{1,0:T(8,128)(2,1)S(1)} collective-permute-done((bf16[4096,128]{1,0:T(8,128)(2,1)}, bf16[4096,128]{1,0:T(8,128)(2,1)S(1)}, u32[]{:S(2)}, u32[]{:S(2)}) %collective-permute-start.4) | collective-permute-done | bytes 1048608 | tf_op jit(solution)/shard_map/ppermute | solution.py:34
  38.2 0.1 shard_map.56
  38.3 0.1 collective-permute-start.6
  38.4 1.4 %collective-permute-start.7 = (bf16[2048,128]{1,0:T(8,128)(2,1)S(1)}, bf16[2048,128]{1,0:T(8,128)(2,1)S(1)}, u32[]{:S(2)}, u32[]{:S(2)}) collective-permute-start(bf16[2048,128]{1,0:T(8,128)(2,1)S(1)} %get-tuple-element.24), channel_id=1, source_target_pairs={{0,8},{4,12},{8,0},{12,4},{16,24},{20,28},{24,16},{28,20},{1,9},{5... | collective-permute-start | bytes 1572872 | tf_op jit(solution)/shard_map/ppermute | solution.py:34
  39.8 0.0 copy-done
  39.9 0.0 copy-done.1
  39.9 3.4 %shard_map.57.refs_4_ = f32[3,768,128]{2,1,0:T(8,128)S(1)} custom-call(bf16[384,4096]{1,0:T(8,128)(2,1)S(1)} %copy-done, bf16[384,4096]{1,0:T(8,128)(2,1)S(1)} %collective-permute-done.refs_1_, bf16[4096,128]{1,0:T(8,128)(2,1)S(1)} %copy-done.1, bf16[4096,128]{1,0:T(8,128)(2,1)S(1)} %collective-permute-done.1.refs_0_.refs_3_, ...), custom_call_target="tpu_custom_call" | custom-call | bytes 1024 | tf_op jit(solution)/shard_map/pallas_call | solution.py:43
  43.3 9.0 %collective-permute-done.6.refs_2_ = bf16[2048,128]{1,0:T(8,128)(2,1)S(1)} collective-permute-done((bf16[2048,128]{1,0:T(8,128)(2,1)S(1)}, bf16[2048,128]{1,0:T(8,128)(2,1)S(1)}, u32[]{:S(2)}, u32[]{:S(2)}) %collective-permute-start.6) | collective-permute-done | bytes 524320 | tf_op jit(solution)/shard_map/ppermute | solution.py:34
  52.3 0.0 collective-permute-done.7.refs_3_
  52.3 1.9 %shard_map.58 = (f32[768,128]{1,0:T(8,128)S(1)}, bf16[768,128]{1,0:T(8,128)(2,1)S(1)}, bf16[768,128]{1,0:T(8,128)(2,1)S(1)}, bf16[768,128]{1,0:T(8,128)(2,1)S(1)}) custom-call(bf16[384,4096]{1,0:T(8,128)(2,1)S(1)} %copy-done, bf16[384,4096]{1,0:T(8,128)(2,1)S(1)} %collective-permute-done.refs_1_, bf16[2048,128]{1,0:T(8,128)(2,1)S(1)} %collective-permute-done.6.refs_2_, ...), custom_call_target="tpu_custom_call" | custom-call | bytes 1024 | tf_op jit(solution)/shard_map/pallas_call | solution.py:43
  54.2 1.4 %collective-permute-start.8 = (bf16[768,128]{1,0:T(8,128)(2,1)S(1)}, bf16[768,128]{1,0:T(8,128)(2,1)S(1)}, u32[]{:S(2)}, u32[]{:S(2)}) collective-permute-start(bf16[768,128]{1,0:T(8,128)(2,1)S(1)} %get-tuple-element.26), channel_id=1, source_target_pairs={{0,1},{1,0},{2,3},{3,2},{4,5},{5,4},{6,7},{7,6},{8,9},{9,8},{10,11... | collective-permute-start | bytes 589832 | tf_op jit(solution)/shard_map/ppermute | solution.py:34
  55.5 2.3 %collective-permute-start.9 = (bf16[768,128]{1,0:T(8,128)(2,1)S(1)}, bf16[768,128]{1,0:T(8,128)(2,1)S(1)}, u32[]{:S(2)}, u32[]{:S(2)}) collective-permute-start(bf16[768,128]{1,0:T(8,128)(2,1)S(1)} %get-tuple-element.27), channel_id=1, source_target_pairs={{0,2},{1,3},{2,0},{3,1},{4,6},{5,7},{6,4},{7,5},{8,10},{9,11},{10,... | collective-permute-start | bytes 589832 | tf_op jit(solution)/shard_map/ppermute | solution.py:34
  57.9 0.0 collective-permute-start.10
  57.9 5.3 %collective-permute-done.8.refs_1_ = bf16[768,128]{1,0:T(8,128)(2,1)S(1)} collective-permute-done((bf16[768,128]{1,0:T(8,128)(2,1)S(1)}, bf16[768,128]{1,0:T(8,128)(2,1)S(1)}, u32[]{:S(2)}, u32[]{:S(2)}) %collective-permute-start.8) | collective-permute-done | bytes 196640 | tf_op jit(solution)/shard_map/ppermute | solution.py:34
  63.2 0.1 collective-permute-done.9.refs_2_
  63.3 7.2 %collective-permute-done.10.refs_3_ = bf16[768,128]{1,0:T(8,128)(2,1)S(1)} collective-permute-done((bf16[768,128]{1,0:T(8,128)(2,1)S(1)}, bf16[768,128]{1,0:T(8,128)(2,1)S(1)}, u32[]{:S(2)}, u32[]{:S(2)}) %collective-permute-start.10) | collective-permute-done | bytes 196640 | tf_op jit(solution)/shard_map/ppermute | solution.py:34
  70.5 0.1 shard_map.59
  70.6 3.2 %collective-permute-start.11 = (f32[384,128]{1,0:T(8,128)S(1)}, f32[384,128]{1,0:T(8,128)S(1)}, u32[]{:S(2)}, u32[]{:S(2)}) collective-permute-start(f32[384,128]{1,0:T(8,128)S(1)} %get-tuple-element.30), channel_id=1, source_target_pairs={{0,4},{4,0},{8,12},{12,8},{16,20},{20,16},{24,28},{28,24},{1,5},{5... | collective-permute-start | bytes 589832 | tf_op jit(solution)/shard_map/ppermute | solution.py:34
  73.8 1.1 %collective-permute-done.11.refs_1_ = f32[384,128]{1,0:T(8,128)S(1)} collective-permute-done((f32[384,128]{1,0:T(8,128)S(1)}, f32[384,128]{1,0:T(8,128)S(1)}, u32[]{:S(2)}, u32[]{:S(2)}) %collective-permute-start.11) | collective-permute-done | bytes 196640 | tf_op jit(solution)/shard_map/ppermute | solution.py:34
  74.9 0.3 shard_map.60
  75.2 3.4 %collective-permute-start.13 = (f32[128,256]{1,0:T(8,128)S(1)}, f32[128,256]{1,0:T(8,128)S(1)}, u32[]{:S(2)}, u32[]{:S(2)}) collective-permute-start(f32[128,256]{1,0:T(8,128)S(1)} %get-tuple-element.36), channel_id=1, source_target_pairs={{0,4},{4,8},{8,12},{12,16},{16,20},{20,24},{24,28},{1,5},{5,9},{9,... | collective-permute-start | bytes 393224 | tf_op jit(solution)/shard_map/ppermute | solution.py:29
  78.6 1.9 %collective-permute-start.12 = (bf16[128,256]{1,0:T(8,128)(2,1)S(1)}, bf16[128,256]{1,0:T(8,128)(2,1)S(1)}, u32[]{:S(2)}, u32[]{:S(2)}) collective-permute-start(bf16[128,256]{1,0:T(8,128)(2,1)S(1)} %get-tuple-element.35), channel_id=1, source_target_pairs={{4,0},{8,4},{12,8},{16,12},{20,16},{24,20},{28,24},{5,1},{9,5},{13... | collective-permute-start | bytes 196616 | tf_op jit(solution)/shard_map/ppermute | solution.py:29
  80.6 0.7 shard_map.61.refs_0_
  81.3 2.9 %collective-permute-done.12.refs_3_ = bf16[128,256]{1,0:T(8,128)(2,1)S(1)} collective-permute-done((bf16[128,256]{1,0:T(8,128)(2,1)S(1)}, bf16[128,256]{1,0:T(8,128)(2,1)S(1)}, u32[]{:S(2)}, u32[]{:S(2)}) %collective-permute-start.12) | collective-permute-done | bytes 65568 | tf_op jit(solution)/shard_map/ppermute | solution.py:29
  84.2 0.0 collective-permute-done.13.refs_4_
  84.2 1.0 %shard_map.62 = f32[384,256]{1,0:T(8,128)} custom-call(f32[384,256]{1,0:T(8,128)S(1)} %shard_map.61.refs_0_, bf16[512,512]{1,0:T(8,128)(2,1)S(1)} %get-tuple-element.31.refs_2_.refs_1_, bf16[384,128]{1,0:T(8,128)(2,1)S(1)} %get-tuple-element.34.refs_4_.refs_2_, bf16[128,256]{1,0:T(8,128)(2,1)S(1)} %collective-permute-done.12.refs_3_, ...), custom_call_target="tpu_custom_call" | custom-call | bytes 1024 | tf_op jit(solution)/shard_map/pallas_call | solution.py:43
Async XLA Ops:
  0.0 39.8 %copy-start = (bf16[384,4096]{1,0:T(8,128)(2,1)S(1)}, bf16[384,4096]{1,0:T(8,128)(2,1)}, u32[]{:S(2)}) copy-start(bf16[384,4096]{1,0:T(8,128)(2,1)} %refs_0_.5) | copy-start | bytes 9437188
  0.0 39.8 %copy-start.1 = (bf16[4096,128]{1,0:T(8,128)(2,1)S(1)}, bf16[4096,128]{1,0:T(8,128)(2,1)}, u32[]{:S(2)}) copy-start(bf16[4096,128]{1,0:T(8,128)(2,1)} %refs_2_.1) | copy-start | bytes 3145732
  0.0 9.5 %collective-permute-start = (bf16[384,4096]{1,0:T(8,128)(2,1)}, bf16[384,4096]{1,0:T(8,128)(2,1)S(1)}, u32[]{:S(2)}, u32[]{:S(2)}) collective-permute-start(bf16[384,4096]{1,0:T(8,128)(2,1)} %refs_0_.5), channel_id=1, source_target_pairs={{0,4},{4,0},{8,12},{12,8},{16,20},{20,16},{24,28},{28,24},{1,5},{5... | collective-permute-start | bytes 9437192 | tf_op jit(solution)/shard_map/ppermute | solution.py:34
  0.1 1.2 %copy-start.2 = (bf16[1,512,512]{2,1,0:T(8,128)(2,1)S(1)}, bf16[1,512,512]{2,1,0:T(8,128)(2,1)}, u32[]{:S(2)}) copy-start(bf16[1,512,512]{2,1,0:T(8,128)(2,1)} %refs_0_.3) | copy-start | bytes 1572868
  1.3 0.8 copy-start.3
  2.1 0.7 copy-start.4
  3.5 6.0 %collective-permute-start.3 = (bf16[128,128]{1,0:T(8,128)(2,1)S(1)}, bf16[128,128]{1,0:T(8,128)(2,1)S(1)}, u32[]{:S(2)}, u32[]{:S(2)}) collective-permute-start(bf16[128,128]{1,0:T(8,128)(2,1)S(1)} %get-tuple-element.21), channel_id=1, source_target_pairs={{0,4},{4,8},{8,12},{12,16},{16,20},{20,24},{24,28},{1,5},{5,9},{9,... | collective-permute-start | bytes 98312 | tf_op jit(solution)/shard_map/ppermute | solution.py:29
  8.0 6.6 %collective-permute-start.2 = (bf16[4096,128]{1,0:T(8,128)(2,1)}, bf16[4096,128]{1,0:T(8,128)(2,1)S(1)}, u32[]{:S(2)}, u32[]{:S(2)}) collective-permute-start(bf16[4096,128]{1,0:T(8,128)(2,1)} %refs_2_.1), channel_id=1, source_target_pairs={{0,16},{8,24},{16,0},{24,8},{1,17},{9,25},{17,1},{25,9},{2,18},{10... | collective-permute-start | bytes 3145736 | tf_op jit(solution)/shard_map/ppermute | solution.py:34
  8.7 5.9 %collective-permute-start.1 = (bf16[4096,128]{1,0:T(8,128)(2,1)}, bf16[4096,128]{1,0:T(8,128)(2,1)S(1)}, u32[]{:S(2)}, u32[]{:S(2)}) collective-permute-start(bf16[4096,128]{1,0:T(8,128)(2,1)} %refs_2_.1), channel_id=1, source_target_pairs={{0,8},{8,0},{16,24},{24,16},{1,9},{9,1},{17,25},{25,17},{2,10},{10... | collective-permute-start | bytes 3145736 | tf_op jit(solution)/shard_map/ppermute | solution.py:34
  9.5 25.1 %collective-permute-start.5 = (bf16[4096,128]{1,0:T(8,128)(2,1)}, bf16[4096,128]{1,0:T(8,128)(2,1)S(1)}, u32[]{:S(2)}, u32[]{:S(2)}) collective-permute-start(bf16[4096,128]{1,0:T(8,128)(2,1)} %refs_2_.1), channel_id=1, source_target_pairs={{4,20},{12,28},{20,4},{28,12},{5,21},{13,29},{21,5},{29,13},{6,22}... | collective-permute-start | bytes 3145736 | tf_op jit(solution)/shard_map/ppermute | solution.py:34
  12.6 25.6 %collective-permute-start.4 = (bf16[4096,128]{1,0:T(8,128)(2,1)}, bf16[4096,128]{1,0:T(8,128)(2,1)S(1)}, u32[]{:S(2)}, u32[]{:S(2)}) collective-permute-start(bf16[4096,128]{1,0:T(8,128)(2,1)} %refs_2_.1), channel_id=1, source_target_pairs={{4,12},{12,4},{20,28},{28,20},{5,13},{13,5},{21,29},{29,21},{6,14}... | collective-permute-start | bytes 3145736 | tf_op jit(solution)/shard_map/ppermute | solution.py:34
  38.3 13.9 %collective-permute-start.6 = (bf16[2048,128]{1,0:T(8,128)(2,1)S(1)}, bf16[2048,128]{1,0:T(8,128)(2,1)S(1)}, u32[]{:S(2)}, u32[]{:S(2)}) collective-permute-start(bf16[2048,128]{1,0:T(8,128)(2,1)S(1)} %get-tuple-element.23), channel_id=1, source_target_pairs={{0,16},{4,20},{8,24},{12,28},{16,0},{20,4},{24,8},{28,12},{1,17},{... | collective-permute-start | bytes 1572872 | tf_op jit(solution)/shard_map/ppermute | solution.py:34
  38.4 13.8 %collective-permute-start.7 = (bf16[2048,128]{1,0:T(8,128)(2,1)S(1)}, bf16[2048,128]{1,0:T(8,128)(2,1)S(1)}, u32[]{:S(2)}, u32[]{:S(2)}) collective-permute-start(bf16[2048,128]{1,0:T(8,128)(2,1)S(1)} %get-tuple-element.24), channel_id=1, source_target_pairs={{0,8},{4,12},{8,0},{12,4},{16,24},{20,28},{24,16},{28,20},{1,9},{5... | collective-permute-start | bytes 1572872 | tf_op jit(solution)/shard_map/ppermute | solution.py:34
  54.2 9.1 %collective-permute-start.8 = (bf16[768,128]{1,0:T(8,128)(2,1)S(1)}, bf16[768,128]{1,0:T(8,128)(2,1)S(1)}, u32[]{:S(2)}, u32[]{:S(2)}) collective-permute-start(bf16[768,128]{1,0:T(8,128)(2,1)S(1)} %get-tuple-element.26), channel_id=1, source_target_pairs={{0,1},{1,0},{2,3},{3,2},{4,5},{5,4},{6,7},{7,6},{8,9},{9,8},{10,11... | collective-permute-start | bytes 589832 | tf_op jit(solution)/shard_map/ppermute | solution.py:34
  55.5 7.8 %collective-permute-start.9 = (bf16[768,128]{1,0:T(8,128)(2,1)S(1)}, bf16[768,128]{1,0:T(8,128)(2,1)S(1)}, u32[]{:S(2)}, u32[]{:S(2)}) collective-permute-start(bf16[768,128]{1,0:T(8,128)(2,1)S(1)} %get-tuple-element.27), channel_id=1, source_target_pairs={{0,2},{1,3},{2,0},{3,1},{4,6},{5,7},{6,4},{7,5},{8,10},{9,11},{10,... | collective-permute-start | bytes 589832 | tf_op jit(solution)/shard_map/ppermute | solution.py:34
  57.9 12.6 %collective-permute-start.10 = (bf16[768,128]{1,0:T(8,128)(2,1)S(1)}, bf16[768,128]{1,0:T(8,128)(2,1)S(1)}, u32[]{:S(2)}, u32[]{:S(2)}) collective-permute-start(bf16[768,128]{1,0:T(8,128)(2,1)S(1)} %get-tuple-element.28), channel_id=1, source_target_pairs={{0,3},{1,2},{2,1},{3,0},{4,7},{5,6},{6,5},{7,4},{8,11},{9,10},{10,... | collective-permute-start | bytes 589832 | tf_op jit(solution)/shard_map/ppermute | solution.py:34
  70.6 4.3 %collective-permute-start.11 = (f32[384,128]{1,0:T(8,128)S(1)}, f32[384,128]{1,0:T(8,128)S(1)}, u32[]{:S(2)}, u32[]{:S(2)}) collective-permute-start(f32[384,128]{1,0:T(8,128)S(1)} %get-tuple-element.30), channel_id=1, source_target_pairs={{0,4},{4,0},{8,12},{12,8},{16,20},{20,16},{24,28},{28,24},{1,5},{5... | collective-permute-start | bytes 589832 | tf_op jit(solution)/shard_map/ppermute | solution.py:34
  75.2 9.0 %collective-permute-start.13 = (f32[128,256]{1,0:T(8,128)S(1)}, f32[128,256]{1,0:T(8,128)S(1)}, u32[]{:S(2)}, u32[]{:S(2)}) collective-permute-start(f32[128,256]{1,0:T(8,128)S(1)} %get-tuple-element.36), channel_id=1, source_target_pairs={{0,4},{4,8},{8,12},{12,16},{16,20},{20,24},{24,28},{1,5},{5,9},{9,... | collective-permute-start | bytes 393224 | tf_op jit(solution)/shard_map/ppermute | solution.py:29
  78.6 5.6 %collective-permute-start.12 = (bf16[128,256]{1,0:T(8,128)(2,1)S(1)}, bf16[128,256]{1,0:T(8,128)(2,1)S(1)}, u32[]{:S(2)}, u32[]{:S(2)}) collective-permute-start(bf16[128,256]{1,0:T(8,128)(2,1)S(1)} %get-tuple-element.35), channel_id=1, source_target_pairs={{4,0},{8,4},{12,8},{16,12},{20,16},{24,20},{28,24},{5,1},{9,5},{13... | collective-permute-start | bytes 196616 | tf_op jit(solution)/shard_map/ppermute | solution.py:29

commit v6 on v5

--- a/solution.py
+++ b/solution.py
@@ -63,17 +63,6 @@
     return lax.bitwise_xor(lax.div(lax.axis_index("domain"), 2), lax.axis_index("band"))
 
 
-def multiply(mine, theirs, pieces, store):
-    rows, width = mine.shape[0], pieces[0].shape[1]
-    for first in range(0, len(pieces), 2):
-        group = pieces[first : first + 2]
-        wide = group[0] if len(group) == 1 else jnp.concatenate(group, 1)
-        for side, states in enumerate((mine, theirs)):
-            result = jnp.dot(states[...], wide, preferred_element_type=F32)
-            for slot in range(len(group)):
-                store(first + slot, slice(side * rows, (side + 1) * rows), result[:, slot * width : (slot + 1) * width])
-
-
 def halves_kernel(near_even, far_even, near_odd, far_odd, top, bottom, done):
     half = top.shape[0]
 
@@ -91,34 +80,40 @@
     pl.when(core() != 0)(lambda: fill(near_odd, far_odd))
 
 
-def early_kernel(mine, theirs, own, near_even, far_even, near_odd, far_odd, blocks):
-    def store(slot, rows, value):
-        blocks[slot, rows] = value
-
+def own_kernel(mine, theirs, own, block):
+    rows = mine.shape[0]
+    for side, states in enumerate((mine, theirs)):
+        block[side * rows : (side + 1) * rows] = jnp.dot(states[...], own[...], preferred_element_type=F32)
+
+
+def early_kernel(mine, theirs, near_even, far_even, near_odd, far_odd, near_block, far_block):
+    rows, width = mine.shape[0], near_even.shape[1]
     first = core() == 0
     near, far = jnp.where(first, near_even[...], near_odd[...]), jnp.where(first, far_even[...], far_odd[...])
-    multiply(mine, theirs, [own[...], near, far], store)
-
-
-def late_kernel(mine, theirs, top, bottom, early, kept, *refs):
+    wide = jnp.concatenate([near, far], 1)
+    for side, states in enumerate((mine, theirs)):
+        result = jnp.dot(states[...], wide, preferred_element_type=F32)
+        near_block[side * rows : (side + 1) * rows] = result[:, :width]
+        far_block[side * rows : (side + 1) * rows] = result[:, width:]
+
+
+def late_kernel(mine, theirs, top, bottom, own, near, far, kept, *refs):
     sent, last = refs[:-1], refs[-1]
     half = top.shape[0]
     rows = mine.shape[0]
     for side, states in enumerate((mine, theirs)):
         result = jnp.dot(states[:, :half], top[...], preferred_element_type=F32)
         last[side * rows : (side + 1) * rows] = result + jnp.dot(states[:, half:], bottom[...], preferred_element_type=F32)
-    count = early.shape[0]
     where = block_of_band()
+
+    def store(out, slot, block):
+        @pl.when(slot == lax.bitwise_xor(where, mask))
+        def _():
+            out[...] = block[...].astype(out.dtype)
+
     for mask, out in enumerate((kept, *sent)):
-        slot = lax.bitwise_xor(where, mask)
-
-        @pl.when(slot < count)
-        def _():
-            out[...] = early[jnp.minimum(slot, count - 1)].astype(out.dtype)
-
-        @pl.when(slot == count)
-        def _():
-            out[...] = last[...].astype(out.dtype)
+        for slot, block in enumerate((own, near, far, last)):
+            store(out, slot, block)
 
 
 def sum_kernel(kept, *refs):
@@ -138,16 +133,18 @@
     half = states // 2
     received = [exchanged(rotation, "domain", NEAR, 0), exchanged(rotation, "domain", FAR, 0)]
     theirs = exchanged(wavefunctions, "domain", CORE)
-    operator = operator()
-    later, _, _ = lax.optimization_barrier((rotation, theirs, operator[1]))
+    block = [shape(2 * rows, width)]
+    own = call(own_kernel, block, (wavefunctions, theirs, rotation))[0]
+    operator = operator(own)
+    later, _ = lax.optimization_barrier((rotation, operator[0]))
     received += [exchanged(later, "domain", NEAR, CORE), exchanged(later, "domain", FAR, CORE)]
     halves = [shape(half, width, dtype=BF16)] * 2
     top, bottom = call(halves_kernel, halves, received, scratch=[pltpu.SemaphoreType.DMA((2,))])
     top, bottom = exchanged(top, "domain", FAR), exchanged(bottom, "domain", NEAR)
-    early = call(early_kernel, [shape(chips - 1, 2 * rows, width)], (wavefunctions, theirs, rotation, *received))[0]
-    outs = [shape(2 * rows, width)] + [shape(2 * rows, width, dtype=BF16)] * (bands - 1)
+    early = call(early_kernel, block * 2, (wavefunctions, theirs, *received))
+    outs = block + [shape(2 * rows, width, dtype=BF16)] * (bands - 1)
     scratch = [pltpu.VMEM((2 * rows, width), F32)]
-    kept, *sent = call(late_kernel, outs, (wavefunctions, theirs, top, bottom, early), scratch=scratch)
+    kept, *sent = call(late_kernel, outs, (wavefunctions, theirs, top, bottom, own, *early), scratch=scratch)
     parts = [exchanged(value, "band", mask) for mask, value in enumerate(sent, 1)]
     mine, others = call(sum_kernel, [shape(rows, width)] * 2, (kept, *parts))
     return mine, exchanged(others, "domain", CORE), operator
@@ -168,32 +165,35 @@
         faces[:, columns] = dot(pick[...], high).astype(BF16)
         outward = assembled[own:, :own]
         back[:, columns] = dot(outward, high) + dot(outward, low)
-
-
-def inner_kernel(total, assembled, corner, pick, spread, out):
+    back[:, 2 * width :] = assembled[own:, own:].astype(F32)
+
+
+def inner_kernel(total, assembled, pick, out, face_high, face_low):
     own = total.shape[0]
     high, low = split(total[...])
     inner = assembled[:own, :own]
-    face_high, face_low = dot(pick[...], high).astype(BF16), dot(pick[...], low).astype(BF16)
-    back_high, back_low = split(dot(corner[...], face_high) + dot(corner[...], face_low))
-    out[...] = dot(inner, high) + dot(inner, low) + dot(spread[...], back_high) + dot(spread[...], back_low)
-
-
-def final_kernel(inner, assembled, spread, incoming, back, out):
-    own = inner.shape[0]
-    high, low = split(back[...])
+    out[...] = dot(inner, high) + dot(inner, low)
+    face_high[...] = dot(pick[...], high).astype(BF16)
+    face_low[...] = dot(pick[...], low).astype(BF16)
+
+
+def final_kernel(inner, face_high, face_low, assembled, spread, incoming, back, out):
+    own, columns = inner.shape
+    corner = back[:, columns:].astype(BF16)
+    high, low = split(back[:, :columns] + dot(corner, face_high[...]) + dot(corner, face_low[...]))
     out[...] = inner[...] + dot(assembled[:own, own:], incoming[...]) + dot(spread[...], high) + dot(spread[...], low)
 
 
 def finish_square(mine, other, operator):
-    assembled, corner, pick, spread = operator
+    assembled, pick, spread = operator
     rows, width = mine.shape
     shared, columns = pick.shape[0], 2 * width
-    outs = [shape(rows, columns), shape(shared, columns, dtype=BF16), shape(shared, columns)]
+    outs = [shape(rows, columns), shape(shared, columns, dtype=BF16), shape(shared, columns + shared)]
     total, faces, back = call(faces_kernel, outs, (mine, other, assembled, pick))
     incoming, back = shifted(faces, "domain", -1), shifted(back, "domain", 1)
-    inner = call(inner_kernel, [shape(rows, columns)], (total, assembled, corner, pick, spread))[0]
-    return call(final_kernel, [shape(rows, columns)], (inner, assembled, spread, incoming, back))[0]
+    outs = [shape(rows, columns)] + [shape(shared, columns, dtype=BF16)] * 2
+    inner, *face = call(inner_kernel, outs, (total, assembled, pick))
+    return call(final_kernel, outs[:1], (inner, *face, assembled, spread, incoming, back))[0]
 
 
 def finish_any(rotated, cell_matrices, cell_nodes, face_map):
@@ -222,24 +222,22 @@
     return assembled, pick, returned
 
 
-def assemble_kernel(matrix, nodes, faces, assembled, corner, pick, spread):
-    own, extent = spread.shape[0], assembled.shape[0]
+def assemble_kernel(matrix, nodes, faces, assembled, pick, spread):
+    extent = assembled.shape[0]
     places = jnp.where(lax.broadcasted_iota(jnp.int32, (extent, extent), 0) == nodes[...], 1.0, 0.0).astype(BF16)
     rows = dot(places, matrix[0]).astype(BF16)
-    whole = lax.dot_general(rows, places, (((1,), (1,)), ((), ())), preferred_element_type=F32).astype(BF16)
-    assembled[...] = whole
-    corner[...] = whole[own:, own:]
+    whole = lax.dot_general(rows, places, (((1,), (1,)), ((), ())), preferred_element_type=F32)
+    assembled[...] = whole.astype(BF16)
     chosen = jnp.where(lax.broadcasted_iota(jnp.int32, spread.shape, 0) == faces[...], 1.0, 0.0)
     spread[...] = chosen.astype(BF16)
     pick[...] = chosen.T.astype(BF16)
 
 
-def assemble(cell_matrices, cell_nodes, face_map, own):
+def assemble(cell_matrices, cell_nodes, face_map, own, after):
     shared = face_map.shape[0]
-    outs = [(own + shared, own + shared), (shared, shared), (shared, own), (own, shared)]
+    outs = [(own + shared, own + shared), (shared, own), (own, shared)]
     operands = (cell_matrices, cell_nodes, face_map.reshape(1, shared))
-    assembled, corner, pick, spread = call(assemble_kernel, [shape(*dims, dtype=BF16) for dims in outs], operands)
-    return assembled, shifted(corner, "domain", 1), pick, spread
+    return call(assemble_kernel, [shape(*dims, dtype=BF16) for dims in outs], operands, after=(after,))
 
 
 def local(wavefunctions, rotation, cell_matrices, cell_nodes, face_map):

time: 87 us -> 73.2 us (0.84)
  waiting for transfers between devices: 49.3 us -> 41.3 us
  starting transfers between devices: 24.8 us -> 19.2 us
    ppermute x11, waiting for transfers between devices: 46.4 us -> 38.1 us  [exchanged(): lax.ppermute(value, axis, [(source, source ^ mask) for source in sources...]
    ppermute x3 -> x2, starting transfers between devices: 9.81 us -> 5.04 us  [shifted(): lax.ppermute(value, axis, [(source, source + steps) for source in range(l...]
    ppermute x11, starting transfers between devices: 15 us -> 14.1 us  [exchanged(): lax.ppermute(value, axis, [(source, source ^ mask) for source in sources...]
    unnamed x10 -> x14, local copies, waits for them, and re-layouts: 2.7 us -> 3.13 us
    ppermute x3 -> x2, waiting for transfers between devices: 2.91 us -> 3.2 us  [shifted(): lax.ppermute(value, axis, [(source, source + steps) for source in range(l...]
    pallas_call x8 -> x9, Pallas kernels: 8.29 us -> 8.37 us  [call(): pl.pallas_call(body, out_shape=outs, in_specs=[pl.BlockSpec(memory_space=...]
  transfers between devices with their start and end apart: 14 -> 13, of which waited for: 8 -> 9; matrix products, arithmetic and copies ran while one was open for 0% -> 0% of each run, Pallas kernels for 6% -> 7%
where the time goes in v6:
time: 73.2 us; the launch traced here: 72.2 us
  waiting for transfers between devices  41.3 us (56%)
  starting transfers between devices  19.2 us (26%)
  Pallas kernels  8.37 us (11%)
  local copies, waits for them, and re-layouts  3.13 us (4%)
    ppermute x11, waiting for transfers between devices, exchanged(): lax.ppermute(value, axis, [(source, source ^ mask) for source in sources...  38.1 us
    ppermute x11, starting transfers between devices, exchanged(): lax.ppermute(value, axis, [(source, source ^ mask) for source in sources...  14.1 us
    pallas_call x9, Pallas kernels, call(): pl.pallas_call(body, out_shape=outs, in_specs=[pl.BlockSpec(memory_space=...  8.37 us
    ppermute x2, starting transfers between devices, shifted(): lax.ppermute(value, axis, [(source, source + steps) for source in range(l...  5.04 us
    ppermute x2, waiting for transfers between devices, shifted(): lax.ppermute(value, axis, [(source, source + steps) for source in range(l...  3.2 us
    unnamed x14, local copies, waits for them, and re-layouts  3.13 us
  transfers between devices with their start and end apart: 13, of which 9 were waited for; matrix products, arithmetic and copies ran while one was open for 0% of the time, Pallas kernels for 7%

profile of v6, /device:TPU:1, one launch (start us, length us, event | category | flops | bytes accessed | tf_op | source)
XLA Modules:
  0.0 72.2 jit_solution(2401999448239153364)
XLA Ops:
  0.0 0.1 collective-permute-start
  0.1 0.7 collective-permute-start.2
  0.8 0.7 %collective-permute-start.1 = (bf16[4096,128]{1,0:T(8,128)(2,1)}, bf16[4096,128]{1,0:T(8,128)(2,1)S(1)}, u32[]{:S(2)}, u32[]{:S(2)}) collective-permute-start(bf16[4096,128]{1,0:T(8,128)(2,1)} %refs_2_.1), channel_id=1, source_target_pairs={{0,8},{8,0},{16,24},{24,16},{1,9},{9,1},{17,25},{25,17},{2,10},{10... | collective-permute-start | bytes 3145736 | tf_op jit(solution)/shard_map/ppermute | solution.py:34
  1.5 4.4 %collective-permute-done.refs_1_ = bf16[384,4096]{1,0:T(8,128)(2,1)S(1)} collective-permute-done((bf16[384,4096]{1,0:T(8,128)(2,1)}, bf16[384,4096]{1,0:T(8,128)(2,1)S(1)}, u32[]{:S(2)}, u32[]{:S(2)}) %collective-permute-start) | collective-permute-done | bytes 3145760 | tf_op jit(solution)/shard_map/ppermute | solution.py:34
  5.9 0.0 copy-start
  5.9 1.9 %copy-done = bf16[384,4096]{1,0:T(8,128)(2,1)S(1)} copy-done((bf16[384,4096]{1,0:T(8,128)(2,1)S(1)}, bf16[384,4096]{1,0:T(8,128)(2,1)}, u32[]{:S(2)}) %copy-start) | copy-done | bytes 3145752
  7.8 0.0 copy-start.2
  7.8 1.2 %copy-done.2 = bf16[4096,128]{1,0:T(8,128)(2,1)S(1)} copy-done((bf16[4096,128]{1,0:T(8,128)(2,1)S(1)}, bf16[4096,128]{1,0:T(8,128)(2,1)}, u32[]{:S(2)}) %copy-start.2) | copy-done | bytes 1048600
  9.0 0.0 copy-start.4
  9.0 0.0 copy-start.5
  9.0 0.0 copy-start.6
  9.0 0.0 copy-start.3
  9.0 1.8 %shard_map.55.refs_3_.refs_4_ = f32[768,128]{1,0:T(8,128)S(1)} custom-call(bf16[384,4096]{1,0:T(8,128)(2,1)S(1)} %copy-done, bf16[384,4096]{1,0:T(8,128)(2,1)S(1)} %collective-permute-done.refs_1_, bf16[4096,128]{1,0:T(8,128)(2,1)S(1)} %copy-done.2), custom_call_target="tpu_custom_call" | custom-call | bytes 1024 | tf_op jit(solution)/shard_map/pallas_call | solution.py:43
  10.8 0.0 copy-start.1
  10.8 0.0 copy-done.4
  10.8 0.0 copy-done.5
  10.8 0.0 copy-done.6
  10.8 0.7 shard_map.56
  11.5 0.0 copy-done.3
  11.5 4.4 %collective-permute-start.4 = (bf16[4096,128]{1,0:T(8,128)(2,1)S(1)}, bf16[4096,128]{1,0:T(8,128)(2,1)S(1)}, u32[]{:S(2)}, u32[]{:S(2)}) collective-permute-start(bf16[4096,128]{1,0:T(8,128)(2,1)S(1)} %copy-done.3), channel_id=1, source_target_pairs={{4,20},{12,28},{20,4},{28,12},{5,21},{13,29},{21,5},{29,13},{6,22}... | collective-permute-start | bytes 3145736 | tf_op jit(solution)/shard_map/ppermute | solution.py:34
  16.0 3.1 %collective-permute-start.3 = (bf16[4096,128]{1,0:T(8,128)(2,1)S(1)}, bf16[4096,128]{1,0:T(8,128)(2,1)S(1)}, u32[]{:S(2)}, u32[]{:S(2)}) collective-permute-start(bf16[4096,128]{1,0:T(8,128)(2,1)S(1)} %copy-done.3), channel_id=1, source_target_pairs={{4,12},{12,4},{20,28},{28,20},{5,13},{13,5},{21,29},{29,21},{6,14}... | collective-permute-start | bytes 3145736 | tf_op jit(solution)/shard_map/ppermute | solution.py:34
  19.1 0.0 collective-permute-done.2.refs_1_.refs_3_
  19.1 0.0 collective-permute-done.1.refs_0_.refs_2_
  19.1 13.9 %collective-permute-done.4.refs_3_.refs_5_ = bf16[4096,128]{1,0:T(8,128)(2,1)S(1)} collective-permute-done((bf16[4096,128]{1,0:T(8,128)(2,1)S(1)}, bf16[4096,128]{1,0:T(8,128)(2,1)S(1)}, u32[]{:S(2)}, u32[]{:S(2)}) %collective-permute-start.4) | collective-permute-done | bytes 1048608 | tf_op jit(solution)/shard_map/ppermute | solution.py:34
  33.0 5.0 %collective-permute-done.3.refs_2_.refs_4_ = bf16[4096,128]{1,0:T(8,128)(2,1)S(1)} collective-permute-done((bf16[4096,128]{1,0:T(8,128)(2,1)S(1)}, bf16[4096,128]{1,0:T(8,128)(2,1)S(1)}, u32[]{:S(2)}, u32[]{:S(2)}) %collective-permute-start.3) | collective-permute-done | bytes 1048608 | tf_op jit(solution)/shard_map/ppermute | solution.py:34
  38.0 0.1 shard_map.57
  38.1 0.1 collective-permute-start.5
  38.2 1.3 %collective-permute-start.6 = (bf16[2048,128]{1,0:T(8,128)(2,1)S(1)}, bf16[2048,128]{1,0:T(8,128)(2,1)S(1)}, u32[]{:S(2)}, u32[]{:S(2)}) collective-permute-start(bf16[2048,128]{1,0:T(8,128)(2,1)S(1)} %get-tuple-element.28), channel_id=1, source_target_pairs={{0,8},{4,12},{8,0},{12,4},{16,24},{20,28},{24,16},{28,20},{1,9},{5... | collective-permute-start | bytes 1572872 | tf_op jit(solution)/shard_map/ppermute | solution.py:34
  39.5 0.0 copy-done.1
  39.5 1.8 %shard_map.58 = (f32[768,128]{1,0:T(8,128)S(1)}, f32[768,128]{1,0:T(8,128)S(1)}) custom-call(bf16[384,4096]{1,0:T(8,128)(2,1)S(1)} %copy-done.1, bf16[384,4096]{1,0:T(8,128)(2,1)S(1)} %collective-permute-done.refs_1_, bf16[4096,128]{1,0:T(8,128)(2,1)S(1)} %collective-permute-done.1.refs_0_.refs_2_, ...), custom_call_target="tpu_custom_call" | custom-call | bytes 1024 | tf_op jit(solution)/shard_map/pallas_call | solution.py:43
  41.3 5.2 %collective-permute-done.5.refs_2_ = bf16[2048,128]{1,0:T(8,128)(2,1)S(1)} collective-permute-done((bf16[2048,128]{1,0:T(8,128)(2,1)S(1)}, bf16[2048,128]{1,0:T(8,128)(2,1)S(1)}, u32[]{:S(2)}, u32[]{:S(2)}) %collective-permute-start.5) | collective-permute-done | bytes 524320 | tf_op jit(solution)/shard_map/ppermute | solution.py:34
  46.5 0.1 collective-permute-done.6.refs_3_
  46.6 1.9 %shard_map.59 = (f32[768,128]{1,0:T(8,128)S(1)}, bf16[768,128]{1,0:T(8,128)(2,1)S(1)}, bf16[768,128]{1,0:T(8,128)(2,1)S(1)}, bf16[768,128]{1,0:T(8,128)(2,1)S(1)}) custom-call(bf16[384,4096]{1,0:T(8,128)(2,1)S(1)} %copy-done.1, bf16[384,4096]{1,0:T(8,128)(2,1)S(1)} %collective-permute-done.refs_1_, bf16[2048,128]{1,0:T(8,128)(2,1)S(1)} %collective-permute-done.5.refs_2_, ...), custom_call_target="tpu_custom_call" | custom-call | bytes 1024 | tf_op jit(solution)/shard_map/pallas_call | solution.py:43
  48.5 1.4 %collective-permute-start.7 = (bf16[768,128]{1,0:T(8,128)(2,1)S(1)}, bf16[768,128]{1,0:T(8,128)(2,1)S(1)}, u32[]{:S(2)}, u32[]{:S(2)}) collective-permute-start(bf16[768,128]{1,0:T(8,128)(2,1)S(1)} %get-tuple-element.32), channel_id=1, source_target_pairs={{0,1},{1,0},{2,3},{3,2},{4,5},{5,4},{6,7},{7,6},{8,9},{9,8},{10,11... | collective-permute-start | bytes 589832 | tf_op jit(solution)/shard_map/ppermute | solution.py:34
  49.9 2.3 %collective-permute-start.8 = (bf16[768,128]{1,0:T(8,128)(2,1)S(1)}, bf16[768,128]{1,0:T(8,128)(2,1)S(1)}, u32[]{:S(2)}, u32[]{:S(2)}) collective-permute-start(bf16[768,128]{1,0:T(8,128)(2,1)S(1)} %get-tuple-element.33), channel_id=1, source_target_pairs={{0,2},{1,3},{2,0},{3,1},{4,6},{5,7},{6,4},{7,5},{8,10},{9,11},{10,... | collective-permute-start | bytes 589832 | tf_op jit(solution)/shard_map/ppermute | solution.py:34
  52.2 0.0 collective-permute-start.9
  52.2 2.5 %collective-permute-done.7.refs_1_ = bf16[768,128]{1,0:T(8,128)(2,1)S(1)} collective-permute-done((bf16[768,128]{1,0:T(8,128)(2,1)S(1)}, bf16[768,128]{1,0:T(8,128)(2,1)S(1)}, u32[]{:S(2)}, u32[]{:S(2)}) %collective-permute-start.7) | collective-permute-done | bytes 196640 | tf_op jit(solution)/shard_map/ppermute | solution.py:34
  54.7 5.6 %collective-permute-done.8.refs_2_ = bf16[768,128]{1,0:T(8,128)(2,1)S(1)} collective-permute-done((bf16[768,128]{1,0:T(8,128)(2,1)S(1)}, bf16[768,128]{1,0:T(8,128)(2,1)S(1)}, u32[]{:S(2)}, u32[]{:S(2)}) %collective-permute-start.8) | collective-permute-done | bytes 196640 | tf_op jit(solution)/shard_map/ppermute | solution.py:34
  60.3 0.0 collective-permute-done.9.refs_3_
  60.3 0.1 shard_map.60
  60.4 0.1 collective-permute-start.10
  60.4 1.4 %collective-permute-done.10.refs_1_ = f32[384,128]{1,0:T(8,128)S(1)} collective-permute-done((f32[384,128]{1,0:T(8,128)S(1)}, f32[384,128]{1,0:T(8,128)S(1)}, u32[]{:S(2)}, u32[]{:S(2)}) %collective-permute-start.10) | collective-permute-done | bytes 196640 | tf_op jit(solution)/shard_map/ppermute | solution.py:34
  61.9 0.3 shard_map.61
  62.2 3.1 %collective-permute-start.12 = (f32[128,384]{1,0:T(8,128)S(1)}, f32[128,384]{1,0:T(8,128)S(1)}, u32[]{:S(2)}, u32[]{:S(2)}) collective-permute-start(f32[128,384]{1,0:T(8,128)S(1)} %get-tuple-element.44), channel_id=1, source_target_pairs={{0,4},{4,8},{8,12},{12,16},{16,20},{20,24},{24,28},{1,5},{5,9},{9,... | collective-permute-start | bytes 589832 | tf_op jit(solution)/shard_map/ppermute | solution.py:29
  65.3 1.9 %collective-permute-start.11 = (bf16[128,256]{1,0:T(8,128)(2,1)S(1)}, bf16[128,256]{1,0:T(8,128)(2,1)S(1)}, u32[]{:S(2)}, u32[]{:S(2)}) collective-permute-start(bf16[128,256]{1,0:T(8,128)(2,1)S(1)} %get-tuple-element.43), channel_id=1, source_target_pairs={{4,0},{8,4},{12,8},{16,12},{20,16},{24,20},{28,24},{5,1},{9,5},{13... | collective-permute-start | bytes 196616 | tf_op jit(solution)/shard_map/ppermute | solution.py:29
  67.3 0.5 shard_map.62
  67.7 3.2 %collective-permute-done.11.refs_5_ = bf16[128,256]{1,0:T(8,128)(2,1)S(1)} collective-permute-done((bf16[128,256]{1,0:T(8,128)(2,1)S(1)}, bf16[128,256]{1,0:T(8,128)(2,1)S(1)}, u32[]{:S(2)}, u32[]{:S(2)}) %collective-permute-start.11) | collective-permute-done | bytes 65568 | tf_op jit(solution)/shard_map/ppermute | solution.py:29
  70.9 0.0 collective-permute-done.12.refs_6_
  70.9 1.3 %shard_map.63 = f32[384,256]{1,0:T(8,128)} custom-call(f32[384,256]{1,0:T(8,128)S(1)} %get-tuple-element.39.refs_0_, bf16[128,256]{1,0:T(8,128)(2,1)S(1)} %get-tuple-element.40.refs_1_, bf16[128,256]{1,0:T(8,128)(2,1)S(1)} %get-tuple-element.41.refs_2_, bf16[512,512]{1,0:T(8,128)(2,1)S(1)} %get-tuple-element.25.refs_2_.refs_1_.refs_3_, ...), custom_call_target="tpu_custom_call" | custom-call | bytes 1024 | tf_op jit(solution)/shard_map/pallas_call | solution.py:43
Async XLA Ops:
  0.0 5.9 %collective-permute-start = (bf16[384,4096]{1,0:T(8,128)(2,1)}, bf16[384,4096]{1,0:T(8,128)(2,1)S(1)}, u32[]{:S(2)}, u32[]{:S(2)}) collective-permute-start(bf16[384,4096]{1,0:T(8,128)(2,1)} %refs_0_.7), channel_id=1, source_target_pairs={{0,4},{4,0},{8,12},{12,8},{16,20},{20,16},{24,28},{28,24},{1,5},{5... | collective-permute-start | bytes 9437192 | tf_op jit(solution)/shard_map/ppermute | solution.py:34
  0.1 19.0 %collective-permute-start.2 = (bf16[4096,128]{1,0:T(8,128)(2,1)}, bf16[4096,128]{1,0:T(8,128)(2,1)S(1)}, u32[]{:S(2)}, u32[]{:S(2)}) collective-permute-start(bf16[4096,128]{1,0:T(8,128)(2,1)} %refs_2_.1), channel_id=1, source_target_pairs={{0,16},{8,24},{16,0},{24,8},{1,17},{9,25},{17,1},{25,9},{2,18},{10... | collective-permute-start | bytes 3145736 | tf_op jit(solution)/shard_map/ppermute | solution.py:34
  0.8 18.3 %collective-permute-start.1 = (bf16[4096,128]{1,0:T(8,128)(2,1)}, bf16[4096,128]{1,0:T(8,128)(2,1)S(1)}, u32[]{:S(2)}, u32[]{:S(2)}) collective-permute-start(bf16[4096,128]{1,0:T(8,128)(2,1)} %refs_2_.1), channel_id=1, source_target_pairs={{0,8},{8,0},{16,24},{24,16},{1,9},{9,1},{17,25},{25,17},{2,10},{10... | collective-permute-start | bytes 3145736 | tf_op jit(solution)/shard_map/ppermute | solution.py:34
  5.9 1.9 %copy-start = (bf16[384,4096]{1,0:T(8,128)(2,1)S(1)}, bf16[384,4096]{1,0:T(8,128)(2,1)}, u32[]{:S(2)}) copy-start(bf16[384,4096]{1,0:T(8,128)(2,1)} %refs_0_.7) | copy-start | bytes 9437188
  7.8 1.2 %copy-start.2 = (bf16[4096,128]{1,0:T(8,128)(2,1)S(1)}, bf16[4096,128]{1,0:T(8,128)(2,1)}, u32[]{:S(2)}) copy-start(bf16[4096,128]{1,0:T(8,128)(2,1)} %refs_2_.1) | copy-start | bytes 3145732
  9.0 1.8 %copy-start.4 = (bf16[1,512,512]{2,1,0:T(8,128)(2,1)S(1)}, bf16[1,512,512]{2,1,0:T(8,128)(2,1)}, u32[]{:S(2)}) copy-start(bf16[1,512,512]{2,1,0:T(8,128)(2,1)} %refs_0_.5) | copy-start | bytes 1572868
  9.0 1.8 %copy-start.5 = (s32[1,512]{1,0:T(1,128)S(1)}, s32[1,512]{1,0:T(1,128)}, u32[]{:S(2)}) copy-start(s32[1,512]{1,0:T(1,128)} %refs_1_.1) | copy-start | bytes 6148
  9.0 1.8 %copy-start.6 = (s32[128]{0:T(128)S(1)}, s32[128]{0:T(128)}, u32[]{:S(2)}) copy-start(s32[128]{0:T(128)} %param.9) | copy-start | bytes 1540
  9.0 2.5 %copy-start.3 = (bf16[4096,128]{1,0:T(8,128)(2,1)S(1)}, bf16[4096,128]{1,0:T(8,128)(2,1)}, u32[]{:S(2)}) copy-start(bf16[4096,128]{1,0:T(8,128)(2,1)} %refs_2_.1) | copy-start | bytes 3145732
  10.8 28.7 %copy-start.1 = (bf16[384,4096]{1,0:T(8,128)(2,1)S(1)}, bf16[384,4096]{1,0:T(8,128)(2,1)}, u32[]{:S(2)}) copy-start(bf16[384,4096]{1,0:T(8,128)(2,1)} %refs_0_.7) | copy-start | bytes 9437188
  11.5 21.4 %collective-permute-start.4 = (bf16[4096,128]{1,0:T(8,128)(2,1)S(1)}, bf16[4096,128]{1,0:T(8,128)(2,1)S(1)}, u32[]{:S(2)}, u32[]{:S(2)}) collective-permute-start(bf16[4096,128]{1,0:T(8,128)(2,1)S(1)} %copy-done.3), channel_id=1, source_target_pairs={{4,20},{12,28},{20,4},{28,12},{5,21},{13,29},{21,5},{29,13},{6,22}... | collective-permute-start | bytes 3145736 | tf_op jit(solution)/shard_map/ppermute | solution.py:34
  16.0 22.0 %collective-permute-start.3 = (bf16[4096,128]{1,0:T(8,128)(2,1)S(1)}, bf16[4096,128]{1,0:T(8,128)(2,1)S(1)}, u32[]{:S(2)}, u32[]{:S(2)}) collective-permute-start(bf16[4096,128]{1,0:T(8,128)(2,1)S(1)} %copy-done.3), channel_id=1, source_target_pairs={{4,12},{12,4},{20,28},{28,20},{5,13},{13,5},{21,29},{29,21},{6,14}... | collective-permute-start | bytes 3145736 | tf_op jit(solution)/shard_map/ppermute | solution.py:34
  38.1 8.4 %collective-permute-start.5 = (bf16[2048,128]{1,0:T(8,128)(2,1)S(1)}, bf16[2048,128]{1,0:T(8,128)(2,1)S(1)}, u32[]{:S(2)}, u32[]{:S(2)}) collective-permute-start(bf16[2048,128]{1,0:T(8,128)(2,1)S(1)} %get-tuple-element.27), channel_id=1, source_target_pairs={{0,16},{4,20},{8,24},{12,28},{16,0},{20,4},{24,8},{28,12},{1,17},{... | collective-permute-start | bytes 1572872 | tf_op jit(solution)/shard_map/ppermute | solution.py:34
  38.2 8.4 %collective-permute-start.6 = (bf16[2048,128]{1,0:T(8,128)(2,1)S(1)}, bf16[2048,128]{1,0:T(8,128)(2,1)S(1)}, u32[]{:S(2)}, u32[]{:S(2)}) collective-permute-start(bf16[2048,128]{1,0:T(8,128)(2,1)S(1)} %get-tuple-element.28), channel_id=1, source_target_pairs={{0,8},{4,12},{8,0},{12,4},{16,24},{20,28},{24,16},{28,20},{1,9},{5... | collective-permute-start | bytes 1572872 | tf_op jit(solution)/shard_map/ppermute | solution.py:34
  48.5 6.2 %collective-permute-start.7 = (bf16[768,128]{1,0:T(8,128)(2,1)S(1)}, bf16[768,128]{1,0:T(8,128)(2,1)S(1)}, u32[]{:S(2)}, u32[]{:S(2)}) collective-permute-start(bf16[768,128]{1,0:T(8,128)(2,1)S(1)} %get-tuple-element.32), channel_id=1, source_target_pairs={{0,1},{1,0},{2,3},{3,2},{4,5},{5,4},{6,7},{7,6},{8,9},{9,8},{10,11... | collective-permute-start | bytes 589832 | tf_op jit(solution)/shard_map/ppermute | solution.py:34
  49.9 10.4 %collective-permute-start.8 = (bf16[768,128]{1,0:T(8,128)(2,1)S(1)}, bf16[768,128]{1,0:T(8,128)(2,1)S(1)}, u32[]{:S(2)}, u32[]{:S(2)}) collective-permute-start(bf16[768,128]{1,0:T(8,128)(2,1)S(1)} %get-tuple-element.33), channel_id=1, source_target_pairs={{0,2},{1,3},{2,0},{3,1},{4,6},{5,7},{6,4},{7,5},{8,10},{9,11},{10,... | collective-permute-start | bytes 589832 | tf_op jit(solution)/shard_map/ppermute | solution.py:34
  52.2 8.1 %collective-permute-start.9 = (bf16[768,128]{1,0:T(8,128)(2,1)S(1)}, bf16[768,128]{1,0:T(8,128)(2,1)S(1)}, u32[]{:S(2)}, u32[]{:S(2)}) collective-permute-start(bf16[768,128]{1,0:T(8,128)(2,1)S(1)} %get-tuple-element.34), channel_id=1, source_target_pairs={{0,3},{1,2},{2,1},{3,0},{4,7},{5,6},{6,5},{7,4},{8,11},{9,10},{10,... | collective-permute-start | bytes 589832 | tf_op jit(solution)/shard_map/ppermute | solution.py:34
  60.4 1.5 %collective-permute-start.10 = (f32[384,128]{1,0:T(8,128)S(1)}, f32[384,128]{1,0:T(8,128)S(1)}, u32[]{:S(2)}, u32[]{:S(2)}) collective-permute-start(f32[384,128]{1,0:T(8,128)S(1)} %get-tuple-element.36), channel_id=1, source_target_pairs={{0,4},{4,0},{8,12},{12,8},{16,20},{20,16},{24,28},{28,24},{1,5},{5... | collective-permute-start | bytes 589832 | tf_op jit(solution)/shard_map/ppermute | solution.py:34
  62.2 8.7 %collective-permute-start.12 = (f32[128,384]{1,0:T(8,128)S(1)}, f32[128,384]{1,0:T(8,128)S(1)}, u32[]{:S(2)}, u32[]{:S(2)}) collective-permute-start(f32[128,384]{1,0:T(8,128)S(1)} %get-tuple-element.44), channel_id=1, source_target_pairs={{0,4},{4,8},{8,12},{12,16},{16,20},{20,24},{24,28},{1,5},{5,9},{9,... | collective-permute-start | bytes 589832 | tf_op jit(solution)/shard_map/ppermute | solution.py:29
  65.3 5.6 %collective-permute-start.11 = (bf16[128,256]{1,0:T(8,128)(2,1)S(1)}, bf16[128,256]{1,0:T(8,128)(2,1)S(1)}, u32[]{:S(2)}, u32[]{:S(2)}) collective-permute-start(bf16[128,256]{1,0:T(8,128)(2,1)S(1)} %get-tuple-element.43), channel_id=1, source_target_pairs={{4,0},{8,4},{12,8},{16,12},{20,16},{24,20},{28,24},{5,1},{9,5},{13... | collective-permute-start | bytes 196616 | tf_op jit(solution)/shard_map/ppermute | solution.py:29

commit v7 on v6

--- a/solution.py
+++ b/solution.py
@@ -63,13 +63,11 @@
     return lax.bitwise_xor(lax.div(lax.axis_index("domain"), 2), lax.axis_index("band"))
 
 
-def halves_kernel(near_even, far_even, near_odd, far_odd, top, bottom, done):
-    half = top.shape[0]
-
+def pieces_kernel(near_even, far_even, near_odd, far_odd, top, bottom, done):
     def fill(near, far):
         copies = [
-            pltpu.make_async_copy(near.at[pl.ds(0, half)], top, done.at[0]),
-            pltpu.make_async_copy(far.at[pl.ds(half, half)], bottom, done.at[1]),
+            pltpu.make_async_copy(near.at[pl.ds(0, top.shape[0])], top, done.at[0]),
+            pltpu.make_async_copy(far.at[pl.ds(top.shape[0], bottom.shape[0])], bottom, done.at[1]),
         ]
         for copy in copies:
             copy.start()
@@ -99,11 +97,11 @@
 
 def late_kernel(mine, theirs, top, bottom, own, near, far, kept, *refs):
     sent, last = refs[:-1], refs[-1]
-    half = top.shape[0]
+    cut = top.shape[0]
     rows = mine.shape[0]
     for side, states in enumerate((mine, theirs)):
-        result = jnp.dot(states[:, :half], top[...], preferred_element_type=F32)
-        last[side * rows : (side + 1) * rows] = result + jnp.dot(states[:, half:], bottom[...], preferred_element_type=F32)
+        result = jnp.dot(states[:, :cut], top[...], preferred_element_type=F32)
+        last[side * rows : (side + 1) * rows] = result + jnp.dot(states[:, cut:], bottom[...], preferred_element_type=F32)
     where = block_of_band()
 
     def store(out, slot, block):
@@ -130,7 +128,7 @@
     bands, chips = lax.axis_size("band"), lax.axis_size("domain") // 2
     rows, states = wavefunctions.shape
     width = rotation.shape[1]
-    half = states // 2
+    cut = states * 9 // 16
     received = [exchanged(rotation, "domain", NEAR, 0), exchanged(rotation, "domain", FAR, 0)]
     theirs = exchanged(wavefunctions, "domain", CORE)
     block = [shape(2 * rows, width)]
@@ -138,14 +136,14 @@
     operator = operator(own)
     later, _ = lax.optimization_barrier((rotation, operator[0]))
     received += [exchanged(later, "domain", NEAR, CORE), exchanged(later, "domain", FAR, CORE)]
-    halves = [shape(half, width, dtype=BF16)] * 2
-    top, bottom = call(halves_kernel, halves, received, scratch=[pltpu.SemaphoreType.DMA((2,))])
+    outs = [shape(count, width, dtype=BF16) for count in (cut, states - cut)]
+    top, bottom = call(pieces_kernel, outs, received, scratch=[pltpu.SemaphoreType.DMA((2,))])
     top, bottom = exchanged(top, "domain", FAR), exchanged(bottom, "domain", NEAR)
     early = call(early_kernel, block * 2, (wavefunctions, theirs, *received))
     outs = block + [shape(2 * rows, width, dtype=BF16)] * (bands - 1)
     scratch = [pltpu.VMEM((2 * rows, width), F32)]
     kept, *sent = call(late_kernel, outs, (wavefunctions, theirs, top, bottom, own, *early), scratch=scratch)
-    parts = [exchanged(value, "band", mask) for mask, value in enumerate(sent, 1)]
+    parts = [exchanged(sent[mask - 1], "band", mask) for mask in reversed(range(1, bands))]
     mine, others = call(sum_kernel, [shape(rows, width)] * 2, (kept, *parts))
     return mine, exchanged(others, "domain", CORE), operator
 
@@ -155,17 +153,25 @@
     return lax.psum_scatter(dot(wavefunctions, columns), "band", scatter_dimension=1, tiled=True)
 
 
-def faces_kernel(mine, other, assembled, pick, total, faces, back):
+def faces_kernel(mine, other, assembled, pick, total, inward, outward):
     own, width = mine.shape
+    columns = 2 * width
     first = core() == 0
     for side, half in enumerate((jnp.where(first, mine[...], other[...]), jnp.where(first, other[...], mine[...]))):
-        columns = slice(side * width, (side + 1) * width)
-        total[:, columns] = half
-        high, low = split(half)
-        faces[:, columns] = dot(pick[...], high).astype(BF16)
-        outward = assembled[own:, :own]
-        back[:, columns] = dot(outward, high) + dot(outward, low)
-    back[:, 2 * width :] = assembled[own:, own:].astype(F32)
+        total[:, side * width : (side + 1) * width] = half
+    high, low = split(total[...])
+    faces = dot(pick[...], high).astype(BF16)
+    onward = (dot(assembled[own:, :own], high) + dot(assembled[own:, :own], low)).astype(BF16)
+    corner = assembled[own:, own:]
+
+    def store(forward, backward):
+        forward[:, :columns] = onward
+        forward[:, columns:] = corner
+        backward[:, :columns] = faces
+        backward[:, columns:] = corner
+
+    pl.when(first)(lambda: store(inward, outward))
+    pl.when(jnp.logical_not(first))(lambda: store(outward, inward))
 
 
 def inner_kernel(total, assembled, pick, out, face_high, face_low):
@@ -177,23 +183,29 @@
     face_low[...] = dot(pick[...], low).astype(BF16)
 
 
-def final_kernel(inner, face_high, face_low, assembled, spread, incoming, back, out):
+def final_kernel(inner, face_high, face_low, assembled, spread, inward, outward, out):
     own, columns = inner.shape
-    corner = back[:, columns:].astype(BF16)
-    high, low = split(back[:, :columns] + dot(corner, face_high[...]) + dot(corner, face_low[...]))
-    out[...] = inner[...] + dot(assembled[:own, own:], incoming[...]) + dot(spread[...], high) + dot(spread[...], low)
+    first = core() == 0
+    incoming = jnp.where(first, inward[:, :columns], outward[:, :columns])
+    back = jnp.where(first, outward[...], inward[...])
+    corner = back[:, columns:]
+    value = back[:, :columns].astype(F32) + dot(corner, face_high[...]) + dot(corner, face_low[...])
+    high, low = split(value)
+    out[...] = inner[...] + dot(assembled[:own, own:], incoming) + dot(spread[...], high) + dot(spread[...], low)
 
 
 def finish_square(mine, other, operator):
     assembled, pick, spread = operator
     rows, width = mine.shape
     shared, columns = pick.shape[0], 2 * width
-    outs = [shape(rows, columns), shape(shared, columns, dtype=BF16), shape(shared, columns + shared)]
-    total, faces, back = call(faces_kernel, outs, (mine, other, assembled, pick))
-    incoming, back = shifted(faces, "domain", -1), shifted(back, "domain", 1)
+    outs = [shape(rows, columns)] + [shape(shared, columns + shared, dtype=BF16)] * 2
+    total, inward, outward = call(faces_kernel, outs, (mine, other, assembled, pick))
+    across = [(place, place + 1) for place in range(CORE, lax.axis_size("domain") - 1, 2)]
+    outward = lax.ppermute(outward, "domain", across + [(target, source) for source, target in across])
+    inward = exchanged(inward, "domain", CORE)
     outs = [shape(rows, columns)] + [shape(shared, columns, dtype=BF16)] * 2
     inner, *face = call(inner_kernel, outs, (total, assembled, pick))
-    return call(final_kernel, outs[:1], (inner, *face, assembled, spread, incoming, back))[0]
+    return call(final_kernel, outs[:1], (inner, *face, assembled, spread, inward, outward))[0]
 
 
 def finish_any(rotated, cell_matrices, cell_nodes, face_map):

time: 73.2 us -> 71 us (0.970); the launches traced: 72.2 us -> 70.8 us
  starting transfers between devices: 19.2 us -> 18.1 us
    ppermute x2 -> x1, starting transfers between devices: 5.04 us -> 3.35 us  [finish_square(): lax.ppermute(outward, 'domain', across + [(target, source) for source, ta...]
    ppermute x11 -> x12, starting transfers between devices: 14.1 us -> 14.7 us  [exchanged(): lax.ppermute(value, axis, [(source, source ^ mask) for source in sources...]
    ppermute x11 -> x12, waiting for transfers between devices: 38.1 us -> 37.8 us  [exchanged(): lax.ppermute(value, axis, [(source, source ^ mask) for source in sources...]
    ppermute x2 -> x1, waiting for transfers between devices: 3.2 us -> 2.94 us  [finish_square(): lax.ppermute(outward, 'domain', across + [(target, source) for source, ta...]
where the time goes in v7:
time: 71 us; the launch traced here: 70.8 us
  waiting for transfers between devices  40.7 us (57%)
  starting transfers between devices  18.1 us (25%)
  Pallas kernels  8.66 us (12%)
  local copies, waits for them, and re-layouts  3.13 us (4%)
    ppermute x12, waiting for transfers between devices, exchanged(): lax.ppermute(value, axis, [(source, source ^ mask) for source in sources...  37.8 us
    ppermute x12, starting transfers between devices, exchanged(): lax.ppermute(value, axis, [(source, source ^ mask) for source in sources...  14.7 us
    pallas_call x9, Pallas kernels, call(): pl.pallas_call(body, out_shape=outs, in_specs=[pl.BlockSpec(memory_space=...  8.66 us
    ppermute x1, starting transfers between devices, finish_square(): lax.ppermute(outward, 'domain', across + [(target, source) for source, ta...  3.35 us
    unnamed x14, local copies, waits for them, and re-layouts  3.13 us
    ppermute x1, waiting for transfers between devices, finish_square(): lax.ppermute(outward, 'domain', across + [(target, source) for source, ta...  2.94 us
  transfers between devices with their start and end apart: 13, of which 9 were waited for; matrix products, arithmetic and copies ran while one was open for 0% of the time, Pallas kernels for 7%

profile of v7, /device:TPU:1, one launch (start us, length us, event | category | flops | bytes accessed | tf_op | source)
XLA Modules:
  0.0 70.8 jit_solution(13173622711579531735)
XLA Ops:
  0.0 0.1 collective-permute-start
  0.1 0.7 %collective-permute-start.2 = (bf16[4096,128]{1,0:T(8,128)(2,1)}, bf16[4096,128]{1,0:T(8,128)(2,1)S(1)}, u32[]{:S(2)}, u32[]{:S(2)}) collective-permute-start(bf16[4096,128]{1,0:T(8,128)(2,1)} %refs_2_.1), channel_id=1, source_target_pairs={{0,16},{8,24},{16,0},{24,8},{1,17},{9,25},{17,1},{25,9},{2,18},{10... | collective-permute-start | bytes 3145736 | tf_op jit(solution)/shard_map/ppermute | solution.py:34
  0.8 0.7 %collective-permute-start.1 = (bf16[4096,128]{1,0:T(8,128)(2,1)}, bf16[4096,128]{1,0:T(8,128)(2,1)S(1)}, u32[]{:S(2)}, u32[]{:S(2)}) collective-permute-start(bf16[4096,128]{1,0:T(8,128)(2,1)} %refs_2_.1), channel_id=1, source_target_pairs={{0,8},{8,0},{16,24},{24,16},{1,9},{9,1},{17,25},{25,17},{2,10},{10... | collective-permute-start | bytes 3145736 | tf_op jit(solution)/shard_map/ppermute | solution.py:34
  1.5 4.4 %collective-permute-done.refs_1_ = bf16[384,4096]{1,0:T(8,128)(2,1)S(1)} collective-permute-done((bf16[384,4096]{1,0:T(8,128)(2,1)}, bf16[384,4096]{1,0:T(8,128)(2,1)S(1)}, u32[]{:S(2)}, u32[]{:S(2)}) %collective-permute-start) | collective-permute-done | bytes 3145760 | tf_op jit(solution)/shard_map/ppermute | solution.py:34
  5.9 0.0 copy-start
  5.9 1.9 %copy-done = bf16[384,4096]{1,0:T(8,128)(2,1)S(1)} copy-done((bf16[384,4096]{1,0:T(8,128)(2,1)S(1)}, bf16[384,4096]{1,0:T(8,128)(2,1)}, u32[]{:S(2)}) %copy-start) | copy-done | bytes 3145752
  7.8 0.0 copy-start.2
  7.8 1.2 %copy-done.2 = bf16[4096,128]{1,0:T(8,128)(2,1)S(1)} copy-done((bf16[4096,128]{1,0:T(8,128)(2,1)S(1)}, bf16[4096,128]{1,0:T(8,128)(2,1)}, u32[]{:S(2)}) %copy-start.2) | copy-done | bytes 1048600
  9.0 0.0 copy-start.4
  9.0 0.0 copy-start.5
  9.0 0.0 copy-start.6
  9.0 0.0 copy-start.3
  9.0 1.8 %shard_map.55.refs_3_.refs_4_ = f32[768,128]{1,0:T(8,128)S(1)} custom-call(bf16[384,4096]{1,0:T(8,128)(2,1)S(1)} %copy-done, bf16[384,4096]{1,0:T(8,128)(2,1)S(1)} %collective-permute-done.refs_1_, bf16[4096,128]{1,0:T(8,128)(2,1)S(1)} %copy-done.2), custom_call_target="tpu_custom_call" | custom-call | bytes 1024 | tf_op jit(solution)/shard_map/pallas_call | solution.py:43
  10.8 0.0 copy-start.1
  10.8 0.0 copy-done.4
  10.8 0.0 copy-done.5
  10.8 0.0 copy-done.6
  10.8 0.7 shard_map.56
  11.5 0.0 copy-done.3
  11.5 4.4 %collective-permute-start.4 = (bf16[4096,128]{1,0:T(8,128)(2,1)S(1)}, bf16[4096,128]{1,0:T(8,128)(2,1)S(1)}, u32[]{:S(2)}, u32[]{:S(2)}) collective-permute-start(bf16[4096,128]{1,0:T(8,128)(2,1)S(1)} %copy-done.3), channel_id=1, source_target_pairs={{4,20},{12,28},{20,4},{28,12},{5,21},{13,29},{21,5},{29,13},{6,22}... | collective-permute-start | bytes 3145736 | tf_op jit(solution)/shard_map/ppermute | solution.py:34
  16.0 3.1 %collective-permute-start.3 = (bf16[4096,128]{1,0:T(8,128)(2,1)S(1)}, bf16[4096,128]{1,0:T(8,128)(2,1)S(1)}, u32[]{:S(2)}, u32[]{:S(2)}) collective-permute-start(bf16[4096,128]{1,0:T(8,128)(2,1)S(1)} %copy-done.3), channel_id=1, source_target_pairs={{4,12},{12,4},{20,28},{28,20},{5,13},{13,5},{21,29},{29,21},{6,14}... | collective-permute-start | bytes 3145736 | tf_op jit(solution)/shard_map/ppermute | solution.py:34
  19.1 0.0 collective-permute-done.2.refs_1_.refs_3_
  19.1 0.0 collective-permute-done.1.refs_0_.refs_2_
  19.1 13.6 %collective-permute-done.4.refs_3_.refs_5_ = bf16[4096,128]{1,0:T(8,128)(2,1)S(1)} collective-permute-done((bf16[4096,128]{1,0:T(8,128)(2,1)S(1)}, bf16[4096,128]{1,0:T(8,128)(2,1)S(1)}, u32[]{:S(2)}, u32[]{:S(2)}) %collective-permute-start.4) | collective-permute-done | bytes 1048608 | tf_op jit(solution)/shard_map/ppermute | solution.py:34
  32.7 4.6 %collective-permute-done.3.refs_2_.refs_4_ = bf16[4096,128]{1,0:T(8,128)(2,1)S(1)} collective-permute-done((bf16[4096,128]{1,0:T(8,128)(2,1)S(1)}, bf16[4096,128]{1,0:T(8,128)(2,1)S(1)}, u32[]{:S(2)}, u32[]{:S(2)}) %collective-permute-start.3) | collective-permute-done | bytes 1048608 | tf_op jit(solution)/shard_map/ppermute | solution.py:34
  37.3 0.4 shard_map.57
  37.7 0.1 collective-permute-start.5
  37.8 1.6 %collective-permute-start.6 = (bf16[1792,128]{1,0:T(8,128)(2,1)S(1)}, bf16[1792,128]{1,0:T(8,128)(2,1)S(1)}, u32[]{:S(2)}, u32[]{:S(2)}) collective-permute-start(bf16[1792,128]{1,0:T(8,128)(2,1)S(1)} %get-tuple-element.28), channel_id=1, source_target_pairs={{0,8},{4,12},{8,0},{12,4},{16,24},{20,28},{24,16},{28,20},{1,9},{5... | collective-permute-start | bytes 1376264 | tf_op jit(solution)/shard_map/ppermute | solution.py:34
  39.4 0.0 copy-done.1
  39.4 1.8 %shard_map.58 = (f32[768,128]{1,0:T(8,128)S(1)}, f32[768,128]{1,0:T(8,128)S(1)}) custom-call(bf16[384,4096]{1,0:T(8,128)(2,1)S(1)} %copy-done.1, bf16[384,4096]{1,0:T(8,128)(2,1)S(1)} %collective-permute-done.refs_1_, bf16[4096,128]{1,0:T(8,128)(2,1)S(1)} %collective-permute-done.1.refs_0_.refs_2_, ...), custom_call_target="tpu_custom_call" | custom-call | bytes 1024 | tf_op jit(solution)/shard_map/pallas_call | solution.py:43
  41.2 4.4 %collective-permute-done.6.refs_3_ = bf16[1792,128]{1,0:T(8,128)(2,1)S(1)} collective-permute-done((bf16[1792,128]{1,0:T(8,128)(2,1)S(1)}, bf16[1792,128]{1,0:T(8,128)(2,1)S(1)}, u32[]{:S(2)}, u32[]{:S(2)}) %collective-permute-start.6) | collective-permute-done | bytes 458784 | tf_op jit(solution)/shard_map/ppermute | solution.py:34
  45.5 1.3 %collective-permute-done.5.refs_2_ = bf16[2304,128]{1,0:T(8,128)(2,1)S(1)} collective-permute-done((bf16[2304,128]{1,0:T(8,128)(2,1)S(1)}, bf16[2304,128]{1,0:T(8,128)(2,1)S(1)}, u32[]{:S(2)}, u32[]{:S(2)}) %collective-permute-start.5) | collective-permute-done | bytes 589856 | tf_op jit(solution)/shard_map/ppermute | solution.py:34
  46.8 1.9 %shard_map.59 = (f32[768,128]{1,0:T(8,128)S(1)}, bf16[768,128]{1,0:T(8,128)(2,1)S(1)}, bf16[768,128]{1,0:T(8,128)(2,1)S(1)}, bf16[768,128]{1,0:T(8,128)(2,1)S(1)}) custom-call(bf16[384,4096]{1,0:T(8,128)(2,1)S(1)} %copy-done.1, bf16[384,4096]{1,0:T(8,128)(2,1)S(1)} %collective-permute-done.refs_1_, bf16[2304,128]{1,0:T(8,128)(2,1)S(1)} %collective-permute-done.5.refs_2_, ...), custom_call_target="tpu_custom_call" | custom-call | bytes 1024 | tf_op jit(solution)/shard_map/pallas_call | solution.py:43
  48.7 3.4 %collective-permute-start.7 = (bf16[768,128]{1,0:T(8,128)(2,1)S(1)}, bf16[768,128]{1,0:T(8,128)(2,1)S(1)}, u32[]{:S(2)}, u32[]{:S(2)}) collective-permute-start(bf16[768,128]{1,0:T(8,128)(2,1)S(1)} %get-tuple-element.32), channel_id=1, source_target_pairs={{0,3},{1,2},{2,1},{3,0},{4,7},{5,6},{6,5},{7,4},{8,11},{9,10},{10,... | collective-permute-start | bytes 589832 | tf_op jit(solution)/shard_map/ppermute | solution.py:34
  52.1 0.0 collective-permute-start.8
  52.1 0.4 collective-permute-start.9
  52.5 2.9 %collective-permute-done.7.refs_1_ = bf16[768,128]{1,0:T(8,128)(2,1)S(1)} collective-permute-done((bf16[768,128]{1,0:T(8,128)(2,1)S(1)}, bf16[768,128]{1,0:T(8,128)(2,1)S(1)}, u32[]{:S(2)}, u32[]{:S(2)}) %collective-permute-start.7) | collective-permute-done | bytes 196640 | tf_op jit(solution)/shard_map/ppermute | solution.py:34
  55.4 5.3 %collective-permute-done.8.refs_2_ = bf16[768,128]{1,0:T(8,128)(2,1)S(1)} collective-permute-done((bf16[768,128]{1,0:T(8,128)(2,1)S(1)}, bf16[768,128]{1,0:T(8,128)(2,1)S(1)}, u32[]{:S(2)}, u32[]{:S(2)}) %collective-permute-start.8) | collective-permute-done | bytes 196640 | tf_op jit(solution)/shard_map/ppermute | solution.py:34
  60.7 0.0 collective-permute-done.9.refs_3_
  60.7 0.1 shard_map.60
  60.7 0.1 collective-permute-start.10
  60.8 1.4 %collective-permute-done.10.refs_1_ = f32[384,128]{1,0:T(8,128)S(1)} collective-permute-done((f32[384,128]{1,0:T(8,128)S(1)}, f32[384,128]{1,0:T(8,128)S(1)}, u32[]{:S(2)}, u32[]{:S(2)}) %collective-permute-start.10) | collective-permute-done | bytes 196640 | tf_op jit(solution)/shard_map/ppermute | solution.py:34
  62.3 0.3 shard_map.61
  62.6 0.2 collective-permute-start.11
  62.8 3.4 %collective-permute-start.12 = (bf16[128,384]{1,0:T(8,128)(2,1)S(1)}, bf16[128,384]{1,0:T(8,128)(2,1)S(1)}, u32[]{:S(2)}, u32[]{:S(2)}) collective-permute-start(bf16[128,384]{1,0:T(8,128)(2,1)S(1)} %get-tuple-element.44), channel_id=1, source_target_pairs={{4,8},{12,16},{20,24},{8,4},{16,12},{24,20},{5,9},{13,17},{21,25},... | collective-permute-start | bytes 294920 | tf_op jit(solution)/shard_map/ppermute | solution.py:204
  66.1 0.4 shard_map.62
  66.6 0.0 collective-permute-done.11.refs_5_
  66.6 2.9 %collective-permute-done.12.refs_6_ = bf16[128,384]{1,0:T(8,128)(2,1)S(1)} collective-permute-done((bf16[128,384]{1,0:T(8,128)(2,1)S(1)}, bf16[128,384]{1,0:T(8,128)(2,1)S(1)}, u32[]{:S(2)}, u32[]{:S(2)}) %collective-permute-start.12) | collective-permute-done | bytes 98336 | tf_op jit(solution)/shard_map/ppermute | solution.py:204
  69.5 1.3 %shard_map.63 = f32[384,256]{1,0:T(8,128)} custom-call(f32[384,256]{1,0:T(8,128)S(1)} %get-tuple-element.39.refs_0_, bf16[128,256]{1,0:T(8,128)(2,1)S(1)} %get-tuple-element.40.refs_1_, bf16[128,256]{1,0:T(8,128)(2,1)S(1)} %get-tuple-element.41.refs_2_, bf16[512,512]{1,0:T(8,128)(2,1)S(1)} %get-tuple-element.25.refs_2_.refs_1_.refs_3_, ...), custom_call_target="tpu_custom_call" | custom-call | bytes 1024 | tf_op jit(solution)/shard_map/pallas_call | solution.py:43
Async XLA Ops:
  0.0 5.9 %collective-permute-start = (bf16[384,4096]{1,0:T(8,128)(2,1)}, bf16[384,4096]{1,0:T(8,128)(2,1)S(1)}, u32[]{:S(2)}, u32[]{:S(2)}) collective-permute-start(bf16[384,4096]{1,0:T(8,128)(2,1)} %refs_0_.7), channel_id=1, source_target_pairs={{0,4},{4,0},{8,12},{12,8},{16,20},{20,16},{24,28},{28,24},{1,5},{5... | collective-permute-start | bytes 9437192 | tf_op jit(solution)/shard_map/ppermute | solution.py:34
  0.1 19.0 %collective-permute-start.2 = (bf16[4096,128]{1,0:T(8,128)(2,1)}, bf16[4096,128]{1,0:T(8,128)(2,1)S(1)}, u32[]{:S(2)}, u32[]{:S(2)}) collective-permute-start(bf16[4096,128]{1,0:T(8,128)(2,1)} %refs_2_.1), channel_id=1, source_target_pairs={{0,16},{8,24},{16,0},{24,8},{1,17},{9,25},{17,1},{25,9},{2,18},{10... | collective-permute-start | bytes 3145736 | tf_op jit(solution)/shard_map/ppermute | solution.py:34
  0.8 18.3 %collective-permute-start.1 = (bf16[4096,128]{1,0:T(8,128)(2,1)}, bf16[4096,128]{1,0:T(8,128)(2,1)S(1)}, u32[]{:S(2)}, u32[]{:S(2)}) collective-permute-start(bf16[4096,128]{1,0:T(8,128)(2,1)} %refs_2_.1), channel_id=1, source_target_pairs={{0,8},{8,0},{16,24},{24,16},{1,9},{9,1},{17,25},{25,17},{2,10},{10... | collective-permute-start | bytes 3145736 | tf_op jit(solution)/shard_map/ppermute | solution.py:34
  5.9 1.9 %copy-start = (bf16[384,4096]{1,0:T(8,128)(2,1)S(1)}, bf16[384,4096]{1,0:T(8,128)(2,1)}, u32[]{:S(2)}) copy-start(bf16[384,4096]{1,0:T(8,128)(2,1)} %refs_0_.7) | copy-start | bytes 9437188
  7.8 1.2 %copy-start.2 = (bf16[4096,128]{1,0:T(8,128)(2,1)S(1)}, bf16[4096,128]{1,0:T(8,128)(2,1)}, u32[]{:S(2)}) copy-start(bf16[4096,128]{1,0:T(8,128)(2,1)} %refs_2_.1) | copy-start | bytes 3145732
  9.0 1.8 %copy-start.4 = (bf16[1,512,512]{2,1,0:T(8,128)(2,1)S(1)}, bf16[1,512,512]{2,1,0:T(8,128)(2,1)}, u32[]{:S(2)}) copy-start(bf16[1,512,512]{2,1,0:T(8,128)(2,1)} %refs_0_.5) | copy-start | bytes 1572868
  9.0 1.8 %copy-start.5 = (s32[1,512]{1,0:T(1,128)S(1)}, s32[1,512]{1,0:T(1,128)}, u32[]{:S(2)}) copy-start(s32[1,512]{1,0:T(1,128)} %refs_1_.1) | copy-start | bytes 6148
  9.0 1.8 %copy-start.6 = (s32[128]{0:T(128)S(1)}, s32[128]{0:T(128)}, u32[]{:S(2)}) copy-start(s32[128]{0:T(128)} %param.9) | copy-start | bytes 1540
  9.0 2.5 %copy-start.3 = (bf16[4096,128]{1,0:T(8,128)(2,1)S(1)}, bf16[4096,128]{1,0:T(8,128)(2,1)}, u32[]{:S(2)}) copy-start(bf16[4096,128]{1,0:T(8,128)(2,1)} %refs_2_.1) | copy-start | bytes 3145732
  10.8 28.6 %copy-start.1 = (bf16[384,4096]{1,0:T(8,128)(2,1)S(1)}, bf16[384,4096]{1,0:T(8,128)(2,1)}, u32[]{:S(2)}) copy-start(bf16[384,4096]{1,0:T(8,128)(2,1)} %refs_0_.7) | copy-start | bytes 9437188
  11.5 21.1 %collective-permute-start.4 = (bf16[4096,128]{1,0:T(8,128)(2,1)S(1)}, bf16[4096,128]{1,0:T(8,128)(2,1)S(1)}, u32[]{:S(2)}, u32[]{:S(2)}) collective-permute-start(bf16[4096,128]{1,0:T(8,128)(2,1)S(1)} %copy-done.3), channel_id=1, source_target_pairs={{4,20},{12,28},{20,4},{28,12},{5,21},{13,29},{21,5},{29,13},{6,22}... | collective-permute-start | bytes 3145736 | tf_op jit(solution)/shard_map/ppermute | solution.py:34
  16.0 21.3 %collective-permute-start.3 = (bf16[4096,128]{1,0:T(8,128)(2,1)S(1)}, bf16[4096,128]{1,0:T(8,128)(2,1)S(1)}, u32[]{:S(2)}, u32[]{:S(2)}) collective-permute-start(bf16[4096,128]{1,0:T(8,128)(2,1)S(1)} %copy-done.3), channel_id=1, source_target_pairs={{4,12},{12,4},{20,28},{28,20},{5,13},{13,5},{21,29},{29,21},{6,14}... | collective-permute-start | bytes 3145736 | tf_op jit(solution)/shard_map/ppermute | solution.py:34
  37.7 9.1 %collective-permute-start.5 = (bf16[2304,128]{1,0:T(8,128)(2,1)S(1)}, bf16[2304,128]{1,0:T(8,128)(2,1)S(1)}, u32[]{:S(2)}, u32[]{:S(2)}) collective-permute-start(bf16[2304,128]{1,0:T(8,128)(2,1)S(1)} %get-tuple-element.27), channel_id=1, source_target_pairs={{0,16},{4,20},{8,24},{12,28},{16,0},{20,4},{24,8},{28,12},{1,17},{... | collective-permute-start | bytes 1769480 | tf_op jit(solution)/shard_map/ppermute | solution.py:34
  37.8 7.7 %collective-permute-start.6 = (bf16[1792,128]{1,0:T(8,128)(2,1)S(1)}, bf16[1792,128]{1,0:T(8,128)(2,1)S(1)}, u32[]{:S(2)}, u32[]{:S(2)}) collective-permute-start(bf16[1792,128]{1,0:T(8,128)(2,1)S(1)} %get-tuple-element.28), channel_id=1, source_target_pairs={{0,8},{4,12},{8,0},{12,4},{16,24},{20,28},{24,16},{28,20},{1,9},{5... | collective-permute-start | bytes 1376264 | tf_op jit(solution)/shard_map/ppermute | solution.py:34
  48.7 6.6 %collective-permute-start.7 = (bf16[768,128]{1,0:T(8,128)(2,1)S(1)}, bf16[768,128]{1,0:T(8,128)(2,1)S(1)}, u32[]{:S(2)}, u32[]{:S(2)}) collective-permute-start(bf16[768,128]{1,0:T(8,128)(2,1)S(1)} %get-tuple-element.32), channel_id=1, source_target_pairs={{0,3},{1,2},{2,1},{3,0},{4,7},{5,6},{6,5},{7,4},{8,11},{9,10},{10,... | collective-permute-start | bytes 589832 | tf_op jit(solution)/shard_map/ppermute | solution.py:34
  52.1 8.5 %collective-permute-start.8 = (bf16[768,128]{1,0:T(8,128)(2,1)S(1)}, bf16[768,128]{1,0:T(8,128)(2,1)S(1)}, u32[]{:S(2)}, u32[]{:S(2)}) collective-permute-start(bf16[768,128]{1,0:T(8,128)(2,1)S(1)} %get-tuple-element.33), channel_id=1, source_target_pairs={{0,2},{1,3},{2,0},{3,1},{4,6},{5,7},{6,4},{7,5},{8,10},{9,11},{10,... | collective-permute-start | bytes 589832 | tf_op jit(solution)/shard_map/ppermute | solution.py:34
  52.1 8.5 %collective-permute-start.9 = (bf16[768,128]{1,0:T(8,128)(2,1)S(1)}, bf16[768,128]{1,0:T(8,128)(2,1)S(1)}, u32[]{:S(2)}, u32[]{:S(2)}) collective-permute-start(bf16[768,128]{1,0:T(8,128)(2,1)S(1)} %get-tuple-element.34), channel_id=1, source_target_pairs={{0,1},{1,0},{2,3},{3,2},{4,5},{5,4},{6,7},{7,6},{8,9},{9,8},{10,11... | collective-permute-start | bytes 589832 | tf_op jit(solution)/shard_map/ppermute | solution.py:34
  60.7 1.5 %collective-permute-start.10 = (f32[384,128]{1,0:T(8,128)S(1)}, f32[384,128]{1,0:T(8,128)S(1)}, u32[]{:S(2)}, u32[]{:S(2)}) collective-permute-start(f32[384,128]{1,0:T(8,128)S(1)} %get-tuple-element.36), channel_id=1, source_target_pairs={{0,4},{4,0},{8,12},{12,8},{16,20},{20,16},{24,28},{28,24},{1,5},{5... | collective-permute-start | bytes 589832 | tf_op jit(solution)/shard_map/ppermute | solution.py:34
  62.6 4.0 %collective-permute-start.11 = (bf16[128,384]{1,0:T(8,128)(2,1)S(1)}, bf16[128,384]{1,0:T(8,128)(2,1)S(1)}, u32[]{:S(2)}, u32[]{:S(2)}) collective-permute-start(bf16[128,384]{1,0:T(8,128)(2,1)S(1)} %get-tuple-element.43), channel_id=1, source_target_pairs={{0,4},{4,0},{8,12},{12,8},{16,20},{20,16},{24,28},{28,24},{1,5},{5... | collective-permute-start | bytes 294920 | tf_op jit(solution)/shard_map/ppermute | solution.py:34
  62.8 6.8 %collective-permute-start.12 = (bf16[128,384]{1,0:T(8,128)(2,1)S(1)}, bf16[128,384]{1,0:T(8,128)(2,1)S(1)}, u32[]{:S(2)}, u32[]{:S(2)}) collective-permute-start(bf16[128,384]{1,0:T(8,128)(2,1)S(1)} %get-tuple-element.44), channel_id=1, source_target_pairs={{4,8},{12,16},{20,24},{8,4},{16,12},{24,20},{5,9},{13,17},{21,25},... | collective-permute-start | bytes 294920 | tf_op jit(solution)/shard_map/ppermute | solution.py:204

commit v8 on v7

--- a/solution.py
+++ b/solution.py
@@ -57,10 +57,6 @@
 
 def core():
     return lax.rem(lax.axis_index("domain"), 2)
-
-
-def block_of_band():
-    return lax.bitwise_xor(lax.div(lax.axis_index("domain"), 2), lax.axis_index("band"))
 
 
 def pieces_kernel(near_even, far_even, near_odd, far_odd, top, bottom, done):
@@ -95,30 +91,32 @@
         far_block[side * rows : (side + 1) * rows] = result[:, width:]
 
 
-def late_kernel(mine, theirs, top, bottom, own, near, far, kept, *refs):
-    sent, last = refs[:-1], refs[-1]
+def late_kernel(mine, theirs, top, bottom, own, near, far, kept, sent, last):
     cut = top.shape[0]
     rows = mine.shape[0]
     for side, states in enumerate((mine, theirs)):
         result = jnp.dot(states[:, :cut], top[...], preferred_element_type=F32)
         last[side * rows : (side + 1) * rows] = result + jnp.dot(states[:, cut:], bottom[...], preferred_element_type=F32)
-    where = block_of_band()
-
-    def store(out, slot, block):
-        @pl.when(slot == lax.bitwise_xor(where, mask))
+    chip, band = lax.div(lax.axis_index("domain"), 2), lax.axis_index("band")
+
+    def store(place, slot, block):
+        @pl.when(place == lax.bitwise_xor(chip, slot))
         def _():
-            out[...] = block[...].astype(out.dtype)
-
-    for mask, out in enumerate((kept, *sent)):
-        for slot, block in enumerate((own, near, far, last)):
-            store(out, slot, block)
-
-
-def sum_kernel(kept, *refs):
-    parts, (mine, theirs) = refs[:-2], refs[-2:]
+            sent[place] = block[...].astype(BF16)
+
+        @pl.when(lax.bitwise_xor(chip, band) == slot)
+        def _():
+            kept[...] = block[...]
+
+    for slot, block in enumerate((own, near, far, last)):
+        for place in range(sent.shape[0]):
+            store(place, slot, block)
+
+
+def sum_kernel(kept, parts, mine, theirs):
     value = kept[...]
-    for part in parts:
-        value = value + part[...].astype(F32)
+    for place in range(parts.shape[0]):
+        value = value + jnp.where(place == lax.axis_index("band"), 0.0, parts[place].astype(F32))
     rows = mine.shape[0]
     mine[...] = value[:rows]
     theirs[...] = value[rows:]
@@ -140,11 +138,11 @@
     top, bottom = call(pieces_kernel, outs, received, scratch=[pltpu.SemaphoreType.DMA((2,))])
     top, bottom = exchanged(top, "domain", FAR), exchanged(bottom, "domain", NEAR)
     early = call(early_kernel, block * 2, (wavefunctions, theirs, *received))
-    outs = block + [shape(2 * rows, width, dtype=BF16)] * (bands - 1)
+    outs = block + [shape(bands, 2 * rows, width, dtype=BF16)]
     scratch = [pltpu.VMEM((2 * rows, width), F32)]
-    kept, *sent = call(late_kernel, outs, (wavefunctions, theirs, top, bottom, own, *early), scratch=scratch)
-    parts = [exchanged(sent[mask - 1], "band", mask) for mask in reversed(range(1, bands))]
-    mine, others = call(sum_kernel, [shape(rows, width)] * 2, (kept, *parts))
+    kept, sent = call(late_kernel, outs, (wavefunctions, theirs, top, bottom, own, *early), scratch=scratch)
+    parts = lax.all_to_all(sent, "band", 0, 0)
+    mine, others = call(sum_kernel, [shape(rows, width)] * 2, (kept, parts))
     return mine, exchanged(others, "domain", CORE), operator
 
 

time: 71 us -> 75.9 us (1.069)
  blocking collectives: 0 us -> 16.6 us
  waiting for transfers between devices: 40.7 us -> 32.4 us
  starting transfers between devices: 18.1 us -> 14.3 us
    all_to_all x0 -> x1, blocking collectives: none -> 16.6 us  [rotate_square(): parts = lax.all_to_all(sent, 'band', 0, 0)]
    ppermute x12 -> x9, waiting for transfers between devices: 37.8 us -> 29.3 us  [exchanged(): lax.ppermute(value, axis, [(source, source ^ mask) for source in sources...]
    ppermute x12 -> x9, starting transfers between devices: 14.7 us -> 11 us  [exchanged(): lax.ppermute(value, axis, [(source, source ^ mask) for source in sources...]
  transfers between devices with their start and end apart: 13 -> 10, of which waited for: 9 -> 7; matrix products, arithmetic and copies ran while one was open for 0% -> 0% of each run, Pallas kernels for 7% -> 6%
where the time goes in v8:
time: 75.9 us; the launch traced here: 75.6 us
  waiting for transfers between devices  32.4 us (43%)
  blocking collectives  16.6 us (22%)
  starting transfers between devices  14.3 us (19%)
  Pallas kernels  8.9 us (12%)
  local copies, waits for them, and re-layouts  3.13 us (4%)
    ppermute x9, waiting for transfers between devices, exchanged(): lax.ppermute(value, axis, [(source, source ^ mask) for source in sources...  29.3 us
    all_to_all x1, blocking collectives, rotate_square(): parts = lax.all_to_all(sent, 'band', 0, 0)  16.6 us
    ppermute x9, starting transfers between devices, exchanged(): lax.ppermute(value, axis, [(source, source ^ mask) for source in sources...  11 us
    pallas_call x9, Pallas kernels, call(): pl.pallas_call(body, out_shape=outs, in_specs=[pl.BlockSpec(memory_space=...  8.9 us
    ppermute x1, starting transfers between devices, finish_square(): lax.ppermute(outward, 'domain', across + [(target, source) for source, ta...  3.37 us
    unnamed x14, local copies, waits for them, and re-layouts  3.13 us
    ppermute x1, waiting for transfers between devices, finish_square(): lax.ppermute(outward, 'domain', across + [(target, source) for source, ta...  3.12 us
  transfers between devices with their start and end apart: 10, of which 7 were waited for; matrix products, arithmetic and copies ran while one was open for 0% of the time, Pallas kernels for 6%

profile of v8, /device:TPU:1, one launch (start us, length us, event | category | flops | bytes accessed | tf_op | source)
XLA Modules:
  0.0 75.6 jit_solution(8935845099962189397)
XLA Ops:
  0.0 0.1 collective-permute-start
  0.1 0.7 collective-permute-start.2
  0.8 0.7 collective-permute-start.1
  1.5 4.4 %collective-permute-done.refs_1_ = bf16[384,4096]{1,0:T(8,128)(2,1)S(1)} collective-permute-done((bf16[384,4096]{1,0:T(8,128)(2,1)}, bf16[384,4096]{1,0:T(8,128)(2,1)S(1)}, u32[]{:S(2)}, u32[]{:S(2)}) %collective-permute-start) | collective-permute-done | bytes 3145760 | tf_op jit(solution)/shard_map/ppermute | solution.py:34
  5.9 0.0 copy-start
  5.9 1.9 %copy-done = bf16[384,4096]{1,0:T(8,128)(2,1)S(1)} copy-done((bf16[384,4096]{1,0:T(8,128)(2,1)S(1)}, bf16[384,4096]{1,0:T(8,128)(2,1)}, u32[]{:S(2)}) %copy-start) | copy-done | bytes 3145752
  7.8 0.0 copy-start.2
  7.8 1.2 %copy-done.2 = bf16[4096,128]{1,0:T(8,128)(2,1)S(1)} copy-done((bf16[4096,128]{1,0:T(8,128)(2,1)S(1)}, bf16[4096,128]{1,0:T(8,128)(2,1)}, u32[]{:S(2)}) %copy-start.2) | copy-done | bytes 1048600
  9.0 0.0 copy-start.4
  9.0 0.0 copy-start.5
  9.0 0.0 copy-start.6
  9.0 0.0 copy-start.3
  9.0 1.8 %shard_map.55.refs_3_.refs_4_ = f32[768,128]{1,0:T(8,128)S(1)} custom-call(bf16[384,4096]{1,0:T(8,128)(2,1)S(1)} %copy-done, bf16[384,4096]{1,0:T(8,128)(2,1)S(1)} %collective-permute-done.refs_1_, bf16[4096,128]{1,0:T(8,128)(2,1)S(1)} %copy-done.2), custom_call_target="tpu_custom_call" | custom-call | bytes 1024 | tf_op jit(solution)/shard_map/pallas_call | solution.py:43
  10.8 0.0 copy-start.1
  10.8 0.0 copy-done.4
  10.8 0.0 copy-done.5
  10.8 0.0 copy-done.6
  10.8 0.7 shard_map.56
  11.5 0.0 copy-done.3
  11.5 4.4 %collective-permute-start.4 = (bf16[4096,128]{1,0:T(8,128)(2,1)S(1)}, bf16[4096,128]{1,0:T(8,128)(2,1)S(1)}, u32[]{:S(2)}, u32[]{:S(2)}) collective-permute-start(bf16[4096,128]{1,0:T(8,128)(2,1)S(1)} %copy-done.3), channel_id=1, source_target_pairs={{4,20},{12,28},{20,4},{28,12},{5,21},{13,29},{21,5},{29,13},{6,22}... | collective-permute-start | bytes 3145736 | tf_op jit(solution)/shard_map/ppermute | solution.py:34
  16.0 3.1 %collective-permute-start.3 = (bf16[4096,128]{1,0:T(8,128)(2,1)S(1)}, bf16[4096,128]{1,0:T(8,128)(2,1)S(1)}, u32[]{:S(2)}, u32[]{:S(2)}) collective-permute-start(bf16[4096,128]{1,0:T(8,128)(2,1)S(1)} %copy-done.3), channel_id=1, source_target_pairs={{4,12},{12,4},{20,28},{28,20},{5,13},{13,5},{21,29},{29,21},{6,14}... | collective-permute-start | bytes 3145736 | tf_op jit(solution)/shard_map/ppermute | solution.py:34
  19.1 0.0 collective-permute-done.2.refs_1_.refs_3_
  19.1 0.0 collective-permute-done.1.refs_0_.refs_2_
  19.1 13.6 %collective-permute-done.4.refs_3_.refs_5_ = bf16[4096,128]{1,0:T(8,128)(2,1)S(1)} collective-permute-done((bf16[4096,128]{1,0:T(8,128)(2,1)S(1)}, bf16[4096,128]{1,0:T(8,128)(2,1)S(1)}, u32[]{:S(2)}, u32[]{:S(2)}) %collective-permute-start.4) | collective-permute-done | bytes 1048608 | tf_op jit(solution)/shard_map/ppermute | solution.py:34
  32.7 4.6 %collective-permute-done.3.refs_2_.refs_4_ = bf16[4096,128]{1,0:T(8,128)(2,1)S(1)} collective-permute-done((bf16[4096,128]{1,0:T(8,128)(2,1)S(1)}, bf16[4096,128]{1,0:T(8,128)(2,1)S(1)}, u32[]{:S(2)}, u32[]{:S(2)}) %collective-permute-start.3) | collective-permute-done | bytes 1048608 | tf_op jit(solution)/shard_map/ppermute | solution.py:34
  37.3 0.4 shard_map.57
  37.7 0.1 collective-permute-start.5
  37.8 1.6 %collective-permute-start.6 = (bf16[1792,128]{1,0:T(8,128)(2,1)S(1)}, bf16[1792,128]{1,0:T(8,128)(2,1)S(1)}, u32[]{:S(2)}, u32[]{:S(2)}) collective-permute-start(bf16[1792,128]{1,0:T(8,128)(2,1)S(1)} %get-tuple-element.26), channel_id=1, source_target_pairs={{0,8},{4,12},{8,0},{12,4},{16,24},{20,28},{24,16},{28,20},{1,9},{5... | collective-permute-start | bytes 1376264 | tf_op jit(solution)/shard_map/ppermute | solution.py:34
  39.4 0.0 copy-done.1
  39.4 1.8 %shard_map.58 = (f32[768,128]{1,0:T(8,128)S(1)}, f32[768,128]{1,0:T(8,128)S(1)}) custom-call(bf16[384,4096]{1,0:T(8,128)(2,1)S(1)} %copy-done.1, bf16[384,4096]{1,0:T(8,128)(2,1)S(1)} %collective-permute-done.refs_1_, bf16[4096,128]{1,0:T(8,128)(2,1)S(1)} %collective-permute-done.1.refs_0_.refs_2_, ...), custom_call_target="tpu_custom_call" | custom-call | bytes 1024 | tf_op jit(solution)/shard_map/pallas_call | solution.py:43
  41.2 4.1 %collective-permute-done.6.refs_3_ = bf16[1792,128]{1,0:T(8,128)(2,1)S(1)} collective-permute-done((bf16[1792,128]{1,0:T(8,128)(2,1)S(1)}, bf16[1792,128]{1,0:T(8,128)(2,1)S(1)}, u32[]{:S(2)}, u32[]{:S(2)}) %collective-permute-start.6) | collective-permute-done | bytes 458784 | tf_op jit(solution)/shard_map/ppermute | solution.py:34
  45.2 1.3 %collective-permute-done.5.refs_2_ = bf16[2304,128]{1,0:T(8,128)(2,1)S(1)} collective-permute-done((bf16[2304,128]{1,0:T(8,128)(2,1)S(1)}, bf16[2304,128]{1,0:T(8,128)(2,1)S(1)}, u32[]{:S(2)}, u32[]{:S(2)}) %collective-permute-start.5) | collective-permute-done | bytes 589856 | tf_op jit(solution)/shard_map/ppermute | solution.py:34
  46.5 2.1 %shard_map.59 = (f32[768,128]{1,0:T(8,128)S(1)}, bf16[4,768,128]{2,1,0:T(8,128)(2,1)S(1)}) custom-call(bf16[384,4096]{1,0:T(8,128)(2,1)S(1)} %copy-done.1, bf16[384,4096]{1,0:T(8,128)(2,1)S(1)} %collective-permute-done.refs_1_, bf16[2304,128]{1,0:T(8,128)(2,1)S(1)} %collective-permute-done.5.refs_2_, bf16[1792,128]{1,0:T(8,128)(2,1)S(1)} %collective-permute-done.6.refs_3_, ...), custom_call_target="tpu_custom_call" | custom-call | bytes 1024 | tf_op jit(solution)/shard_map/pallas_call | solution.py:43
  48.6 16.6 %all_to_all.5.refs_1_ = bf16[4,768,128]{2,1,0:T(8,128)(2,1)S(1)} all-to-all(bf16[4,768,128]{2,1,0:T(8,128)(2,1)S(1)} %get-tuple-element.30), channel_id=1, replica_groups=mesh['domain'=8,'band'=4] {'band'}, dimensions={0} | all-to-all | bytes 1572864 | tf_op jit(solution)/shard_map/all_to_all | solution.py:144
  65.2 0.2 shard_map.60
  65.4 0.1 collective-permute-start.7
  65.5 1.4 %collective-permute-done.7.refs_1_ = f32[384,128]{1,0:T(8,128)S(1)} collective-permute-done((f32[384,128]{1,0:T(8,128)S(1)}, f32[384,128]{1,0:T(8,128)S(1)}, u32[]{:S(2)}, u32[]{:S(2)}) %collective-permute-start.7) | collective-permute-done | bytes 196640 | tf_op jit(solution)/shard_map/ppermute | solution.py:34
  66.9 0.3 shard_map.61
  67.2 0.2 collective-permute-start.8
  67.4 3.4 %collective-permute-start.9 = (bf16[128,384]{1,0:T(8,128)(2,1)S(1)}, bf16[128,384]{1,0:T(8,128)(2,1)S(1)}, u32[]{:S(2)}, u32[]{:S(2)}) collective-permute-start(bf16[128,384]{1,0:T(8,128)(2,1)S(1)} %get-tuple-element.40), channel_id=1, source_target_pairs={{4,8},{12,16},{20,24},{8,4},{16,12},{24,20},{5,9},{13,17},{21,25},... | collective-permute-start | bytes 294920 | tf_op jit(solution)/shard_map/ppermute | solution.py:202
  70.8 0.4 shard_map.62
  71.2 0.0 collective-permute-done.8.refs_5_
  71.2 3.1 %collective-permute-done.9.refs_6_ = bf16[128,384]{1,0:T(8,128)(2,1)S(1)} collective-permute-done((bf16[128,384]{1,0:T(8,128)(2,1)S(1)}, bf16[128,384]{1,0:T(8,128)(2,1)S(1)}, u32[]{:S(2)}, u32[]{:S(2)}) %collective-permute-start.9) | collective-permute-done | bytes 98336 | tf_op jit(solution)/shard_map/ppermute | solution.py:202
  74.4 1.2 %shard_map.63 = f32[384,256]{1,0:T(8,128)} custom-call(f32[384,256]{1,0:T(8,128)S(1)} %get-tuple-element.35.refs_0_, bf16[128,256]{1,0:T(8,128)(2,1)S(1)} %get-tuple-element.36.refs_1_, bf16[128,256]{1,0:T(8,128)(2,1)S(1)} %get-tuple-element.37.refs_2_, bf16[512,512]{1,0:T(8,128)(2,1)S(1)} %get-tuple-element.23.refs_2_.refs_1_.refs_3_, ...), custom_call_target="tpu_custom_call" | custom-call | bytes 1024 | tf_op jit(solution)/shard_map/pallas_call | solution.py:43
Async XLA Ops:
  0.0 5.9 %collective-permute-start = (bf16[384,4096]{1,0:T(8,128)(2,1)}, bf16[384,4096]{1,0:T(8,128)(2,1)S(1)}, u32[]{:S(2)}, u32[]{:S(2)}) collective-permute-start(bf16[384,4096]{1,0:T(8,128)(2,1)} %refs_0_.7), channel_id=1, source_target_pairs={{0,4},{4,0},{8,12},{12,8},{16,20},{20,16},{24,28},{28,24},{1,5},{5... | collective-permute-start | bytes 9437192 | tf_op jit(solution)/shard_map/ppermute | solution.py:34
  0.1 19.0 %collective-permute-start.2 = (bf16[4096,128]{1,0:T(8,128)(2,1)}, bf16[4096,128]{1,0:T(8,128)(2,1)S(1)}, u32[]{:S(2)}, u32[]{:S(2)}) collective-permute-start(bf16[4096,128]{1,0:T(8,128)(2,1)} %refs_2_.1), channel_id=1, source_target_pairs={{0,16},{8,24},{16,0},{24,8},{1,17},{9,25},{17,1},{25,9},{2,18},{10... | collective-permute-start | bytes 3145736 | tf_op jit(solution)/shard_map/ppermute | solution.py:34
  0.8 18.3 %collective-permute-start.1 = (bf16[4096,128]{1,0:T(8,128)(2,1)}, bf16[4096,128]{1,0:T(8,128)(2,1)S(1)}, u32[]{:S(2)}, u32[]{:S(2)}) collective-permute-start(bf16[4096,128]{1,0:T(8,128)(2,1)} %refs_2_.1), channel_id=1, source_target_pairs={{0,8},{8,0},{16,24},{24,16},{1,9},{9,1},{17,25},{25,17},{2,10},{10... | collective-permute-start | bytes 3145736 | tf_op jit(solution)/shard_map/ppermute | solution.py:34
  5.9 1.9 %copy-start = (bf16[384,4096]{1,0:T(8,128)(2,1)S(1)}, bf16[384,4096]{1,0:T(8,128)(2,1)}, u32[]{:S(2)}) copy-start(bf16[384,4096]{1,0:T(8,128)(2,1)} %refs_0_.7) | copy-start | bytes 9437188
  7.8 1.2 %copy-start.2 = (bf16[4096,128]{1,0:T(8,128)(2,1)S(1)}, bf16[4096,128]{1,0:T(8,128)(2,1)}, u32[]{:S(2)}) copy-start(bf16[4096,128]{1,0:T(8,128)(2,1)} %refs_2_.1) | copy-start | bytes 3145732
  9.0 1.8 %copy-start.4 = (bf16[1,512,512]{2,1,0:T(8,128)(2,1)S(1)}, bf16[1,512,512]{2,1,0:T(8,128)(2,1)}, u32[]{:S(2)}) copy-start(bf16[1,512,512]{2,1,0:T(8,128)(2,1)} %refs_0_.5) | copy-start | bytes 1572868
  9.0 1.8 %copy-start.5 = (s32[1,512]{1,0:T(1,128)S(1)}, s32[1,512]{1,0:T(1,128)}, u32[]{:S(2)}) copy-start(s32[1,512]{1,0:T(1,128)} %refs_1_.1) | copy-start | bytes 6148
  9.0 1.8 %copy-start.6 = (s32[128]{0:T(128)S(1)}, s32[128]{0:T(128)}, u32[]{:S(2)}) copy-start(s32[128]{0:T(128)} %param.9) | copy-start | bytes 1540
  9.0 2.5 %copy-start.3 = (bf16[4096,128]{1,0:T(8,128)(2,1)S(1)}, bf16[4096,128]{1,0:T(8,128)(2,1)}, u32[]{:S(2)}) copy-start(bf16[4096,128]{1,0:T(8,128)(2,1)} %refs_2_.1) | copy-start | bytes 3145732
  10.8 28.6 %copy-start.1 = (bf16[384,4096]{1,0:T(8,128)(2,1)S(1)}, bf16[384,4096]{1,0:T(8,128)(2,1)}, u32[]{:S(2)}) copy-start(bf16[384,4096]{1,0:T(8,128)(2,1)} %refs_0_.7) | copy-start | bytes 9437188
  11.5 21.1 %collective-permute-start.4 = (bf16[4096,128]{1,0:T(8,128)(2,1)S(1)}, bf16[4096,128]{1,0:T(8,128)(2,1)S(1)}, u32[]{:S(2)}, u32[]{:S(2)}) collective-permute-start(bf16[4096,128]{1,0:T(8,128)(2,1)S(1)} %copy-done.3), channel_id=1, source_target_pairs={{4,20},{12,28},{20,4},{28,12},{5,21},{13,29},{21,5},{29,13},{6,22}... | collective-permute-start | bytes 3145736 | tf_op jit(solution)/shard_map/ppermute | solution.py:34
  16.0 21.3 %collective-permute-start.3 = (bf16[4096,128]{1,0:T(8,128)(2,1)S(1)}, bf16[4096,128]{1,0:T(8,128)(2,1)S(1)}, u32[]{:S(2)}, u32[]{:S(2)}) collective-permute-start(bf16[4096,128]{1,0:T(8,128)(2,1)S(1)} %copy-done.3), channel_id=1, source_target_pairs={{4,12},{12,4},{20,28},{28,20},{5,13},{13,5},{21,29},{29,21},{6,14}... | collective-permute-start | bytes 3145736 | tf_op jit(solution)/shard_map/ppermute | solution.py:34
  37.7 8.8 %collective-permute-start.5 = (bf16[2304,128]{1,0:T(8,128)(2,1)S(1)}, bf16[2304,128]{1,0:T(8,128)(2,1)S(1)}, u32[]{:S(2)}, u32[]{:S(2)}) collective-permute-start(bf16[2304,128]{1,0:T(8,128)(2,1)S(1)} %get-tuple-element.25), channel_id=1, source_target_pairs={{0,16},{4,20},{8,24},{12,28},{16,0},{20,4},{24,8},{28,12},{1,17},{... | collective-permute-start | bytes 1769480 | tf_op jit(solution)/shard_map/ppermute | solution.py:34
  37.8 7.5 %collective-permute-start.6 = (bf16[1792,128]{1,0:T(8,128)(2,1)S(1)}, bf16[1792,128]{1,0:T(8,128)(2,1)S(1)}, u32[]{:S(2)}, u32[]{:S(2)}) collective-permute-start(bf16[1792,128]{1,0:T(8,128)(2,1)S(1)} %get-tuple-element.26), channel_id=1, source_target_pairs={{0,8},{4,12},{8,0},{12,4},{16,24},{20,28},{24,16},{28,20},{1,9},{5... | collective-permute-start | bytes 1376264 | tf_op jit(solution)/shard_map/ppermute | solution.py:34
  65.4 1.5 %collective-permute-start.7 = (f32[384,128]{1,0:T(8,128)S(1)}, f32[384,128]{1,0:T(8,128)S(1)}, u32[]{:S(2)}, u32[]{:S(2)}) collective-permute-start(f32[384,128]{1,0:T(8,128)S(1)} %get-tuple-element.32), channel_id=1, source_target_pairs={{0,4},{4,0},{8,12},{12,8},{16,20},{20,16},{24,28},{28,24},{1,5},{5... | collective-permute-start | bytes 589832 | tf_op jit(solution)/shard_map/ppermute | solution.py:34
  67.2 4.0 %collective-permute-start.8 = (bf16[128,384]{1,0:T(8,128)(2,1)S(1)}, bf16[128,384]{1,0:T(8,128)(2,1)S(1)}, u32[]{:S(2)}, u32[]{:S(2)}) collective-permute-start(bf16[128,384]{1,0:T(8,128)(2,1)S(1)} %get-tuple-element.39), channel_id=1, source_target_pairs={{0,4},{4,0},{8,12},{12,8},{16,20},{20,16},{24,28},{28,24},{1,5},{5... | collective-permute-start | bytes 294920 | tf_op jit(solution)/shard_map/ppermute | solution.py:34
  67.4 7.0 %collective-permute-start.9 = (bf16[128,384]{1,0:T(8,128)(2,1)S(1)}, bf16[128,384]{1,0:T(8,128)(2,1)S(1)}, u32[]{:S(2)}, u32[]{:S(2)}) collective-permute-start(bf16[128,384]{1,0:T(8,128)(2,1)S(1)} %get-tuple-element.40), channel_id=1, source_target_pairs={{4,8},{12,16},{20,24},{8,4},{16,12},{24,20},{5,9},{13,17},{21,25},... | collective-permute-start | bytes 294920 | tf_op jit(solution)/shard_map/ppermute | solution.py:202

commit v9 on v7

--- a/solution.py
+++ b/solution.py
@@ -63,19 +63,19 @@
     return lax.bitwise_xor(lax.div(lax.axis_index("domain"), 2), lax.axis_index("band"))
 
 
-def pieces_kernel(near_even, far_even, near_odd, far_odd, top, bottom, done):
-    def fill(near, far):
-        copies = [
-            pltpu.make_async_copy(near.at[pl.ds(0, top.shape[0])], top, done.at[0]),
-            pltpu.make_async_copy(far.at[pl.ds(top.shape[0], bottom.shape[0])], bottom, done.at[1]),
-        ]
+def pieces_kernel(near_even, far_even, near_odd, far_first, far_rest, top, bottom, done):
+    upper, lower = pl.ds(0, top.shape[0]), pl.ds(top.shape[0], bottom.shape[0])
+    rest = pl.ds(top.shape[0] - far_first.shape[0], bottom.shape[0])
+
+    def fill(*pairs):
+        copies = [pltpu.make_async_copy(source, target, done.at[number]) for number, (source, target) in enumerate(pairs)]
         for copy in copies:
             copy.start()
         for copy in copies:
             copy.wait()
 
-    pl.when(core() == 0)(lambda: fill(near_even, far_even))
-    pl.when(core() != 0)(lambda: fill(near_odd, far_odd))
+    pl.when(core() == 0)(lambda: fill((near_even.at[upper], top), (far_even.at[lower], bottom)))
+    pl.when(core() != 0)(lambda: fill((near_odd.at[upper], top), (far_rest.at[rest], bottom)))
 
 
 def own_kernel(mine, theirs, own, block):
@@ -84,10 +84,11 @@
         block[side * rows : (side + 1) * rows] = jnp.dot(states[...], own[...], preferred_element_type=F32)
 
 
-def early_kernel(mine, theirs, near_even, far_even, near_odd, far_odd, near_block, far_block):
+def early_kernel(mine, theirs, near_even, far_even, near_odd, far_first, far_rest, near_block, far_block):
     rows, width = mine.shape[0], near_even.shape[1]
     first = core() == 0
-    near, far = jnp.where(first, near_even[...], near_odd[...]), jnp.where(first, far_even[...], far_odd[...])
+    far_odd = jnp.concatenate([far_first[...], far_rest[...]], 0)
+    near, far = jnp.where(first, near_even[...], near_odd[...]), jnp.where(first, far_even[...], far_odd)
     wide = jnp.concatenate([near, far], 1)
     for side, states in enumerate((mine, theirs)):
         result = jnp.dot(states[...], wide, preferred_element_type=F32)
@@ -95,13 +96,20 @@
         far_block[side * rows : (side + 1) * rows] = result[:, width:]
 
 
-def late_kernel(mine, theirs, top, bottom, own, near, far, kept, *refs):
+def lower_kernel(mine, theirs, bottom, block):
+    start, rows = mine.shape[1] - bottom.shape[0], mine.shape[0]
+    for side, states in enumerate((mine, theirs)):
+        result = jnp.dot(states[:, start:], bottom[...], preferred_element_type=F32)
+        block[side * rows : (side + 1) * rows] = result
+
+
+def late_kernel(mine, theirs, top, lower, own, near, far, kept, *refs):
     sent, last = refs[:-1], refs[-1]
     cut = top.shape[0]
     rows = mine.shape[0]
     for side, states in enumerate((mine, theirs)):
-        result = jnp.dot(states[:, :cut], top[...], preferred_element_type=F32)
-        last[side * rows : (side + 1) * rows] = result + jnp.dot(states[:, cut:], bottom[...], preferred_element_type=F32)
+        span = slice(side * rows, (side + 1) * rows)
+        last[span] = lower[span] + jnp.dot(states[:, :cut], top[...], preferred_element_type=F32)
     where = block_of_band()
 
     def store(out, slot, block):
@@ -128,21 +136,23 @@
     bands, chips = lax.axis_size("band"), lax.axis_size("domain") // 2
     rows, states = wavefunctions.shape
     width = rotation.shape[1]
-    cut = states * 9 // 16
+    cut, part = states // 2, states // 4
+    first = exchanged(rotation[:part], "domain", FAR, CORE)
     received = [exchanged(rotation, "domain", NEAR, 0), exchanged(rotation, "domain", FAR, 0)]
     theirs = exchanged(wavefunctions, "domain", CORE)
+    later, _, first = lax.optimization_barrier((rotation, theirs, first))
+    received += [exchanged(later, "domain", NEAR, CORE), first, exchanged(later[part:], "domain", FAR, CORE)]
     block = [shape(2 * rows, width)]
-    own = call(own_kernel, block, (wavefunctions, theirs, rotation))[0]
+    own = call(own_kernel, block, (wavefunctions, theirs, rotation), after=(later,))[0]
     operator = operator(own)
-    later, _ = lax.optimization_barrier((rotation, operator[0]))
-    received += [exchanged(later, "domain", NEAR, CORE), exchanged(later, "domain", FAR, CORE)]
     outs = [shape(count, width, dtype=BF16) for count in (cut, states - cut)]
-    top, bottom = call(pieces_kernel, outs, received, scratch=[pltpu.SemaphoreType.DMA((2,))])
+    top, bottom = call(pieces_kernel, outs, received, after=operator[:1], scratch=[pltpu.SemaphoreType.DMA((2,))])
     top, bottom = exchanged(top, "domain", FAR), exchanged(bottom, "domain", NEAR)
     early = call(early_kernel, block * 2, (wavefunctions, theirs, *received))
     outs = block + [shape(2 * rows, width, dtype=BF16)] * (bands - 1)
     scratch = [pltpu.VMEM((2 * rows, width), F32)]
-    kept, *sent = call(late_kernel, outs, (wavefunctions, theirs, top, bottom, own, *early), scratch=scratch)
+    lower = call(lower_kernel, block, (wavefunctions, theirs, bottom))[0]
+    kept, *sent = call(late_kernel, outs, (wavefunctions, theirs, top, lower, own, *early), scratch=scratch)
     parts = [exchanged(sent[mask - 1], "band", mask) for mask in reversed(range(1, bands))]
     mine, others = call(sum_kernel, [shape(rows, width)] * 2, (kept, *parts))
     return mine, exchanged(others, "domain", CORE), operator
@@ -174,24 +184,24 @@
     pl.when(jnp.logical_not(first))(lambda: store(outward, inward))
 
 
-def inner_kernel(total, assembled, pick, out, face_high, face_low):
-    own = total.shape[0]
+def inner_kernel(total, assembled, pick, out, faces):
+    own, columns = total.shape
     high, low = split(total[...])
     inner = assembled[:own, :own]
     out[...] = dot(inner, high) + dot(inner, low)
-    face_high[...] = dot(pick[...], high).astype(BF16)
-    face_low[...] = dot(pick[...], low).astype(BF16)
-
-
-def final_kernel(inner, face_high, face_low, assembled, spread, inward, outward, out):
+    faces[:, :columns] = dot(pick[...], high).astype(BF16)
+    faces[:, columns:] = dot(pick[...], low).astype(BF16)
+
+
+def final_kernel(inner, faces, assembled, spread, inward, outward, out):
     own, columns = inner.shape
     first = core() == 0
     incoming = jnp.where(first, inward[:, :columns], outward[:, :columns])
     back = jnp.where(first, outward[...], inward[...])
-    corner = back[:, columns:]
-    value = back[:, :columns].astype(F32) + dot(corner, face_high[...]) + dot(corner, face_low[...])
-    high, low = split(value)
-    out[...] = inner[...] + dot(assembled[:own, own:], incoming) + dot(spread[...], high) + dot(spread[...], low)
+    extra = dot(back[:, columns:], faces[...])
+    high, low = split(back[:, :columns].astype(F32) + extra[:, :columns] + extra[:, columns:])
+    matrix = jnp.concatenate([assembled[:own, own:], spread[...], spread[...]], 1)
+    out[...] = inner[...] + dot(matrix, jnp.concatenate([incoming, high, low], 0))
 
 
 def finish_square(mine, other, operator):
@@ -203,9 +213,9 @@
     across = [(place, place + 1) for place in range(CORE, lax.axis_size("domain") - 1, 2)]
     outward = lax.ppermute(outward, "domain", across + [(target, source) for source, target in across])
     inward = exchanged(inward, "domain", CORE)
-    outs = [shape(rows, columns)] + [shape(shared, columns, dtype=BF16)] * 2
-    inner, *face = call(inner_kernel, outs, (total, assembled, pick))
-    return call(final_kernel, outs[:1], (inner, *face, assembled, spread, inward, outward))[0]
+    outs = [shape(rows, columns), shape(shared, 2 * columns, dtype=BF16)]
+    inner, faces = call(inner_kernel, outs, (total, assembled, pick))
+    return call(final_kernel, outs[:1], (inner, faces, assembled, spread, inward, outward))[0]
 
 
 def finish_any(rotated, cell_matrices, cell_nodes, face_map):

time: 71 us -> 73.6 us (1.037)
  starting transfers between devices: 18.1 us -> 22.1 us
  waiting for transfers between devices: 40.7 us -> 36.9 us
  local copies, waits for them, and re-layouts: 3.13 us -> 5.29 us
    ppermute x12 -> x13, starting transfers between devices: 14.7 us -> 18.9 us  [exchanged(): lax.ppermute(value, axis, [(source, source ^ mask) for source in sources...]
    ppermute x12 -> x13, waiting for transfers between devices: 37.8 us -> 34.2 us  [exchanged(): lax.ppermute(value, axis, [(source, source ^ mask) for source in sources...]
    slice x0 -> x2, local copies, waits for them, and re-layouts: none -> 2.16 us  [the longest x1 1.2 us: rotate_square(): later[part:]]
    pallas_call x9 -> x10, Pallas kernels: 8.66 us -> 8.48 us  [call(): pl.pallas_call(body, out_shape=outs, in_specs=[pl.BlockSpec(memory_space=...]
    unnamed x14 -> x12, local copies, waits for them, and re-layouts: 3.13 us -> 3.13 us
  transfers between devices with their start and end apart: 13 -> 14, of which waited for: 9 -> 8; matrix products, arithmetic and copies ran while one was open for 0% -> 3% of each run, Pallas kernels for 7% -> 8%
where the time goes in v9:
time: 73.6 us; the launch traced here: 73 us
  waiting for transfers between devices  36.9 us (50%)
  starting transfers between devices  22.1 us (30%)
  Pallas kernels  8.48 us (12%)
  local copies, waits for them, and re-layouts  5.29 us (7%)
    ppermute x13, waiting for transfers between devices, exchanged(): lax.ppermute(value, axis, [(source, source ^ mask) for source in sources...  34.2 us
    ppermute x13, starting transfers between devices, exchanged(): lax.ppermute(value, axis, [(source, source ^ mask) for source in sources...  18.9 us
    pallas_call x10, Pallas kernels, call(): pl.pallas_call(body, out_shape=outs, in_specs=[pl.BlockSpec(memory_space=...  8.48 us
    ppermute x1, starting transfers between devices, finish_square(): lax.ppermute(outward, 'domain', across + [(target, source) for source, ta...  3.2 us
    unnamed x12, local copies, waits for them, and re-layouts  3.13 us
    ppermute x1, waiting for transfers between devices, finish_square(): lax.ppermute(outward, 'domain', across + [(target, source) for source, ta...  2.7 us
  transfers between devices with their start and end apart: 14, of which 8 were waited for; matrix products, arithmetic and copies ran while one was open for 3% of the time, Pallas kernels for 8%

profile of v9, /device:TPU:1, one launch (start us, length us, event | category | flops | bytes accessed | tf_op | source)
XLA Modules:
  0.0 73.0 jit_solution(6649375722603447660)
XLA Ops:
  0.0 0.1 collective-permute-start
  0.1 1.0 %slice.6 = bf16[1024,128]{1,0:T(8,128)(2,1)S(1)} slice(bf16[4096,128]{1,0:T(8,128)(2,1)} %refs_3_), slice={[0:1024], [0:128]} | slice | bytes 524288 | tf_op jit(solution)/shard_map/slice | solution.py:140
  1.0 4.6 %collective-permute-start.3 = (bf16[1024,128]{1,0:T(8,128)(2,1)S(1)}, bf16[1024,128]{1,0:T(8,128)(2,1)S(1)}, u32[]{:S(2)}, u32[]{:S(2)}) collective-permute-start(bf16[1024,128]{1,0:T(8,128)(2,1)S(1)} %slice.6), channel_id=1, source_target_pairs={{4,20},{12,28},{20,4},{28,12},{5,21},{13,29},{21,5},{29,13},{6,22}... | collective-permute-start | bytes 786440 | tf_op jit(solution)/shard_map/ppermute | solution.py:34
  5.6 0.7 collective-permute-start.1
  6.4 0.7 collective-permute-start.2
  7.1 2.6 %collective-permute-done.3.refs_3_.refs_5_ = bf16[1024,128]{1,0:T(8,128)(2,1)S(1)} collective-permute-done((bf16[1024,128]{1,0:T(8,128)(2,1)S(1)}, bf16[1024,128]{1,0:T(8,128)(2,1)S(1)}, u32[]{:S(2)}, u32[]{:S(2)}) %collective-permute-start.3) | collective-permute-done | bytes 262176 | tf_op jit(solution)/shard_map/ppermute | solution.py:34
  9.7 0.0 collective-permute-done.refs_1_
  9.7 3.3 %collective-permute-start.4 = (bf16[4096,128]{1,0:T(8,128)(2,1)}, bf16[4096,128]{1,0:T(8,128)(2,1)S(1)}, u32[]{:S(2)}, u32[]{:S(2)}) collective-permute-start(bf16[4096,128]{1,0:T(8,128)(2,1)} %refs_3_), channel_id=1, source_target_pairs={{4,12},{12,4},{20,28},{28,20},{5,13},{13,5},{21,29},{29,21},{6,14}... | collective-permute-start | bytes 3145736 | tf_op jit(solution)/shard_map/ppermute | solution.py:34
  13.0 1.2 %slice.7 = bf16[3072,128]{1,0:T(8,128)(2,1)S(1)} slice(bf16[4096,128]{1,0:T(8,128)(2,1)} %refs_3_), slice={[1024:4096], [0:128]} | slice | bytes 1572864 | tf_op jit(solution)/shard_map/slice | solution.py:144
  14.2 3.1 %collective-permute-start.5 = (bf16[3072,128]{1,0:T(8,128)(2,1)S(1)}, bf16[3072,128]{1,0:T(8,128)(2,1)S(1)}, u32[]{:S(2)}, u32[]{:S(2)}) collective-permute-start(bf16[3072,128]{1,0:T(8,128)(2,1)S(1)} %slice.7), channel_id=1, source_target_pairs={{4,20},{12,28},{20,4},{28,12},{5,21},{13,29},{21,5},{29,13},{6,22}... | collective-permute-start | bytes 2359304 | tf_op jit(solution)/shard_map/ppermute | solution.py:34
  17.4 0.0 copy-start
  17.4 1.9 %copy-done = bf16[384,4096]{1,0:T(8,128)(2,1)S(1)} copy-done((bf16[384,4096]{1,0:T(8,128)(2,1)S(1)}, bf16[384,4096]{1,0:T(8,128)(2,1)}, u32[]{:S(2)}) %copy-start) | copy-done | bytes 3145752
  19.3 0.0 copy-start.2
  19.3 1.2 %copy-done.2 = bf16[4096,128]{1,0:T(8,128)(2,1)S(1)} copy-done((bf16[4096,128]{1,0:T(8,128)(2,1)S(1)}, bf16[4096,128]{1,0:T(8,128)(2,1)}, u32[]{:S(2)}) %copy-start.2) | copy-done | bytes 1048600
  20.5 0.0 copy-start.3
  20.5 0.0 copy-start.4
  20.5 0.0 copy-start.5
  20.5 1.8 %shard_map.55.refs_3_.refs_4_ = f32[768,128]{1,0:T(8,128)S(1)} custom-call(bf16[384,4096]{1,0:T(8,128)(2,1)S(1)} %copy-done, bf16[384,4096]{1,0:T(8,128)(2,1)S(1)} %collective-permute-done.refs_1_, bf16[4096,128]{1,0:T(8,128)(2,1)S(1)} %copy-done.2, bf16[4096,128]{1,0:T(8,128)(2,1)S(1)} %copy-done.2), custom_call_target="tpu_custom_call" | custom-call | bytes 1024 | tf_op jit(solution)/shard_map/pallas_call | solution.py:43
  22.3 0.0 copy-start.1
  22.3 0.0 copy-done.3
  22.3 0.0 copy-done.4
  22.3 0.0 copy-done.5
  22.3 0.7 shard_map.56
  23.0 0.0 collective-permute-done.1.refs_0_.refs_2_
  23.0 0.0 collective-permute-done.2.refs_1_.refs_3_
  23.0 8.8 %collective-permute-done.5.refs_4_.refs_6_ = bf16[3072,128]{1,0:T(8,128)(2,1)S(1)} collective-permute-done((bf16[3072,128]{1,0:T(8,128)(2,1)S(1)}, bf16[3072,128]{1,0:T(8,128)(2,1)S(1)}, u32[]{:S(2)}, u32[]{:S(2)}) %collective-permute-start.5) | collective-permute-done | bytes 786464 | tf_op jit(solution)/shard_map/ppermute | solution.py:34
  31.8 0.0 collective-permute-done.4.refs_2_.refs_4_
  31.8 0.1 shard_map.57
  31.9 1.6 %collective-permute-start.7 = (bf16[2048,128]{1,0:T(8,128)(2,1)S(1)}, bf16[2048,128]{1,0:T(8,128)(2,1)S(1)}, u32[]{:S(2)}, u32[]{:S(2)}) collective-permute-start(bf16[2048,128]{1,0:T(8,128)(2,1)S(1)} %get-tuple-element.29), channel_id=1, source_target_pairs={{0,8},{4,12},{8,0},{12,4},{16,24},{20,28},{24,16},{28,20},{1,9},{5... | collective-permute-start | bytes 1572872 | tf_op jit(solution)/shard_map/ppermute | solution.py:34
  33.6 0.7 collective-permute-start.6
  34.3 0.0 copy-done.1
  34.3 1.8 %shard_map.59 = (f32[768,128]{1,0:T(8,128)S(1)}, f32[768,128]{1,0:T(8,128)S(1)}) custom-call(bf16[384,4096]{1,0:T(8,128)(2,1)S(1)} %copy-done.1, bf16[384,4096]{1,0:T(8,128)(2,1)S(1)} %collective-permute-done.refs_1_, bf16[4096,128]{1,0:T(8,128)(2,1)S(1)} %collective-permute-done.1.refs_0_.refs_2_, ...), custom_call_target="tpu_custom_call" | custom-call | bytes 1024 | tf_op jit(solution)/shard_map/pallas_call | solution.py:43
  36.1 5.9 %collective-permute-done.7.refs_2_ = bf16[2048,128]{1,0:T(8,128)(2,1)S(1)} collective-permute-done((bf16[2048,128]{1,0:T(8,128)(2,1)S(1)}, bf16[2048,128]{1,0:T(8,128)(2,1)S(1)}, u32[]{:S(2)}, u32[]{:S(2)}) %collective-permute-start.7) | collective-permute-done | bytes 524320 | tf_op jit(solution)/shard_map/ppermute | solution.py:34
  42.0 1.0 %shard_map.58.refs_3_ = f32[768,128]{1,0:T(8,128)S(1)} custom-call(bf16[384,4096]{1,0:T(8,128)(2,1)S(1)} %copy-done.1, bf16[384,4096]{1,0:T(8,128)(2,1)S(1)} %collective-permute-done.refs_1_, bf16[2048,128]{1,0:T(8,128)(2,1)S(1)} %collective-permute-done.7.refs_2_), custom_call_target="tpu_custom_call" | custom-call | bytes 1024 | tf_op jit(solution)/shard_map/pallas_call | solution.py:43
  42.9 0.0 collective-permute-done.6.refs_2_
  43.0 1.1 %shard_map.60 = (f32[768,128]{1,0:T(8,128)S(1)}, bf16[768,128]{1,0:T(8,128)(2,1)S(1)}, bf16[768,128]{1,0:T(8,128)(2,1)S(1)}, bf16[768,128]{1,0:T(8,128)(2,1)S(1)}) custom-call(bf16[384,4096]{1,0:T(8,128)(2,1)S(1)} %copy-done.1, bf16[384,4096]{1,0:T(8,128)(2,1)S(1)} %collective-permute-done.refs_1_, bf16[2048,128]{1,0:T(8,128)(2,1)S(1)} %collective-permute-done.6.refs_2_, ...), custom_call_target="tpu_custom_call" | custom-call | bytes 1024 | tf_op jit(solution)/shard_map/pallas_call | solution.py:43
  44.1 1.4 %collective-permute-start.10 = (bf16[768,128]{1,0:T(8,128)(2,1)S(1)}, bf16[768,128]{1,0:T(8,128)(2,1)S(1)}, u32[]{:S(2)}, u32[]{:S(2)}) collective-permute-start(bf16[768,128]{1,0:T(8,128)(2,1)S(1)} %get-tuple-element.35), channel_id=1, source_target_pairs={{0,1},{1,0},{2,3},{3,2},{4,5},{5,4},{6,7},{7,6},{8,9},{9,8},{10,11... | collective-permute-start | bytes 589832 | tf_op jit(solution)/shard_map/ppermute | solution.py:34
  45.5 2.2 %collective-permute-start.8 = (bf16[768,128]{1,0:T(8,128)(2,1)S(1)}, bf16[768,128]{1,0:T(8,128)(2,1)S(1)}, u32[]{:S(2)}, u32[]{:S(2)}) collective-permute-start(bf16[768,128]{1,0:T(8,128)(2,1)S(1)} %get-tuple-element.33), channel_id=1, source_target_pairs={{0,3},{1,2},{2,1},{3,0},{4,7},{5,6},{6,5},{7,4},{8,11},{9,10},{10,... | collective-permute-start | bytes 589832 | tf_op jit(solution)/shard_map/ppermute | solution.py:34
  47.6 0.1 collective-permute-start.9
  47.8 2.2 %collective-permute-done.10.refs_3_ = bf16[768,128]{1,0:T(8,128)(2,1)S(1)} collective-permute-done((bf16[768,128]{1,0:T(8,128)(2,1)S(1)}, bf16[768,128]{1,0:T(8,128)(2,1)S(1)}, u32[]{:S(2)}, u32[]{:S(2)}) %collective-permute-start.10) | collective-permute-done | bytes 196640 | tf_op jit(solution)/shard_map/ppermute | solution.py:34
  50.0 6.9 %collective-permute-done.8.refs_1_ = bf16[768,128]{1,0:T(8,128)(2,1)S(1)} collective-permute-done((bf16[768,128]{1,0:T(8,128)(2,1)S(1)}, bf16[768,128]{1,0:T(8,128)(2,1)S(1)}, u32[]{:S(2)}, u32[]{:S(2)}) %collective-permute-start.8) | collective-permute-done | bytes 196640 | tf_op jit(solution)/shard_map/ppermute | solution.py:34
  56.9 6.4 %collective-permute-done.9.refs_2_ = bf16[768,128]{1,0:T(8,128)(2,1)S(1)} collective-permute-done((bf16[768,128]{1,0:T(8,128)(2,1)S(1)}, bf16[768,128]{1,0:T(8,128)(2,1)S(1)}, u32[]{:S(2)}, u32[]{:S(2)}) %collective-permute-start.9) | collective-permute-done | bytes 196640 | tf_op jit(solution)/shard_map/ppermute | solution.py:34
  63.3 0.1 shard_map.61
  63.4 0.1 collective-permute-start.11
  63.4 1.4 %collective-permute-done.11.refs_1_ = f32[384,128]{1,0:T(8,128)S(1)} collective-permute-done((f32[384,128]{1,0:T(8,128)S(1)}, f32[384,128]{1,0:T(8,128)S(1)}, u32[]{:S(2)}, u32[]{:S(2)}) %collective-permute-start.11) | collective-permute-done | bytes 196640 | tf_op jit(solution)/shard_map/ppermute | solution.py:34
  64.9 0.3 shard_map.62
  65.2 0.2 collective-permute-start.12
  65.4 3.2 %collective-permute-start.13 = (bf16[128,384]{1,0:T(8,128)(2,1)S(1)}, bf16[128,384]{1,0:T(8,128)(2,1)S(1)}, u32[]{:S(2)}, u32[]{:S(2)}) collective-permute-start(bf16[128,384]{1,0:T(8,128)(2,1)S(1)} %get-tuple-element.44), channel_id=1, source_target_pairs={{4,8},{12,16},{20,24},{8,4},{16,12},{24,20},{5,9},{13,17},{21,25},... | collective-permute-start | bytes 294920 | tf_op jit(solution)/shard_map/ppermute | solution.py:214
  68.6 0.4 shard_map.63
  69.1 0.0 collective-permute-done.12.refs_4_
  69.1 2.7 %collective-permute-done.13.refs_5_ = bf16[128,384]{1,0:T(8,128)(2,1)S(1)} collective-permute-done((bf16[128,384]{1,0:T(8,128)(2,1)S(1)}, bf16[128,384]{1,0:T(8,128)(2,1)S(1)}, u32[]{:S(2)}, u32[]{:S(2)}) %collective-permute-start.13) | collective-permute-done | bytes 98336 | tf_op jit(solution)/shard_map/ppermute | solution.py:214
  71.8 1.2 %shard_map.64 = f32[384,256]{1,0:T(8,128)} custom-call(f32[384,256]{1,0:T(8,128)S(1)} %get-tuple-element.40.refs_0_, bf16[128,512]{1,0:T(8,128)(2,1)S(1)} %get-tuple-element.41.refs_1_, bf16[512,512]{1,0:T(8,128)(2,1)S(1)} %get-tuple-element.27.refs_5_.refs_2_.refs_1_, bf16[384,128]{1,0:T(8,128)(2,1)S(1)} %get-tuple-element.42.refs_3_, ...), custom_call_target="tpu_custom_call" | custom-call | bytes 1024 | tf_op jit(solution)/shard_map/pallas_call | solution.py:43
Async XLA Ops:
  0.0 9.7 %collective-permute-start = (bf16[384,4096]{1,0:T(8,128)(2,1)}, bf16[384,4096]{1,0:T(8,128)(2,1)S(1)}, u32[]{:S(2)}, u32[]{:S(2)}) collective-permute-start(bf16[384,4096]{1,0:T(8,128)(2,1)} %refs_0_.9), channel_id=1, source_target_pairs={{0,4},{4,0},{8,12},{12,8},{16,20},{20,16},{24,28},{28,24},{1,5},{5... | collective-permute-start | bytes 9437192 | tf_op jit(solution)/shard_map/ppermute | solution.py:34
  1.0 8.6 %collective-permute-start.3 = (bf16[1024,128]{1,0:T(8,128)(2,1)S(1)}, bf16[1024,128]{1,0:T(8,128)(2,1)S(1)}, u32[]{:S(2)}, u32[]{:S(2)}) collective-permute-start(bf16[1024,128]{1,0:T(8,128)(2,1)S(1)} %slice.6), channel_id=1, source_target_pairs={{4,20},{12,28},{20,4},{28,12},{5,21},{13,29},{21,5},{29,13},{6,22}... | collective-permute-start | bytes 786440 | tf_op jit(solution)/shard_map/ppermute | solution.py:34
  5.6 17.4 %collective-permute-start.1 = (bf16[4096,128]{1,0:T(8,128)(2,1)}, bf16[4096,128]{1,0:T(8,128)(2,1)S(1)}, u32[]{:S(2)}, u32[]{:S(2)}) collective-permute-start(bf16[4096,128]{1,0:T(8,128)(2,1)} %refs_3_), channel_id=1, source_target_pairs={{0,8},{8,0},{16,24},{24,16},{1,9},{9,1},{17,25},{25,17},{2,10},{10... | collective-permute-start | bytes 3145736 | tf_op jit(solution)/shard_map/ppermute | solution.py:34
  6.4 16.7 %collective-permute-start.2 = (bf16[4096,128]{1,0:T(8,128)(2,1)}, bf16[4096,128]{1,0:T(8,128)(2,1)S(1)}, u32[]{:S(2)}, u32[]{:S(2)}) collective-permute-start(bf16[4096,128]{1,0:T(8,128)(2,1)} %refs_3_), channel_id=1, source_target_pairs={{0,16},{8,24},{16,0},{24,8},{1,17},{9,25},{17,1},{25,9},{2,18},{10... | collective-permute-start | bytes 3145736 | tf_op jit(solution)/shard_map/ppermute | solution.py:34
  9.7 22.2 %collective-permute-start.4 = (bf16[4096,128]{1,0:T(8,128)(2,1)}, bf16[4096,128]{1,0:T(8,128)(2,1)S(1)}, u32[]{:S(2)}, u32[]{:S(2)}) collective-permute-start(bf16[4096,128]{1,0:T(8,128)(2,1)} %refs_3_), channel_id=1, source_target_pairs={{4,12},{12,4},{20,28},{28,20},{5,13},{13,5},{21,29},{29,21},{6,14}... | collective-permute-start | bytes 3145736 | tf_op jit(solution)/shard_map/ppermute | solution.py:34
  14.2 17.6 %collective-permute-start.5 = (bf16[3072,128]{1,0:T(8,128)(2,1)S(1)}, bf16[3072,128]{1,0:T(8,128)(2,1)S(1)}, u32[]{:S(2)}, u32[]{:S(2)}) collective-permute-start(bf16[3072,128]{1,0:T(8,128)(2,1)S(1)} %slice.7), channel_id=1, source_target_pairs={{4,20},{12,28},{20,4},{28,12},{5,21},{13,29},{21,5},{29,13},{6,22}... | collective-permute-start | bytes 2359304 | tf_op jit(solution)/shard_map/ppermute | solution.py:34
  17.4 1.9 %copy-start = (bf16[384,4096]{1,0:T(8,128)(2,1)S(1)}, bf16[384,4096]{1,0:T(8,128)(2,1)}, u32[]{:S(2)}) copy-start(bf16[384,4096]{1,0:T(8,128)(2,1)} %refs_0_.9) | copy-start | bytes 9437188
  19.3 1.2 %copy-start.2 = (bf16[4096,128]{1,0:T(8,128)(2,1)S(1)}, bf16[4096,128]{1,0:T(8,128)(2,1)}, u32[]{:S(2)}) copy-start(bf16[4096,128]{1,0:T(8,128)(2,1)} %refs_3_) | copy-start | bytes 3145732
  20.5 1.8 %copy-start.3 = (bf16[1,512,512]{2,1,0:T(8,128)(2,1)S(1)}, bf16[1,512,512]{2,1,0:T(8,128)(2,1)}, u32[]{:S(2)}) copy-start(bf16[1,512,512]{2,1,0:T(8,128)(2,1)} %refs_0_.6) | copy-start | bytes 1572868
  20.5 1.8 %copy-start.4 = (s32[1,512]{1,0:T(1,128)S(1)}, s32[1,512]{1,0:T(1,128)}, u32[]{:S(2)}) copy-start(s32[1,512]{1,0:T(1,128)} %refs_1_.1) | copy-start | bytes 6148
  20.5 1.8 %copy-start.5 = (s32[128]{0:T(128)S(1)}, s32[128]{0:T(128)}, u32[]{:S(2)}) copy-start(s32[128]{0:T(128)} %param.9) | copy-start | bytes 1540
  22.3 12.0 %copy-start.1 = (bf16[384,4096]{1,0:T(8,128)(2,1)S(1)}, bf16[384,4096]{1,0:T(8,128)(2,1)}, u32[]{:S(2)}) copy-start(bf16[384,4096]{1,0:T(8,128)(2,1)} %refs_0_.9) | copy-start | bytes 9437188
  31.9 10.0 %collective-permute-start.7 = (bf16[2048,128]{1,0:T(8,128)(2,1)S(1)}, bf16[2048,128]{1,0:T(8,128)(2,1)S(1)}, u32[]{:S(2)}, u32[]{:S(2)}) collective-permute-start(bf16[2048,128]{1,0:T(8,128)(2,1)S(1)} %get-tuple-element.29), channel_id=1, source_target_pairs={{0,8},{4,12},{8,0},{12,4},{16,24},{20,28},{24,16},{28,20},{1,9},{5... | collective-permute-start | bytes 1572872 | tf_op jit(solution)/shard_map/ppermute | solution.py:34
  33.6 9.4 %collective-permute-start.6 = (bf16[2048,128]{1,0:T(8,128)(2,1)S(1)}, bf16[2048,128]{1,0:T(8,128)(2,1)S(1)}, u32[]{:S(2)}, u32[]{:S(2)}) collective-permute-start(bf16[2048,128]{1,0:T(8,128)(2,1)S(1)} %get-tuple-element.28), channel_id=1, source_target_pairs={{0,16},{4,20},{8,24},{12,28},{16,0},{20,4},{24,8},{28,12},{1,17},{... | collective-permute-start | bytes 1572872 | tf_op jit(solution)/shard_map/ppermute | solution.py:34
  44.1 5.9 %collective-permute-start.10 = (bf16[768,128]{1,0:T(8,128)(2,1)S(1)}, bf16[768,128]{1,0:T(8,128)(2,1)S(1)}, u32[]{:S(2)}, u32[]{:S(2)}) collective-permute-start(bf16[768,128]{1,0:T(8,128)(2,1)S(1)} %get-tuple-element.35), channel_id=1, source_target_pairs={{0,1},{1,0},{2,3},{3,2},{4,5},{5,4},{6,7},{7,6},{8,9},{9,8},{10,11... | collective-permute-start | bytes 589832 | tf_op jit(solution)/shard_map/ppermute | solution.py:34
  45.5 11.4 %collective-permute-start.8 = (bf16[768,128]{1,0:T(8,128)(2,1)S(1)}, bf16[768,128]{1,0:T(8,128)(2,1)S(1)}, u32[]{:S(2)}, u32[]{:S(2)}) collective-permute-start(bf16[768,128]{1,0:T(8,128)(2,1)S(1)} %get-tuple-element.33), channel_id=1, source_target_pairs={{0,3},{1,2},{2,1},{3,0},{4,7},{5,6},{6,5},{7,4},{8,11},{9,10},{10,... | collective-permute-start | bytes 589832 | tf_op jit(solution)/shard_map/ppermute | solution.py:34
  47.6 15.6 %collective-permute-start.9 = (bf16[768,128]{1,0:T(8,128)(2,1)S(1)}, bf16[768,128]{1,0:T(8,128)(2,1)S(1)}, u32[]{:S(2)}, u32[]{:S(2)}) collective-permute-start(bf16[768,128]{1,0:T(8,128)(2,1)S(1)} %get-tuple-element.34), channel_id=1, source_target_pairs={{0,2},{1,3},{2,0},{3,1},{4,6},{5,7},{6,4},{7,5},{8,10},{9,11},{10,... | collective-permute-start | bytes 589832 | tf_op jit(solution)/shard_map/ppermute | solution.py:34
  63.4 1.5 %collective-permute-start.11 = (f32[384,128]{1,0:T(8,128)S(1)}, f32[384,128]{1,0:T(8,128)S(1)}, u32[]{:S(2)}, u32[]{:S(2)}) collective-permute-start(f32[384,128]{1,0:T(8,128)S(1)} %get-tuple-element.37), channel_id=1, source_target_pairs={{0,4},{4,0},{8,12},{12,8},{16,20},{20,16},{24,28},{28,24},{1,5},{5... | collective-permute-start | bytes 589832 | tf_op jit(solution)/shard_map/ppermute | solution.py:34
  65.2 3.9 %collective-permute-start.12 = (bf16[128,384]{1,0:T(8,128)(2,1)S(1)}, bf16[128,384]{1,0:T(8,128)(2,1)S(1)}, u32[]{:S(2)}, u32[]{:S(2)}) collective-permute-start(bf16[128,384]{1,0:T(8,128)(2,1)S(1)} %get-tuple-element.43), channel_id=1, source_target_pairs={{0,4},{4,0},{8,12},{12,8},{16,20},{20,16},{24,28},{28,24},{1,5},{5... | collective-permute-start | bytes 294920 | tf_op jit(solution)/shard_map/ppermute | solution.py:34
  65.4 6.4 %collective-permute-start.13 = (bf16[128,384]{1,0:T(8,128)(2,1)S(1)}, bf16[128,384]{1,0:T(8,128)(2,1)S(1)}, u32[]{:S(2)}, u32[]{:S(2)}) collective-permute-start(bf16[128,384]{1,0:T(8,128)(2,1)S(1)} %get-tuple-element.44), channel_id=1, source_target_pairs={{4,8},{12,16},{20,24},{8,4},{16,12},{24,20},{5,9},{13,17},{21,25},... | collective-permute-start | bytes 294920 | tf_op jit(solution)/shard_map/ppermute | solution.py:214

commit v10 on v7

--- a/solution.py
+++ b/solution.py
@@ -95,13 +95,20 @@
         far_block[side * rows : (side + 1) * rows] = result[:, width:]
 
 
-def late_kernel(mine, theirs, top, bottom, own, near, far, kept, *refs):
+def lower_kernel(mine, theirs, bottom, block):
+    start, rows = mine.shape[1] - bottom.shape[0], mine.shape[0]
+    for side, states in enumerate((mine, theirs)):
+        result = jnp.dot(states[:, start:], bottom[...], preferred_element_type=F32)
+        block[side * rows : (side + 1) * rows] = result
+
+
+def late_kernel(mine, theirs, top, lower, own, near, far, kept, *refs):
     sent, last = refs[:-1], refs[-1]
     cut = top.shape[0]
     rows = mine.shape[0]
     for side, states in enumerate((mine, theirs)):
-        result = jnp.dot(states[:, :cut], top[...], preferred_element_type=F32)
-        last[side * rows : (side + 1) * rows] = result + jnp.dot(states[:, cut:], bottom[...], preferred_element_type=F32)
+        span = slice(side * rows, (side + 1) * rows)
+        last[span] = lower[span] + jnp.dot(states[:, :cut], top[...], preferred_element_type=F32)
     where = block_of_band()
 
     def store(out, slot, block):
@@ -115,13 +122,31 @@
 
 
 def sum_kernel(kept, *refs):
-    parts, (mine, theirs) = refs[:-2], refs[-2:]
+    parts, (own_message, other_message, mine, swap, local, *sent) = refs[:-9], refs[-9:]
     value = kept[...]
     for part in parts:
         value = value + part[...].astype(F32)
-    rows = mine.shape[0]
+    rows, shared = mine.shape[0], local.shape[0]
+    first = core() == 0
+    results = []
+    for message, block in ((own_message, value[:rows]), (other_message, value[rows:])):
+        high, low = split(block)
+        matrix = message[:, :rows]
+        result = dot(matrix, high) + dot(matrix, low)
+        results += [result[:shared], result[shared:]]
+    own_back, own_faces, other_back, other_faces = results
     mine[...] = value[:rows]
-    theirs[...] = value[rows:]
+    swap[:rows] = value[rows:]
+    swap[rows:] = jnp.where(first, own_back, own_faces)
+    local[...] = jnp.where(first, other_faces, other_back)
+    other_back_sent, own_back_sent, own_faces_sent, other_faces_sent = sent
+    other_back_sent[...] = other_back.astype(BF16)
+    own_back_sent[:, : own_back.shape[1]] = own_back.astype(BF16)
+    own_back_sent[:, own_back.shape[1] : own_back.shape[1] + shared] = own_message[:shared, rows:]
+    rest = own_back_sent.shape[1] - own_back.shape[1] - shared
+    own_back_sent[:, -rest:] = jnp.zeros((shared, rest), BF16)
+    own_faces_sent[...] = own_faces.astype(BF16)
+    other_faces_sent[...] = other_faces.astype(BF16)
 
 
 def rotate_square(wavefunctions, rotation, operator):
@@ -132,20 +157,37 @@
     received = [exchanged(rotation, "domain", NEAR, 0), exchanged(rotation, "domain", FAR, 0)]
     theirs = exchanged(wavefunctions, "domain", CORE)
     block = [shape(2 * rows, width)]
-    own = call(own_kernel, block, (wavefunctions, theirs, rotation))[0]
-    operator = operator(own)
-    later, _ = lax.optimization_barrier((rotation, operator[0]))
+    assembled, message, matrix = operator(theirs)
+    other_message = exchanged(message, "domain", CORE)
+    own = call(own_kernel, block, (wavefunctions, theirs, rotation), after=(message,))[0]
+    later, _ = lax.optimization_barrier((rotation, own))
     received += [exchanged(later, "domain", NEAR, CORE), exchanged(later, "domain", FAR, CORE)]
     outs = [shape(count, width, dtype=BF16) for count in (cut, states - cut)]
-    top, bottom = call(pieces_kernel, outs, received, scratch=[pltpu.SemaphoreType.DMA((2,))])
+    top, bottom = call(pieces_kernel, outs, received, after=(other_message,), scratch=[pltpu.SemaphoreType.DMA((2,))])
     top, bottom = exchanged(top, "domain", FAR), exchanged(bottom, "domain", NEAR)
     early = call(early_kernel, block * 2, (wavefunctions, theirs, *received))
     outs = block + [shape(2 * rows, width, dtype=BF16)] * (bands - 1)
     scratch = [pltpu.VMEM((2 * rows, width), F32)]
-    kept, *sent = call(late_kernel, outs, (wavefunctions, theirs, top, bottom, own, *early), scratch=scratch)
+    lower = call(lower_kernel, block, (wavefunctions, theirs, bottom))[0]
+    kept, *sent = call(late_kernel, outs, (wavefunctions, theirs, top, lower, own, *early), scratch=scratch)
     parts = [exchanged(sent[mask - 1], "band", mask) for mask in reversed(range(1, bands))]
-    mine, others = call(sum_kernel, [shape(rows, width)] * 2, (kept, *parts))
-    return mine, exchanged(others, "domain", CORE), operator
+
+    shared = message.shape[0] // 2
+    small = shape(shared, width, dtype=BF16)
+    outs = [shape(rows, width), shape(rows + shared, width), shape(shared, width)]
+    outs += [small, shape(shared, 9 * width, dtype=BF16), small, small]
+    mine, swap, local, *sent = call(sum_kernel, outs, (kept, *parts, message, other_message))
+    chips = [2 * chip for chip in range(chips - 1)]
+    back_even = lax.ppermute(sent[0], "domain", [(place, place + 2) for place in chips])
+    back_odd = lax.ppermute(sent[1], "domain", [(place + 1, place + 2) for place in chips])
+    faces_even = lax.ppermute(sent[2], "domain", [(place + 2, place + 1) for place in chips])
+    faces_odd = lax.ppermute(sent[3], "domain", [(place + 3, place + 1) for place in chips])
+    swap = exchanged(swap, "domain", CORE)
+    outs = [shape(rows, width), shape(shared, width), shape(shared, 2 * width, dtype=BF16), shape(shared, 2 * width)]
+    outs += [shape(shared, shared, dtype=BF16)]
+    operands = (mine, assembled, message, other_message, local, back_even, back_odd, faces_even, faces_odd)
+    partial = call(inner_kernel, outs, operands)
+    return call(final_kernel, [shape(rows, 2 * width)], (*partial, swap, assembled, message, matrix))[0]
 
 
 def rotate_any(wavefunctions, rotation):
@@ -153,59 +195,47 @@
     return lax.psum_scatter(dot(wavefunctions, columns), "band", scatter_dimension=1, tiled=True)
 
 
-def faces_kernel(mine, other, assembled, pick, total, inward, outward):
+def own_terms(block, assembled, message, corner):
+    own = block.shape[0]
+    high, low = split(block)
+    inner, pick = assembled[:own, :own], message[message.shape[0] // 2 :, :own]
+    faces = dot(corner, dot(pick, high).astype(BF16)) + dot(corner, dot(pick, low).astype(BF16))
+    return dot(inner, high) + dot(inner, low), faces
+
+
+def inner_kernel(
+    mine, assembled, message, other_message, local, back_even, back_odd, faces_even, faces_odd, inner, terms, faces, back, corner
+):
     own, width = mine.shape
-    columns = 2 * width
     first = core() == 0
-    for side, half in enumerate((jnp.where(first, mine[...], other[...]), jnp.where(first, other[...], mine[...]))):
-        total[:, side * width : (side + 1) * width] = half
-    high, low = split(total[...])
-    faces = dot(pick[...], high).astype(BF16)
-    onward = (dot(assembled[own:, :own], high) + dot(assembled[own:, :own], low)).astype(BF16)
-    corner = assembled[own:, own:]
-
-    def store(forward, backward):
-        forward[:, :columns] = onward
-        forward[:, columns:] = corner
-        backward[:, :columns] = faces
-        backward[:, columns:] = corner
-
-    pl.when(first)(lambda: store(inward, outward))
-    pl.when(jnp.logical_not(first))(lambda: store(outward, inward))
-
-
-def inner_kernel(total, assembled, pick, out, face_high, face_low):
-    own = total.shape[0]
-    high, low = split(total[...])
-    inner = assembled[:own, :own]
-    out[...] = dot(inner, high) + dot(inner, low)
-    face_high[...] = dot(pick[...], high).astype(BF16)
-    face_low[...] = dot(pick[...], low).astype(BF16)
-
-
-def final_kernel(inner, face_high, face_low, assembled, spread, inward, outward, out):
-    own, columns = inner.shape
+    block = jnp.where(first, back_odd[:, width : width + corner.shape[1]], other_message[: corner.shape[0], own:])
+    corner[...] = block
+    inner[...], terms[...] = own_terms(mine[...], assembled, message, block)
+    both = jnp.concatenate([local[...], local[...]], 1)
+    faces[...] = jnp.where(first, both.astype(BF16), jnp.concatenate([faces_even[...], faces_odd[...]], 1))
+    back[...] = jnp.where(first, jnp.concatenate([back_even[...], back_odd[:, :width]], 1).astype(F32), both)
+
+
+def final_kernel(inner, terms, faces, back, corner, swap, assembled, message, matrix, out):
+    own, width = inner.shape
+    other, extra = swap[:own], swap[own:]
+    other_inner, other_terms = own_terms(other, assembled, message, corner[...])
     first = core() == 0
-    incoming = jnp.where(first, inward[:, :columns], outward[:, :columns])
-    back = jnp.where(first, outward[...], inward[...])
-    corner = back[:, columns:]
-    value = back[:, :columns].astype(F32) + dot(corner, face_high[...]) + dot(corner, face_low[...])
-    high, low = split(value)
-    out[...] = inner[...] + dot(assembled[:own, own:], incoming) + dot(spread[...], high) + dot(spread[...], low)
-
-
-def finish_square(mine, other, operator):
-    assembled, pick, spread = operator
-    rows, width = mine.shape
-    shared, columns = pick.shape[0], 2 * width
-    outs = [shape(rows, columns)] + [shape(shared, columns + shared, dtype=BF16)] * 2
-    total, inward, outward = call(faces_kernel, outs, (mine, other, assembled, pick))
-    across = [(place, place + 1) for place in range(CORE, lax.axis_size("domain") - 1, 2)]
-    outward = lax.ppermute(outward, "domain", across + [(target, source) for source, target in across])
-    inward = exchanged(inward, "domain", CORE)
-    outs = [shape(rows, columns)] + [shape(shared, columns, dtype=BF16)] * 2
-    inner, *face = call(inner_kernel, outs, (total, assembled, pick))
-    return call(final_kernel, outs[:1], (inner, *face, assembled, spread, inward, outward))[0]
+
+    def half(side, block, more, incoming, sums):
+        high, low = split(sums + more)
+        value = block + dot(matrix[...], jnp.concatenate([incoming, high, low], 0))
+        out[:, side * width : (side + 1) * width] = value
+
+    @pl.when(first)
+    def _():
+        half(0, inner[...], terms[...], faces[:, :width], back[:, :width])
+        half(1, other_inner, other_terms, extra.astype(BF16), back[:, width:])
+
+    @pl.when(jnp.logical_not(first))
+    def _():
+        half(0, other_inner, other_terms, faces[:, :width], extra)
+        half(1, inner[...], terms[...], faces[:, width:], back[:, width:])
 
 
 def finish_any(rotated, cell_matrices, cell_nodes, face_map):
@@ -234,29 +264,35 @@
     return assembled, pick, returned
 
 
-def assemble_kernel(matrix, nodes, faces, assembled, pick, spread):
-    extent = assembled.shape[0]
+def assemble_kernel(cell, nodes, faces, assembled, message, matrix):
+    extent, shared = assembled.shape[0], faces.shape[1]
+    own = extent - shared
     places = jnp.where(lax.broadcasted_iota(jnp.int32, (extent, extent), 0) == nodes[...], 1.0, 0.0).astype(BF16)
-    rows = dot(places, matrix[0]).astype(BF16)
-    whole = lax.dot_general(rows, places, (((1,), (1,)), ((), ())), preferred_element_type=F32)
-    assembled[...] = whole.astype(BF16)
-    chosen = jnp.where(lax.broadcasted_iota(jnp.int32, spread.shape, 0) == faces[...], 1.0, 0.0)
-    spread[...] = chosen.astype(BF16)
-    pick[...] = chosen.T.astype(BF16)
+    rows = dot(places, cell[0]).astype(BF16)
+    whole = lax.dot_general(rows, places, (((1,), (1,)), ((), ())), preferred_element_type=F32).astype(BF16)
+    chosen = jnp.where(lax.broadcasted_iota(jnp.int32, (own, shared), 0) == faces[...], 1.0, 0.0)
+    assembled[...] = whole
+    message[:shared] = whole[own:]
+    message[shared:, :own] = chosen.T.astype(BF16)
+    message[shared:, own:] = jnp.zeros((shared, shared), BF16)
+    matrix[:, :shared] = whole[:own, own:]
+    matrix[:, shared : 2 * shared] = chosen.astype(BF16)
+    matrix[:, 2 * shared :] = chosen.astype(BF16)
 
 
 def assemble(cell_matrices, cell_nodes, face_map, own, after):
     shared = face_map.shape[0]
-    outs = [(own + shared, own + shared), (shared, own), (own, shared)]
+    extent = own + shared
+    outs = [shape(*dims, dtype=BF16) for dims in ((extent, extent), (2 * shared, extent), (own, 3 * shared))]
     operands = (cell_matrices, cell_nodes, face_map.reshape(1, shared))
-    return call(assemble_kernel, [shape(*dims, dtype=BF16) for dims in outs], operands, after=(after,))
+    return call(assemble_kernel, outs, operands, after=(after,))
 
 
 def local(wavefunctions, rotation, cell_matrices, cell_nodes, face_map):
     chips = lax.axis_size("domain") // 2
     if chips == FAR and chips == lax.axis_size("band") and cell_nodes.shape[0] == 1:
         operator = functools.partial(assemble, cell_matrices, cell_nodes, face_map, wavefunctions.shape[0])
-        return finish_square(*rotate_square(wavefunctions, rotation, operator))
+        return rotate_square(wavefunctions, rotation, operator)
     return finish_any(rotate_any(wavefunctions, rotation), cell_matrices, cell_nodes, face_map)
 
 

time: 71 us -> 75 us (1.056)
  waiting for transfers between devices: 40.7 us -> 42.6 us
  starting transfers between devices: 18.1 us -> 19 us
    ppermute x1 -> x4, starting transfers between devices: 3.35 us -> 4.56 us  [the longest x1 1.31 us: rotate_square(): lax.ppermute(sent[1], 'domain', [(place + 1, place + 2) for place in chips])]
    ppermute x12, waiting for transfers between devices: 37.8 us -> 38.8 us  [exchanged(): lax.ppermute(value, axis, [(source, source ^ mask) for source in sources...]
    ppermute x1 -> x4, waiting for transfers between devices: 2.94 us -> 3.81 us  [the longest x1 3.8 us: rotate_square(): lax.ppermute(sent[2], 'domain', [(place + 2, place + 1) for place in chips])]
    unnamed x14 -> x10, local copies, waits for them, and re-layouts: 3.13 us -> 3.6 us
  transfers between devices with their start and end apart: 13 -> 16, of which waited for: 9 -> 9; matrix products, arithmetic and copies ran while one was open for 0% -> 0% of each run, Pallas kernels for 7% -> 8%
where the time goes in v10:
time: 75 us; the launch traced here: 74.7 us
  waiting for transfers between devices  42.6 us (57%)
  starting transfers between devices  19 us (25%)
  Pallas kernels  9.28 us (12%)
  local copies, waits for them, and re-layouts  3.6 us (5%)
    ppermute x12, waiting for transfers between devices, exchanged(): lax.ppermute(value, axis, [(source, source ^ mask) for source in sources...  38.8 us
    ppermute x12, starting transfers between devices, exchanged(): lax.ppermute(value, axis, [(source, source ^ mask) for source in sources...  14.5 us
    pallas_call x9, Pallas kernels, call(): pl.pallas_call(body, out_shape=outs, in_specs=[pl.BlockSpec(memory_space=...  9.28 us
    ppermute x1, waiting for transfers between devices, rotate_square(): lax.ppermute(sent[2], 'domain', [(place + 2, place + 1) for place in chips])  3.8 us
    unnamed x10, local copies, waits for them, and re-layouts  3.6 us
  transfers between devices with their start and end apart: 16, of which 9 were waited for; matrix products, arithmetic and copies ran while one was open for 0% of the time, Pallas kernels for 8%

profile of v10, /device:TPU:1, one launch (start us, length us, event | category | flops | bytes accessed | tf_op | source)
XLA Modules:
  0.0 74.7 jit_solution(1506845267154129820)
XLA Ops:
  0.0 0.0 copy-start
  0.0 0.1 collective-permute-start
  0.1 0.8 %collective-permute-start.1 = (bf16[4096,128]{1,0:T(8,128)(2,1)}, bf16[4096,128]{1,0:T(8,128)(2,1)S(1)}, u32[]{:S(2)}, u32[]{:S(2)}) collective-permute-start(bf16[4096,128]{1,0:T(8,128)(2,1)} %refs_2_.1), channel_id=1, source_target_pairs={{0,8},{8,0},{16,24},{24,16},{1,9},{9,1},{17,25},{25,17},{2,10},{10... | collective-permute-start | bytes 3145736 | tf_op jit(solution)/shard_map/ppermute | solution.py:34
  0.9 0.9 %collective-permute-start.2 = (bf16[4096,128]{1,0:T(8,128)(2,1)}, bf16[4096,128]{1,0:T(8,128)(2,1)S(1)}, u32[]{:S(2)}, u32[]{:S(2)}) collective-permute-start(bf16[4096,128]{1,0:T(8,128)(2,1)} %refs_2_.1), channel_id=1, source_target_pairs={{0,16},{8,24},{16,0},{24,8},{1,17},{9,25},{17,1},{25,9},{2,18},{10... | collective-permute-start | bytes 3145736 | tf_op jit(solution)/shard_map/ppermute | solution.py:34
  1.8 4.1 %collective-permute-done.refs_3_.refs_1_ = bf16[384,4096]{1,0:T(8,128)(2,1)S(1)} collective-permute-done((bf16[384,4096]{1,0:T(8,128)(2,1)}, bf16[384,4096]{1,0:T(8,128)(2,1)S(1)}, u32[]{:S(2)}, u32[]{:S(2)}) %collective-permute-start) | collective-permute-done | bytes 3145760 | tf_op jit(solution)/shard_map/ppermute | solution.py:34
  5.9 0.0 copy-start.2
  5.9 1.0 %copy-done.2 = bf16[1,512,512]{2,1,0:T(8,128)(2,1)S(1)} copy-done((bf16[1,512,512]{2,1,0:T(8,128)(2,1)S(1)}, bf16[1,512,512]{2,1,0:T(8,128)(2,1)}, u32[]{:S(2)}) %copy-start.2) | copy-done | bytes 524312
  6.9 0.0 copy-start.3
  6.9 0.7 copy-done.3
  7.6 0.0 copy-start.4
  7.6 0.7 copy-done.4
  8.3 0.7 shard_map.55
  9.0 0.0 copy-done
  9.0 0.0 copy-start.1
  9.0 1.2 %copy-done.1 = bf16[4096,128]{1,0:T(8,128)(2,1)S(1)} copy-done((bf16[4096,128]{1,0:T(8,128)(2,1)S(1)}, bf16[4096,128]{1,0:T(8,128)(2,1)}, u32[]{:S(2)}) %copy-start.1) | copy-done | bytes 1048600
  10.2 1.8 %shard_map.56.refs_4_ = f32[768,128]{1,0:T(8,128)S(1)} custom-call(bf16[384,4096]{1,0:T(8,128)(2,1)S(1)} %copy-done, bf16[384,4096]{1,0:T(8,128)(2,1)S(1)} %collective-permute-done.refs_3_.refs_1_, bf16[4096,128]{1,0:T(8,128)(2,1)S(1)} %copy-done.1, bf16[256,512]{1,0:T(8,128)(2,1)S(1)} %get-tuple-element.29.refs_3_.refs_4_.refs_2_.refs_7_), custom_call_target="tpu_custom_call" | custom-call | bytes 1024 | tf_op jit(solution)/shard_map/pallas_call | solution.py:43
  12.0 4.3 %collective-permute-start.3 = (bf16[4096,128]{1,0:T(8,128)(2,1)S(1)}, bf16[4096,128]{1,0:T(8,128)(2,1)S(1)}, u32[]{:S(2)}, u32[]{:S(2)}) collective-permute-start(bf16[4096,128]{1,0:T(8,128)(2,1)S(1)} %copy-done.1), channel_id=1, source_target_pairs={{4,12},{12,4},{20,28},{28,20},{5,13},{13,5},{21,29},{29,21},{6,14}... | collective-permute-start | bytes 3145736 | tf_op jit(solution)/shard_map/ppermute | solution.py:34
  16.2 3.1 %collective-permute-start.4 = (bf16[4096,128]{1,0:T(8,128)(2,1)S(1)}, bf16[4096,128]{1,0:T(8,128)(2,1)S(1)}, u32[]{:S(2)}, u32[]{:S(2)}) collective-permute-start(bf16[4096,128]{1,0:T(8,128)(2,1)S(1)} %copy-done.1), channel_id=1, source_target_pairs={{4,20},{12,28},{20,4},{28,12},{5,21},{13,29},{21,5},{29,13},{6,22}... | collective-permute-start | bytes 3145736 | tf_op jit(solution)/shard_map/ppermute | solution.py:34
  19.4 0.1 collective-permute-start.5
  19.5 0.0 collective-permute-done.1.refs_0_.refs_2_
  19.5 0.0 collective-permute-done.2.refs_1_.refs_3_
  19.5 1.5 %collective-permute-done.5.refs_4_.refs_5_.refs_3_ = bf16[256,512]{1,0:T(8,128)(2,1)S(1)} collective-permute-done((bf16[256,512]{1,0:T(8,128)(2,1)S(1)}, bf16[256,512]{1,0:T(8,128)(2,1)S(1)}, u32[]{:S(2)}, u32[]{:S(2)}) %collective-permute-start.5) | collective-permute-done | bytes 262176 | tf_op jit(solution)/shard_map/ppermute | solution.py:34
  21.0 9.9 %collective-permute-done.3.refs_2_.refs_4_ = bf16[4096,128]{1,0:T(8,128)(2,1)S(1)} collective-permute-done((bf16[4096,128]{1,0:T(8,128)(2,1)S(1)}, bf16[4096,128]{1,0:T(8,128)(2,1)S(1)}, u32[]{:S(2)}, u32[]{:S(2)}) %collective-permute-start.3) | collective-permute-done | bytes 1048608 | tf_op jit(solution)/shard_map/ppermute | solution.py:34
  30.9 8.4 %collective-permute-done.4.refs_3_.refs_5_ = bf16[4096,128]{1,0:T(8,128)(2,1)S(1)} collective-permute-done((bf16[4096,128]{1,0:T(8,128)(2,1)S(1)}, bf16[4096,128]{1,0:T(8,128)(2,1)S(1)}, u32[]{:S(2)}, u32[]{:S(2)}) %collective-permute-start.4) | collective-permute-done | bytes 1048608 | tf_op jit(solution)/shard_map/ppermute | solution.py:34
  39.2 0.4 shard_map.57
  39.6 1.3 %collective-permute-start.6 = (bf16[2304,128]{1,0:T(8,128)(2,1)S(1)}, bf16[2304,128]{1,0:T(8,128)(2,1)S(1)}, u32[]{:S(2)}, u32[]{:S(2)}) collective-permute-start(bf16[2304,128]{1,0:T(8,128)(2,1)S(1)} %get-tuple-element.31), channel_id=1, source_target_pairs={{0,16},{4,20},{8,24},{12,28},{16,0},{20,4},{24,8},{28,12},{1,17},{... | collective-permute-start | bytes 1769480 | tf_op jit(solution)/shard_map/ppermute | solution.py:34
  41.0 0.3 collective-permute-start.7
  41.2 1.8 %shard_map.59 = (f32[768,128]{1,0:T(8,128)S(1)}, f32[768,128]{1,0:T(8,128)S(1)}) custom-call(bf16[384,4096]{1,0:T(8,128)(2,1)S(1)} %copy-done, bf16[384,4096]{1,0:T(8,128)(2,1)S(1)} %collective-permute-done.refs_3_.refs_1_, bf16[4096,128]{1,0:T(8,128)(2,1)S(1)} %collective-permute-done.1.refs_0_.refs_2_, ...), custom_call_target="tpu_custom_call" | custom-call | bytes 1024 | tf_op jit(solution)/shard_map/pallas_call | solution.py:43
  43.0 5.6 %collective-permute-done.7.refs_2_ = bf16[1792,128]{1,0:T(8,128)(2,1)S(1)} collective-permute-done((bf16[1792,128]{1,0:T(8,128)(2,1)S(1)}, bf16[1792,128]{1,0:T(8,128)(2,1)S(1)}, u32[]{:S(2)}, u32[]{:S(2)}) %collective-permute-start.7) | collective-permute-done | bytes 458784 | tf_op jit(solution)/shard_map/ppermute | solution.py:34
  48.6 0.9 %shard_map.58.refs_3_ = f32[768,128]{1,0:T(8,128)S(1)} custom-call(bf16[384,4096]{1,0:T(8,128)(2,1)S(1)} %copy-done, bf16[384,4096]{1,0:T(8,128)(2,1)S(1)} %collective-permute-done.refs_3_.refs_1_, bf16[1792,128]{1,0:T(8,128)(2,1)S(1)} %collective-permute-done.7.refs_2_), custom_call_target="tpu_custom_call" | custom-call | bytes 1024 | tf_op jit(solution)/shard_map/pallas_call | solution.py:43
  49.4 0.0 collective-permute-done.6.refs_2_
  49.5 1.2 %shard_map.60 = (f32[768,128]{1,0:T(8,128)S(1)}, bf16[768,128]{1,0:T(8,128)(2,1)S(1)}, bf16[768,128]{1,0:T(8,128)(2,1)S(1)}, bf16[768,128]{1,0:T(8,128)(2,1)S(1)}) custom-call(bf16[384,4096]{1,0:T(8,128)(2,1)S(1)} %copy-done, bf16[384,4096]{1,0:T(8,128)(2,1)S(1)} %collective-permute-done.refs_3_.refs_1_, ...), custom_call_target="tpu_custom_call" | custom-call | bytes 1024 | tf_op jit(solution)/shard_map/pallas_call | solution.py:43
  50.7 1.4 %collective-permute-start.10 = (bf16[768,128]{1,0:T(8,128)(2,1)S(1)}, bf16[768,128]{1,0:T(8,128)(2,1)S(1)}, u32[]{:S(2)}, u32[]{:S(2)}) collective-permute-start(bf16[768,128]{1,0:T(8,128)(2,1)S(1)} %get-tuple-element.38), channel_id=1, source_target_pairs={{0,1},{1,0},{2,3},{3,2},{4,5},{5,4},{6,7},{7,6},{8,9},{9,8},{10,11... | collective-permute-start | bytes 589832 | tf_op jit(solution)/shard_map/ppermute | solution.py:34
  52.1 2.2 %collective-permute-start.8 = (bf16[768,128]{1,0:T(8,128)(2,1)S(1)}, bf16[768,128]{1,0:T(8,128)(2,1)S(1)}, u32[]{:S(2)}, u32[]{:S(2)}) collective-permute-start(bf16[768,128]{1,0:T(8,128)(2,1)S(1)} %get-tuple-element.36), channel_id=1, source_target_pairs={{0,3},{1,2},{2,1},{3,0},{4,7},{5,6},{6,5},{7,4},{8,11},{9,10},{10,... | collective-permute-start | bytes 589832 | tf_op jit(solution)/shard_map/ppermute | solution.py:34
  54.3 0.1 collective-permute-start.9
  54.3 2.2 %collective-permute-done.10.refs_3_ = bf16[768,128]{1,0:T(8,128)(2,1)S(1)} collective-permute-done((bf16[768,128]{1,0:T(8,128)(2,1)S(1)}, bf16[768,128]{1,0:T(8,128)(2,1)S(1)}, u32[]{:S(2)}, u32[]{:S(2)}) %collective-permute-start.10) | collective-permute-done | bytes 196640 | tf_op jit(solution)/shard_map/ppermute | solution.py:34
  56.5 3.0 %collective-permute-done.8.refs_1_ = bf16[768,128]{1,0:T(8,128)(2,1)S(1)} collective-permute-done((bf16[768,128]{1,0:T(8,128)(2,1)S(1)}, bf16[768,128]{1,0:T(8,128)(2,1)S(1)}, u32[]{:S(2)}, u32[]{:S(2)}) %collective-permute-start.8) | collective-permute-done | bytes 196640 | tf_op jit(solution)/shard_map/ppermute | solution.py:34
  59.5 4.2 %collective-permute-done.9.refs_2_ = bf16[768,128]{1,0:T(8,128)(2,1)S(1)} collective-permute-done((bf16[768,128]{1,0:T(8,128)(2,1)S(1)}, bf16[768,128]{1,0:T(8,128)(2,1)S(1)}, u32[]{:S(2)}, u32[]{:S(2)}) %collective-permute-start.9) | collective-permute-done | bytes 196640 | tf_op jit(solution)/shard_map/ppermute | solution.py:34
  63.7 0.4 shard_map.61
  64.1 1.3 %collective-permute-start.12 = (bf16[128,1152]{1,0:T(8,128)(2,1)S(1)}, bf16[128,1152]{1,0:T(8,128)(2,1)S(1)}, u32[]{:S(2)}, u32[]{:S(2)}) collective-permute-start(bf16[128,1152]{1,0:T(8,128)(2,1)S(1)} %get-tuple-element.43), channel_id=1, source_target_pairs={{4,8},{12,16},{20,24},{5,9},{13,17},{21,25},{6,10},{14,18},{22,26}... | collective-permute-start | bytes 884744 | tf_op jit(solution)/shard_map/ppermute | solution.py:182
  65.4 0.1 collective-permute-start.15
  65.5 0.7 collective-permute-start.11
  66.2 1.3 %collective-permute-start.13 = (bf16[128,128]{1,0:T(8,128)(2,1)S(1)}, bf16[128,128]{1,0:T(8,128)(2,1)S(1)}, u32[]{:S(2)}, u32[]{:S(2)}) collective-permute-start(bf16[128,128]{1,0:T(8,128)(2,1)S(1)} %get-tuple-element.44), channel_id=1, source_target_pairs={{8,4},{16,12},{24,20},{9,5},{17,13},{25,21},{10,6},{18,14},{26,22}... | collective-permute-start | bytes 98312 | tf_op jit(solution)/shard_map/ppermute | solution.py:183
  67.5 1.3 %collective-permute-start.14 = (bf16[128,128]{1,0:T(8,128)(2,1)S(1)}, bf16[128,128]{1,0:T(8,128)(2,1)S(1)}, u32[]{:S(2)}, u32[]{:S(2)}) collective-permute-start(bf16[128,128]{1,0:T(8,128)(2,1)S(1)} %get-tuple-element.45), channel_id=1, source_target_pairs={{12,4},{20,12},{28,20},{13,5},{21,13},{29,21},{14,6},{22,14},{30,2... | collective-permute-start | bytes 98312 | tf_op jit(solution)/shard_map/ppermute | solution.py:184
  68.8 0.0 collective-permute-done.11.refs_5_
  68.8 3.8 %collective-permute-done.13.refs_7_ = bf16[128,128]{1,0:T(8,128)(2,1)S(1)} collective-permute-done((bf16[128,128]{1,0:T(8,128)(2,1)S(1)}, bf16[128,128]{1,0:T(8,128)(2,1)S(1)}, u32[]{:S(2)}, u32[]{:S(2)}) %collective-permute-start.13) | collective-permute-done | bytes 32800 | tf_op jit(solution)/shard_map/ppermute | solution.py:183
  72.6 0.0 collective-permute-done.14.refs_8_
  72.6 0.0 collective-permute-done.12.refs_6_
  72.6 0.5 shard_map.62
  73.1 0.0 collective-permute-done.15.refs_5_
  73.1 1.6 %shard_map.63 = f32[384,256]{1,0:T(8,128)} custom-call(f32[384,128]{1,0:T(8,128)S(1)} %get-tuple-element.46.refs_0_, f32[128,128]{1,0:T(8,128)S(1)} %get-tuple-element.47.refs_1_, bf16[128,256]{1,0:T(8,128)(2,1)S(1)} %get-tuple-element.48.refs_2_, f32[128,256]{1,0:T(8,128)S(1)} %get-tuple-element.49.refs_3_, bf16[128,128]{1,0:T(8,128)(2,1)S(1)} %get-tuple-element.50.refs_4_, ...), custom_call_target="tpu_custom_call" | custom-call | bytes 1024 | tf_op jit(solution)/shard_map/pallas_call | solution.py:43
Async XLA Ops:
  0.0 9.0 %copy-start = (bf16[384,4096]{1,0:T(8,128)(2,1)S(1)}, bf16[384,4096]{1,0:T(8,128)(2,1)}, u32[]{:S(2)}) copy-start(bf16[384,4096]{1,0:T(8,128)(2,1)} %refs_0_.9) | copy-start | bytes 9437188
  0.0 5.9 %collective-permute-start = (bf16[384,4096]{1,0:T(8,128)(2,1)}, bf16[384,4096]{1,0:T(8,128)(2,1)S(1)}, u32[]{:S(2)}, u32[]{:S(2)}) collective-permute-start(bf16[384,4096]{1,0:T(8,128)(2,1)} %refs_0_.9), channel_id=1, source_target_pairs={{0,4},{4,0},{8,12},{12,8},{16,20},{20,16},{24,28},{28,24},{1,5},{5... | collective-permute-start | bytes 9437192 | tf_op jit(solution)/shard_map/ppermute | solution.py:34
  0.1 19.4 %collective-permute-start.1 = (bf16[4096,128]{1,0:T(8,128)(2,1)}, bf16[4096,128]{1,0:T(8,128)(2,1)S(1)}, u32[]{:S(2)}, u32[]{:S(2)}) collective-permute-start(bf16[4096,128]{1,0:T(8,128)(2,1)} %refs_2_.1), channel_id=1, source_target_pairs={{0,8},{8,0},{16,24},{24,16},{1,9},{9,1},{17,25},{25,17},{2,10},{10... | collective-permute-start | bytes 3145736 | tf_op jit(solution)/shard_map/ppermute | solution.py:34
  0.9 18.6 %collective-permute-start.2 = (bf16[4096,128]{1,0:T(8,128)(2,1)}, bf16[4096,128]{1,0:T(8,128)(2,1)S(1)}, u32[]{:S(2)}, u32[]{:S(2)}) collective-permute-start(bf16[4096,128]{1,0:T(8,128)(2,1)} %refs_2_.1), channel_id=1, source_target_pairs={{0,16},{8,24},{16,0},{24,8},{1,17},{9,25},{17,1},{25,9},{2,18},{10... | collective-permute-start | bytes 3145736 | tf_op jit(solution)/shard_map/ppermute | solution.py:34
  5.9 1.0 %copy-start.2 = (bf16[1,512,512]{2,1,0:T(8,128)(2,1)S(1)}, bf16[1,512,512]{2,1,0:T(8,128)(2,1)}, u32[]{:S(2)}) copy-start(bf16[1,512,512]{2,1,0:T(8,128)(2,1)} %refs_0_.5) | copy-start | bytes 1572868
  6.9 0.7 copy-start.3
  7.6 0.7 copy-start.4
  9.0 1.2 %copy-start.1 = (bf16[4096,128]{1,0:T(8,128)(2,1)S(1)}, bf16[4096,128]{1,0:T(8,128)(2,1)}, u32[]{:S(2)}) copy-start(bf16[4096,128]{1,0:T(8,128)(2,1)} %refs_2_.1) | copy-start | bytes 3145732
  12.0 18.9 %collective-permute-start.3 = (bf16[4096,128]{1,0:T(8,128)(2,1)S(1)}, bf16[4096,128]{1,0:T(8,128)(2,1)S(1)}, u32[]{:S(2)}, u32[]{:S(2)}) collective-permute-start(bf16[4096,128]{1,0:T(8,128)(2,1)S(1)} %copy-done.1), channel_id=1, source_target_pairs={{4,12},{12,4},{20,28},{28,20},{5,13},{13,5},{21,29},{29,21},{6,14}... | collective-permute-start | bytes 3145736 | tf_op jit(solution)/shard_map/ppermute | solution.py:34
  16.2 23.0 %collective-permute-start.4 = (bf16[4096,128]{1,0:T(8,128)(2,1)S(1)}, bf16[4096,128]{1,0:T(8,128)(2,1)S(1)}, u32[]{:S(2)}, u32[]{:S(2)}) collective-permute-start(bf16[4096,128]{1,0:T(8,128)(2,1)S(1)} %copy-done.1), channel_id=1, source_target_pairs={{4,20},{12,28},{20,4},{28,12},{5,21},{13,29},{21,5},{29,13},{6,22}... | collective-permute-start | bytes 3145736 | tf_op jit(solution)/shard_map/ppermute | solution.py:34
  19.4 1.6 %collective-permute-start.5 = (bf16[256,512]{1,0:T(8,128)(2,1)S(1)}, bf16[256,512]{1,0:T(8,128)(2,1)S(1)}, u32[]{:S(2)}, u32[]{:S(2)}) collective-permute-start(bf16[256,512]{1,0:T(8,128)(2,1)S(1)} %get-tuple-element.29.refs_3_.refs_4_.refs_2_.refs_7_), channel_id=1, source_target_pairs={{0,4},{4,0},{8,12},{12,8},{16,20},{20,16},{24,28},{28,24},{1,5},{5... | collective-permute-start | bytes 786440 | tf_op jit(solution)/shard_map/ppermute | solution.py:34
  39.6 9.8 %collective-permute-start.6 = (bf16[2304,128]{1,0:T(8,128)(2,1)S(1)}, bf16[2304,128]{1,0:T(8,128)(2,1)S(1)}, u32[]{:S(2)}, u32[]{:S(2)}) collective-permute-start(bf16[2304,128]{1,0:T(8,128)(2,1)S(1)} %get-tuple-element.31), channel_id=1, source_target_pairs={{0,16},{4,20},{8,24},{12,28},{16,0},{20,4},{24,8},{28,12},{1,17},{... | collective-permute-start | bytes 1769480 | tf_op jit(solution)/shard_map/ppermute | solution.py:34
  41.0 7.6 %collective-permute-start.7 = (bf16[1792,128]{1,0:T(8,128)(2,1)S(1)}, bf16[1792,128]{1,0:T(8,128)(2,1)S(1)}, u32[]{:S(2)}, u32[]{:S(2)}) collective-permute-start(bf16[1792,128]{1,0:T(8,128)(2,1)S(1)} %get-tuple-element.32), channel_id=1, source_target_pairs={{0,8},{4,12},{8,0},{12,4},{16,24},{20,28},{24,16},{28,20},{1,9},{5... | collective-permute-start | bytes 1376264 | tf_op jit(solution)/shard_map/ppermute | solution.py:34
  50.7 5.8 %collective-permute-start.10 = (bf16[768,128]{1,0:T(8,128)(2,1)S(1)}, bf16[768,128]{1,0:T(8,128)(2,1)S(1)}, u32[]{:S(2)}, u32[]{:S(2)}) collective-permute-start(bf16[768,128]{1,0:T(8,128)(2,1)S(1)} %get-tuple-element.38), channel_id=1, source_target_pairs={{0,1},{1,0},{2,3},{3,2},{4,5},{5,4},{6,7},{7,6},{8,9},{9,8},{10,11... | collective-permute-start | bytes 589832 | tf_op jit(solution)/shard_map/ppermute | solution.py:34
  52.1 7.5 %collective-permute-start.8 = (bf16[768,128]{1,0:T(8,128)(2,1)S(1)}, bf16[768,128]{1,0:T(8,128)(2,1)S(1)}, u32[]{:S(2)}, u32[]{:S(2)}) collective-permute-start(bf16[768,128]{1,0:T(8,128)(2,1)S(1)} %get-tuple-element.36), channel_id=1, source_target_pairs={{0,3},{1,2},{2,1},{3,0},{4,7},{5,6},{6,5},{7,4},{8,11},{9,10},{10,... | collective-permute-start | bytes 589832 | tf_op jit(solution)/shard_map/ppermute | solution.py:34
  54.3 9.4 %collective-permute-start.9 = (bf16[768,128]{1,0:T(8,128)(2,1)S(1)}, bf16[768,128]{1,0:T(8,128)(2,1)S(1)}, u32[]{:S(2)}, u32[]{:S(2)}) collective-permute-start(bf16[768,128]{1,0:T(8,128)(2,1)S(1)} %get-tuple-element.37), channel_id=1, source_target_pairs={{0,2},{1,3},{2,0},{3,1},{4,6},{5,7},{6,4},{7,5},{8,10},{9,11},{10,... | collective-permute-start | bytes 589832 | tf_op jit(solution)/shard_map/ppermute | solution.py:34
  64.1 8.5 %collective-permute-start.12 = (bf16[128,1152]{1,0:T(8,128)(2,1)S(1)}, bf16[128,1152]{1,0:T(8,128)(2,1)S(1)}, u32[]{:S(2)}, u32[]{:S(2)}) collective-permute-start(bf16[128,1152]{1,0:T(8,128)(2,1)S(1)} %get-tuple-element.43), channel_id=1, source_target_pairs={{4,8},{12,16},{20,24},{5,9},{13,17},{21,25},{6,10},{14,18},{22,26}... | collective-permute-start | bytes 884744 | tf_op jit(solution)/shard_map/ppermute | solution.py:182
  65.4 7.7 %collective-permute-start.15 = (f32[512,128]{1,0:T(8,128)S(1)}, f32[512,128]{1,0:T(8,128)S(1)}, u32[]{:S(2)}, u32[]{:S(2)}) collective-permute-start(f32[512,128]{1,0:T(8,128)S(1)} %get-tuple-element.51), channel_id=1, source_target_pairs={{0,4},{4,0},{8,12},{12,8},{16,20},{20,16},{24,28},{28,24},{1,5},{5... | collective-permute-start | bytes 786440 | tf_op jit(solution)/shard_map/ppermute | solution.py:34
  65.5 3.3 %collective-permute-start.11 = (bf16[128,128]{1,0:T(8,128)(2,1)S(1)}, bf16[128,128]{1,0:T(8,128)(2,1)S(1)}, u32[]{:S(2)}, u32[]{:S(2)}) collective-permute-start(bf16[128,128]{1,0:T(8,128)(2,1)S(1)} %get-tuple-element.42), channel_id=1, source_target_pairs={{0,8},{8,16},{16,24},{1,9},{9,17},{17,25},{2,10},{10,18},{18,26},{... | collective-permute-start | bytes 98312 | tf_op jit(solution)/shard_map/ppermute | solution.py:181
  66.2 6.4 %collective-permute-start.13 = (bf16[128,128]{1,0:T(8,128)(2,1)S(1)}, bf16[128,128]{1,0:T(8,128)(2,1)S(1)}, u32[]{:S(2)}, u32[]{:S(2)}) collective-permute-start(bf16[128,128]{1,0:T(8,128)(2,1)S(1)} %get-tuple-element.44), channel_id=1, source_target_pairs={{8,4},{16,12},{24,20},{9,5},{17,13},{25,21},{10,6},{18,14},{26,22}... | collective-permute-start | bytes 98312 | tf_op jit(solution)/shard_map/ppermute | solution.py:183
  67.5 5.1 %collective-permute-start.14 = (bf16[128,128]{1,0:T(8,128)(2,1)S(1)}, bf16[128,128]{1,0:T(8,128)(2,1)S(1)}, u32[]{:S(2)}, u32[]{:S(2)}) collective-permute-start(bf16[128,128]{1,0:T(8,128)(2,1)S(1)} %get-tuple-element.45), channel_id=1, source_target_pairs={{12,4},{20,12},{28,20},{13,5},{21,13},{29,21},{14,6},{22,14},{30,2... | collective-permute-start | bytes 98312 | tf_op jit(solution)/shard_map/ppermute | solution.py:184

commit v11 on v7

--- a/solution.py
+++ b/solution.py
@@ -35,6 +35,7 @@
 
 
 def call(kernel, outs, operands, after=(), spaces=None, scratch=()):
+    after = tuple(after)
     count = len(operands)
 
     def body(*refs):
@@ -84,7 +85,7 @@
         block[side * rows : (side + 1) * rows] = jnp.dot(states[...], own[...], preferred_element_type=F32)
 
 
-def early_kernel(mine, theirs, near_even, far_even, near_odd, far_odd, near_block, far_block):
+def early_kernel(mine, theirs, own, near_even, far_even, near_odd, far_odd, near_block, far_block, *sent):
     rows, width = mine.shape[0], near_even.shape[1]
     first = core() == 0
     near, far = jnp.where(first, near_even[...], near_odd[...]), jnp.where(first, far_even[...], far_odd[...])
@@ -93,6 +94,16 @@
         result = jnp.dot(states[...], wide, preferred_element_type=F32)
         near_block[side * rows : (side + 1) * rows] = result[:, :width]
         far_block[side * rows : (side + 1) * rows] = result[:, width:]
+    where = block_of_band()
+
+    def store(out, slot, block):
+        @pl.when(slot == lax.bitwise_xor(where, mask))
+        def _():
+            out[...] = block[...].astype(out.dtype)
+
+    for mask, out in enumerate(sent, 1):
+        for slot, block in enumerate((own, near_block, far_block)):
+            store(out, slot, block)
 
 
 def late_kernel(mine, theirs, top, bottom, own, near, far, kept, *refs):
@@ -128,22 +139,37 @@
     bands, chips = lax.axis_size("band"), lax.axis_size("domain") // 2
     rows, states = wavefunctions.shape
     width = rotation.shape[1]
+
+    def across(value, mask, ahead):
+        pairs = []
+        for chip in range(chips):
+            for band in range(bands):
+                place = 2 * chip * bands
+                if ((chip ^ band ^ mask) != chips - 1) == ahead:
+                    pairs.append((place + band, place + (band ^ mask)))
+                if not ahead:
+                    pairs.append((place + bands + band, place + bands + (band ^ mask)))
+        return lax.ppermute(value, ("domain", "band"), pairs)
+
     cut = states * 9 // 16
     received = [exchanged(rotation, "domain", NEAR, 0), exchanged(rotation, "domain", FAR, 0)]
     theirs = exchanged(wavefunctions, "domain", CORE)
     block = [shape(2 * rows, width)]
-    own = call(own_kernel, block, (wavefunctions, theirs, rotation))[0]
-    operator = operator(own)
+    operator = operator(theirs)
     later, _ = lax.optimization_barrier((rotation, operator[0]))
     received += [exchanged(later, "domain", NEAR, CORE), exchanged(later, "domain", FAR, CORE)]
+    own = call(own_kernel, block, (wavefunctions, theirs, rotation), after=(later,))[0]
     outs = [shape(count, width, dtype=BF16) for count in (cut, states - cut)]
-    top, bottom = call(pieces_kernel, outs, received, scratch=[pltpu.SemaphoreType.DMA((2,))])
+    top, bottom = call(pieces_kernel, outs, received, after=(own,), scratch=[pltpu.SemaphoreType.DMA((2,))])
     top, bottom = exchanged(top, "domain", FAR), exchanged(bottom, "domain", NEAR)
-    early = call(early_kernel, block * 2, (wavefunctions, theirs, *received))
-    outs = block + [shape(2 * rows, width, dtype=BF16)] * (bands - 1)
+    messages = [shape(2 * rows, width, dtype=BF16)] * (bands - 1)
+    near, far, *sent = call(early_kernel, block * 2 + messages, (wavefunctions, theirs, own, *received))
+    masks = range(1, bands)[::-1]
+    parts = [across(sent[mask - 1], mask, True) for mask in masks]
     scratch = [pltpu.VMEM((2 * rows, width), F32)]
-    kept, *sent = call(late_kernel, outs, (wavefunctions, theirs, top, bottom, own, *early), scratch=scratch)
-    parts = [exchanged(sent[mask - 1], "band", mask) for mask in reversed(range(1, bands))]
+    operands = (wavefunctions, theirs, top, bottom, own, near, far)
+    kept, *sent = call(late_kernel, block + messages, operands, after=parts, scratch=scratch)
+    parts += [across(sent[mask - 1], mask, False) for mask in masks]
     mine, others = call(sum_kernel, [shape(rows, width)] * 2, (kept, *parts))
     return mine, exchanged(others, "domain", CORE), operator
 

time: 71 us -> 73.6 us (1.037); the launches traced: 70.8 us -> 72.2 us
  starting transfers between devices: 18.1 us -> 24.9 us
  waiting for transfers between devices: 40.7 us -> 34.6 us
    ppermute x0 -> x6, starting transfers between devices: none -> 11.3 us  [across(): return lax.ppermute(value, ('domain', 'band'), pairs)]
    ppermute x12 -> x9, waiting for transfers between devices: 37.8 us -> 26.7 us  [exchanged(): lax.ppermute(value, axis, [(source, source ^ mask) for source in sources...]
    ppermute x0 -> x6, waiting for transfers between devices: none -> 5.69 us  [across(): return lax.ppermute(value, ('domain', 'band'), pairs)]
    ppermute x12 -> x9, starting transfers between devices: 14.7 us -> 10.4 us  [exchanged(): lax.ppermute(value, axis, [(source, source ^ mask) for source in sources...]
    ppermute x1, waiting for transfers between devices: 2.94 us -> 2.17 us  [finish_square(): lax.ppermute(outward, 'domain', across + [(target, source) for source, ta...]
    unnamed x14 -> x10, local copies, waits for them, and re-layouts: 3.13 us -> 3.6 us
  transfers between devices with their start and end apart: 13 -> 16, of which waited for: 9 -> 9; matrix products, arithmetic and copies ran while one was open for 0% -> 0% of each run, Pallas kernels for 7% -> 7%
where the time goes in v11:
time: 73.6 us; the launch traced here: 72.2 us
  waiting for transfers between devices  34.6 us (47%)
  starting transfers between devices  24.9 us (34%)
  Pallas kernels  8.81 us (12%)
  local copies, waits for them, and re-layouts  3.6 us (5%)
    ppermute x9, waiting for transfers between devices, exchanged(): lax.ppermute(value, axis, [(source, source ^ mask) for source in sources...  26.7 us
    ppermute x6, starting transfers between devices, across(): return lax.ppermute(value, ('domain', 'band'), pairs)  11.3 us
    ppermute x9, starting transfers between devices, exchanged(): lax.ppermute(value, axis, [(source, source ^ mask) for source in sources...  10.4 us
    pallas_call x9, Pallas kernels, call(): pl.pallas_call(body, out_shape=outs, in_specs=[pl.BlockSpec(memory_space=...  8.81 us
    ppermute x6, waiting for transfers between devices, across(): return lax.ppermute(value, ('domain', 'band'), pairs)  5.69 us
    unnamed x10, local copies, waits for them, and re-layouts  3.6 us
    ppermute x1, starting transfers between devices, finish_square(): lax.ppermute(outward, 'domain', across + [(target, source) for source, ta...  3.28 us
    ppermute x1, waiting for transfers between devices, finish_square(): lax.ppermute(outward, 'domain', across + [(target, source) for source, ta...  2.17 us
  transfers between devices with their start and end apart: 16, of which 9 were waited for; matrix products, arithmetic and copies ran while one was open for 0% of the time, Pallas kernels for 7%

profile of v11, /device:TPU:1, one launch (start us, length us, event | category | flops | bytes accessed | tf_op | source)
XLA Modules:
  0.0 72.2 jit_solution(9071852493558230327)
XLA Ops:
  0.0 0.0 copy-start
  0.0 0.1 collective-permute-start
  0.1 0.8 %collective-permute-start.2 = (bf16[4096,128]{1,0:T(8,128)(2,1)}, bf16[4096,128]{1,0:T(8,128)(2,1)S(1)}, u32[]{:S(2)}, u32[]{:S(2)}) collective-permute-start(bf16[4096,128]{1,0:T(8,128)(2,1)} %refs_3_), channel_id=1, source_target_pairs={{0,16},{8,24},{16,0},{24,8},{1,17},{9,25},{17,1},{25,9},{2,18},{10... | collective-permute-start | bytes 3145736 | tf_op jit(solution)/shard_map/ppermute | solution.py:34
  0.9 0.9 %collective-permute-start.1 = (bf16[4096,128]{1,0:T(8,128)(2,1)}, bf16[4096,128]{1,0:T(8,128)(2,1)S(1)}, u32[]{:S(2)}, u32[]{:S(2)}) collective-permute-start(bf16[4096,128]{1,0:T(8,128)(2,1)} %refs_3_), channel_id=1, source_target_pairs={{0,8},{8,0},{16,24},{24,16},{1,9},{9,1},{17,25},{25,17},{2,10},{10... | collective-permute-start | bytes 3145736 | tf_op jit(solution)/shard_map/ppermute | solution.py:34
  1.8 4.1 %collective-permute-done.refs_3_.refs_1_ = bf16[384,4096]{1,0:T(8,128)(2,1)S(1)} collective-permute-done((bf16[384,4096]{1,0:T(8,128)(2,1)}, bf16[384,4096]{1,0:T(8,128)(2,1)S(1)}, u32[]{:S(2)}, u32[]{:S(2)}) %collective-permute-start) | collective-permute-done | bytes 3145760 | tf_op jit(solution)/shard_map/ppermute | solution.py:34
  5.9 0.0 copy-start.2
  5.9 1.0 %copy-done.2 = bf16[1,512,512]{2,1,0:T(8,128)(2,1)S(1)} copy-done((bf16[1,512,512]{2,1,0:T(8,128)(2,1)S(1)}, bf16[1,512,512]{2,1,0:T(8,128)(2,1)}, u32[]{:S(2)}) %copy-start.2) | copy-done | bytes 524312
  6.9 0.0 copy-start.3
  6.9 0.7 copy-done.3
  7.6 0.0 copy-start.4
  7.6 0.7 copy-done.4
  8.3 0.7 shard_map.55
  9.0 4.3 %collective-permute-start.4 = (bf16[4096,128]{1,0:T(8,128)(2,1)}, bf16[4096,128]{1,0:T(8,128)(2,1)S(1)}, u32[]{:S(2)}, u32[]{:S(2)}) collective-permute-start(bf16[4096,128]{1,0:T(8,128)(2,1)} %refs_3_), channel_id=1, source_target_pairs={{4,20},{12,28},{20,4},{28,12},{5,21},{13,29},{21,5},{29,13},{6,22}... | collective-permute-start | bytes 3145736 | tf_op jit(solution)/shard_map/ppermute | solution.py:34
  13.3 3.1 %collective-permute-start.3 = (bf16[4096,128]{1,0:T(8,128)(2,1)}, bf16[4096,128]{1,0:T(8,128)(2,1)S(1)}, u32[]{:S(2)}, u32[]{:S(2)}) collective-permute-start(bf16[4096,128]{1,0:T(8,128)(2,1)} %refs_3_), channel_id=1, source_target_pairs={{4,12},{12,4},{20,28},{28,20},{5,13},{13,5},{21,29},{29,21},{6,14}... | collective-permute-start | bytes 3145736 | tf_op jit(solution)/shard_map/ppermute | solution.py:34
  16.4 0.0 copy-done
  16.4 0.0 copy-start.1
  16.4 1.2 %copy-done.1 = bf16[4096,128]{1,0:T(8,128)(2,1)S(1)} copy-done((bf16[4096,128]{1,0:T(8,128)(2,1)S(1)}, bf16[4096,128]{1,0:T(8,128)(2,1)}, u32[]{:S(2)}) %copy-start.1) | copy-done | bytes 1048600
  17.6 1.8 %shard_map.56.refs_4_.refs_2_ = f32[768,128]{1,0:T(8,128)S(1)} custom-call(bf16[384,4096]{1,0:T(8,128)(2,1)S(1)} %copy-done, bf16[384,4096]{1,0:T(8,128)(2,1)S(1)} %collective-permute-done.refs_3_.refs_1_, bf16[4096,128]{1,0:T(8,128)(2,1)S(1)} %copy-done.1, bf16[4096,128]{1,0:T(8,128)(2,1)S(1)} %copy-done.1), custom_call_target="tpu_custom_call" | custom-call | bytes 1024 | tf_op jit(solution)/shard_map/pallas_call | solution.py:44
  19.4 0.0 collective-permute-done.2.refs_1_.refs_4_
  19.4 0.0 collective-permute-done.1.refs_0_.refs_3_
  19.4 10.8 %collective-permute-done.4.refs_3_.refs_6_ = bf16[4096,128]{1,0:T(8,128)(2,1)S(1)} collective-permute-done((bf16[4096,128]{1,0:T(8,128)(2,1)}, bf16[4096,128]{1,0:T(8,128)(2,1)S(1)}, u32[]{:S(2)}, u32[]{:S(2)}) %collective-permute-start.4) | collective-permute-done | bytes 1048608 | tf_op jit(solution)/shard_map/ppermute | solution.py:34
  30.3 6.1 %collective-permute-done.3.refs_2_.refs_5_ = bf16[4096,128]{1,0:T(8,128)(2,1)S(1)} collective-permute-done((bf16[4096,128]{1,0:T(8,128)(2,1)}, bf16[4096,128]{1,0:T(8,128)(2,1)S(1)}, u32[]{:S(2)}, u32[]{:S(2)}) %collective-permute-start.3) | collective-permute-done | bytes 1048608 | tf_op jit(solution)/shard_map/ppermute | solution.py:34
  36.4 0.4 shard_map.57
  36.8 0.1 collective-permute-start.5
  36.9 0.8 %collective-permute-start.6 = (bf16[1792,128]{1,0:T(8,128)(2,1)S(1)}, bf16[1792,128]{1,0:T(8,128)(2,1)S(1)}, u32[]{:S(2)}, u32[]{:S(2)}) collective-permute-start(bf16[1792,128]{1,0:T(8,128)(2,1)S(1)} %get-tuple-element.31), channel_id=1, source_target_pairs={{0,8},{4,12},{8,0},{12,4},{16,24},{20,28},{24,16},{28,20},{1,9},{5... | collective-permute-start | bytes 1376264 | tf_op jit(solution)/shard_map/ppermute | solution.py:34
  37.8 1.9 %shard_map.58 = (f32[768,128]{1,0:T(8,128)S(1)}, f32[768,128]{1,0:T(8,128)S(1)}, bf16[768,128]{1,0:T(8,128)(2,1)S(1)}, bf16[768,128]{1,0:T(8,128)(2,1)S(1)}, bf16[768,128]{1,0:T(8,128)(2,1)S(1)}) custom-call(bf16[384,4096]{1,0:T(8,128)(2,1)S(1)} %copy-done, bf16[384,4096]{1,0:T(8,128)(2,1)S(1)} %collective-permute-done.refs_3_.refs_1_, ...), custom_call_target="tpu_custom_call" | custom-call | bytes 1024 | tf_op jit(solution)/shard_map/pallas_call | solution.py:44
  39.6 0.7 collective-permute-start.7
  40.3 0.7 collective-permute-start.8
  41.0 0.7 collective-permute-start.9
  41.7 0.0 collective-permute-done.7.refs_7_.refs_1_
  41.7 0.0 collective-permute-done.8.refs_8_.refs_2_
  41.7 0.0 collective-permute-done.9.refs_9_.refs_3_
  41.7 2.9 %collective-permute-done.6.refs_3_ = bf16[1792,128]{1,0:T(8,128)(2,1)S(1)} collective-permute-done((bf16[1792,128]{1,0:T(8,128)(2,1)S(1)}, bf16[1792,128]{1,0:T(8,128)(2,1)S(1)}, u32[]{:S(2)}, u32[]{:S(2)}) %collective-permute-start.6) | collective-permute-done | bytes 458784 | tf_op jit(solution)/shard_map/ppermute | solution.py:34
  44.6 1.3 %collective-permute-done.5.refs_2_ = bf16[2304,128]{1,0:T(8,128)(2,1)S(1)} collective-permute-done((bf16[2304,128]{1,0:T(8,128)(2,1)S(1)}, bf16[2304,128]{1,0:T(8,128)(2,1)S(1)}, u32[]{:S(2)}, u32[]{:S(2)}) %collective-permute-start.5) | collective-permute-done | bytes 589856 | tf_op jit(solution)/shard_map/ppermute | solution.py:34
  45.9 1.9 %shard_map.59 = (f32[768,128]{1,0:T(8,128)S(1)}, bf16[768,128]{1,0:T(8,128)(2,1)S(1)}, bf16[768,128]{1,0:T(8,128)(2,1)S(1)}, bf16[768,128]{1,0:T(8,128)(2,1)S(1)}) custom-call(bf16[384,4096]{1,0:T(8,128)(2,1)S(1)} %copy-done, bf16[384,4096]{1,0:T(8,128)(2,1)S(1)} %collective-permute-done.refs_3_.refs_1_, ...), custom_call_target="tpu_custom_call" | custom-call | bytes 1024 | tf_op jit(solution)/shard_map/pallas_call | solution.py:44
  47.8 4.5 %collective-permute-start.10 = (bf16[768,128]{1,0:T(8,128)(2,1)S(1)}, bf16[768,128]{1,0:T(8,128)(2,1)S(1)}, u32[]{:S(2)}, u32[]{:S(2)}) collective-permute-start(bf16[768,128]{1,0:T(8,128)(2,1)S(1)} %get-tuple-element.38), channel_id=1, source_target_pairs={{0,3},{4,7},{5,6},{6,5},{7,4},{12,15},{9,10},{13,14},{14,13},{15,1... | collective-permute-start | bytes 589832 | tf_op jit(solution)/shard_map/ppermute | solution.py:152
  52.4 1.9 %collective-permute-start.11 = (bf16[768,128]{1,0:T(8,128)(2,1)S(1)}, bf16[768,128]{1,0:T(8,128)(2,1)S(1)}, u32[]{:S(2)}, u32[]{:S(2)}) collective-permute-start(bf16[768,128]{1,0:T(8,128)(2,1)S(1)} %get-tuple-element.39), channel_id=1, source_target_pairs={{4,6},{1,3},{5,7},{6,4},{7,5},{8,10},{12,14},{13,15},{14,12},{15,1... | collective-permute-start | bytes 589832 | tf_op jit(solution)/shard_map/ppermute | solution.py:152
  54.3 2.8 %collective-permute-start.12 = (bf16[768,128]{1,0:T(8,128)(2,1)S(1)}, bf16[768,128]{1,0:T(8,128)(2,1)S(1)}, u32[]{:S(2)}, u32[]{:S(2)}) collective-permute-start(bf16[768,128]{1,0:T(8,128)(2,1)S(1)} %get-tuple-element.40), channel_id=1, source_target_pairs={{4,5},{5,4},{2,3},{6,7},{7,6},{12,13},{13,12},{14,15},{11,10},{15,... | collective-permute-start | bytes 589832 | tf_op jit(solution)/shard_map/ppermute | solution.py:152
  57.1 0.0 collective-permute-done.10.refs_4_
  57.1 3.9 %collective-permute-done.11.refs_5_ = bf16[768,128]{1,0:T(8,128)(2,1)S(1)} collective-permute-done((bf16[768,128]{1,0:T(8,128)(2,1)S(1)}, bf16[768,128]{1,0:T(8,128)(2,1)S(1)}, u32[]{:S(2)}, u32[]{:S(2)}) %collective-permute-start.11) | collective-permute-done | bytes 196640 | tf_op jit(solution)/shard_map/ppermute | solution.py:152
  61.0 1.8 %collective-permute-done.12.refs_6_ = bf16[768,128]{1,0:T(8,128)(2,1)S(1)} collective-permute-done((bf16[768,128]{1,0:T(8,128)(2,1)S(1)}, bf16[768,128]{1,0:T(8,128)(2,1)S(1)}, u32[]{:S(2)}, u32[]{:S(2)}) %collective-permute-start.12) | collective-permute-done | bytes 196640 | tf_op jit(solution)/shard_map/ppermute | solution.py:152
  62.8 0.2 shard_map.60
  63.0 0.1 collective-permute-start.13
  63.0 1.4 %collective-permute-done.13.refs_1_ = f32[384,128]{1,0:T(8,128)S(1)} collective-permute-done((f32[384,128]{1,0:T(8,128)S(1)}, f32[384,128]{1,0:T(8,128)S(1)}, u32[]{:S(2)}, u32[]{:S(2)}) %collective-permute-start.13) | collective-permute-done | bytes 196640 | tf_op jit(solution)/shard_map/ppermute | solution.py:34
  64.5 0.3 shard_map.61
  64.8 0.2 collective-permute-start.14
  65.0 3.3 %collective-permute-start.15 = (bf16[128,384]{1,0:T(8,128)(2,1)S(1)}, bf16[128,384]{1,0:T(8,128)(2,1)S(1)}, u32[]{:S(2)}, u32[]{:S(2)}) collective-permute-start(bf16[128,384]{1,0:T(8,128)(2,1)S(1)} %get-tuple-element.50), channel_id=1, source_target_pairs={{4,8},{12,16},{20,24},{8,4},{16,12},{24,20},{5,9},{13,17},{21,25},... | collective-permute-start | bytes 294920 | tf_op jit(solution)/shard_map/ppermute | solution.py:230
  68.3 0.5 shard_map.62
  68.7 0.0 collective-permute-done.14.refs_5_
  68.7 2.2 %collective-permute-done.15.refs_6_ = bf16[128,384]{1,0:T(8,128)(2,1)S(1)} collective-permute-done((bf16[128,384]{1,0:T(8,128)(2,1)S(1)}, bf16[128,384]{1,0:T(8,128)(2,1)S(1)}, u32[]{:S(2)}, u32[]{:S(2)}) %collective-permute-start.15) | collective-permute-done | bytes 98336 | tf_op jit(solution)/shard_map/ppermute | solution.py:230
  70.9 1.2 %shard_map.63 = f32[384,256]{1,0:T(8,128)} custom-call(f32[384,256]{1,0:T(8,128)S(1)} %get-tuple-element.45.refs_0_, bf16[128,256]{1,0:T(8,128)(2,1)S(1)} %get-tuple-element.46.refs_1_, bf16[128,256]{1,0:T(8,128)(2,1)S(1)} %get-tuple-element.47.refs_2_, bf16[512,512]{1,0:T(8,128)(2,1)S(1)} %get-tuple-element.28.refs_2_.refs_1_.refs_3_, ...), custom_call_target="tpu_custom_call" | custom-call | bytes 1024 | tf_op jit(solution)/shard_map/pallas_call | solution.py:44
Async XLA Ops:
  0.0 16.4 %copy-start = (bf16[384,4096]{1,0:T(8,128)(2,1)S(1)}, bf16[384,4096]{1,0:T(8,128)(2,1)}, u32[]{:S(2)}) copy-start(bf16[384,4096]{1,0:T(8,128)(2,1)} %refs_0_.7) | copy-start | bytes 9437188
  0.0 5.9 %collective-permute-start = (bf16[384,4096]{1,0:T(8,128)(2,1)}, bf16[384,4096]{1,0:T(8,128)(2,1)S(1)}, u32[]{:S(2)}, u32[]{:S(2)}) collective-permute-start(bf16[384,4096]{1,0:T(8,128)(2,1)} %refs_0_.7), channel_id=1, source_target_pairs={{0,4},{4,0},{8,12},{12,8},{16,20},{20,16},{24,28},{28,24},{1,5},{5... | collective-permute-start | bytes 9437192 | tf_op jit(solution)/shard_map/ppermute | solution.py:34
  0.1 19.3 %collective-permute-start.2 = (bf16[4096,128]{1,0:T(8,128)(2,1)}, bf16[4096,128]{1,0:T(8,128)(2,1)S(1)}, u32[]{:S(2)}, u32[]{:S(2)}) collective-permute-start(bf16[4096,128]{1,0:T(8,128)(2,1)} %refs_3_), channel_id=1, source_target_pairs={{0,16},{8,24},{16,0},{24,8},{1,17},{9,25},{17,1},{25,9},{2,18},{10... | collective-permute-start | bytes 3145736 | tf_op jit(solution)/shard_map/ppermute | solution.py:34
  0.9 18.5 %collective-permute-start.1 = (bf16[4096,128]{1,0:T(8,128)(2,1)}, bf16[4096,128]{1,0:T(8,128)(2,1)S(1)}, u32[]{:S(2)}, u32[]{:S(2)}) collective-permute-start(bf16[4096,128]{1,0:T(8,128)(2,1)} %refs_3_), channel_id=1, source_target_pairs={{0,8},{8,0},{16,24},{24,16},{1,9},{9,1},{17,25},{25,17},{2,10},{10... | collective-permute-start | bytes 3145736 | tf_op jit(solution)/shard_map/ppermute | solution.py:34
  5.9 1.0 %copy-start.2 = (bf16[1,512,512]{2,1,0:T(8,128)(2,1)S(1)}, bf16[1,512,512]{2,1,0:T(8,128)(2,1)}, u32[]{:S(2)}) copy-start(bf16[1,512,512]{2,1,0:T(8,128)(2,1)} %refs_0_.4) | copy-start | bytes 1572868
  6.9 0.7 copy-start.3
  7.6 0.7 copy-start.4
  9.0 21.3 %collective-permute-start.4 = (bf16[4096,128]{1,0:T(8,128)(2,1)}, bf16[4096,128]{1,0:T(8,128)(2,1)S(1)}, u32[]{:S(2)}, u32[]{:S(2)}) collective-permute-start(bf16[4096,128]{1,0:T(8,128)(2,1)} %refs_3_), channel_id=1, source_target_pairs={{4,20},{12,28},{20,4},{28,12},{5,21},{13,29},{21,5},{29,13},{6,22}... | collective-permute-start | bytes 3145736 | tf_op jit(solution)/shard_map/ppermute | solution.py:34
  13.3 23.2 %collective-permute-start.3 = (bf16[4096,128]{1,0:T(8,128)(2,1)}, bf16[4096,128]{1,0:T(8,128)(2,1)S(1)}, u32[]{:S(2)}, u32[]{:S(2)}) collective-permute-start(bf16[4096,128]{1,0:T(8,128)(2,1)} %refs_3_), channel_id=1, source_target_pairs={{4,12},{12,4},{20,28},{28,20},{5,13},{13,5},{21,29},{29,21},{6,14}... | collective-permute-start | bytes 3145736 | tf_op jit(solution)/shard_map/ppermute | solution.py:34
  16.4 1.2 %copy-start.1 = (bf16[4096,128]{1,0:T(8,128)(2,1)S(1)}, bf16[4096,128]{1,0:T(8,128)(2,1)}, u32[]{:S(2)}) copy-start(bf16[4096,128]{1,0:T(8,128)(2,1)} %refs_3_) | copy-start | bytes 3145732
  36.8 9.1 %collective-permute-start.5 = (bf16[2304,128]{1,0:T(8,128)(2,1)S(1)}, bf16[2304,128]{1,0:T(8,128)(2,1)S(1)}, u32[]{:S(2)}, u32[]{:S(2)}) collective-permute-start(bf16[2304,128]{1,0:T(8,128)(2,1)S(1)} %get-tuple-element.30), channel_id=1, source_target_pairs={{0,16},{4,20},{8,24},{12,28},{16,0},{20,4},{24,8},{28,12},{1,17},{... | collective-permute-start | bytes 1769480 | tf_op jit(solution)/shard_map/ppermute | solution.py:34
  36.9 7.7 %collective-permute-start.6 = (bf16[1792,128]{1,0:T(8,128)(2,1)S(1)}, bf16[1792,128]{1,0:T(8,128)(2,1)S(1)}, u32[]{:S(2)}, u32[]{:S(2)}) collective-permute-start(bf16[1792,128]{1,0:T(8,128)(2,1)S(1)} %get-tuple-element.31), channel_id=1, source_target_pairs={{0,8},{4,12},{8,0},{12,4},{16,24},{20,28},{24,16},{28,20},{1,9},{5... | collective-permute-start | bytes 1376264 | tf_op jit(solution)/shard_map/ppermute | solution.py:34
  39.6 2.0 %collective-permute-start.7 = (bf16[768,128]{1,0:T(8,128)(2,1)S(1)}, bf16[768,128]{1,0:T(8,128)(2,1)S(1)}, u32[]{:S(2)}, u32[]{:S(2)}) collective-permute-start(bf16[768,128]{1,0:T(8,128)(2,1)S(1)} %get-tuple-element.34), channel_id=1, source_target_pairs={{1,2},{2,1},{3,0},{8,11},{10,9},{11,8},{16,19},{17,18},{19,16},{24... | collective-permute-start | bytes 589832 | tf_op jit(solution)/shard_map/ppermute | solution.py:152
  40.3 1.4 %collective-permute-start.8 = (bf16[768,128]{1,0:T(8,128)(2,1)S(1)}, bf16[768,128]{1,0:T(8,128)(2,1)S(1)}, u32[]{:S(2)}, u32[]{:S(2)}) collective-permute-start(bf16[768,128]{1,0:T(8,128)(2,1)S(1)} %get-tuple-element.35), channel_id=1, source_target_pairs={{0,2},{2,0},{3,1},{9,11},{10,8},{11,9},{16,18},{17,19},{18,16},{24... | collective-permute-start | bytes 589832 | tf_op jit(solution)/shard_map/ppermute | solution.py:152
  41.0 0.7 collective-permute-start.9
  47.8 9.3 %collective-permute-start.10 = (bf16[768,128]{1,0:T(8,128)(2,1)S(1)}, bf16[768,128]{1,0:T(8,128)(2,1)S(1)}, u32[]{:S(2)}, u32[]{:S(2)}) collective-permute-start(bf16[768,128]{1,0:T(8,128)(2,1)S(1)} %get-tuple-element.38), channel_id=1, source_target_pairs={{0,3},{4,7},{5,6},{6,5},{7,4},{12,15},{9,10},{13,14},{14,13},{15,1... | collective-permute-start | bytes 589832 | tf_op jit(solution)/shard_map/ppermute | solution.py:152
  52.4 8.6 %collective-permute-start.11 = (bf16[768,128]{1,0:T(8,128)(2,1)S(1)}, bf16[768,128]{1,0:T(8,128)(2,1)S(1)}, u32[]{:S(2)}, u32[]{:S(2)}) collective-permute-start(bf16[768,128]{1,0:T(8,128)(2,1)S(1)} %get-tuple-element.39), channel_id=1, source_target_pairs={{4,6},{1,3},{5,7},{6,4},{7,5},{8,10},{12,14},{13,15},{14,12},{15,1... | collective-permute-start | bytes 589832 | tf_op jit(solution)/shard_map/ppermute | solution.py:152
  54.3 8.5 %collective-permute-start.12 = (bf16[768,128]{1,0:T(8,128)(2,1)S(1)}, bf16[768,128]{1,0:T(8,128)(2,1)S(1)}, u32[]{:S(2)}, u32[]{:S(2)}) collective-permute-start(bf16[768,128]{1,0:T(8,128)(2,1)S(1)} %get-tuple-element.40), channel_id=1, source_target_pairs={{4,5},{5,4},{2,3},{6,7},{7,6},{12,13},{13,12},{14,15},{11,10},{15,... | collective-permute-start | bytes 589832 | tf_op jit(solution)/shard_map/ppermute | solution.py:152
  63.0 1.5 %collective-permute-start.13 = (f32[384,128]{1,0:T(8,128)S(1)}, f32[384,128]{1,0:T(8,128)S(1)}, u32[]{:S(2)}, u32[]{:S(2)}) collective-permute-start(f32[384,128]{1,0:T(8,128)S(1)} %get-tuple-element.42), channel_id=1, source_target_pairs={{0,4},{4,0},{8,12},{12,8},{16,20},{20,16},{24,28},{28,24},{1,5},{5... | collective-permute-start | bytes 589832 | tf_op jit(solution)/shard_map/ppermute | solution.py:34
  64.8 4.0 %collective-permute-start.14 = (bf16[128,384]{1,0:T(8,128)(2,1)S(1)}, bf16[128,384]{1,0:T(8,128)(2,1)S(1)}, u32[]{:S(2)}, u32[]{:S(2)}) collective-permute-start(bf16[128,384]{1,0:T(8,128)(2,1)S(1)} %get-tuple-element.49), channel_id=1, source_target_pairs={{0,4},{4,0},{8,12},{12,8},{16,20},{20,16},{24,28},{28,24},{1,5},{5... | collective-permute-start | bytes 294920 | tf_op jit(solution)/shard_map/ppermute | solution.py:34
  65.0 5.9 %collective-permute-start.15 = (bf16[128,384]{1,0:T(8,128)(2,1)S(1)}, bf16[128,384]{1,0:T(8,128)(2,1)S(1)}, u32[]{:S(2)}, u32[]{:S(2)}) collective-permute-start(bf16[128,384]{1,0:T(8,128)(2,1)S(1)} %get-tuple-element.50), channel_id=1, source_target_pairs={{4,8},{12,16},{20,24},{8,4},{16,12},{24,20},{5,9},{13,17},{21,25},... | collective-permute-start | bytes 294920 | tf_op jit(solution)/shard_map/ppermute | solution.py:230

commit v12 on v7

--- a/solution.py
+++ b/solution.py
@@ -35,6 +35,7 @@
 
 
 def call(kernel, outs, operands, after=(), spaces=None, scratch=()):
+    after = tuple(after)
     count = len(operands)
 
     def body(*refs):
@@ -63,19 +64,16 @@
     return lax.bitwise_xor(lax.div(lax.axis_index("domain"), 2), lax.axis_index("band"))
 
 
-def pieces_kernel(near_even, far_even, near_odd, far_odd, top, bottom, done):
-    def fill(near, far):
-        copies = [
-            pltpu.make_async_copy(near.at[pl.ds(0, top.shape[0])], top, done.at[0]),
-            pltpu.make_async_copy(far.at[pl.ds(top.shape[0], bottom.shape[0])], bottom, done.at[1]),
-        ]
-        for copy in copies:
-            copy.start()
-        for copy in copies:
-            copy.wait()
-
-    pl.when(core() == 0)(lambda: fill(near_even, far_even))
-    pl.when(core() != 0)(lambda: fill(near_odd, far_odd))
+def pieces_kernel(far, near, top, bottom, done):
+    cut, rest = top.shape[0], bottom.shape[0]
+    copies = [
+        pltpu.make_async_copy(near.at[pl.ds(0, cut)], top, done.at[0]),
+        pltpu.make_async_copy(far.at[pl.ds(cut, rest)], bottom, done.at[1]),
+    ]
+    for copy in copies:
+        copy.start()
+    for copy in copies:
+        copy.wait()
 
 
 def own_kernel(mine, theirs, own, block):
@@ -95,13 +93,18 @@
         far_block[side * rows : (side + 1) * rows] = result[:, width:]
 
 
-def late_kernel(mine, theirs, top, bottom, own, near, far, kept, *refs):
+def late_kernel(mine, theirs, top_even, bottom_even, top_odd, bottom_odd, own, near, far, kept, *refs):
     sent, last = refs[:-1], refs[-1]
-    cut = top.shape[0]
     rows = mine.shape[0]
-    for side, states in enumerate((mine, theirs)):
-        result = jnp.dot(states[:, :cut], top[...], preferred_element_type=F32)
-        last[side * rows : (side + 1) * rows] = result + jnp.dot(states[:, cut:], bottom[...], preferred_element_type=F32)
+
+    def multiply(top, bottom):
+        cut = top.shape[0]
+        for side, states in enumerate((mine, theirs)):
+            result = jnp.dot(states[:, :cut], top[...], preferred_element_type=F32)
+            last[side * rows : (side + 1) * rows] = result + jnp.dot(states[:, cut:], bottom[...], preferred_element_type=F32)
+
+    pl.when(core() == 0)(lambda: multiply(top_even, bottom_even))
+    pl.when(core() != 0)(lambda: multiply(top_odd, bottom_odd))
     where = block_of_band()
 
     def store(out, slot, block):
@@ -128,7 +131,6 @@
     bands, chips = lax.axis_size("band"), lax.axis_size("domain") // 2
     rows, states = wavefunctions.shape
     width = rotation.shape[1]
-    cut = states * 9 // 16
     received = [exchanged(rotation, "domain", NEAR, 0), exchanged(rotation, "domain", FAR, 0)]
     theirs = exchanged(wavefunctions, "domain", CORE)
     block = [shape(2 * rows, width)]
@@ -136,14 +138,19 @@
     operator = operator(own)
     later, _ = lax.optimization_barrier((rotation, operator[0]))
     received += [exchanged(later, "domain", NEAR, CORE), exchanged(later, "domain", FAR, CORE)]
-    outs = [shape(count, width, dtype=BF16) for count in (cut, states - cut)]
-    top, bottom = call(pieces_kernel, outs, received, scratch=[pltpu.SemaphoreType.DMA((2,))])
-    top, bottom = exchanged(top, "domain", FAR), exchanged(bottom, "domain", NEAR)
+    passed, previous = [], []
+    for one, share in ((0, 21), (CORE, 17)):
+        cut = states * share // 32
+        outs = [shape(count, width, dtype=BF16) for count in (cut, states - cut)]
+        pair = received[2 * one : 2 * one + 2][::-1]
+        top, bottom = call(pieces_kernel, outs, pair, after=previous, scratch=[pltpu.SemaphoreType.DMA((2,))])
+        previous = [bottom]
+        passed += [exchanged(top, "domain", FAR, one), exchanged(bottom, "domain", NEAR, one)]
     early = call(early_kernel, block * 2, (wavefunctions, theirs, *received))
     outs = block + [shape(2 * rows, width, dtype=BF16)] * (bands - 1)
     scratch = [pltpu.VMEM((2 * rows, width), F32)]
-    kept, *sent = call(late_kernel, outs, (wavefunctions, theirs, top, bottom, own, *early), scratch=scratch)
-    parts = [exchanged(sent[mask - 1], "band", mask) for mask in reversed(range(1, bands))]
+    kept, *sent = call(late_kernel, outs, (wavefunctions, theirs, *passed, own, *early), scratch=scratch)
+    parts = [exchanged(sent[mask - 1], "band", mask) for mask in (1, *reversed(range(2, bands)))]
     mine, others = call(sum_kernel, [shape(rows, width)] * 2, (kept, *parts))
     return mine, exchanged(others, "domain", CORE), operator
 

time: 71 us -> 70.3 us (level)
  waiting for transfers between devices: 40.7 us -> 34.8 us
  starting transfers between devices: 18.1 us -> 22.2 us
    ppermute x12 -> x14, waiting for transfers between devices: 37.8 us -> 32.3 us  [exchanged(): lax.ppermute(value, axis, [(source, source ^ mask) for source in sources...]
    ppermute x12 -> x14, starting transfers between devices: 14.7 us -> 18.8 us  [exchanged(): lax.ppermute(value, axis, [(source, source ^ mask) for source in sources...]
    pallas_call x9 -> x10, Pallas kernels: 8.66 us -> 9.12 us  [call(): pl.pallas_call(body, out_shape=outs, in_specs=[pl.BlockSpec(memory_space=...]
  transfers between devices with their start and end apart: 13 -> 15, of which waited for: 9 -> 8; matrix products, arithmetic and copies ran while one was open for 0% -> 0% of each run, Pallas kernels for 7% -> 8%
where the time goes in v12:
time: 70.3 us; the launch traced here: 69.5 us
  waiting for transfers between devices  34.8 us (50%)
  starting transfers between devices  22.2 us (32%)
  Pallas kernels  9.12 us (13%)
  local copies, waits for them, and re-layouts  3.13 us (4%)
    ppermute x14, waiting for transfers between devices, exchanged(): lax.ppermute(value, axis, [(source, source ^ mask) for source in sources...  32.3 us
    ppermute x14, starting transfers between devices, exchanged(): lax.ppermute(value, axis, [(source, source ^ mask) for source in sources...  18.8 us
    pallas_call x10, Pallas kernels, call(): pl.pallas_call(body, out_shape=outs, in_specs=[pl.BlockSpec(memory_space=...  9.12 us
    ppermute x1, starting transfers between devices, finish_square(): lax.ppermute(outward, 'domain', across + [(target, source) for source, ta...  3.37 us
    unnamed x14, local copies, waits for them, and re-layouts  3.13 us
    ppermute x1, waiting for transfers between devices, finish_square(): lax.ppermute(outward, 'domain', across + [(target, source) for source, ta...  2.53 us
  transfers between devices with their start and end apart: 15, of which 8 were waited for; matrix products, arithmetic and copies ran while one was open for 0% of the time, Pallas kernels for 8%

profile of v12, /device:TPU:1, one launch (start us, length us, event | category | flops | bytes accessed | tf_op | source)
XLA Modules:
  0.0 69.5 jit_solution(3582954734476299630)
XLA Ops:
  0.0 0.1 collective-permute-start
  0.1 0.7 %collective-permute-start.1 = (bf16[4096,128]{1,0:T(8,128)(2,1)}, bf16[4096,128]{1,0:T(8,128)(2,1)S(1)}, u32[]{:S(2)}, u32[]{:S(2)}) collective-permute-start(bf16[4096,128]{1,0:T(8,128)(2,1)} %refs_2_.1), channel_id=1, source_target_pairs={{0,16},{8,24},{16,0},{24,8},{1,17},{9,25},{17,1},{25,9},{2,18},{10... | collective-permute-start | bytes 3145736 | tf_op jit(solution)/shard_map/ppermute | solution.py:34
  0.8 0.7 %collective-permute-start.2 = (bf16[4096,128]{1,0:T(8,128)(2,1)}, bf16[4096,128]{1,0:T(8,128)(2,1)S(1)}, u32[]{:S(2)}, u32[]{:S(2)}) collective-permute-start(bf16[4096,128]{1,0:T(8,128)(2,1)} %refs_2_.1), channel_id=1, source_target_pairs={{0,8},{8,0},{16,24},{24,16},{1,9},{9,1},{17,25},{25,17},{2,10},{10... | collective-permute-start | bytes 3145736 | tf_op jit(solution)/shard_map/ppermute | solution.py:34
  1.5 4.4 %collective-permute-done.refs_1_ = bf16[384,4096]{1,0:T(8,128)(2,1)S(1)} collective-permute-done((bf16[384,4096]{1,0:T(8,128)(2,1)}, bf16[384,4096]{1,0:T(8,128)(2,1)S(1)}, u32[]{:S(2)}, u32[]{:S(2)}) %collective-permute-start) | collective-permute-done | bytes 3145760 | tf_op jit(solution)/shard_map/ppermute | solution.py:34
  5.9 0.0 copy-start
  5.9 1.9 %copy-done = bf16[384,4096]{1,0:T(8,128)(2,1)S(1)} copy-done((bf16[384,4096]{1,0:T(8,128)(2,1)S(1)}, bf16[384,4096]{1,0:T(8,128)(2,1)}, u32[]{:S(2)}) %copy-start) | copy-done | bytes 3145752
  7.8 0.0 copy-start.2
  7.8 1.2 %copy-done.2 = bf16[4096,128]{1,0:T(8,128)(2,1)S(1)} copy-done((bf16[4096,128]{1,0:T(8,128)(2,1)S(1)}, bf16[4096,128]{1,0:T(8,128)(2,1)}, u32[]{:S(2)}) %copy-start.2) | copy-done | bytes 1048600
  9.0 0.0 copy-start.4
  9.0 0.0 copy-start.5
  9.0 0.0 copy-start.6
  9.0 0.0 copy-start.3
  9.0 1.8 %shard_map.56.refs_3_.refs_6_ = f32[768,128]{1,0:T(8,128)S(1)} custom-call(bf16[384,4096]{1,0:T(8,128)(2,1)S(1)} %copy-done, bf16[384,4096]{1,0:T(8,128)(2,1)S(1)} %collective-permute-done.refs_1_, bf16[4096,128]{1,0:T(8,128)(2,1)S(1)} %copy-done.2), custom_call_target="tpu_custom_call" | custom-call | bytes 1024 | tf_op jit(solution)/shard_map/pallas_call | solution.py:44
  10.8 0.0 copy-start.1
  10.8 0.0 copy-done.4
  10.8 0.0 copy-done.5
  10.8 0.0 copy-done.6
  10.8 0.7 %shard_map.57 = (bf16[512,512]{1,0:T(8,128)(2,1)S(1)}, bf16[128,384]{1,0:T(8,128)(2,1)S(1)}, bf16[384,128]{1,0:T(8,128)(2,1)S(1)}) custom-call(bf16[1,512,512]{2,1,0:T(8,128)(2,1)S(1)} %copy-done.4, s32[1,512]{1,0:T(1,128)S(1)} %copy-done.5, s32[1,128]{1,0:T(1,128)S(1)} %bitcast.1, f32[768,128]{1,0:T(8,128)S(1)} %shard_map.56.refs_3_.refs_6_), custom_call_target="tpu_custom_call" | custom-call | bytes 1024 | tf_op jit(solution)/shard_map/pallas_call | solution.py:44
  11.5 0.0 copy-done.3
  11.5 4.4 %collective-permute-start.5 = (bf16[4096,128]{1,0:T(8,128)(2,1)S(1)}, bf16[4096,128]{1,0:T(8,128)(2,1)S(1)}, u32[]{:S(2)}, u32[]{:S(2)}) collective-permute-start(bf16[4096,128]{1,0:T(8,128)(2,1)S(1)} %copy-done.3), channel_id=1, source_target_pairs={{4,20},{12,28},{20,4},{28,12},{5,21},{13,29},{21,5},{29,13},{6,22}... | collective-permute-start | bytes 3145736 | tf_op jit(solution)/shard_map/ppermute | solution.py:34
  16.0 3.1 %collective-permute-start.6 = (bf16[4096,128]{1,0:T(8,128)(2,1)S(1)}, bf16[4096,128]{1,0:T(8,128)(2,1)S(1)}, u32[]{:S(2)}, u32[]{:S(2)}) collective-permute-start(bf16[4096,128]{1,0:T(8,128)(2,1)S(1)} %copy-done.3), channel_id=1, source_target_pairs={{4,12},{12,4},{20,28},{28,20},{5,13},{13,5},{21,29},{29,21},{6,14}... | collective-permute-start | bytes 3145736 | tf_op jit(solution)/shard_map/ppermute | solution.py:34
  19.1 0.0 collective-permute-done.1.refs_0_.refs_3_
  19.1 0.0 collective-permute-done.2.refs_1_.refs_2_
  19.1 0.4 shard_map.55
  19.5 0.7 %collective-permute-start.3 = (bf16[2688,128]{1,0:T(8,128)(2,1)S(1)}, bf16[2688,128]{1,0:T(8,128)(2,1)S(1)}, u32[]{:S(2)}, u32[]{:S(2)}) collective-permute-start(bf16[2688,128]{1,0:T(8,128)(2,1)S(1)} %get-tuple-element.27), channel_id=1, source_target_pairs={{0,16},{8,24},{16,0},{24,8},{1,17},{9,25},{17,1},{25,9},{2,18},{10... | collective-permute-start | bytes 2064392 | tf_op jit(solution)/shard_map/ppermute | solution.py:34
  20.2 10.6 %collective-permute-done.5.refs_0_.refs_5_ = bf16[4096,128]{1,0:T(8,128)(2,1)S(1)} collective-permute-done((bf16[4096,128]{1,0:T(8,128)(2,1)S(1)}, bf16[4096,128]{1,0:T(8,128)(2,1)S(1)}, u32[]{:S(2)}, u32[]{:S(2)}) %collective-permute-start.5) | collective-permute-done | bytes 1048608 | tf_op jit(solution)/shard_map/ppermute | solution.py:34
  30.8 2.5 %collective-permute-done.6.refs_1_.refs_4_ = bf16[4096,128]{1,0:T(8,128)(2,1)S(1)} collective-permute-done((bf16[4096,128]{1,0:T(8,128)(2,1)S(1)}, bf16[4096,128]{1,0:T(8,128)(2,1)S(1)}, u32[]{:S(2)}, u32[]{:S(2)}) %collective-permute-start.6) | collective-permute-done | bytes 1048608 | tf_op jit(solution)/shard_map/ppermute | solution.py:34
  33.4 0.4 shard_map.58
  33.8 1.9 %collective-permute-start.7 = (bf16[2176,128]{1,0:T(8,128)(2,1)S(1)}, bf16[2176,128]{1,0:T(8,128)(2,1)S(1)}, u32[]{:S(2)}, u32[]{:S(2)}) collective-permute-start(bf16[2176,128]{1,0:T(8,128)(2,1)S(1)} %get-tuple-element.31), channel_id=1, source_target_pairs={{4,20},{12,28},{20,4},{28,12},{5,21},{13,29},{21,5},{29,13},{6,22}... | collective-permute-start | bytes 1671176 | tf_op jit(solution)/shard_map/ppermute | solution.py:34
  35.7 2.6 %collective-permute-start.8 = (bf16[1920,128]{1,0:T(8,128)(2,1)S(1)}, bf16[1920,128]{1,0:T(8,128)(2,1)S(1)}, u32[]{:S(2)}, u32[]{:S(2)}) collective-permute-start(bf16[1920,128]{1,0:T(8,128)(2,1)S(1)} %get-tuple-element.32), channel_id=1, source_target_pairs={{4,12},{12,4},{20,28},{28,20},{5,13},{13,5},{21,29},{29,21},{6,14}... | collective-permute-start | bytes 1474568 | tf_op jit(solution)/shard_map/ppermute | solution.py:34
  38.4 0.7 collective-permute-start.4
  39.1 0.0 copy-done.1
  39.1 1.8 %shard_map.59 = (f32[768,128]{1,0:T(8,128)S(1)}, f32[768,128]{1,0:T(8,128)S(1)}) custom-call(bf16[384,4096]{1,0:T(8,128)(2,1)S(1)} %copy-done.1, bf16[384,4096]{1,0:T(8,128)(2,1)S(1)} %collective-permute-done.refs_1_, bf16[4096,128]{1,0:T(8,128)(2,1)S(1)} %collective-permute-done.2.refs_1_.refs_2_, ...), custom_call_target="tpu_custom_call" | custom-call | bytes 1024 | tf_op jit(solution)/shard_map/pallas_call | solution.py:44
  40.9 0.0 collective-permute-done.4.refs_3_
  40.9 0.0 collective-permute-done.3.refs_2_
  40.9 4.7 %collective-permute-done.8.refs_5_ = bf16[1920,128]{1,0:T(8,128)(2,1)S(1)} collective-permute-done((bf16[1920,128]{1,0:T(8,128)(2,1)S(1)}, bf16[1920,128]{1,0:T(8,128)(2,1)S(1)}, u32[]{:S(2)}, u32[]{:S(2)}) %collective-permute-start.8) | collective-permute-done | bytes 491552 | tf_op jit(solution)/shard_map/ppermute | solution.py:34
  45.6 0.0 collective-permute-done.7.refs_4_
  45.6 1.9 %shard_map.60 = (f32[768,128]{1,0:T(8,128)S(1)}, bf16[768,128]{1,0:T(8,128)(2,1)S(1)}, bf16[768,128]{1,0:T(8,128)(2,1)S(1)}, bf16[768,128]{1,0:T(8,128)(2,1)S(1)}) custom-call(bf16[384,4096]{1,0:T(8,128)(2,1)S(1)} %copy-done.1, bf16[384,4096]{1,0:T(8,128)(2,1)S(1)} %collective-permute-done.refs_1_, bf16[2688,128]{1,0:T(8,128)(2,1)S(1)} %collective-permute-done.3.refs_2_, ...), custom_call_target="tpu_custom_call" | custom-call | bytes 1024 | tf_op jit(solution)/shard_map/pallas_call | solution.py:44
  47.6 2.9 %collective-permute-start.10 = (bf16[768,128]{1,0:T(8,128)(2,1)S(1)}, bf16[768,128]{1,0:T(8,128)(2,1)S(1)}, u32[]{:S(2)}, u32[]{:S(2)}) collective-permute-start(bf16[768,128]{1,0:T(8,128)(2,1)S(1)} %get-tuple-element.37), channel_id=1, source_target_pairs={{0,3},{1,2},{2,1},{3,0},{4,7},{5,6},{6,5},{7,4},{8,11},{9,10},{10,... | collective-permute-start | bytes 589832 | tf_op jit(solution)/shard_map/ppermute | solution.py:34
  50.4 0.0 collective-permute-start.11
  50.4 0.7 %collective-permute-start.9 = (bf16[768,128]{1,0:T(8,128)(2,1)S(1)}, bf16[768,128]{1,0:T(8,128)(2,1)S(1)}, u32[]{:S(2)}, u32[]{:S(2)}) collective-permute-start(bf16[768,128]{1,0:T(8,128)(2,1)S(1)} %get-tuple-element.36), channel_id=1, source_target_pairs={{0,1},{1,0},{2,3},{3,2},{4,5},{5,4},{6,7},{7,6},{8,9},{9,8},{10,11... | collective-permute-start | bytes 589832 | tf_op jit(solution)/shard_map/ppermute | solution.py:34
  51.2 3.0 %collective-permute-done.10.refs_2_ = bf16[768,128]{1,0:T(8,128)(2,1)S(1)} collective-permute-done((bf16[768,128]{1,0:T(8,128)(2,1)S(1)}, bf16[768,128]{1,0:T(8,128)(2,1)S(1)}, u32[]{:S(2)}, u32[]{:S(2)}) %collective-permute-start.10) | collective-permute-done | bytes 196640 | tf_op jit(solution)/shard_map/ppermute | solution.py:34
  54.1 5.6 %collective-permute-done.11.refs_3_ = bf16[768,128]{1,0:T(8,128)(2,1)S(1)} collective-permute-done((bf16[768,128]{1,0:T(8,128)(2,1)S(1)}, bf16[768,128]{1,0:T(8,128)(2,1)S(1)}, u32[]{:S(2)}, u32[]{:S(2)}) %collective-permute-start.11) | collective-permute-done | bytes 196640 | tf_op jit(solution)/shard_map/ppermute | solution.py:34
  59.8 0.0 collective-permute-done.9.refs_1_
  59.8 0.1 shard_map.61
  59.9 0.1 collective-permute-start.12
  60.0 1.4 %collective-permute-done.12.refs_1_ = f32[384,128]{1,0:T(8,128)S(1)} collective-permute-done((f32[384,128]{1,0:T(8,128)S(1)}, f32[384,128]{1,0:T(8,128)S(1)}, u32[]{:S(2)}, u32[]{:S(2)}) %collective-permute-start.12) | collective-permute-done | bytes 196640 | tf_op jit(solution)/shard_map/ppermute | solution.py:34
  61.4 0.3 shard_map.62
  61.7 0.2 collective-permute-start.13
  61.9 3.4 %collective-permute-start.14 = (bf16[128,384]{1,0:T(8,128)(2,1)S(1)}, bf16[128,384]{1,0:T(8,128)(2,1)S(1)}, u32[]{:S(2)}, u32[]{:S(2)}) collective-permute-start(bf16[128,384]{1,0:T(8,128)(2,1)S(1)} %get-tuple-element.48), channel_id=1, source_target_pairs={{4,8},{12,16},{20,24},{8,4},{16,12},{24,20},{5,9},{13,17},{21,25},... | collective-permute-start | bytes 294920 | tf_op jit(solution)/shard_map/ppermute | solution.py:211
  65.3 0.4 shard_map.63
  65.7 0.0 collective-permute-done.13.refs_5_
  65.7 2.5 %collective-permute-done.14.refs_6_ = bf16[128,384]{1,0:T(8,128)(2,1)S(1)} collective-permute-done((bf16[128,384]{1,0:T(8,128)(2,1)S(1)}, bf16[128,384]{1,0:T(8,128)(2,1)S(1)}, u32[]{:S(2)}, u32[]{:S(2)}) %collective-permute-start.14) | collective-permute-done | bytes 98336 | tf_op jit(solution)/shard_map/ppermute | solution.py:211
  68.3 1.3 %shard_map.64 = f32[384,256]{1,0:T(8,128)} custom-call(f32[384,256]{1,0:T(8,128)S(1)} %get-tuple-element.43.refs_0_, bf16[128,256]{1,0:T(8,128)(2,1)S(1)} %get-tuple-element.44.refs_1_, bf16[128,256]{1,0:T(8,128)(2,1)S(1)} %get-tuple-element.45.refs_2_, bf16[512,512]{1,0:T(8,128)(2,1)S(1)} %get-tuple-element.29.refs_2_.refs_1_.refs_3_, ...), custom_call_target="tpu_custom_call" | custom-call | bytes 1024 | tf_op jit(solution)/shard_map/pallas_call | solution.py:44
Async XLA Ops:
  0.0 5.9 %collective-permute-start = (bf16[384,4096]{1,0:T(8,128)(2,1)}, bf16[384,4096]{1,0:T(8,128)(2,1)S(1)}, u32[]{:S(2)}, u32[]{:S(2)}) collective-permute-start(bf16[384,4096]{1,0:T(8,128)(2,1)} %refs_0_.7), channel_id=1, source_target_pairs={{0,4},{4,0},{8,12},{12,8},{16,20},{20,16},{24,28},{28,24},{1,5},{5... | collective-permute-start | bytes 9437192 | tf_op jit(solution)/shard_map/ppermute | solution.py:34
  0.1 19.0 %collective-permute-start.1 = (bf16[4096,128]{1,0:T(8,128)(2,1)}, bf16[4096,128]{1,0:T(8,128)(2,1)S(1)}, u32[]{:S(2)}, u32[]{:S(2)}) collective-permute-start(bf16[4096,128]{1,0:T(8,128)(2,1)} %refs_2_.1), channel_id=1, source_target_pairs={{0,16},{8,24},{16,0},{24,8},{1,17},{9,25},{17,1},{25,9},{2,18},{10... | collective-permute-start | bytes 3145736 | tf_op jit(solution)/shard_map/ppermute | solution.py:34
  0.8 18.3 %collective-permute-start.2 = (bf16[4096,128]{1,0:T(8,128)(2,1)}, bf16[4096,128]{1,0:T(8,128)(2,1)S(1)}, u32[]{:S(2)}, u32[]{:S(2)}) collective-permute-start(bf16[4096,128]{1,0:T(8,128)(2,1)} %refs_2_.1), channel_id=1, source_target_pairs={{0,8},{8,0},{16,24},{24,16},{1,9},{9,1},{17,25},{25,17},{2,10},{10... | collective-permute-start | bytes 3145736 | tf_op jit(solution)/shard_map/ppermute | solution.py:34
  5.9 1.9 %copy-start = (bf16[384,4096]{1,0:T(8,128)(2,1)S(1)}, bf16[384,4096]{1,0:T(8,128)(2,1)}, u32[]{:S(2)}) copy-start(bf16[384,4096]{1,0:T(8,128)(2,1)} %refs_0_.7) | copy-start | bytes 9437188
  7.8 1.2 %copy-start.2 = (bf16[4096,128]{1,0:T(8,128)(2,1)S(1)}, bf16[4096,128]{1,0:T(8,128)(2,1)}, u32[]{:S(2)}) copy-start(bf16[4096,128]{1,0:T(8,128)(2,1)} %refs_2_.1) | copy-start | bytes 3145732
  9.0 1.8 %copy-start.4 = (bf16[1,512,512]{2,1,0:T(8,128)(2,1)S(1)}, bf16[1,512,512]{2,1,0:T(8,128)(2,1)}, u32[]{:S(2)}) copy-start(bf16[1,512,512]{2,1,0:T(8,128)(2,1)} %refs_0_.5) | copy-start | bytes 1572868
  9.0 1.8 %copy-start.5 = (s32[1,512]{1,0:T(1,128)S(1)}, s32[1,512]{1,0:T(1,128)}, u32[]{:S(2)}) copy-start(s32[1,512]{1,0:T(1,128)} %refs_1_.1) | copy-start | bytes 6148
  9.0 1.8 %copy-start.6 = (s32[128]{0:T(128)S(1)}, s32[128]{0:T(128)}, u32[]{:S(2)}) copy-start(s32[128]{0:T(128)} %param.9) | copy-start | bytes 1540
  9.0 2.5 %copy-start.3 = (bf16[4096,128]{1,0:T(8,128)(2,1)S(1)}, bf16[4096,128]{1,0:T(8,128)(2,1)}, u32[]{:S(2)}) copy-start(bf16[4096,128]{1,0:T(8,128)(2,1)} %refs_2_.1) | copy-start | bytes 3145732
  10.8 28.3 %copy-start.1 = (bf16[384,4096]{1,0:T(8,128)(2,1)S(1)}, bf16[384,4096]{1,0:T(8,128)(2,1)}, u32[]{:S(2)}) copy-start(bf16[384,4096]{1,0:T(8,128)(2,1)} %refs_0_.7) | copy-start | bytes 9437188
  11.5 19.3 %collective-permute-start.5 = (bf16[4096,128]{1,0:T(8,128)(2,1)S(1)}, bf16[4096,128]{1,0:T(8,128)(2,1)S(1)}, u32[]{:S(2)}, u32[]{:S(2)}) collective-permute-start(bf16[4096,128]{1,0:T(8,128)(2,1)S(1)} %copy-done.3), channel_id=1, source_target_pairs={{4,20},{12,28},{20,4},{28,12},{5,21},{13,29},{21,5},{29,13},{6,22}... | collective-permute-start | bytes 3145736 | tf_op jit(solution)/shard_map/ppermute | solution.py:34
  16.0 17.4 %collective-permute-start.6 = (bf16[4096,128]{1,0:T(8,128)(2,1)S(1)}, bf16[4096,128]{1,0:T(8,128)(2,1)S(1)}, u32[]{:S(2)}, u32[]{:S(2)}) collective-permute-start(bf16[4096,128]{1,0:T(8,128)(2,1)S(1)} %copy-done.3), channel_id=1, source_target_pairs={{4,12},{12,4},{20,28},{28,20},{5,13},{13,5},{21,29},{29,21},{6,14}... | collective-permute-start | bytes 3145736 | tf_op jit(solution)/shard_map/ppermute | solution.py:34
  19.5 21.4 %collective-permute-start.3 = (bf16[2688,128]{1,0:T(8,128)(2,1)S(1)}, bf16[2688,128]{1,0:T(8,128)(2,1)S(1)}, u32[]{:S(2)}, u32[]{:S(2)}) collective-permute-start(bf16[2688,128]{1,0:T(8,128)(2,1)S(1)} %get-tuple-element.27), channel_id=1, source_target_pairs={{0,16},{8,24},{16,0},{24,8},{1,17},{9,25},{17,1},{25,9},{2,18},{10... | collective-permute-start | bytes 2064392 | tf_op jit(solution)/shard_map/ppermute | solution.py:34
  33.8 11.8 %collective-permute-start.7 = (bf16[2176,128]{1,0:T(8,128)(2,1)S(1)}, bf16[2176,128]{1,0:T(8,128)(2,1)S(1)}, u32[]{:S(2)}, u32[]{:S(2)}) collective-permute-start(bf16[2176,128]{1,0:T(8,128)(2,1)S(1)} %get-tuple-element.31), channel_id=1, source_target_pairs={{4,20},{12,28},{20,4},{28,12},{5,21},{13,29},{21,5},{29,13},{6,22}... | collective-permute-start | bytes 1671176 | tf_op jit(solution)/shard_map/ppermute | solution.py:34
  35.7 9.9 %collective-permute-start.8 = (bf16[1920,128]{1,0:T(8,128)(2,1)S(1)}, bf16[1920,128]{1,0:T(8,128)(2,1)S(1)}, u32[]{:S(2)}, u32[]{:S(2)}) collective-permute-start(bf16[1920,128]{1,0:T(8,128)(2,1)S(1)} %get-tuple-element.32), channel_id=1, source_target_pairs={{4,12},{12,4},{20,28},{28,20},{5,13},{13,5},{21,29},{29,21},{6,14}... | collective-permute-start | bytes 1474568 | tf_op jit(solution)/shard_map/ppermute | solution.py:34
  38.4 2.5 %collective-permute-start.4 = (bf16[1408,128]{1,0:T(8,128)(2,1)S(1)}, bf16[1408,128]{1,0:T(8,128)(2,1)S(1)}, u32[]{:S(2)}, u32[]{:S(2)}) collective-permute-start(bf16[1408,128]{1,0:T(8,128)(2,1)S(1)} %get-tuple-element.28.refs_2_), channel_id=1, source_target_pairs={{0,8},{8,0},{16,24},{24,16},{1,9},{9,1},{17,25},{25,17},{2,10},{10... | collective-permute-start | bytes 1081352 | tf_op jit(solution)/shard_map/ppermute | solution.py:34
  47.6 6.6 %collective-permute-start.10 = (bf16[768,128]{1,0:T(8,128)(2,1)S(1)}, bf16[768,128]{1,0:T(8,128)(2,1)S(1)}, u32[]{:S(2)}, u32[]{:S(2)}) collective-permute-start(bf16[768,128]{1,0:T(8,128)(2,1)S(1)} %get-tuple-element.37), channel_id=1, source_target_pairs={{0,3},{1,2},{2,1},{3,0},{4,7},{5,6},{6,5},{7,4},{8,11},{9,10},{10,... | collective-permute-start | bytes 589832 | tf_op jit(solution)/shard_map/ppermute | solution.py:34
  50.4 9.3 %collective-permute-start.11 = (bf16[768,128]{1,0:T(8,128)(2,1)S(1)}, bf16[768,128]{1,0:T(8,128)(2,1)S(1)}, u32[]{:S(2)}, u32[]{:S(2)}) collective-permute-start(bf16[768,128]{1,0:T(8,128)(2,1)S(1)} %get-tuple-element.38), channel_id=1, source_target_pairs={{0,2},{1,3},{2,0},{3,1},{4,6},{5,7},{6,4},{7,5},{8,10},{9,11},{10,... | collective-permute-start | bytes 589832 | tf_op jit(solution)/shard_map/ppermute | solution.py:34
  50.4 9.3 %collective-permute-start.9 = (bf16[768,128]{1,0:T(8,128)(2,1)S(1)}, bf16[768,128]{1,0:T(8,128)(2,1)S(1)}, u32[]{:S(2)}, u32[]{:S(2)}) collective-permute-start(bf16[768,128]{1,0:T(8,128)(2,1)S(1)} %get-tuple-element.36), channel_id=1, source_target_pairs={{0,1},{1,0},{2,3},{3,2},{4,5},{5,4},{6,7},{7,6},{8,9},{9,8},{10,11... | collective-permute-start | bytes 589832 | tf_op jit(solution)/shard_map/ppermute | solution.py:34
  59.9 1.5 %collective-permute-start.12 = (f32[384,128]{1,0:T(8,128)S(1)}, f32[384,128]{1,0:T(8,128)S(1)}, u32[]{:S(2)}, u32[]{:S(2)}) collective-permute-start(f32[384,128]{1,0:T(8,128)S(1)} %get-tuple-element.40), channel_id=1, source_target_pairs={{0,4},{4,0},{8,12},{12,8},{16,20},{20,16},{24,28},{28,24},{1,5},{5... | collective-permute-start | bytes 589832 | tf_op jit(solution)/shard_map/ppermute | solution.py:34
  61.7 4.0 %collective-permute-start.13 = (bf16[128,384]{1,0:T(8,128)(2,1)S(1)}, bf16[128,384]{1,0:T(8,128)(2,1)S(1)}, u32[]{:S(2)}, u32[]{:S(2)}) collective-permute-start(bf16[128,384]{1,0:T(8,128)(2,1)S(1)} %get-tuple-element.47), channel_id=1, source_target_pairs={{0,4},{4,0},{8,12},{12,8},{16,20},{20,16},{24,28},{28,24},{1,5},{5... | collective-permute-start | bytes 294920 | tf_op jit(solution)/shard_map/ppermute | solution.py:34
  61.9 6.4 %collective-permute-start.14 = (bf16[128,384]{1,0:T(8,128)(2,1)S(1)}, bf16[128,384]{1,0:T(8,128)(2,1)S(1)}, u32[]{:S(2)}, u32[]{:S(2)}) collective-permute-start(bf16[128,384]{1,0:T(8,128)(2,1)S(1)} %get-tuple-element.48), channel_id=1, source_target_pairs={{4,8},{12,16},{20,24},{8,4},{16,12},{24,20},{5,9},{13,17},{21,25},... | collective-permute-start | bytes 294920 | tf_op jit(solution)/shard_map/ppermute | solution.py:211

commit v13 on v12

--- a/solution.py
+++ b/solution.py
@@ -64,16 +64,10 @@
     return lax.bitwise_xor(lax.div(lax.axis_index("domain"), 2), lax.axis_index("band"))
 
 
-def pieces_kernel(far, near, top, bottom, done):
-    cut, rest = top.shape[0], bottom.shape[0]
-    copies = [
-        pltpu.make_async_copy(near.at[pl.ds(0, cut)], top, done.at[0]),
-        pltpu.make_async_copy(far.at[pl.ds(cut, rest)], bottom, done.at[1]),
-    ]
-    for copy in copies:
-        copy.start()
-    for copy in copies:
-        copy.wait()
+def piece_kernel(start, shard, out, done):
+    copy = pltpu.make_async_copy(shard.at[pl.ds(start, out.shape[0])], out, done)
+    copy.start()
+    copy.wait()
 
 
 def own_kernel(mine, theirs, own, block):
@@ -93,18 +87,31 @@
         far_block[side * rows : (side + 1) * rows] = result[:, width:]
 
 
-def late_kernel(mine, theirs, top_even, bottom_even, top_odd, bottom_odd, own, near, far, kept, *refs):
+def lower_kernel(mine, theirs, bottom_even, bottom_odd, block):
+    rows = mine.shape[0]
+
+    def multiply(bottom):
+        start = mine.shape[1] - bottom.shape[0]
+        for side, states in enumerate((mine, theirs)):
+            result = jnp.dot(states[:, start:], bottom[...], preferred_element_type=F32)
+            block[side * rows : (side + 1) * rows] = result
+
+    pl.when(core() == 0)(lambda: multiply(bottom_even))
+    pl.when(core() != 0)(lambda: multiply(bottom_odd))
+
+
+def late_kernel(mine, theirs, top_even, top_odd, lower, own, near, far, kept, *refs):
     sent, last = refs[:-1], refs[-1]
     rows = mine.shape[0]
 
-    def multiply(top, bottom):
+    def finish(top):
         cut = top.shape[0]
         for side, states in enumerate((mine, theirs)):
-            result = jnp.dot(states[:, :cut], top[...], preferred_element_type=F32)
-            last[side * rows : (side + 1) * rows] = result + jnp.dot(states[:, cut:], bottom[...], preferred_element_type=F32)
-
-    pl.when(core() == 0)(lambda: multiply(top_even, bottom_even))
-    pl.when(core() != 0)(lambda: multiply(top_odd, bottom_odd))
+            span = slice(side * rows, (side + 1) * rows)
+            last[span] = lower[span] + jnp.dot(states[:, :cut], top[...], preferred_element_type=F32)
+
+    pl.when(core() == 0)(lambda: finish(top_even))
+    pl.when(core() != 0)(lambda: finish(top_odd))
     where = block_of_band()
 
     def store(out, slot, block):
@@ -138,18 +145,19 @@
     operator = operator(own)
     later, _ = lax.optimization_barrier((rotation, operator[0]))
     received += [exchanged(later, "domain", NEAR, CORE), exchanged(later, "domain", FAR, CORE)]
-    passed, previous = [], []
-    for one, share in ((0, 21), (CORE, 17)):
+    tops, bottoms, previous = [], [], []
+    for one, share in ((0, 17), (CORE, 13)):
         cut = states * share // 32
-        outs = [shape(count, width, dtype=BF16) for count in (cut, states - cut)]
-        pair = received[2 * one : 2 * one + 2][::-1]
-        top, bottom = call(pieces_kernel, outs, pair, after=previous, scratch=[pltpu.SemaphoreType.DMA((2,))])
-        previous = [bottom]
-        passed += [exchanged(top, "domain", FAR, one), exchanged(bottom, "domain", NEAR, one)]
+        near, far = received[2 * one : 2 * one + 2]
+        for parts, shard, start, count, mask in ((bottoms, far, cut, states - cut, NEAR), (tops, near, 0, cut, FAR)):
+            kernel, outs = functools.partial(piece_kernel, start), [shape(count, width, dtype=BF16)]
+            previous = call(kernel, outs, (shard,), after=previous, scratch=[pltpu.SemaphoreType.DMA])
+            parts.append(exchanged(previous[0], "domain", mask, one))
     early = call(early_kernel, block * 2, (wavefunctions, theirs, *received))
+    lower = call(lower_kernel, block, (wavefunctions, theirs, *bottoms), after=early[:1])[0]
     outs = block + [shape(2 * rows, width, dtype=BF16)] * (bands - 1)
     scratch = [pltpu.VMEM((2 * rows, width), F32)]
-    kept, *sent = call(late_kernel, outs, (wavefunctions, theirs, *passed, own, *early), scratch=scratch)
+    kept, *sent = call(late_kernel, outs, (wavefunctions, theirs, *tops, lower, own, *early), scratch=scratch)
     parts = [exchanged(sent[mask - 1], "band", mask) for mask in (1, *reversed(range(2, bands)))]
     mine, others = call(sum_kernel, [shape(rows, width)] * 2, (kept, *parts))
     return mine, exchanged(others, "domain", CORE), operator

time: 70.3 us -> 77.6 us (1.10)
  waiting for transfers between devices: 34.8 us -> 41.6 us
    ppermute x14, waiting for transfers between devices: 32.3 us -> 38.1 us  [exchanged(): lax.ppermute(value, axis, [(source, source ^ mask) for source in sources...]
    ppermute x14, starting transfers between devices: 18.8 us -> 21 us  [exchanged(): lax.ppermute(value, axis, [(source, source ^ mask) for source in sources...]
    ppermute x1, starting transfers between devices: 3.37 us -> 1.91 us  [finish_square(): lax.ppermute(outward, 'domain', across + [(target, source) for source, ta...]
    ppermute x1, waiting for transfers between devices: 2.53 us -> 3.54 us  [finish_square(): lax.ppermute(outward, 'domain', across + [(target, source) for source, ta...]
    pallas_call x10 -> x13, Pallas kernels: 9.12 us -> 9.28 us  [call(): pl.pallas_call(body, out_shape=outs, in_specs=[pl.BlockSpec(memory_space=...]
  transfers between devices with their start and end apart: 15 -> 15, of which waited for: 8 -> 7; matrix products, arithmetic and copies ran while one was open for 0% -> 0% of each run, Pallas kernels for 8% -> 9%
where the time goes in v13:
time: 77.6 us; the launch traced here: 77.3 us
  waiting for transfers between devices  41.6 us (54%)
  starting transfers between devices  22.9 us (30%)
  Pallas kernels  9.28 us (12%)
  local copies, waits for them, and re-layouts  3.13 us (4%)
    ppermute x14, waiting for transfers between devices, exchanged(): lax.ppermute(value, axis, [(source, source ^ mask) for source in sources...  38.1 us
    ppermute x14, starting transfers between devices, exchanged(): lax.ppermute(value, axis, [(source, source ^ mask) for source in sources...  21 us
    pallas_call x13, Pallas kernels, call(): pl.pallas_call(body, out_shape=outs, in_specs=[pl.BlockSpec(memory_space=...  9.28 us
    ppermute x1, waiting for transfers between devices, finish_square(): lax.ppermute(outward, 'domain', across + [(target, source) for source, ta...  3.54 us
    unnamed x14, local copies, waits for them, and re-layouts  3.13 us
    ppermute x1, starting transfers between devices, finish_square(): lax.ppermute(outward, 'domain', across + [(target, source) for source, ta...  1.91 us
  transfers between devices with their start and end apart: 15, of which 7 were waited for; matrix products, arithmetic and copies ran while one was open for 0% of the time, Pallas kernels for 9%

profile of v13, /device:TPU:1, one launch (start us, length us, event | category | flops | bytes accessed | tf_op | source)
XLA Modules:
  0.0 77.3 jit_solution(7944591978325119827)
XLA Ops:
  0.0 0.1 collective-permute-start
  0.1 0.7 collective-permute-start.1
  0.8 0.7 collective-permute-start.2
  1.5 4.4 %collective-permute-done.refs_1_ = bf16[384,4096]{1,0:T(8,128)(2,1)S(1)} collective-permute-done((bf16[384,4096]{1,0:T(8,128)(2,1)}, bf16[384,4096]{1,0:T(8,128)(2,1)S(1)}, u32[]{:S(2)}, u32[]{:S(2)}) %collective-permute-start) | collective-permute-done | bytes 3145760 | tf_op jit(solution)/shard_map/ppermute | solution.py:34
  5.9 0.0 copy-start
  5.9 1.9 %copy-done = bf16[384,4096]{1,0:T(8,128)(2,1)S(1)} copy-done((bf16[384,4096]{1,0:T(8,128)(2,1)S(1)}, bf16[384,4096]{1,0:T(8,128)(2,1)}, u32[]{:S(2)}) %copy-start) | copy-done | bytes 3145752
  7.8 0.0 copy-start.2
  7.8 1.2 %copy-done.2 = bf16[4096,128]{1,0:T(8,128)(2,1)S(1)} copy-done((bf16[4096,128]{1,0:T(8,128)(2,1)S(1)}, bf16[4096,128]{1,0:T(8,128)(2,1)}, u32[]{:S(2)}) %copy-start.2) | copy-done | bytes 1048600
  9.0 0.0 copy-start.4
  9.0 0.0 copy-start.5
  9.0 0.0 copy-start.6
  9.0 0.0 copy-start.3
  9.0 1.8 %shard_map.57.refs_3_.refs_5_ = f32[768,128]{1,0:T(8,128)S(1)} custom-call(bf16[384,4096]{1,0:T(8,128)(2,1)S(1)} %copy-done, bf16[384,4096]{1,0:T(8,128)(2,1)S(1)} %collective-permute-done.refs_1_, bf16[4096,128]{1,0:T(8,128)(2,1)S(1)} %copy-done.2), custom_call_target="tpu_custom_call" | custom-call | bytes 1024 | tf_op jit(solution)/shard_map/pallas_call | solution.py:44
  10.8 0.0 copy-done.4
  10.8 0.0 copy-done.5
  10.8 0.0 copy-done.6
  10.8 0.7 shard_map.58
  11.5 0.0 copy-done.3
  11.5 4.3 %collective-permute-start.5 = (bf16[4096,128]{1,0:T(8,128)(2,1)S(1)}, bf16[4096,128]{1,0:T(8,128)(2,1)S(1)}, u32[]{:S(2)}, u32[]{:S(2)}) collective-permute-start(bf16[4096,128]{1,0:T(8,128)(2,1)S(1)} %copy-done.3), channel_id=1, source_target_pairs={{4,20},{12,28},{20,4},{28,12},{5,21},{13,29},{21,5},{29,13},{6,22}... | collective-permute-start | bytes 3145736 | tf_op jit(solution)/shard_map/ppermute | solution.py:34
  15.8 3.1 %collective-permute-start.4 = (bf16[4096,128]{1,0:T(8,128)(2,1)S(1)}, bf16[4096,128]{1,0:T(8,128)(2,1)S(1)}, u32[]{:S(2)}, u32[]{:S(2)}) collective-permute-start(bf16[4096,128]{1,0:T(8,128)(2,1)S(1)} %copy-done.3), channel_id=1, source_target_pairs={{4,12},{12,4},{20,28},{28,20},{5,13},{13,5},{21,29},{29,21},{6,14}... | collective-permute-start | bytes 3145736 | tf_op jit(solution)/shard_map/ppermute | solution.py:34
  18.9 0.0 collective-permute-done.2.refs_0_.refs_3_
  19.0 0.3 shard_map.55.refs_1_
  19.3 0.0 copy-start.1
  19.3 0.0 collective-permute-done.1.refs_0_.refs_2_
  19.3 0.1 shard_map.56.refs_1_
  19.4 12.9 %collective-permute-done.5.refs_0_.refs_5_ = bf16[4096,128]{1,0:T(8,128)(2,1)S(1)} collective-permute-done((bf16[4096,128]{1,0:T(8,128)(2,1)S(1)}, bf16[4096,128]{1,0:T(8,128)(2,1)S(1)}, u32[]{:S(2)}, u32[]{:S(2)}) %collective-permute-start.5) | collective-permute-done | bytes 1048608 | tf_op jit(solution)/shard_map/ppermute | solution.py:34
  32.4 0.2 shard_map.59.refs_1_
  32.5 3.1 %collective-permute-start.8 = (bf16[2432,128]{1,0:T(8,128)(2,1)S(1)}, bf16[2432,128]{1,0:T(8,128)(2,1)S(1)}, u32[]{:S(2)}, u32[]{:S(2)}) collective-permute-start(bf16[2432,128]{1,0:T(8,128)(2,1)S(1)} %shard_map.59.refs_1_), channel_id=1, source_target_pairs={{4,12},{12,4},{20,28},{28,20},{5,13},{13,5},{21,29},{29,21},{6,14}... | collective-permute-start | bytes 1867784 | tf_op jit(solution)/shard_map/ppermute | solution.py:34
  35.6 0.7 collective-permute-start.3
  36.3 0.7 collective-permute-start.7
  37.0 0.0 collective-permute-done.4.refs_0_.refs_4_
  37.0 0.2 shard_map.60
  37.3 3.6 %collective-permute-start.6 = (bf16[1664,128]{1,0:T(8,128)(2,1)S(1)}, bf16[1664,128]{1,0:T(8,128)(2,1)S(1)}, u32[]{:S(2)}, u32[]{:S(2)}) collective-permute-start(bf16[1664,128]{1,0:T(8,128)(2,1)S(1)} %shard_map.60), channel_id=1, source_target_pairs={{4,20},{12,28},{20,4},{28,12},{5,21},{13,29},{21,5},{29,13},{6,22}... | collective-permute-start | bytes 1277960 | tf_op jit(solution)/shard_map/ppermute | solution.py:34
  40.9 0.0 copy-done.1
  40.9 1.8 %shard_map.61 = (f32[768,128]{1,0:T(8,128)S(1)}, f32[768,128]{1,0:T(8,128)S(1)}) custom-call(bf16[384,4096]{1,0:T(8,128)(2,1)S(1)} %copy-done.1, bf16[384,4096]{1,0:T(8,128)(2,1)S(1)} %collective-permute-done.refs_1_, bf16[4096,128]{1,0:T(8,128)(2,1)S(1)} %collective-permute-done.1.refs_0_.refs_2_, ...), custom_call_target="tpu_custom_call" | custom-call | bytes 1024 | tf_op jit(solution)/shard_map/pallas_call | solution.py:44
  42.7 0.0 collective-permute-done.7.refs_2_
  42.7 4.8 %collective-permute-done.8.refs_3_ = bf16[2432,128]{1,0:T(8,128)(2,1)S(1)} collective-permute-done((bf16[2432,128]{1,0:T(8,128)(2,1)S(1)}, bf16[2432,128]{1,0:T(8,128)(2,1)S(1)}, u32[]{:S(2)}, u32[]{:S(2)}) %collective-permute-start.8) | collective-permute-done | bytes 622624 | tf_op jit(solution)/shard_map/ppermute | solution.py:34
  47.5 1.1 %shard_map.62.refs_4_ = f32[768,128]{1,0:T(8,128)S(1)} custom-call(bf16[384,4096]{1,0:T(8,128)(2,1)S(1)} %copy-done.1, bf16[384,4096]{1,0:T(8,128)(2,1)S(1)} %collective-permute-done.refs_1_, bf16[1920,128]{1,0:T(8,128)(2,1)S(1)} %collective-permute-done.7.refs_2_, bf16[2432,128]{1,0:T(8,128)(2,1)S(1)} %collective-permute-done.8.refs_3_, ...), custom_call_target="tpu_custom_call" | custom-call | bytes 1024 | tf_op jit(solution)/shard_map/pallas_call | solution.py:44
  48.6 0.0 collective-permute-done.3.refs_2_
  48.6 0.0 collective-permute-done.6.refs_3_
  48.7 1.0 %shard_map.63 = (f32[768,128]{1,0:T(8,128)S(1)}, bf16[768,128]{1,0:T(8,128)(2,1)S(1)}, bf16[768,128]{1,0:T(8,128)(2,1)S(1)}, bf16[768,128]{1,0:T(8,128)(2,1)S(1)}) custom-call(bf16[384,4096]{1,0:T(8,128)(2,1)S(1)} %copy-done.1, bf16[384,4096]{1,0:T(8,128)(2,1)S(1)} %collective-permute-done.refs_1_, bf16[2176,128]{1,0:T(8,128)(2,1)S(1)} %collective-permute-done.3.refs_2_, ...), custom_call_target="tpu_custom_call" | custom-call | bytes 1024 | tf_op jit(solution)/shard_map/pallas_call | solution.py:44
  49.6 3.4 %collective-permute-start.10 = (bf16[768,128]{1,0:T(8,128)(2,1)S(1)}, bf16[768,128]{1,0:T(8,128)(2,1)S(1)}, u32[]{:S(2)}, u32[]{:S(2)}) collective-permute-start(bf16[768,128]{1,0:T(8,128)(2,1)S(1)} %get-tuple-element.29), channel_id=1, source_target_pairs={{0,3},{1,2},{2,1},{3,0},{4,7},{5,6},{6,5},{7,4},{8,11},{9,10},{10,... | collective-permute-start | bytes 589832 | tf_op jit(solution)/shard_map/ppermute | solution.py:34
  53.0 0.0 collective-permute-start.11
  53.0 0.4 collective-permute-start.9
  53.4 4.9 %collective-permute-done.10.refs_2_ = bf16[768,128]{1,0:T(8,128)(2,1)S(1)} collective-permute-done((bf16[768,128]{1,0:T(8,128)(2,1)S(1)}, bf16[768,128]{1,0:T(8,128)(2,1)S(1)}, u32[]{:S(2)}, u32[]{:S(2)}) %collective-permute-start.10) | collective-permute-done | bytes 196640 | tf_op jit(solution)/shard_map/ppermute | solution.py:34
  58.3 9.6 %collective-permute-done.11.refs_3_ = bf16[768,128]{1,0:T(8,128)(2,1)S(1)} collective-permute-done((bf16[768,128]{1,0:T(8,128)(2,1)S(1)}, bf16[768,128]{1,0:T(8,128)(2,1)S(1)}, u32[]{:S(2)}, u32[]{:S(2)}) %collective-permute-start.11) | collective-permute-done | bytes 196640 | tf_op jit(solution)/shard_map/ppermute | solution.py:34
  68.0 0.0 collective-permute-done.9.refs_1_
  68.0 0.1 shard_map.64
  68.1 0.1 collective-permute-start.12
  68.1 1.4 %collective-permute-done.12.refs_1_ = f32[384,128]{1,0:T(8,128)S(1)} collective-permute-done((f32[384,128]{1,0:T(8,128)S(1)}, f32[384,128]{1,0:T(8,128)S(1)}, u32[]{:S(2)}, u32[]{:S(2)}) %collective-permute-start.12) | collective-permute-done | bytes 196640 | tf_op jit(solution)/shard_map/ppermute | solution.py:34
  69.6 0.3 shard_map.65
  69.9 0.2 collective-permute-start.13
  70.1 1.9 %collective-permute-start.14 = (bf16[128,384]{1,0:T(8,128)(2,1)S(1)}, bf16[128,384]{1,0:T(8,128)(2,1)S(1)}, u32[]{:S(2)}, u32[]{:S(2)}) collective-permute-start(bf16[128,384]{1,0:T(8,128)(2,1)S(1)} %get-tuple-element.40), channel_id=1, source_target_pairs={{4,8},{12,16},{20,24},{8,4},{16,12},{24,20},{5,9},{13,17},{21,25},... | collective-permute-start | bytes 294920 | tf_op jit(solution)/shard_map/ppermute | solution.py:219
  72.0 0.5 shard_map.66
  72.5 0.0 collective-permute-done.13.refs_5_
  72.5 3.5 %collective-permute-done.14.refs_6_ = bf16[128,384]{1,0:T(8,128)(2,1)S(1)} collective-permute-done((bf16[128,384]{1,0:T(8,128)(2,1)S(1)}, bf16[128,384]{1,0:T(8,128)(2,1)S(1)}, u32[]{:S(2)}, u32[]{:S(2)}) %collective-permute-start.14) | collective-permute-done | bytes 98336 | tf_op jit(solution)/shard_map/ppermute | solution.py:219
  76.0 1.2 %shard_map.67 = f32[384,256]{1,0:T(8,128)} custom-call(f32[384,256]{1,0:T(8,128)S(1)} %get-tuple-element.35.refs_0_, bf16[128,256]{1,0:T(8,128)(2,1)S(1)} %get-tuple-element.36.refs_1_, bf16[128,256]{1,0:T(8,128)(2,1)S(1)} %get-tuple-element.37.refs_2_, bf16[512,512]{1,0:T(8,128)(2,1)S(1)} %get-tuple-element.23.refs_2_.refs_1_.refs_3_, ...), custom_call_target="tpu_custom_call" | custom-call | bytes 1024 | tf_op jit(solution)/shard_map/pallas_call | solution.py:44
Async XLA Ops:
  0.0 5.9 %collective-permute-start = (bf16[384,4096]{1,0:T(8,128)(2,1)}, bf16[384,4096]{1,0:T(8,128)(2,1)S(1)}, u32[]{:S(2)}, u32[]{:S(2)}) collective-permute-start(bf16[384,4096]{1,0:T(8,128)(2,1)} %refs_0_.9), channel_id=1, source_target_pairs={{0,4},{4,0},{8,12},{12,8},{16,20},{20,16},{24,28},{28,24},{1,5},{5... | collective-permute-start | bytes 9437192 | tf_op jit(solution)/shard_map/ppermute | solution.py:34
  0.1 19.2 %collective-permute-start.1 = (bf16[4096,128]{1,0:T(8,128)(2,1)}, bf16[4096,128]{1,0:T(8,128)(2,1)S(1)}, u32[]{:S(2)}, u32[]{:S(2)}) collective-permute-start(bf16[4096,128]{1,0:T(8,128)(2,1)} %refs_2_.1), channel_id=1, source_target_pairs={{0,8},{8,0},{16,24},{24,16},{1,9},{9,1},{17,25},{25,17},{2,10},{10... | collective-permute-start | bytes 3145736 | tf_op jit(solution)/shard_map/ppermute | solution.py:34
  0.8 18.2 %collective-permute-start.2 = (bf16[4096,128]{1,0:T(8,128)(2,1)}, bf16[4096,128]{1,0:T(8,128)(2,1)S(1)}, u32[]{:S(2)}, u32[]{:S(2)}) collective-permute-start(bf16[4096,128]{1,0:T(8,128)(2,1)} %refs_2_.1), channel_id=1, source_target_pairs={{0,16},{8,24},{16,0},{24,8},{1,17},{9,25},{17,1},{25,9},{2,18},{10... | collective-permute-start | bytes 3145736 | tf_op jit(solution)/shard_map/ppermute | solution.py:34
  5.9 1.9 %copy-start = (bf16[384,4096]{1,0:T(8,128)(2,1)S(1)}, bf16[384,4096]{1,0:T(8,128)(2,1)}, u32[]{:S(2)}) copy-start(bf16[384,4096]{1,0:T(8,128)(2,1)} %refs_0_.9) | copy-start | bytes 9437188
  7.8 1.2 %copy-start.2 = (bf16[4096,128]{1,0:T(8,128)(2,1)S(1)}, bf16[4096,128]{1,0:T(8,128)(2,1)}, u32[]{:S(2)}) copy-start(bf16[4096,128]{1,0:T(8,128)(2,1)} %refs_2_.1) | copy-start | bytes 3145732
  9.0 1.8 %copy-start.4 = (bf16[1,512,512]{2,1,0:T(8,128)(2,1)S(1)}, bf16[1,512,512]{2,1,0:T(8,128)(2,1)}, u32[]{:S(2)}) copy-start(bf16[1,512,512]{2,1,0:T(8,128)(2,1)} %refs_0_.6) | copy-start | bytes 1572868
  9.0 1.8 %copy-start.5 = (s32[1,512]{1,0:T(1,128)S(1)}, s32[1,512]{1,0:T(1,128)}, u32[]{:S(2)}) copy-start(s32[1,512]{1,0:T(1,128)} %refs_1_.1) | copy-start | bytes 6148
  9.0 1.8 %copy-start.6 = (s32[128]{0:T(128)S(1)}, s32[128]{0:T(128)}, u32[]{:S(2)}) copy-start(s32[128]{0:T(128)} %param.9) | copy-start | bytes 1540
  9.0 2.5 %copy-start.3 = (bf16[4096,128]{1,0:T(8,128)(2,1)S(1)}, bf16[4096,128]{1,0:T(8,128)(2,1)}, u32[]{:S(2)}) copy-start(bf16[4096,128]{1,0:T(8,128)(2,1)} %refs_2_.1) | copy-start | bytes 3145732
  11.5 20.8 %collective-permute-start.5 = (bf16[4096,128]{1,0:T(8,128)(2,1)S(1)}, bf16[4096,128]{1,0:T(8,128)(2,1)S(1)}, u32[]{:S(2)}, u32[]{:S(2)}) collective-permute-start(bf16[4096,128]{1,0:T(8,128)(2,1)S(1)} %copy-done.3), channel_id=1, source_target_pairs={{4,20},{12,28},{20,4},{28,12},{5,21},{13,29},{21,5},{29,13},{6,22}... | collective-permute-start | bytes 3145736 | tf_op jit(solution)/shard_map/ppermute | solution.py:34
  15.8 21.2 %collective-permute-start.4 = (bf16[4096,128]{1,0:T(8,128)(2,1)S(1)}, bf16[4096,128]{1,0:T(8,128)(2,1)S(1)}, u32[]{:S(2)}, u32[]{:S(2)}) collective-permute-start(bf16[4096,128]{1,0:T(8,128)(2,1)S(1)} %copy-done.3), channel_id=1, source_target_pairs={{4,12},{12,4},{20,28},{28,20},{5,13},{13,5},{21,29},{29,21},{6,14}... | collective-permute-start | bytes 3145736 | tf_op jit(solution)/shard_map/ppermute | solution.py:34
  19.3 21.6 %copy-start.1 = (bf16[384,4096]{1,0:T(8,128)(2,1)S(1)}, bf16[384,4096]{1,0:T(8,128)(2,1)}, u32[]{:S(2)}) copy-start(bf16[384,4096]{1,0:T(8,128)(2,1)} %refs_0_.9) | copy-start | bytes 9437188
  32.5 15.0 %collective-permute-start.8 = (bf16[2432,128]{1,0:T(8,128)(2,1)S(1)}, bf16[2432,128]{1,0:T(8,128)(2,1)S(1)}, u32[]{:S(2)}, u32[]{:S(2)}) collective-permute-start(bf16[2432,128]{1,0:T(8,128)(2,1)S(1)} %shard_map.59.refs_1_), channel_id=1, source_target_pairs={{4,12},{12,4},{20,28},{28,20},{5,13},{13,5},{21,29},{29,21},{6,14}... | collective-permute-start | bytes 1867784 | tf_op jit(solution)/shard_map/ppermute | solution.py:34
  35.6 13.0 %collective-permute-start.3 = (bf16[2176,128]{1,0:T(8,128)(2,1)S(1)}, bf16[2176,128]{1,0:T(8,128)(2,1)S(1)}, u32[]{:S(2)}, u32[]{:S(2)}) collective-permute-start(bf16[2176,128]{1,0:T(8,128)(2,1)S(1)} %shard_map.56.refs_1_), channel_id=1, source_target_pairs={{0,16},{8,24},{16,0},{24,8},{1,17},{9,25},{17,1},{25,9},{2,18},{10... | collective-permute-start | bytes 1671176 | tf_op jit(solution)/shard_map/ppermute | solution.py:34
  36.3 6.4 %collective-permute-start.7 = (bf16[1920,128]{1,0:T(8,128)(2,1)S(1)}, bf16[1920,128]{1,0:T(8,128)(2,1)S(1)}, u32[]{:S(2)}, u32[]{:S(2)}) collective-permute-start(bf16[1920,128]{1,0:T(8,128)(2,1)S(1)} %shard_map.55.refs_1_), channel_id=1, source_target_pairs={{0,8},{8,0},{16,24},{24,16},{1,9},{9,1},{17,25},{25,17},{2,10},{10... | collective-permute-start | bytes 1474568 | tf_op jit(solution)/shard_map/ppermute | solution.py:34
  37.3 11.4 %collective-permute-start.6 = (bf16[1664,128]{1,0:T(8,128)(2,1)S(1)}, bf16[1664,128]{1,0:T(8,128)(2,1)S(1)}, u32[]{:S(2)}, u32[]{:S(2)}) collective-permute-start(bf16[1664,128]{1,0:T(8,128)(2,1)S(1)} %shard_map.60), channel_id=1, source_target_pairs={{4,20},{12,28},{20,4},{28,12},{5,21},{13,29},{21,5},{29,13},{6,22}... | collective-permute-start | bytes 1277960 | tf_op jit(solution)/shard_map/ppermute | solution.py:34
  49.6 8.7 %collective-permute-start.10 = (bf16[768,128]{1,0:T(8,128)(2,1)S(1)}, bf16[768,128]{1,0:T(8,128)(2,1)S(1)}, u32[]{:S(2)}, u32[]{:S(2)}) collective-permute-start(bf16[768,128]{1,0:T(8,128)(2,1)S(1)} %get-tuple-element.29), channel_id=1, source_target_pairs={{0,3},{1,2},{2,1},{3,0},{4,7},{5,6},{6,5},{7,4},{8,11},{9,10},{10,... | collective-permute-start | bytes 589832 | tf_op jit(solution)/shard_map/ppermute | solution.py:34
  53.0 14.9 %collective-permute-start.11 = (bf16[768,128]{1,0:T(8,128)(2,1)S(1)}, bf16[768,128]{1,0:T(8,128)(2,1)S(1)}, u32[]{:S(2)}, u32[]{:S(2)}) collective-permute-start(bf16[768,128]{1,0:T(8,128)(2,1)S(1)} %get-tuple-element.30), channel_id=1, source_target_pairs={{0,2},{1,3},{2,0},{3,1},{4,6},{5,7},{6,4},{7,5},{8,10},{9,11},{10,... | collective-permute-start | bytes 589832 | tf_op jit(solution)/shard_map/ppermute | solution.py:34
  53.0 14.9 %collective-permute-start.9 = (bf16[768,128]{1,0:T(8,128)(2,1)S(1)}, bf16[768,128]{1,0:T(8,128)(2,1)S(1)}, u32[]{:S(2)}, u32[]{:S(2)}) collective-permute-start(bf16[768,128]{1,0:T(8,128)(2,1)S(1)} %get-tuple-element.28), channel_id=1, source_target_pairs={{0,1},{1,0},{2,3},{3,2},{4,5},{5,4},{6,7},{7,6},{8,9},{9,8},{10,11... | collective-permute-start | bytes 589832 | tf_op jit(solution)/shard_map/ppermute | solution.py:34
  68.1 1.5 %collective-permute-start.12 = (f32[384,128]{1,0:T(8,128)S(1)}, f32[384,128]{1,0:T(8,128)S(1)}, u32[]{:S(2)}, u32[]{:S(2)}) collective-permute-start(f32[384,128]{1,0:T(8,128)S(1)} %get-tuple-element.32), channel_id=1, source_target_pairs={{0,4},{4,0},{8,12},{12,8},{16,20},{20,16},{24,28},{28,24},{1,5},{5... | collective-permute-start | bytes 589832 | tf_op jit(solution)/shard_map/ppermute | solution.py:34
  69.9 2.6 %collective-permute-start.13 = (bf16[128,384]{1,0:T(8,128)(2,1)S(1)}, bf16[128,384]{1,0:T(8,128)(2,1)S(1)}, u32[]{:S(2)}, u32[]{:S(2)}) collective-permute-start(bf16[128,384]{1,0:T(8,128)(2,1)S(1)} %get-tuple-element.39), channel_id=1, source_target_pairs={{0,4},{4,0},{8,12},{12,8},{16,20},{20,16},{24,28},{28,24},{1,5},{5... | collective-permute-start | bytes 294920 | tf_op jit(solution)/shard_map/ppermute | solution.py:34
  70.1 5.9 %collective-permute-start.14 = (bf16[128,384]{1,0:T(8,128)(2,1)S(1)}, bf16[128,384]{1,0:T(8,128)(2,1)S(1)}, u32[]{:S(2)}, u32[]{:S(2)}) collective-permute-start(bf16[128,384]{1,0:T(8,128)(2,1)S(1)} %get-tuple-element.40), channel_id=1, source_target_pairs={{4,8},{12,16},{20,24},{8,4},{16,12},{24,20},{5,9},{13,17},{21,25},... | collective-permute-start | bytes 294920 | tf_op jit(solution)/shard_map/ppermute | solution.py:219

commit v14 on v12

--- a/solution.py
+++ b/solution.py
@@ -31,7 +31,8 @@
 
 def exchanged(value, axis, mask, core=None):
     sources = range(lax.axis_size(axis))
-    return lax.ppermute(value, axis, [(source, source ^ mask) for source in sources if core in (None, source & CORE)])
+    pairs = [(source, source ^ mask if core in (None, source & CORE) else source) for source in sources]
+    return lax.ppermute(value, axis, pairs)
 
 
 def call(kernel, outs, operands, after=(), spaces=None, scratch=()):

time: 70.3 us -> 70.3 us (level)
  starting transfers between devices: 22.2 us -> 24.5 us
  waiting for transfers between devices: 34.8 us -> 32.5 us
    ppermute x14, starting transfers between devices: 18.8 us -> 21.1 us  [exchanged(): return lax.ppermute(value, axis, pairs)]
    ppermute x14, waiting for transfers between devices: 32.3 us -> 30 us  [exchanged(): return lax.ppermute(value, axis, pairs)]
where the time goes in v14:
time: 70.3 us; the launch traced here: 69.5 us
  waiting for transfers between devices  32.5 us (46%)
  starting transfers between devices  24.5 us (35%)
  Pallas kernels  9.12 us (13%)
  local copies, waits for them, and re-layouts  3.13 us (4%)
    ppermute x14, waiting for transfers between devices, exchanged(): return lax.ppermute(value, axis, pairs)  30 us
    ppermute x14, starting transfers between devices, exchanged(): return lax.ppermute(value, axis, pairs)  21.1 us
    pallas_call x10, Pallas kernels, call(): pl.pallas_call(body, out_shape=outs, in_specs=[pl.BlockSpec(memory_space=...  9.12 us
    ppermute x1, starting transfers between devices, finish_square(): lax.ppermute(outward, 'domain', across + [(target, source) for source, ta...  3.37 us
    unnamed x14, local copies, waits for them, and re-layouts  3.13 us
    ppermute x1, waiting for transfers between devices, finish_square(): lax.ppermute(outward, 'domain', across + [(target, source) for source, ta...  2.53 us
  transfers between devices with their start and end apart: 15, of which 8 were waited for; matrix products, arithmetic and copies ran while one was open for 0% of the time, Pallas kernels for 8%

profile of v14, /device:TPU:1, one launch (start us, length us, event | category | flops | bytes accessed | tf_op | source)
XLA Modules:
  0.0 69.5 jit_solution(2136619539020422388)
XLA Ops:
  0.0 0.1 collective-permute-start
  0.1 1.9 %collective-permute-start.1 = (bf16[4096,128]{1,0:T(8,128)(2,1)}, bf16[4096,128]{1,0:T(8,128)(2,1)S(1)}, u32[]{:S(2)}, u32[]{:S(2)}) collective-permute-start(bf16[4096,128]{1,0:T(8,128)(2,1)} %refs_2_.1), channel_id=1, source_target_pairs={{0,16},{4,4},{8,24},{12,12},{16,0},{20,20},{24,8},{28,28},{1,17},{... | collective-permute-start | bytes 3145736 | tf_op jit(solution)/shard_map/ppermute | solution.py:35
  1.9 1.9 %collective-permute-start.2 = (bf16[4096,128]{1,0:T(8,128)(2,1)}, bf16[4096,128]{1,0:T(8,128)(2,1)S(1)}, u32[]{:S(2)}, u32[]{:S(2)}) collective-permute-start(bf16[4096,128]{1,0:T(8,128)(2,1)} %refs_2_.1), channel_id=1, source_target_pairs={{0,8},{4,4},{8,0},{12,12},{16,24},{20,20},{24,16},{28,28},{1,9},{5... | collective-permute-start | bytes 3145736 | tf_op jit(solution)/shard_map/ppermute | solution.py:35
  3.8 2.1 %collective-permute-done.refs_1_ = bf16[384,4096]{1,0:T(8,128)(2,1)S(1)} collective-permute-done((bf16[384,4096]{1,0:T(8,128)(2,1)}, bf16[384,4096]{1,0:T(8,128)(2,1)S(1)}, u32[]{:S(2)}, u32[]{:S(2)}) %collective-permute-start) | collective-permute-done | bytes 3145760 | tf_op jit(solution)/shard_map/ppermute | solution.py:35
  5.9 0.0 copy-start
  5.9 1.9 %copy-done = bf16[384,4096]{1,0:T(8,128)(2,1)S(1)} copy-done((bf16[384,4096]{1,0:T(8,128)(2,1)S(1)}, bf16[384,4096]{1,0:T(8,128)(2,1)}, u32[]{:S(2)}) %copy-start) | copy-done | bytes 3145752
  7.8 0.0 copy-start.2
  7.8 1.2 %copy-done.2 = bf16[4096,128]{1,0:T(8,128)(2,1)S(1)} copy-done((bf16[4096,128]{1,0:T(8,128)(2,1)S(1)}, bf16[4096,128]{1,0:T(8,128)(2,1)}, u32[]{:S(2)}) %copy-start.2) | copy-done | bytes 1048600
  9.0 0.0 copy-start.4
  9.0 0.0 copy-start.5
  9.0 0.0 copy-start.6
  9.0 0.0 copy-start.3
  9.0 1.8 %shard_map.56.refs_3_.refs_6_ = f32[768,128]{1,0:T(8,128)S(1)} custom-call(bf16[384,4096]{1,0:T(8,128)(2,1)S(1)} %copy-done, bf16[384,4096]{1,0:T(8,128)(2,1)S(1)} %collective-permute-done.refs_1_, bf16[4096,128]{1,0:T(8,128)(2,1)S(1)} %copy-done.2), custom_call_target="tpu_custom_call" | custom-call | bytes 1024 | tf_op jit(solution)/shard_map/pallas_call | solution.py:45
  10.8 0.0 copy-start.1
  10.8 0.0 copy-done.4
  10.8 0.0 copy-done.5
  10.8 0.0 copy-done.6
  10.8 0.7 %shard_map.57 = (bf16[512,512]{1,0:T(8,128)(2,1)S(1)}, bf16[128,384]{1,0:T(8,128)(2,1)S(1)}, bf16[384,128]{1,0:T(8,128)(2,1)S(1)}) custom-call(bf16[1,512,512]{2,1,0:T(8,128)(2,1)S(1)} %copy-done.4, s32[1,512]{1,0:T(1,128)S(1)} %copy-done.5, s32[1,128]{1,0:T(1,128)S(1)} %bitcast.1, f32[768,128]{1,0:T(8,128)S(1)} %shard_map.56.refs_3_.refs_6_), custom_call_target="tpu_custom_call" | custom-call | bytes 1024 | tf_op jit(solution)/shard_map/pallas_call | solution.py:45
  11.5 0.0 copy-done.3
  11.5 4.4 %collective-permute-start.5 = (bf16[4096,128]{1,0:T(8,128)(2,1)S(1)}, bf16[4096,128]{1,0:T(8,128)(2,1)S(1)}, u32[]{:S(2)}, u32[]{:S(2)}) collective-permute-start(bf16[4096,128]{1,0:T(8,128)(2,1)S(1)} %copy-done.3), channel_id=1, source_target_pairs={{0,0},{4,20},{8,8},{12,28},{16,16},{20,4},{24,24},{28,12},{1,1},{5... | collective-permute-start | bytes 3145736 | tf_op jit(solution)/shard_map/ppermute | solution.py:35
  16.0 3.1 %collective-permute-start.6 = (bf16[4096,128]{1,0:T(8,128)(2,1)S(1)}, bf16[4096,128]{1,0:T(8,128)(2,1)S(1)}, u32[]{:S(2)}, u32[]{:S(2)}) collective-permute-start(bf16[4096,128]{1,0:T(8,128)(2,1)S(1)} %copy-done.3), channel_id=1, source_target_pairs={{0,0},{4,12},{8,8},{12,4},{16,16},{20,28},{24,24},{28,20},{1,1},{5... | collective-permute-start | bytes 3145736 | tf_op jit(solution)/shard_map/ppermute | solution.py:35
  19.1 0.0 collective-permute-done.1.refs_0_.refs_3_
  19.1 0.0 collective-permute-done.2.refs_1_.refs_2_
  19.1 0.4 shard_map.55
  19.5 0.7 %collective-permute-start.3 = (bf16[2688,128]{1,0:T(8,128)(2,1)S(1)}, bf16[2688,128]{1,0:T(8,128)(2,1)S(1)}, u32[]{:S(2)}, u32[]{:S(2)}) collective-permute-start(bf16[2688,128]{1,0:T(8,128)(2,1)S(1)} %get-tuple-element.27), channel_id=1, source_target_pairs={{0,16},{4,4},{8,24},{12,12},{16,0},{20,20},{24,8},{28,28},{1,17},{... | collective-permute-start | bytes 2064392 | tf_op jit(solution)/shard_map/ppermute | solution.py:35
  20.2 10.6 %collective-permute-done.5.refs_0_.refs_5_ = bf16[4096,128]{1,0:T(8,128)(2,1)S(1)} collective-permute-done((bf16[4096,128]{1,0:T(8,128)(2,1)S(1)}, bf16[4096,128]{1,0:T(8,128)(2,1)S(1)}, u32[]{:S(2)}, u32[]{:S(2)}) %collective-permute-start.5) | collective-permute-done | bytes 1048608 | tf_op jit(solution)/shard_map/ppermute | solution.py:35
  30.8 2.5 %collective-permute-done.6.refs_1_.refs_4_ = bf16[4096,128]{1,0:T(8,128)(2,1)S(1)} collective-permute-done((bf16[4096,128]{1,0:T(8,128)(2,1)S(1)}, bf16[4096,128]{1,0:T(8,128)(2,1)S(1)}, u32[]{:S(2)}, u32[]{:S(2)}) %collective-permute-start.6) | collective-permute-done | bytes 1048608 | tf_op jit(solution)/shard_map/ppermute | solution.py:35
  33.4 0.4 shard_map.58
  33.8 1.9 %collective-permute-start.7 = (bf16[2176,128]{1,0:T(8,128)(2,1)S(1)}, bf16[2176,128]{1,0:T(8,128)(2,1)S(1)}, u32[]{:S(2)}, u32[]{:S(2)}) collective-permute-start(bf16[2176,128]{1,0:T(8,128)(2,1)S(1)} %get-tuple-element.31), channel_id=1, source_target_pairs={{0,0},{4,20},{8,8},{12,28},{16,16},{20,4},{24,24},{28,12},{1,1},{5... | collective-permute-start | bytes 1671176 | tf_op jit(solution)/shard_map/ppermute | solution.py:35
  35.7 2.6 %collective-permute-start.8 = (bf16[1920,128]{1,0:T(8,128)(2,1)S(1)}, bf16[1920,128]{1,0:T(8,128)(2,1)S(1)}, u32[]{:S(2)}, u32[]{:S(2)}) collective-permute-start(bf16[1920,128]{1,0:T(8,128)(2,1)S(1)} %get-tuple-element.32), channel_id=1, source_target_pairs={{0,0},{4,12},{8,8},{12,4},{16,16},{20,28},{24,24},{28,20},{1,1},{5... | collective-permute-start | bytes 1474568 | tf_op jit(solution)/shard_map/ppermute | solution.py:35
  38.4 0.7 collective-permute-start.4
  39.1 0.0 copy-done.1
  39.1 1.8 %shard_map.59 = (f32[768,128]{1,0:T(8,128)S(1)}, f32[768,128]{1,0:T(8,128)S(1)}) custom-call(bf16[384,4096]{1,0:T(8,128)(2,1)S(1)} %copy-done.1, bf16[384,4096]{1,0:T(8,128)(2,1)S(1)} %collective-permute-done.refs_1_, bf16[4096,128]{1,0:T(8,128)(2,1)S(1)} %collective-permute-done.2.refs_1_.refs_2_, ...), custom_call_target="tpu_custom_call" | custom-call | bytes 1024 | tf_op jit(solution)/shard_map/pallas_call | solution.py:45
  40.9 0.0 collective-permute-done.4.refs_3_
  40.9 0.0 collective-permute-done.3.refs_2_
  40.9 4.7 %collective-permute-done.8.refs_5_ = bf16[1920,128]{1,0:T(8,128)(2,1)S(1)} collective-permute-done((bf16[1920,128]{1,0:T(8,128)(2,1)S(1)}, bf16[1920,128]{1,0:T(8,128)(2,1)S(1)}, u32[]{:S(2)}, u32[]{:S(2)}) %collective-permute-start.8) | collective-permute-done | bytes 491552 | tf_op jit(solution)/shard_map/ppermute | solution.py:35
  45.6 0.0 collective-permute-done.7.refs_4_
  45.6 1.9 %shard_map.60 = (f32[768,128]{1,0:T(8,128)S(1)}, bf16[768,128]{1,0:T(8,128)(2,1)S(1)}, bf16[768,128]{1,0:T(8,128)(2,1)S(1)}, bf16[768,128]{1,0:T(8,128)(2,1)S(1)}) custom-call(bf16[384,4096]{1,0:T(8,128)(2,1)S(1)} %copy-done.1, bf16[384,4096]{1,0:T(8,128)(2,1)S(1)} %collective-permute-done.refs_1_, bf16[2688,128]{1,0:T(8,128)(2,1)S(1)} %collective-permute-done.3.refs_2_, ...), custom_call_target="tpu_custom_call" | custom-call | bytes 1024 | tf_op jit(solution)/shard_map/pallas_call | solution.py:45
  47.6 2.9 %collective-permute-start.10 = (bf16[768,128]{1,0:T(8,128)(2,1)S(1)}, bf16[768,128]{1,0:T(8,128)(2,1)S(1)}, u32[]{:S(2)}, u32[]{:S(2)}) collective-permute-start(bf16[768,128]{1,0:T(8,128)(2,1)S(1)} %get-tuple-element.37), channel_id=1, source_target_pairs={{0,3},{1,2},{2,1},{3,0},{4,7},{5,6},{6,5},{7,4},{8,11},{9,10},{10,... | collective-permute-start | bytes 589832 | tf_op jit(solution)/shard_map/ppermute | solution.py:35
  50.4 0.0 collective-permute-start.11
  50.4 0.7 %collective-permute-start.9 = (bf16[768,128]{1,0:T(8,128)(2,1)S(1)}, bf16[768,128]{1,0:T(8,128)(2,1)S(1)}, u32[]{:S(2)}, u32[]{:S(2)}) collective-permute-start(bf16[768,128]{1,0:T(8,128)(2,1)S(1)} %get-tuple-element.36), channel_id=1, source_target_pairs={{0,1},{1,0},{2,3},{3,2},{4,5},{5,4},{6,7},{7,6},{8,9},{9,8},{10,11... | collective-permute-start | bytes 589832 | tf_op jit(solution)/shard_map/ppermute | solution.py:35
  51.2 3.0 %collective-permute-done.10.refs_2_ = bf16[768,128]{1,0:T(8,128)(2,1)S(1)} collective-permute-done((bf16[768,128]{1,0:T(8,128)(2,1)S(1)}, bf16[768,128]{1,0:T(8,128)(2,1)S(1)}, u32[]{:S(2)}, u32[]{:S(2)}) %collective-permute-start.10) | collective-permute-done | bytes 196640 | tf_op jit(solution)/shard_map/ppermute | solution.py:35
  54.1 5.6 %collective-permute-done.11.refs_3_ = bf16[768,128]{1,0:T(8,128)(2,1)S(1)} collective-permute-done((bf16[768,128]{1,0:T(8,128)(2,1)S(1)}, bf16[768,128]{1,0:T(8,128)(2,1)S(1)}, u32[]{:S(2)}, u32[]{:S(2)}) %collective-permute-start.11) | collective-permute-done | bytes 196640 | tf_op jit(solution)/shard_map/ppermute | solution.py:35
  59.8 0.0 collective-permute-done.9.refs_1_
  59.8 0.1 shard_map.61
  59.9 0.1 collective-permute-start.12
  60.0 1.4 %collective-permute-done.12.refs_1_ = f32[384,128]{1,0:T(8,128)S(1)} collective-permute-done((f32[384,128]{1,0:T(8,128)S(1)}, f32[384,128]{1,0:T(8,128)S(1)}, u32[]{:S(2)}, u32[]{:S(2)}) %collective-permute-start.12) | collective-permute-done | bytes 196640 | tf_op jit(solution)/shard_map/ppermute | solution.py:35
  61.4 0.3 shard_map.62
  61.7 0.2 collective-permute-start.13
  61.9 3.4 %collective-permute-start.14 = (bf16[128,384]{1,0:T(8,128)(2,1)S(1)}, bf16[128,384]{1,0:T(8,128)(2,1)S(1)}, u32[]{:S(2)}, u32[]{:S(2)}) collective-permute-start(bf16[128,384]{1,0:T(8,128)(2,1)S(1)} %get-tuple-element.48), channel_id=1, source_target_pairs={{4,8},{12,16},{20,24},{8,4},{16,12},{24,20},{5,9},{13,17},{21,25},... | collective-permute-start | bytes 294920 | tf_op jit(solution)/shard_map/ppermute | solution.py:212
  65.3 0.4 shard_map.63
  65.7 0.0 collective-permute-done.13.refs_5_
  65.7 2.5 %collective-permute-done.14.refs_6_ = bf16[128,384]{1,0:T(8,128)(2,1)S(1)} collective-permute-done((bf16[128,384]{1,0:T(8,128)(2,1)S(1)}, bf16[128,384]{1,0:T(8,128)(2,1)S(1)}, u32[]{:S(2)}, u32[]{:S(2)}) %collective-permute-start.14) | collective-permute-done | bytes 98336 | tf_op jit(solution)/shard_map/ppermute | solution.py:212
  68.3 1.3 %shard_map.64 = f32[384,256]{1,0:T(8,128)} custom-call(f32[384,256]{1,0:T(8,128)S(1)} %get-tuple-element.43.refs_0_, bf16[128,256]{1,0:T(8,128)(2,1)S(1)} %get-tuple-element.44.refs_1_, bf16[128,256]{1,0:T(8,128)(2,1)S(1)} %get-tuple-element.45.refs_2_, bf16[512,512]{1,0:T(8,128)(2,1)S(1)} %get-tuple-element.29.refs_2_.refs_1_.refs_3_, ...), custom_call_target="tpu_custom_call" | custom-call | bytes 1024 | tf_op jit(solution)/shard_map/pallas_call | solution.py:45
Async XLA Ops:
  0.0 5.9 %collective-permute-start = (bf16[384,4096]{1,0:T(8,128)(2,1)}, bf16[384,4096]{1,0:T(8,128)(2,1)S(1)}, u32[]{:S(2)}, u32[]{:S(2)}) collective-permute-start(bf16[384,4096]{1,0:T(8,128)(2,1)} %refs_0_.7), channel_id=1, source_target_pairs={{0,4},{4,0},{8,12},{12,8},{16,20},{20,16},{24,28},{28,24},{1,5},{5... | collective-permute-start | bytes 9437192 | tf_op jit(solution)/shard_map/ppermute | solution.py:35
  0.1 19.0 %collective-permute-start.1 = (bf16[4096,128]{1,0:T(8,128)(2,1)}, bf16[4096,128]{1,0:T(8,128)(2,1)S(1)}, u32[]{:S(2)}, u32[]{:S(2)}) collective-permute-start(bf16[4096,128]{1,0:T(8,128)(2,1)} %refs_2_.1), channel_id=1, source_target_pairs={{0,16},{4,4},{8,24},{12,12},{16,0},{20,20},{24,8},{28,28},{1,17},{... | collective-permute-start | bytes 3145736 | tf_op jit(solution)/shard_map/ppermute | solution.py:35
  1.9 17.2 %collective-permute-start.2 = (bf16[4096,128]{1,0:T(8,128)(2,1)}, bf16[4096,128]{1,0:T(8,128)(2,1)S(1)}, u32[]{:S(2)}, u32[]{:S(2)}) collective-permute-start(bf16[4096,128]{1,0:T(8,128)(2,1)} %refs_2_.1), channel_id=1, source_target_pairs={{0,8},{4,4},{8,0},{12,12},{16,24},{20,20},{24,16},{28,28},{1,9},{5... | collective-permute-start | bytes 3145736 | tf_op jit(solution)/shard_map/ppermute | solution.py:35
  5.9 1.9 %copy-start = (bf16[384,4096]{1,0:T(8,128)(2,1)S(1)}, bf16[384,4096]{1,0:T(8,128)(2,1)}, u32[]{:S(2)}) copy-start(bf16[384,4096]{1,0:T(8,128)(2,1)} %refs_0_.7) | copy-start | bytes 9437188
  7.8 1.2 %copy-start.2 = (bf16[4096,128]{1,0:T(8,128)(2,1)S(1)}, bf16[4096,128]{1,0:T(8,128)(2,1)}, u32[]{:S(2)}) copy-start(bf16[4096,128]{1,0:T(8,128)(2,1)} %refs_2_.1) | copy-start | bytes 3145732
  9.0 1.8 %copy-start.4 = (bf16[1,512,512]{2,1,0:T(8,128)(2,1)S(1)}, bf16[1,512,512]{2,1,0:T(8,128)(2,1)}, u32[]{:S(2)}) copy-start(bf16[1,512,512]{2,1,0:T(8,128)(2,1)} %refs_0_.5) | copy-start | bytes 1572868
  9.0 1.8 %copy-start.5 = (s32[1,512]{1,0:T(1,128)S(1)}, s32[1,512]{1,0:T(1,128)}, u32[]{:S(2)}) copy-start(s32[1,512]{1,0:T(1,128)} %refs_1_.1) | copy-start | bytes 6148
  9.0 1.8 %copy-start.6 = (s32[128]{0:T(128)S(1)}, s32[128]{0:T(128)}, u32[]{:S(2)}) copy-start(s32[128]{0:T(128)} %param.9) | copy-start | bytes 1540
  9.0 2.5 %copy-start.3 = (bf16[4096,128]{1,0:T(8,128)(2,1)S(1)}, bf16[4096,128]{1,0:T(8,128)(2,1)}, u32[]{:S(2)}) copy-start(bf16[4096,128]{1,0:T(8,128)(2,1)} %refs_2_.1) | copy-start | bytes 3145732
  10.8 28.3 %copy-start.1 = (bf16[384,4096]{1,0:T(8,128)(2,1)S(1)}, bf16[384,4096]{1,0:T(8,128)(2,1)}, u32[]{:S(2)}) copy-start(bf16[384,4096]{1,0:T(8,128)(2,1)} %refs_0_.7) | copy-start | bytes 9437188
  11.5 19.3 %collective-permute-start.5 = (bf16[4096,128]{1,0:T(8,128)(2,1)S(1)}, bf16[4096,128]{1,0:T(8,128)(2,1)S(1)}, u32[]{:S(2)}, u32[]{:S(2)}) collective-permute-start(bf16[4096,128]{1,0:T(8,128)(2,1)S(1)} %copy-done.3), channel_id=1, source_target_pairs={{0,0},{4,20},{8,8},{12,28},{16,16},{20,4},{24,24},{28,12},{1,1},{5... | collective-permute-start | bytes 3145736 | tf_op jit(solution)/shard_map/ppermute | solution.py:35
  16.0 17.4 %collective-permute-start.6 = (bf16[4096,128]{1,0:T(8,128)(2,1)S(1)}, bf16[4096,128]{1,0:T(8,128)(2,1)S(1)}, u32[]{:S(2)}, u32[]{:S(2)}) collective-permute-start(bf16[4096,128]{1,0:T(8,128)(2,1)S(1)} %copy-done.3), channel_id=1, source_target_pairs={{0,0},{4,12},{8,8},{12,4},{16,16},{20,28},{24,24},{28,20},{1,1},{5... | collective-permute-start | bytes 3145736 | tf_op jit(solution)/shard_map/ppermute | solution.py:35
  19.5 21.4 %collective-permute-start.3 = (bf16[2688,128]{1,0:T(8,128)(2,1)S(1)}, bf16[2688,128]{1,0:T(8,128)(2,1)S(1)}, u32[]{:S(2)}, u32[]{:S(2)}) collective-permute-start(bf16[2688,128]{1,0:T(8,128)(2,1)S(1)} %get-tuple-element.27), channel_id=1, source_target_pairs={{0,16},{4,4},{8,24},{12,12},{16,0},{20,20},{24,8},{28,28},{1,17},{... | collective-permute-start | bytes 2064392 | tf_op jit(solution)/shard_map/ppermute | solution.py:35
  33.8 11.8 %collective-permute-start.7 = (bf16[2176,128]{1,0:T(8,128)(2,1)S(1)}, bf16[2176,128]{1,0:T(8,128)(2,1)S(1)}, u32[]{:S(2)}, u32[]{:S(2)}) collective-permute-start(bf16[2176,128]{1,0:T(8,128)(2,1)S(1)} %get-tuple-element.31), channel_id=1, source_target_pairs={{0,0},{4,20},{8,8},{12,28},{16,16},{20,4},{24,24},{28,12},{1,1},{5... | collective-permute-start | bytes 1671176 | tf_op jit(solution)/shard_map/ppermute | solution.py:35
  35.7 9.9 %collective-permute-start.8 = (bf16[1920,128]{1,0:T(8,128)(2,1)S(1)}, bf16[1920,128]{1,0:T(8,128)(2,1)S(1)}, u32[]{:S(2)}, u32[]{:S(2)}) collective-permute-start(bf16[1920,128]{1,0:T(8,128)(2,1)S(1)} %get-tuple-element.32), channel_id=1, source_target_pairs={{0,0},{4,12},{8,8},{12,4},{16,16},{20,28},{24,24},{28,20},{1,1},{5... | collective-permute-start | bytes 1474568 | tf_op jit(solution)/shard_map/ppermute | solution.py:35
  38.4 2.5 %collective-permute-start.4 = (bf16[1408,128]{1,0:T(8,128)(2,1)S(1)}, bf16[1408,128]{1,0:T(8,128)(2,1)S(1)}, u32[]{:S(2)}, u32[]{:S(2)}) collective-permute-start(bf16[1408,128]{1,0:T(8,128)(2,1)S(1)} %get-tuple-element.28.refs_2_), channel_id=1, source_target_pairs={{0,8},{4,4},{8,0},{12,12},{16,24},{20,20},{24,16},{28,28},{1,9},{5... | collective-permute-start | bytes 1081352 | tf_op jit(solution)/shard_map/ppermute | solution.py:35
  47.6 6.6 %collective-permute-start.10 = (bf16[768,128]{1,0:T(8,128)(2,1)S(1)}, bf16[768,128]{1,0:T(8,128)(2,1)S(1)}, u32[]{:S(2)}, u32[]{:S(2)}) collective-permute-start(bf16[768,128]{1,0:T(8,128)(2,1)S(1)} %get-tuple-element.37), channel_id=1, source_target_pairs={{0,3},{1,2},{2,1},{3,0},{4,7},{5,6},{6,5},{7,4},{8,11},{9,10},{10,... | collective-permute-start | bytes 589832 | tf_op jit(solution)/shard_map/ppermute | solution.py:35
  50.4 9.3 %collective-permute-start.11 = (bf16[768,128]{1,0:T(8,128)(2,1)S(1)}, bf16[768,128]{1,0:T(8,128)(2,1)S(1)}, u32[]{:S(2)}, u32[]{:S(2)}) collective-permute-start(bf16[768,128]{1,0:T(8,128)(2,1)S(1)} %get-tuple-element.38), channel_id=1, source_target_pairs={{0,2},{1,3},{2,0},{3,1},{4,6},{5,7},{6,4},{7,5},{8,10},{9,11},{10,... | collective-permute-start | bytes 589832 | tf_op jit(solution)/shard_map/ppermute | solution.py:35
  50.4 9.3 %collective-permute-start.9 = (bf16[768,128]{1,0:T(8,128)(2,1)S(1)}, bf16[768,128]{1,0:T(8,128)(2,1)S(1)}, u32[]{:S(2)}, u32[]{:S(2)}) collective-permute-start(bf16[768,128]{1,0:T(8,128)(2,1)S(1)} %get-tuple-element.36), channel_id=1, source_target_pairs={{0,1},{1,0},{2,3},{3,2},{4,5},{5,4},{6,7},{7,6},{8,9},{9,8},{10,11... | collective-permute-start | bytes 589832 | tf_op jit(solution)/shard_map/ppermute | solution.py:35
  59.9 1.5 %collective-permute-start.12 = (f32[384,128]{1,0:T(8,128)S(1)}, f32[384,128]{1,0:T(8,128)S(1)}, u32[]{:S(2)}, u32[]{:S(2)}) collective-permute-start(f32[384,128]{1,0:T(8,128)S(1)} %get-tuple-element.40), channel_id=1, source_target_pairs={{0,4},{4,0},{8,12},{12,8},{16,20},{20,16},{24,28},{28,24},{1,5},{5... | collective-permute-start | bytes 589832 | tf_op jit(solution)/shard_map/ppermute | solution.py:35
  61.7 4.0 %collective-permute-start.13 = (bf16[128,384]{1,0:T(8,128)(2,1)S(1)}, bf16[128,384]{1,0:T(8,128)(2,1)S(1)}, u32[]{:S(2)}, u32[]{:S(2)}) collective-permute-start(bf16[128,384]{1,0:T(8,128)(2,1)S(1)} %get-tuple-element.47), channel_id=1, source_target_pairs={{0,4},{4,0},{8,12},{12,8},{16,20},{20,16},{24,28},{28,24},{1,5},{5... | collective-permute-start | bytes 294920 | tf_op jit(solution)/shard_map/ppermute | solution.py:35
  61.9 6.4 %collective-permute-start.14 = (bf16[128,384]{1,0:T(8,128)(2,1)S(1)}, bf16[128,384]{1,0:T(8,128)(2,1)S(1)}, u32[]{:S(2)}, u32[]{:S(2)}) collective-permute-start(bf16[128,384]{1,0:T(8,128)(2,1)S(1)} %get-tuple-element.48), channel_id=1, source_target_pairs={{4,8},{12,16},{20,24},{8,4},{16,12},{24,20},{5,9},{13,17},{21,25},... | collective-permute-start | bytes 294920 | tf_op jit(solution)/shard_map/ppermute | solution.py:212

commit v15 on v12

--- a/solution.py
+++ b/solution.py
@@ -64,16 +64,19 @@
     return lax.bitwise_xor(lax.div(lax.axis_index("domain"), 2), lax.axis_index("band"))
 
 
-def pieces_kernel(far, near, top, bottom, done):
+def pieces_kernel(one, far, near, top, bottom, done):
     cut, rest = top.shape[0], bottom.shape[0]
-    copies = [
-        pltpu.make_async_copy(near.at[pl.ds(0, cut)], top, done.at[0]),
-        pltpu.make_async_copy(far.at[pl.ds(cut, rest)], bottom, done.at[1]),
-    ]
-    for copy in copies:
-        copy.start()
-    for copy in copies:
-        copy.wait()
+
+    @pl.when(core() == one)
+    def _():
+        copies = [
+            pltpu.make_async_copy(near.at[pl.ds(0, cut)], top, done.at[0]),
+            pltpu.make_async_copy(far.at[pl.ds(cut, rest)], bottom, done.at[1]),
+        ]
+        for copy in copies:
+            copy.start()
+        for copy in copies:
+            copy.wait()
 
 
 def own_kernel(mine, theirs, own, block):
@@ -139,11 +142,12 @@
     later, _ = lax.optimization_barrier((rotation, operator[0]))
     received += [exchanged(later, "domain", NEAR, CORE), exchanged(later, "domain", FAR, CORE)]
     passed, previous = [], []
-    for one, share in ((0, 21), (CORE, 17)):
+    for one, share in ((0, 21), (CORE, 19)):
         cut = states * share // 32
         outs = [shape(count, width, dtype=BF16) for count in (cut, states - cut)]
         pair = received[2 * one : 2 * one + 2][::-1]
-        top, bottom = call(pieces_kernel, outs, pair, after=previous, scratch=[pltpu.SemaphoreType.DMA((2,))])
+        kernel = functools.partial(pieces_kernel, one)
+        top, bottom = call(kernel, outs, pair, after=previous, scratch=[pltpu.SemaphoreType.DMA((2,))])
         previous = [bottom]
         passed += [exchanged(top, "domain", FAR, one), exchanged(bottom, "domain", NEAR, one)]
     early = call(early_kernel, block * 2, (wavefunctions, theirs, *received))
@@ -181,24 +185,24 @@
     pl.when(jnp.logical_not(first))(lambda: store(outward, inward))
 
 
-def inner_kernel(total, assembled, pick, out, face_high, face_low):
-    own = total.shape[0]
+def inner_kernel(total, assembled, pick, out, faces):
+    own, columns = total.shape
     high, low = split(total[...])
     inner = assembled[:own, :own]
     out[...] = dot(inner, high) + dot(inner, low)
-    face_high[...] = dot(pick[...], high).astype(BF16)
-    face_low[...] = dot(pick[...], low).astype(BF16)
-
-
-def final_kernel(inner, face_high, face_low, assembled, spread, inward, outward, out):
+    faces[:, :columns] = dot(pick[...], high).astype(BF16)
+    faces[:, columns:] = dot(pick[...], low).astype(BF16)
+
+
+def final_kernel(inner, faces, assembled, spread, inward, outward, out):
     own, columns = inner.shape
     first = core() == 0
     incoming = jnp.where(first, inward[:, :columns], outward[:, :columns])
     back = jnp.where(first, outward[...], inward[...])
-    corner = back[:, columns:]
-    value = back[:, :columns].astype(F32) + dot(corner, face_high[...]) + dot(corner, face_low[...])
-    high, low = split(value)
-    out[...] = inner[...] + dot(assembled[:own, own:], incoming) + dot(spread[...], high) + dot(spread[...], low)
+    extra = dot(back[:, columns:], faces[...])
+    high, low = split(back[:, :columns].astype(F32) + extra[:, :columns] + extra[:, columns:])
+    matrix = jnp.concatenate([assembled[:own, own:], spread[...], spread[...]], 1)
+    out[...] = inner[...] + dot(matrix, jnp.concatenate([incoming, high, low], 0))
 
 
 def finish_square(mine, other, operator):
@@ -210,9 +214,9 @@
     across = [(place, place + 1) for place in range(CORE, lax.axis_size("domain") - 1, 2)]
     outward = lax.ppermute(outward, "domain", across + [(target, source) for source, target in across])
     inward = exchanged(inward, "domain", CORE)
-    outs = [shape(rows, columns)] + [shape(shared, columns, dtype=BF16)] * 2
-    inner, *face = call(inner_kernel, outs, (total, assembled, pick))
-    return call(final_kernel, outs[:1], (inner, *face, assembled, spread, inward, outward))[0]
+    outs = [shape(rows, columns), shape(shared, 2 * columns, dtype=BF16)]
+    inner, faces = call(inner_kernel, outs, (total, assembled, pick))
+    return call(final_kernel, outs[:1], (inner, faces, assembled, spread, inward, outward))[0]
 
 
 def finish_any(rotated, cell_matrices, cell_nodes, face_map):

time: 70.3 us -> 70.2 us (level)
  transfers between devices with their start and end apart: 15 -> 15, of which waited for: 8 -> 9; matrix products, arithmetic and copies ran while one was open for 0% -> 0% of each run, Pallas kernels for 8% -> 7%
where the time goes in v15:
time: 70.2 us; the launch traced here: 69.5 us
  waiting for transfers between devices  35.2 us (50%)
  starting transfers between devices  22.2 us (32%)
  Pallas kernels  8.7 us (12%)
  local copies, waits for them, and re-layouts  3.13 us (4%)
    ppermute x14, waiting for transfers between devices, exchanged(): lax.ppermute(value, axis, [(source, source ^ mask) for source in sources...  32.7 us
    ppermute x14, starting transfers between devices, exchanged(): lax.ppermute(value, axis, [(source, source ^ mask) for source in sources...  18.8 us
    pallas_call x10, Pallas kernels, call(): pl.pallas_call(body, out_shape=outs, in_specs=[pl.BlockSpec(memory_space=...  8.7 us
    ppermute x1, starting transfers between devices, finish_square(): lax.ppermute(outward, 'domain', across + [(target, source) for source, ta...  3.37 us
    unnamed x14, local copies, waits for them, and re-layouts  3.13 us
    ppermute x1, waiting for transfers between devices, finish_square(): lax.ppermute(outward, 'domain', across + [(target, source) for source, ta...  2.53 us
  transfers between devices with their start and end apart: 15, of which 9 were waited for; matrix products, arithmetic and copies ran while one was open for 0% of the time, Pallas kernels for 7%

profile of v15, /device:TPU:1, one launch (start us, length us, event | category | flops | bytes accessed | tf_op | source)
XLA Modules:
  0.0 69.5 jit_solution(7649997993228687824)
XLA Ops:
  0.0 0.1 collective-permute-start
  0.1 0.7 %collective-permute-start.1 = (bf16[4096,128]{1,0:T(8,128)(2,1)}, bf16[4096,128]{1,0:T(8,128)(2,1)S(1)}, u32[]{:S(2)}, u32[]{:S(2)}) collective-permute-start(bf16[4096,128]{1,0:T(8,128)(2,1)} %refs_2_.1), channel_id=1, source_target_pairs={{0,16},{8,24},{16,0},{24,8},{1,17},{9,25},{17,1},{25,9},{2,18},{10... | collective-permute-start | bytes 3145736 | tf_op jit(solution)/shard_map/ppermute | solution.py:34
  0.8 0.7 %collective-permute-start.2 = (bf16[4096,128]{1,0:T(8,128)(2,1)}, bf16[4096,128]{1,0:T(8,128)(2,1)S(1)}, u32[]{:S(2)}, u32[]{:S(2)}) collective-permute-start(bf16[4096,128]{1,0:T(8,128)(2,1)} %refs_2_.1), channel_id=1, source_target_pairs={{0,8},{8,0},{16,24},{24,16},{1,9},{9,1},{17,25},{25,17},{2,10},{10... | collective-permute-start | bytes 3145736 | tf_op jit(solution)/shard_map/ppermute | solution.py:34
  1.5 4.4 %collective-permute-done.refs_1_ = bf16[384,4096]{1,0:T(8,128)(2,1)S(1)} collective-permute-done((bf16[384,4096]{1,0:T(8,128)(2,1)}, bf16[384,4096]{1,0:T(8,128)(2,1)S(1)}, u32[]{:S(2)}, u32[]{:S(2)}) %collective-permute-start) | collective-permute-done | bytes 3145760 | tf_op jit(solution)/shard_map/ppermute | solution.py:34
  5.9 0.0 copy-start
  5.9 1.9 %copy-done = bf16[384,4096]{1,0:T(8,128)(2,1)S(1)} copy-done((bf16[384,4096]{1,0:T(8,128)(2,1)S(1)}, bf16[384,4096]{1,0:T(8,128)(2,1)}, u32[]{:S(2)}) %copy-start) | copy-done | bytes 3145752
  7.8 0.0 copy-start.2
  7.8 1.2 %copy-done.2 = bf16[4096,128]{1,0:T(8,128)(2,1)S(1)} copy-done((bf16[4096,128]{1,0:T(8,128)(2,1)S(1)}, bf16[4096,128]{1,0:T(8,128)(2,1)}, u32[]{:S(2)}) %copy-start.2) | copy-done | bytes 1048600
  9.0 0.0 copy-start.4
  9.0 0.0 copy-start.5
  9.0 0.0 copy-start.6
  9.0 0.0 copy-start.3
  9.0 1.8 %shard_map.56.refs_3_.refs_6_ = f32[768,128]{1,0:T(8,128)S(1)} custom-call(bf16[384,4096]{1,0:T(8,128)(2,1)S(1)} %copy-done, bf16[384,4096]{1,0:T(8,128)(2,1)S(1)} %collective-permute-done.refs_1_, bf16[4096,128]{1,0:T(8,128)(2,1)S(1)} %copy-done.2), custom_call_target="tpu_custom_call" | custom-call | bytes 1024 | tf_op jit(solution)/shard_map/pallas_call | solution.py:44
  10.8 0.0 copy-start.1
  10.8 0.0 copy-done.4
  10.8 0.0 copy-done.5
  10.8 0.0 copy-done.6
  10.8 0.7 %shard_map.57 = (bf16[512,512]{1,0:T(8,128)(2,1)S(1)}, bf16[128,384]{1,0:T(8,128)(2,1)S(1)}, bf16[384,128]{1,0:T(8,128)(2,1)S(1)}) custom-call(bf16[1,512,512]{2,1,0:T(8,128)(2,1)S(1)} %copy-done.4, s32[1,512]{1,0:T(1,128)S(1)} %copy-done.5, s32[1,128]{1,0:T(1,128)S(1)} %bitcast.1, f32[768,128]{1,0:T(8,128)S(1)} %shard_map.56.refs_3_.refs_6_), custom_call_target="tpu_custom_call" | custom-call | bytes 1024 | tf_op jit(solution)/shard_map/pallas_call | solution.py:44
  11.5 0.0 copy-done.3
  11.5 4.4 %collective-permute-start.5 = (bf16[4096,128]{1,0:T(8,128)(2,1)S(1)}, bf16[4096,128]{1,0:T(8,128)(2,1)S(1)}, u32[]{:S(2)}, u32[]{:S(2)}) collective-permute-start(bf16[4096,128]{1,0:T(8,128)(2,1)S(1)} %copy-done.3), channel_id=1, source_target_pairs={{4,20},{12,28},{20,4},{28,12},{5,21},{13,29},{21,5},{29,13},{6,22}... | collective-permute-start | bytes 3145736 | tf_op jit(solution)/shard_map/ppermute | solution.py:34
  16.0 3.1 %collective-permute-start.6 = (bf16[4096,128]{1,0:T(8,128)(2,1)S(1)}, bf16[4096,128]{1,0:T(8,128)(2,1)S(1)}, u32[]{:S(2)}, u32[]{:S(2)}) collective-permute-start(bf16[4096,128]{1,0:T(8,128)(2,1)S(1)} %copy-done.3), channel_id=1, source_target_pairs={{4,12},{12,4},{20,28},{28,20},{5,13},{13,5},{21,29},{29,21},{6,14}... | collective-permute-start | bytes 3145736 | tf_op jit(solution)/shard_map/ppermute | solution.py:34
  19.1 0.0 collective-permute-done.1.refs_0_.refs_3_
  19.1 0.0 collective-permute-done.2.refs_1_.refs_2_
  19.2 0.7 %collective-permute-start.3 = (bf16[2688,128]{1,0:T(8,128)(2,1)S(1)}, bf16[2688,128]{1,0:T(8,128)(2,1)S(1)}, u32[]{:S(2)}, u32[]{:S(2)}) collective-permute-start(bf16[2688,128]{1,0:T(8,128)(2,1)S(1)} %get-tuple-element.26), channel_id=1, source_target_pairs={{0,16},{8,24},{16,0},{24,8},{1,17},{9,25},{17,1},{25,9},{2,18},{10... | collective-permute-start | bytes 2064392 | tf_op jit(solution)/shard_map/ppermute | solution.py:34
  19.9 11.0 %collective-permute-done.5.refs_0_.refs_5_ = bf16[4096,128]{1,0:T(8,128)(2,1)S(1)} collective-permute-done((bf16[4096,128]{1,0:T(8,128)(2,1)S(1)}, bf16[4096,128]{1,0:T(8,128)(2,1)S(1)}, u32[]{:S(2)}, u32[]{:S(2)}) %collective-permute-start.5) | collective-permute-done | bytes 1048608 | tf_op jit(solution)/shard_map/ppermute | solution.py:34
  30.8 2.9 %collective-permute-done.6.refs_1_.refs_4_ = bf16[4096,128]{1,0:T(8,128)(2,1)S(1)} collective-permute-done((bf16[4096,128]{1,0:T(8,128)(2,1)S(1)}, bf16[4096,128]{1,0:T(8,128)(2,1)S(1)}, u32[]{:S(2)}, u32[]{:S(2)}) %collective-permute-start.6) | collective-permute-done | bytes 1048608 | tf_op jit(solution)/shard_map/ppermute | solution.py:34
  33.8 0.4 shard_map.58
  34.2 1.9 %collective-permute-start.7 = (bf16[2432,128]{1,0:T(8,128)(2,1)S(1)}, bf16[2432,128]{1,0:T(8,128)(2,1)S(1)}, u32[]{:S(2)}, u32[]{:S(2)}) collective-permute-start(bf16[2432,128]{1,0:T(8,128)(2,1)S(1)} %get-tuple-element.30), channel_id=1, source_target_pairs={{4,20},{12,28},{20,4},{28,12},{5,21},{13,29},{21,5},{29,13},{6,22}... | collective-permute-start | bytes 1867784 | tf_op jit(solution)/shard_map/ppermute | solution.py:34
  36.1 2.6 %collective-permute-start.8 = (bf16[1664,128]{1,0:T(8,128)(2,1)S(1)}, bf16[1664,128]{1,0:T(8,128)(2,1)S(1)}, u32[]{:S(2)}, u32[]{:S(2)}) collective-permute-start(bf16[1664,128]{1,0:T(8,128)(2,1)S(1)} %get-tuple-element.31), channel_id=1, source_target_pairs={{4,12},{12,4},{20,28},{28,20},{5,13},{13,5},{21,29},{29,21},{6,14}... | collective-permute-start | bytes 1277960 | tf_op jit(solution)/shard_map/ppermute | solution.py:34
  38.7 0.7 collective-permute-start.4
  39.4 0.0 copy-done.1
  39.4 1.8 %shard_map.59 = (f32[768,128]{1,0:T(8,128)S(1)}, f32[768,128]{1,0:T(8,128)S(1)}) custom-call(bf16[384,4096]{1,0:T(8,128)(2,1)S(1)} %copy-done.1, bf16[384,4096]{1,0:T(8,128)(2,1)S(1)} %collective-permute-done.refs_1_, bf16[4096,128]{1,0:T(8,128)(2,1)S(1)} %collective-permute-done.2.refs_1_.refs_2_, ...), custom_call_target="tpu_custom_call" | custom-call | bytes 1024 | tf_op jit(solution)/shard_map/pallas_call | solution.py:44
  41.2 0.0 collective-permute-done.4.refs_3_
  41.3 0.0 collective-permute-done.3.refs_2_
  41.3 4.0 %collective-permute-done.8.refs_5_ = bf16[1664,128]{1,0:T(8,128)(2,1)S(1)} collective-permute-done((bf16[1664,128]{1,0:T(8,128)(2,1)S(1)}, bf16[1664,128]{1,0:T(8,128)(2,1)S(1)}, u32[]{:S(2)}, u32[]{:S(2)}) %collective-permute-start.8) | collective-permute-done | bytes 426016 | tf_op jit(solution)/shard_map/ppermute | solution.py:34
  45.3 0.2 collective-permute-done.7.refs_4_
  45.5 1.9 %shard_map.60 = (f32[768,128]{1,0:T(8,128)S(1)}, bf16[768,128]{1,0:T(8,128)(2,1)S(1)}, bf16[768,128]{1,0:T(8,128)(2,1)S(1)}, bf16[768,128]{1,0:T(8,128)(2,1)S(1)}) custom-call(bf16[384,4096]{1,0:T(8,128)(2,1)S(1)} %copy-done.1, bf16[384,4096]{1,0:T(8,128)(2,1)S(1)} %collective-permute-done.refs_1_, bf16[2688,128]{1,0:T(8,128)(2,1)S(1)} %collective-permute-done.3.refs_2_, ...), custom_call_target="tpu_custom_call" | custom-call | bytes 1024 | tf_op jit(solution)/shard_map/pallas_call | solution.py:44
  47.4 2.9 %collective-permute-start.10 = (bf16[768,128]{1,0:T(8,128)(2,1)S(1)}, bf16[768,128]{1,0:T(8,128)(2,1)S(1)}, u32[]{:S(2)}, u32[]{:S(2)}) collective-permute-start(bf16[768,128]{1,0:T(8,128)(2,1)S(1)} %get-tuple-element.36), channel_id=1, source_target_pairs={{0,3},{1,2},{2,1},{3,0},{4,7},{5,6},{6,5},{7,4},{8,11},{9,10},{10,... | collective-permute-start | bytes 589832 | tf_op jit(solution)/shard_map/ppermute | solution.py:34
  50.3 0.0 collective-permute-start.11
  50.3 0.7 %collective-permute-start.9 = (bf16[768,128]{1,0:T(8,128)(2,1)S(1)}, bf16[768,128]{1,0:T(8,128)(2,1)S(1)}, u32[]{:S(2)}, u32[]{:S(2)}) collective-permute-start(bf16[768,128]{1,0:T(8,128)(2,1)S(1)} %get-tuple-element.35), channel_id=1, source_target_pairs={{0,1},{1,0},{2,3},{3,2},{4,5},{5,4},{6,7},{7,6},{8,9},{9,8},{10,11... | collective-permute-start | bytes 589832 | tf_op jit(solution)/shard_map/ppermute | solution.py:34
  51.0 3.0 %collective-permute-done.10.refs_2_ = bf16[768,128]{1,0:T(8,128)(2,1)S(1)} collective-permute-done((bf16[768,128]{1,0:T(8,128)(2,1)S(1)}, bf16[768,128]{1,0:T(8,128)(2,1)S(1)}, u32[]{:S(2)}, u32[]{:S(2)}) %collective-permute-start.10) | collective-permute-done | bytes 196640 | tf_op jit(solution)/shard_map/ppermute | solution.py:34
  54.0 5.8 %collective-permute-done.11.refs_3_ = bf16[768,128]{1,0:T(8,128)(2,1)S(1)} collective-permute-done((bf16[768,128]{1,0:T(8,128)(2,1)S(1)}, bf16[768,128]{1,0:T(8,128)(2,1)S(1)}, u32[]{:S(2)}, u32[]{:S(2)}) %collective-permute-start.11) | collective-permute-done | bytes 196640 | tf_op jit(solution)/shard_map/ppermute | solution.py:34
  59.8 0.0 collective-permute-done.9.refs_1_
  59.8 0.1 shard_map.61
  59.9 0.1 collective-permute-start.12
  60.0 1.4 %collective-permute-done.12.refs_1_ = f32[384,128]{1,0:T(8,128)S(1)} collective-permute-done((f32[384,128]{1,0:T(8,128)S(1)}, f32[384,128]{1,0:T(8,128)S(1)}, u32[]{:S(2)}, u32[]{:S(2)}) %collective-permute-start.12) | collective-permute-done | bytes 196640 | tf_op jit(solution)/shard_map/ppermute | solution.py:34
  61.4 0.3 shard_map.62
  61.7 0.2 collective-permute-start.13
  61.9 3.4 %collective-permute-start.14 = (bf16[128,384]{1,0:T(8,128)(2,1)S(1)}, bf16[128,384]{1,0:T(8,128)(2,1)S(1)}, u32[]{:S(2)}, u32[]{:S(2)}) collective-permute-start(bf16[128,384]{1,0:T(8,128)(2,1)S(1)} %get-tuple-element.46), channel_id=1, source_target_pairs={{4,8},{12,16},{20,24},{8,4},{16,12},{24,20},{5,9},{13,17},{21,25},... | collective-permute-start | bytes 294920 | tf_op jit(solution)/shard_map/ppermute | solution.py:215
  65.3 0.4 shard_map.63
  65.7 0.0 collective-permute-done.13.refs_4_
  65.7 2.5 %collective-permute-done.14.refs_5_ = bf16[128,384]{1,0:T(8,128)(2,1)S(1)} collective-permute-done((bf16[128,384]{1,0:T(8,128)(2,1)S(1)}, bf16[128,384]{1,0:T(8,128)(2,1)S(1)}, u32[]{:S(2)}, u32[]{:S(2)}) %collective-permute-start.14) | collective-permute-done | bytes 98336 | tf_op jit(solution)/shard_map/ppermute | solution.py:215
  68.3 1.2 %shard_map.64 = f32[384,256]{1,0:T(8,128)} custom-call(f32[384,256]{1,0:T(8,128)S(1)} %get-tuple-element.42.refs_0_, bf16[128,512]{1,0:T(8,128)(2,1)S(1)} %get-tuple-element.43.refs_1_, bf16[512,512]{1,0:T(8,128)(2,1)S(1)} %get-tuple-element.28.refs_2_.refs_1_, bf16[384,128]{1,0:T(8,128)(2,1)S(1)} %get-tuple-element.44.refs_3_, ...), custom_call_target="tpu_custom_call" | custom-call | bytes 1024 | tf_op jit(solution)/shard_map/pallas_call | solution.py:44
  (1 shorter events, 0.0 us)
Async XLA Ops:
  0.0 5.9 %collective-permute-start = (bf16[384,4096]{1,0:T(8,128)(2,1)}, bf16[384,4096]{1,0:T(8,128)(2,1)S(1)}, u32[]{:S(2)}, u32[]{:S(2)}) collective-permute-start(bf16[384,4096]{1,0:T(8,128)(2,1)} %refs_0_.7), channel_id=1, source_target_pairs={{0,4},{4,0},{8,12},{12,8},{16,20},{20,16},{24,28},{28,24},{1,5},{5... | collective-permute-start | bytes 9437192 | tf_op jit(solution)/shard_map/ppermute | solution.py:34
  0.1 19.0 %collective-permute-start.1 = (bf16[4096,128]{1,0:T(8,128)(2,1)}, bf16[4096,128]{1,0:T(8,128)(2,1)S(1)}, u32[]{:S(2)}, u32[]{:S(2)}) collective-permute-start(bf16[4096,128]{1,0:T(8,128)(2,1)} %refs_2_.1), channel_id=1, source_target_pairs={{0,16},{8,24},{16,0},{24,8},{1,17},{9,25},{17,1},{25,9},{2,18},{10... | collective-permute-start | bytes 3145736 | tf_op jit(solution)/shard_map/ppermute | solution.py:34
  0.8 18.3 %collective-permute-start.2 = (bf16[4096,128]{1,0:T(8,128)(2,1)}, bf16[4096,128]{1,0:T(8,128)(2,1)S(1)}, u32[]{:S(2)}, u32[]{:S(2)}) collective-permute-start(bf16[4096,128]{1,0:T(8,128)(2,1)} %refs_2_.1), channel_id=1, source_target_pairs={{0,8},{8,0},{16,24},{24,16},{1,9},{9,1},{17,25},{25,17},{2,10},{10... | collective-permute-start | bytes 3145736 | tf_op jit(solution)/shard_map/ppermute | solution.py:34
  5.9 1.9 %copy-start = (bf16[384,4096]{1,0:T(8,128)(2,1)S(1)}, bf16[384,4096]{1,0:T(8,128)(2,1)}, u32[]{:S(2)}) copy-start(bf16[384,4096]{1,0:T(8,128)(2,1)} %refs_0_.7) | copy-start | bytes 9437188
  7.8 1.2 %copy-start.2 = (bf16[4096,128]{1,0:T(8,128)(2,1)S(1)}, bf16[4096,128]{1,0:T(8,128)(2,1)}, u32[]{:S(2)}) copy-start(bf16[4096,128]{1,0:T(8,128)(2,1)} %refs_2_.1) | copy-start | bytes 3145732
  9.0 1.8 %copy-start.4 = (bf16[1,512,512]{2,1,0:T(8,128)(2,1)S(1)}, bf16[1,512,512]{2,1,0:T(8,128)(2,1)}, u32[]{:S(2)}) copy-start(bf16[1,512,512]{2,1,0:T(8,128)(2,1)} %refs_0_.5) | copy-start | bytes 1572868
  9.0 1.8 %copy-start.5 = (s32[1,512]{1,0:T(1,128)S(1)}, s32[1,512]{1,0:T(1,128)}, u32[]{:S(2)}) copy-start(s32[1,512]{1,0:T(1,128)} %refs_1_.1) | copy-start | bytes 6148
  9.0 1.8 %copy-start.6 = (s32[128]{0:T(128)S(1)}, s32[128]{0:T(128)}, u32[]{:S(2)}) copy-start(s32[128]{0:T(128)} %param.9) | copy-start | bytes 1540
  9.0 2.5 %copy-start.3 = (bf16[4096,128]{1,0:T(8,128)(2,1)S(1)}, bf16[4096,128]{1,0:T(8,128)(2,1)}, u32[]{:S(2)}) copy-start(bf16[4096,128]{1,0:T(8,128)(2,1)} %refs_2_.1) | copy-start | bytes 3145732
  10.8 28.7 %copy-start.1 = (bf16[384,4096]{1,0:T(8,128)(2,1)S(1)}, bf16[384,4096]{1,0:T(8,128)(2,1)}, u32[]{:S(2)}) copy-start(bf16[384,4096]{1,0:T(8,128)(2,1)} %refs_0_.7) | copy-start | bytes 9437188
  11.5 19.3 %collective-permute-start.5 = (bf16[4096,128]{1,0:T(8,128)(2,1)S(1)}, bf16[4096,128]{1,0:T(8,128)(2,1)S(1)}, u32[]{:S(2)}, u32[]{:S(2)}) collective-permute-start(bf16[4096,128]{1,0:T(8,128)(2,1)S(1)} %copy-done.3), channel_id=1, source_target_pairs={{4,20},{12,28},{20,4},{28,12},{5,21},{13,29},{21,5},{29,13},{6,22}... | collective-permute-start | bytes 3145736 | tf_op jit(solution)/shard_map/ppermute | solution.py:34
  16.0 17.8 %collective-permute-start.6 = (bf16[4096,128]{1,0:T(8,128)(2,1)S(1)}, bf16[4096,128]{1,0:T(8,128)(2,1)S(1)}, u32[]{:S(2)}, u32[]{:S(2)}) collective-permute-start(bf16[4096,128]{1,0:T(8,128)(2,1)S(1)} %copy-done.3), channel_id=1, source_target_pairs={{4,12},{12,4},{20,28},{28,20},{5,13},{13,5},{21,29},{29,21},{6,14}... | collective-permute-start | bytes 3145736 | tf_op jit(solution)/shard_map/ppermute | solution.py:34
  19.2 22.1 %collective-permute-start.3 = (bf16[2688,128]{1,0:T(8,128)(2,1)S(1)}, bf16[2688,128]{1,0:T(8,128)(2,1)S(1)}, u32[]{:S(2)}, u32[]{:S(2)}) collective-permute-start(bf16[2688,128]{1,0:T(8,128)(2,1)S(1)} %get-tuple-element.26), channel_id=1, source_target_pairs={{0,16},{8,24},{16,0},{24,8},{1,17},{9,25},{17,1},{25,9},{2,18},{10... | collective-permute-start | bytes 2064392 | tf_op jit(solution)/shard_map/ppermute | solution.py:34
  34.2 11.3 %collective-permute-start.7 = (bf16[2432,128]{1,0:T(8,128)(2,1)S(1)}, bf16[2432,128]{1,0:T(8,128)(2,1)S(1)}, u32[]{:S(2)}, u32[]{:S(2)}) collective-permute-start(bf16[2432,128]{1,0:T(8,128)(2,1)S(1)} %get-tuple-element.30), channel_id=1, source_target_pairs={{4,20},{12,28},{20,4},{28,12},{5,21},{13,29},{21,5},{29,13},{6,22}... | collective-permute-start | bytes 1867784 | tf_op jit(solution)/shard_map/ppermute | solution.py:34
  36.1 9.2 %collective-permute-start.8 = (bf16[1664,128]{1,0:T(8,128)(2,1)S(1)}, bf16[1664,128]{1,0:T(8,128)(2,1)S(1)}, u32[]{:S(2)}, u32[]{:S(2)}) collective-permute-start(bf16[1664,128]{1,0:T(8,128)(2,1)S(1)} %get-tuple-element.31), channel_id=1, source_target_pairs={{4,12},{12,4},{20,28},{28,20},{5,13},{13,5},{21,29},{29,21},{6,14}... | collective-permute-start | bytes 1277960 | tf_op jit(solution)/shard_map/ppermute | solution.py:34
  38.7 2.5 %collective-permute-start.4 = (bf16[1408,128]{1,0:T(8,128)(2,1)S(1)}, bf16[1408,128]{1,0:T(8,128)(2,1)S(1)}, u32[]{:S(2)}, u32[]{:S(2)}) collective-permute-start(bf16[1408,128]{1,0:T(8,128)(2,1)S(1)} %get-tuple-element.27.refs_2_), channel_id=1, source_target_pairs={{0,8},{8,0},{16,24},{24,16},{1,9},{9,1},{17,25},{25,17},{2,10},{10... | collective-permute-start | bytes 1081352 | tf_op jit(solution)/shard_map/ppermute | solution.py:34
  47.4 6.6 %collective-permute-start.10 = (bf16[768,128]{1,0:T(8,128)(2,1)S(1)}, bf16[768,128]{1,0:T(8,128)(2,1)S(1)}, u32[]{:S(2)}, u32[]{:S(2)}) collective-permute-start(bf16[768,128]{1,0:T(8,128)(2,1)S(1)} %get-tuple-element.36), channel_id=1, source_target_pairs={{0,3},{1,2},{2,1},{3,0},{4,7},{5,6},{6,5},{7,4},{8,11},{9,10},{10,... | collective-permute-start | bytes 589832 | tf_op jit(solution)/shard_map/ppermute | solution.py:34
  50.3 9.5 %collective-permute-start.11 = (bf16[768,128]{1,0:T(8,128)(2,1)S(1)}, bf16[768,128]{1,0:T(8,128)(2,1)S(1)}, u32[]{:S(2)}, u32[]{:S(2)}) collective-permute-start(bf16[768,128]{1,0:T(8,128)(2,1)S(1)} %get-tuple-element.37), channel_id=1, source_target_pairs={{0,2},{1,3},{2,0},{3,1},{4,6},{5,7},{6,4},{7,5},{8,10},{9,11},{10,... | collective-permute-start | bytes 589832 | tf_op jit(solution)/shard_map/ppermute | solution.py:34
  50.3 9.5 %collective-permute-start.9 = (bf16[768,128]{1,0:T(8,128)(2,1)S(1)}, bf16[768,128]{1,0:T(8,128)(2,1)S(1)}, u32[]{:S(2)}, u32[]{:S(2)}) collective-permute-start(bf16[768,128]{1,0:T(8,128)(2,1)S(1)} %get-tuple-element.35), channel_id=1, source_target_pairs={{0,1},{1,0},{2,3},{3,2},{4,5},{5,4},{6,7},{7,6},{8,9},{9,8},{10,11... | collective-permute-start | bytes 589832 | tf_op jit(solution)/shard_map/ppermute | solution.py:34
  59.9 1.5 %collective-permute-start.12 = (f32[384,128]{1,0:T(8,128)S(1)}, f32[384,128]{1,0:T(8,128)S(1)}, u32[]{:S(2)}, u32[]{:S(2)}) collective-permute-start(f32[384,128]{1,0:T(8,128)S(1)} %get-tuple-element.39), channel_id=1, source_target_pairs={{0,4},{4,0},{8,12},{12,8},{16,20},{20,16},{24,28},{28,24},{1,5},{5... | collective-permute-start | bytes 589832 | tf_op jit(solution)/shard_map/ppermute | solution.py:34
  61.7 4.0 %collective-permute-start.13 = (bf16[128,384]{1,0:T(8,128)(2,1)S(1)}, bf16[128,384]{1,0:T(8,128)(2,1)S(1)}, u32[]{:S(2)}, u32[]{:S(2)}) collective-permute-start(bf16[128,384]{1,0:T(8,128)(2,1)S(1)} %get-tuple-element.45), channel_id=1, source_target_pairs={{0,4},{4,0},{8,12},{12,8},{16,20},{20,16},{24,28},{28,24},{1,5},{5... | collective-permute-start | bytes 294920 | tf_op jit(solution)/shard_map/ppermute | solution.py:34
  61.9 6.4 %collective-permute-start.14 = (bf16[128,384]{1,0:T(8,128)(2,1)S(1)}, bf16[128,384]{1,0:T(8,128)(2,1)S(1)}, u32[]{:S(2)}, u32[]{:S(2)}) collective-permute-start(bf16[128,384]{1,0:T(8,128)(2,1)S(1)} %get-tuple-element.46), channel_id=1, source_target_pairs={{4,8},{12,16},{20,24},{8,4},{16,12},{24,20},{5,9},{13,17},{21,25},... | collective-permute-start | bytes 294920 | tf_op jit(solution)/shard_map/ppermute | solution.py:215

commit v16 on v9

--- a/solution.py
+++ b/solution.py
@@ -35,6 +35,7 @@
 
 
 def call(kernel, outs, operands, after=(), spaces=None, scratch=()):
+    after = tuple(after)
     count = len(operands)
 
     def body(*refs):
@@ -63,98 +64,175 @@
     return lax.bitwise_xor(lax.div(lax.axis_index("domain"), 2), lax.axis_index("band"))
 
 
-def pieces_kernel(near_even, far_even, near_odd, far_first, far_rest, top, bottom, done):
-    upper, lower = pl.ds(0, top.shape[0]), pl.ds(top.shape[0], bottom.shape[0])
-    rest = pl.ds(top.shape[0] - far_first.shape[0], bottom.shape[0])
-
-    def fill(*pairs):
-        copies = [pltpu.make_async_copy(source, target, done.at[number]) for number, (source, target) in enumerate(pairs)]
-        for copy in copies:
+def only(one):
+    return pl.when(core() == one)
+
+
+def pieces_kernel(one, *refs):
+    (*shards, done), count = refs, (len(refs) - 1) // 2
+
+    @only(one)
+    def _():
+        start = 0
+        for number in range(count):
+            out = shards[count + number]
+            rows = out.shape[0]
+            copy = pltpu.make_async_copy(shards[number].at[pl.ds(start, rows)], out, done)
             copy.start()
-        for copy in copies:
             copy.wait()
-
-    pl.when(core() == 0)(lambda: fill((near_even.at[upper], top), (far_even.at[lower], bottom)))
-    pl.when(core() != 0)(lambda: fill((near_odd.at[upper], top), (far_rest.at[rest], bottom)))
+            start += rows
+
+
+def part_kernel(start, one, shard, out, done):
+    @only(one)
+    def _():
+        copy = pltpu.make_async_copy(shard.at[pl.ds(start, out.shape[0])], out, done)
+        copy.start()
+        copy.wait()
+
+
+def multiply(mine, theirs, right, blocks, start=0, add=None):
+    rows, width = mine.shape[0], right.shape[1] // len(blocks)
+    for side, states in enumerate((mine, theirs)):
+        span = slice(side * rows, (side + 1) * rows)
+        result = jnp.dot(states[:, start : start + right.shape[0]], right, preferred_element_type=F32)
+        for slot, block in enumerate(blocks):
+            value = result[:, slot * width : (slot + 1) * width]
+            block[span] = value if add is None else value + add[span]
+
+
+def send(blocks, outs, masks):
+    where = block_of_band()
+    for mask, out in zip(masks, outs):
+        for slot, block in blocks:
+
+            @pl.when(slot == lax.bitwise_xor(where, mask))
+            def _():
+                out[...] = block[...].astype(out.dtype)
 
 
 def own_kernel(mine, theirs, own, block):
-    rows = mine.shape[0]
-    for side, states in enumerate((mine, theirs)):
-        block[side * rows : (side + 1) * rows] = jnp.dot(states[...], own[...], preferred_element_type=F32)
-
-
-def early_kernel(mine, theirs, near_even, far_even, near_odd, far_first, far_rest, near_block, far_block):
-    rows, width = mine.shape[0], near_even.shape[1]
-    first = core() == 0
-    far_odd = jnp.concatenate([far_first[...], far_rest[...]], 0)
-    near, far = jnp.where(first, near_even[...], near_odd[...]), jnp.where(first, far_even[...], far_odd)
-    wide = jnp.concatenate([near, far], 1)
-    for side, states in enumerate((mine, theirs)):
-        result = jnp.dot(states[...], wide, preferred_element_type=F32)
-        near_block[side * rows : (side + 1) * rows] = result[:, :width]
-        far_block[side * rows : (side + 1) * rows] = result[:, width:]
+    multiply(mine, theirs, own[...], [block])
+
+
+def far_kernel(mine, theirs, far, own, block, *sent):
+    @only(0)
+    def _():
+        multiply(mine, theirs, far[...], [block])
+        send([(0, own), (2, block)], sent, range(1, len(sent) + 1))
+
+
+def near_kernel(mine, theirs, near, block):
+    only(0)(lambda: multiply(mine, theirs, near[...], [block]))
+
+
+def first_late_kernel(mine, theirs, top, bottom, own, near, far, kept, *refs):
+    sent, last = refs[:-1], refs[-1]
+
+    @only(0)
+    def _():
+        multiply(mine, theirs, top[...], [last])
+        multiply(mine, theirs, bottom[...], [last], top.shape[0], last)
+        send([(0, own), (1, near), (2, far), (3, last)], [kept], [0])
+        send([(1, near), (3, last)], sent, range(1, len(sent) + 1))
+
+
+def early_kernel(mine, theirs, near, far, near_block, far_block):
+    only(CORE)(lambda: multiply(mine, theirs, jnp.concatenate([near[...], far[...]], 1), [near_block, far_block]))
 
 
 def lower_kernel(mine, theirs, bottom, block):
-    start, rows = mine.shape[1] - bottom.shape[0], mine.shape[0]
-    for side, states in enumerate((mine, theirs)):
-        result = jnp.dot(states[:, start:], bottom[...], preferred_element_type=F32)
-        block[side * rows : (side + 1) * rows] = result
+    only(CORE)(lambda: multiply(mine, theirs, bottom[...], [block], mine.shape[1] - bottom.shape[0]))
 
 
 def late_kernel(mine, theirs, top, lower, own, near, far, kept, *refs):
     sent, last = refs[:-1], refs[-1]
-    cut = top.shape[0]
-    rows = mine.shape[0]
-    for side, states in enumerate((mine, theirs)):
-        span = slice(side * rows, (side + 1) * rows)
-        last[span] = lower[span] + jnp.dot(states[:, :cut], top[...], preferred_element_type=F32)
-    where = block_of_band()
-
-    def store(out, slot, block):
-        @pl.when(slot == lax.bitwise_xor(where, mask))
-        def _():
-            out[...] = block[...].astype(out.dtype)
-
-    for mask, out in enumerate((kept, *sent)):
-        for slot, block in enumerate((own, near, far, last)):
-            store(out, slot, block)
-
-
-def sum_kernel(kept, *refs):
-    parts, (mine, theirs) = refs[:-2], refs[-2:]
+
+    @only(CORE)
+    def _():
+        multiply(mine, theirs, top[...], [last], 0, lower)
+        send([(0, own), (1, near), (2, far), (3, last)], [kept, *sent], range(len(sent) + 1))
+
+
+def total_of(kept, parts):
     value = kept[...]
     for part in parts:
         value = value + part[...].astype(F32)
+    return value
+
+
+def first_sum_kernel(kept, *refs):
+    parts, out = refs[:-1], refs[-1]
+
+    @only(0)
+    def _():
+        out[...] = total_of(kept, parts)
+
+
+def sum_kernel(other_total, kept, *refs):
+    parts, (mine, theirs) = refs[:-2], refs[-2:]
     rows = mine.shape[0]
-    mine[...] = value[:rows]
-    theirs[...] = value[rows:]
+
+    def store(value):
+        mine[...] = value[:rows]
+        theirs[...] = value[rows:]
+
+    only(0)(lambda: store(other_total[...]))
+    only(CORE)(lambda: store(total_of(kept, parts)))
 
 
 def rotate_square(wavefunctions, rotation, operator):
     bands, chips = lax.axis_size("band"), lax.axis_size("domain") // 2
     rows, states = wavefunctions.shape
     width = rotation.shape[1]
-    cut, part = states // 2, states // 4
-    first = exchanged(rotation[:part], "domain", FAR, CORE)
-    received = [exchanged(rotation, "domain", NEAR, 0), exchanged(rotation, "domain", FAR, 0)]
+    block = [shape(2 * rows, width)]
+    messages = [shape(2 * rows, width, dtype=BF16)] * (bands - 1)
+    masks = range(1, bands)[::-1]
+    scratch = [pltpu.VMEM((2 * rows, width), F32)]
+    semaphore = [pltpu.SemaphoreType.DMA]
+
+    def across(sent, one, slots):
+        results = []
+        for mask in masks:
+            pairs = []
+            for chip in range(chips):
+                for band in range(bands):
+                    if chip ^ band ^ mask in slots:
+                        place = (2 * chip + one) * bands
+                        pairs.append((place + band, place + (band ^ mask)))
+            results.append(lax.ppermute(sent[mask - 1], ("domain", "band"), pairs))
+        return results
+
+    near, far = exchanged(rotation, "domain", NEAR, 0), exchanged(rotation, "domain", FAR, 0)
     theirs = exchanged(wavefunctions, "domain", CORE)
-    later, _, first = lax.optimization_barrier((rotation, theirs, first))
-    received += [exchanged(later, "domain", NEAR, CORE), first, exchanged(later[part:], "domain", FAR, CORE)]
-    block = [shape(2 * rows, width)]
-    own = call(own_kernel, block, (wavefunctions, theirs, rotation), after=(later,))[0]
-    operator = operator(own)
+    both = (wavefunctions, theirs)
+    own = call(own_kernel, block, (*both, rotation))[0]
+    far_block, *sent = call(far_kernel, block + messages, (*both, far, own))
+    parts = across(sent, 0, (0, 2))
+    cut = states * 17 // 32
     outs = [shape(count, width, dtype=BF16) for count in (cut, states - cut)]
-    top, bottom = call(pieces_kernel, outs, received, after=operator[:1], scratch=[pltpu.SemaphoreType.DMA((2,))])
-    top, bottom = exchanged(top, "domain", FAR), exchanged(bottom, "domain", NEAR)
-    early = call(early_kernel, block * 2, (wavefunctions, theirs, *received))
-    outs = block + [shape(2 * rows, width, dtype=BF16)] * (bands - 1)
-    scratch = [pltpu.VMEM((2 * rows, width), F32)]
-    lower = call(lower_kernel, block, (wavefunctions, theirs, bottom))[0]
-    kept, *sent = call(late_kernel, outs, (wavefunctions, theirs, top, lower, own, *early), scratch=scratch)
-    parts = [exchanged(sent[mask - 1], "band", mask) for mask in reversed(range(1, bands))]
-    mine, others = call(sum_kernel, [shape(rows, width)] * 2, (kept, *parts))
+    top, bottom = call(functools.partial(pieces_kernel, 0), outs, (near, far), after=(far_block,), scratch=semaphore)
+    top, bottom = exchanged(top, "domain", FAR, 0), exchanged(bottom, "domain", NEAR, 0)
+    near_block = call(near_kernel, block, (*both, near))[0]
+    operands = (*both, top, bottom, own, near_block, far_block)
+    kept, *sent = call(first_late_kernel, block + messages, operands, after=parts, scratch=scratch)
+    parts += across(sent, 0, (1, 3))
+    first_total = call(first_sum_kernel, block, (kept, *parts))[0]
+
+    later, _ = lax.optimization_barrier((rotation, first_total))
+    near, far = exchanged(later, "domain", NEAR, CORE), exchanged(later, "domain", FAR, CORE)
+    operator = operator(later)
+    cut = states * 13 // 32
+    outs = [shape(states - cut, width, dtype=BF16), shape(cut, width, dtype=BF16)]
+    after = operator[:1]
+    bottom = call(functools.partial(part_kernel, cut, CORE), outs[:1], (far,), after=after, scratch=semaphore)[0]
+    top = call(functools.partial(part_kernel, 0, CORE), outs[1:], (near,), after=(bottom,), scratch=semaphore)[0]
+    bottom, top = exchanged(bottom, "domain", NEAR, CORE), exchanged(top, "domain", FAR, CORE)
+    early = call(early_kernel, block * 2, (*both, near, far))
+    lower = call(lower_kernel, block, (*both, bottom), after=early[:1])[0]
+    kept, *sent = call(late_kernel, block + messages, (*both, top, lower, own, *early), scratch=scratch)
+    parts = across(sent, 1, range(chips))
+    mine, others = call(sum_kernel, [shape(rows, width)] * 2, (first_total, kept, *parts))
     return mine, exchanged(others, "domain", CORE), operator
 
 

time: 73.6 us -> 79.5 us (1.080)
  starting transfers between devices: 22.1 us -> 33.9 us
  waiting for transfers between devices: 36.9 us -> 32.5 us
  local copies, waits for them, and re-layouts: 5.29 us -> 3.14 us
    ppermute x0 -> x9, starting transfers between devices: none -> 13.8 us  [across(): results.append(lax.ppermute(sent[mask - 1], ('domain', 'band'), pairs))]
    ppermute x13 -> x11, waiting for transfers between devices: 34.2 us -> 23.2 us  [exchanged(): lax.ppermute(value, axis, [(source, source ^ mask) for source in sources...]
    ppermute x0 -> x9, waiting for transfers between devices: none -> 6.33 us  [across(): results.append(lax.ppermute(sent[mask - 1], ('domain', 'band'), pairs))]
    slice x2 -> x0, local copies, waits for them, and re-layouts: 2.16 us -> none  [the longest x1 1.2 us: rotate_square(): later[part:]]
    ppermute x13 -> x11, starting transfers between devices: 18.9 us -> 17.3 us  [exchanged(): lax.ppermute(value, axis, [(source, source ^ mask) for source in sources...]
    pallas_call x10 -> x16, Pallas kernels: 8.48 us -> 8.92 us  [call(): pl.pallas_call(body, out_shape=outs, in_specs=[pl.BlockSpec(memory_space=...]
  transfers between devices with their start and end apart: 14 -> 21, of which waited for: 8 -> 8; matrix products, arithmetic and copies ran while one was open for 3% -> 0% of each run, Pallas kernels for 8% -> 8%
where the time goes in v16:
time: 79.5 us; the launch traced here: 79 us
  starting transfers between devices  33.9 us (43%)
  waiting for transfers between devices  32.5 us (41%)
  Pallas kernels  8.92 us (11%)
  local copies, waits for them, and re-layouts  3.14 us (4%)
    ppermute x11, waiting for transfers between devices, exchanged(): lax.ppermute(value, axis, [(source, source ^ mask) for source in sources...  23.2 us
    ppermute x11, starting transfers between devices, exchanged(): lax.ppermute(value, axis, [(source, source ^ mask) for source in sources...  17.3 us
    ppermute x9, starting transfers between devices, across(): results.append(lax.ppermute(sent[mask - 1], ('domain', 'band'), pairs))  13.8 us
    pallas_call x16, Pallas kernels, call(): pl.pallas_call(body, out_shape=outs, in_specs=[pl.BlockSpec(memory_space=...  8.92 us
    ppermute x9, waiting for transfers between devices, across(): results.append(lax.ppermute(sent[mask - 1], ('domain', 'band'), pairs))  6.33 us
    unnamed x12, local copies, waits for them, and re-layouts  3.14 us
    ppermute x1, waiting for transfers between devices, finish_square(): lax.ppermute(outward, 'domain', across + [(target, source) for source, ta...  3.06 us
    ppermute x1, starting transfers between devices, finish_square(): lax.ppermute(outward, 'domain', across + [(target, source) for source, ta...  2.83 us
  transfers between devices with their start and end apart: 21, of which 8 were waited for; matrix products, arithmetic and copies ran while one was open for 0% of the time, Pallas kernels for 8%

profile of v16, /device:TPU:1, one launch (start us, length us, event | category | flops | bytes accessed | tf_op | source)
XLA Modules:
  0.0 79.0 jit_solution(13030226842138468782)
XLA Ops:
  0.0 0.1 collective-permute-start
  0.1 0.7 collective-permute-start.2
  0.8 0.7 collective-permute-start.1
  1.5 4.4 %collective-permute-done.refs_1_ = bf16[384,4096]{1,0:T(8,128)(2,1)S(1)} collective-permute-done((bf16[384,4096]{1,0:T(8,128)(2,1)}, bf16[384,4096]{1,0:T(8,128)(2,1)S(1)}, u32[]{:S(2)}, u32[]{:S(2)}) %collective-permute-start) | collective-permute-done | bytes 3145760 | tf_op jit(solution)/shard_map/ppermute | solution.py:34
  5.9 0.0 copy-start
  5.9 1.9 %copy-done = bf16[384,4096]{1,0:T(8,128)(2,1)S(1)} copy-done((bf16[384,4096]{1,0:T(8,128)(2,1)S(1)}, bf16[384,4096]{1,0:T(8,128)(2,1)}, u32[]{:S(2)}) %copy-start) | copy-done | bytes 3145752
  7.8 1.2 %copy-done.2 = bf16[4096,128]{1,0:T(8,128)(2,1)S(1)} copy-done((bf16[4096,128]{1,0:T(8,128)(2,1)S(1)}, bf16[4096,128]{1,0:T(8,128)(2,1)}, u32[]{:S(2)}) %copy-start.2) | copy-done | bytes 1048600
  9.0 1.8 %shard_map.55.refs_3_.refs_4_ = f32[768,128]{1,0:T(8,128)S(1)} custom-call(bf16[384,4096]{1,0:T(8,128)(2,1)S(1)} %copy-done, bf16[384,4096]{1,0:T(8,128)(2,1)S(1)} %collective-permute-done.refs_1_, bf16[4096,128]{1,0:T(8,128)(2,1)S(1)} %copy-done.2), custom_call_target="tpu_custom_call" | custom-call | bytes 1024 | tf_op jit(solution)/shard_map/pallas_call | solution.py:44
  10.8 0.0 collective-permute-done.2.refs_2_.refs_1_
  10.8 0.0 copy-start.1
  10.8 0.0 collective-permute-done.1.refs_0_.refs_2_
  10.9 0.8 %collective-permute-start.3 = (bf16[2176,128]{1,0:T(8,128)(2,1)S(1)}, bf16[2176,128]{1,0:T(8,128)(2,1)S(1)}, u32[]{:S(2)}, u32[]{:S(2)}) collective-permute-start(bf16[2176,128]{1,0:T(8,128)(2,1)S(1)} %get-tuple-element.33), channel_id=1, source_target_pairs={{0,16},{8,24},{16,0},{24,8},{1,17},{9,25},{17,1},{25,9},{2,18},{10... | collective-permute-start | bytes 1671176 | tf_op jit(solution)/shard_map/ppermute | solution.py:34
  11.7 0.8 %collective-permute-start.4 = (bf16[1920,128]{1,0:T(8,128)(2,1)S(1)}, bf16[1920,128]{1,0:T(8,128)(2,1)S(1)}, u32[]{:S(2)}, u32[]{:S(2)}) collective-permute-start(bf16[1920,128]{1,0:T(8,128)(2,1)S(1)} %get-tuple-element.34), channel_id=1, source_target_pairs={{0,8},{8,0},{16,24},{24,16},{1,9},{9,1},{17,25},{25,17},{2,10},{10... | collective-permute-start | bytes 1474568 | tf_op jit(solution)/shard_map/ppermute | solution.py:34
  12.5 0.7 collective-permute-start.5
  13.2 0.7 collective-permute-start.6
  13.9 0.7 collective-permute-start.7
  14.6 0.0 copy-done.1
  14.6 0.0 copy-start.3
  14.6 0.0 copy-start.4
  14.6 0.0 copy-start.5
  14.6 0.0 collective-permute-done.5.refs_7_.refs_1_
  14.7 0.0 collective-permute-done.6.refs_8_.refs_2_
  14.7 0.0 collective-permute-done.7.refs_9_.refs_3_
  14.7 0.0 collective-permute-done.4.refs_3_
  14.7 0.0 collective-permute-done.3.refs_2_
  14.7 0.8 %collective-permute-start.10 = (bf16[768,128]{1,0:T(8,128)(2,1)S(1)}, bf16[768,128]{1,0:T(8,128)(2,1)S(1)}, u32[]{:S(2)}, u32[]{:S(2)}) collective-permute-start(bf16[768,128]{1,0:T(8,128)(2,1)S(1)} %get-tuple-element.41), channel_id=1, source_target_pairs={{0,1},{2,3},{9,8},{11,10},{16,17},{18,19},{25,24},{27,26}} | collective-permute-start | bytes 589832 | tf_op jit(solution)/shard_map/ppermute | solution.py:203
  15.5 0.7 collective-permute-start.8
  16.2 0.7 collective-permute-start.9
  16.9 0.0 collective-permute-done.10.refs_6_
  16.9 0.0 collective-permute-done.8.refs_4_
  16.9 0.0 collective-permute-done.9.refs_5_
  17.0 4.3 %collective-permute-start.12 = (bf16[4096,128]{1,0:T(8,128)(2,1)S(1)}, bf16[4096,128]{1,0:T(8,128)(2,1)S(1)}, u32[]{:S(2)}, u32[]{:S(2)}) collective-permute-start(bf16[4096,128]{1,0:T(8,128)(2,1)S(1)} %copy-done.2), channel_id=1, source_target_pairs={{4,20},{12,28},{20,4},{28,12},{5,21},{13,29},{21,5},{29,13},{6,22}... | collective-permute-start | bytes 3145736 | tf_op jit(solution)/shard_map/ppermute | solution.py:34
  21.3 3.1 %collective-permute-start.11 = (bf16[4096,128]{1,0:T(8,128)(2,1)S(1)}, bf16[4096,128]{1,0:T(8,128)(2,1)S(1)}, u32[]{:S(2)}, u32[]{:S(2)}) collective-permute-start(bf16[4096,128]{1,0:T(8,128)(2,1)S(1)} %copy-done.2), channel_id=1, source_target_pairs={{4,12},{12,4},{20,28},{28,20},{5,13},{13,5},{21,29},{29,21},{6,14}... | collective-permute-start | bytes 3145736 | tf_op jit(solution)/shard_map/ppermute | solution.py:34
  24.4 0.0 copy-done.3
  24.4 0.0 copy-done.4
  24.4 0.0 copy-done.5
  24.4 0.7 shard_map.61
  25.1 14.6 %collective-permute-done.12.refs_0_.refs_3_ = bf16[4096,128]{1,0:T(8,128)(2,1)S(1)} collective-permute-done((bf16[4096,128]{1,0:T(8,128)(2,1)S(1)}, bf16[4096,128]{1,0:T(8,128)(2,1)S(1)}, u32[]{:S(2)}, u32[]{:S(2)}) %collective-permute-start.12) | collective-permute-done | bytes 1048608 | tf_op jit(solution)/shard_map/ppermute | solution.py:34
  39.7 0.2 shard_map.62.refs_1_
  39.9 3.3 %collective-permute-start.14 = (bf16[2432,128]{1,0:T(8,128)(2,1)S(1)}, bf16[2432,128]{1,0:T(8,128)(2,1)S(1)}, u32[]{:S(2)}, u32[]{:S(2)}) collective-permute-start(bf16[2432,128]{1,0:T(8,128)(2,1)S(1)} %shard_map.62.refs_1_), channel_id=1, source_target_pairs={{4,12},{12,4},{20,28},{28,20},{5,13},{13,5},{21,29},{29,21},{6,14}... | collective-permute-start | bytes 1867784 | tf_op jit(solution)/shard_map/ppermute | solution.py:34
  43.2 0.0 collective-permute-done.11.refs_0_.refs_2_
  43.2 0.3 shard_map.63
  43.5 3.1 %collective-permute-start.13 = (bf16[1664,128]{1,0:T(8,128)(2,1)S(1)}, bf16[1664,128]{1,0:T(8,128)(2,1)S(1)}, u32[]{:S(2)}, u32[]{:S(2)}) collective-permute-start(bf16[1664,128]{1,0:T(8,128)(2,1)S(1)} %shard_map.63), channel_id=1, source_target_pairs={{4,20},{12,28},{20,4},{28,12},{5,21},{13,29},{21,5},{29,13},{6,22}... | collective-permute-start | bytes 1277960 | tf_op jit(solution)/shard_map/ppermute | solution.py:34
  46.6 1.8 %shard_map.64 = (f32[768,128]{1,0:T(8,128)S(1)}, f32[768,128]{1,0:T(8,128)S(1)}) custom-call(bf16[384,4096]{1,0:T(8,128)(2,1)S(1)} %copy-done.1, bf16[384,4096]{1,0:T(8,128)(2,1)S(1)} %collective-permute-done.refs_1_, bf16[4096,128]{1,0:T(8,128)(2,1)S(1)} %collective-permute-done.11.refs_0_.refs_2_, bf16[4096,128]{1,0:T(8,128)(2,1)S(1)} %collective-permute-done.12.refs_0_.refs_3_), custom_call_target="tpu_custom_call" | custom-call | bytes 1024 | tf_op jit(solution)/shard_map/pallas_call | solution.py:44
  48.4 2.4 %collective-permute-done.14.refs_2_ = bf16[2432,128]{1,0:T(8,128)(2,1)S(1)} collective-permute-done((bf16[2432,128]{1,0:T(8,128)(2,1)S(1)}, bf16[2432,128]{1,0:T(8,128)(2,1)S(1)}, u32[]{:S(2)}, u32[]{:S(2)}) %collective-permute-start.14) | collective-permute-done | bytes 622624 | tf_op jit(solution)/shard_map/ppermute | solution.py:34
  50.8 1.1 %shard_map.65.refs_3_ = f32[768,128]{1,0:T(8,128)S(1)} custom-call(bf16[384,4096]{1,0:T(8,128)(2,1)S(1)} %copy-done.1, bf16[384,4096]{1,0:T(8,128)(2,1)S(1)} %collective-permute-done.refs_1_, bf16[2432,128]{1,0:T(8,128)(2,1)S(1)} %collective-permute-done.14.refs_2_, f32[768,128]{1,0:T(8,128)S(1)} %get-tuple-element.44.refs_3_.refs_5_), custom_call_target="tpu_custom_call" | custom-call | bytes 1024 | tf_op jit(solution)/shard_map/pallas_call | solution.py:44
  52.0 0.4 collective-permute-done.13.refs_2_
  52.4 0.9 %shard_map.66 = (f32[768,128]{1,0:T(8,128)S(1)}, bf16[768,128]{1,0:T(8,128)(2,1)S(1)}, bf16[768,128]{1,0:T(8,128)(2,1)S(1)}, bf16[768,128]{1,0:T(8,128)(2,1)S(1)}) custom-call(bf16[384,4096]{1,0:T(8,128)(2,1)S(1)} %copy-done.1, bf16[384,4096]{1,0:T(8,128)(2,1)S(1)} %collective-permute-done.refs_1_, bf16[1664,128]{1,0:T(8,128)(2,1)S(1)} %collective-permute-done.13.refs_2_, ...), custom_call_target="tpu_custom_call" | custom-call | bytes 1024 | tf_op jit(solution)/shard_map/pallas_call | solution.py:44
  53.3 5.5 %collective-permute-start.15 = (bf16[768,128]{1,0:T(8,128)(2,1)S(1)}, bf16[768,128]{1,0:T(8,128)(2,1)S(1)}, u32[]{:S(2)}, u32[]{:S(2)}) collective-permute-start(bf16[768,128]{1,0:T(8,128)(2,1)S(1)} %get-tuple-element.47), channel_id=1, source_target_pairs={{4,7},{5,6},{6,5},{7,4},{12,15},{13,14},{14,13},{15,12},{20,23},{2... | collective-permute-start | bytes 589832 | tf_op jit(solution)/shard_map/ppermute | solution.py:203
  58.8 1.9 %collective-permute-start.16 = (bf16[768,128]{1,0:T(8,128)(2,1)S(1)}, bf16[768,128]{1,0:T(8,128)(2,1)S(1)}, u32[]{:S(2)}, u32[]{:S(2)}) collective-permute-start(bf16[768,128]{1,0:T(8,128)(2,1)S(1)} %get-tuple-element.48), channel_id=1, source_target_pairs={{4,6},{5,7},{6,4},{7,5},{12,14},{13,15},{14,12},{15,13},{20,22},{2... | collective-permute-start | bytes 589832 | tf_op jit(solution)/shard_map/ppermute | solution.py:203
  60.8 2.2 %collective-permute-start.17 = (bf16[768,128]{1,0:T(8,128)(2,1)S(1)}, bf16[768,128]{1,0:T(8,128)(2,1)S(1)}, u32[]{:S(2)}, u32[]{:S(2)}) collective-permute-start(bf16[768,128]{1,0:T(8,128)(2,1)S(1)} %get-tuple-element.49), channel_id=1, source_target_pairs={{4,5},{5,4},{6,7},{7,6},{12,13},{13,12},{14,15},{15,14},{20,21},{2... | collective-permute-start | bytes 589832 | tf_op jit(solution)/shard_map/ppermute | solution.py:203
  63.0 0.0 collective-permute-done.15.refs_2_
  63.0 4.5 %collective-permute-done.16.refs_3_ = bf16[768,128]{1,0:T(8,128)(2,1)S(1)} collective-permute-done((bf16[768,128]{1,0:T(8,128)(2,1)S(1)}, bf16[768,128]{1,0:T(8,128)(2,1)S(1)}, u32[]{:S(2)}, u32[]{:S(2)}) %collective-permute-start.16) | collective-permute-done | bytes 196640 | tf_op jit(solution)/shard_map/ppermute | solution.py:203
  67.5 1.8 %collective-permute-done.17.refs_4_ = bf16[768,128]{1,0:T(8,128)(2,1)S(1)} collective-permute-done((bf16[768,128]{1,0:T(8,128)(2,1)S(1)}, bf16[768,128]{1,0:T(8,128)(2,1)S(1)}, u32[]{:S(2)}, u32[]{:S(2)}) %collective-permute-start.17) | collective-permute-done | bytes 196640 | tf_op jit(solution)/shard_map/ppermute | solution.py:203
  69.3 0.1 shard_map.67
  69.4 0.1 collective-permute-start.18
  69.5 1.4 %collective-permute-done.18.refs_1_ = f32[384,128]{1,0:T(8,128)S(1)} collective-permute-done((f32[384,128]{1,0:T(8,128)S(1)}, f32[384,128]{1,0:T(8,128)S(1)}, u32[]{:S(2)}, u32[]{:S(2)}) %collective-permute-start.18) | collective-permute-done | bytes 196640 | tf_op jit(solution)/shard_map/ppermute | solution.py:34
  70.9 0.3 shard_map.68
  71.2 0.2 collective-permute-start.19
  71.4 2.8 %collective-permute-start.20 = (bf16[128,384]{1,0:T(8,128)(2,1)S(1)}, bf16[128,384]{1,0:T(8,128)(2,1)S(1)}, u32[]{:S(2)}, u32[]{:S(2)}) collective-permute-start(bf16[128,384]{1,0:T(8,128)(2,1)S(1)} %get-tuple-element.58), channel_id=1, source_target_pairs={{4,8},{12,16},{20,24},{8,4},{16,12},{24,20},{5,9},{13,17},{21,25},... | collective-permute-start | bytes 294920 | tf_op jit(solution)/shard_map/ppermute | solution.py:292
  74.2 0.5 shard_map.69
  74.7 0.0 collective-permute-done.19.refs_4_
  74.7 3.1 %collective-permute-done.20.refs_5_ = bf16[128,384]{1,0:T(8,128)(2,1)S(1)} collective-permute-done((bf16[128,384]{1,0:T(8,128)(2,1)S(1)}, bf16[128,384]{1,0:T(8,128)(2,1)S(1)}, u32[]{:S(2)}, u32[]{:S(2)}) %collective-permute-start.20) | collective-permute-done | bytes 98336 | tf_op jit(solution)/shard_map/ppermute | solution.py:292
  77.8 1.2 %shard_map.70 = f32[384,256]{1,0:T(8,128)} custom-call(f32[384,256]{1,0:T(8,128)S(1)} %get-tuple-element.54.refs_0_, bf16[128,512]{1,0:T(8,128)(2,1)S(1)} %get-tuple-element.55.refs_1_, bf16[512,512]{1,0:T(8,128)(2,1)S(1)} %get-tuple-element.43.refs_1_.refs_2_, bf16[384,128]{1,0:T(8,128)(2,1)S(1)} %get-tuple-element.56.refs_3_, ...), custom_call_target="tpu_custom_call" | custom-call | bytes 1024 | tf_op jit(solution)/shard_map/pallas_call | solution.py:44
  (6 shorter events, 0.1 us)
Async XLA Ops:
  0.0 5.9 %collective-permute-start = (bf16[384,4096]{1,0:T(8,128)(2,1)}, bf16[384,4096]{1,0:T(8,128)(2,1)S(1)}, u32[]{:S(2)}, u32[]{:S(2)}) collective-permute-start(bf16[384,4096]{1,0:T(8,128)(2,1)} %refs_0_.15), channel_id=1, source_target_pairs={{0,4},{4,0},{8,12},{12,8},{16,20},{20,16},{24,28},{28,24},{1,5},{5... | collective-permute-start | bytes 9437192 | tf_op jit(solution)/shard_map/ppermute | solution.py:34
  0.1 10.7 %collective-permute-start.2 = (bf16[4096,128]{1,0:T(8,128)(2,1)}, bf16[4096,128]{1,0:T(8,128)(2,1)S(1)}, u32[]{:S(2)}, u32[]{:S(2)}) collective-permute-start(bf16[4096,128]{1,0:T(8,128)(2,1)} %refs_3_), channel_id=1, source_target_pairs={{0,16},{8,24},{16,0},{24,8},{1,17},{9,25},{17,1},{25,9},{2,18},{10... | collective-permute-start | bytes 3145736 | tf_op jit(solution)/shard_map/ppermute | solution.py:34
  0.8 10.0 %collective-permute-start.1 = (bf16[4096,128]{1,0:T(8,128)(2,1)}, bf16[4096,128]{1,0:T(8,128)(2,1)S(1)}, u32[]{:S(2)}, u32[]{:S(2)}) collective-permute-start(bf16[4096,128]{1,0:T(8,128)(2,1)} %refs_3_), channel_id=1, source_target_pairs={{0,8},{8,0},{16,24},{24,16},{1,9},{9,1},{17,25},{25,17},{2,10},{10... | collective-permute-start | bytes 3145736 | tf_op jit(solution)/shard_map/ppermute | solution.py:34
  5.9 1.9 %copy-start = (bf16[384,4096]{1,0:T(8,128)(2,1)S(1)}, bf16[384,4096]{1,0:T(8,128)(2,1)}, u32[]{:S(2)}) copy-start(bf16[384,4096]{1,0:T(8,128)(2,1)} %refs_0_.15) | copy-start | bytes 9437188
  7.8 1.2 %copy-start.2 = (bf16[4096,128]{1,0:T(8,128)(2,1)S(1)}, bf16[4096,128]{1,0:T(8,128)(2,1)}, u32[]{:S(2)}) copy-start(bf16[4096,128]{1,0:T(8,128)(2,1)} %refs_3_) | copy-start | bytes 3145732
  10.8 3.8 %copy-start.1 = (bf16[384,4096]{1,0:T(8,128)(2,1)S(1)}, bf16[384,4096]{1,0:T(8,128)(2,1)}, u32[]{:S(2)}) copy-start(bf16[384,4096]{1,0:T(8,128)(2,1)} %refs_0_.15) | copy-start | bytes 9437188
  10.9 3.8 %collective-permute-start.3 = (bf16[2176,128]{1,0:T(8,128)(2,1)S(1)}, bf16[2176,128]{1,0:T(8,128)(2,1)S(1)}, u32[]{:S(2)}, u32[]{:S(2)}) collective-permute-start(bf16[2176,128]{1,0:T(8,128)(2,1)S(1)} %get-tuple-element.33), channel_id=1, source_target_pairs={{0,16},{8,24},{16,0},{24,8},{1,17},{9,25},{17,1},{25,9},{2,18},{10... | collective-permute-start | bytes 1671176 | tf_op jit(solution)/shard_map/ppermute | solution.py:34
  11.7 3.0 %collective-permute-start.4 = (bf16[1920,128]{1,0:T(8,128)(2,1)S(1)}, bf16[1920,128]{1,0:T(8,128)(2,1)S(1)}, u32[]{:S(2)}, u32[]{:S(2)}) collective-permute-start(bf16[1920,128]{1,0:T(8,128)(2,1)S(1)} %get-tuple-element.34), channel_id=1, source_target_pairs={{0,8},{8,0},{16,24},{24,16},{1,9},{9,1},{17,25},{25,17},{2,10},{10... | collective-permute-start | bytes 1474568 | tf_op jit(solution)/shard_map/ppermute | solution.py:34
  12.5 2.1 %collective-permute-start.5 = (bf16[768,128]{1,0:T(8,128)(2,1)S(1)}, bf16[768,128]{1,0:T(8,128)(2,1)S(1)}, u32[]{:S(2)}, u32[]{:S(2)}) collective-permute-start(bf16[768,128]{1,0:T(8,128)(2,1)S(1)} %get-tuple-element.35), channel_id=1, source_target_pairs={{1,2},{3,0},{8,11},{10,9},{17,18},{19,16},{24,27},{26,25}} | collective-permute-start | bytes 589832 | tf_op jit(solution)/shard_map/ppermute | solution.py:203
  13.2 1.4 %collective-permute-start.6 = (bf16[768,128]{1,0:T(8,128)(2,1)S(1)}, bf16[768,128]{1,0:T(8,128)(2,1)S(1)}, u32[]{:S(2)}, u32[]{:S(2)}) collective-permute-start(bf16[768,128]{1,0:T(8,128)(2,1)S(1)} %get-tuple-element.36), channel_id=1, source_target_pairs={{0,2},{2,0},{9,11},{11,9},{16,18},{18,16},{25,27},{27,25}} | collective-permute-start | bytes 589832 | tf_op jit(solution)/shard_map/ppermute | solution.py:203
  13.9 0.8 collective-permute-start.7
  14.6 9.8 %copy-start.3 = (bf16[1,512,512]{2,1,0:T(8,128)(2,1)S(1)}, bf16[1,512,512]{2,1,0:T(8,128)(2,1)}, u32[]{:S(2)}) copy-start(bf16[1,512,512]{2,1,0:T(8,128)(2,1)} %refs_0_.12) | copy-start | bytes 1572868
  14.6 9.8 %copy-start.4 = (s32[1,512]{1,0:T(1,128)S(1)}, s32[1,512]{1,0:T(1,128)}, u32[]{:S(2)}) copy-start(s32[1,512]{1,0:T(1,128)} %refs_1_.1) | copy-start | bytes 6148
  14.6 9.8 %copy-start.5 = (s32[128]{0:T(128)S(1)}, s32[128]{0:T(128)}, u32[]{:S(2)}) copy-start(s32[128]{0:T(128)} %param.9) | copy-start | bytes 1540
  14.7 2.2 %collective-permute-start.10 = (bf16[768,128]{1,0:T(8,128)(2,1)S(1)}, bf16[768,128]{1,0:T(8,128)(2,1)S(1)}, u32[]{:S(2)}, u32[]{:S(2)}) collective-permute-start(bf16[768,128]{1,0:T(8,128)(2,1)S(1)} %get-tuple-element.41), channel_id=1, source_target_pairs={{0,1},{2,3},{9,8},{11,10},{16,17},{18,19},{25,24},{27,26}} | collective-permute-start | bytes 589832 | tf_op jit(solution)/shard_map/ppermute | solution.py:203
  15.5 1.4 %collective-permute-start.8 = (bf16[768,128]{1,0:T(8,128)(2,1)S(1)}, bf16[768,128]{1,0:T(8,128)(2,1)S(1)}, u32[]{:S(2)}, u32[]{:S(2)}) collective-permute-start(bf16[768,128]{1,0:T(8,128)(2,1)S(1)} %get-tuple-element.39), channel_id=1, source_target_pairs={{0,3},{2,1},{9,10},{11,8},{16,19},{18,17},{25,26},{27,24}} | collective-permute-start | bytes 589832 | tf_op jit(solution)/shard_map/ppermute | solution.py:203
  16.2 0.7 collective-permute-start.9
  17.0 22.7 %collective-permute-start.12 = (bf16[4096,128]{1,0:T(8,128)(2,1)S(1)}, bf16[4096,128]{1,0:T(8,128)(2,1)S(1)}, u32[]{:S(2)}, u32[]{:S(2)}) collective-permute-start(bf16[4096,128]{1,0:T(8,128)(2,1)S(1)} %copy-done.2), channel_id=1, source_target_pairs={{4,20},{12,28},{20,4},{28,12},{5,21},{13,29},{21,5},{29,13},{6,22}... | collective-permute-start | bytes 3145736 | tf_op jit(solution)/shard_map/ppermute | solution.py:34
  21.3 22.0 %collective-permute-start.11 = (bf16[4096,128]{1,0:T(8,128)(2,1)S(1)}, bf16[4096,128]{1,0:T(8,128)(2,1)S(1)}, u32[]{:S(2)}, u32[]{:S(2)}) collective-permute-start(bf16[4096,128]{1,0:T(8,128)(2,1)S(1)} %copy-done.2), channel_id=1, source_target_pairs={{4,12},{12,4},{20,28},{28,20},{5,13},{13,5},{21,29},{29,21},{6,14}... | collective-permute-start | bytes 3145736 | tf_op jit(solution)/shard_map/ppermute | solution.py:34
  39.9 11.0 %collective-permute-start.14 = (bf16[2432,128]{1,0:T(8,128)(2,1)S(1)}, bf16[2432,128]{1,0:T(8,128)(2,1)S(1)}, u32[]{:S(2)}, u32[]{:S(2)}) collective-permute-start(bf16[2432,128]{1,0:T(8,128)(2,1)S(1)} %shard_map.62.refs_1_), channel_id=1, source_target_pairs={{4,12},{12,4},{20,28},{28,20},{5,13},{13,5},{21,29},{29,21},{6,14}... | collective-permute-start | bytes 1867784 | tf_op jit(solution)/shard_map/ppermute | solution.py:34
  43.5 8.9 %collective-permute-start.13 = (bf16[1664,128]{1,0:T(8,128)(2,1)S(1)}, bf16[1664,128]{1,0:T(8,128)(2,1)S(1)}, u32[]{:S(2)}, u32[]{:S(2)}) collective-permute-start(bf16[1664,128]{1,0:T(8,128)(2,1)S(1)} %shard_map.63), channel_id=1, source_target_pairs={{4,20},{12,28},{20,4},{28,12},{5,21},{13,29},{21,5},{29,13},{6,22}... | collective-permute-start | bytes 1277960 | tf_op jit(solution)/shard_map/ppermute | solution.py:34
  53.3 9.7 %collective-permute-start.15 = (bf16[768,128]{1,0:T(8,128)(2,1)S(1)}, bf16[768,128]{1,0:T(8,128)(2,1)S(1)}, u32[]{:S(2)}, u32[]{:S(2)}) collective-permute-start(bf16[768,128]{1,0:T(8,128)(2,1)S(1)} %get-tuple-element.47), channel_id=1, source_target_pairs={{4,7},{5,6},{6,5},{7,4},{12,15},{13,14},{14,13},{15,12},{20,23},{2... | collective-permute-start | bytes 589832 | tf_op jit(solution)/shard_map/ppermute | solution.py:203
  58.8 8.6 %collective-permute-start.16 = (bf16[768,128]{1,0:T(8,128)(2,1)S(1)}, bf16[768,128]{1,0:T(8,128)(2,1)S(1)}, u32[]{:S(2)}, u32[]{:S(2)}) collective-permute-start(bf16[768,128]{1,0:T(8,128)(2,1)S(1)} %get-tuple-element.48), channel_id=1, source_target_pairs={{4,6},{5,7},{6,4},{7,5},{12,14},{13,15},{14,12},{15,13},{20,22},{2... | collective-permute-start | bytes 589832 | tf_op jit(solution)/shard_map/ppermute | solution.py:203
  60.8 8.5 %collective-permute-start.17 = (bf16[768,128]{1,0:T(8,128)(2,1)S(1)}, bf16[768,128]{1,0:T(8,128)(2,1)S(1)}, u32[]{:S(2)}, u32[]{:S(2)}) collective-permute-start(bf16[768,128]{1,0:T(8,128)(2,1)S(1)} %get-tuple-element.49), channel_id=1, source_target_pairs={{4,5},{5,4},{6,7},{7,6},{12,13},{13,12},{14,15},{15,14},{20,21},{2... | collective-permute-start | bytes 589832 | tf_op jit(solution)/shard_map/ppermute | solution.py:203
  69.4 1.5 %collective-permute-start.18 = (f32[384,128]{1,0:T(8,128)S(1)}, f32[384,128]{1,0:T(8,128)S(1)}, u32[]{:S(2)}, u32[]{:S(2)}) collective-permute-start(f32[384,128]{1,0:T(8,128)S(1)} %get-tuple-element.51), channel_id=1, source_target_pairs={{0,4},{4,0},{8,12},{12,8},{16,20},{20,16},{24,28},{28,24},{1,5},{5... | collective-permute-start | bytes 589832 | tf_op jit(solution)/shard_map/ppermute | solution.py:34
  71.2 3.5 %collective-permute-start.19 = (bf16[128,384]{1,0:T(8,128)(2,1)S(1)}, bf16[128,384]{1,0:T(8,128)(2,1)S(1)}, u32[]{:S(2)}, u32[]{:S(2)}) collective-permute-start(bf16[128,384]{1,0:T(8,128)(2,1)S(1)} %get-tuple-element.57), channel_id=1, source_target_pairs={{0,4},{4,0},{8,12},{12,8},{16,20},{20,16},{24,28},{28,24},{1,5},{5... | collective-permute-start | bytes 294920 | tf_op jit(solution)/shard_map/ppermute | solution.py:34
  71.4 6.4 %collective-permute-start.20 = (bf16[128,384]{1,0:T(8,128)(2,1)S(1)}, bf16[128,384]{1,0:T(8,128)(2,1)S(1)}, u32[]{:S(2)}, u32[]{:S(2)}) collective-permute-start(bf16[128,384]{1,0:T(8,128)(2,1)S(1)} %get-tuple-element.58), channel_id=1, source_target_pairs={{4,8},{12,16},{20,24},{8,4},{16,12},{24,20},{5,9},{13,17},{21,25},... | collective-permute-start | bytes 294920 | tf_op jit(solution)/shard_map/ppermute | solution.py:292

commit v17 on v15

--- a/solution.py
+++ b/solution.py
@@ -142,7 +142,7 @@
     later, _ = lax.optimization_barrier((rotation, operator[0]))
     received += [exchanged(later, "domain", NEAR, CORE), exchanged(later, "domain", FAR, CORE)]
     passed, previous = [], []
-    for one, share in ((0, 21), (CORE, 19)):
+    for one, share in ((0, 21), (CORE, 18)):
         cut = states * share // 32
         outs = [shape(count, width, dtype=BF16) for count in (cut, states - cut)]
         pair = received[2 * one : 2 * one + 2][::-1]
@@ -194,11 +194,14 @@
     faces[:, columns:] = dot(pick[...], low).astype(BF16)
 
 
-def final_kernel(inner, faces, assembled, spread, inward, outward, out):
+def final_kernel(inner, faces, assembled, spread, inward, one_hop, two_hops, out):
     own, columns = inner.shape
+    domain, count = lax.axis_index("domain"), lax.axis_size("domain")
     first = core() == 0
+    outward = jnp.where(lax.div(domain + 1, 2) == count // 4, two_hops[...], one_hop[...])
+    outward = jnp.where((domain == 0) | (domain == count - 1), jnp.zeros_like(outward), outward)
     incoming = jnp.where(first, inward[:, :columns], outward[:, :columns])
-    back = jnp.where(first, outward[...], inward[...])
+    back = jnp.where(first, outward, inward[...])
     extra = dot(back[:, columns:], faces[...])
     high, low = split(back[:, :columns].astype(F32) + extra[:, :columns] + extra[:, columns:])
     matrix = jnp.concatenate([assembled[:own, own:], spread[...], spread[...]], 1)
@@ -211,12 +214,11 @@
     shared, columns = pick.shape[0], 2 * width
     outs = [shape(rows, columns)] + [shape(shared, columns + shared, dtype=BF16)] * 2
     total, inward, outward = call(faces_kernel, outs, (mine, other, assembled, pick))
-    across = [(place, place + 1) for place in range(CORE, lax.axis_size("domain") - 1, 2)]
-    outward = lax.ppermute(outward, "domain", across + [(target, source) for source, target in across])
+    outward = [exchanged(outward, "domain", mask) for mask in (CORE | NEAR, CORE | NEAR | FAR)]
     inward = exchanged(inward, "domain", CORE)
     outs = [shape(rows, columns), shape(shared, 2 * columns, dtype=BF16)]
     inner, faces = call(inner_kernel, outs, (total, assembled, pick))
-    return call(final_kernel, outs[:1], (inner, faces, assembled, spread, inward, outward))[0]
+    return call(final_kernel, outs[:1], (inner, faces, assembled, spread, inward, *outward))[0]
 
 
 def finish_any(rotated, cell_matrices, cell_nodes, face_map):

time: 70.2 us -> 71.6 us (1.020)
  waiting for transfers between devices: 35.2 us -> 37.3 us
    ppermute x14 -> x16, waiting for transfers between devices: 32.7 us -> 37.3 us  [exchanged(): lax.ppermute(value, axis, [(source, source ^ mask) for source in sources...]
    ppermute x1 -> x0, starting transfers between devices: 3.37 us -> none  [finish_square(): lax.ppermute(outward, 'domain', across + [(target, source) for source, ta...]
    ppermute x14 -> x16, starting transfers between devices: 18.8 us -> 21.6 us  [exchanged(): lax.ppermute(value, axis, [(source, source ^ mask) for source in sources...]
    ppermute x1 -> x0, waiting for transfers between devices: 2.53 us -> none  [finish_square(): lax.ppermute(outward, 'domain', across + [(target, source) for source, ta...]
  transfers between devices with their start and end apart: 15 -> 16, of which waited for: 9 -> 9; matrix products, arithmetic and copies ran while one was open for 0% -> 0% of each run, Pallas kernels for 7% -> 7%
where the time goes in v17:
time: 71.6 us; the launch traced here: 70.9 us
  waiting for transfers between devices  37.3 us (52%)
  starting transfers between devices  21.6 us (30%)
  Pallas kernels  8.68 us (12%)
  local copies, waits for them, and re-layouts  3.13 us (4%)
    ppermute x16, waiting for transfers between devices, exchanged(): lax.ppermute(value, axis, [(source, source ^ mask) for source in sources...  37.3 us
    ppermute x16, starting transfers between devices, exchanged(): lax.ppermute(value, axis, [(source, source ^ mask) for source in sources...  21.6 us
    pallas_call x10, Pallas kernels, call(): pl.pallas_call(body, out_shape=outs, in_specs=[pl.BlockSpec(memory_space=...  8.68 us
    unnamed x14, local copies, waits for them, and re-layouts  3.13 us
  transfers between devices with their start and end apart: 16, of which 9 were waited for; matrix products, arithmetic and copies ran while one was open for 0% of the time, Pallas kernels for 7%

profile of v17, /device:TPU:1, one launch (start us, length us, event | category | flops | bytes accessed | tf_op | source)
XLA Modules:
  0.0 70.9 jit_solution(2384801683233258431)
XLA Ops:
  0.0 0.1 collective-permute-start
  0.1 0.7 %collective-permute-start.1 = (bf16[4096,128]{1,0:T(8,128)(2,1)}, bf16[4096,128]{1,0:T(8,128)(2,1)S(1)}, u32[]{:S(2)}, u32[]{:S(2)}) collective-permute-start(bf16[4096,128]{1,0:T(8,128)(2,1)} %refs_2_.1), channel_id=1, source_target_pairs={{0,16},{8,24},{16,0},{24,8},{1,17},{9,25},{17,1},{25,9},{2,18},{10... | collective-permute-start | bytes 3145736 | tf_op jit(solution)/shard_map/ppermute | solution.py:34
  0.8 0.7 %collective-permute-start.2 = (bf16[4096,128]{1,0:T(8,128)(2,1)}, bf16[4096,128]{1,0:T(8,128)(2,1)S(1)}, u32[]{:S(2)}, u32[]{:S(2)}) collective-permute-start(bf16[4096,128]{1,0:T(8,128)(2,1)} %refs_2_.1), channel_id=1, source_target_pairs={{0,8},{8,0},{16,24},{24,16},{1,9},{9,1},{17,25},{25,17},{2,10},{10... | collective-permute-start | bytes 3145736 | tf_op jit(solution)/shard_map/ppermute | solution.py:34
  1.5 4.4 %collective-permute-done.refs_1_ = bf16[384,4096]{1,0:T(8,128)(2,1)S(1)} collective-permute-done((bf16[384,4096]{1,0:T(8,128)(2,1)}, bf16[384,4096]{1,0:T(8,128)(2,1)S(1)}, u32[]{:S(2)}, u32[]{:S(2)}) %collective-permute-start) | collective-permute-done | bytes 3145760 | tf_op jit(solution)/shard_map/ppermute | solution.py:34
  5.9 0.0 copy-start
  5.9 1.9 %copy-done = bf16[384,4096]{1,0:T(8,128)(2,1)S(1)} copy-done((bf16[384,4096]{1,0:T(8,128)(2,1)S(1)}, bf16[384,4096]{1,0:T(8,128)(2,1)}, u32[]{:S(2)}) %copy-start) | copy-done | bytes 3145752
  7.8 0.0 copy-start.2
  7.8 1.2 %copy-done.2 = bf16[4096,128]{1,0:T(8,128)(2,1)S(1)} copy-done((bf16[4096,128]{1,0:T(8,128)(2,1)S(1)}, bf16[4096,128]{1,0:T(8,128)(2,1)}, u32[]{:S(2)}) %copy-start.2) | copy-done | bytes 1048600
  9.0 0.0 copy-start.4
  9.0 0.0 copy-start.5
  9.0 0.0 copy-start.6
  9.0 0.0 copy-start.3
  9.0 1.8 %shard_map.56.refs_3_.refs_6_ = f32[768,128]{1,0:T(8,128)S(1)} custom-call(bf16[384,4096]{1,0:T(8,128)(2,1)S(1)} %copy-done, bf16[384,4096]{1,0:T(8,128)(2,1)S(1)} %collective-permute-done.refs_1_, bf16[4096,128]{1,0:T(8,128)(2,1)S(1)} %copy-done.2), custom_call_target="tpu_custom_call" | custom-call | bytes 1024 | tf_op jit(solution)/shard_map/pallas_call | solution.py:44
  10.8 0.0 copy-start.1
  10.8 0.0 copy-done.4
  10.8 0.0 copy-done.5
  10.8 0.0 copy-done.6
  10.8 0.7 shard_map.57
  11.5 0.0 copy-done.3
  11.5 4.4 %collective-permute-start.5 = (bf16[4096,128]{1,0:T(8,128)(2,1)S(1)}, bf16[4096,128]{1,0:T(8,128)(2,1)S(1)}, u32[]{:S(2)}, u32[]{:S(2)}) collective-permute-start(bf16[4096,128]{1,0:T(8,128)(2,1)S(1)} %copy-done.3), channel_id=1, source_target_pairs={{4,20},{12,28},{20,4},{28,12},{5,21},{13,29},{21,5},{29,13},{6,22}... | collective-permute-start | bytes 3145736 | tf_op jit(solution)/shard_map/ppermute | solution.py:34
  16.0 3.1 %collective-permute-start.6 = (bf16[4096,128]{1,0:T(8,128)(2,1)S(1)}, bf16[4096,128]{1,0:T(8,128)(2,1)S(1)}, u32[]{:S(2)}, u32[]{:S(2)}) collective-permute-start(bf16[4096,128]{1,0:T(8,128)(2,1)S(1)} %copy-done.3), channel_id=1, source_target_pairs={{4,12},{12,4},{20,28},{28,20},{5,13},{13,5},{21,29},{29,21},{6,14}... | collective-permute-start | bytes 3145736 | tf_op jit(solution)/shard_map/ppermute | solution.py:34
  19.1 0.0 collective-permute-done.1.refs_0_.refs_3_
  19.1 0.0 collective-permute-done.2.refs_1_.refs_2_
  19.2 0.7 collective-permute-start.3
  19.9 11.0 %collective-permute-done.5.refs_0_.refs_5_ = bf16[4096,128]{1,0:T(8,128)(2,1)S(1)} collective-permute-done((bf16[4096,128]{1,0:T(8,128)(2,1)S(1)}, bf16[4096,128]{1,0:T(8,128)(2,1)S(1)}, u32[]{:S(2)}, u32[]{:S(2)}) %collective-permute-start.5) | collective-permute-done | bytes 1048608 | tf_op jit(solution)/shard_map/ppermute | solution.py:34
  30.8 2.9 %collective-permute-done.6.refs_1_.refs_4_ = bf16[4096,128]{1,0:T(8,128)(2,1)S(1)} collective-permute-done((bf16[4096,128]{1,0:T(8,128)(2,1)S(1)}, bf16[4096,128]{1,0:T(8,128)(2,1)S(1)}, u32[]{:S(2)}, u32[]{:S(2)}) %collective-permute-start.6) | collective-permute-done | bytes 1048608 | tf_op jit(solution)/shard_map/ppermute | solution.py:34
  33.8 0.4 shard_map.58
  34.2 1.9 %collective-permute-start.7 = (bf16[2304,128]{1,0:T(8,128)(2,1)S(1)}, bf16[2304,128]{1,0:T(8,128)(2,1)S(1)}, u32[]{:S(2)}, u32[]{:S(2)}) collective-permute-start(bf16[2304,128]{1,0:T(8,128)(2,1)S(1)} %get-tuple-element.30), channel_id=1, source_target_pairs={{4,20},{12,28},{20,4},{28,12},{5,21},{13,29},{21,5},{29,13},{6,22}... | collective-permute-start | bytes 1769480 | tf_op jit(solution)/shard_map/ppermute | solution.py:34
  36.1 2.6 %collective-permute-start.8 = (bf16[1792,128]{1,0:T(8,128)(2,1)S(1)}, bf16[1792,128]{1,0:T(8,128)(2,1)S(1)}, u32[]{:S(2)}, u32[]{:S(2)}) collective-permute-start(bf16[1792,128]{1,0:T(8,128)(2,1)S(1)} %get-tuple-element.31), channel_id=1, source_target_pairs={{4,12},{12,4},{20,28},{28,20},{5,13},{13,5},{21,29},{29,21},{6,14}... | collective-permute-start | bytes 1376264 | tf_op jit(solution)/shard_map/ppermute | solution.py:34
  38.7 0.7 collective-permute-start.4
  39.4 0.0 copy-done.1
  39.4 1.8 %shard_map.59 = (f32[768,128]{1,0:T(8,128)S(1)}, f32[768,128]{1,0:T(8,128)S(1)}) custom-call(bf16[384,4096]{1,0:T(8,128)(2,1)S(1)} %copy-done.1, bf16[384,4096]{1,0:T(8,128)(2,1)S(1)} %collective-permute-done.refs_1_, bf16[4096,128]{1,0:T(8,128)(2,1)S(1)} %collective-permute-done.2.refs_1_.refs_2_, ...), custom_call_target="tpu_custom_call" | custom-call | bytes 1024 | tf_op jit(solution)/shard_map/pallas_call | solution.py:44
  41.2 0.0 collective-permute-done.4.refs_3_
  41.3 0.0 collective-permute-done.3.refs_2_
  41.3 4.4 %collective-permute-done.8.refs_5_ = bf16[1792,128]{1,0:T(8,128)(2,1)S(1)} collective-permute-done((bf16[1792,128]{1,0:T(8,128)(2,1)S(1)}, bf16[1792,128]{1,0:T(8,128)(2,1)S(1)}, u32[]{:S(2)}, u32[]{:S(2)}) %collective-permute-start.8) | collective-permute-done | bytes 458784 | tf_op jit(solution)/shard_map/ppermute | solution.py:34
  45.6 0.0 collective-permute-done.7.refs_4_
  45.6 1.9 %shard_map.60 = (f32[768,128]{1,0:T(8,128)S(1)}, bf16[768,128]{1,0:T(8,128)(2,1)S(1)}, bf16[768,128]{1,0:T(8,128)(2,1)S(1)}, bf16[768,128]{1,0:T(8,128)(2,1)S(1)}) custom-call(bf16[384,4096]{1,0:T(8,128)(2,1)S(1)} %copy-done.1, bf16[384,4096]{1,0:T(8,128)(2,1)S(1)} %collective-permute-done.refs_1_, bf16[2688,128]{1,0:T(8,128)(2,1)S(1)} %collective-permute-done.3.refs_2_, ...), custom_call_target="tpu_custom_call" | custom-call | bytes 1024 | tf_op jit(solution)/shard_map/pallas_call | solution.py:44
  47.6 2.9 %collective-permute-start.10 = (bf16[768,128]{1,0:T(8,128)(2,1)S(1)}, bf16[768,128]{1,0:T(8,128)(2,1)S(1)}, u32[]{:S(2)}, u32[]{:S(2)}) collective-permute-start(bf16[768,128]{1,0:T(8,128)(2,1)S(1)} %get-tuple-element.36), channel_id=1, source_target_pairs={{0,3},{1,2},{2,1},{3,0},{4,7},{5,6},{6,5},{7,4},{8,11},{9,10},{10,... | collective-permute-start | bytes 589832 | tf_op jit(solution)/shard_map/ppermute | solution.py:34
  50.4 0.0 collective-permute-start.11
  50.4 0.7 %collective-permute-start.9 = (bf16[768,128]{1,0:T(8,128)(2,1)S(1)}, bf16[768,128]{1,0:T(8,128)(2,1)S(1)}, u32[]{:S(2)}, u32[]{:S(2)}) collective-permute-start(bf16[768,128]{1,0:T(8,128)(2,1)S(1)} %get-tuple-element.35), channel_id=1, source_target_pairs={{0,1},{1,0},{2,3},{3,2},{4,5},{5,4},{6,7},{7,6},{8,9},{9,8},{10,11... | collective-permute-start | bytes 589832 | tf_op jit(solution)/shard_map/ppermute | solution.py:34
  51.2 3.0 %collective-permute-done.10.refs_2_ = bf16[768,128]{1,0:T(8,128)(2,1)S(1)} collective-permute-done((bf16[768,128]{1,0:T(8,128)(2,1)S(1)}, bf16[768,128]{1,0:T(8,128)(2,1)S(1)}, u32[]{:S(2)}, u32[]{:S(2)}) %collective-permute-start.10) | collective-permute-done | bytes 196640 | tf_op jit(solution)/shard_map/ppermute | solution.py:34
  54.2 5.6 %collective-permute-done.11.refs_3_ = bf16[768,128]{1,0:T(8,128)(2,1)S(1)} collective-permute-done((bf16[768,128]{1,0:T(8,128)(2,1)S(1)}, bf16[768,128]{1,0:T(8,128)(2,1)S(1)}, u32[]{:S(2)}, u32[]{:S(2)}) %collective-permute-start.11) | collective-permute-done | bytes 196640 | tf_op jit(solution)/shard_map/ppermute | solution.py:34
  59.8 0.0 collective-permute-done.9.refs_1_
  59.8 0.1 shard_map.61
  59.9 0.1 collective-permute-start.12
  60.0 1.4 %collective-permute-done.12.refs_1_ = f32[384,128]{1,0:T(8,128)S(1)} collective-permute-done((f32[384,128]{1,0:T(8,128)S(1)}, f32[384,128]{1,0:T(8,128)S(1)}, u32[]{:S(2)}, u32[]{:S(2)}) %collective-permute-start.12) | collective-permute-done | bytes 196640 | tf_op jit(solution)/shard_map/ppermute | solution.py:34
  61.4 0.3 shard_map.62
  61.7 0.2 collective-permute-start.13
  61.9 1.5 %collective-permute-start.14 = (bf16[128,384]{1,0:T(8,128)(2,1)S(1)}, bf16[128,384]{1,0:T(8,128)(2,1)S(1)}, u32[]{:S(2)}, u32[]{:S(2)}) collective-permute-start(bf16[128,384]{1,0:T(8,128)(2,1)S(1)} %get-tuple-element.46), channel_id=1, source_target_pairs={{0,12},{4,8},{8,4},{12,0},{16,28},{20,24},{24,20},{28,16},{1,13},{... | collective-permute-start | bytes 294920 | tf_op jit(solution)/shard_map/ppermute | solution.py:34
  63.4 1.2 %collective-permute-start.15 = (bf16[128,384]{1,0:T(8,128)(2,1)S(1)}, bf16[128,384]{1,0:T(8,128)(2,1)S(1)}, u32[]{:S(2)}, u32[]{:S(2)}) collective-permute-start(bf16[128,384]{1,0:T(8,128)(2,1)S(1)} %get-tuple-element.46), channel_id=1, source_target_pairs={{0,28},{4,24},{8,20},{12,16},{16,12},{20,8},{24,4},{28,0},{1,29},{... | collective-permute-start | bytes 294920 | tf_op jit(solution)/shard_map/ppermute | solution.py:34
  64.6 0.5 shard_map.63
  65.1 0.0 collective-permute-done.13.refs_4_
  65.1 1.6 %collective-permute-done.14.refs_5_ = bf16[128,384]{1,0:T(8,128)(2,1)S(1)} collective-permute-done((bf16[128,384]{1,0:T(8,128)(2,1)S(1)}, bf16[128,384]{1,0:T(8,128)(2,1)S(1)}, u32[]{:S(2)}, u32[]{:S(2)}) %collective-permute-start.14) | collective-permute-done | bytes 98336 | tf_op jit(solution)/shard_map/ppermute | solution.py:34
  66.7 3.1 %collective-permute-done.15.refs_6_ = bf16[128,384]{1,0:T(8,128)(2,1)S(1)} collective-permute-done((bf16[128,384]{1,0:T(8,128)(2,1)S(1)}, bf16[128,384]{1,0:T(8,128)(2,1)S(1)}, u32[]{:S(2)}, u32[]{:S(2)}) %collective-permute-start.15) | collective-permute-done | bytes 98336 | tf_op jit(solution)/shard_map/ppermute | solution.py:34
  69.7 1.2 %shard_map.64 = f32[384,256]{1,0:T(8,128)} custom-call(f32[384,256]{1,0:T(8,128)S(1)} %get-tuple-element.42.refs_0_, bf16[128,512]{1,0:T(8,128)(2,1)S(1)} %get-tuple-element.43.refs_1_, bf16[512,512]{1,0:T(8,128)(2,1)S(1)} %get-tuple-element.28.refs_2_.refs_1_, bf16[384,128]{1,0:T(8,128)(2,1)S(1)} %get-tuple-element.44.refs_3_, ...), custom_call_target="tpu_custom_call" | custom-call | bytes 1024 | tf_op jit(solution)/shard_map/pallas_call | solution.py:44
  (1 shorter events, 0.0 us)
Async XLA Ops:
  0.0 5.9 %collective-permute-start = (bf16[384,4096]{1,0:T(8,128)(2,1)}, bf16[384,4096]{1,0:T(8,128)(2,1)S(1)}, u32[]{:S(2)}, u32[]{:S(2)}) collective-permute-start(bf16[384,4096]{1,0:T(8,128)(2,1)} %refs_0_.7), channel_id=1, source_target_pairs={{0,4},{4,0},{8,12},{12,8},{16,20},{20,16},{24,28},{28,24},{1,5},{5... | collective-permute-start | bytes 9437192 | tf_op jit(solution)/shard_map/ppermute | solution.py:34
  0.1 19.0 %collective-permute-start.1 = (bf16[4096,128]{1,0:T(8,128)(2,1)}, bf16[4096,128]{1,0:T(8,128)(2,1)S(1)}, u32[]{:S(2)}, u32[]{:S(2)}) collective-permute-start(bf16[4096,128]{1,0:T(8,128)(2,1)} %refs_2_.1), channel_id=1, source_target_pairs={{0,16},{8,24},{16,0},{24,8},{1,17},{9,25},{17,1},{25,9},{2,18},{10... | collective-permute-start | bytes 3145736 | tf_op jit(solution)/shard_map/ppermute | solution.py:34
  0.8 18.3 %collective-permute-start.2 = (bf16[4096,128]{1,0:T(8,128)(2,1)}, bf16[4096,128]{1,0:T(8,128)(2,1)S(1)}, u32[]{:S(2)}, u32[]{:S(2)}) collective-permute-start(bf16[4096,128]{1,0:T(8,128)(2,1)} %refs_2_.1), channel_id=1, source_target_pairs={{0,8},{8,0},{16,24},{24,16},{1,9},{9,1},{17,25},{25,17},{2,10},{10... | collective-permute-start | bytes 3145736 | tf_op jit(solution)/shard_map/ppermute | solution.py:34
  5.9 1.9 %copy-start = (bf16[384,4096]{1,0:T(8,128)(2,1)S(1)}, bf16[384,4096]{1,0:T(8,128)(2,1)}, u32[]{:S(2)}) copy-start(bf16[384,4096]{1,0:T(8,128)(2,1)} %refs_0_.7) | copy-start | bytes 9437188
  7.8 1.2 %copy-start.2 = (bf16[4096,128]{1,0:T(8,128)(2,1)S(1)}, bf16[4096,128]{1,0:T(8,128)(2,1)}, u32[]{:S(2)}) copy-start(bf16[4096,128]{1,0:T(8,128)(2,1)} %refs_2_.1) | copy-start | bytes 3145732
  9.0 1.8 %copy-start.4 = (bf16[1,512,512]{2,1,0:T(8,128)(2,1)S(1)}, bf16[1,512,512]{2,1,0:T(8,128)(2,1)}, u32[]{:S(2)}) copy-start(bf16[1,512,512]{2,1,0:T(8,128)(2,1)} %refs_0_.5) | copy-start | bytes 1572868
  9.0 1.8 %copy-start.5 = (s32[1,512]{1,0:T(1,128)S(1)}, s32[1,512]{1,0:T(1,128)}, u32[]{:S(2)}) copy-start(s32[1,512]{1,0:T(1,128)} %refs_1_.1) | copy-start | bytes 6148
  9.0 1.8 %copy-start.6 = (s32[128]{0:T(128)S(1)}, s32[128]{0:T(128)}, u32[]{:S(2)}) copy-start(s32[128]{0:T(128)} %param.9) | copy-start | bytes 1540
  9.0 2.5 %copy-start.3 = (bf16[4096,128]{1,0:T(8,128)(2,1)S(1)}, bf16[4096,128]{1,0:T(8,128)(2,1)}, u32[]{:S(2)}) copy-start(bf16[4096,128]{1,0:T(8,128)(2,1)} %refs_2_.1) | copy-start | bytes 3145732
  10.8 28.7 %copy-start.1 = (bf16[384,4096]{1,0:T(8,128)(2,1)S(1)}, bf16[384,4096]{1,0:T(8,128)(2,1)}, u32[]{:S(2)}) copy-start(bf16[384,4096]{1,0:T(8,128)(2,1)} %refs_0_.7) | copy-start | bytes 9437188
  11.5 19.3 %collective-permute-start.5 = (bf16[4096,128]{1,0:T(8,128)(2,1)S(1)}, bf16[4096,128]{1,0:T(8,128)(2,1)S(1)}, u32[]{:S(2)}, u32[]{:S(2)}) collective-permute-start(bf16[4096,128]{1,0:T(8,128)(2,1)S(1)} %copy-done.3), channel_id=1, source_target_pairs={{4,20},{12,28},{20,4},{28,12},{5,21},{13,29},{21,5},{29,13},{6,22}... | collective-permute-start | bytes 3145736 | tf_op jit(solution)/shard_map/ppermute | solution.py:34
  16.0 17.8 %collective-permute-start.6 = (bf16[4096,128]{1,0:T(8,128)(2,1)S(1)}, bf16[4096,128]{1,0:T(8,128)(2,1)S(1)}, u32[]{:S(2)}, u32[]{:S(2)}) collective-permute-start(bf16[4096,128]{1,0:T(8,128)(2,1)S(1)} %copy-done.3), channel_id=1, source_target_pairs={{4,12},{12,4},{20,28},{28,20},{5,13},{13,5},{21,29},{29,21},{6,14}... | collective-permute-start | bytes 3145736 | tf_op jit(solution)/shard_map/ppermute | solution.py:34
  19.2 22.1 %collective-permute-start.3 = (bf16[2688,128]{1,0:T(8,128)(2,1)S(1)}, bf16[2688,128]{1,0:T(8,128)(2,1)S(1)}, u32[]{:S(2)}, u32[]{:S(2)}) collective-permute-start(bf16[2688,128]{1,0:T(8,128)(2,1)S(1)} %get-tuple-element.26), channel_id=1, source_target_pairs={{0,16},{8,24},{16,0},{24,8},{1,17},{9,25},{17,1},{25,9},{2,18},{10... | collective-permute-start | bytes 2064392 | tf_op jit(solution)/shard_map/ppermute | solution.py:34
  34.2 11.4 %collective-permute-start.7 = (bf16[2304,128]{1,0:T(8,128)(2,1)S(1)}, bf16[2304,128]{1,0:T(8,128)(2,1)S(1)}, u32[]{:S(2)}, u32[]{:S(2)}) collective-permute-start(bf16[2304,128]{1,0:T(8,128)(2,1)S(1)} %get-tuple-element.30), channel_id=1, source_target_pairs={{4,20},{12,28},{20,4},{28,12},{5,21},{13,29},{21,5},{29,13},{6,22}... | collective-permute-start | bytes 1769480 | tf_op jit(solution)/shard_map/ppermute | solution.py:34
  36.1 9.5 %collective-permute-start.8 = (bf16[1792,128]{1,0:T(8,128)(2,1)S(1)}, bf16[1792,128]{1,0:T(8,128)(2,1)S(1)}, u32[]{:S(2)}, u32[]{:S(2)}) collective-permute-start(bf16[1792,128]{1,0:T(8,128)(2,1)S(1)} %get-tuple-element.31), channel_id=1, source_target_pairs={{4,12},{12,4},{20,28},{28,20},{5,13},{13,5},{21,29},{29,21},{6,14}... | collective-permute-start | bytes 1376264 | tf_op jit(solution)/shard_map/ppermute | solution.py:34
  38.7 2.5 %collective-permute-start.4 = (bf16[1408,128]{1,0:T(8,128)(2,1)S(1)}, bf16[1408,128]{1,0:T(8,128)(2,1)S(1)}, u32[]{:S(2)}, u32[]{:S(2)}) collective-permute-start(bf16[1408,128]{1,0:T(8,128)(2,1)S(1)} %get-tuple-element.27.refs_2_), channel_id=1, source_target_pairs={{0,8},{8,0},{16,24},{24,16},{1,9},{9,1},{17,25},{25,17},{2,10},{10... | collective-permute-start | bytes 1081352 | tf_op jit(solution)/shard_map/ppermute | solution.py:34
  47.6 6.6 %collective-permute-start.10 = (bf16[768,128]{1,0:T(8,128)(2,1)S(1)}, bf16[768,128]{1,0:T(8,128)(2,1)S(1)}, u32[]{:S(2)}, u32[]{:S(2)}) collective-permute-start(bf16[768,128]{1,0:T(8,128)(2,1)S(1)} %get-tuple-element.36), channel_id=1, source_target_pairs={{0,3},{1,2},{2,1},{3,0},{4,7},{5,6},{6,5},{7,4},{8,11},{9,10},{10,... | collective-permute-start | bytes 589832 | tf_op jit(solution)/shard_map/ppermute | solution.py:34
  50.4 9.3 %collective-permute-start.11 = (bf16[768,128]{1,0:T(8,128)(2,1)S(1)}, bf16[768,128]{1,0:T(8,128)(2,1)S(1)}, u32[]{:S(2)}, u32[]{:S(2)}) collective-permute-start(bf16[768,128]{1,0:T(8,128)(2,1)S(1)} %get-tuple-element.37), channel_id=1, source_target_pairs={{0,2},{1,3},{2,0},{3,1},{4,6},{5,7},{6,4},{7,5},{8,10},{9,11},{10,... | collective-permute-start | bytes 589832 | tf_op jit(solution)/shard_map/ppermute | solution.py:34
  50.4 9.3 %collective-permute-start.9 = (bf16[768,128]{1,0:T(8,128)(2,1)S(1)}, bf16[768,128]{1,0:T(8,128)(2,1)S(1)}, u32[]{:S(2)}, u32[]{:S(2)}) collective-permute-start(bf16[768,128]{1,0:T(8,128)(2,1)S(1)} %get-tuple-element.35), channel_id=1, source_target_pairs={{0,1},{1,0},{2,3},{3,2},{4,5},{5,4},{6,7},{7,6},{8,9},{9,8},{10,11... | collective-permute-start | bytes 589832 | tf_op jit(solution)/shard_map/ppermute | solution.py:34
  59.9 1.5 %collective-permute-start.12 = (f32[384,128]{1,0:T(8,128)S(1)}, f32[384,128]{1,0:T(8,128)S(1)}, u32[]{:S(2)}, u32[]{:S(2)}) collective-permute-start(f32[384,128]{1,0:T(8,128)S(1)} %get-tuple-element.39), channel_id=1, source_target_pairs={{0,4},{4,0},{8,12},{12,8},{16,20},{20,16},{24,28},{28,24},{1,5},{5... | collective-permute-start | bytes 589832 | tf_op jit(solution)/shard_map/ppermute | solution.py:34
  61.7 3.4 %collective-permute-start.13 = (bf16[128,384]{1,0:T(8,128)(2,1)S(1)}, bf16[128,384]{1,0:T(8,128)(2,1)S(1)}, u32[]{:S(2)}, u32[]{:S(2)}) collective-permute-start(bf16[128,384]{1,0:T(8,128)(2,1)S(1)} %get-tuple-element.45), channel_id=1, source_target_pairs={{0,4},{4,0},{8,12},{12,8},{16,20},{20,16},{24,28},{28,24},{1,5},{5... | collective-permute-start | bytes 294920 | tf_op jit(solution)/shard_map/ppermute | solution.py:34
  61.9 4.8 %collective-permute-start.14 = (bf16[128,384]{1,0:T(8,128)(2,1)S(1)}, bf16[128,384]{1,0:T(8,128)(2,1)S(1)}, u32[]{:S(2)}, u32[]{:S(2)}) collective-permute-start(bf16[128,384]{1,0:T(8,128)(2,1)S(1)} %get-tuple-element.46), channel_id=1, source_target_pairs={{0,12},{4,8},{8,4},{12,0},{16,28},{20,24},{24,20},{28,16},{1,13},{... | collective-permute-start | bytes 294920 | tf_op jit(solution)/shard_map/ppermute | solution.py:34
  63.4 6.4 %collective-permute-start.15 = (bf16[128,384]{1,0:T(8,128)(2,1)S(1)}, bf16[128,384]{1,0:T(8,128)(2,1)S(1)}, u32[]{:S(2)}, u32[]{:S(2)}) collective-permute-start(bf16[128,384]{1,0:T(8,128)(2,1)S(1)} %get-tuple-element.46), channel_id=1, source_target_pairs={{0,28},{4,24},{8,20},{12,16},{16,12},{20,8},{24,4},{28,0},{1,29},{... | collective-permute-start | bytes 294920 | tf_op jit(solution)/shard_map/ppermute | solution.py:34

commit v18 on v17

--- a/solution.py
+++ b/solution.py
@@ -164,25 +164,16 @@
     return lax.psum_scatter(dot(wavefunctions, columns), "band", scatter_dimension=1, tiled=True)
 
 
-def faces_kernel(mine, other, assembled, pick, total, inward, outward):
+def faces_kernel(mine, other, assembled, pick, total, faces, onward):
     own, width = mine.shape
     columns = 2 * width
     first = core() == 0
     for side, half in enumerate((jnp.where(first, mine[...], other[...]), jnp.where(first, other[...], mine[...]))):
         total[:, side * width : (side + 1) * width] = half
     high, low = split(total[...])
-    faces = dot(pick[...], high).astype(BF16)
-    onward = (dot(assembled[own:, :own], high) + dot(assembled[own:, :own], low)).astype(BF16)
-    corner = assembled[own:, own:]
-
-    def store(forward, backward):
-        forward[:, :columns] = onward
-        forward[:, columns:] = corner
-        backward[:, :columns] = faces
-        backward[:, columns:] = corner
-
-    pl.when(first)(lambda: store(inward, outward))
-    pl.when(jnp.logical_not(first))(lambda: store(outward, inward))
+    faces[...] = dot(pick[...], high).astype(BF16)
+    onward[:, :columns] = (dot(assembled[own:, :own], high) + dot(assembled[own:, :own], low)).astype(BF16)
+    onward[:, columns:] = assembled[own:, own:]
 
 
 def inner_kernel(total, assembled, pick, out, faces):
@@ -194,31 +185,32 @@
     faces[:, columns:] = dot(pick[...], low).astype(BF16)
 
 
-def final_kernel(inner, faces, assembled, spread, inward, one_hop, two_hops, out):
+def final_kernel(inner, faces, assembled, spread, incoming, back, out):
     own, columns = inner.shape
     domain, count = lax.axis_index("domain"), lax.axis_size("domain")
-    first = core() == 0
-    outward = jnp.where(lax.div(domain + 1, 2) == count // 4, two_hops[...], one_hop[...])
-    outward = jnp.where((domain == 0) | (domain == count - 1), jnp.zeros_like(outward), outward)
-    incoming = jnp.where(first, inward[:, :columns], outward[:, :columns])
-    back = jnp.where(first, outward, inward[...])
+    incoming = jnp.where(domain == count - 1, jnp.zeros(incoming.shape, BF16), incoming[...])
+    back = jnp.where(domain == 0, jnp.zeros(back.shape, BF16), back[...])
     extra = dot(back[:, columns:], faces[...])
     high, low = split(back[:, :columns].astype(F32) + extra[:, :columns] + extra[:, columns:])
     matrix = jnp.concatenate([assembled[:own, own:], spread[...], spread[...]], 1)
     out[...] = inner[...] + dot(matrix, jnp.concatenate([incoming, high, low], 0))
 
 
+def rotated(value, axis, steps):
+    count = lax.axis_size(axis)
+    return lax.ppermute(value, axis, [(source, (source + steps) % count) for source in range(count)])
+
+
 def finish_square(mine, other, operator):
     assembled, pick, spread = operator
     rows, width = mine.shape
     shared, columns = pick.shape[0], 2 * width
-    outs = [shape(rows, columns)] + [shape(shared, columns + shared, dtype=BF16)] * 2
-    total, inward, outward = call(faces_kernel, outs, (mine, other, assembled, pick))
-    outward = [exchanged(outward, "domain", mask) for mask in (CORE | NEAR, CORE | NEAR | FAR)]
-    inward = exchanged(inward, "domain", CORE)
+    outs = [shape(rows, columns), shape(shared, columns, dtype=BF16), shape(shared, columns + shared, dtype=BF16)]
+    total, faces, onward = call(faces_kernel, outs, (mine, other, assembled, pick))
+    back, incoming = rotated(onward, "domain", 1), rotated(faces, "domain", -1)
     outs = [shape(rows, columns), shape(shared, 2 * columns, dtype=BF16)]
     inner, faces = call(inner_kernel, outs, (total, assembled, pick))
-    return call(final_kernel, outs[:1], (inner, faces, assembled, spread, inward, *outward))[0]
+    return call(final_kernel, outs[:1], (inner, faces, assembled, spread, incoming, back))[0]
 
 
 def finish_any(rotated, cell_matrices, cell_nodes, face_map):

time: 71.6 us -> 68.4 us (0.955)
  starting transfers between devices: 21.6 us -> 19.9 us
  waiting for transfers between devices: 37.3 us -> 36.1 us
    ppermute x16 -> x13, waiting for transfers between devices: 37.3 us -> 32.7 us  [exchanged(): lax.ppermute(value, axis, [(source, source ^ mask) for source in sources...]
    ppermute x0 -> x2, waiting for transfers between devices: none -> 3.46 us  [rotated(): lax.ppermute(value, axis, [(source, (source + steps) % count) for source...]
    ppermute x16 -> x13, starting transfers between devices: 21.6 us -> 18.6 us  [exchanged(): lax.ppermute(value, axis, [(source, source ^ mask) for source in sources...]
    ppermute x0 -> x2, starting transfers between devices: none -> 1.3 us  [rotated(): lax.ppermute(value, axis, [(source, (source + steps) % count) for source...]
  transfers between devices with their start and end apart: 16 -> 15, of which waited for: 9 -> 8; matrix products, arithmetic and copies ran while one was open for 0% -> 0% of each run, Pallas kernels for 7% -> 8%
where the time goes in v18:
time: 68.4 us; the launch traced here: 68.1 us
  waiting for transfers between devices  36.1 us (53%)
  starting transfers between devices  19.9 us (29%)
  Pallas kernels  8.66 us (13%)
  local copies, waits for them, and re-layouts  3.13 us (5%)
    ppermute x13, waiting for transfers between devices, exchanged(): lax.ppermute(value, axis, [(source, source ^ mask) for source in sources...  32.7 us
    ppermute x13, starting transfers between devices, exchanged(): lax.ppermute(value, axis, [(source, source ^ mask) for source in sources...  18.6 us
    pallas_call x10, Pallas kernels, call(): pl.pallas_call(body, out_shape=outs, in_specs=[pl.BlockSpec(memory_space=...  8.66 us
    ppermute x2, waiting for transfers between devices, rotated(): lax.ppermute(value, axis, [(source, (source + steps) % count) for source...  3.46 us
    unnamed x14, local copies, waits for them, and re-layouts  3.13 us
  transfers between devices with their start and end apart: 15, of which 8 were waited for; matrix products, arithmetic and copies ran while one was open for 0% of the time, Pallas kernels for 8%

profile of v18, /device:TPU:1, one launch (start us, length us, event | category | flops | bytes accessed | tf_op | source)
XLA Modules:
  0.0 68.1 jit_solution(13068779531287710565)
XLA Ops:
  0.0 0.1 collective-permute-start
  0.1 0.7 %collective-permute-start.1 = (bf16[4096,128]{1,0:T(8,128)(2,1)}, bf16[4096,128]{1,0:T(8,128)(2,1)S(1)}, u32[]{:S(2)}, u32[]{:S(2)}) collective-permute-start(bf16[4096,128]{1,0:T(8,128)(2,1)} %refs_2_.1), channel_id=1, source_target_pairs={{0,16},{8,24},{16,0},{24,8},{1,17},{9,25},{17,1},{25,9},{2,18},{10... | collective-permute-start | bytes 3145736 | tf_op jit(solution)/shard_map/ppermute | solution.py:34
  0.8 0.7 %collective-permute-start.2 = (bf16[4096,128]{1,0:T(8,128)(2,1)}, bf16[4096,128]{1,0:T(8,128)(2,1)S(1)}, u32[]{:S(2)}, u32[]{:S(2)}) collective-permute-start(bf16[4096,128]{1,0:T(8,128)(2,1)} %refs_2_.1), channel_id=1, source_target_pairs={{0,8},{8,0},{16,24},{24,16},{1,9},{9,1},{17,25},{25,17},{2,10},{10... | collective-permute-start | bytes 3145736 | tf_op jit(solution)/shard_map/ppermute | solution.py:34
  1.5 4.4 %collective-permute-done.refs_1_ = bf16[384,4096]{1,0:T(8,128)(2,1)S(1)} collective-permute-done((bf16[384,4096]{1,0:T(8,128)(2,1)}, bf16[384,4096]{1,0:T(8,128)(2,1)S(1)}, u32[]{:S(2)}, u32[]{:S(2)}) %collective-permute-start) | collective-permute-done | bytes 3145760 | tf_op jit(solution)/shard_map/ppermute | solution.py:34
  5.9 0.0 copy-start
  5.9 1.9 %copy-done = bf16[384,4096]{1,0:T(8,128)(2,1)S(1)} copy-done((bf16[384,4096]{1,0:T(8,128)(2,1)S(1)}, bf16[384,4096]{1,0:T(8,128)(2,1)}, u32[]{:S(2)}) %copy-start) | copy-done | bytes 3145752
  7.8 0.0 copy-start.2
  7.8 1.2 %copy-done.2 = bf16[4096,128]{1,0:T(8,128)(2,1)S(1)} copy-done((bf16[4096,128]{1,0:T(8,128)(2,1)S(1)}, bf16[4096,128]{1,0:T(8,128)(2,1)}, u32[]{:S(2)}) %copy-start.2) | copy-done | bytes 1048600
  9.0 0.0 copy-start.4
  9.0 0.0 copy-start.5
  9.0 0.0 copy-start.6
  9.0 0.0 copy-start.3
  9.0 1.8 %shard_map.56.refs_3_.refs_6_ = f32[768,128]{1,0:T(8,128)S(1)} custom-call(bf16[384,4096]{1,0:T(8,128)(2,1)S(1)} %copy-done, bf16[384,4096]{1,0:T(8,128)(2,1)S(1)} %collective-permute-done.refs_1_, bf16[4096,128]{1,0:T(8,128)(2,1)S(1)} %copy-done.2), custom_call_target="tpu_custom_call" | custom-call | bytes 1024 | tf_op jit(solution)/shard_map/pallas_call | solution.py:44
  10.8 0.0 copy-start.1
  10.8 0.0 copy-done.4
  10.8 0.0 copy-done.5
  10.8 0.0 copy-done.6
  10.8 0.7 %shard_map.57 = (bf16[512,512]{1,0:T(8,128)(2,1)S(1)}, bf16[128,384]{1,0:T(8,128)(2,1)S(1)}, bf16[384,128]{1,0:T(8,128)(2,1)S(1)}) custom-call(bf16[1,512,512]{2,1,0:T(8,128)(2,1)S(1)} %copy-done.4, s32[1,512]{1,0:T(1,128)S(1)} %copy-done.5, s32[1,128]{1,0:T(1,128)S(1)} %bitcast.1, f32[768,128]{1,0:T(8,128)S(1)} %shard_map.56.refs_3_.refs_6_), custom_call_target="tpu_custom_call" | custom-call | bytes 1024 | tf_op jit(solution)/shard_map/pallas_call | solution.py:44
  11.5 0.0 copy-done.3
  11.5 4.4 %collective-permute-start.5 = (bf16[4096,128]{1,0:T(8,128)(2,1)S(1)}, bf16[4096,128]{1,0:T(8,128)(2,1)S(1)}, u32[]{:S(2)}, u32[]{:S(2)}) collective-permute-start(bf16[4096,128]{1,0:T(8,128)(2,1)S(1)} %copy-done.3), channel_id=1, source_target_pairs={{4,20},{12,28},{20,4},{28,12},{5,21},{13,29},{21,5},{29,13},{6,22}... | collective-permute-start | bytes 3145736 | tf_op jit(solution)/shard_map/ppermute | solution.py:34
  16.0 3.1 %collective-permute-start.6 = (bf16[4096,128]{1,0:T(8,128)(2,1)S(1)}, bf16[4096,128]{1,0:T(8,128)(2,1)S(1)}, u32[]{:S(2)}, u32[]{:S(2)}) collective-permute-start(bf16[4096,128]{1,0:T(8,128)(2,1)S(1)} %copy-done.3), channel_id=1, source_target_pairs={{4,12},{12,4},{20,28},{28,20},{5,13},{13,5},{21,29},{29,21},{6,14}... | collective-permute-start | bytes 3145736 | tf_op jit(solution)/shard_map/ppermute | solution.py:34
  19.1 0.0 collective-permute-done.1.refs_0_.refs_3_
  19.1 0.0 collective-permute-done.2.refs_1_.refs_2_
  19.2 0.7 %collective-permute-start.3 = (bf16[2688,128]{1,0:T(8,128)(2,1)S(1)}, bf16[2688,128]{1,0:T(8,128)(2,1)S(1)}, u32[]{:S(2)}, u32[]{:S(2)}) collective-permute-start(bf16[2688,128]{1,0:T(8,128)(2,1)S(1)} %get-tuple-element.26), channel_id=1, source_target_pairs={{0,16},{8,24},{16,0},{24,8},{1,17},{9,25},{17,1},{25,9},{2,18},{10... | collective-permute-start | bytes 2064392 | tf_op jit(solution)/shard_map/ppermute | solution.py:34
  19.9 11.0 %collective-permute-done.5.refs_0_.refs_5_ = bf16[4096,128]{1,0:T(8,128)(2,1)S(1)} collective-permute-done((bf16[4096,128]{1,0:T(8,128)(2,1)S(1)}, bf16[4096,128]{1,0:T(8,128)(2,1)S(1)}, u32[]{:S(2)}, u32[]{:S(2)}) %collective-permute-start.5) | collective-permute-done | bytes 1048608 | tf_op jit(solution)/shard_map/ppermute | solution.py:34
  30.8 2.9 %collective-permute-done.6.refs_1_.refs_4_ = bf16[4096,128]{1,0:T(8,128)(2,1)S(1)} collective-permute-done((bf16[4096,128]{1,0:T(8,128)(2,1)S(1)}, bf16[4096,128]{1,0:T(8,128)(2,1)S(1)}, u32[]{:S(2)}, u32[]{:S(2)}) %collective-permute-start.6) | collective-permute-done | bytes 1048608 | tf_op jit(solution)/shard_map/ppermute | solution.py:34
  33.8 0.4 shard_map.58
  34.2 1.9 %collective-permute-start.7 = (bf16[2304,128]{1,0:T(8,128)(2,1)S(1)}, bf16[2304,128]{1,0:T(8,128)(2,1)S(1)}, u32[]{:S(2)}, u32[]{:S(2)}) collective-permute-start(bf16[2304,128]{1,0:T(8,128)(2,1)S(1)} %get-tuple-element.30), channel_id=1, source_target_pairs={{4,20},{12,28},{20,4},{28,12},{5,21},{13,29},{21,5},{29,13},{6,22}... | collective-permute-start | bytes 1769480 | tf_op jit(solution)/shard_map/ppermute | solution.py:34
  36.1 2.6 %collective-permute-start.8 = (bf16[1792,128]{1,0:T(8,128)(2,1)S(1)}, bf16[1792,128]{1,0:T(8,128)(2,1)S(1)}, u32[]{:S(2)}, u32[]{:S(2)}) collective-permute-start(bf16[1792,128]{1,0:T(8,128)(2,1)S(1)} %get-tuple-element.31), channel_id=1, source_target_pairs={{4,12},{12,4},{20,28},{28,20},{5,13},{13,5},{21,29},{29,21},{6,14}... | collective-permute-start | bytes 1376264 | tf_op jit(solution)/shard_map/ppermute | solution.py:34
  38.7 0.7 %collective-permute-start.4 = (bf16[1408,128]{1,0:T(8,128)(2,1)S(1)}, bf16[1408,128]{1,0:T(8,128)(2,1)S(1)}, u32[]{:S(2)}, u32[]{:S(2)}) collective-permute-start(bf16[1408,128]{1,0:T(8,128)(2,1)S(1)} %get-tuple-element.27.refs_2_), channel_id=1, source_target_pairs={{0,8},{8,0},{16,24},{24,16},{1,9},{9,1},{17,25},{25,17},{2,10},{10... | collective-permute-start | bytes 1081352 | tf_op jit(solution)/shard_map/ppermute | solution.py:34
  39.4 0.0 copy-done.1
  39.4 1.8 %shard_map.59 = (f32[768,128]{1,0:T(8,128)S(1)}, f32[768,128]{1,0:T(8,128)S(1)}) custom-call(bf16[384,4096]{1,0:T(8,128)(2,1)S(1)} %copy-done.1, bf16[384,4096]{1,0:T(8,128)(2,1)S(1)} %collective-permute-done.refs_1_, bf16[4096,128]{1,0:T(8,128)(2,1)S(1)} %collective-permute-done.2.refs_1_.refs_2_, ...), custom_call_target="tpu_custom_call" | custom-call | bytes 1024 | tf_op jit(solution)/shard_map/pallas_call | solution.py:44
  41.2 0.0 collective-permute-done.4.refs_3_
  41.3 0.0 collective-permute-done.3.refs_2_
  41.3 4.4 %collective-permute-done.8.refs_5_ = bf16[1792,128]{1,0:T(8,128)(2,1)S(1)} collective-permute-done((bf16[1792,128]{1,0:T(8,128)(2,1)S(1)}, bf16[1792,128]{1,0:T(8,128)(2,1)S(1)}, u32[]{:S(2)}, u32[]{:S(2)}) %collective-permute-start.8) | collective-permute-done | bytes 458784 | tf_op jit(solution)/shard_map/ppermute | solution.py:34
  45.6 0.0 collective-permute-done.7.refs_4_
  45.6 1.9 %shard_map.60 = (f32[768,128]{1,0:T(8,128)S(1)}, bf16[768,128]{1,0:T(8,128)(2,1)S(1)}, bf16[768,128]{1,0:T(8,128)(2,1)S(1)}, bf16[768,128]{1,0:T(8,128)(2,1)S(1)}) custom-call(bf16[384,4096]{1,0:T(8,128)(2,1)S(1)} %copy-done.1, bf16[384,4096]{1,0:T(8,128)(2,1)S(1)} %collective-permute-done.refs_1_, bf16[2688,128]{1,0:T(8,128)(2,1)S(1)} %collective-permute-done.3.refs_2_, ...), custom_call_target="tpu_custom_call" | custom-call | bytes 1024 | tf_op jit(solution)/shard_map/pallas_call | solution.py:44
  47.6 2.9 %collective-permute-start.10 = (bf16[768,128]{1,0:T(8,128)(2,1)S(1)}, bf16[768,128]{1,0:T(8,128)(2,1)S(1)}, u32[]{:S(2)}, u32[]{:S(2)}) collective-permute-start(bf16[768,128]{1,0:T(8,128)(2,1)S(1)} %get-tuple-element.36), channel_id=1, source_target_pairs={{0,3},{1,2},{2,1},{3,0},{4,7},{5,6},{6,5},{7,4},{8,11},{9,10},{10,... | collective-permute-start | bytes 589832 | tf_op jit(solution)/shard_map/ppermute | solution.py:34
  50.4 0.0 collective-permute-start.11
  50.4 0.7 %collective-permute-start.9 = (bf16[768,128]{1,0:T(8,128)(2,1)S(1)}, bf16[768,128]{1,0:T(8,128)(2,1)S(1)}, u32[]{:S(2)}, u32[]{:S(2)}) collective-permute-start(bf16[768,128]{1,0:T(8,128)(2,1)S(1)} %get-tuple-element.35), channel_id=1, source_target_pairs={{0,1},{1,0},{2,3},{3,2},{4,5},{5,4},{6,7},{7,6},{8,9},{9,8},{10,11... | collective-permute-start | bytes 589832 | tf_op jit(solution)/shard_map/ppermute | solution.py:34
  51.2 3.0 %collective-permute-done.10.refs_2_ = bf16[768,128]{1,0:T(8,128)(2,1)S(1)} collective-permute-done((bf16[768,128]{1,0:T(8,128)(2,1)S(1)}, bf16[768,128]{1,0:T(8,128)(2,1)S(1)}, u32[]{:S(2)}, u32[]{:S(2)}) %collective-permute-start.10) | collective-permute-done | bytes 196640 | tf_op jit(solution)/shard_map/ppermute | solution.py:34
  54.2 5.6 %collective-permute-done.11.refs_3_ = bf16[768,128]{1,0:T(8,128)(2,1)S(1)} collective-permute-done((bf16[768,128]{1,0:T(8,128)(2,1)S(1)}, bf16[768,128]{1,0:T(8,128)(2,1)S(1)}, u32[]{:S(2)}, u32[]{:S(2)}) %collective-permute-start.11) | collective-permute-done | bytes 196640 | tf_op jit(solution)/shard_map/ppermute | solution.py:34
  59.8 0.0 collective-permute-done.9.refs_1_
  59.8 0.1 shard_map.61
  59.9 0.1 collective-permute-start.12
  60.0 1.4 %collective-permute-done.12.refs_1_ = f32[384,128]{1,0:T(8,128)S(1)} collective-permute-done((f32[384,128]{1,0:T(8,128)S(1)}, f32[384,128]{1,0:T(8,128)S(1)}, u32[]{:S(2)}, u32[]{:S(2)}) %collective-permute-start.12) | collective-permute-done | bytes 196640 | tf_op jit(solution)/shard_map/ppermute | solution.py:34
  61.4 0.3 shard_map.62
  61.7 1.3 %collective-permute-start.14 = (bf16[128,384]{1,0:T(8,128)(2,1)S(1)}, bf16[128,384]{1,0:T(8,128)(2,1)S(1)}, u32[]{:S(2)}, u32[]{:S(2)}) collective-permute-start(bf16[128,384]{1,0:T(8,128)(2,1)S(1)} %get-tuple-element.46), channel_id=1, source_target_pairs={{0,4},{4,8},{8,12},{12,16},{16,20},{20,24},{24,28},{28,0},{1,5},{5... | collective-permute-start | bytes 294920 | tf_op jit(solution)/shard_map/ppermute | solution.py:201
  63.0 0.0 collective-permute-start.13
  63.0 0.4 shard_map.63
  63.4 3.5 %collective-permute-done.13.refs_4_ = bf16[128,256]{1,0:T(8,128)(2,1)S(1)} collective-permute-done((bf16[128,256]{1,0:T(8,128)(2,1)S(1)}, bf16[128,256]{1,0:T(8,128)(2,1)S(1)}, u32[]{:S(2)}, u32[]{:S(2)}) %collective-permute-start.13) | collective-permute-done | bytes 65568 | tf_op jit(solution)/shard_map/ppermute | solution.py:201
  66.9 0.0 collective-permute-done.14.refs_5_
  66.9 1.2 %shard_map.64 = f32[384,256]{1,0:T(8,128)} custom-call(f32[384,256]{1,0:T(8,128)S(1)} %get-tuple-element.42.refs_0_, bf16[128,512]{1,0:T(8,128)(2,1)S(1)} %get-tuple-element.43.refs_1_, bf16[512,512]{1,0:T(8,128)(2,1)S(1)} %get-tuple-element.28.refs_2_.refs_1_, bf16[384,128]{1,0:T(8,128)(2,1)S(1)} %get-tuple-element.44.refs_3_, ...), custom_call_target="tpu_custom_call" | custom-call | bytes 1024 | tf_op jit(solution)/shard_map/pallas_call | solution.py:44
  (1 shorter events, 0.0 us)
Async XLA Ops:
  0.0 5.9 %collective-permute-start = (bf16[384,4096]{1,0:T(8,128)(2,1)}, bf16[384,4096]{1,0:T(8,128)(2,1)S(1)}, u32[]{:S(2)}, u32[]{:S(2)}) collective-permute-start(bf16[384,4096]{1,0:T(8,128)(2,1)} %refs_0_.7), channel_id=1, source_target_pairs={{0,4},{4,0},{8,12},{12,8},{16,20},{20,16},{24,28},{28,24},{1,5},{5... | collective-permute-start | bytes 9437192 | tf_op jit(solution)/shard_map/ppermute | solution.py:34
  0.1 19.0 %collective-permute-start.1 = (bf16[4096,128]{1,0:T(8,128)(2,1)}, bf16[4096,128]{1,0:T(8,128)(2,1)S(1)}, u32[]{:S(2)}, u32[]{:S(2)}) collective-permute-start(bf16[4096,128]{1,0:T(8,128)(2,1)} %refs_2_.1), channel_id=1, source_target_pairs={{0,16},{8,24},{16,0},{24,8},{1,17},{9,25},{17,1},{25,9},{2,18},{10... | collective-permute-start | bytes 3145736 | tf_op jit(solution)/shard_map/ppermute | solution.py:34
  0.8 18.3 %collective-permute-start.2 = (bf16[4096,128]{1,0:T(8,128)(2,1)}, bf16[4096,128]{1,0:T(8,128)(2,1)S(1)}, u32[]{:S(2)}, u32[]{:S(2)}) collective-permute-start(bf16[4096,128]{1,0:T(8,128)(2,1)} %refs_2_.1), channel_id=1, source_target_pairs={{0,8},{8,0},{16,24},{24,16},{1,9},{9,1},{17,25},{25,17},{2,10},{10... | collective-permute-start | bytes 3145736 | tf_op jit(solution)/shard_map/ppermute | solution.py:34
  5.9 1.9 %copy-start = (bf16[384,4096]{1,0:T(8,128)(2,1)S(1)}, bf16[384,4096]{1,0:T(8,128)(2,1)}, u32[]{:S(2)}) copy-start(bf16[384,4096]{1,0:T(8,128)(2,1)} %refs_0_.7) | copy-start | bytes 9437188
  7.8 1.2 %copy-start.2 = (bf16[4096,128]{1,0:T(8,128)(2,1)S(1)}, bf16[4096,128]{1,0:T(8,128)(2,1)}, u32[]{:S(2)}) copy-start(bf16[4096,128]{1,0:T(8,128)(2,1)} %refs_2_.1) | copy-start | bytes 3145732
  9.0 1.8 %copy-start.4 = (bf16[1,512,512]{2,1,0:T(8,128)(2,1)S(1)}, bf16[1,512,512]{2,1,0:T(8,128)(2,1)}, u32[]{:S(2)}) copy-start(bf16[1,512,512]{2,1,0:T(8,128)(2,1)} %refs_0_.5) | copy-start | bytes 1572868
  9.0 1.8 %copy-start.5 = (s32[1,512]{1,0:T(1,128)S(1)}, s32[1,512]{1,0:T(1,128)}, u32[]{:S(2)}) copy-start(s32[1,512]{1,0:T(1,128)} %refs_1_.1) | copy-start | bytes 6148
  9.0 1.8 %copy-start.6 = (s32[128]{0:T(128)S(1)}, s32[128]{0:T(128)}, u32[]{:S(2)}) copy-start(s32[128]{0:T(128)} %param.9) | copy-start | bytes 1540
  9.0 2.5 %copy-start.3 = (bf16[4096,128]{1,0:T(8,128)(2,1)S(1)}, bf16[4096,128]{1,0:T(8,128)(2,1)}, u32[]{:S(2)}) copy-start(bf16[4096,128]{1,0:T(8,128)(2,1)} %refs_2_.1) | copy-start | bytes 3145732
  10.8 28.7 %copy-start.1 = (bf16[384,4096]{1,0:T(8,128)(2,1)S(1)}, bf16[384,4096]{1,0:T(8,128)(2,1)}, u32[]{:S(2)}) copy-start(bf16[384,4096]{1,0:T(8,128)(2,1)} %refs_0_.7) | copy-start | bytes 9437188
  11.5 19.3 %collective-permute-start.5 = (bf16[4096,128]{1,0:T(8,128)(2,1)S(1)}, bf16[4096,128]{1,0:T(8,128)(2,1)S(1)}, u32[]{:S(2)}, u32[]{:S(2)}) collective-permute-start(bf16[4096,128]{1,0:T(8,128)(2,1)S(1)} %copy-done.3), channel_id=1, source_target_pairs={{4,20},{12,28},{20,4},{28,12},{5,21},{13,29},{21,5},{29,13},{6,22}... | collective-permute-start | bytes 3145736 | tf_op jit(solution)/shard_map/ppermute | solution.py:34
  16.0 17.8 %collective-permute-start.6 = (bf16[4096,128]{1,0:T(8,128)(2,1)S(1)}, bf16[4096,128]{1,0:T(8,128)(2,1)S(1)}, u32[]{:S(2)}, u32[]{:S(2)}) collective-permute-start(bf16[4096,128]{1,0:T(8,128)(2,1)S(1)} %copy-done.3), channel_id=1, source_target_pairs={{4,12},{12,4},{20,28},{28,20},{5,13},{13,5},{21,29},{29,21},{6,14}... | collective-permute-start | bytes 3145736 | tf_op jit(solution)/shard_map/ppermute | solution.py:34
  19.2 22.1 %collective-permute-start.3 = (bf16[2688,128]{1,0:T(8,128)(2,1)S(1)}, bf16[2688,128]{1,0:T(8,128)(2,1)S(1)}, u32[]{:S(2)}, u32[]{:S(2)}) collective-permute-start(bf16[2688,128]{1,0:T(8,128)(2,1)S(1)} %get-tuple-element.26), channel_id=1, source_target_pairs={{0,16},{8,24},{16,0},{24,8},{1,17},{9,25},{17,1},{25,9},{2,18},{10... | collective-permute-start | bytes 2064392 | tf_op jit(solution)/shard_map/ppermute | solution.py:34
  34.2 11.4 %collective-permute-start.7 = (bf16[2304,128]{1,0:T(8,128)(2,1)S(1)}, bf16[2304,128]{1,0:T(8,128)(2,1)S(1)}, u32[]{:S(2)}, u32[]{:S(2)}) collective-permute-start(bf16[2304,128]{1,0:T(8,128)(2,1)S(1)} %get-tuple-element.30), channel_id=1, source_target_pairs={{4,20},{12,28},{20,4},{28,12},{5,21},{13,29},{21,5},{29,13},{6,22}... | collective-permute-start | bytes 1769480 | tf_op jit(solution)/shard_map/ppermute | solution.py:34
  36.1 9.5 %collective-permute-start.8 = (bf16[1792,128]{1,0:T(8,128)(2,1)S(1)}, bf16[1792,128]{1,0:T(8,128)(2,1)S(1)}, u32[]{:S(2)}, u32[]{:S(2)}) collective-permute-start(bf16[1792,128]{1,0:T(8,128)(2,1)S(1)} %get-tuple-element.31), channel_id=1, source_target_pairs={{4,12},{12,4},{20,28},{28,20},{5,13},{13,5},{21,29},{29,21},{6,14}... | collective-permute-start | bytes 1376264 | tf_op jit(solution)/shard_map/ppermute | solution.py:34
  38.7 2.5 %collective-permute-start.4 = (bf16[1408,128]{1,0:T(8,128)(2,1)S(1)}, bf16[1408,128]{1,0:T(8,128)(2,1)S(1)}, u32[]{:S(2)}, u32[]{:S(2)}) collective-permute-start(bf16[1408,128]{1,0:T(8,128)(2,1)S(1)} %get-tuple-element.27.refs_2_), channel_id=1, source_target_pairs={{0,8},{8,0},{16,24},{24,16},{1,9},{9,1},{17,25},{25,17},{2,10},{10... | collective-permute-start | bytes 1081352 | tf_op jit(solution)/shard_map/ppermute | solution.py:34
  47.6 6.6 %collective-permute-start.10 = (bf16[768,128]{1,0:T(8,128)(2,1)S(1)}, bf16[768,128]{1,0:T(8,128)(2,1)S(1)}, u32[]{:S(2)}, u32[]{:S(2)}) collective-permute-start(bf16[768,128]{1,0:T(8,128)(2,1)S(1)} %get-tuple-element.36), channel_id=1, source_target_pairs={{0,3},{1,2},{2,1},{3,0},{4,7},{5,6},{6,5},{7,4},{8,11},{9,10},{10,... | collective-permute-start | bytes 589832 | tf_op jit(solution)/shard_map/ppermute | solution.py:34
  50.4 9.3 %collective-permute-start.11 = (bf16[768,128]{1,0:T(8,128)(2,1)S(1)}, bf16[768,128]{1,0:T(8,128)(2,1)S(1)}, u32[]{:S(2)}, u32[]{:S(2)}) collective-permute-start(bf16[768,128]{1,0:T(8,128)(2,1)S(1)} %get-tuple-element.37), channel_id=1, source_target_pairs={{0,2},{1,3},{2,0},{3,1},{4,6},{5,7},{6,4},{7,5},{8,10},{9,11},{10,... | collective-permute-start | bytes 589832 | tf_op jit(solution)/shard_map/ppermute | solution.py:34
  50.4 9.3 %collective-permute-start.9 = (bf16[768,128]{1,0:T(8,128)(2,1)S(1)}, bf16[768,128]{1,0:T(8,128)(2,1)S(1)}, u32[]{:S(2)}, u32[]{:S(2)}) collective-permute-start(bf16[768,128]{1,0:T(8,128)(2,1)S(1)} %get-tuple-element.35), channel_id=1, source_target_pairs={{0,1},{1,0},{2,3},{3,2},{4,5},{5,4},{6,7},{7,6},{8,9},{9,8},{10,11... | collective-permute-start | bytes 589832 | tf_op jit(solution)/shard_map/ppermute | solution.py:34
  59.9 1.5 %collective-permute-start.12 = (f32[384,128]{1,0:T(8,128)S(1)}, f32[384,128]{1,0:T(8,128)S(1)}, u32[]{:S(2)}, u32[]{:S(2)}) collective-permute-start(f32[384,128]{1,0:T(8,128)S(1)} %get-tuple-element.39), channel_id=1, source_target_pairs={{0,4},{4,0},{8,12},{12,8},{16,20},{20,16},{24,28},{28,24},{1,5},{5... | collective-permute-start | bytes 589832 | tf_op jit(solution)/shard_map/ppermute | solution.py:34
  61.7 5.2 %collective-permute-start.14 = (bf16[128,384]{1,0:T(8,128)(2,1)S(1)}, bf16[128,384]{1,0:T(8,128)(2,1)S(1)}, u32[]{:S(2)}, u32[]{:S(2)}) collective-permute-start(bf16[128,384]{1,0:T(8,128)(2,1)S(1)} %get-tuple-element.46), channel_id=1, source_target_pairs={{0,4},{4,8},{8,12},{12,16},{16,20},{20,24},{24,28},{28,0},{1,5},{5... | collective-permute-start | bytes 294920 | tf_op jit(solution)/shard_map/ppermute | solution.py:201
  63.0 3.9 %collective-permute-start.13 = (bf16[128,256]{1,0:T(8,128)(2,1)S(1)}, bf16[128,256]{1,0:T(8,128)(2,1)S(1)}, u32[]{:S(2)}, u32[]{:S(2)}) collective-permute-start(bf16[128,256]{1,0:T(8,128)(2,1)S(1)} %get-tuple-element.45), channel_id=1, source_target_pairs={{0,28},{4,0},{8,4},{12,8},{16,12},{20,16},{24,20},{28,24},{1,29},{... | collective-permute-start | bytes 196616 | tf_op jit(solution)/shard_map/ppermute | solution.py:201

commit v19 on v18

--- a/solution.py
+++ b/solution.py
@@ -96,18 +96,30 @@
         far_block[side * rows : (side + 1) * rows] = result[:, width:]
 
 
-def late_kernel(mine, theirs, top_even, bottom_even, top_odd, bottom_odd, own, near, far, kept, *refs):
+def upper_kernel(mine, theirs, top_even, top_odd, block):
+    rows = mine.shape[0]
+
+    def multiply(top):
+        for side, states in enumerate((mine, theirs)):
+            result = jnp.dot(states[:, : top.shape[0]], top[...], preferred_element_type=F32)
+            block[side * rows : (side + 1) * rows] = result
+
+    pl.when(core() == 0)(lambda: multiply(top_even))
+    pl.when(core() != 0)(lambda: multiply(top_odd))
+
+
+def late_kernel(mine, theirs, bottom_even, bottom_odd, upper, own, near, far, kept, *refs):
     sent, last = refs[:-1], refs[-1]
     rows = mine.shape[0]
 
-    def multiply(top, bottom):
-        cut = top.shape[0]
+    def multiply(bottom):
+        start = mine.shape[1] - bottom.shape[0]
         for side, states in enumerate((mine, theirs)):
-            result = jnp.dot(states[:, :cut], top[...], preferred_element_type=F32)
-            last[side * rows : (side + 1) * rows] = result + jnp.dot(states[:, cut:], bottom[...], preferred_element_type=F32)
-
-    pl.when(core() == 0)(lambda: multiply(top_even, bottom_even))
-    pl.when(core() != 0)(lambda: multiply(top_odd, bottom_odd))
+            span = slice(side * rows, (side + 1) * rows)
+            last[span] = upper[span] + jnp.dot(states[:, start:], bottom[...], preferred_element_type=F32)
+
+    pl.when(core() == 0)(lambda: multiply(bottom_even))
+    pl.when(core() != 0)(lambda: multiply(bottom_odd))
     where = block_of_band()
 
     def store(out, slot, block):
@@ -153,7 +165,9 @@
     early = call(early_kernel, block * 2, (wavefunctions, theirs, *received))
     outs = block + [shape(2 * rows, width, dtype=BF16)] * (bands - 1)
     scratch = [pltpu.VMEM((2 * rows, width), F32)]
-    kept, *sent = call(late_kernel, outs, (wavefunctions, theirs, *passed, own, *early), scratch=scratch)
+    upper = call(upper_kernel, block, (wavefunctions, theirs, *passed[::2]), after=early[:1])[0]
+    operands = (wavefunctions, theirs, *passed[1::2], upper, own, *early)
+    kept, *sent = call(late_kernel, outs, operands, scratch=scratch)
     parts = [exchanged(sent[mask - 1], "band", mask) for mask in (1, *reversed(range(2, bands)))]
     mine, others = call(sum_kernel, [shape(rows, width)] * 2, (kept, *parts))
     return mine, exchanged(others, "domain", CORE), operator

time: 68.4 us -> 68.6 us (level)
    pallas_call x10 -> x11, Pallas kernels: 8.66 us -> 8.85 us  [call(): pl.pallas_call(body, out_shape=outs, in_specs=[pl.BlockSpec(memory_space=...]
  transfers between devices with their start and end apart: 15 -> 15, of which waited for: 8 -> 8; matrix products, arithmetic and copies ran while one was open for 0% -> 0% of each run, Pallas kernels for 8% -> 9%
where the time goes in v19:
time: 68.6 us; the launch traced here: 68.3 us
  waiting for transfers between devices  36.1 us (53%)
  starting transfers between devices  19.9 us (29%)
  Pallas kernels  8.85 us (13%)
  local copies, waits for them, and re-layouts  3.13 us (5%)
    ppermute x13, waiting for transfers between devices, exchanged(): lax.ppermute(value, axis, [(source, source ^ mask) for source in sources...  32.6 us
    ppermute x13, starting transfers between devices, exchanged(): lax.ppermute(value, axis, [(source, source ^ mask) for source in sources...  18.6 us
    pallas_call x11, Pallas kernels, call(): pl.pallas_call(body, out_shape=outs, in_specs=[pl.BlockSpec(memory_space=...  8.85 us
    ppermute x2, waiting for transfers between devices, rotated(): lax.ppermute(value, axis, [(source, (source + steps) % count) for source...  3.46 us
    unnamed x14, local copies, waits for them, and re-layouts  3.13 us
  transfers between devices with their start and end apart: 15, of which 8 were waited for; matrix products, arithmetic and copies ran while one was open for 0% of the time, Pallas kernels for 9%

profile of v19, /device:TPU:1, one launch (start us, length us, event | category | flops | bytes accessed | tf_op | source)
XLA Modules:
  0.0 68.3 jit_solution(10795660324856049208)
XLA Ops:
  0.0 0.1 collective-permute-start
  0.1 0.7 %collective-permute-start.1 = (bf16[4096,128]{1,0:T(8,128)(2,1)}, bf16[4096,128]{1,0:T(8,128)(2,1)S(1)}, u32[]{:S(2)}, u32[]{:S(2)}) collective-permute-start(bf16[4096,128]{1,0:T(8,128)(2,1)} %refs_2_.1), channel_id=1, source_target_pairs={{0,16},{8,24},{16,0},{24,8},{1,17},{9,25},{17,1},{25,9},{2,18},{10... | collective-permute-start | bytes 3145736 | tf_op jit(solution)/shard_map/ppermute | solution.py:34
  0.8 0.7 %collective-permute-start.2 = (bf16[4096,128]{1,0:T(8,128)(2,1)}, bf16[4096,128]{1,0:T(8,128)(2,1)S(1)}, u32[]{:S(2)}, u32[]{:S(2)}) collective-permute-start(bf16[4096,128]{1,0:T(8,128)(2,1)} %refs_2_.1), channel_id=1, source_target_pairs={{0,8},{8,0},{16,24},{24,16},{1,9},{9,1},{17,25},{25,17},{2,10},{10... | collective-permute-start | bytes 3145736 | tf_op jit(solution)/shard_map/ppermute | solution.py:34
  1.5 4.4 %collective-permute-done.refs_1_ = bf16[384,4096]{1,0:T(8,128)(2,1)S(1)} collective-permute-done((bf16[384,4096]{1,0:T(8,128)(2,1)}, bf16[384,4096]{1,0:T(8,128)(2,1)S(1)}, u32[]{:S(2)}, u32[]{:S(2)}) %collective-permute-start) | collective-permute-done | bytes 3145760 | tf_op jit(solution)/shard_map/ppermute | solution.py:34
  5.9 0.0 copy-start
  5.9 1.9 %copy-done = bf16[384,4096]{1,0:T(8,128)(2,1)S(1)} copy-done((bf16[384,4096]{1,0:T(8,128)(2,1)S(1)}, bf16[384,4096]{1,0:T(8,128)(2,1)}, u32[]{:S(2)}) %copy-start) | copy-done | bytes 3145752
  7.8 0.0 copy-start.2
  7.8 1.2 %copy-done.2 = bf16[4096,128]{1,0:T(8,128)(2,1)S(1)} copy-done((bf16[4096,128]{1,0:T(8,128)(2,1)S(1)}, bf16[4096,128]{1,0:T(8,128)(2,1)}, u32[]{:S(2)}) %copy-start.2) | copy-done | bytes 1048600
  9.0 0.0 copy-start.4
  9.0 0.0 copy-start.5
  9.0 0.0 copy-start.6
  9.0 0.0 copy-start.3
  9.0 1.8 %shard_map.56.refs_3_.refs_5_ = f32[768,128]{1,0:T(8,128)S(1)} custom-call(bf16[384,4096]{1,0:T(8,128)(2,1)S(1)} %copy-done, bf16[384,4096]{1,0:T(8,128)(2,1)S(1)} %collective-permute-done.refs_1_, bf16[4096,128]{1,0:T(8,128)(2,1)S(1)} %copy-done.2), custom_call_target="tpu_custom_call" | custom-call | bytes 1024 | tf_op jit(solution)/shard_map/pallas_call | solution.py:44
  10.8 0.0 copy-start.1
  10.8 0.0 copy-done.4
  10.8 0.0 copy-done.5
  10.8 0.0 copy-done.6
  10.8 0.7 %shard_map.57 = (bf16[512,512]{1,0:T(8,128)(2,1)S(1)}, bf16[128,384]{1,0:T(8,128)(2,1)S(1)}, bf16[384,128]{1,0:T(8,128)(2,1)S(1)}) custom-call(bf16[1,512,512]{2,1,0:T(8,128)(2,1)S(1)} %copy-done.4, s32[1,512]{1,0:T(1,128)S(1)} %copy-done.5, s32[1,128]{1,0:T(1,128)S(1)} %bitcast.1, f32[768,128]{1,0:T(8,128)S(1)} %shard_map.56.refs_3_.refs_5_), custom_call_target="tpu_custom_call" | custom-call | bytes 1024 | tf_op jit(solution)/shard_map/pallas_call | solution.py:44
  11.5 0.0 copy-done.3
  11.5 4.4 %collective-permute-start.4 = (bf16[4096,128]{1,0:T(8,128)(2,1)S(1)}, bf16[4096,128]{1,0:T(8,128)(2,1)S(1)}, u32[]{:S(2)}, u32[]{:S(2)}) collective-permute-start(bf16[4096,128]{1,0:T(8,128)(2,1)S(1)} %copy-done.3), channel_id=1, source_target_pairs={{4,20},{12,28},{20,4},{28,12},{5,21},{13,29},{21,5},{29,13},{6,22}... | collective-permute-start | bytes 3145736 | tf_op jit(solution)/shard_map/ppermute | solution.py:34
  16.0 3.1 %collective-permute-start.5 = (bf16[4096,128]{1,0:T(8,128)(2,1)S(1)}, bf16[4096,128]{1,0:T(8,128)(2,1)S(1)}, u32[]{:S(2)}, u32[]{:S(2)}) collective-permute-start(bf16[4096,128]{1,0:T(8,128)(2,1)S(1)} %copy-done.3), channel_id=1, source_target_pairs={{4,12},{12,4},{20,28},{28,20},{5,13},{13,5},{21,29},{29,21},{6,14}... | collective-permute-start | bytes 3145736 | tf_op jit(solution)/shard_map/ppermute | solution.py:34
  19.1 0.0 collective-permute-done.1.refs_0_.refs_3_
  19.1 0.0 collective-permute-done.2.refs_1_.refs_2_
  19.2 0.7 %collective-permute-start.7 = (bf16[2688,128]{1,0:T(8,128)(2,1)S(1)}, bf16[2688,128]{1,0:T(8,128)(2,1)S(1)}, u32[]{:S(2)}, u32[]{:S(2)}) collective-permute-start(bf16[2688,128]{1,0:T(8,128)(2,1)S(1)} %get-tuple-element.30), channel_id=1, source_target_pairs={{0,16},{8,24},{16,0},{24,8},{1,17},{9,25},{17,1},{25,9},{2,18},{10... | collective-permute-start | bytes 2064392 | tf_op jit(solution)/shard_map/ppermute | solution.py:34
  19.9 11.0 %collective-permute-done.4.refs_0_.refs_5_ = bf16[4096,128]{1,0:T(8,128)(2,1)S(1)} collective-permute-done((bf16[4096,128]{1,0:T(8,128)(2,1)S(1)}, bf16[4096,128]{1,0:T(8,128)(2,1)S(1)}, u32[]{:S(2)}, u32[]{:S(2)}) %collective-permute-start.4) | collective-permute-done | bytes 1048608 | tf_op jit(solution)/shard_map/ppermute | solution.py:34
  30.8 2.9 %collective-permute-done.5.refs_1_.refs_4_ = bf16[4096,128]{1,0:T(8,128)(2,1)S(1)} collective-permute-done((bf16[4096,128]{1,0:T(8,128)(2,1)S(1)}, bf16[4096,128]{1,0:T(8,128)(2,1)S(1)}, u32[]{:S(2)}, u32[]{:S(2)}) %collective-permute-start.5) | collective-permute-done | bytes 1048608 | tf_op jit(solution)/shard_map/ppermute | solution.py:34
  33.8 0.4 shard_map.58
  34.2 1.9 %collective-permute-start.8 = (bf16[2304,128]{1,0:T(8,128)(2,1)S(1)}, bf16[2304,128]{1,0:T(8,128)(2,1)S(1)}, u32[]{:S(2)}, u32[]{:S(2)}) collective-permute-start(bf16[2304,128]{1,0:T(8,128)(2,1)S(1)} %get-tuple-element.31), channel_id=1, source_target_pairs={{4,20},{12,28},{20,4},{28,12},{5,21},{13,29},{21,5},{29,13},{6,22}... | collective-permute-start | bytes 1769480 | tf_op jit(solution)/shard_map/ppermute | solution.py:34
  36.1 2.6 %collective-permute-start.6 = (bf16[1792,128]{1,0:T(8,128)(2,1)S(1)}, bf16[1792,128]{1,0:T(8,128)(2,1)S(1)}, u32[]{:S(2)}, u32[]{:S(2)}) collective-permute-start(bf16[1792,128]{1,0:T(8,128)(2,1)S(1)} %get-tuple-element.29), channel_id=1, source_target_pairs={{4,12},{12,4},{20,28},{28,20},{5,13},{13,5},{21,29},{29,21},{6,14}... | collective-permute-start | bytes 1376264 | tf_op jit(solution)/shard_map/ppermute | solution.py:34
  38.7 0.7 %collective-permute-start.3 = (bf16[1408,128]{1,0:T(8,128)(2,1)S(1)}, bf16[1408,128]{1,0:T(8,128)(2,1)S(1)}, u32[]{:S(2)}, u32[]{:S(2)}) collective-permute-start(bf16[1408,128]{1,0:T(8,128)(2,1)S(1)} %get-tuple-element.26.refs_2_), channel_id=1, source_target_pairs={{0,8},{8,0},{16,24},{24,16},{1,9},{9,1},{17,25},{25,17},{2,10},{10... | collective-permute-start | bytes 1081352 | tf_op jit(solution)/shard_map/ppermute | solution.py:34
  39.4 0.0 copy-done.1
  39.4 1.8 %shard_map.59 = (f32[768,128]{1,0:T(8,128)S(1)}, f32[768,128]{1,0:T(8,128)S(1)}) custom-call(bf16[384,4096]{1,0:T(8,128)(2,1)S(1)} %copy-done.1, bf16[384,4096]{1,0:T(8,128)(2,1)S(1)} %collective-permute-done.refs_1_, bf16[4096,128]{1,0:T(8,128)(2,1)S(1)} %collective-permute-done.2.refs_1_.refs_2_, ...), custom_call_target="tpu_custom_call" | custom-call | bytes 1024 | tf_op jit(solution)/shard_map/pallas_call | solution.py:44
  41.2 0.0 collective-permute-done.7.refs_2_
  41.3 3.9 %collective-permute-done.8.refs_3_ = bf16[2304,128]{1,0:T(8,128)(2,1)S(1)} collective-permute-done((bf16[2304,128]{1,0:T(8,128)(2,1)S(1)}, bf16[2304,128]{1,0:T(8,128)(2,1)S(1)}, u32[]{:S(2)}, u32[]{:S(2)}) %collective-permute-start.8) | collective-permute-done | bytes 589856 | tf_op jit(solution)/shard_map/ppermute | solution.py:34
  45.1 1.1 %shard_map.60.refs_4_ = f32[768,128]{1,0:T(8,128)S(1)} custom-call(bf16[384,4096]{1,0:T(8,128)(2,1)S(1)} %copy-done.1, bf16[384,4096]{1,0:T(8,128)(2,1)S(1)} %collective-permute-done.refs_1_, bf16[2688,128]{1,0:T(8,128)(2,1)S(1)} %collective-permute-done.7.refs_2_, bf16[2304,128]{1,0:T(8,128)(2,1)S(1)} %collective-permute-done.8.refs_3_, ...), custom_call_target="tpu_custom_call" | custom-call | bytes 1024 | tf_op jit(solution)/shard_map/pallas_call | solution.py:44
  46.2 0.0 collective-permute-done.3.refs_2_
  46.2 0.0 collective-permute-done.6.refs_3_
  46.2 1.1 %shard_map.61 = (f32[768,128]{1,0:T(8,128)S(1)}, bf16[768,128]{1,0:T(8,128)(2,1)S(1)}, bf16[768,128]{1,0:T(8,128)(2,1)S(1)}, bf16[768,128]{1,0:T(8,128)(2,1)S(1)}) custom-call(bf16[384,4096]{1,0:T(8,128)(2,1)S(1)} %copy-done.1, bf16[384,4096]{1,0:T(8,128)(2,1)S(1)} %collective-permute-done.refs_1_, bf16[1408,128]{1,0:T(8,128)(2,1)S(1)} %collective-permute-done.3.refs_2_, ...), custom_call_target="tpu_custom_call" | custom-call | bytes 1024 | tf_op jit(solution)/shard_map/pallas_call | solution.py:44
  47.3 2.9 %collective-permute-start.10 = (bf16[768,128]{1,0:T(8,128)(2,1)S(1)}, bf16[768,128]{1,0:T(8,128)(2,1)S(1)}, u32[]{:S(2)}, u32[]{:S(2)}) collective-permute-start(bf16[768,128]{1,0:T(8,128)(2,1)S(1)} %get-tuple-element.36), channel_id=1, source_target_pairs={{0,3},{1,2},{2,1},{3,0},{4,7},{5,6},{6,5},{7,4},{8,11},{9,10},{10,... | collective-permute-start | bytes 589832 | tf_op jit(solution)/shard_map/ppermute | solution.py:34
  50.1 0.0 collective-permute-start.11
  50.1 0.7 %collective-permute-start.9 = (bf16[768,128]{1,0:T(8,128)(2,1)S(1)}, bf16[768,128]{1,0:T(8,128)(2,1)S(1)}, u32[]{:S(2)}, u32[]{:S(2)}) collective-permute-start(bf16[768,128]{1,0:T(8,128)(2,1)S(1)} %get-tuple-element.35), channel_id=1, source_target_pairs={{0,1},{1,0},{2,3},{3,2},{4,5},{5,4},{6,7},{7,6},{8,9},{9,8},{10,11... | collective-permute-start | bytes 589832 | tf_op jit(solution)/shard_map/ppermute | solution.py:34
  50.9 3.0 %collective-permute-done.10.refs_2_ = bf16[768,128]{1,0:T(8,128)(2,1)S(1)} collective-permute-done((bf16[768,128]{1,0:T(8,128)(2,1)S(1)}, bf16[768,128]{1,0:T(8,128)(2,1)S(1)}, u32[]{:S(2)}, u32[]{:S(2)}) %collective-permute-start.10) | collective-permute-done | bytes 196640 | tf_op jit(solution)/shard_map/ppermute | solution.py:34
  53.9 6.1 %collective-permute-done.11.refs_3_ = bf16[768,128]{1,0:T(8,128)(2,1)S(1)} collective-permute-done((bf16[768,128]{1,0:T(8,128)(2,1)S(1)}, bf16[768,128]{1,0:T(8,128)(2,1)S(1)}, u32[]{:S(2)}, u32[]{:S(2)}) %collective-permute-start.11) | collective-permute-done | bytes 196640 | tf_op jit(solution)/shard_map/ppermute | solution.py:34
  60.0 0.0 collective-permute-done.9.refs_1_
  60.0 0.1 shard_map.62
  60.0 0.1 collective-permute-start.12
  60.1 1.4 %collective-permute-done.12.refs_1_ = f32[384,128]{1,0:T(8,128)S(1)} collective-permute-done((f32[384,128]{1,0:T(8,128)S(1)}, f32[384,128]{1,0:T(8,128)S(1)}, u32[]{:S(2)}, u32[]{:S(2)}) %collective-permute-start.12) | collective-permute-done | bytes 196640 | tf_op jit(solution)/shard_map/ppermute | solution.py:34
  61.6 0.3 shard_map.63
  61.8 1.3 %collective-permute-start.14 = (bf16[128,384]{1,0:T(8,128)(2,1)S(1)}, bf16[128,384]{1,0:T(8,128)(2,1)S(1)}, u32[]{:S(2)}, u32[]{:S(2)}) collective-permute-start(bf16[128,384]{1,0:T(8,128)(2,1)S(1)} %get-tuple-element.46), channel_id=1, source_target_pairs={{0,4},{4,8},{8,12},{12,16},{16,20},{20,24},{24,28},{28,0},{1,5},{5... | collective-permute-start | bytes 294920 | tf_op jit(solution)/shard_map/ppermute | solution.py:215
  63.1 0.0 collective-permute-start.13
  63.1 0.4 shard_map.64
  63.6 3.5 %collective-permute-done.13.refs_4_ = bf16[128,256]{1,0:T(8,128)(2,1)S(1)} collective-permute-done((bf16[128,256]{1,0:T(8,128)(2,1)S(1)}, bf16[128,256]{1,0:T(8,128)(2,1)S(1)}, u32[]{:S(2)}, u32[]{:S(2)}) %collective-permute-start.13) | collective-permute-done | bytes 65568 | tf_op jit(solution)/shard_map/ppermute | solution.py:215
  67.1 0.0 collective-permute-done.14.refs_5_
  67.1 1.2 %shard_map.65 = f32[384,256]{1,0:T(8,128)} custom-call(f32[384,256]{1,0:T(8,128)S(1)} %get-tuple-element.42.refs_0_, bf16[128,512]{1,0:T(8,128)(2,1)S(1)} %get-tuple-element.43.refs_1_, bf16[512,512]{1,0:T(8,128)(2,1)S(1)} %get-tuple-element.27.refs_2_.refs_1_, bf16[384,128]{1,0:T(8,128)(2,1)S(1)} %get-tuple-element.44.refs_3_, ...), custom_call_target="tpu_custom_call" | custom-call | bytes 1024 | tf_op jit(solution)/shard_map/pallas_call | solution.py:44
  (1 shorter events, 0.0 us)
Async XLA Ops:
  0.0 5.9 %collective-permute-start = (bf16[384,4096]{1,0:T(8,128)(2,1)}, bf16[384,4096]{1,0:T(8,128)(2,1)S(1)}, u32[]{:S(2)}, u32[]{:S(2)}) collective-permute-start(bf16[384,4096]{1,0:T(8,128)(2,1)} %refs_0_.9), channel_id=1, source_target_pairs={{0,4},{4,0},{8,12},{12,8},{16,20},{20,16},{24,28},{28,24},{1,5},{5... | collective-permute-start | bytes 9437192 | tf_op jit(solution)/shard_map/ppermute | solution.py:34
  0.1 19.0 %collective-permute-start.1 = (bf16[4096,128]{1,0:T(8,128)(2,1)}, bf16[4096,128]{1,0:T(8,128)(2,1)S(1)}, u32[]{:S(2)}, u32[]{:S(2)}) collective-permute-start(bf16[4096,128]{1,0:T(8,128)(2,1)} %refs_2_.1), channel_id=1, source_target_pairs={{0,16},{8,24},{16,0},{24,8},{1,17},{9,25},{17,1},{25,9},{2,18},{10... | collective-permute-start | bytes 3145736 | tf_op jit(solution)/shard_map/ppermute | solution.py:34
  0.8 18.3 %collective-permute-start.2 = (bf16[4096,128]{1,0:T(8,128)(2,1)}, bf16[4096,128]{1,0:T(8,128)(2,1)S(1)}, u32[]{:S(2)}, u32[]{:S(2)}) collective-permute-start(bf16[4096,128]{1,0:T(8,128)(2,1)} %refs_2_.1), channel_id=1, source_target_pairs={{0,8},{8,0},{16,24},{24,16},{1,9},{9,1},{17,25},{25,17},{2,10},{10... | collective-permute-start | bytes 3145736 | tf_op jit(solution)/shard_map/ppermute | solution.py:34
  5.9 1.9 %copy-start = (bf16[384,4096]{1,0:T(8,128)(2,1)S(1)}, bf16[384,4096]{1,0:T(8,128)(2,1)}, u32[]{:S(2)}) copy-start(bf16[384,4096]{1,0:T(8,128)(2,1)} %refs_0_.9) | copy-start | bytes 9437188
  7.8 1.2 %copy-start.2 = (bf16[4096,128]{1,0:T(8,128)(2,1)S(1)}, bf16[4096,128]{1,0:T(8,128)(2,1)}, u32[]{:S(2)}) copy-start(bf16[4096,128]{1,0:T(8,128)(2,1)} %refs_2_.1) | copy-start | bytes 3145732
  9.0 1.8 %copy-start.4 = (bf16[1,512,512]{2,1,0:T(8,128)(2,1)S(1)}, bf16[1,512,512]{2,1,0:T(8,128)(2,1)}, u32[]{:S(2)}) copy-start(bf16[1,512,512]{2,1,0:T(8,128)(2,1)} %refs_0_.6) | copy-start | bytes 1572868
  9.0 1.8 %copy-start.5 = (s32[1,512]{1,0:T(1,128)S(1)}, s32[1,512]{1,0:T(1,128)}, u32[]{:S(2)}) copy-start(s32[1,512]{1,0:T(1,128)} %refs_1_.1) | copy-start | bytes 6148
  9.0 1.8 %copy-start.6 = (s32[128]{0:T(128)S(1)}, s32[128]{0:T(128)}, u32[]{:S(2)}) copy-start(s32[128]{0:T(128)} %param.9) | copy-start | bytes 1540
  9.0 2.5 %copy-start.3 = (bf16[4096,128]{1,0:T(8,128)(2,1)S(1)}, bf16[4096,128]{1,0:T(8,128)(2,1)}, u32[]{:S(2)}) copy-start(bf16[4096,128]{1,0:T(8,128)(2,1)} %refs_2_.1) | copy-start | bytes 3145732
  10.8 28.7 %copy-start.1 = (bf16[384,4096]{1,0:T(8,128)(2,1)S(1)}, bf16[384,4096]{1,0:T(8,128)(2,1)}, u32[]{:S(2)}) copy-start(bf16[384,4096]{1,0:T(8,128)(2,1)} %refs_0_.9) | copy-start | bytes 9437188
  11.5 19.3 %collective-permute-start.4 = (bf16[4096,128]{1,0:T(8,128)(2,1)S(1)}, bf16[4096,128]{1,0:T(8,128)(2,1)S(1)}, u32[]{:S(2)}, u32[]{:S(2)}) collective-permute-start(bf16[4096,128]{1,0:T(8,128)(2,1)S(1)} %copy-done.3), channel_id=1, source_target_pairs={{4,20},{12,28},{20,4},{28,12},{5,21},{13,29},{21,5},{29,13},{6,22}... | collective-permute-start | bytes 3145736 | tf_op jit(solution)/shard_map/ppermute | solution.py:34
  16.0 17.8 %collective-permute-start.5 = (bf16[4096,128]{1,0:T(8,128)(2,1)S(1)}, bf16[4096,128]{1,0:T(8,128)(2,1)S(1)}, u32[]{:S(2)}, u32[]{:S(2)}) collective-permute-start(bf16[4096,128]{1,0:T(8,128)(2,1)S(1)} %copy-done.3), channel_id=1, source_target_pairs={{4,12},{12,4},{20,28},{28,20},{5,13},{13,5},{21,29},{29,21},{6,14}... | collective-permute-start | bytes 3145736 | tf_op jit(solution)/shard_map/ppermute | solution.py:34
  19.2 22.1 %collective-permute-start.7 = (bf16[2688,128]{1,0:T(8,128)(2,1)S(1)}, bf16[2688,128]{1,0:T(8,128)(2,1)S(1)}, u32[]{:S(2)}, u32[]{:S(2)}) collective-permute-start(bf16[2688,128]{1,0:T(8,128)(2,1)S(1)} %get-tuple-element.30), channel_id=1, source_target_pairs={{0,16},{8,24},{16,0},{24,8},{1,17},{9,25},{17,1},{25,9},{2,18},{10... | collective-permute-start | bytes 2064392 | tf_op jit(solution)/shard_map/ppermute | solution.py:34
  34.2 10.9 %collective-permute-start.8 = (bf16[2304,128]{1,0:T(8,128)(2,1)S(1)}, bf16[2304,128]{1,0:T(8,128)(2,1)S(1)}, u32[]{:S(2)}, u32[]{:S(2)}) collective-permute-start(bf16[2304,128]{1,0:T(8,128)(2,1)S(1)} %get-tuple-element.31), channel_id=1, source_target_pairs={{4,20},{12,28},{20,4},{28,12},{5,21},{13,29},{21,5},{29,13},{6,22}... | collective-permute-start | bytes 1769480 | tf_op jit(solution)/shard_map/ppermute | solution.py:34
  36.1 10.1 %collective-permute-start.6 = (bf16[1792,128]{1,0:T(8,128)(2,1)S(1)}, bf16[1792,128]{1,0:T(8,128)(2,1)S(1)}, u32[]{:S(2)}, u32[]{:S(2)}) collective-permute-start(bf16[1792,128]{1,0:T(8,128)(2,1)S(1)} %get-tuple-element.29), channel_id=1, source_target_pairs={{4,12},{12,4},{20,28},{28,20},{5,13},{13,5},{21,29},{29,21},{6,14}... | collective-permute-start | bytes 1376264 | tf_op jit(solution)/shard_map/ppermute | solution.py:34
  38.7 7.4 %collective-permute-start.3 = (bf16[1408,128]{1,0:T(8,128)(2,1)S(1)}, bf16[1408,128]{1,0:T(8,128)(2,1)S(1)}, u32[]{:S(2)}, u32[]{:S(2)}) collective-permute-start(bf16[1408,128]{1,0:T(8,128)(2,1)S(1)} %get-tuple-element.26.refs_2_), channel_id=1, source_target_pairs={{0,8},{8,0},{16,24},{24,16},{1,9},{9,1},{17,25},{25,17},{2,10},{10... | collective-permute-start | bytes 1081352 | tf_op jit(solution)/shard_map/ppermute | solution.py:34
  47.3 6.6 %collective-permute-start.10 = (bf16[768,128]{1,0:T(8,128)(2,1)S(1)}, bf16[768,128]{1,0:T(8,128)(2,1)S(1)}, u32[]{:S(2)}, u32[]{:S(2)}) collective-permute-start(bf16[768,128]{1,0:T(8,128)(2,1)S(1)} %get-tuple-element.36), channel_id=1, source_target_pairs={{0,3},{1,2},{2,1},{3,0},{4,7},{5,6},{6,5},{7,4},{8,11},{9,10},{10,... | collective-permute-start | bytes 589832 | tf_op jit(solution)/shard_map/ppermute | solution.py:34
  50.1 9.8 %collective-permute-start.11 = (bf16[768,128]{1,0:T(8,128)(2,1)S(1)}, bf16[768,128]{1,0:T(8,128)(2,1)S(1)}, u32[]{:S(2)}, u32[]{:S(2)}) collective-permute-start(bf16[768,128]{1,0:T(8,128)(2,1)S(1)} %get-tuple-element.37), channel_id=1, source_target_pairs={{0,2},{1,3},{2,0},{3,1},{4,6},{5,7},{6,4},{7,5},{8,10},{9,11},{10,... | collective-permute-start | bytes 589832 | tf_op jit(solution)/shard_map/ppermute | solution.py:34
  50.1 9.8 %collective-permute-start.9 = (bf16[768,128]{1,0:T(8,128)(2,1)S(1)}, bf16[768,128]{1,0:T(8,128)(2,1)S(1)}, u32[]{:S(2)}, u32[]{:S(2)}) collective-permute-start(bf16[768,128]{1,0:T(8,128)(2,1)S(1)} %get-tuple-element.35), channel_id=1, source_target_pairs={{0,1},{1,0},{2,3},{3,2},{4,5},{5,4},{6,7},{7,6},{8,9},{9,8},{10,11... | collective-permute-start | bytes 589832 | tf_op jit(solution)/shard_map/ppermute | solution.py:34
  60.0 1.5 %collective-permute-start.12 = (f32[384,128]{1,0:T(8,128)S(1)}, f32[384,128]{1,0:T(8,128)S(1)}, u32[]{:S(2)}, u32[]{:S(2)}) collective-permute-start(f32[384,128]{1,0:T(8,128)S(1)} %get-tuple-element.39), channel_id=1, source_target_pairs={{0,4},{4,0},{8,12},{12,8},{16,20},{20,16},{24,28},{28,24},{1,5},{5... | collective-permute-start | bytes 589832 | tf_op jit(solution)/shard_map/ppermute | solution.py:34
  61.8 5.2 %collective-permute-start.14 = (bf16[128,384]{1,0:T(8,128)(2,1)S(1)}, bf16[128,384]{1,0:T(8,128)(2,1)S(1)}, u32[]{:S(2)}, u32[]{:S(2)}) collective-permute-start(bf16[128,384]{1,0:T(8,128)(2,1)S(1)} %get-tuple-element.46), channel_id=1, source_target_pairs={{0,4},{4,8},{8,12},{12,16},{16,20},{20,24},{24,28},{28,0},{1,5},{5... | collective-permute-start | bytes 294920 | tf_op jit(solution)/shard_map/ppermute | solution.py:215
  63.1 3.9 %collective-permute-start.13 = (bf16[128,256]{1,0:T(8,128)(2,1)S(1)}, bf16[128,256]{1,0:T(8,128)(2,1)S(1)}, u32[]{:S(2)}, u32[]{:S(2)}) collective-permute-start(bf16[128,256]{1,0:T(8,128)(2,1)S(1)} %get-tuple-element.45), channel_id=1, source_target_pairs={{0,28},{4,0},{8,4},{12,8},{16,12},{20,16},{24,20},{28,24},{1,29},{... | collective-permute-start | bytes 196616 | tf_op jit(solution)/shard_map/ppermute | solution.py:215

commit v20 on v19

--- a/solution.py
+++ b/solution.py
@@ -32,6 +32,16 @@
 def exchanged(value, axis, mask, core=None):
     sources = range(lax.axis_size(axis))
     return lax.ppermute(value, axis, [(source, source ^ mask) for source in sources if core in (None, source & CORE)])
+
+
+def paired(value, mask, one):
+    count, bands = lax.axis_size("domain"), lax.axis_size("band")
+    pairs = []
+    for place in range(count):
+        for band in range(bands):
+            partner = (place ^ mask, band) if place & CORE == one else (place, band ^ 1)
+            pairs.append((place * bands + band, partner[0] * bands + partner[1]))
+    return lax.ppermute(value, ("domain", "band"), pairs)
 
 
 def call(kernel, outs, operands, after=(), spaces=None, scratch=()):
@@ -146,7 +156,7 @@
     bands, chips = lax.axis_size("band"), lax.axis_size("domain") // 2
     rows, states = wavefunctions.shape
     width = rotation.shape[1]
-    received = [exchanged(rotation, "domain", NEAR, 0), exchanged(rotation, "domain", FAR, 0)]
+    received = [paired(rotation, NEAR, 0), paired(rotation, FAR, 0)]
     theirs = exchanged(wavefunctions, "domain", CORE)
     block = [shape(2 * rows, width)]
     own = call(own_kernel, block, (wavefunctions, theirs, rotation))[0]

time: 68.6 us -> 69.5 us (1.013)
  starting transfers between devices: 19.9 us -> 22.2 us
  waiting for transfers between devices: 36.1 us -> 34.8 us
    ppermute x13 -> x11, waiting for transfers between devices: 32.6 us -> 23.9 us  [exchanged(): lax.ppermute(value, axis, [(source, source ^ mask) for source in sources...]
    ppermute x0 -> x2, waiting for transfers between devices: none -> 7.63 us  [paired(): return lax.ppermute(value, ('domain', 'band'), pairs)]
    ppermute x0 -> x2, starting transfers between devices: none -> 2.78 us  [paired(): return lax.ppermute(value, ('domain', 'band'), pairs)]
    ppermute x13 -> x11, starting transfers between devices: 18.6 us -> 18.1 us  [exchanged(): lax.ppermute(value, axis, [(source, source ^ mask) for source in sources...]
  transfers between devices with their start and end apart: 15 -> 15, of which waited for: 8 -> 9; matrix products, arithmetic and copies ran while one was open for 0% -> 0% of each run, Pallas kernels for 9% -> 9%
where the time goes in v20:
time: 69.5 us; the launch traced here: 69.1 us
  waiting for transfers between devices  34.8 us (50%)
  starting transfers between devices  22.2 us (32%)
  Pallas kernels  8.83 us (13%)
  local copies, waits for them, and re-layouts  3.13 us (5%)
    ppermute x11, waiting for transfers between devices, exchanged(): lax.ppermute(value, axis, [(source, source ^ mask) for source in sources...  23.9 us
    ppermute x11, starting transfers between devices, exchanged(): lax.ppermute(value, axis, [(source, source ^ mask) for source in sources...  18.1 us
    pallas_call x11, Pallas kernels, call(): pl.pallas_call(body, out_shape=outs, in_specs=[pl.BlockSpec(memory_space=...  8.83 us
    ppermute x2, waiting for transfers between devices, paired(): return lax.ppermute(value, ('domain', 'band'), pairs)  7.63 us
    ppermute x2, waiting for transfers between devices, rotated(): lax.ppermute(value, axis, [(source, (source + steps) % count) for source...  3.24 us
    unnamed x14, local copies, waits for them, and re-layouts  3.13 us
    ppermute x2, starting transfers between devices, paired(): return lax.ppermute(value, ('domain', 'band'), pairs)  2.78 us
  transfers between devices with their start and end apart: 15, of which 9 were waited for; matrix products, arithmetic and copies ran while one was open for 0% of the time, Pallas kernels for 9%

profile of v20, /device:TPU:1, one launch (start us, length us, event | category | flops | bytes accessed | tf_op | source)
XLA Modules:
  0.0 69.1 jit_solution(315265154652605603)
XLA Ops:
  0.0 0.1 collective-permute-start
  0.1 2.7 %collective-permute-start.1 = (bf16[4096,128]{1,0:T(8,128)(2,1)}, bf16[4096,128]{1,0:T(8,128)(2,1)S(1)}, u32[]{:S(2)}, u32[]{:S(2)}) collective-permute-start(bf16[4096,128]{1,0:T(8,128)(2,1)} %refs_2_.1), channel_id=1, source_target_pairs={{0,16},{1,17},{2,18},{3,19},{4,5},{5,4},{6,7},{7,6},{8,24},{9,25},... | collective-permute-start | bytes 3145736 | tf_op jit(solution)/shard_map/ppermute | solution.py:44
  2.8 0.0 collective-permute-start.2
  2.8 3.0 %collective-permute-done.refs_1_ = bf16[384,4096]{1,0:T(8,128)(2,1)S(1)} collective-permute-done((bf16[384,4096]{1,0:T(8,128)(2,1)}, bf16[384,4096]{1,0:T(8,128)(2,1)S(1)}, u32[]{:S(2)}, u32[]{:S(2)}) %collective-permute-start) | collective-permute-done | bytes 3145760 | tf_op jit(solution)/shard_map/ppermute | solution.py:34
  5.9 0.0 copy-start
  5.9 1.9 %copy-done = bf16[384,4096]{1,0:T(8,128)(2,1)S(1)} copy-done((bf16[384,4096]{1,0:T(8,128)(2,1)S(1)}, bf16[384,4096]{1,0:T(8,128)(2,1)}, u32[]{:S(2)}) %copy-start) | copy-done | bytes 3145752
  7.8 0.0 copy-start.2
  7.8 1.2 %copy-done.2 = bf16[4096,128]{1,0:T(8,128)(2,1)S(1)} copy-done((bf16[4096,128]{1,0:T(8,128)(2,1)S(1)}, bf16[4096,128]{1,0:T(8,128)(2,1)}, u32[]{:S(2)}) %copy-start.2) | copy-done | bytes 1048600
  9.0 0.0 copy-start.4
  9.0 0.0 copy-start.5
  9.0 0.0 copy-start.6
  9.0 0.0 copy-start.3
  9.0 1.8 %shard_map.56.refs_3_.refs_5_ = f32[768,128]{1,0:T(8,128)S(1)} custom-call(bf16[384,4096]{1,0:T(8,128)(2,1)S(1)} %copy-done, bf16[384,4096]{1,0:T(8,128)(2,1)S(1)} %collective-permute-done.refs_1_, bf16[4096,128]{1,0:T(8,128)(2,1)S(1)} %copy-done.2), custom_call_target="tpu_custom_call" | custom-call | bytes 1024 | tf_op jit(solution)/shard_map/pallas_call | solution.py:54
  10.8 0.0 copy-start.1
  10.8 0.0 copy-done.4
  10.8 0.0 copy-done.5
  10.8 0.0 copy-done.6
  10.8 0.7 %shard_map.57 = (bf16[512,512]{1,0:T(8,128)(2,1)S(1)}, bf16[128,384]{1,0:T(8,128)(2,1)S(1)}, bf16[384,128]{1,0:T(8,128)(2,1)S(1)}) custom-call(bf16[1,512,512]{2,1,0:T(8,128)(2,1)S(1)} %copy-done.4, s32[1,512]{1,0:T(1,128)S(1)} %copy-done.5, s32[1,128]{1,0:T(1,128)S(1)} %bitcast.1, f32[768,128]{1,0:T(8,128)S(1)} %shard_map.56.refs_3_.refs_5_), custom_call_target="tpu_custom_call" | custom-call | bytes 1024 | tf_op jit(solution)/shard_map/pallas_call | solution.py:54
  11.5 0.0 copy-done.3
  11.5 4.4 %collective-permute-start.4 = (bf16[4096,128]{1,0:T(8,128)(2,1)S(1)}, bf16[4096,128]{1,0:T(8,128)(2,1)S(1)}, u32[]{:S(2)}, u32[]{:S(2)}) collective-permute-start(bf16[4096,128]{1,0:T(8,128)(2,1)S(1)} %copy-done.3), channel_id=1, source_target_pairs={{4,20},{12,28},{20,4},{28,12},{5,21},{13,29},{21,5},{29,13},{6,22}... | collective-permute-start | bytes 3145736 | tf_op jit(solution)/shard_map/ppermute | solution.py:34
  16.0 3.1 %collective-permute-start.5 = (bf16[4096,128]{1,0:T(8,128)(2,1)S(1)}, bf16[4096,128]{1,0:T(8,128)(2,1)S(1)}, u32[]{:S(2)}, u32[]{:S(2)}) collective-permute-start(bf16[4096,128]{1,0:T(8,128)(2,1)S(1)} %copy-done.3), channel_id=1, source_target_pairs={{4,12},{12,4},{20,28},{28,20},{5,13},{13,5},{21,29},{29,21},{6,14}... | collective-permute-start | bytes 3145736 | tf_op jit(solution)/shard_map/ppermute | solution.py:34
  19.1 0.0 collective-permute-done.1.refs_0_.refs_3_
  19.1 7.6 %collective-permute-done.2.refs_1_.refs_2_ = bf16[4096,128]{1,0:T(8,128)(2,1)S(1)} collective-permute-done((bf16[4096,128]{1,0:T(8,128)(2,1)}, bf16[4096,128]{1,0:T(8,128)(2,1)S(1)}, u32[]{:S(2)}, u32[]{:S(2)}) %collective-permute-start.2) | collective-permute-done | bytes 1048608 | tf_op jit(solution)/shard_map/ppermute | solution.py:44
  26.8 0.7 %collective-permute-start.7 = (bf16[2688,128]{1,0:T(8,128)(2,1)S(1)}, bf16[2688,128]{1,0:T(8,128)(2,1)S(1)}, u32[]{:S(2)}, u32[]{:S(2)}) collective-permute-start(bf16[2688,128]{1,0:T(8,128)(2,1)S(1)} %get-tuple-element.30), channel_id=1, source_target_pairs={{0,16},{8,24},{16,0},{24,8},{1,17},{9,25},{17,1},{25,9},{2,18},{10... | collective-permute-start | bytes 2064392 | tf_op jit(solution)/shard_map/ppermute | solution.py:34
  27.5 6.7 %collective-permute-done.4.refs_0_.refs_5_ = bf16[4096,128]{1,0:T(8,128)(2,1)S(1)} collective-permute-done((bf16[4096,128]{1,0:T(8,128)(2,1)S(1)}, bf16[4096,128]{1,0:T(8,128)(2,1)S(1)}, u32[]{:S(2)}, u32[]{:S(2)}) %collective-permute-start.4) | collective-permute-done | bytes 1048608 | tf_op jit(solution)/shard_map/ppermute | solution.py:34
  34.2 1.5 %collective-permute-done.5.refs_1_.refs_4_ = bf16[4096,128]{1,0:T(8,128)(2,1)S(1)} collective-permute-done((bf16[4096,128]{1,0:T(8,128)(2,1)S(1)}, bf16[4096,128]{1,0:T(8,128)(2,1)S(1)}, u32[]{:S(2)}, u32[]{:S(2)}) %collective-permute-start.5) | collective-permute-done | bytes 1048608 | tf_op jit(solution)/shard_map/ppermute | solution.py:34
  35.7 0.4 shard_map.58
  36.1 2.6 %collective-permute-start.8 = (bf16[2304,128]{1,0:T(8,128)(2,1)S(1)}, bf16[2304,128]{1,0:T(8,128)(2,1)S(1)}, u32[]{:S(2)}, u32[]{:S(2)}) collective-permute-start(bf16[2304,128]{1,0:T(8,128)(2,1)S(1)} %get-tuple-element.31), channel_id=1, source_target_pairs={{4,20},{12,28},{20,4},{28,12},{5,21},{13,29},{21,5},{29,13},{6,22}... | collective-permute-start | bytes 1769480 | tf_op jit(solution)/shard_map/ppermute | solution.py:34
  38.7 2.7 %collective-permute-start.6 = (bf16[1792,128]{1,0:T(8,128)(2,1)S(1)}, bf16[1792,128]{1,0:T(8,128)(2,1)S(1)}, u32[]{:S(2)}, u32[]{:S(2)}) collective-permute-start(bf16[1792,128]{1,0:T(8,128)(2,1)S(1)} %get-tuple-element.29), channel_id=1, source_target_pairs={{4,12},{12,4},{20,28},{28,20},{5,13},{13,5},{21,29},{29,21},{6,14}... | collective-permute-start | bytes 1376264 | tf_op jit(solution)/shard_map/ppermute | solution.py:34
  41.4 0.7 collective-permute-start.3
  42.1 0.0 copy-done.1
  42.1 1.8 %shard_map.59 = (f32[768,128]{1,0:T(8,128)S(1)}, f32[768,128]{1,0:T(8,128)S(1)}) custom-call(bf16[384,4096]{1,0:T(8,128)(2,1)S(1)} %copy-done.1, bf16[384,4096]{1,0:T(8,128)(2,1)S(1)} %collective-permute-done.refs_1_, bf16[4096,128]{1,0:T(8,128)(2,1)S(1)} %collective-permute-done.2.refs_1_.refs_2_, ...), custom_call_target="tpu_custom_call" | custom-call | bytes 1024 | tf_op jit(solution)/shard_map/pallas_call | solution.py:54
  43.9 0.0 collective-permute-done.7.refs_2_
  43.9 3.1 %collective-permute-done.8.refs_3_ = bf16[2304,128]{1,0:T(8,128)(2,1)S(1)} collective-permute-done((bf16[2304,128]{1,0:T(8,128)(2,1)S(1)}, bf16[2304,128]{1,0:T(8,128)(2,1)S(1)}, u32[]{:S(2)}, u32[]{:S(2)}) %collective-permute-start.8) | collective-permute-done | bytes 589856 | tf_op jit(solution)/shard_map/ppermute | solution.py:34
  47.0 1.1 %shard_map.60.refs_4_ = f32[768,128]{1,0:T(8,128)S(1)} custom-call(bf16[384,4096]{1,0:T(8,128)(2,1)S(1)} %copy-done.1, bf16[384,4096]{1,0:T(8,128)(2,1)S(1)} %collective-permute-done.refs_1_, bf16[2688,128]{1,0:T(8,128)(2,1)S(1)} %collective-permute-done.7.refs_2_, bf16[2304,128]{1,0:T(8,128)(2,1)S(1)} %collective-permute-done.8.refs_3_, ...), custom_call_target="tpu_custom_call" | custom-call | bytes 1024 | tf_op jit(solution)/shard_map/pallas_call | solution.py:54
  48.1 0.0 collective-permute-done.3.refs_2_
  48.1 0.0 collective-permute-done.6.refs_3_
  48.1 1.1 %shard_map.61 = (f32[768,128]{1,0:T(8,128)S(1)}, bf16[768,128]{1,0:T(8,128)(2,1)S(1)}, bf16[768,128]{1,0:T(8,128)(2,1)S(1)}, bf16[768,128]{1,0:T(8,128)(2,1)S(1)}) custom-call(bf16[384,4096]{1,0:T(8,128)(2,1)S(1)} %copy-done.1, bf16[384,4096]{1,0:T(8,128)(2,1)S(1)} %collective-permute-done.refs_1_, bf16[1408,128]{1,0:T(8,128)(2,1)S(1)} %collective-permute-done.3.refs_2_, ...), custom_call_target="tpu_custom_call" | custom-call | bytes 1024 | tf_op jit(solution)/shard_map/pallas_call | solution.py:54
  49.2 3.4 %collective-permute-start.10 = (bf16[768,128]{1,0:T(8,128)(2,1)S(1)}, bf16[768,128]{1,0:T(8,128)(2,1)S(1)}, u32[]{:S(2)}, u32[]{:S(2)}) collective-permute-start(bf16[768,128]{1,0:T(8,128)(2,1)S(1)} %get-tuple-element.36), channel_id=1, source_target_pairs={{0,3},{1,2},{2,1},{3,0},{4,7},{5,6},{6,5},{7,4},{8,11},{9,10},{10,... | collective-permute-start | bytes 589832 | tf_op jit(solution)/shard_map/ppermute | solution.py:34
  52.5 0.0 collective-permute-start.11
  52.5 0.4 collective-permute-start.9
  52.9 2.9 %collective-permute-done.10.refs_2_ = bf16[768,128]{1,0:T(8,128)(2,1)S(1)} collective-permute-done((bf16[768,128]{1,0:T(8,128)(2,1)S(1)}, bf16[768,128]{1,0:T(8,128)(2,1)S(1)}, u32[]{:S(2)}, u32[]{:S(2)}) %collective-permute-start.10) | collective-permute-done | bytes 196640 | tf_op jit(solution)/shard_map/ppermute | solution.py:34
  55.8 5.3 %collective-permute-done.11.refs_3_ = bf16[768,128]{1,0:T(8,128)(2,1)S(1)} collective-permute-done((bf16[768,128]{1,0:T(8,128)(2,1)S(1)}, bf16[768,128]{1,0:T(8,128)(2,1)S(1)}, u32[]{:S(2)}, u32[]{:S(2)}) %collective-permute-start.11) | collective-permute-done | bytes 196640 | tf_op jit(solution)/shard_map/ppermute | solution.py:34
  61.1 0.0 collective-permute-done.9.refs_1_
  61.1 0.1 shard_map.62
  61.2 0.1 collective-permute-start.12
  61.2 1.4 %collective-permute-done.12.refs_1_ = f32[384,128]{1,0:T(8,128)S(1)} collective-permute-done((f32[384,128]{1,0:T(8,128)S(1)}, f32[384,128]{1,0:T(8,128)S(1)}, u32[]{:S(2)}, u32[]{:S(2)}) %collective-permute-start.12) | collective-permute-done | bytes 196640 | tf_op jit(solution)/shard_map/ppermute | solution.py:34
  62.7 0.3 shard_map.63
  63.0 1.3 %collective-permute-start.14 = (bf16[128,384]{1,0:T(8,128)(2,1)S(1)}, bf16[128,384]{1,0:T(8,128)(2,1)S(1)}, u32[]{:S(2)}, u32[]{:S(2)}) collective-permute-start(bf16[128,384]{1,0:T(8,128)(2,1)S(1)} %get-tuple-element.46), channel_id=1, source_target_pairs={{0,4},{4,8},{8,12},{12,16},{16,20},{20,24},{24,28},{28,0},{1,5},{5... | collective-permute-start | bytes 294920 | tf_op jit(solution)/shard_map/ppermute | solution.py:225
  64.2 0.0 collective-permute-start.13
  64.2 0.4 shard_map.64
  64.7 3.2 %collective-permute-done.13.refs_4_ = bf16[128,256]{1,0:T(8,128)(2,1)S(1)} collective-permute-done((bf16[128,256]{1,0:T(8,128)(2,1)S(1)}, bf16[128,256]{1,0:T(8,128)(2,1)S(1)}, u32[]{:S(2)}, u32[]{:S(2)}) %collective-permute-start.13) | collective-permute-done | bytes 65568 | tf_op jit(solution)/shard_map/ppermute | solution.py:225
  67.9 0.0 collective-permute-done.14.refs_5_
  67.9 1.2 %shard_map.65 = f32[384,256]{1,0:T(8,128)} custom-call(f32[384,256]{1,0:T(8,128)S(1)} %get-tuple-element.42.refs_0_, bf16[128,512]{1,0:T(8,128)(2,1)S(1)} %get-tuple-element.43.refs_1_, bf16[512,512]{1,0:T(8,128)(2,1)S(1)} %get-tuple-element.27.refs_2_.refs_1_, bf16[384,128]{1,0:T(8,128)(2,1)S(1)} %get-tuple-element.44.refs_3_, ...), custom_call_target="tpu_custom_call" | custom-call | bytes 1024 | tf_op jit(solution)/shard_map/pallas_call | solution.py:54
  (1 shorter events, 0.0 us)
Async XLA Ops:
  0.0 5.9 %collective-permute-start = (bf16[384,4096]{1,0:T(8,128)(2,1)}, bf16[384,4096]{1,0:T(8,128)(2,1)S(1)}, u32[]{:S(2)}, u32[]{:S(2)}) collective-permute-start(bf16[384,4096]{1,0:T(8,128)(2,1)} %refs_0_.9), channel_id=1, source_target_pairs={{0,4},{4,0},{8,12},{12,8},{16,20},{20,16},{24,28},{28,24},{1,5},{5... | collective-permute-start | bytes 9437192 | tf_op jit(solution)/shard_map/ppermute | solution.py:34
  0.1 19.0 %collective-permute-start.1 = (bf16[4096,128]{1,0:T(8,128)(2,1)}, bf16[4096,128]{1,0:T(8,128)(2,1)S(1)}, u32[]{:S(2)}, u32[]{:S(2)}) collective-permute-start(bf16[4096,128]{1,0:T(8,128)(2,1)} %refs_2_.1), channel_id=1, source_target_pairs={{0,16},{1,17},{2,18},{3,19},{4,5},{5,4},{6,7},{7,6},{8,24},{9,25},... | collective-permute-start | bytes 3145736 | tf_op jit(solution)/shard_map/ppermute | solution.py:44
  2.8 23.9 %collective-permute-start.2 = (bf16[4096,128]{1,0:T(8,128)(2,1)}, bf16[4096,128]{1,0:T(8,128)(2,1)S(1)}, u32[]{:S(2)}, u32[]{:S(2)}) collective-permute-start(bf16[4096,128]{1,0:T(8,128)(2,1)} %refs_2_.1), channel_id=1, source_target_pairs={{0,8},{1,9},{2,10},{3,11},{4,5},{5,4},{6,7},{7,6},{8,0},{9,1},{10,... | collective-permute-start | bytes 3145736 | tf_op jit(solution)/shard_map/ppermute | solution.py:44
  5.9 1.9 %copy-start = (bf16[384,4096]{1,0:T(8,128)(2,1)S(1)}, bf16[384,4096]{1,0:T(8,128)(2,1)}, u32[]{:S(2)}) copy-start(bf16[384,4096]{1,0:T(8,128)(2,1)} %refs_0_.9) | copy-start | bytes 9437188
  7.8 1.2 %copy-start.2 = (bf16[4096,128]{1,0:T(8,128)(2,1)S(1)}, bf16[4096,128]{1,0:T(8,128)(2,1)}, u32[]{:S(2)}) copy-start(bf16[4096,128]{1,0:T(8,128)(2,1)} %refs_2_.1) | copy-start | bytes 3145732
  9.0 1.8 %copy-start.4 = (bf16[1,512,512]{2,1,0:T(8,128)(2,1)S(1)}, bf16[1,512,512]{2,1,0:T(8,128)(2,1)}, u32[]{:S(2)}) copy-start(bf16[1,512,512]{2,1,0:T(8,128)(2,1)} %refs_0_.6) | copy-start | bytes 1572868
  9.0 1.8 %copy-start.5 = (s32[1,512]{1,0:T(1,128)S(1)}, s32[1,512]{1,0:T(1,128)}, u32[]{:S(2)}) copy-start(s32[1,512]{1,0:T(1,128)} %refs_1_.1) | copy-start | bytes 6148
  9.0 1.8 %copy-start.6 = (s32[128]{0:T(128)S(1)}, s32[128]{0:T(128)}, u32[]{:S(2)}) copy-start(s32[128]{0:T(128)} %param.9) | copy-start | bytes 1540
  9.0 2.5 %copy-start.3 = (bf16[4096,128]{1,0:T(8,128)(2,1)S(1)}, bf16[4096,128]{1,0:T(8,128)(2,1)}, u32[]{:S(2)}) copy-start(bf16[4096,128]{1,0:T(8,128)(2,1)} %refs_2_.1) | copy-start | bytes 3145732
  10.8 31.3 %copy-start.1 = (bf16[384,4096]{1,0:T(8,128)(2,1)S(1)}, bf16[384,4096]{1,0:T(8,128)(2,1)}, u32[]{:S(2)}) copy-start(bf16[384,4096]{1,0:T(8,128)(2,1)} %refs_0_.9) | copy-start | bytes 9437188
  11.5 22.7 %collective-permute-start.4 = (bf16[4096,128]{1,0:T(8,128)(2,1)S(1)}, bf16[4096,128]{1,0:T(8,128)(2,1)S(1)}, u32[]{:S(2)}, u32[]{:S(2)}) collective-permute-start(bf16[4096,128]{1,0:T(8,128)(2,1)S(1)} %copy-done.3), channel_id=1, source_target_pairs={{4,20},{12,28},{20,4},{28,12},{5,21},{13,29},{21,5},{29,13},{6,22}... | collective-permute-start | bytes 3145736 | tf_op jit(solution)/shard_map/ppermute | solution.py:34
  16.0 19.7 %collective-permute-start.5 = (bf16[4096,128]{1,0:T(8,128)(2,1)S(1)}, bf16[4096,128]{1,0:T(8,128)(2,1)S(1)}, u32[]{:S(2)}, u32[]{:S(2)}) collective-permute-start(bf16[4096,128]{1,0:T(8,128)(2,1)S(1)} %copy-done.3), channel_id=1, source_target_pairs={{4,12},{12,4},{20,28},{28,20},{5,13},{13,5},{21,29},{29,21},{6,14}... | collective-permute-start | bytes 3145736 | tf_op jit(solution)/shard_map/ppermute | solution.py:34
  26.8 17.2 %collective-permute-start.7 = (bf16[2688,128]{1,0:T(8,128)(2,1)S(1)}, bf16[2688,128]{1,0:T(8,128)(2,1)S(1)}, u32[]{:S(2)}, u32[]{:S(2)}) collective-permute-start(bf16[2688,128]{1,0:T(8,128)(2,1)S(1)} %get-tuple-element.30), channel_id=1, source_target_pairs={{0,16},{8,24},{16,0},{24,8},{1,17},{9,25},{17,1},{25,9},{2,18},{10... | collective-permute-start | bytes 2064392 | tf_op jit(solution)/shard_map/ppermute | solution.py:34
  36.1 10.9 %collective-permute-start.8 = (bf16[2304,128]{1,0:T(8,128)(2,1)S(1)}, bf16[2304,128]{1,0:T(8,128)(2,1)S(1)}, u32[]{:S(2)}, u32[]{:S(2)}) collective-permute-start(bf16[2304,128]{1,0:T(8,128)(2,1)S(1)} %get-tuple-element.31), channel_id=1, source_target_pairs={{4,20},{12,28},{20,4},{28,12},{5,21},{13,29},{21,5},{29,13},{6,22}... | collective-permute-start | bytes 1769480 | tf_op jit(solution)/shard_map/ppermute | solution.py:34
  38.7 9.4 %collective-permute-start.6 = (bf16[1792,128]{1,0:T(8,128)(2,1)S(1)}, bf16[1792,128]{1,0:T(8,128)(2,1)S(1)}, u32[]{:S(2)}, u32[]{:S(2)}) collective-permute-start(bf16[1792,128]{1,0:T(8,128)(2,1)S(1)} %get-tuple-element.29), channel_id=1, source_target_pairs={{4,12},{12,4},{20,28},{28,20},{5,13},{13,5},{21,29},{29,21},{6,14}... | collective-permute-start | bytes 1376264 | tf_op jit(solution)/shard_map/ppermute | solution.py:34
  41.4 6.7 %collective-permute-start.3 = (bf16[1408,128]{1,0:T(8,128)(2,1)S(1)}, bf16[1408,128]{1,0:T(8,128)(2,1)S(1)}, u32[]{:S(2)}, u32[]{:S(2)}) collective-permute-start(bf16[1408,128]{1,0:T(8,128)(2,1)S(1)} %get-tuple-element.26.refs_2_), channel_id=1, source_target_pairs={{0,8},{8,0},{16,24},{24,16},{1,9},{9,1},{17,25},{25,17},{2,10},{10... | collective-permute-start | bytes 1081352 | tf_op jit(solution)/shard_map/ppermute | solution.py:34
  49.2 6.6 %collective-permute-start.10 = (bf16[768,128]{1,0:T(8,128)(2,1)S(1)}, bf16[768,128]{1,0:T(8,128)(2,1)S(1)}, u32[]{:S(2)}, u32[]{:S(2)}) collective-permute-start(bf16[768,128]{1,0:T(8,128)(2,1)S(1)} %get-tuple-element.36), channel_id=1, source_target_pairs={{0,3},{1,2},{2,1},{3,0},{4,7},{5,6},{6,5},{7,4},{8,11},{9,10},{10,... | collective-permute-start | bytes 589832 | tf_op jit(solution)/shard_map/ppermute | solution.py:34
  52.5 8.5 %collective-permute-start.11 = (bf16[768,128]{1,0:T(8,128)(2,1)S(1)}, bf16[768,128]{1,0:T(8,128)(2,1)S(1)}, u32[]{:S(2)}, u32[]{:S(2)}) collective-permute-start(bf16[768,128]{1,0:T(8,128)(2,1)S(1)} %get-tuple-element.37), channel_id=1, source_target_pairs={{0,2},{1,3},{2,0},{3,1},{4,6},{5,7},{6,4},{7,5},{8,10},{9,11},{10,... | collective-permute-start | bytes 589832 | tf_op jit(solution)/shard_map/ppermute | solution.py:34
  52.5 8.5 %collective-permute-start.9 = (bf16[768,128]{1,0:T(8,128)(2,1)S(1)}, bf16[768,128]{1,0:T(8,128)(2,1)S(1)}, u32[]{:S(2)}, u32[]{:S(2)}) collective-permute-start(bf16[768,128]{1,0:T(8,128)(2,1)S(1)} %get-tuple-element.35), channel_id=1, source_target_pairs={{0,1},{1,0},{2,3},{3,2},{4,5},{5,4},{6,7},{7,6},{8,9},{9,8},{10,11... | collective-permute-start | bytes 589832 | tf_op jit(solution)/shard_map/ppermute | solution.py:34
  61.2 1.5 %collective-permute-start.12 = (f32[384,128]{1,0:T(8,128)S(1)}, f32[384,128]{1,0:T(8,128)S(1)}, u32[]{:S(2)}, u32[]{:S(2)}) collective-permute-start(f32[384,128]{1,0:T(8,128)S(1)} %get-tuple-element.39), channel_id=1, source_target_pairs={{0,4},{4,0},{8,12},{12,8},{16,20},{20,16},{24,28},{28,24},{1,5},{5... | collective-permute-start | bytes 589832 | tf_op jit(solution)/shard_map/ppermute | solution.py:34
  63.0 5.0 %collective-permute-start.14 = (bf16[128,384]{1,0:T(8,128)(2,1)S(1)}, bf16[128,384]{1,0:T(8,128)(2,1)S(1)}, u32[]{:S(2)}, u32[]{:S(2)}) collective-permute-start(bf16[128,384]{1,0:T(8,128)(2,1)S(1)} %get-tuple-element.46), channel_id=1, source_target_pairs={{0,4},{4,8},{8,12},{12,16},{16,20},{20,24},{24,28},{28,0},{1,5},{5... | collective-permute-start | bytes 294920 | tf_op jit(solution)/shard_map/ppermute | solution.py:225
  64.2 3.7 %collective-permute-start.13 = (bf16[128,256]{1,0:T(8,128)(2,1)S(1)}, bf16[128,256]{1,0:T(8,128)(2,1)S(1)}, u32[]{:S(2)}, u32[]{:S(2)}) collective-permute-start(bf16[128,256]{1,0:T(8,128)(2,1)S(1)} %get-tuple-element.45), channel_id=1, source_target_pairs={{0,28},{4,0},{8,4},{12,8},{16,12},{20,16},{24,20},{28,24},{1,29},{... | collective-permute-start | bytes 196616 | tf_op jit(solution)/shard_map/ppermute | solution.py:225

commit v21 on v20

--- a/solution.py
+++ b/solution.py
@@ -80,8 +80,8 @@
     @pl.when(core() == one)
     def _():
         copies = [
-            pltpu.make_async_copy(near.at[pl.ds(0, cut)], top, done.at[0]),
-            pltpu.make_async_copy(far.at[pl.ds(cut, rest)], bottom, done.at[1]),
+            pltpu.make_async_copy(far.at[pl.ds(0, cut)], top, done.at[0]),
+            pltpu.make_async_copy(near.at[pl.ds(cut, rest)], bottom, done.at[1]),
         ]
         for copy in copies:
             copy.start()
@@ -159,11 +159,11 @@
     received = [paired(rotation, NEAR, 0), paired(rotation, FAR, 0)]
     theirs = exchanged(wavefunctions, "domain", CORE)
     block = [shape(2 * rows, width)]
-    own = call(own_kernel, block, (wavefunctions, theirs, rotation))[0]
-    operator = operator(own)
+    operator = operator(theirs)
     later, _ = lax.optimization_barrier((rotation, operator[0]))
+    own = call(own_kernel, block, (wavefunctions, theirs, rotation), after=(later,))[0]
     received += [exchanged(later, "domain", NEAR, CORE), exchanged(later, "domain", FAR, CORE)]
-    passed, previous = [], []
+    passed, previous = [], [own]
     for one, share in ((0, 21), (CORE, 18)):
         cut = states * share // 32
         outs = [shape(count, width, dtype=BF16) for count in (cut, states - cut)]
@@ -171,14 +171,17 @@
         kernel = functools.partial(pieces_kernel, one)
         top, bottom = call(kernel, outs, pair, after=previous, scratch=[pltpu.SemaphoreType.DMA((2,))])
         previous = [bottom]
-        passed += [exchanged(top, "domain", FAR, one), exchanged(bottom, "domain", NEAR, one)]
+        if one:
+            passed += [paired(top, NEAR, one), paired(bottom, FAR, one)]
+        else:
+            passed += [exchanged(top, "domain", NEAR, one), exchanged(bottom, "domain", FAR, one)]
     early = call(early_kernel, block * 2, (wavefunctions, theirs, *received))
     outs = block + [shape(2 * rows, width, dtype=BF16)] * (bands - 1)
     scratch = [pltpu.VMEM((2 * rows, width), F32)]
     upper = call(upper_kernel, block, (wavefunctions, theirs, *passed[::2]), after=early[:1])[0]
     operands = (wavefunctions, theirs, *passed[1::2], upper, own, *early)
     kept, *sent = call(late_kernel, outs, operands, scratch=scratch)
-    parts = [exchanged(sent[mask - 1], "band", mask) for mask in (1, *reversed(range(2, bands)))]
+    parts = [exchanged(sent[mask - 1], "band", mask) for mask in reversed(range(1, bands))]
     mine, others = call(sum_kernel, [shape(rows, width)] * 2, (kept, *parts))
     return mine, exchanged(others, "domain", CORE), operator
 

time: 69.5 us -> 68.8 us (0.990)
  starting transfers between devices: 22.2 us -> 20.5 us
    ppermute x11 -> x9, starting transfers between devices: 18.1 us -> 13 us  [exchanged(): lax.ppermute(value, axis, [(source, source ^ mask) for source in sources...]
    ppermute x2 -> x4, waiting for transfers between devices: 7.63 us -> 12.6 us  [paired(): return lax.ppermute(value, ('domain', 'band'), pairs)]
    ppermute x11 -> x9, waiting for transfers between devices: 23.9 us -> 19.3 us  [exchanged(): lax.ppermute(value, axis, [(source, source ^ mask) for source in sources...]
    ppermute x2 -> x4, starting transfers between devices: 2.78 us -> 6.18 us  [paired(): return lax.ppermute(value, ('domain', 'band'), pairs)]
    unnamed x14 -> x10, local copies, waits for them, and re-layouts: 3.13 us -> 3.6 us
  transfers between devices with their start and end apart: 15 -> 15, of which waited for: 9 -> 8; matrix products, arithmetic and copies ran while one was open for 0% -> 0% of each run, Pallas kernels for 9% -> 9%
where the time goes in v21:
time: 68.8 us; the launch traced here: 68.5 us
  waiting for transfers between devices  35.4 us (51%)
  starting transfers between devices  20.5 us (30%)
  Pallas kernels  8.83 us (13%)
  local copies, waits for them, and re-layouts  3.6 us (5%)
    ppermute x9, waiting for transfers between devices, exchanged(): lax.ppermute(value, axis, [(source, source ^ mask) for source in sources...  19.3 us
    ppermute x9, starting transfers between devices, exchanged(): lax.ppermute(value, axis, [(source, source ^ mask) for source in sources...  13 us
    ppermute x4, waiting for transfers between devices, paired(): return lax.ppermute(value, ('domain', 'band'), pairs)  12.6 us
    pallas_call x11, Pallas kernels, call(): pl.pallas_call(body, out_shape=outs, in_specs=[pl.BlockSpec(memory_space=...  8.83 us
    ppermute x4, starting transfers between devices, paired(): return lax.ppermute(value, ('domain', 'band'), pairs)  6.18 us
    unnamed x10, local copies, waits for them, and re-layouts  3.6 us
    ppermute x2, waiting for transfers between devices, rotated(): lax.ppermute(value, axis, [(source, (source + steps) % count) for source...  3.46 us
  transfers between devices with their start and end apart: 15, of which 8 were waited for; matrix products, arithmetic and copies ran while one was open for 0% of the time, Pallas kernels for 9%

profile of v21, /device:TPU:1, one launch (start us, length us, event | category | flops | bytes accessed | tf_op | source)
XLA Modules:
  0.0 68.5 jit_solution(5652043640537202535)
XLA Ops:
  0.0 0.0 copy-start
  0.0 0.1 collective-permute-start
  0.1 2.7 %collective-permute-start.2 = (bf16[4096,128]{1,0:T(8,128)(2,1)}, bf16[4096,128]{1,0:T(8,128)(2,1)S(1)}, u32[]{:S(2)}, u32[]{:S(2)}) collective-permute-start(bf16[4096,128]{1,0:T(8,128)(2,1)} %refs_3_), channel_id=1, source_target_pairs={{0,8},{1,9},{2,10},{3,11},{4,5},{5,4},{6,7},{7,6},{8,0},{9,1},{10,... | collective-permute-start | bytes 3145736 | tf_op jit(solution)/shard_map/ppermute | solution.py:44
  2.8 0.0 collective-permute-start.1
  2.8 3.0 %collective-permute-done.refs_3_.refs_1_ = bf16[384,4096]{1,0:T(8,128)(2,1)S(1)} collective-permute-done((bf16[384,4096]{1,0:T(8,128)(2,1)}, bf16[384,4096]{1,0:T(8,128)(2,1)S(1)}, u32[]{:S(2)}, u32[]{:S(2)}) %collective-permute-start) | collective-permute-done | bytes 3145760 | tf_op jit(solution)/shard_map/ppermute | solution.py:34
  5.9 0.0 copy-start.2
  5.9 1.0 %copy-done.2 = bf16[1,512,512]{2,1,0:T(8,128)(2,1)S(1)} copy-done((bf16[1,512,512]{2,1,0:T(8,128)(2,1)S(1)}, bf16[1,512,512]{2,1,0:T(8,128)(2,1)}, u32[]{:S(2)}) %copy-start.2) | copy-done | bytes 524312
  6.9 0.0 copy-start.3
  6.9 0.7 copy-done.3
  7.6 0.0 copy-start.4
  7.6 0.7 copy-done.4
  8.3 0.7 %shard_map.55 = (bf16[512,512]{1,0:T(8,128)(2,1)S(1)}, bf16[128,384]{1,0:T(8,128)(2,1)S(1)}, bf16[384,128]{1,0:T(8,128)(2,1)S(1)}) custom-call(bf16[1,512,512]{2,1,0:T(8,128)(2,1)S(1)} %copy-done.2, s32[1,512]{1,0:T(1,128)S(1)} %copy-done.3, s32[1,128]{1,0:T(1,128)S(1)} %bitcast.1, bf16[384,4096]{1,0:T(8,128)(2,1)S(1)} %collective-permute-done.refs_3_.refs_1_), custom_call_target="tpu_custom_call" | custom-call | bytes 1024 | tf_op jit(solution)/shard_map/pallas_call | solution.py:54
  9.0 4.3 %collective-permute-start.5 = (bf16[4096,128]{1,0:T(8,128)(2,1)}, bf16[4096,128]{1,0:T(8,128)(2,1)S(1)}, u32[]{:S(2)}, u32[]{:S(2)}) collective-permute-start(bf16[4096,128]{1,0:T(8,128)(2,1)} %refs_3_), channel_id=1, source_target_pairs={{4,12},{12,4},{20,28},{28,20},{5,13},{13,5},{21,29},{29,21},{6,14}... | collective-permute-start | bytes 3145736 | tf_op jit(solution)/shard_map/ppermute | solution.py:34
  13.2 3.1 %collective-permute-start.4 = (bf16[4096,128]{1,0:T(8,128)(2,1)}, bf16[4096,128]{1,0:T(8,128)(2,1)S(1)}, u32[]{:S(2)}, u32[]{:S(2)}) collective-permute-start(bf16[4096,128]{1,0:T(8,128)(2,1)} %refs_3_), channel_id=1, source_target_pairs={{4,20},{12,28},{20,4},{28,12},{5,21},{13,29},{21,5},{29,13},{6,22}... | collective-permute-start | bytes 3145736 | tf_op jit(solution)/shard_map/ppermute | solution.py:34
  16.4 0.0 copy-done
  16.4 0.0 copy-start.1
  16.4 1.2 %copy-done.1 = bf16[4096,128]{1,0:T(8,128)(2,1)S(1)} copy-done((bf16[4096,128]{1,0:T(8,128)(2,1)S(1)}, bf16[4096,128]{1,0:T(8,128)(2,1)}, u32[]{:S(2)}) %copy-start.1) | copy-done | bytes 1048600
  17.6 1.8 %shard_map.56.refs_2_.refs_5_ = f32[768,128]{1,0:T(8,128)S(1)} custom-call(bf16[384,4096]{1,0:T(8,128)(2,1)S(1)} %copy-done, bf16[384,4096]{1,0:T(8,128)(2,1)S(1)} %collective-permute-done.refs_3_.refs_1_, bf16[4096,128]{1,0:T(8,128)(2,1)S(1)} %copy-done.1, bf16[4096,128]{1,0:T(8,128)(2,1)S(1)} %copy-done.1), custom_call_target="tpu_custom_call" | custom-call | bytes 1024 | tf_op jit(solution)/shard_map/pallas_call | solution.py:54
  19.4 0.0 collective-permute-done.2.refs_1_.refs_2_
  19.4 9.1 %collective-permute-done.1.refs_0_.refs_3_ = bf16[4096,128]{1,0:T(8,128)(2,1)S(1)} collective-permute-done((bf16[4096,128]{1,0:T(8,128)(2,1)}, bf16[4096,128]{1,0:T(8,128)(2,1)S(1)}, u32[]{:S(2)}, u32[]{:S(2)}) %collective-permute-start.1) | collective-permute-done | bytes 1048608 | tf_op jit(solution)/shard_map/ppermute | solution.py:44
  28.5 0.7 %collective-permute-start.7 = (bf16[2688,128]{1,0:T(8,128)(2,1)S(1)}, bf16[2688,128]{1,0:T(8,128)(2,1)S(1)}, u32[]{:S(2)}, u32[]{:S(2)}) collective-permute-start(bf16[2688,128]{1,0:T(8,128)(2,1)S(1)} %get-tuple-element.30), channel_id=1, source_target_pairs={{0,8},{8,0},{16,24},{24,16},{1,9},{9,1},{17,25},{25,17},{2,10},{10... | collective-permute-start | bytes 2064392 | tf_op jit(solution)/shard_map/ppermute | solution.py:34
  29.2 1.4 %collective-permute-done.5.refs_1_.refs_4_ = bf16[4096,128]{1,0:T(8,128)(2,1)S(1)} collective-permute-done((bf16[4096,128]{1,0:T(8,128)(2,1)}, bf16[4096,128]{1,0:T(8,128)(2,1)S(1)}, u32[]{:S(2)}, u32[]{:S(2)}) %collective-permute-start.5) | collective-permute-done | bytes 1048608 | tf_op jit(solution)/shard_map/ppermute | solution.py:34
  30.6 0.0 collective-permute-done.4.refs_0_.refs_5_
  30.6 0.4 shard_map.58
  31.0 2.2 %collective-permute-start.8 = (bf16[2304,128]{1,0:T(8,128)(2,1)S(1)}, bf16[2304,128]{1,0:T(8,128)(2,1)S(1)}, u32[]{:S(2)}, u32[]{:S(2)}) collective-permute-start(bf16[2304,128]{1,0:T(8,128)(2,1)S(1)} %get-tuple-element.31), channel_id=1, source_target_pairs={{0,1},{1,0},{2,3},{3,2},{4,12},{5,13},{6,14},{7,15},{8,9},{9,8},{1... | collective-permute-start | bytes 1769480 | tf_op jit(solution)/shard_map/ppermute | solution.py:44
  33.2 1.2 %collective-permute-start.6 = (bf16[1792,128]{1,0:T(8,128)(2,1)S(1)}, bf16[1792,128]{1,0:T(8,128)(2,1)S(1)}, u32[]{:S(2)}, u32[]{:S(2)}) collective-permute-start(bf16[1792,128]{1,0:T(8,128)(2,1)S(1)} %get-tuple-element.29), channel_id=1, source_target_pairs={{0,1},{1,0},{2,3},{3,2},{4,20},{5,21},{6,22},{7,23},{8,9},{9,8},{1... | collective-permute-start | bytes 1376264 | tf_op jit(solution)/shard_map/ppermute | solution.py:44
  34.4 0.7 collective-permute-start.3
  35.1 1.8 %shard_map.59 = (f32[768,128]{1,0:T(8,128)S(1)}, f32[768,128]{1,0:T(8,128)S(1)}) custom-call(bf16[384,4096]{1,0:T(8,128)(2,1)S(1)} %copy-done, bf16[384,4096]{1,0:T(8,128)(2,1)S(1)} %collective-permute-done.refs_3_.refs_1_, bf16[4096,128]{1,0:T(8,128)(2,1)S(1)} %collective-permute-done.2.refs_1_.refs_2_, ...), custom_call_target="tpu_custom_call" | custom-call | bytes 1024 | tf_op jit(solution)/shard_map/pallas_call | solution.py:54
  36.9 0.0 collective-permute-done.7.refs_2_
  36.9 3.5 %collective-permute-done.8.refs_3_ = bf16[2304,128]{1,0:T(8,128)(2,1)S(1)} collective-permute-done((bf16[2304,128]{1,0:T(8,128)(2,1)S(1)}, bf16[2304,128]{1,0:T(8,128)(2,1)S(1)}, u32[]{:S(2)}, u32[]{:S(2)}) %collective-permute-start.8) | collective-permute-done | bytes 589856 | tf_op jit(solution)/shard_map/ppermute | solution.py:44
  40.5 1.1 %shard_map.60.refs_4_ = f32[768,128]{1,0:T(8,128)S(1)} custom-call(bf16[384,4096]{1,0:T(8,128)(2,1)S(1)} %copy-done, bf16[384,4096]{1,0:T(8,128)(2,1)S(1)} %collective-permute-done.refs_3_.refs_1_, bf16[2688,128]{1,0:T(8,128)(2,1)S(1)} %collective-permute-done.7.refs_2_, bf16[2304,128]{1,0:T(8,128)(2,1)S(1)} %collective-permute-done.8.refs_3_, ...), custom_call_target="tpu_custom_call" | custom-call | bytes 1024 | tf_op jit(solution)/shard_map/pallas_call | solution.py:54
  41.5 0.0 collective-permute-done.3.refs_2_
  41.6 0.0 collective-permute-done.6.refs_3_
  41.6 1.1 %shard_map.61 = (f32[768,128]{1,0:T(8,128)S(1)}, bf16[768,128]{1,0:T(8,128)(2,1)S(1)}, bf16[768,128]{1,0:T(8,128)(2,1)S(1)}, bf16[768,128]{1,0:T(8,128)(2,1)S(1)}) custom-call(bf16[384,4096]{1,0:T(8,128)(2,1)S(1)} %copy-done, bf16[384,4096]{1,0:T(8,128)(2,1)S(1)} %collective-permute-done.refs_3_.refs_1_, ...), custom_call_target="tpu_custom_call" | custom-call | bytes 1024 | tf_op jit(solution)/shard_map/pallas_call | solution.py:54
  42.6 3.7 %collective-permute-start.9 = (bf16[768,128]{1,0:T(8,128)(2,1)S(1)}, bf16[768,128]{1,0:T(8,128)(2,1)S(1)}, u32[]{:S(2)}, u32[]{:S(2)}) collective-permute-start(bf16[768,128]{1,0:T(8,128)(2,1)S(1)} %get-tuple-element.35), channel_id=1, source_target_pairs={{0,3},{1,2},{2,1},{3,0},{4,7},{5,6},{6,5},{7,4},{8,11},{9,10},{10,... | collective-permute-start | bytes 589832 | tf_op jit(solution)/shard_map/ppermute | solution.py:34
  46.4 0.0 collective-permute-start.10
  46.4 0.4 collective-permute-start.11
  46.7 4.9 %collective-permute-done.9.refs_1_ = bf16[768,128]{1,0:T(8,128)(2,1)S(1)} collective-permute-done((bf16[768,128]{1,0:T(8,128)(2,1)S(1)}, bf16[768,128]{1,0:T(8,128)(2,1)S(1)}, u32[]{:S(2)}, u32[]{:S(2)}) %collective-permute-start.9) | collective-permute-done | bytes 196640 | tf_op jit(solution)/shard_map/ppermute | solution.py:34
  51.6 8.6 %collective-permute-done.10.refs_2_ = bf16[768,128]{1,0:T(8,128)(2,1)S(1)} collective-permute-done((bf16[768,128]{1,0:T(8,128)(2,1)S(1)}, bf16[768,128]{1,0:T(8,128)(2,1)S(1)}, u32[]{:S(2)}, u32[]{:S(2)}) %collective-permute-start.10) | collective-permute-done | bytes 196640 | tf_op jit(solution)/shard_map/ppermute | solution.py:34
  60.2 0.0 collective-permute-done.11.refs_3_
  60.2 0.1 shard_map.62
  60.3 0.1 collective-permute-start.12
  60.4 1.4 %collective-permute-done.12.refs_1_ = f32[384,128]{1,0:T(8,128)S(1)} collective-permute-done((f32[384,128]{1,0:T(8,128)S(1)}, f32[384,128]{1,0:T(8,128)S(1)}, u32[]{:S(2)}, u32[]{:S(2)}) %collective-permute-start.12) | collective-permute-done | bytes 196640 | tf_op jit(solution)/shard_map/ppermute | solution.py:34
  61.8 0.3 shard_map.63
  62.1 1.3 %collective-permute-start.14 = (bf16[128,384]{1,0:T(8,128)(2,1)S(1)}, bf16[128,384]{1,0:T(8,128)(2,1)S(1)}, u32[]{:S(2)}, u32[]{:S(2)}) collective-permute-start(bf16[128,384]{1,0:T(8,128)(2,1)S(1)} %get-tuple-element.46), channel_id=1, source_target_pairs={{0,4},{4,8},{8,12},{12,16},{16,20},{20,24},{24,28},{28,0},{1,5},{5... | collective-permute-start | bytes 294920 | tf_op jit(solution)/shard_map/ppermute | solution.py:228
  63.4 0.0 collective-permute-start.13
  63.4 0.4 shard_map.64
  63.8 3.5 %collective-permute-done.13.refs_4_ = bf16[128,256]{1,0:T(8,128)(2,1)S(1)} collective-permute-done((bf16[128,256]{1,0:T(8,128)(2,1)S(1)}, bf16[128,256]{1,0:T(8,128)(2,1)S(1)}, u32[]{:S(2)}, u32[]{:S(2)}) %collective-permute-start.13) | collective-permute-done | bytes 65568 | tf_op jit(solution)/shard_map/ppermute | solution.py:228
  67.3 0.0 collective-permute-done.14.refs_5_
  67.3 1.2 %shard_map.65 = f32[384,256]{1,0:T(8,128)} custom-call(f32[384,256]{1,0:T(8,128)S(1)} %get-tuple-element.42.refs_0_, bf16[128,512]{1,0:T(8,128)(2,1)S(1)} %get-tuple-element.43.refs_1_, bf16[512,512]{1,0:T(8,128)(2,1)S(1)} %get-tuple-element.26.refs_2_.refs_1_, bf16[384,128]{1,0:T(8,128)(2,1)S(1)} %get-tuple-element.44.refs_3_, ...), custom_call_target="tpu_custom_call" | custom-call | bytes 1024 | tf_op jit(solution)/shard_map/pallas_call | solution.py:54
  (1 shorter events, 0.0 us)
Async XLA Ops:
  0.0 16.4 %copy-start = (bf16[384,4096]{1,0:T(8,128)(2,1)S(1)}, bf16[384,4096]{1,0:T(8,128)(2,1)}, u32[]{:S(2)}) copy-start(bf16[384,4096]{1,0:T(8,128)(2,1)} %refs_0_.9) | copy-start | bytes 9437188
  0.0 5.9 %collective-permute-start = (bf16[384,4096]{1,0:T(8,128)(2,1)}, bf16[384,4096]{1,0:T(8,128)(2,1)S(1)}, u32[]{:S(2)}, u32[]{:S(2)}) collective-permute-start(bf16[384,4096]{1,0:T(8,128)(2,1)} %refs_0_.9), channel_id=1, source_target_pairs={{0,4},{4,0},{8,12},{12,8},{16,20},{20,16},{24,28},{28,24},{1,5},{5... | collective-permute-start | bytes 9437192 | tf_op jit(solution)/shard_map/ppermute | solution.py:34
  0.1 19.3 %collective-permute-start.2 = (bf16[4096,128]{1,0:T(8,128)(2,1)}, bf16[4096,128]{1,0:T(8,128)(2,1)S(1)}, u32[]{:S(2)}, u32[]{:S(2)}) collective-permute-start(bf16[4096,128]{1,0:T(8,128)(2,1)} %refs_3_), channel_id=1, source_target_pairs={{0,8},{1,9},{2,10},{3,11},{4,5},{5,4},{6,7},{7,6},{8,0},{9,1},{10,... | collective-permute-start | bytes 3145736 | tf_op jit(solution)/shard_map/ppermute | solution.py:44
  2.8 25.7 %collective-permute-start.1 = (bf16[4096,128]{1,0:T(8,128)(2,1)}, bf16[4096,128]{1,0:T(8,128)(2,1)S(1)}, u32[]{:S(2)}, u32[]{:S(2)}) collective-permute-start(bf16[4096,128]{1,0:T(8,128)(2,1)} %refs_3_), channel_id=1, source_target_pairs={{0,16},{1,17},{2,18},{3,19},{4,5},{5,4},{6,7},{7,6},{8,24},{9,25},... | collective-permute-start | bytes 3145736 | tf_op jit(solution)/shard_map/ppermute | solution.py:44
  5.9 1.0 %copy-start.2 = (bf16[1,512,512]{2,1,0:T(8,128)(2,1)S(1)}, bf16[1,512,512]{2,1,0:T(8,128)(2,1)}, u32[]{:S(2)}) copy-start(bf16[1,512,512]{2,1,0:T(8,128)(2,1)} %refs_0_.5) | copy-start | bytes 1572868
  6.9 0.7 copy-start.3
  7.6 0.7 copy-start.4
  9.0 21.7 %collective-permute-start.5 = (bf16[4096,128]{1,0:T(8,128)(2,1)}, bf16[4096,128]{1,0:T(8,128)(2,1)S(1)}, u32[]{:S(2)}, u32[]{:S(2)}) collective-permute-start(bf16[4096,128]{1,0:T(8,128)(2,1)} %refs_3_), channel_id=1, source_target_pairs={{4,12},{12,4},{20,28},{28,20},{5,13},{13,5},{21,29},{29,21},{6,14}... | collective-permute-start | bytes 3145736 | tf_op jit(solution)/shard_map/ppermute | solution.py:34
  13.2 17.4 %collective-permute-start.4 = (bf16[4096,128]{1,0:T(8,128)(2,1)}, bf16[4096,128]{1,0:T(8,128)(2,1)S(1)}, u32[]{:S(2)}, u32[]{:S(2)}) collective-permute-start(bf16[4096,128]{1,0:T(8,128)(2,1)} %refs_3_), channel_id=1, source_target_pairs={{4,20},{12,28},{20,4},{28,12},{5,21},{13,29},{21,5},{29,13},{6,22}... | collective-permute-start | bytes 3145736 | tf_op jit(solution)/shard_map/ppermute | solution.py:34
  16.4 1.2 %copy-start.1 = (bf16[4096,128]{1,0:T(8,128)(2,1)S(1)}, bf16[4096,128]{1,0:T(8,128)(2,1)}, u32[]{:S(2)}) copy-start(bf16[4096,128]{1,0:T(8,128)(2,1)} %refs_3_) | copy-start | bytes 3145732
  28.5 8.4 %collective-permute-start.7 = (bf16[2688,128]{1,0:T(8,128)(2,1)S(1)}, bf16[2688,128]{1,0:T(8,128)(2,1)S(1)}, u32[]{:S(2)}, u32[]{:S(2)}) collective-permute-start(bf16[2688,128]{1,0:T(8,128)(2,1)S(1)} %get-tuple-element.30), channel_id=1, source_target_pairs={{0,8},{8,0},{16,24},{24,16},{1,9},{9,1},{17,25},{25,17},{2,10},{10... | collective-permute-start | bytes 2064392 | tf_op jit(solution)/shard_map/ppermute | solution.py:34
  31.0 9.4 %collective-permute-start.8 = (bf16[2304,128]{1,0:T(8,128)(2,1)S(1)}, bf16[2304,128]{1,0:T(8,128)(2,1)S(1)}, u32[]{:S(2)}, u32[]{:S(2)}) collective-permute-start(bf16[2304,128]{1,0:T(8,128)(2,1)S(1)} %get-tuple-element.31), channel_id=1, source_target_pairs={{0,1},{1,0},{2,3},{3,2},{4,12},{5,13},{6,14},{7,15},{8,9},{9,8},{1... | collective-permute-start | bytes 1769480 | tf_op jit(solution)/shard_map/ppermute | solution.py:44
  33.2 8.4 %collective-permute-start.6 = (bf16[1792,128]{1,0:T(8,128)(2,1)S(1)}, bf16[1792,128]{1,0:T(8,128)(2,1)S(1)}, u32[]{:S(2)}, u32[]{:S(2)}) collective-permute-start(bf16[1792,128]{1,0:T(8,128)(2,1)S(1)} %get-tuple-element.29), channel_id=1, source_target_pairs={{0,1},{1,0},{2,3},{3,2},{4,20},{5,21},{6,22},{7,23},{8,9},{9,8},{1... | collective-permute-start | bytes 1376264 | tf_op jit(solution)/shard_map/ppermute | solution.py:44
  34.4 7.1 %collective-permute-start.3 = (bf16[1408,128]{1,0:T(8,128)(2,1)S(1)}, bf16[1408,128]{1,0:T(8,128)(2,1)S(1)}, u32[]{:S(2)}, u32[]{:S(2)}) collective-permute-start(bf16[1408,128]{1,0:T(8,128)(2,1)S(1)} %get-tuple-element.28.refs_2_), channel_id=1, source_target_pairs={{0,16},{8,24},{16,0},{24,8},{1,17},{9,25},{17,1},{25,9},{2,18},{10... | collective-permute-start | bytes 1081352 | tf_op jit(solution)/shard_map/ppermute | solution.py:34
  42.6 9.0 %collective-permute-start.9 = (bf16[768,128]{1,0:T(8,128)(2,1)S(1)}, bf16[768,128]{1,0:T(8,128)(2,1)S(1)}, u32[]{:S(2)}, u32[]{:S(2)}) collective-permute-start(bf16[768,128]{1,0:T(8,128)(2,1)S(1)} %get-tuple-element.35), channel_id=1, source_target_pairs={{0,3},{1,2},{2,1},{3,0},{4,7},{5,6},{6,5},{7,4},{8,11},{9,10},{10,... | collective-permute-start | bytes 589832 | tf_op jit(solution)/shard_map/ppermute | solution.py:34
  46.4 13.8 %collective-permute-start.10 = (bf16[768,128]{1,0:T(8,128)(2,1)S(1)}, bf16[768,128]{1,0:T(8,128)(2,1)S(1)}, u32[]{:S(2)}, u32[]{:S(2)}) collective-permute-start(bf16[768,128]{1,0:T(8,128)(2,1)S(1)} %get-tuple-element.36), channel_id=1, source_target_pairs={{0,2},{1,3},{2,0},{3,1},{4,6},{5,7},{6,4},{7,5},{8,10},{9,11},{10,... | collective-permute-start | bytes 589832 | tf_op jit(solution)/shard_map/ppermute | solution.py:34
  46.4 13.8 %collective-permute-start.11 = (bf16[768,128]{1,0:T(8,128)(2,1)S(1)}, bf16[768,128]{1,0:T(8,128)(2,1)S(1)}, u32[]{:S(2)}, u32[]{:S(2)}) collective-permute-start(bf16[768,128]{1,0:T(8,128)(2,1)S(1)} %get-tuple-element.37), channel_id=1, source_target_pairs={{0,1},{1,0},{2,3},{3,2},{4,5},{5,4},{6,7},{7,6},{8,9},{9,8},{10,11... | collective-permute-start | bytes 589832 | tf_op jit(solution)/shard_map/ppermute | solution.py:34
  60.3 1.5 %collective-permute-start.12 = (f32[384,128]{1,0:T(8,128)S(1)}, f32[384,128]{1,0:T(8,128)S(1)}, u32[]{:S(2)}, u32[]{:S(2)}) collective-permute-start(f32[384,128]{1,0:T(8,128)S(1)} %get-tuple-element.39), channel_id=1, source_target_pairs={{0,4},{4,0},{8,12},{12,8},{16,20},{20,16},{24,28},{28,24},{1,5},{5... | collective-permute-start | bytes 589832 | tf_op jit(solution)/shard_map/ppermute | solution.py:34
  62.1 5.2 %collective-permute-start.14 = (bf16[128,384]{1,0:T(8,128)(2,1)S(1)}, bf16[128,384]{1,0:T(8,128)(2,1)S(1)}, u32[]{:S(2)}, u32[]{:S(2)}) collective-permute-start(bf16[128,384]{1,0:T(8,128)(2,1)S(1)} %get-tuple-element.46), channel_id=1, source_target_pairs={{0,4},{4,8},{8,12},{12,16},{16,20},{20,24},{24,28},{28,0},{1,5},{5... | collective-permute-start | bytes 294920 | tf_op jit(solution)/shard_map/ppermute | solution.py:228
  63.4 3.9 %collective-permute-start.13 = (bf16[128,256]{1,0:T(8,128)(2,1)S(1)}, bf16[128,256]{1,0:T(8,128)(2,1)S(1)}, u32[]{:S(2)}, u32[]{:S(2)}) collective-permute-start(bf16[128,256]{1,0:T(8,128)(2,1)S(1)} %get-tuple-element.45), channel_id=1, source_target_pairs={{0,28},{4,0},{8,4},{12,8},{16,12},{20,16},{24,20},{28,24},{1,29},{... | collective-permute-start | bytes 196616 | tf_op jit(solution)/shard_map/ppermute | solution.py:228

commit v22 on v21

--- a/solution.py
+++ b/solution.py
@@ -171,10 +171,8 @@
         kernel = functools.partial(pieces_kernel, one)
         top, bottom = call(kernel, outs, pair, after=previous, scratch=[pltpu.SemaphoreType.DMA((2,))])
         previous = [bottom]
-        if one:
-            passed += [paired(top, NEAR, one), paired(bottom, FAR, one)]
-        else:
-            passed += [exchanged(top, "domain", NEAR, one), exchanged(bottom, "domain", FAR, one)]
+        passed.append(exchanged(top, "domain", NEAR, one))
+        passed.append(paired(bottom, FAR, one) if one else exchanged(bottom, "domain", FAR, one))
     early = call(early_kernel, block * 2, (wavefunctions, theirs, *received))
     outs = block + [shape(2 * rows, width, dtype=BF16)] * (bands - 1)
     scratch = [pltpu.VMEM((2 * rows, width), F32)]

time: 68.8 us -> 66.8 us (0.971)
  waiting for transfers between devices: 35.4 us -> 31.8 us
  starting transfers between devices: 20.5 us -> 22 us
    ppermute x4 -> x3, waiting for transfers between devices: 12.6 us -> 8.37 us  [paired(): return lax.ppermute(value, ('domain', 'band'), pairs)]
    ppermute x9 -> x10, starting transfers between devices: 13 us -> 16.7 us  [exchanged(): lax.ppermute(value, axis, [(source, source ^ mask) for source in sources...]
    ppermute x4 -> x3, starting transfers between devices: 6.18 us -> 4.08 us  [paired(): return lax.ppermute(value, ('domain', 'band'), pairs)]
    ppermute x9 -> x10, waiting for transfers between devices: 19.3 us -> 20 us  [exchanged(): lax.ppermute(value, axis, [(source, source ^ mask) for source in sources...]
where the time goes in v22:
time: 66.8 us; the launch traced here: 66.4 us
  waiting for transfers between devices  31.8 us (48%)
  starting transfers between devices  22 us (33%)
  Pallas kernels  8.84 us (13%)
  local copies, waits for them, and re-layouts  3.6 us (5%)
    ppermute x10, waiting for transfers between devices, exchanged(): lax.ppermute(value, axis, [(source, source ^ mask) for source in sources...  20 us
    ppermute x10, starting transfers between devices, exchanged(): lax.ppermute(value, axis, [(source, source ^ mask) for source in sources...  16.7 us
    pallas_call x11, Pallas kernels, call(): pl.pallas_call(body, out_shape=outs, in_specs=[pl.BlockSpec(memory_space=...  8.84 us
    ppermute x3, waiting for transfers between devices, paired(): return lax.ppermute(value, ('domain', 'band'), pairs)  8.37 us
    ppermute x3, starting transfers between devices, paired(): return lax.ppermute(value, ('domain', 'band'), pairs)  4.08 us
    unnamed x10, local copies, waits for them, and re-layouts  3.6 us
    ppermute x2, waiting for transfers between devices, rotated(): lax.ppermute(value, axis, [(source, (source + steps) % count) for source...  3.46 us
  transfers between devices with their start and end apart: 15, of which 8 were waited for; matrix products, arithmetic and copies ran while one was open for 0% of the time, Pallas kernels for 9%

profile of v22, /device:TPU:1, one launch (start us, length us, event | category | flops | bytes accessed | tf_op | source)
XLA Modules:
  0.0 66.4 jit_solution(6417233044075707095)
XLA Ops:
  0.0 0.0 copy-start
  0.0 0.1 collective-permute-start
  0.1 2.7 %collective-permute-start.2 = (bf16[4096,128]{1,0:T(8,128)(2,1)}, bf16[4096,128]{1,0:T(8,128)(2,1)S(1)}, u32[]{:S(2)}, u32[]{:S(2)}) collective-permute-start(bf16[4096,128]{1,0:T(8,128)(2,1)} %refs_3_), channel_id=1, source_target_pairs={{0,8},{1,9},{2,10},{3,11},{4,5},{5,4},{6,7},{7,6},{8,0},{9,1},{10,... | collective-permute-start | bytes 3145736 | tf_op jit(solution)/shard_map/ppermute | solution.py:44
  2.8 0.0 collective-permute-start.1
  2.8 3.0 %collective-permute-done.refs_3_.refs_1_ = bf16[384,4096]{1,0:T(8,128)(2,1)S(1)} collective-permute-done((bf16[384,4096]{1,0:T(8,128)(2,1)}, bf16[384,4096]{1,0:T(8,128)(2,1)S(1)}, u32[]{:S(2)}, u32[]{:S(2)}) %collective-permute-start) | collective-permute-done | bytes 3145760 | tf_op jit(solution)/shard_map/ppermute | solution.py:34
  5.9 0.0 copy-start.2
  5.9 1.0 %copy-done.2 = bf16[1,512,512]{2,1,0:T(8,128)(2,1)S(1)} copy-done((bf16[1,512,512]{2,1,0:T(8,128)(2,1)S(1)}, bf16[1,512,512]{2,1,0:T(8,128)(2,1)}, u32[]{:S(2)}) %copy-start.2) | copy-done | bytes 524312
  6.9 0.0 copy-start.3
  6.9 0.7 %copy-done.3 = s32[1,512]{1,0:T(1,128)S(1)} copy-done((s32[1,512]{1,0:T(1,128)S(1)}, s32[1,512]{1,0:T(1,128)}, u32[]{:S(2)}) %copy-start.3) | copy-done | bytes 2072
  7.6 0.0 copy-start.4
  7.6 0.7 copy-done.4
  8.3 0.7 %shard_map.55 = (bf16[512,512]{1,0:T(8,128)(2,1)S(1)}, bf16[128,384]{1,0:T(8,128)(2,1)S(1)}, bf16[384,128]{1,0:T(8,128)(2,1)S(1)}) custom-call(bf16[1,512,512]{2,1,0:T(8,128)(2,1)S(1)} %copy-done.2, s32[1,512]{1,0:T(1,128)S(1)} %copy-done.3, s32[1,128]{1,0:T(1,128)S(1)} %bitcast.1, bf16[384,4096]{1,0:T(8,128)(2,1)S(1)} %collective-permute-done.refs_3_.refs_1_), custom_call_target="tpu_custom_call" | custom-call | bytes 1024 | tf_op jit(solution)/shard_map/pallas_call | solution.py:54
  9.0 4.3 %collective-permute-start.5 = (bf16[4096,128]{1,0:T(8,128)(2,1)}, bf16[4096,128]{1,0:T(8,128)(2,1)S(1)}, u32[]{:S(2)}, u32[]{:S(2)}) collective-permute-start(bf16[4096,128]{1,0:T(8,128)(2,1)} %refs_3_), channel_id=1, source_target_pairs={{4,12},{12,4},{20,28},{28,20},{5,13},{13,5},{21,29},{29,21},{6,14}... | collective-permute-start | bytes 3145736 | tf_op jit(solution)/shard_map/ppermute | solution.py:34
  13.2 3.1 %collective-permute-start.4 = (bf16[4096,128]{1,0:T(8,128)(2,1)}, bf16[4096,128]{1,0:T(8,128)(2,1)S(1)}, u32[]{:S(2)}, u32[]{:S(2)}) collective-permute-start(bf16[4096,128]{1,0:T(8,128)(2,1)} %refs_3_), channel_id=1, source_target_pairs={{4,20},{12,28},{20,4},{28,12},{5,21},{13,29},{21,5},{29,13},{6,22}... | collective-permute-start | bytes 3145736 | tf_op jit(solution)/shard_map/ppermute | solution.py:34
  16.4 0.0 copy-done
  16.4 0.0 copy-start.1
  16.4 1.2 %copy-done.1 = bf16[4096,128]{1,0:T(8,128)(2,1)S(1)} copy-done((bf16[4096,128]{1,0:T(8,128)(2,1)S(1)}, bf16[4096,128]{1,0:T(8,128)(2,1)}, u32[]{:S(2)}) %copy-start.1) | copy-done | bytes 1048600
  17.6 1.8 %shard_map.56.refs_2_.refs_5_ = f32[768,128]{1,0:T(8,128)S(1)} custom-call(bf16[384,4096]{1,0:T(8,128)(2,1)S(1)} %copy-done, bf16[384,4096]{1,0:T(8,128)(2,1)S(1)} %collective-permute-done.refs_3_.refs_1_, bf16[4096,128]{1,0:T(8,128)(2,1)S(1)} %copy-done.1, bf16[4096,128]{1,0:T(8,128)(2,1)S(1)} %copy-done.1), custom_call_target="tpu_custom_call" | custom-call | bytes 1024 | tf_op jit(solution)/shard_map/pallas_call | solution.py:54
  19.4 0.0 collective-permute-done.2.refs_1_.refs_2_
  19.4 8.4 %collective-permute-done.1.refs_0_.refs_3_ = bf16[4096,128]{1,0:T(8,128)(2,1)S(1)} collective-permute-done((bf16[4096,128]{1,0:T(8,128)(2,1)}, bf16[4096,128]{1,0:T(8,128)(2,1)S(1)}, u32[]{:S(2)}, u32[]{:S(2)}) %collective-permute-start.1) | collective-permute-done | bytes 1048608 | tf_op jit(solution)/shard_map/ppermute | solution.py:44
  27.8 0.7 %collective-permute-start.7 = (bf16[2688,128]{1,0:T(8,128)(2,1)S(1)}, bf16[2688,128]{1,0:T(8,128)(2,1)S(1)}, u32[]{:S(2)}, u32[]{:S(2)}) collective-permute-start(bf16[2688,128]{1,0:T(8,128)(2,1)S(1)} %get-tuple-element.30), channel_id=1, source_target_pairs={{0,8},{8,0},{16,24},{24,16},{1,9},{9,1},{17,25},{25,17},{2,10},{10... | collective-permute-start | bytes 2064392 | tf_op jit(solution)/shard_map/ppermute | solution.py:34
  28.5 2.1 %collective-permute-done.5.refs_1_.refs_4_ = bf16[4096,128]{1,0:T(8,128)(2,1)S(1)} collective-permute-done((bf16[4096,128]{1,0:T(8,128)(2,1)}, bf16[4096,128]{1,0:T(8,128)(2,1)S(1)}, u32[]{:S(2)}, u32[]{:S(2)}) %collective-permute-start.5) | collective-permute-done | bytes 1048608 | tf_op jit(solution)/shard_map/ppermute | solution.py:34
  30.6 0.0 collective-permute-done.4.refs_0_.refs_5_
  30.6 0.4 shard_map.58
  31.0 4.0 %collective-permute-start.8 = (bf16[2304,128]{1,0:T(8,128)(2,1)S(1)}, bf16[2304,128]{1,0:T(8,128)(2,1)S(1)}, u32[]{:S(2)}, u32[]{:S(2)}) collective-permute-start(bf16[2304,128]{1,0:T(8,128)(2,1)S(1)} %get-tuple-element.31), channel_id=1, source_target_pairs={{4,12},{12,4},{20,28},{28,20},{5,13},{13,5},{21,29},{29,21},{6,14}... | collective-permute-start | bytes 1769480 | tf_op jit(solution)/shard_map/ppermute | solution.py:34
  35.0 1.3 %collective-permute-start.6 = (bf16[1792,128]{1,0:T(8,128)(2,1)S(1)}, bf16[1792,128]{1,0:T(8,128)(2,1)S(1)}, u32[]{:S(2)}, u32[]{:S(2)}) collective-permute-start(bf16[1792,128]{1,0:T(8,128)(2,1)S(1)} %get-tuple-element.29), channel_id=1, source_target_pairs={{0,1},{1,0},{2,3},{3,2},{4,20},{5,21},{6,22},{7,23},{8,9},{9,8},{1... | collective-permute-start | bytes 1376264 | tf_op jit(solution)/shard_map/ppermute | solution.py:44
  36.4 0.7 %collective-permute-start.3 = (bf16[1408,128]{1,0:T(8,128)(2,1)S(1)}, bf16[1408,128]{1,0:T(8,128)(2,1)S(1)}, u32[]{:S(2)}, u32[]{:S(2)}) collective-permute-start(bf16[1408,128]{1,0:T(8,128)(2,1)S(1)} %get-tuple-element.28.refs_2_), channel_id=1, source_target_pairs={{0,16},{8,24},{16,0},{24,8},{1,17},{9,25},{17,1},{25,9},{2,18},{10... | collective-permute-start | bytes 1081352 | tf_op jit(solution)/shard_map/ppermute | solution.py:34
  37.0 1.8 %shard_map.59 = (f32[768,128]{1,0:T(8,128)S(1)}, f32[768,128]{1,0:T(8,128)S(1)}) custom-call(bf16[384,4096]{1,0:T(8,128)(2,1)S(1)} %copy-done, bf16[384,4096]{1,0:T(8,128)(2,1)S(1)} %collective-permute-done.refs_3_.refs_1_, bf16[4096,128]{1,0:T(8,128)(2,1)S(1)} %collective-permute-done.2.refs_1_.refs_2_, ...), custom_call_target="tpu_custom_call" | custom-call | bytes 1024 | tf_op jit(solution)/shard_map/pallas_call | solution.py:54
  38.8 0.0 collective-permute-done.7.refs_2_
  38.8 3.8 %collective-permute-done.8.refs_3_ = bf16[2304,128]{1,0:T(8,128)(2,1)S(1)} collective-permute-done((bf16[2304,128]{1,0:T(8,128)(2,1)S(1)}, bf16[2304,128]{1,0:T(8,128)(2,1)S(1)}, u32[]{:S(2)}, u32[]{:S(2)}) %collective-permute-start.8) | collective-permute-done | bytes 589856 | tf_op jit(solution)/shard_map/ppermute | solution.py:34
  42.6 1.1 %shard_map.60.refs_4_ = f32[768,128]{1,0:T(8,128)S(1)} custom-call(bf16[384,4096]{1,0:T(8,128)(2,1)S(1)} %copy-done, bf16[384,4096]{1,0:T(8,128)(2,1)S(1)} %collective-permute-done.refs_3_.refs_1_, bf16[2688,128]{1,0:T(8,128)(2,1)S(1)} %collective-permute-done.7.refs_2_, bf16[2304,128]{1,0:T(8,128)(2,1)S(1)} %collective-permute-done.8.refs_3_, ...), custom_call_target="tpu_custom_call" | custom-call | bytes 1024 | tf_op jit(solution)/shard_map/pallas_call | solution.py:54
  43.7 0.0 collective-permute-done.3.refs_2_
  43.7 0.0 collective-permute-done.6.refs_3_
  43.7 1.1 %shard_map.61 = (f32[768,128]{1,0:T(8,128)S(1)}, bf16[768,128]{1,0:T(8,128)(2,1)S(1)}, bf16[768,128]{1,0:T(8,128)(2,1)S(1)}, bf16[768,128]{1,0:T(8,128)(2,1)S(1)}) custom-call(bf16[384,4096]{1,0:T(8,128)(2,1)S(1)} %copy-done, bf16[384,4096]{1,0:T(8,128)(2,1)S(1)} %collective-permute-done.refs_3_.refs_1_, ...), custom_call_target="tpu_custom_call" | custom-call | bytes 1024 | tf_op jit(solution)/shard_map/pallas_call | solution.py:54
  44.8 3.4 %collective-permute-start.9 = (bf16[768,128]{1,0:T(8,128)(2,1)S(1)}, bf16[768,128]{1,0:T(8,128)(2,1)S(1)}, u32[]{:S(2)}, u32[]{:S(2)}) collective-permute-start(bf16[768,128]{1,0:T(8,128)(2,1)S(1)} %get-tuple-element.35), channel_id=1, source_target_pairs={{0,3},{1,2},{2,1},{3,0},{4,7},{5,6},{6,5},{7,4},{8,11},{9,10},{10,... | collective-permute-start | bytes 589832 | tf_op jit(solution)/shard_map/ppermute | solution.py:34
  48.1 0.0 collective-permute-start.10
  48.1 0.4 collective-permute-start.11
  48.5 2.9 %collective-permute-done.9.refs_1_ = bf16[768,128]{1,0:T(8,128)(2,1)S(1)} collective-permute-done((bf16[768,128]{1,0:T(8,128)(2,1)S(1)}, bf16[768,128]{1,0:T(8,128)(2,1)S(1)}, u32[]{:S(2)}, u32[]{:S(2)}) %collective-permute-start.9) | collective-permute-done | bytes 196640 | tf_op jit(solution)/shard_map/ppermute | solution.py:34
  51.4 6.8 %collective-permute-done.10.refs_2_ = bf16[768,128]{1,0:T(8,128)(2,1)S(1)} collective-permute-done((bf16[768,128]{1,0:T(8,128)(2,1)S(1)}, bf16[768,128]{1,0:T(8,128)(2,1)S(1)}, u32[]{:S(2)}, u32[]{:S(2)}) %collective-permute-start.10) | collective-permute-done | bytes 196640 | tf_op jit(solution)/shard_map/ppermute | solution.py:34
  58.1 0.0 collective-permute-done.11.refs_3_
  58.2 0.1 shard_map.62
  58.2 0.1 collective-permute-start.12
  58.3 1.4 %collective-permute-done.12.refs_1_ = f32[384,128]{1,0:T(8,128)S(1)} collective-permute-done((f32[384,128]{1,0:T(8,128)S(1)}, f32[384,128]{1,0:T(8,128)S(1)}, u32[]{:S(2)}, u32[]{:S(2)}) %collective-permute-start.12) | collective-permute-done | bytes 196640 | tf_op jit(solution)/shard_map/ppermute | solution.py:34
  59.7 0.3 shard_map.63
  60.0 1.3 %collective-permute-start.14 = (bf16[128,384]{1,0:T(8,128)(2,1)S(1)}, bf16[128,384]{1,0:T(8,128)(2,1)S(1)}, u32[]{:S(2)}, u32[]{:S(2)}) collective-permute-start(bf16[128,384]{1,0:T(8,128)(2,1)S(1)} %get-tuple-element.46), channel_id=1, source_target_pairs={{0,4},{4,8},{8,12},{12,16},{16,20},{20,24},{24,28},{28,0},{1,5},{5... | collective-permute-start | bytes 294920 | tf_op jit(solution)/shard_map/ppermute | solution.py:226
  61.3 0.0 collective-permute-start.13
  61.3 0.4 shard_map.64
  61.8 3.5 %collective-permute-done.13.refs_4_ = bf16[128,256]{1,0:T(8,128)(2,1)S(1)} collective-permute-done((bf16[128,256]{1,0:T(8,128)(2,1)S(1)}, bf16[128,256]{1,0:T(8,128)(2,1)S(1)}, u32[]{:S(2)}, u32[]{:S(2)}) %collective-permute-start.13) | collective-permute-done | bytes 65568 | tf_op jit(solution)/shard_map/ppermute | solution.py:226
  65.2 0.0 collective-permute-done.14.refs_5_
  65.2 1.2 %shard_map.65 = f32[384,256]{1,0:T(8,128)} custom-call(f32[384,256]{1,0:T(8,128)S(1)} %get-tuple-element.42.refs_0_, bf16[128,512]{1,0:T(8,128)(2,1)S(1)} %get-tuple-element.43.refs_1_, bf16[512,512]{1,0:T(8,128)(2,1)S(1)} %get-tuple-element.26.refs_2_.refs_1_, bf16[384,128]{1,0:T(8,128)(2,1)S(1)} %get-tuple-element.44.refs_3_, ...), custom_call_target="tpu_custom_call" | custom-call | bytes 1024 | tf_op jit(solution)/shard_map/pallas_call | solution.py:54
  (1 shorter events, 0.0 us)
Async XLA Ops:
  0.0 16.4 %copy-start = (bf16[384,4096]{1,0:T(8,128)(2,1)S(1)}, bf16[384,4096]{1,0:T(8,128)(2,1)}, u32[]{:S(2)}) copy-start(bf16[384,4096]{1,0:T(8,128)(2,1)} %refs_0_.9) | copy-start | bytes 9437188
  0.0 5.9 %collective-permute-start = (bf16[384,4096]{1,0:T(8,128)(2,1)}, bf16[384,4096]{1,0:T(8,128)(2,1)S(1)}, u32[]{:S(2)}, u32[]{:S(2)}) collective-permute-start(bf16[384,4096]{1,0:T(8,128)(2,1)} %refs_0_.9), channel_id=1, source_target_pairs={{0,4},{4,0},{8,12},{12,8},{16,20},{20,16},{24,28},{28,24},{1,5},{5... | collective-permute-start | bytes 9437192 | tf_op jit(solution)/shard_map/ppermute | solution.py:34
  0.1 19.3 %collective-permute-start.2 = (bf16[4096,128]{1,0:T(8,128)(2,1)}, bf16[4096,128]{1,0:T(8,128)(2,1)S(1)}, u32[]{:S(2)}, u32[]{:S(2)}) collective-permute-start(bf16[4096,128]{1,0:T(8,128)(2,1)} %refs_3_), channel_id=1, source_target_pairs={{0,8},{1,9},{2,10},{3,11},{4,5},{5,4},{6,7},{7,6},{8,0},{9,1},{10,... | collective-permute-start | bytes 3145736 | tf_op jit(solution)/shard_map/ppermute | solution.py:44
  2.8 25.0 %collective-permute-start.1 = (bf16[4096,128]{1,0:T(8,128)(2,1)}, bf16[4096,128]{1,0:T(8,128)(2,1)S(1)}, u32[]{:S(2)}, u32[]{:S(2)}) collective-permute-start(bf16[4096,128]{1,0:T(8,128)(2,1)} %refs_3_), channel_id=1, source_target_pairs={{0,16},{1,17},{2,18},{3,19},{4,5},{5,4},{6,7},{7,6},{8,24},{9,25},... | collective-permute-start | bytes 3145736 | tf_op jit(solution)/shard_map/ppermute | solution.py:44
  5.9 1.0 %copy-start.2 = (bf16[1,512,512]{2,1,0:T(8,128)(2,1)S(1)}, bf16[1,512,512]{2,1,0:T(8,128)(2,1)}, u32[]{:S(2)}) copy-start(bf16[1,512,512]{2,1,0:T(8,128)(2,1)} %refs_0_.5) | copy-start | bytes 1572868
  6.9 0.7 %copy-start.3 = (s32[1,512]{1,0:T(1,128)S(1)}, s32[1,512]{1,0:T(1,128)}, u32[]{:S(2)}) copy-start(s32[1,512]{1,0:T(1,128)} %refs_1_.1) | copy-start | bytes 6148
  7.6 0.7 copy-start.4
  9.0 21.7 %collective-permute-start.5 = (bf16[4096,128]{1,0:T(8,128)(2,1)}, bf16[4096,128]{1,0:T(8,128)(2,1)S(1)}, u32[]{:S(2)}, u32[]{:S(2)}) collective-permute-start(bf16[4096,128]{1,0:T(8,128)(2,1)} %refs_3_), channel_id=1, source_target_pairs={{4,12},{12,4},{20,28},{28,20},{5,13},{13,5},{21,29},{29,21},{6,14}... | collective-permute-start | bytes 3145736 | tf_op jit(solution)/shard_map/ppermute | solution.py:34
  13.2 17.4 %collective-permute-start.4 = (bf16[4096,128]{1,0:T(8,128)(2,1)}, bf16[4096,128]{1,0:T(8,128)(2,1)S(1)}, u32[]{:S(2)}, u32[]{:S(2)}) collective-permute-start(bf16[4096,128]{1,0:T(8,128)(2,1)} %refs_3_), channel_id=1, source_target_pairs={{4,20},{12,28},{20,4},{28,12},{5,21},{13,29},{21,5},{29,13},{6,22}... | collective-permute-start | bytes 3145736 | tf_op jit(solution)/shard_map/ppermute | solution.py:34
  16.4 1.2 %copy-start.1 = (bf16[4096,128]{1,0:T(8,128)(2,1)S(1)}, bf16[4096,128]{1,0:T(8,128)(2,1)}, u32[]{:S(2)}) copy-start(bf16[4096,128]{1,0:T(8,128)(2,1)} %refs_3_) | copy-start | bytes 3145732
  27.8 11.0 %collective-permute-start.7 = (bf16[2688,128]{1,0:T(8,128)(2,1)S(1)}, bf16[2688,128]{1,0:T(8,128)(2,1)S(1)}, u32[]{:S(2)}, u32[]{:S(2)}) collective-permute-start(bf16[2688,128]{1,0:T(8,128)(2,1)S(1)} %get-tuple-element.30), channel_id=1, source_target_pairs={{0,8},{8,0},{16,24},{24,16},{1,9},{9,1},{17,25},{25,17},{2,10},{10... | collective-permute-start | bytes 2064392 | tf_op jit(solution)/shard_map/ppermute | solution.py:34
  31.0 11.6 %collective-permute-start.8 = (bf16[2304,128]{1,0:T(8,128)(2,1)S(1)}, bf16[2304,128]{1,0:T(8,128)(2,1)S(1)}, u32[]{:S(2)}, u32[]{:S(2)}) collective-permute-start(bf16[2304,128]{1,0:T(8,128)(2,1)S(1)} %get-tuple-element.31), channel_id=1, source_target_pairs={{4,12},{12,4},{20,28},{28,20},{5,13},{13,5},{21,29},{29,21},{6,14}... | collective-permute-start | bytes 1769480 | tf_op jit(solution)/shard_map/ppermute | solution.py:34
  35.0 8.6 %collective-permute-start.6 = (bf16[1792,128]{1,0:T(8,128)(2,1)S(1)}, bf16[1792,128]{1,0:T(8,128)(2,1)S(1)}, u32[]{:S(2)}, u32[]{:S(2)}) collective-permute-start(bf16[1792,128]{1,0:T(8,128)(2,1)S(1)} %get-tuple-element.29), channel_id=1, source_target_pairs={{0,1},{1,0},{2,3},{3,2},{4,20},{5,21},{6,22},{7,23},{8,9},{9,8},{1... | collective-permute-start | bytes 1376264 | tf_op jit(solution)/shard_map/ppermute | solution.py:44
  36.4 7.3 %collective-permute-start.3 = (bf16[1408,128]{1,0:T(8,128)(2,1)S(1)}, bf16[1408,128]{1,0:T(8,128)(2,1)S(1)}, u32[]{:S(2)}, u32[]{:S(2)}) collective-permute-start(bf16[1408,128]{1,0:T(8,128)(2,1)S(1)} %get-tuple-element.28.refs_2_), channel_id=1, source_target_pairs={{0,16},{8,24},{16,0},{24,8},{1,17},{9,25},{17,1},{25,9},{2,18},{10... | collective-permute-start | bytes 1081352 | tf_op jit(solution)/shard_map/ppermute | solution.py:34
  44.8 6.6 %collective-permute-start.9 = (bf16[768,128]{1,0:T(8,128)(2,1)S(1)}, bf16[768,128]{1,0:T(8,128)(2,1)S(1)}, u32[]{:S(2)}, u32[]{:S(2)}) collective-permute-start(bf16[768,128]{1,0:T(8,128)(2,1)S(1)} %get-tuple-element.35), channel_id=1, source_target_pairs={{0,3},{1,2},{2,1},{3,0},{4,7},{5,6},{6,5},{7,4},{8,11},{9,10},{10,... | collective-permute-start | bytes 589832 | tf_op jit(solution)/shard_map/ppermute | solution.py:34
  48.1 10.0 %collective-permute-start.10 = (bf16[768,128]{1,0:T(8,128)(2,1)S(1)}, bf16[768,128]{1,0:T(8,128)(2,1)S(1)}, u32[]{:S(2)}, u32[]{:S(2)}) collective-permute-start(bf16[768,128]{1,0:T(8,128)(2,1)S(1)} %get-tuple-element.36), channel_id=1, source_target_pairs={{0,2},{1,3},{2,0},{3,1},{4,6},{5,7},{6,4},{7,5},{8,10},{9,11},{10,... | collective-permute-start | bytes 589832 | tf_op jit(solution)/shard_map/ppermute | solution.py:34
  48.1 10.0 %collective-permute-start.11 = (bf16[768,128]{1,0:T(8,128)(2,1)S(1)}, bf16[768,128]{1,0:T(8,128)(2,1)S(1)}, u32[]{:S(2)}, u32[]{:S(2)}) collective-permute-start(bf16[768,128]{1,0:T(8,128)(2,1)S(1)} %get-tuple-element.37), channel_id=1, source_target_pairs={{0,1},{1,0},{2,3},{3,2},{4,5},{5,4},{6,7},{7,6},{8,9},{9,8},{10,11... | collective-permute-start | bytes 589832 | tf_op jit(solution)/shard_map/ppermute | solution.py:34
  58.2 1.5 %collective-permute-start.12 = (f32[384,128]{1,0:T(8,128)S(1)}, f32[384,128]{1,0:T(8,128)S(1)}, u32[]{:S(2)}, u32[]{:S(2)}) collective-permute-start(f32[384,128]{1,0:T(8,128)S(1)} %get-tuple-element.39), channel_id=1, source_target_pairs={{0,4},{4,0},{8,12},{12,8},{16,20},{20,16},{24,28},{28,24},{1,5},{5... | collective-permute-start | bytes 589832 | tf_op jit(solution)/shard_map/ppermute | solution.py:34
  60.0 5.2 %collective-permute-start.14 = (bf16[128,384]{1,0:T(8,128)(2,1)S(1)}, bf16[128,384]{1,0:T(8,128)(2,1)S(1)}, u32[]{:S(2)}, u32[]{:S(2)}) collective-permute-start(bf16[128,384]{1,0:T(8,128)(2,1)S(1)} %get-tuple-element.46), channel_id=1, source_target_pairs={{0,4},{4,8},{8,12},{12,16},{16,20},{20,24},{24,28},{28,0},{1,5},{5... | collective-permute-start | bytes 294920 | tf_op jit(solution)/shard_map/ppermute | solution.py:226
  61.3 3.9 %collective-permute-start.13 = (bf16[128,256]{1,0:T(8,128)(2,1)S(1)}, bf16[128,256]{1,0:T(8,128)(2,1)S(1)}, u32[]{:S(2)}, u32[]{:S(2)}) collective-permute-start(bf16[128,256]{1,0:T(8,128)(2,1)S(1)} %get-tuple-element.45), channel_id=1, source_target_pairs={{0,28},{4,0},{8,4},{12,8},{16,12},{20,16},{24,20},{28,24},{1,29},{... | collective-permute-start | bytes 196616 | tf_op jit(solution)/shard_map/ppermute | solution.py:226

commit v23 on v22

--- a/solution.py
+++ b/solution.py
@@ -171,7 +171,7 @@
         kernel = functools.partial(pieces_kernel, one)
         top, bottom = call(kernel, outs, pair, after=previous, scratch=[pltpu.SemaphoreType.DMA((2,))])
         previous = [bottom]
-        passed.append(exchanged(top, "domain", NEAR, one))
+        passed.append(exchanged(top, "domain", NEAR, one) if one else paired(top, NEAR, one))
         passed.append(paired(bottom, FAR, one) if one else exchanged(bottom, "domain", FAR, one))
     early = call(early_kernel, block * 2, (wavefunctions, theirs, *received))
     outs = block + [shape(2 * rows, width, dtype=BF16)] * (bands - 1)

time: 66.8 us -> 67.1 us (level)
  starting transfers between devices: 22 us -> 23.3 us
  waiting for transfers between devices: 31.8 us -> 31 us
    ppermute x10 -> x9, waiting for transfers between devices: 20 us -> 17.5 us  [exchanged(): lax.ppermute(value, axis, [(source, source ^ mask) for source in sources...]
    ppermute x3 -> x4, waiting for transfers between devices: 8.37 us -> 10.3 us  [paired(): return lax.ppermute(value, ('domain', 'band'), pairs)]
    ppermute x3 -> x4, starting transfers between devices: 4.08 us -> 5.77 us  [paired(): return lax.ppermute(value, ('domain', 'band'), pairs)]
    ppermute x10 -> x9, starting transfers between devices: 16.7 us -> 16 us  [exchanged(): lax.ppermute(value, axis, [(source, source ^ mask) for source in sources...]
where the time goes in v23:
time: 67.1 us; the launch traced here: 66.8 us
  waiting for transfers between devices  31 us (46%)
  starting transfers between devices  23.3 us (35%)
  Pallas kernels  8.83 us (13%)
  local copies, waits for them, and re-layouts  3.6 us (5%)
    ppermute x9, waiting for transfers between devices, exchanged(): lax.ppermute(value, axis, [(source, source ^ mask) for source in sources...  17.5 us
    ppermute x9, starting transfers between devices, exchanged(): lax.ppermute(value, axis, [(source, source ^ mask) for source in sources...  16 us
    ppermute x4, waiting for transfers between devices, paired(): return lax.ppermute(value, ('domain', 'band'), pairs)  10.3 us
    pallas_call x11, Pallas kernels, call(): pl.pallas_call(body, out_shape=outs, in_specs=[pl.BlockSpec(memory_space=...  8.83 us
    ppermute x4, starting transfers between devices, paired(): return lax.ppermute(value, ('domain', 'band'), pairs)  5.77 us
    unnamed x10, local copies, waits for them, and re-layouts  3.6 us
    ppermute x2, waiting for transfers between devices, rotated(): lax.ppermute(value, axis, [(source, (source + steps) % count) for source...  3.24 us
    ppermute x2, starting transfers between devices, rotated(): lax.ppermute(value, axis, [(source, (source + steps) % count) for source...  1.53 us
  transfers between devices with their start and end apart: 15, of which 8 were waited for; matrix products, arithmetic and copies ran while one was open for 0% of the time, Pallas kernels for 9%

profile of v23, /device:TPU:1, one launch (start us, length us, event | category | flops | bytes accessed | tf_op | source)
XLA Modules:
  0.0 66.8 jit_solution(16068565011443069561)
XLA Ops:
  0.0 0.0 copy-start
  0.0 0.1 collective-permute-start
  0.1 2.7 %collective-permute-start.2 = (bf16[4096,128]{1,0:T(8,128)(2,1)}, bf16[4096,128]{1,0:T(8,128)(2,1)S(1)}, u32[]{:S(2)}, u32[]{:S(2)}) collective-permute-start(bf16[4096,128]{1,0:T(8,128)(2,1)} %refs_3_), channel_id=1, source_target_pairs={{0,8},{1,9},{2,10},{3,11},{4,5},{5,4},{6,7},{7,6},{8,0},{9,1},{10,... | collective-permute-start | bytes 3145736 | tf_op jit(solution)/shard_map/ppermute | solution.py:44
  2.8 0.0 collective-permute-start.1
  2.8 3.0 %collective-permute-done.refs_3_.refs_1_ = bf16[384,4096]{1,0:T(8,128)(2,1)S(1)} collective-permute-done((bf16[384,4096]{1,0:T(8,128)(2,1)}, bf16[384,4096]{1,0:T(8,128)(2,1)S(1)}, u32[]{:S(2)}, u32[]{:S(2)}) %collective-permute-start) | collective-permute-done | bytes 3145760 | tf_op jit(solution)/shard_map/ppermute | solution.py:34
  5.9 0.0 copy-start.2
  5.9 1.0 %copy-done.2 = bf16[1,512,512]{2,1,0:T(8,128)(2,1)S(1)} copy-done((bf16[1,512,512]{2,1,0:T(8,128)(2,1)S(1)}, bf16[1,512,512]{2,1,0:T(8,128)(2,1)}, u32[]{:S(2)}) %copy-start.2) | copy-done | bytes 524312
  6.9 0.0 copy-start.3
  6.9 0.7 %copy-done.3 = s32[1,512]{1,0:T(1,128)S(1)} copy-done((s32[1,512]{1,0:T(1,128)S(1)}, s32[1,512]{1,0:T(1,128)}, u32[]{:S(2)}) %copy-start.3) | copy-done | bytes 2072
  7.6 0.0 copy-start.4
  7.6 0.7 copy-done.4
  8.3 0.7 %shard_map.55 = (bf16[512,512]{1,0:T(8,128)(2,1)S(1)}, bf16[128,384]{1,0:T(8,128)(2,1)S(1)}, bf16[384,128]{1,0:T(8,128)(2,1)S(1)}) custom-call(bf16[1,512,512]{2,1,0:T(8,128)(2,1)S(1)} %copy-done.2, s32[1,512]{1,0:T(1,128)S(1)} %copy-done.3, s32[1,128]{1,0:T(1,128)S(1)} %bitcast.1, bf16[384,4096]{1,0:T(8,128)(2,1)S(1)} %collective-permute-done.refs_3_.refs_1_), custom_call_target="tpu_custom_call" | custom-call | bytes 1024 | tf_op jit(solution)/shard_map/pallas_call | solution.py:54
  9.0 4.3 %collective-permute-start.5 = (bf16[4096,128]{1,0:T(8,128)(2,1)}, bf16[4096,128]{1,0:T(8,128)(2,1)S(1)}, u32[]{:S(2)}, u32[]{:S(2)}) collective-permute-start(bf16[4096,128]{1,0:T(8,128)(2,1)} %refs_3_), channel_id=1, source_target_pairs={{4,12},{12,4},{20,28},{28,20},{5,13},{13,5},{21,29},{29,21},{6,14}... | collective-permute-start | bytes 3145736 | tf_op jit(solution)/shard_map/ppermute | solution.py:34
  13.2 3.1 %collective-permute-start.4 = (bf16[4096,128]{1,0:T(8,128)(2,1)}, bf16[4096,128]{1,0:T(8,128)(2,1)S(1)}, u32[]{:S(2)}, u32[]{:S(2)}) collective-permute-start(bf16[4096,128]{1,0:T(8,128)(2,1)} %refs_3_), channel_id=1, source_target_pairs={{4,20},{12,28},{20,4},{28,12},{5,21},{13,29},{21,5},{29,13},{6,22}... | collective-permute-start | bytes 3145736 | tf_op jit(solution)/shard_map/ppermute | solution.py:34
  16.4 0.0 copy-done
  16.4 0.0 copy-start.1
  16.4 1.2 %copy-done.1 = bf16[4096,128]{1,0:T(8,128)(2,1)S(1)} copy-done((bf16[4096,128]{1,0:T(8,128)(2,1)S(1)}, bf16[4096,128]{1,0:T(8,128)(2,1)}, u32[]{:S(2)}) %copy-start.1) | copy-done | bytes 1048600
  17.6 1.8 %shard_map.56.refs_2_.refs_5_ = f32[768,128]{1,0:T(8,128)S(1)} custom-call(bf16[384,4096]{1,0:T(8,128)(2,1)S(1)} %copy-done, bf16[384,4096]{1,0:T(8,128)(2,1)S(1)} %collective-permute-done.refs_3_.refs_1_, bf16[4096,128]{1,0:T(8,128)(2,1)S(1)} %copy-done.1, bf16[4096,128]{1,0:T(8,128)(2,1)S(1)} %copy-done.1), custom_call_target="tpu_custom_call" | custom-call | bytes 1024 | tf_op jit(solution)/shard_map/pallas_call | solution.py:54
  19.4 0.0 collective-permute-done.2.refs_1_.refs_2_
  19.4 10.2 %collective-permute-done.1.refs_0_.refs_3_ = bf16[4096,128]{1,0:T(8,128)(2,1)S(1)} collective-permute-done((bf16[4096,128]{1,0:T(8,128)(2,1)}, bf16[4096,128]{1,0:T(8,128)(2,1)S(1)}, u32[]{:S(2)}, u32[]{:S(2)}) %collective-permute-start.1) | collective-permute-done | bytes 1048608 | tf_op jit(solution)/shard_map/ppermute | solution.py:44
  29.7 1.7 %collective-permute-start.7 = (bf16[2688,128]{1,0:T(8,128)(2,1)S(1)}, bf16[2688,128]{1,0:T(8,128)(2,1)S(1)}, u32[]{:S(2)}, u32[]{:S(2)}) collective-permute-start(bf16[2688,128]{1,0:T(8,128)(2,1)S(1)} %get-tuple-element.30), channel_id=1, source_target_pairs={{0,8},{1,9},{2,10},{3,11},{4,5},{5,4},{6,7},{7,6},{8,0},{9,1},{10,... | collective-permute-start | bytes 2064392 | tf_op jit(solution)/shard_map/ppermute | solution.py:44
  31.4 1.1 %collective-permute-done.5.refs_1_.refs_4_ = bf16[4096,128]{1,0:T(8,128)(2,1)S(1)} collective-permute-done((bf16[4096,128]{1,0:T(8,128)(2,1)}, bf16[4096,128]{1,0:T(8,128)(2,1)S(1)}, u32[]{:S(2)}, u32[]{:S(2)}) %collective-permute-start.5) | collective-permute-done | bytes 1048608 | tf_op jit(solution)/shard_map/ppermute | solution.py:34
  32.5 0.0 collective-permute-done.4.refs_0_.refs_5_
  32.5 0.4 shard_map.58
  32.9 4.0 %collective-permute-start.8 = (bf16[2304,128]{1,0:T(8,128)(2,1)S(1)}, bf16[2304,128]{1,0:T(8,128)(2,1)S(1)}, u32[]{:S(2)}, u32[]{:S(2)}) collective-permute-start(bf16[2304,128]{1,0:T(8,128)(2,1)S(1)} %get-tuple-element.31), channel_id=1, source_target_pairs={{4,12},{12,4},{20,28},{28,20},{5,13},{13,5},{21,29},{29,21},{6,14}... | collective-permute-start | bytes 1769480 | tf_op jit(solution)/shard_map/ppermute | solution.py:34
  36.9 1.3 %collective-permute-start.6 = (bf16[1792,128]{1,0:T(8,128)(2,1)S(1)}, bf16[1792,128]{1,0:T(8,128)(2,1)S(1)}, u32[]{:S(2)}, u32[]{:S(2)}) collective-permute-start(bf16[1792,128]{1,0:T(8,128)(2,1)S(1)} %get-tuple-element.29), channel_id=1, source_target_pairs={{0,1},{1,0},{2,3},{3,2},{4,20},{5,21},{6,22},{7,23},{8,9},{9,8},{1... | collective-permute-start | bytes 1376264 | tf_op jit(solution)/shard_map/ppermute | solution.py:44
  38.2 0.7 %collective-permute-start.3 = (bf16[1408,128]{1,0:T(8,128)(2,1)S(1)}, bf16[1408,128]{1,0:T(8,128)(2,1)S(1)}, u32[]{:S(2)}, u32[]{:S(2)}) collective-permute-start(bf16[1408,128]{1,0:T(8,128)(2,1)S(1)} %get-tuple-element.28.refs_2_), channel_id=1, source_target_pairs={{0,16},{8,24},{16,0},{24,8},{1,17},{9,25},{17,1},{25,9},{2,18},{10... | collective-permute-start | bytes 1081352 | tf_op jit(solution)/shard_map/ppermute | solution.py:34
  38.9 1.8 %shard_map.59 = (f32[768,128]{1,0:T(8,128)S(1)}, f32[768,128]{1,0:T(8,128)S(1)}) custom-call(bf16[384,4096]{1,0:T(8,128)(2,1)S(1)} %copy-done, bf16[384,4096]{1,0:T(8,128)(2,1)S(1)} %collective-permute-done.refs_3_.refs_1_, bf16[4096,128]{1,0:T(8,128)(2,1)S(1)} %collective-permute-done.2.refs_1_.refs_2_, ...), custom_call_target="tpu_custom_call" | custom-call | bytes 1024 | tf_op jit(solution)/shard_map/pallas_call | solution.py:54
  40.7 0.0 collective-permute-done.7.refs_2_
  40.7 3.8 %collective-permute-done.8.refs_3_ = bf16[2304,128]{1,0:T(8,128)(2,1)S(1)} collective-permute-done((bf16[2304,128]{1,0:T(8,128)(2,1)S(1)}, bf16[2304,128]{1,0:T(8,128)(2,1)S(1)}, u32[]{:S(2)}, u32[]{:S(2)}) %collective-permute-start.8) | collective-permute-done | bytes 589856 | tf_op jit(solution)/shard_map/ppermute | solution.py:34
  44.4 1.1 %shard_map.60.refs_4_ = f32[768,128]{1,0:T(8,128)S(1)} custom-call(bf16[384,4096]{1,0:T(8,128)(2,1)S(1)} %copy-done, bf16[384,4096]{1,0:T(8,128)(2,1)S(1)} %collective-permute-done.refs_3_.refs_1_, bf16[2688,128]{1,0:T(8,128)(2,1)S(1)} %collective-permute-done.7.refs_2_, bf16[2304,128]{1,0:T(8,128)(2,1)S(1)} %collective-permute-done.8.refs_3_, ...), custom_call_target="tpu_custom_call" | custom-call | bytes 1024 | tf_op jit(solution)/shard_map/pallas_call | solution.py:54
  45.5 0.0 collective-permute-done.3.refs_2_
  45.5 0.0 collective-permute-done.6.refs_3_
  45.5 1.1 %shard_map.61 = (f32[768,128]{1,0:T(8,128)S(1)}, bf16[768,128]{1,0:T(8,128)(2,1)S(1)}, bf16[768,128]{1,0:T(8,128)(2,1)S(1)}, bf16[768,128]{1,0:T(8,128)(2,1)S(1)}) custom-call(bf16[384,4096]{1,0:T(8,128)(2,1)S(1)} %copy-done, bf16[384,4096]{1,0:T(8,128)(2,1)S(1)} %collective-permute-done.refs_3_.refs_1_, ...), custom_call_target="tpu_custom_call" | custom-call | bytes 1024 | tf_op jit(solution)/shard_map/pallas_call | solution.py:54
  46.6 3.4 %collective-permute-start.9 = (bf16[768,128]{1,0:T(8,128)(2,1)S(1)}, bf16[768,128]{1,0:T(8,128)(2,1)S(1)}, u32[]{:S(2)}, u32[]{:S(2)}) collective-permute-start(bf16[768,128]{1,0:T(8,128)(2,1)S(1)} %get-tuple-element.35), channel_id=1, source_target_pairs={{0,3},{1,2},{2,1},{3,0},{4,7},{5,6},{6,5},{7,4},{8,11},{9,10},{10,... | collective-permute-start | bytes 589832 | tf_op jit(solution)/shard_map/ppermute | solution.py:34
  50.0 0.0 collective-permute-start.10
  50.0 0.4 collective-permute-start.11
  50.3 2.9 %collective-permute-done.9.refs_1_ = bf16[768,128]{1,0:T(8,128)(2,1)S(1)} collective-permute-done((bf16[768,128]{1,0:T(8,128)(2,1)S(1)}, bf16[768,128]{1,0:T(8,128)(2,1)S(1)}, u32[]{:S(2)}, u32[]{:S(2)}) %collective-permute-start.9) | collective-permute-done | bytes 196640 | tf_op jit(solution)/shard_map/ppermute | solution.py:34
  53.2 5.3 %collective-permute-done.10.refs_2_ = bf16[768,128]{1,0:T(8,128)(2,1)S(1)} collective-permute-done((bf16[768,128]{1,0:T(8,128)(2,1)S(1)}, bf16[768,128]{1,0:T(8,128)(2,1)S(1)}, u32[]{:S(2)}, u32[]{:S(2)}) %collective-permute-start.10) | collective-permute-done | bytes 196640 | tf_op jit(solution)/shard_map/ppermute | solution.py:34
  58.5 0.0 collective-permute-done.11.refs_3_
  58.5 0.1 shard_map.62
  58.6 0.1 collective-permute-start.12
  58.7 1.4 %collective-permute-done.12.refs_1_ = f32[384,128]{1,0:T(8,128)S(1)} collective-permute-done((f32[384,128]{1,0:T(8,128)S(1)}, f32[384,128]{1,0:T(8,128)S(1)}, u32[]{:S(2)}, u32[]{:S(2)}) %collective-permute-start.12) | collective-permute-done | bytes 196640 | tf_op jit(solution)/shard_map/ppermute | solution.py:34
  60.1 0.3 shard_map.63
  60.4 1.5 %collective-permute-start.14 = (bf16[128,384]{1,0:T(8,128)(2,1)S(1)}, bf16[128,384]{1,0:T(8,128)(2,1)S(1)}, u32[]{:S(2)}, u32[]{:S(2)}) collective-permute-start(bf16[128,384]{1,0:T(8,128)(2,1)S(1)} %get-tuple-element.46), channel_id=1, source_target_pairs={{0,4},{4,8},{8,12},{12,16},{16,20},{20,24},{24,28},{28,0},{1,5},{5... | collective-permute-start | bytes 294920 | tf_op jit(solution)/shard_map/ppermute | solution.py:226
  61.9 0.0 collective-permute-start.13
  61.9 0.4 shard_map.64
  62.4 3.2 %collective-permute-done.13.refs_4_ = bf16[128,256]{1,0:T(8,128)(2,1)S(1)} collective-permute-done((bf16[128,256]{1,0:T(8,128)(2,1)S(1)}, bf16[128,256]{1,0:T(8,128)(2,1)S(1)}, u32[]{:S(2)}, u32[]{:S(2)}) %collective-permute-start.13) | collective-permute-done | bytes 65568 | tf_op jit(solution)/shard_map/ppermute | solution.py:226
  65.6 0.0 collective-permute-done.14.refs_5_
  65.6 1.2 %shard_map.65 = f32[384,256]{1,0:T(8,128)} custom-call(f32[384,256]{1,0:T(8,128)S(1)} %get-tuple-element.42.refs_0_, bf16[128,512]{1,0:T(8,128)(2,1)S(1)} %get-tuple-element.43.refs_1_, bf16[512,512]{1,0:T(8,128)(2,1)S(1)} %get-tuple-element.26.refs_2_.refs_1_, bf16[384,128]{1,0:T(8,128)(2,1)S(1)} %get-tuple-element.44.refs_3_, ...), custom_call_target="tpu_custom_call" | custom-call | bytes 1024 | tf_op jit(solution)/shard_map/pallas_call | solution.py:54
  (1 shorter events, 0.0 us)
Async XLA Ops:
  0.0 16.4 %copy-start = (bf16[384,4096]{1,0:T(8,128)(2,1)S(1)}, bf16[384,4096]{1,0:T(8,128)(2,1)}, u32[]{:S(2)}) copy-start(bf16[384,4096]{1,0:T(8,128)(2,1)} %refs_0_.9) | copy-start | bytes 9437188
  0.0 5.9 %collective-permute-start = (bf16[384,4096]{1,0:T(8,128)(2,1)}, bf16[384,4096]{1,0:T(8,128)(2,1)S(1)}, u32[]{:S(2)}, u32[]{:S(2)}) collective-permute-start(bf16[384,4096]{1,0:T(8,128)(2,1)} %refs_0_.9), channel_id=1, source_target_pairs={{0,4},{4,0},{8,12},{12,8},{16,20},{20,16},{24,28},{28,24},{1,5},{5... | collective-permute-start | bytes 9437192 | tf_op jit(solution)/shard_map/ppermute | solution.py:34
  0.1 19.3 %collective-permute-start.2 = (bf16[4096,128]{1,0:T(8,128)(2,1)}, bf16[4096,128]{1,0:T(8,128)(2,1)S(1)}, u32[]{:S(2)}, u32[]{:S(2)}) collective-permute-start(bf16[4096,128]{1,0:T(8,128)(2,1)} %refs_3_), channel_id=1, source_target_pairs={{0,8},{1,9},{2,10},{3,11},{4,5},{5,4},{6,7},{7,6},{8,0},{9,1},{10,... | collective-permute-start | bytes 3145736 | tf_op jit(solution)/shard_map/ppermute | solution.py:44
  2.8 26.9 %collective-permute-start.1 = (bf16[4096,128]{1,0:T(8,128)(2,1)}, bf16[4096,128]{1,0:T(8,128)(2,1)S(1)}, u32[]{:S(2)}, u32[]{:S(2)}) collective-permute-start(bf16[4096,128]{1,0:T(8,128)(2,1)} %refs_3_), channel_id=1, source_target_pairs={{0,16},{1,17},{2,18},{3,19},{4,5},{5,4},{6,7},{7,6},{8,24},{9,25},... | collective-permute-start | bytes 3145736 | tf_op jit(solution)/shard_map/ppermute | solution.py:44
  5.9 1.0 %copy-start.2 = (bf16[1,512,512]{2,1,0:T(8,128)(2,1)S(1)}, bf16[1,512,512]{2,1,0:T(8,128)(2,1)}, u32[]{:S(2)}) copy-start(bf16[1,512,512]{2,1,0:T(8,128)(2,1)} %refs_0_.5) | copy-start | bytes 1572868
  6.9 0.7 %copy-start.3 = (s32[1,512]{1,0:T(1,128)S(1)}, s32[1,512]{1,0:T(1,128)}, u32[]{:S(2)}) copy-start(s32[1,512]{1,0:T(1,128)} %refs_1_.1) | copy-start | bytes 6148
  7.6 0.7 copy-start.4
  9.0 23.5 %collective-permute-start.5 = (bf16[4096,128]{1,0:T(8,128)(2,1)}, bf16[4096,128]{1,0:T(8,128)(2,1)S(1)}, u32[]{:S(2)}, u32[]{:S(2)}) collective-permute-start(bf16[4096,128]{1,0:T(8,128)(2,1)} %refs_3_), channel_id=1, source_target_pairs={{4,12},{12,4},{20,28},{28,20},{5,13},{13,5},{21,29},{29,21},{6,14}... | collective-permute-start | bytes 3145736 | tf_op jit(solution)/shard_map/ppermute | solution.py:34
  13.2 19.2 %collective-permute-start.4 = (bf16[4096,128]{1,0:T(8,128)(2,1)}, bf16[4096,128]{1,0:T(8,128)(2,1)S(1)}, u32[]{:S(2)}, u32[]{:S(2)}) collective-permute-start(bf16[4096,128]{1,0:T(8,128)(2,1)} %refs_3_), channel_id=1, source_target_pairs={{4,20},{12,28},{20,4},{28,12},{5,21},{13,29},{21,5},{29,13},{6,22}... | collective-permute-start | bytes 3145736 | tf_op jit(solution)/shard_map/ppermute | solution.py:34
  16.4 1.2 %copy-start.1 = (bf16[4096,128]{1,0:T(8,128)(2,1)S(1)}, bf16[4096,128]{1,0:T(8,128)(2,1)}, u32[]{:S(2)}) copy-start(bf16[4096,128]{1,0:T(8,128)(2,1)} %refs_3_) | copy-start | bytes 3145732
  29.7 11.0 %collective-permute-start.7 = (bf16[2688,128]{1,0:T(8,128)(2,1)S(1)}, bf16[2688,128]{1,0:T(8,128)(2,1)S(1)}, u32[]{:S(2)}, u32[]{:S(2)}) collective-permute-start(bf16[2688,128]{1,0:T(8,128)(2,1)S(1)} %get-tuple-element.30), channel_id=1, source_target_pairs={{0,8},{1,9},{2,10},{3,11},{4,5},{5,4},{6,7},{7,6},{8,0},{9,1},{10,... | collective-permute-start | bytes 2064392 | tf_op jit(solution)/shard_map/ppermute | solution.py:44
  32.9 11.6 %collective-permute-start.8 = (bf16[2304,128]{1,0:T(8,128)(2,1)S(1)}, bf16[2304,128]{1,0:T(8,128)(2,1)S(1)}, u32[]{:S(2)}, u32[]{:S(2)}) collective-permute-start(bf16[2304,128]{1,0:T(8,128)(2,1)S(1)} %get-tuple-element.31), channel_id=1, source_target_pairs={{4,12},{12,4},{20,28},{28,20},{5,13},{13,5},{21,29},{29,21},{6,14}... | collective-permute-start | bytes 1769480 | tf_op jit(solution)/shard_map/ppermute | solution.py:34
  36.9 8.6 %collective-permute-start.6 = (bf16[1792,128]{1,0:T(8,128)(2,1)S(1)}, bf16[1792,128]{1,0:T(8,128)(2,1)S(1)}, u32[]{:S(2)}, u32[]{:S(2)}) collective-permute-start(bf16[1792,128]{1,0:T(8,128)(2,1)S(1)} %get-tuple-element.29), channel_id=1, source_target_pairs={{0,1},{1,0},{2,3},{3,2},{4,20},{5,21},{6,22},{7,23},{8,9},{9,8},{1... | collective-permute-start | bytes 1376264 | tf_op jit(solution)/shard_map/ppermute | solution.py:44
  38.2 7.3 %collective-permute-start.3 = (bf16[1408,128]{1,0:T(8,128)(2,1)S(1)}, bf16[1408,128]{1,0:T(8,128)(2,1)S(1)}, u32[]{:S(2)}, u32[]{:S(2)}) collective-permute-start(bf16[1408,128]{1,0:T(8,128)(2,1)S(1)} %get-tuple-element.28.refs_2_), channel_id=1, source_target_pairs={{0,16},{8,24},{16,0},{24,8},{1,17},{9,25},{17,1},{25,9},{2,18},{10... | collective-permute-start | bytes 1081352 | tf_op jit(solution)/shard_map/ppermute | solution.py:34
  46.6 6.6 %collective-permute-start.9 = (bf16[768,128]{1,0:T(8,128)(2,1)S(1)}, bf16[768,128]{1,0:T(8,128)(2,1)S(1)}, u32[]{:S(2)}, u32[]{:S(2)}) collective-permute-start(bf16[768,128]{1,0:T(8,128)(2,1)S(1)} %get-tuple-element.35), channel_id=1, source_target_pairs={{0,3},{1,2},{2,1},{3,0},{4,7},{5,6},{6,5},{7,4},{8,11},{9,10},{10,... | collective-permute-start | bytes 589832 | tf_op jit(solution)/shard_map/ppermute | solution.py:34
  50.0 8.5 %collective-permute-start.10 = (bf16[768,128]{1,0:T(8,128)(2,1)S(1)}, bf16[768,128]{1,0:T(8,128)(2,1)S(1)}, u32[]{:S(2)}, u32[]{:S(2)}) collective-permute-start(bf16[768,128]{1,0:T(8,128)(2,1)S(1)} %get-tuple-element.36), channel_id=1, source_target_pairs={{0,2},{1,3},{2,0},{3,1},{4,6},{5,7},{6,4},{7,5},{8,10},{9,11},{10,... | collective-permute-start | bytes 589832 | tf_op jit(solution)/shard_map/ppermute | solution.py:34
  50.0 8.5 %collective-permute-start.11 = (bf16[768,128]{1,0:T(8,128)(2,1)S(1)}, bf16[768,128]{1,0:T(8,128)(2,1)S(1)}, u32[]{:S(2)}, u32[]{:S(2)}) collective-permute-start(bf16[768,128]{1,0:T(8,128)(2,1)S(1)} %get-tuple-element.37), channel_id=1, source_target_pairs={{0,1},{1,0},{2,3},{3,2},{4,5},{5,4},{6,7},{7,6},{8,9},{9,8},{10,11... | collective-permute-start | bytes 589832 | tf_op jit(solution)/shard_map/ppermute | solution.py:34
  58.6 1.5 %collective-permute-start.12 = (f32[384,128]{1,0:T(8,128)S(1)}, f32[384,128]{1,0:T(8,128)S(1)}, u32[]{:S(2)}, u32[]{:S(2)}) collective-permute-start(f32[384,128]{1,0:T(8,128)S(1)} %get-tuple-element.39), channel_id=1, source_target_pairs={{0,4},{4,0},{8,12},{12,8},{16,20},{20,16},{24,28},{28,24},{1,5},{5... | collective-permute-start | bytes 589832 | tf_op jit(solution)/shard_map/ppermute | solution.py:34
  60.4 5.2 %collective-permute-start.14 = (bf16[128,384]{1,0:T(8,128)(2,1)S(1)}, bf16[128,384]{1,0:T(8,128)(2,1)S(1)}, u32[]{:S(2)}, u32[]{:S(2)}) collective-permute-start(bf16[128,384]{1,0:T(8,128)(2,1)S(1)} %get-tuple-element.46), channel_id=1, source_target_pairs={{0,4},{4,8},{8,12},{12,16},{16,20},{20,24},{24,28},{28,0},{1,5},{5... | collective-permute-start | bytes 294920 | tf_op jit(solution)/shard_map/ppermute | solution.py:226
  61.9 3.7 %collective-permute-start.13 = (bf16[128,256]{1,0:T(8,128)(2,1)S(1)}, bf16[128,256]{1,0:T(8,128)(2,1)S(1)}, u32[]{:S(2)}, u32[]{:S(2)}) collective-permute-start(bf16[128,256]{1,0:T(8,128)(2,1)S(1)} %get-tuple-element.45), channel_id=1, source_target_pairs={{0,28},{4,0},{8,4},{12,8},{16,12},{20,16},{24,20},{28,24},{1,29},{... | collective-permute-start | bytes 196616 | tf_op jit(solution)/shard_map/ppermute | solution.py:226

commit v24 on v22

--- a/solution.py
+++ b/solution.py
@@ -164,7 +164,7 @@
     own = call(own_kernel, block, (wavefunctions, theirs, rotation), after=(later,))[0]
     received += [exchanged(later, "domain", NEAR, CORE), exchanged(later, "domain", FAR, CORE)]
     passed, previous = [], [own]
-    for one, share in ((0, 21), (CORE, 18)):
+    for one, share in ((0, 19), (CORE, 17)):
         cut = states * share // 32
         outs = [shape(count, width, dtype=BF16) for count in (cut, states - cut)]
         pair = received[2 * one : 2 * one + 2][::-1]

time: 66.8 us -> 66.1 us (0.990)
  waiting for transfers between devices: 31.8 us -> 31.1 us
    ppermute x10, waiting for transfers between devices: 20 us -> 19.3 us  [exchanged(): lax.ppermute(value, axis, [(source, source ^ mask) for source in sources...]
where the time goes in v24:
time: 66.1 us; the launch traced here: 65.7 us
  waiting for transfers between devices  31.1 us (47%)
  starting transfers between devices  22 us (33%)
  Pallas kernels  8.84 us (13%)
  local copies, waits for them, and re-layouts  3.6 us (5%)
    ppermute x10, waiting for transfers between devices, exchanged(): lax.ppermute(value, axis, [(source, source ^ mask) for source in sources...  19.3 us
    ppermute x10, starting transfers between devices, exchanged(): lax.ppermute(value, axis, [(source, source ^ mask) for source in sources...  16.7 us
    pallas_call x11, Pallas kernels, call(): pl.pallas_call(body, out_shape=outs, in_specs=[pl.BlockSpec(memory_space=...  8.84 us
    ppermute x3, waiting for transfers between devices, paired(): return lax.ppermute(value, ('domain', 'band'), pairs)  8.37 us
    ppermute x3, starting transfers between devices, paired(): return lax.ppermute(value, ('domain', 'band'), pairs)  4.08 us
    unnamed x10, local copies, waits for them, and re-layouts  3.6 us
    ppermute x2, waiting for transfers between devices, rotated(): lax.ppermute(value, axis, [(source, (source + steps) % count) for source...  3.46 us
  transfers between devices with their start and end apart: 15, of which 8 were waited for; matrix products, arithmetic and copies ran while one was open for 0% of the time, Pallas kernels for 9%

profile of v24, /device:TPU:1, one launch (start us, length us, event | category | flops | bytes accessed | tf_op | source)
XLA Modules:
  0.0 65.7 jit_solution(5488056844633374355)
XLA Ops:
  0.0 0.0 copy-start
  0.0 0.1 collective-permute-start
  0.1 2.7 %collective-permute-start.2 = (bf16[4096,128]{1,0:T(8,128)(2,1)}, bf16[4096,128]{1,0:T(8,128)(2,1)S(1)}, u32[]{:S(2)}, u32[]{:S(2)}) collective-permute-start(bf16[4096,128]{1,0:T(8,128)(2,1)} %refs_3_), channel_id=1, source_target_pairs={{0,8},{1,9},{2,10},{3,11},{4,5},{5,4},{6,7},{7,6},{8,0},{9,1},{10,... | collective-permute-start | bytes 3145736 | tf_op jit(solution)/shard_map/ppermute | solution.py:44
  2.8 0.0 collective-permute-start.1
  2.8 3.0 %collective-permute-done.refs_3_.refs_1_ = bf16[384,4096]{1,0:T(8,128)(2,1)S(1)} collective-permute-done((bf16[384,4096]{1,0:T(8,128)(2,1)}, bf16[384,4096]{1,0:T(8,128)(2,1)S(1)}, u32[]{:S(2)}, u32[]{:S(2)}) %collective-permute-start) | collective-permute-done | bytes 3145760 | tf_op jit(solution)/shard_map/ppermute | solution.py:34
  5.9 0.0 copy-start.2
  5.9 1.0 %copy-done.2 = bf16[1,512,512]{2,1,0:T(8,128)(2,1)S(1)} copy-done((bf16[1,512,512]{2,1,0:T(8,128)(2,1)S(1)}, bf16[1,512,512]{2,1,0:T(8,128)(2,1)}, u32[]{:S(2)}) %copy-start.2) | copy-done | bytes 524312
  6.9 0.0 copy-start.3
  6.9 0.7 %copy-done.3 = s32[1,512]{1,0:T(1,128)S(1)} copy-done((s32[1,512]{1,0:T(1,128)S(1)}, s32[1,512]{1,0:T(1,128)}, u32[]{:S(2)}) %copy-start.3) | copy-done | bytes 2072
  7.6 0.0 copy-start.4
  7.6 0.7 copy-done.4
  8.3 0.7 %shard_map.55 = (bf16[512,512]{1,0:T(8,128)(2,1)S(1)}, bf16[128,384]{1,0:T(8,128)(2,1)S(1)}, bf16[384,128]{1,0:T(8,128)(2,1)S(1)}) custom-call(bf16[1,512,512]{2,1,0:T(8,128)(2,1)S(1)} %copy-done.2, s32[1,512]{1,0:T(1,128)S(1)} %copy-done.3, s32[1,128]{1,0:T(1,128)S(1)} %bitcast.1, bf16[384,4096]{1,0:T(8,128)(2,1)S(1)} %collective-permute-done.refs_3_.refs_1_), custom_call_target="tpu_custom_call" | custom-call | bytes 1024 | tf_op jit(solution)/shard_map/pallas_call | solution.py:54
  9.0 4.3 %collective-permute-start.5 = (bf16[4096,128]{1,0:T(8,128)(2,1)}, bf16[4096,128]{1,0:T(8,128)(2,1)S(1)}, u32[]{:S(2)}, u32[]{:S(2)}) collective-permute-start(bf16[4096,128]{1,0:T(8,128)(2,1)} %refs_3_), channel_id=1, source_target_pairs={{4,12},{12,4},{20,28},{28,20},{5,13},{13,5},{21,29},{29,21},{6,14}... | collective-permute-start | bytes 3145736 | tf_op jit(solution)/shard_map/ppermute | solution.py:34
  13.2 3.1 %collective-permute-start.4 = (bf16[4096,128]{1,0:T(8,128)(2,1)}, bf16[4096,128]{1,0:T(8,128)(2,1)S(1)}, u32[]{:S(2)}, u32[]{:S(2)}) collective-permute-start(bf16[4096,128]{1,0:T(8,128)(2,1)} %refs_3_), channel_id=1, source_target_pairs={{4,20},{12,28},{20,4},{28,12},{5,21},{13,29},{21,5},{29,13},{6,22}... | collective-permute-start | bytes 3145736 | tf_op jit(solution)/shard_map/ppermute | solution.py:34
  16.4 0.0 copy-done
  16.4 0.0 copy-start.1
  16.4 1.2 %copy-done.1 = bf16[4096,128]{1,0:T(8,128)(2,1)S(1)} copy-done((bf16[4096,128]{1,0:T(8,128)(2,1)S(1)}, bf16[4096,128]{1,0:T(8,128)(2,1)}, u32[]{:S(2)}) %copy-start.1) | copy-done | bytes 1048600
  17.6 1.8 %shard_map.56.refs_2_.refs_5_ = f32[768,128]{1,0:T(8,128)S(1)} custom-call(bf16[384,4096]{1,0:T(8,128)(2,1)S(1)} %copy-done, bf16[384,4096]{1,0:T(8,128)(2,1)S(1)} %collective-permute-done.refs_3_.refs_1_, bf16[4096,128]{1,0:T(8,128)(2,1)S(1)} %copy-done.1, bf16[4096,128]{1,0:T(8,128)(2,1)S(1)} %copy-done.1), custom_call_target="tpu_custom_call" | custom-call | bytes 1024 | tf_op jit(solution)/shard_map/pallas_call | solution.py:54
  19.4 0.0 collective-permute-done.2.refs_1_.refs_2_
  19.4 8.4 %collective-permute-done.1.refs_0_.refs_3_ = bf16[4096,128]{1,0:T(8,128)(2,1)S(1)} collective-permute-done((bf16[4096,128]{1,0:T(8,128)(2,1)}, bf16[4096,128]{1,0:T(8,128)(2,1)S(1)}, u32[]{:S(2)}, u32[]{:S(2)}) %collective-permute-start.1) | collective-permute-done | bytes 1048608 | tf_op jit(solution)/shard_map/ppermute | solution.py:44
  27.8 0.7 %collective-permute-start.7 = (bf16[2432,128]{1,0:T(8,128)(2,1)S(1)}, bf16[2432,128]{1,0:T(8,128)(2,1)S(1)}, u32[]{:S(2)}, u32[]{:S(2)}) collective-permute-start(bf16[2432,128]{1,0:T(8,128)(2,1)S(1)} %get-tuple-element.30), channel_id=1, source_target_pairs={{0,8},{8,0},{16,24},{24,16},{1,9},{9,1},{17,25},{25,17},{2,10},{10... | collective-permute-start | bytes 1867784 | tf_op jit(solution)/shard_map/ppermute | solution.py:34
  28.5 2.1 %collective-permute-done.5.refs_1_.refs_4_ = bf16[4096,128]{1,0:T(8,128)(2,1)S(1)} collective-permute-done((bf16[4096,128]{1,0:T(8,128)(2,1)}, bf16[4096,128]{1,0:T(8,128)(2,1)S(1)}, u32[]{:S(2)}, u32[]{:S(2)}) %collective-permute-start.5) | collective-permute-done | bytes 1048608 | tf_op jit(solution)/shard_map/ppermute | solution.py:34
  30.6 0.0 collective-permute-done.4.refs_0_.refs_5_
  30.6 0.4 shard_map.58
  31.0 4.0 %collective-permute-start.8 = (bf16[2176,128]{1,0:T(8,128)(2,1)S(1)}, bf16[2176,128]{1,0:T(8,128)(2,1)S(1)}, u32[]{:S(2)}, u32[]{:S(2)}) collective-permute-start(bf16[2176,128]{1,0:T(8,128)(2,1)S(1)} %get-tuple-element.31), channel_id=1, source_target_pairs={{4,12},{12,4},{20,28},{28,20},{5,13},{13,5},{21,29},{29,21},{6,14}... | collective-permute-start | bytes 1671176 | tf_op jit(solution)/shard_map/ppermute | solution.py:34
  35.0 1.3 %collective-permute-start.6 = (bf16[1920,128]{1,0:T(8,128)(2,1)S(1)}, bf16[1920,128]{1,0:T(8,128)(2,1)S(1)}, u32[]{:S(2)}, u32[]{:S(2)}) collective-permute-start(bf16[1920,128]{1,0:T(8,128)(2,1)S(1)} %get-tuple-element.29), channel_id=1, source_target_pairs={{0,1},{1,0},{2,3},{3,2},{4,20},{5,21},{6,22},{7,23},{8,9},{9,8},{1... | collective-permute-start | bytes 1474568 | tf_op jit(solution)/shard_map/ppermute | solution.py:44
  36.4 0.7 %collective-permute-start.3 = (bf16[1664,128]{1,0:T(8,128)(2,1)S(1)}, bf16[1664,128]{1,0:T(8,128)(2,1)S(1)}, u32[]{:S(2)}, u32[]{:S(2)}) collective-permute-start(bf16[1664,128]{1,0:T(8,128)(2,1)S(1)} %get-tuple-element.28.refs_2_), channel_id=1, source_target_pairs={{0,16},{8,24},{16,0},{24,8},{1,17},{9,25},{17,1},{25,9},{2,18},{10... | collective-permute-start | bytes 1277960 | tf_op jit(solution)/shard_map/ppermute | solution.py:34
  37.0 1.8 %shard_map.59 = (f32[768,128]{1,0:T(8,128)S(1)}, f32[768,128]{1,0:T(8,128)S(1)}) custom-call(bf16[384,4096]{1,0:T(8,128)(2,1)S(1)} %copy-done, bf16[384,4096]{1,0:T(8,128)(2,1)S(1)} %collective-permute-done.refs_3_.refs_1_, bf16[4096,128]{1,0:T(8,128)(2,1)S(1)} %collective-permute-done.2.refs_1_.refs_2_, ...), custom_call_target="tpu_custom_call" | custom-call | bytes 1024 | tf_op jit(solution)/shard_map/pallas_call | solution.py:54
  38.9 0.0 collective-permute-done.7.refs_2_
  38.9 3.4 %collective-permute-done.8.refs_3_ = bf16[2176,128]{1,0:T(8,128)(2,1)S(1)} collective-permute-done((bf16[2176,128]{1,0:T(8,128)(2,1)S(1)}, bf16[2176,128]{1,0:T(8,128)(2,1)S(1)}, u32[]{:S(2)}, u32[]{:S(2)}) %collective-permute-start.8) | collective-permute-done | bytes 557088 | tf_op jit(solution)/shard_map/ppermute | solution.py:34
  42.3 1.0 %shard_map.60.refs_4_ = f32[768,128]{1,0:T(8,128)S(1)} custom-call(bf16[384,4096]{1,0:T(8,128)(2,1)S(1)} %copy-done, bf16[384,4096]{1,0:T(8,128)(2,1)S(1)} %collective-permute-done.refs_3_.refs_1_, bf16[2432,128]{1,0:T(8,128)(2,1)S(1)} %collective-permute-done.7.refs_2_, bf16[2176,128]{1,0:T(8,128)(2,1)S(1)} %collective-permute-done.8.refs_3_, ...), custom_call_target="tpu_custom_call" | custom-call | bytes 1024 | tf_op jit(solution)/shard_map/pallas_call | solution.py:54
  43.3 0.0 collective-permute-done.3.refs_2_
  43.3 0.0 collective-permute-done.6.refs_3_
  43.3 1.1 %shard_map.61 = (f32[768,128]{1,0:T(8,128)S(1)}, bf16[768,128]{1,0:T(8,128)(2,1)S(1)}, bf16[768,128]{1,0:T(8,128)(2,1)S(1)}, bf16[768,128]{1,0:T(8,128)(2,1)S(1)}) custom-call(bf16[384,4096]{1,0:T(8,128)(2,1)S(1)} %copy-done, bf16[384,4096]{1,0:T(8,128)(2,1)S(1)} %collective-permute-done.refs_3_.refs_1_, ...), custom_call_target="tpu_custom_call" | custom-call | bytes 1024 | tf_op jit(solution)/shard_map/pallas_call | solution.py:54
  44.4 3.4 %collective-permute-start.9 = (bf16[768,128]{1,0:T(8,128)(2,1)S(1)}, bf16[768,128]{1,0:T(8,128)(2,1)S(1)}, u32[]{:S(2)}, u32[]{:S(2)}) collective-permute-start(bf16[768,128]{1,0:T(8,128)(2,1)S(1)} %get-tuple-element.35), channel_id=1, source_target_pairs={{0,3},{1,2},{2,1},{3,0},{4,7},{5,6},{6,5},{7,4},{8,11},{9,10},{10,... | collective-permute-start | bytes 589832 | tf_op jit(solution)/shard_map/ppermute | solution.py:34
  47.8 0.0 collective-permute-start.10
  47.8 0.4 collective-permute-start.11
  48.1 2.9 %collective-permute-done.9.refs_1_ = bf16[768,128]{1,0:T(8,128)(2,1)S(1)} collective-permute-done((bf16[768,128]{1,0:T(8,128)(2,1)S(1)}, bf16[768,128]{1,0:T(8,128)(2,1)S(1)}, u32[]{:S(2)}, u32[]{:S(2)}) %collective-permute-start.9) | collective-permute-done | bytes 196640 | tf_op jit(solution)/shard_map/ppermute | solution.py:34
  51.0 6.4 %collective-permute-done.10.refs_2_ = bf16[768,128]{1,0:T(8,128)(2,1)S(1)} collective-permute-done((bf16[768,128]{1,0:T(8,128)(2,1)S(1)}, bf16[768,128]{1,0:T(8,128)(2,1)S(1)}, u32[]{:S(2)}, u32[]{:S(2)}) %collective-permute-start.10) | collective-permute-done | bytes 196640 | tf_op jit(solution)/shard_map/ppermute | solution.py:34
  57.4 0.0 collective-permute-done.11.refs_3_
  57.5 0.1 shard_map.62
  57.5 0.1 collective-permute-start.12
  57.6 1.4 %collective-permute-done.12.refs_1_ = f32[384,128]{1,0:T(8,128)S(1)} collective-permute-done((f32[384,128]{1,0:T(8,128)S(1)}, f32[384,128]{1,0:T(8,128)S(1)}, u32[]{:S(2)}, u32[]{:S(2)}) %collective-permute-start.12) | collective-permute-done | bytes 196640 | tf_op jit(solution)/shard_map/ppermute | solution.py:34
  59.0 0.3 shard_map.63
  59.3 1.3 %collective-permute-start.14 = (bf16[128,384]{1,0:T(8,128)(2,1)S(1)}, bf16[128,384]{1,0:T(8,128)(2,1)S(1)}, u32[]{:S(2)}, u32[]{:S(2)}) collective-permute-start(bf16[128,384]{1,0:T(8,128)(2,1)S(1)} %get-tuple-element.46), channel_id=1, source_target_pairs={{0,4},{4,8},{8,12},{12,16},{16,20},{20,24},{24,28},{28,0},{1,5},{5... | collective-permute-start | bytes 294920 | tf_op jit(solution)/shard_map/ppermute | solution.py:226
  60.6 0.0 collective-permute-start.13
  60.6 0.4 shard_map.64
  61.1 3.5 %collective-permute-done.13.refs_4_ = bf16[128,256]{1,0:T(8,128)(2,1)S(1)} collective-permute-done((bf16[128,256]{1,0:T(8,128)(2,1)S(1)}, bf16[128,256]{1,0:T(8,128)(2,1)S(1)}, u32[]{:S(2)}, u32[]{:S(2)}) %collective-permute-start.13) | collective-permute-done | bytes 65568 | tf_op jit(solution)/shard_map/ppermute | solution.py:226
  64.5 0.0 collective-permute-done.14.refs_5_
  64.5 1.2 %shard_map.65 = f32[384,256]{1,0:T(8,128)} custom-call(f32[384,256]{1,0:T(8,128)S(1)} %get-tuple-element.42.refs_0_, bf16[128,512]{1,0:T(8,128)(2,1)S(1)} %get-tuple-element.43.refs_1_, bf16[512,512]{1,0:T(8,128)(2,1)S(1)} %get-tuple-element.26.refs_2_.refs_1_, bf16[384,128]{1,0:T(8,128)(2,1)S(1)} %get-tuple-element.44.refs_3_, ...), custom_call_target="tpu_custom_call" | custom-call | bytes 1024 | tf_op jit(solution)/shard_map/pallas_call | solution.py:54
  (1 shorter events, 0.0 us)
Async XLA Ops:
  0.0 16.4 %copy-start = (bf16[384,4096]{1,0:T(8,128)(2,1)S(1)}, bf16[384,4096]{1,0:T(8,128)(2,1)}, u32[]{:S(2)}) copy-start(bf16[384,4096]{1,0:T(8,128)(2,1)} %refs_0_.9) | copy-start | bytes 9437188
  0.0 5.9 %collective-permute-start = (bf16[384,4096]{1,0:T(8,128)(2,1)}, bf16[384,4096]{1,0:T(8,128)(2,1)S(1)}, u32[]{:S(2)}, u32[]{:S(2)}) collective-permute-start(bf16[384,4096]{1,0:T(8,128)(2,1)} %refs_0_.9), channel_id=1, source_target_pairs={{0,4},{4,0},{8,12},{12,8},{16,20},{20,16},{24,28},{28,24},{1,5},{5... | collective-permute-start | bytes 9437192 | tf_op jit(solution)/shard_map/ppermute | solution.py:34
  0.1 19.3 %collective-permute-start.2 = (bf16[4096,128]{1,0:T(8,128)(2,1)}, bf16[4096,128]{1,0:T(8,128)(2,1)S(1)}, u32[]{:S(2)}, u32[]{:S(2)}) collective-permute-start(bf16[4096,128]{1,0:T(8,128)(2,1)} %refs_3_), channel_id=1, source_target_pairs={{0,8},{1,9},{2,10},{3,11},{4,5},{5,4},{6,7},{7,6},{8,0},{9,1},{10,... | collective-permute-start | bytes 3145736 | tf_op jit(solution)/shard_map/ppermute | solution.py:44
  2.8 25.0 %collective-permute-start.1 = (bf16[4096,128]{1,0:T(8,128)(2,1)}, bf16[4096,128]{1,0:T(8,128)(2,1)S(1)}, u32[]{:S(2)}, u32[]{:S(2)}) collective-permute-start(bf16[4096,128]{1,0:T(8,128)(2,1)} %refs_3_), channel_id=1, source_target_pairs={{0,16},{1,17},{2,18},{3,19},{4,5},{5,4},{6,7},{7,6},{8,24},{9,25},... | collective-permute-start | bytes 3145736 | tf_op jit(solution)/shard_map/ppermute | solution.py:44
  5.9 1.0 %copy-start.2 = (bf16[1,512,512]{2,1,0:T(8,128)(2,1)S(1)}, bf16[1,512,512]{2,1,0:T(8,128)(2,1)}, u32[]{:S(2)}) copy-start(bf16[1,512,512]{2,1,0:T(8,128)(2,1)} %refs_0_.5) | copy-start | bytes 1572868
  6.9 0.7 %copy-start.3 = (s32[1,512]{1,0:T(1,128)S(1)}, s32[1,512]{1,0:T(1,128)}, u32[]{:S(2)}) copy-start(s32[1,512]{1,0:T(1,128)} %refs_1_.1) | copy-start | bytes 6148
  7.6 0.7 copy-start.4
  9.0 21.7 %collective-permute-start.5 = (bf16[4096,128]{1,0:T(8,128)(2,1)}, bf16[4096,128]{1,0:T(8,128)(2,1)S(1)}, u32[]{:S(2)}, u32[]{:S(2)}) collective-permute-start(bf16[4096,128]{1,0:T(8,128)(2,1)} %refs_3_), channel_id=1, source_target_pairs={{4,12},{12,4},{20,28},{28,20},{5,13},{13,5},{21,29},{29,21},{6,14}... | collective-permute-start | bytes 3145736 | tf_op jit(solution)/shard_map/ppermute | solution.py:34
  13.2 17.4 %collective-permute-start.4 = (bf16[4096,128]{1,0:T(8,128)(2,1)}, bf16[4096,128]{1,0:T(8,128)(2,1)S(1)}, u32[]{:S(2)}, u32[]{:S(2)}) collective-permute-start(bf16[4096,128]{1,0:T(8,128)(2,1)} %refs_3_), channel_id=1, source_target_pairs={{4,20},{12,28},{20,4},{28,12},{5,21},{13,29},{21,5},{29,13},{6,22}... | collective-permute-start | bytes 3145736 | tf_op jit(solution)/shard_map/ppermute | solution.py:34
  16.4 1.2 %copy-start.1 = (bf16[4096,128]{1,0:T(8,128)(2,1)S(1)}, bf16[4096,128]{1,0:T(8,128)(2,1)}, u32[]{:S(2)}) copy-start(bf16[4096,128]{1,0:T(8,128)(2,1)} %refs_3_) | copy-start | bytes 3145732
  27.8 11.1 %collective-permute-start.7 = (bf16[2432,128]{1,0:T(8,128)(2,1)S(1)}, bf16[2432,128]{1,0:T(8,128)(2,1)S(1)}, u32[]{:S(2)}, u32[]{:S(2)}) collective-permute-start(bf16[2432,128]{1,0:T(8,128)(2,1)S(1)} %get-tuple-element.30), channel_id=1, source_target_pairs={{0,8},{8,0},{16,24},{24,16},{1,9},{9,1},{17,25},{25,17},{2,10},{10... | collective-permute-start | bytes 1867784 | tf_op jit(solution)/shard_map/ppermute | solution.py:34
  31.0 11.2 %collective-permute-start.8 = (bf16[2176,128]{1,0:T(8,128)(2,1)S(1)}, bf16[2176,128]{1,0:T(8,128)(2,1)S(1)}, u32[]{:S(2)}, u32[]{:S(2)}) collective-permute-start(bf16[2176,128]{1,0:T(8,128)(2,1)S(1)} %get-tuple-element.31), channel_id=1, source_target_pairs={{4,12},{12,4},{20,28},{28,20},{5,13},{13,5},{21,29},{29,21},{6,14}... | collective-permute-start | bytes 1671176 | tf_op jit(solution)/shard_map/ppermute | solution.py:34
  35.0 8.2 %collective-permute-start.6 = (bf16[1920,128]{1,0:T(8,128)(2,1)S(1)}, bf16[1920,128]{1,0:T(8,128)(2,1)S(1)}, u32[]{:S(2)}, u32[]{:S(2)}) collective-permute-start(bf16[1920,128]{1,0:T(8,128)(2,1)S(1)} %get-tuple-element.29), channel_id=1, source_target_pairs={{0,1},{1,0},{2,3},{3,2},{4,20},{5,21},{6,22},{7,23},{8,9},{9,8},{1... | collective-permute-start | bytes 1474568 | tf_op jit(solution)/shard_map/ppermute | solution.py:44
  36.4 6.9 %collective-permute-start.3 = (bf16[1664,128]{1,0:T(8,128)(2,1)S(1)}, bf16[1664,128]{1,0:T(8,128)(2,1)S(1)}, u32[]{:S(2)}, u32[]{:S(2)}) collective-permute-start(bf16[1664,128]{1,0:T(8,128)(2,1)S(1)} %get-tuple-element.28.refs_2_), channel_id=1, source_target_pairs={{0,16},{8,24},{16,0},{24,8},{1,17},{9,25},{17,1},{25,9},{2,18},{10... | collective-permute-start | bytes 1277960 | tf_op jit(solution)/shard_map/ppermute | solution.py:34
  44.4 6.6 %collective-permute-start.9 = (bf16[768,128]{1,0:T(8,128)(2,1)S(1)}, bf16[768,128]{1,0:T(8,128)(2,1)S(1)}, u32[]{:S(2)}, u32[]{:S(2)}) collective-permute-start(bf16[768,128]{1,0:T(8,128)(2,1)S(1)} %get-tuple-element.35), channel_id=1, source_target_pairs={{0,3},{1,2},{2,1},{3,0},{4,7},{5,6},{6,5},{7,4},{8,11},{9,10},{10,... | collective-permute-start | bytes 589832 | tf_op jit(solution)/shard_map/ppermute | solution.py:34
  47.8 9.7 %collective-permute-start.10 = (bf16[768,128]{1,0:T(8,128)(2,1)S(1)}, bf16[768,128]{1,0:T(8,128)(2,1)S(1)}, u32[]{:S(2)}, u32[]{:S(2)}) collective-permute-start(bf16[768,128]{1,0:T(8,128)(2,1)S(1)} %get-tuple-element.36), channel_id=1, source_target_pairs={{0,2},{1,3},{2,0},{3,1},{4,6},{5,7},{6,4},{7,5},{8,10},{9,11},{10,... | collective-permute-start | bytes 589832 | tf_op jit(solution)/shard_map/ppermute | solution.py:34
  47.8 9.7 %collective-permute-start.11 = (bf16[768,128]{1,0:T(8,128)(2,1)S(1)}, bf16[768,128]{1,0:T(8,128)(2,1)S(1)}, u32[]{:S(2)}, u32[]{:S(2)}) collective-permute-start(bf16[768,128]{1,0:T(8,128)(2,1)S(1)} %get-tuple-element.37), channel_id=1, source_target_pairs={{0,1},{1,0},{2,3},{3,2},{4,5},{5,4},{6,7},{7,6},{8,9},{9,8},{10,11... | collective-permute-start | bytes 589832 | tf_op jit(solution)/shard_map/ppermute | solution.py:34
  57.5 1.5 %collective-permute-start.12 = (f32[384,128]{1,0:T(8,128)S(1)}, f32[384,128]{1,0:T(8,128)S(1)}, u32[]{:S(2)}, u32[]{:S(2)}) collective-permute-start(f32[384,128]{1,0:T(8,128)S(1)} %get-tuple-element.39), channel_id=1, source_target_pairs={{0,4},{4,0},{8,12},{12,8},{16,20},{20,16},{24,28},{28,24},{1,5},{5... | collective-permute-start | bytes 589832 | tf_op jit(solution)/shard_map/ppermute | solution.py:34
  59.3 5.2 %collective-permute-start.14 = (bf16[128,384]{1,0:T(8,128)(2,1)S(1)}, bf16[128,384]{1,0:T(8,128)(2,1)S(1)}, u32[]{:S(2)}, u32[]{:S(2)}) collective-permute-start(bf16[128,384]{1,0:T(8,128)(2,1)S(1)} %get-tuple-element.46), channel_id=1, source_target_pairs={{0,4},{4,8},{8,12},{12,16},{16,20},{20,24},{24,28},{28,0},{1,5},{5... | collective-permute-start | bytes 294920 | tf_op jit(solution)/shard_map/ppermute | solution.py:226
  60.6 3.9 %collective-permute-start.13 = (bf16[128,256]{1,0:T(8,128)(2,1)S(1)}, bf16[128,256]{1,0:T(8,128)(2,1)S(1)}, u32[]{:S(2)}, u32[]{:S(2)}) collective-permute-start(bf16[128,256]{1,0:T(8,128)(2,1)S(1)} %get-tuple-element.45), channel_id=1, source_target_pairs={{0,28},{4,0},{8,4},{12,8},{16,12},{20,16},{24,20},{28,24},{1,29},{... | collective-permute-start | bytes 196616 | tf_op jit(solution)/shard_map/ppermute | solution.py:226

commit v25 on v24

--- a/solution.py
+++ b/solution.py
@@ -164,7 +164,7 @@
     own = call(own_kernel, block, (wavefunctions, theirs, rotation), after=(later,))[0]
     received += [exchanged(later, "domain", NEAR, CORE), exchanged(later, "domain", FAR, CORE)]
     passed, previous = [], [own]
-    for one, share in ((0, 19), (CORE, 17)):
+    for one, share in ((0, 18), (CORE, 17)):
         cut = states * share // 32
         outs = [shape(count, width, dtype=BF16) for count in (cut, states - cut)]
         pair = received[2 * one : 2 * one + 2][::-1]

time: 66.1 us -> 65.7 us (level)
  no operation moved by 1% of the time
where the time goes in v25:
time: 65.7 us; the launch traced here: 65.4 us
  waiting for transfers between devices  30.8 us (47%)
  starting transfers between devices  22 us (33%)
  Pallas kernels  8.85 us (13%)
  local copies, waits for them, and re-layouts  3.6 us (5%)
    ppermute x10, waiting for transfers between devices, exchanged(): lax.ppermute(value, axis, [(source, source ^ mask) for source in sources...  18.9 us
    ppermute x10, starting transfers between devices, exchanged(): lax.ppermute(value, axis, [(source, source ^ mask) for source in sources...  16.7 us
    pallas_call x11, Pallas kernels, call(): pl.pallas_call(body, out_shape=outs, in_specs=[pl.BlockSpec(memory_space=...  8.85 us
    ppermute x3, waiting for transfers between devices, paired(): return lax.ppermute(value, ('domain', 'band'), pairs)  8.37 us
    ppermute x3, starting transfers between devices, paired(): return lax.ppermute(value, ('domain', 'band'), pairs)  4.08 us
    unnamed x10, local copies, waits for them, and re-layouts  3.6 us
    ppermute x2, waiting for transfers between devices, rotated(): lax.ppermute(value, axis, [(source, (source + steps) % count) for source...  3.46 us
  transfers between devices with their start and end apart: 15, of which 8 were waited for; matrix products, arithmetic and copies ran while one was open for 0% of the time, Pallas kernels for 9%

profile of v25, /device:TPU:1, one launch (start us, length us, event | category | flops | bytes accessed | tf_op | source)
XLA Modules:
  0.0 65.4 jit_solution(13548442125847370414)
XLA Ops:
  0.0 0.0 copy-start
  0.0 0.1 collective-permute-start
  0.1 2.7 %collective-permute-start.2 = (bf16[4096,128]{1,0:T(8,128)(2,1)}, bf16[4096,128]{1,0:T(8,128)(2,1)S(1)}, u32[]{:S(2)}, u32[]{:S(2)}) collective-permute-start(bf16[4096,128]{1,0:T(8,128)(2,1)} %refs_3_), channel_id=1, source_target_pairs={{0,8},{1,9},{2,10},{3,11},{4,5},{5,4},{6,7},{7,6},{8,0},{9,1},{10,... | collective-permute-start | bytes 3145736 | tf_op jit(solution)/shard_map/ppermute | solution.py:44
  2.8 0.0 collective-permute-start.1
  2.8 3.0 %collective-permute-done.refs_3_.refs_1_ = bf16[384,4096]{1,0:T(8,128)(2,1)S(1)} collective-permute-done((bf16[384,4096]{1,0:T(8,128)(2,1)}, bf16[384,4096]{1,0:T(8,128)(2,1)S(1)}, u32[]{:S(2)}, u32[]{:S(2)}) %collective-permute-start) | collective-permute-done | bytes 3145760 | tf_op jit(solution)/shard_map/ppermute | solution.py:34
  5.9 0.0 copy-start.2
  5.9 1.0 %copy-done.2 = bf16[1,512,512]{2,1,0:T(8,128)(2,1)S(1)} copy-done((bf16[1,512,512]{2,1,0:T(8,128)(2,1)S(1)}, bf16[1,512,512]{2,1,0:T(8,128)(2,1)}, u32[]{:S(2)}) %copy-start.2) | copy-done | bytes 524312
  6.9 0.0 copy-start.3
  6.9 0.7 %copy-done.3 = s32[1,512]{1,0:T(1,128)S(1)} copy-done((s32[1,512]{1,0:T(1,128)S(1)}, s32[1,512]{1,0:T(1,128)}, u32[]{:S(2)}) %copy-start.3) | copy-done | bytes 2072
  7.6 0.0 copy-start.4
  7.6 0.7 copy-done.4
  8.3 0.7 %shard_map.55 = (bf16[512,512]{1,0:T(8,128)(2,1)S(1)}, bf16[128,384]{1,0:T(8,128)(2,1)S(1)}, bf16[384,128]{1,0:T(8,128)(2,1)S(1)}) custom-call(bf16[1,512,512]{2,1,0:T(8,128)(2,1)S(1)} %copy-done.2, s32[1,512]{1,0:T(1,128)S(1)} %copy-done.3, s32[1,128]{1,0:T(1,128)S(1)} %bitcast.1, bf16[384,4096]{1,0:T(8,128)(2,1)S(1)} %collective-permute-done.refs_3_.refs_1_), custom_call_target="tpu_custom_call" | custom-call | bytes 1024 | tf_op jit(solution)/shard_map/pallas_call | solution.py:54
  9.0 4.3 %collective-permute-start.5 = (bf16[4096,128]{1,0:T(8,128)(2,1)}, bf16[4096,128]{1,0:T(8,128)(2,1)S(1)}, u32[]{:S(2)}, u32[]{:S(2)}) collective-permute-start(bf16[4096,128]{1,0:T(8,128)(2,1)} %refs_3_), channel_id=1, source_target_pairs={{4,12},{12,4},{20,28},{28,20},{5,13},{13,5},{21,29},{29,21},{6,14}... | collective-permute-start | bytes 3145736 | tf_op jit(solution)/shard_map/ppermute | solution.py:34
  13.2 3.1 %collective-permute-start.4 = (bf16[4096,128]{1,0:T(8,128)(2,1)}, bf16[4096,128]{1,0:T(8,128)(2,1)S(1)}, u32[]{:S(2)}, u32[]{:S(2)}) collective-permute-start(bf16[4096,128]{1,0:T(8,128)(2,1)} %refs_3_), channel_id=1, source_target_pairs={{4,20},{12,28},{20,4},{28,12},{5,21},{13,29},{21,5},{29,13},{6,22}... | collective-permute-start | bytes 3145736 | tf_op jit(solution)/shard_map/ppermute | solution.py:34
  16.4 0.0 copy-done
  16.4 0.0 copy-start.1
  16.4 1.2 %copy-done.1 = bf16[4096,128]{1,0:T(8,128)(2,1)S(1)} copy-done((bf16[4096,128]{1,0:T(8,128)(2,1)S(1)}, bf16[4096,128]{1,0:T(8,128)(2,1)}, u32[]{:S(2)}) %copy-start.1) | copy-done | bytes 1048600
  17.6 1.8 %shard_map.56.refs_2_.refs_5_ = f32[768,128]{1,0:T(8,128)S(1)} custom-call(bf16[384,4096]{1,0:T(8,128)(2,1)S(1)} %copy-done, bf16[384,4096]{1,0:T(8,128)(2,1)S(1)} %collective-permute-done.refs_3_.refs_1_, bf16[4096,128]{1,0:T(8,128)(2,1)S(1)} %copy-done.1, bf16[4096,128]{1,0:T(8,128)(2,1)S(1)} %copy-done.1), custom_call_target="tpu_custom_call" | custom-call | bytes 1024 | tf_op jit(solution)/shard_map/pallas_call | solution.py:54
  19.4 0.0 collective-permute-done.2.refs_1_.refs_2_
  19.4 8.4 %collective-permute-done.1.refs_0_.refs_3_ = bf16[4096,128]{1,0:T(8,128)(2,1)S(1)} collective-permute-done((bf16[4096,128]{1,0:T(8,128)(2,1)}, bf16[4096,128]{1,0:T(8,128)(2,1)S(1)}, u32[]{:S(2)}, u32[]{:S(2)}) %collective-permute-start.1) | collective-permute-done | bytes 1048608 | tf_op jit(solution)/shard_map/ppermute | solution.py:44
  27.8 0.7 %collective-permute-start.7 = (bf16[2304,128]{1,0:T(8,128)(2,1)S(1)}, bf16[2304,128]{1,0:T(8,128)(2,1)S(1)}, u32[]{:S(2)}, u32[]{:S(2)}) collective-permute-start(bf16[2304,128]{1,0:T(8,128)(2,1)S(1)} %get-tuple-element.30), channel_id=1, source_target_pairs={{0,8},{8,0},{16,24},{24,16},{1,9},{9,1},{17,25},{25,17},{2,10},{10... | collective-permute-start | bytes 1769480 | tf_op jit(solution)/shard_map/ppermute | solution.py:34
  28.5 2.1 %collective-permute-done.5.refs_1_.refs_4_ = bf16[4096,128]{1,0:T(8,128)(2,1)S(1)} collective-permute-done((bf16[4096,128]{1,0:T(8,128)(2,1)}, bf16[4096,128]{1,0:T(8,128)(2,1)S(1)}, u32[]{:S(2)}, u32[]{:S(2)}) %collective-permute-start.5) | collective-permute-done | bytes 1048608 | tf_op jit(solution)/shard_map/ppermute | solution.py:34
  30.6 0.0 collective-permute-done.4.refs_0_.refs_5_
  30.6 0.4 shard_map.58
  31.0 4.0 %collective-permute-start.8 = (bf16[2176,128]{1,0:T(8,128)(2,1)S(1)}, bf16[2176,128]{1,0:T(8,128)(2,1)S(1)}, u32[]{:S(2)}, u32[]{:S(2)}) collective-permute-start(bf16[2176,128]{1,0:T(8,128)(2,1)S(1)} %get-tuple-element.31), channel_id=1, source_target_pairs={{4,12},{12,4},{20,28},{28,20},{5,13},{13,5},{21,29},{29,21},{6,14}... | collective-permute-start | bytes 1671176 | tf_op jit(solution)/shard_map/ppermute | solution.py:34
  35.0 1.3 %collective-permute-start.6 = (bf16[1920,128]{1,0:T(8,128)(2,1)S(1)}, bf16[1920,128]{1,0:T(8,128)(2,1)S(1)}, u32[]{:S(2)}, u32[]{:S(2)}) collective-permute-start(bf16[1920,128]{1,0:T(8,128)(2,1)S(1)} %get-tuple-element.29), channel_id=1, source_target_pairs={{0,1},{1,0},{2,3},{3,2},{4,20},{5,21},{6,22},{7,23},{8,9},{9,8},{1... | collective-permute-start | bytes 1474568 | tf_op jit(solution)/shard_map/ppermute | solution.py:44
  36.4 0.7 %collective-permute-start.3 = (bf16[1792,128]{1,0:T(8,128)(2,1)S(1)}, bf16[1792,128]{1,0:T(8,128)(2,1)S(1)}, u32[]{:S(2)}, u32[]{:S(2)}) collective-permute-start(bf16[1792,128]{1,0:T(8,128)(2,1)S(1)} %get-tuple-element.28.refs_2_), channel_id=1, source_target_pairs={{0,16},{8,24},{16,0},{24,8},{1,17},{9,25},{17,1},{25,9},{2,18},{10... | collective-permute-start | bytes 1376264 | tf_op jit(solution)/shard_map/ppermute | solution.py:34
  37.0 1.8 %shard_map.59 = (f32[768,128]{1,0:T(8,128)S(1)}, f32[768,128]{1,0:T(8,128)S(1)}) custom-call(bf16[384,4096]{1,0:T(8,128)(2,1)S(1)} %copy-done, bf16[384,4096]{1,0:T(8,128)(2,1)S(1)} %collective-permute-done.refs_3_.refs_1_, bf16[4096,128]{1,0:T(8,128)(2,1)S(1)} %collective-permute-done.2.refs_1_.refs_2_, ...), custom_call_target="tpu_custom_call" | custom-call | bytes 1024 | tf_op jit(solution)/shard_map/pallas_call | solution.py:54
  38.9 0.0 collective-permute-done.7.refs_2_
  38.9 3.4 %collective-permute-done.8.refs_3_ = bf16[2176,128]{1,0:T(8,128)(2,1)S(1)} collective-permute-done((bf16[2176,128]{1,0:T(8,128)(2,1)S(1)}, bf16[2176,128]{1,0:T(8,128)(2,1)S(1)}, u32[]{:S(2)}, u32[]{:S(2)}) %collective-permute-start.8) | collective-permute-done | bytes 557088 | tf_op jit(solution)/shard_map/ppermute | solution.py:34
  42.3 1.0 %shard_map.60.refs_4_ = f32[768,128]{1,0:T(8,128)S(1)} custom-call(bf16[384,4096]{1,0:T(8,128)(2,1)S(1)} %copy-done, bf16[384,4096]{1,0:T(8,128)(2,1)S(1)} %collective-permute-done.refs_3_.refs_1_, bf16[2304,128]{1,0:T(8,128)(2,1)S(1)} %collective-permute-done.7.refs_2_, bf16[2176,128]{1,0:T(8,128)(2,1)S(1)} %collective-permute-done.8.refs_3_, ...), custom_call_target="tpu_custom_call" | custom-call | bytes 1024 | tf_op jit(solution)/shard_map/pallas_call | solution.py:54
  43.3 0.0 collective-permute-done.3.refs_2_
  43.3 0.0 collective-permute-done.6.refs_3_
  43.3 1.1 %shard_map.61 = (f32[768,128]{1,0:T(8,128)S(1)}, bf16[768,128]{1,0:T(8,128)(2,1)S(1)}, bf16[768,128]{1,0:T(8,128)(2,1)S(1)}, bf16[768,128]{1,0:T(8,128)(2,1)S(1)}) custom-call(bf16[384,4096]{1,0:T(8,128)(2,1)S(1)} %copy-done, bf16[384,4096]{1,0:T(8,128)(2,1)S(1)} %collective-permute-done.refs_3_.refs_1_, ...), custom_call_target="tpu_custom_call" | custom-call | bytes 1024 | tf_op jit(solution)/shard_map/pallas_call | solution.py:54
  44.4 3.4 %collective-permute-start.9 = (bf16[768,128]{1,0:T(8,128)(2,1)S(1)}, bf16[768,128]{1,0:T(8,128)(2,1)S(1)}, u32[]{:S(2)}, u32[]{:S(2)}) collective-permute-start(bf16[768,128]{1,0:T(8,128)(2,1)S(1)} %get-tuple-element.35), channel_id=1, source_target_pairs={{0,3},{1,2},{2,1},{3,0},{4,7},{5,6},{6,5},{7,4},{8,11},{9,10},{10,... | collective-permute-start | bytes 589832 | tf_op jit(solution)/shard_map/ppermute | solution.py:34
  47.8 0.0 collective-permute-start.10
  47.8 0.4 collective-permute-start.11
  48.1 2.9 %collective-permute-done.9.refs_1_ = bf16[768,128]{1,0:T(8,128)(2,1)S(1)} collective-permute-done((bf16[768,128]{1,0:T(8,128)(2,1)S(1)}, bf16[768,128]{1,0:T(8,128)(2,1)S(1)}, u32[]{:S(2)}, u32[]{:S(2)}) %collective-permute-start.9) | collective-permute-done | bytes 196640 | tf_op jit(solution)/shard_map/ppermute | solution.py:34
  51.0 6.1 %collective-permute-done.10.refs_2_ = bf16[768,128]{1,0:T(8,128)(2,1)S(1)} collective-permute-done((bf16[768,128]{1,0:T(8,128)(2,1)S(1)}, bf16[768,128]{1,0:T(8,128)(2,1)S(1)}, u32[]{:S(2)}, u32[]{:S(2)}) %collective-permute-start.10) | collective-permute-done | bytes 196640 | tf_op jit(solution)/shard_map/ppermute | solution.py:34
  57.1 0.0 collective-permute-done.11.refs_3_
  57.1 0.1 shard_map.62
  57.2 0.1 collective-permute-start.12
  57.3 1.4 %collective-permute-done.12.refs_1_ = f32[384,128]{1,0:T(8,128)S(1)} collective-permute-done((f32[384,128]{1,0:T(8,128)S(1)}, f32[384,128]{1,0:T(8,128)S(1)}, u32[]{:S(2)}, u32[]{:S(2)}) %collective-permute-start.12) | collective-permute-done | bytes 196640 | tf_op jit(solution)/shard_map/ppermute | solution.py:34
  58.7 0.3 shard_map.63
  59.0 1.3 %collective-permute-start.14 = (bf16[128,384]{1,0:T(8,128)(2,1)S(1)}, bf16[128,384]{1,0:T(8,128)(2,1)S(1)}, u32[]{:S(2)}, u32[]{:S(2)}) collective-permute-start(bf16[128,384]{1,0:T(8,128)(2,1)S(1)} %get-tuple-element.46), channel_id=1, source_target_pairs={{0,4},{4,8},{8,12},{12,16},{16,20},{20,24},{24,28},{28,0},{1,5},{5... | collective-permute-start | bytes 294920 | tf_op jit(solution)/shard_map/ppermute | solution.py:226
  60.3 0.0 collective-permute-start.13
  60.3 0.4 shard_map.64
  60.7 3.5 %collective-permute-done.13.refs_4_ = bf16[128,256]{1,0:T(8,128)(2,1)S(1)} collective-permute-done((bf16[128,256]{1,0:T(8,128)(2,1)S(1)}, bf16[128,256]{1,0:T(8,128)(2,1)S(1)}, u32[]{:S(2)}, u32[]{:S(2)}) %collective-permute-start.13) | collective-permute-done | bytes 65568 | tf_op jit(solution)/shard_map/ppermute | solution.py:226
  64.2 0.0 collective-permute-done.14.refs_5_
  64.2 1.2 %shard_map.65 = f32[384,256]{1,0:T(8,128)} custom-call(f32[384,256]{1,0:T(8,128)S(1)} %get-tuple-element.42.refs_0_, bf16[128,512]{1,0:T(8,128)(2,1)S(1)} %get-tuple-element.43.refs_1_, bf16[512,512]{1,0:T(8,128)(2,1)S(1)} %get-tuple-element.26.refs_2_.refs_1_, bf16[384,128]{1,0:T(8,128)(2,1)S(1)} %get-tuple-element.44.refs_3_, ...), custom_call_target="tpu_custom_call" | custom-call | bytes 1024 | tf_op jit(solution)/shard_map/pallas_call | solution.py:54
  (1 shorter events, 0.0 us)
Async XLA Ops:
  0.0 16.4 %copy-start = (bf16[384,4096]{1,0:T(8,128)(2,1)S(1)}, bf16[384,4096]{1,0:T(8,128)(2,1)}, u32[]{:S(2)}) copy-start(bf16[384,4096]{1,0:T(8,128)(2,1)} %refs_0_.9) | copy-start | bytes 9437188
  0.0 5.9 %collective-permute-start = (bf16[384,4096]{1,0:T(8,128)(2,1)}, bf16[384,4096]{1,0:T(8,128)(2,1)S(1)}, u32[]{:S(2)}, u32[]{:S(2)}) collective-permute-start(bf16[384,4096]{1,0:T(8,128)(2,1)} %refs_0_.9), channel_id=1, source_target_pairs={{0,4},{4,0},{8,12},{12,8},{16,20},{20,16},{24,28},{28,24},{1,5},{5... | collective-permute-start | bytes 9437192 | tf_op jit(solution)/shard_map/ppermute | solution.py:34
  0.1 19.3 %collective-permute-start.2 = (bf16[4096,128]{1,0:T(8,128)(2,1)}, bf16[4096,128]{1,0:T(8,128)(2,1)S(1)}, u32[]{:S(2)}, u32[]{:S(2)}) collective-permute-start(bf16[4096,128]{1,0:T(8,128)(2,1)} %refs_3_), channel_id=1, source_target_pairs={{0,8},{1,9},{2,10},{3,11},{4,5},{5,4},{6,7},{7,6},{8,0},{9,1},{10,... | collective-permute-start | bytes 3145736 | tf_op jit(solution)/shard_map/ppermute | solution.py:44
  2.8 25.0 %collective-permute-start.1 = (bf16[4096,128]{1,0:T(8,128)(2,1)}, bf16[4096,128]{1,0:T(8,128)(2,1)S(1)}, u32[]{:S(2)}, u32[]{:S(2)}) collective-permute-start(bf16[4096,128]{1,0:T(8,128)(2,1)} %refs_3_), channel_id=1, source_target_pairs={{0,16},{1,17},{2,18},{3,19},{4,5},{5,4},{6,7},{7,6},{8,24},{9,25},... | collective-permute-start | bytes 3145736 | tf_op jit(solution)/shard_map/ppermute | solution.py:44
  5.9 1.0 %copy-start.2 = (bf16[1,512,512]{2,1,0:T(8,128)(2,1)S(1)}, bf16[1,512,512]{2,1,0:T(8,128)(2,1)}, u32[]{:S(2)}) copy-start(bf16[1,512,512]{2,1,0:T(8,128)(2,1)} %refs_0_.5) | copy-start | bytes 1572868
  6.9 0.7 %copy-start.3 = (s32[1,512]{1,0:T(1,128)S(1)}, s32[1,512]{1,0:T(1,128)}, u32[]{:S(2)}) copy-start(s32[1,512]{1,0:T(1,128)} %refs_1_.1) | copy-start | bytes 6148
  7.6 0.7 %copy-start.4 = (s32[128]{0:T(128)S(1)}, s32[128]{0:T(128)}, u32[]{:S(2)}) copy-start(s32[128]{0:T(128)} %param.9) | copy-start | bytes 1540
  9.0 21.7 %collective-permute-start.5 = (bf16[4096,128]{1,0:T(8,128)(2,1)}, bf16[4096,128]{1,0:T(8,128)(2,1)S(1)}, u32[]{:S(2)}, u32[]{:S(2)}) collective-permute-start(bf16[4096,128]{1,0:T(8,128)(2,1)} %refs_3_), channel_id=1, source_target_pairs={{4,12},{12,4},{20,28},{28,20},{5,13},{13,5},{21,29},{29,21},{6,14}... | collective-permute-start | bytes 3145736 | tf_op jit(solution)/shard_map/ppermute | solution.py:34
  13.2 17.4 %collective-permute-start.4 = (bf16[4096,128]{1,0:T(8,128)(2,1)}, bf16[4096,128]{1,0:T(8,128)(2,1)S(1)}, u32[]{:S(2)}, u32[]{:S(2)}) collective-permute-start(bf16[4096,128]{1,0:T(8,128)(2,1)} %refs_3_), channel_id=1, source_target_pairs={{4,20},{12,28},{20,4},{28,12},{5,21},{13,29},{21,5},{29,13},{6,22}... | collective-permute-start | bytes 3145736 | tf_op jit(solution)/shard_map/ppermute | solution.py:34
  16.4 1.2 %copy-start.1 = (bf16[4096,128]{1,0:T(8,128)(2,1)S(1)}, bf16[4096,128]{1,0:T(8,128)(2,1)}, u32[]{:S(2)}) copy-start(bf16[4096,128]{1,0:T(8,128)(2,1)} %refs_3_) | copy-start | bytes 3145732
  27.8 11.1 %collective-permute-start.7 = (bf16[2304,128]{1,0:T(8,128)(2,1)S(1)}, bf16[2304,128]{1,0:T(8,128)(2,1)S(1)}, u32[]{:S(2)}, u32[]{:S(2)}) collective-permute-start(bf16[2304,128]{1,0:T(8,128)(2,1)S(1)} %get-tuple-element.30), channel_id=1, source_target_pairs={{0,8},{8,0},{16,24},{24,16},{1,9},{9,1},{17,25},{25,17},{2,10},{10... | collective-permute-start | bytes 1769480 | tf_op jit(solution)/shard_map/ppermute | solution.py:34
  31.0 11.2 %collective-permute-start.8 = (bf16[2176,128]{1,0:T(8,128)(2,1)S(1)}, bf16[2176,128]{1,0:T(8,128)(2,1)S(1)}, u32[]{:S(2)}, u32[]{:S(2)}) collective-permute-start(bf16[2176,128]{1,0:T(8,128)(2,1)S(1)} %get-tuple-element.31), channel_id=1, source_target_pairs={{4,12},{12,4},{20,28},{28,20},{5,13},{13,5},{21,29},{29,21},{6,14}... | collective-permute-start | bytes 1671176 | tf_op jit(solution)/shard_map/ppermute | solution.py:34
  35.0 8.2 %collective-permute-start.6 = (bf16[1920,128]{1,0:T(8,128)(2,1)S(1)}, bf16[1920,128]{1,0:T(8,128)(2,1)S(1)}, u32[]{:S(2)}, u32[]{:S(2)}) collective-permute-start(bf16[1920,128]{1,0:T(8,128)(2,1)S(1)} %get-tuple-element.29), channel_id=1, source_target_pairs={{0,1},{1,0},{2,3},{3,2},{4,20},{5,21},{6,22},{7,23},{8,9},{9,8},{1... | collective-permute-start | bytes 1474568 | tf_op jit(solution)/shard_map/ppermute | solution.py:44
  36.4 6.9 %collective-permute-start.3 = (bf16[1792,128]{1,0:T(8,128)(2,1)S(1)}, bf16[1792,128]{1,0:T(8,128)(2,1)S(1)}, u32[]{:S(2)}, u32[]{:S(2)}) collective-permute-start(bf16[1792,128]{1,0:T(8,128)(2,1)S(1)} %get-tuple-element.28.refs_2_), channel_id=1, source_target_pairs={{0,16},{8,24},{16,0},{24,8},{1,17},{9,25},{17,1},{25,9},{2,18},{10... | collective-permute-start | bytes 1376264 | tf_op jit(solution)/shard_map/ppermute | solution.py:34
  44.4 6.6 %collective-permute-start.9 = (bf16[768,128]{1,0:T(8,128)(2,1)S(1)}, bf16[768,128]{1,0:T(8,128)(2,1)S(1)}, u32[]{:S(2)}, u32[]{:S(2)}) collective-permute-start(bf16[768,128]{1,0:T(8,128)(2,1)S(1)} %get-tuple-element.35), channel_id=1, source_target_pairs={{0,3},{1,2},{2,1},{3,0},{4,7},{5,6},{6,5},{7,4},{8,11},{9,10},{10,... | collective-permute-start | bytes 589832 | tf_op jit(solution)/shard_map/ppermute | solution.py:34
  47.8 9.3 %collective-permute-start.10 = (bf16[768,128]{1,0:T(8,128)(2,1)S(1)}, bf16[768,128]{1,0:T(8,128)(2,1)S(1)}, u32[]{:S(2)}, u32[]{:S(2)}) collective-permute-start(bf16[768,128]{1,0:T(8,128)(2,1)S(1)} %get-tuple-element.36), channel_id=1, source_target_pairs={{0,2},{1,3},{2,0},{3,1},{4,6},{5,7},{6,4},{7,5},{8,10},{9,11},{10,... | collective-permute-start | bytes 589832 | tf_op jit(solution)/shard_map/ppermute | solution.py:34
  47.8 9.3 %collective-permute-start.11 = (bf16[768,128]{1,0:T(8,128)(2,1)S(1)}, bf16[768,128]{1,0:T(8,128)(2,1)S(1)}, u32[]{:S(2)}, u32[]{:S(2)}) collective-permute-start(bf16[768,128]{1,0:T(8,128)(2,1)S(1)} %get-tuple-element.37), channel_id=1, source_target_pairs={{0,1},{1,0},{2,3},{3,2},{4,5},{5,4},{6,7},{7,6},{8,9},{9,8},{10,11... | collective-permute-start | bytes 589832 | tf_op jit(solution)/shard_map/ppermute | solution.py:34
  57.2 1.5 %collective-permute-start.12 = (f32[384,128]{1,0:T(8,128)S(1)}, f32[384,128]{1,0:T(8,128)S(1)}, u32[]{:S(2)}, u32[]{:S(2)}) collective-permute-start(f32[384,128]{1,0:T(8,128)S(1)} %get-tuple-element.39), channel_id=1, source_target_pairs={{0,4},{4,0},{8,12},{12,8},{16,20},{20,16},{24,28},{28,24},{1,5},{5... | collective-permute-start | bytes 589832 | tf_op jit(solution)/shard_map/ppermute | solution.py:34
  59.0 5.2 %collective-permute-start.14 = (bf16[128,384]{1,0:T(8,128)(2,1)S(1)}, bf16[128,384]{1,0:T(8,128)(2,1)S(1)}, u32[]{:S(2)}, u32[]{:S(2)}) collective-permute-start(bf16[128,384]{1,0:T(8,128)(2,1)S(1)} %get-tuple-element.46), channel_id=1, source_target_pairs={{0,4},{4,8},{8,12},{12,16},{16,20},{20,24},{24,28},{28,0},{1,5},{5... | collective-permute-start | bytes 294920 | tf_op jit(solution)/shard_map/ppermute | solution.py:226
  60.3 3.9 %collective-permute-start.13 = (bf16[128,256]{1,0:T(8,128)(2,1)S(1)}, bf16[128,256]{1,0:T(8,128)(2,1)S(1)}, u32[]{:S(2)}, u32[]{:S(2)}) collective-permute-start(bf16[128,256]{1,0:T(8,128)(2,1)S(1)} %get-tuple-element.45), channel_id=1, source_target_pairs={{0,28},{4,0},{8,4},{12,8},{16,12},{20,16},{24,20},{28,24},{1,29},{... | collective-permute-start | bytes 196616 | tf_op jit(solution)/shard_map/ppermute | solution.py:226

commit v26 on v25

--- a/solution.py
+++ b/solution.py
@@ -164,7 +164,7 @@
     own = call(own_kernel, block, (wavefunctions, theirs, rotation), after=(later,))[0]
     received += [exchanged(later, "domain", NEAR, CORE), exchanged(later, "domain", FAR, CORE)]
     passed, previous = [], [own]
-    for one, share in ((0, 18), (CORE, 17)):
+    for one, share in ((0, 17), (CORE, 17)):
         cut = states * share // 32
         outs = [shape(count, width, dtype=BF16) for count in (cut, states - cut)]
         pair = received[2 * one : 2 * one + 2][::-1]

time: 65.7 us -> 65.4 us (level)
    ppermute x10, waiting for transfers between devices: 18.9 us -> 19.6 us  [exchanged(): lax.ppermute(value, axis, [(source, source ^ mask) for source in sources...]
  transfers between devices with their start and end apart: 15 -> 15, of which waited for: 8 -> 10; matrix products, arithmetic and copies ran while one was open for 0% -> 0% of each run, Pallas kernels for 9% -> 9%
where the time goes in v26:
time: 65.4 us; the launch traced here: 65.1 us
  waiting for transfers between devices  31 us (47%)
  starting transfers between devices  21.5 us (33%)
  Pallas kernels  8.82 us (13%)
  local copies, waits for them, and re-layouts  3.6 us (6%)
    ppermute x10, waiting for transfers between devices, exchanged(): lax.ppermute(value, axis, [(source, source ^ mask) for source in sources...  19.6 us
    ppermute x10, starting transfers between devices, exchanged(): lax.ppermute(value, axis, [(source, source ^ mask) for source in sources...  16.3 us
    pallas_call x11, Pallas kernels, call(): pl.pallas_call(body, out_shape=outs, in_specs=[pl.BlockSpec(memory_space=...  8.82 us
    ppermute x3, waiting for transfers between devices, paired(): return lax.ppermute(value, ('domain', 'band'), pairs)  7.83 us
    ppermute x3, starting transfers between devices, paired(): return lax.ppermute(value, ('domain', 'band'), pairs)  4.08 us
    unnamed x10, local copies, waits for them, and re-layouts  3.6 us
    ppermute x2, waiting for transfers between devices, rotated(): lax.ppermute(value, axis, [(source, (source + steps) % count) for source...  3.55 us
  transfers between devices with their start and end apart: 15, of which 10 were waited for; matrix products, arithmetic and copies ran while one was open for 0% of the time, Pallas kernels for 9%

profile of v26, /device:TPU:1, one launch (start us, length us, event | category | flops | bytes accessed | tf_op | source)
XLA Modules:
  0.0 65.1 jit_solution(10470674696761766368)
XLA Ops:
  0.0 0.0 copy-start
  0.0 0.1 collective-permute-start
  0.1 2.7 %collective-permute-start.2 = (bf16[4096,128]{1,0:T(8,128)(2,1)}, bf16[4096,128]{1,0:T(8,128)(2,1)S(1)}, u32[]{:S(2)}, u32[]{:S(2)}) collective-permute-start(bf16[4096,128]{1,0:T(8,128)(2,1)} %refs_3_), channel_id=1, source_target_pairs={{0,8},{1,9},{2,10},{3,11},{4,5},{5,4},{6,7},{7,6},{8,0},{9,1},{10,... | collective-permute-start | bytes 3145736 | tf_op jit(solution)/shard_map/ppermute | solution.py:44
  2.8 0.0 collective-permute-start.1
  2.8 3.0 %collective-permute-done.refs_3_.refs_1_ = bf16[384,4096]{1,0:T(8,128)(2,1)S(1)} collective-permute-done((bf16[384,4096]{1,0:T(8,128)(2,1)}, bf16[384,4096]{1,0:T(8,128)(2,1)S(1)}, u32[]{:S(2)}, u32[]{:S(2)}) %collective-permute-start) | collective-permute-done | bytes 3145760 | tf_op jit(solution)/shard_map/ppermute | solution.py:34
  5.9 0.0 copy-start.2
  5.9 1.0 %copy-done.2 = bf16[1,512,512]{2,1,0:T(8,128)(2,1)S(1)} copy-done((bf16[1,512,512]{2,1,0:T(8,128)(2,1)S(1)}, bf16[1,512,512]{2,1,0:T(8,128)(2,1)}, u32[]{:S(2)}) %copy-start.2) | copy-done | bytes 524312
  6.9 0.0 copy-start.3
  6.9 0.7 %copy-done.3 = s32[1,512]{1,0:T(1,128)S(1)} copy-done((s32[1,512]{1,0:T(1,128)S(1)}, s32[1,512]{1,0:T(1,128)}, u32[]{:S(2)}) %copy-start.3) | copy-done | bytes 2072
  7.6 0.0 copy-start.4
  7.6 0.7 %copy-done.4 = s32[128]{0:T(128)S(1)} copy-done((s32[128]{0:T(128)S(1)}, s32[128]{0:T(128)}, u32[]{:S(2)}) %copy-start.4) | copy-done | bytes 536
  8.3 0.7 %shard_map.55 = (bf16[512,512]{1,0:T(8,128)(2,1)S(1)}, bf16[128,384]{1,0:T(8,128)(2,1)S(1)}, bf16[384,128]{1,0:T(8,128)(2,1)S(1)}) custom-call(bf16[1,512,512]{2,1,0:T(8,128)(2,1)S(1)} %copy-done.2, s32[1,512]{1,0:T(1,128)S(1)} %copy-done.3, s32[1,128]{1,0:T(1,128)S(1)} %bitcast.1, bf16[384,4096]{1,0:T(8,128)(2,1)S(1)} %collective-permute-done.refs_3_.refs_1_), custom_call_target="tpu_custom_call" | custom-call | bytes 1024 | tf_op jit(solution)/shard_map/pallas_call | solution.py:54
  9.0 4.3 %collective-permute-start.5 = (bf16[4096,128]{1,0:T(8,128)(2,1)}, bf16[4096,128]{1,0:T(8,128)(2,1)S(1)}, u32[]{:S(2)}, u32[]{:S(2)}) collective-permute-start(bf16[4096,128]{1,0:T(8,128)(2,1)} %refs_3_), channel_id=1, source_target_pairs={{4,12},{12,4},{20,28},{28,20},{5,13},{13,5},{21,29},{29,21},{6,14}... | collective-permute-start | bytes 3145736 | tf_op jit(solution)/shard_map/ppermute | solution.py:34
  13.2 3.1 %collective-permute-start.4 = (bf16[4096,128]{1,0:T(8,128)(2,1)}, bf16[4096,128]{1,0:T(8,128)(2,1)S(1)}, u32[]{:S(2)}, u32[]{:S(2)}) collective-permute-start(bf16[4096,128]{1,0:T(8,128)(2,1)} %refs_3_), channel_id=1, source_target_pairs={{4,20},{12,28},{20,4},{28,12},{5,21},{13,29},{21,5},{29,13},{6,22}... | collective-permute-start | bytes 3145736 | tf_op jit(solution)/shard_map/ppermute | solution.py:34
  16.4 0.0 copy-done
  16.4 0.0 copy-start.1
  16.4 1.2 %copy-done.1 = bf16[4096,128]{1,0:T(8,128)(2,1)S(1)} copy-done((bf16[4096,128]{1,0:T(8,128)(2,1)S(1)}, bf16[4096,128]{1,0:T(8,128)(2,1)}, u32[]{:S(2)}) %copy-start.1) | copy-done | bytes 1048600
  17.6 1.8 %shard_map.56.refs_2_.refs_5_ = f32[768,128]{1,0:T(8,128)S(1)} custom-call(bf16[384,4096]{1,0:T(8,128)(2,1)S(1)} %copy-done, bf16[384,4096]{1,0:T(8,128)(2,1)S(1)} %collective-permute-done.refs_3_.refs_1_, bf16[4096,128]{1,0:T(8,128)(2,1)S(1)} %copy-done.1, bf16[4096,128]{1,0:T(8,128)(2,1)S(1)} %copy-done.1), custom_call_target="tpu_custom_call" | custom-call | bytes 1024 | tf_op jit(solution)/shard_map/pallas_call | solution.py:54
  19.4 0.0 collective-permute-done.2.refs_1_.refs_2_
  19.4 7.3 %collective-permute-done.1.refs_0_.refs_3_ = bf16[4096,128]{1,0:T(8,128)(2,1)S(1)} collective-permute-done((bf16[4096,128]{1,0:T(8,128)(2,1)}, bf16[4096,128]{1,0:T(8,128)(2,1)S(1)}, u32[]{:S(2)}, u32[]{:S(2)}) %collective-permute-start.1) | collective-permute-done | bytes 1048608 | tf_op jit(solution)/shard_map/ppermute | solution.py:44
  26.8 0.7 %collective-permute-start.7 = (bf16[2176,128]{1,0:T(8,128)(2,1)S(1)}, bf16[2176,128]{1,0:T(8,128)(2,1)S(1)}, u32[]{:S(2)}, u32[]{:S(2)}) collective-permute-start(bf16[2176,128]{1,0:T(8,128)(2,1)S(1)} %get-tuple-element.30), channel_id=1, source_target_pairs={{0,8},{8,0},{16,24},{24,16},{1,9},{9,1},{17,25},{25,17},{2,10},{10... | collective-permute-start | bytes 1671176 | tf_op jit(solution)/shard_map/ppermute | solution.py:34
  27.5 3.2 %collective-permute-done.5.refs_1_.refs_4_ = bf16[4096,128]{1,0:T(8,128)(2,1)S(1)} collective-permute-done((bf16[4096,128]{1,0:T(8,128)(2,1)}, bf16[4096,128]{1,0:T(8,128)(2,1)S(1)}, u32[]{:S(2)}, u32[]{:S(2)}) %collective-permute-start.5) | collective-permute-done | bytes 1048608 | tf_op jit(solution)/shard_map/ppermute | solution.py:34
  30.6 0.4 collective-permute-done.4.refs_0_.refs_5_
  31.0 0.4 shard_map.58
  31.5 3.6 %collective-permute-start.8 = (bf16[2176,128]{1,0:T(8,128)(2,1)S(1)}, bf16[2176,128]{1,0:T(8,128)(2,1)S(1)}, u32[]{:S(2)}, u32[]{:S(2)}) collective-permute-start(bf16[2176,128]{1,0:T(8,128)(2,1)S(1)} %get-tuple-element.31), channel_id=1, source_target_pairs={{4,12},{12,4},{20,28},{28,20},{5,13},{13,5},{21,29},{29,21},{6,14}... | collective-permute-start | bytes 1671176 | tf_op jit(solution)/shard_map/ppermute | solution.py:34
  35.0 0.7 %collective-permute-start.3 = (bf16[1920,128]{1,0:T(8,128)(2,1)S(1)}, bf16[1920,128]{1,0:T(8,128)(2,1)S(1)}, u32[]{:S(2)}, u32[]{:S(2)}) collective-permute-start(bf16[1920,128]{1,0:T(8,128)(2,1)S(1)} %get-tuple-element.28.refs_2_), channel_id=1, source_target_pairs={{0,16},{8,24},{16,0},{24,8},{1,17},{9,25},{17,1},{25,9},{2,18},{10... | collective-permute-start | bytes 1474568 | tf_op jit(solution)/shard_map/ppermute | solution.py:34
  35.7 1.3 %collective-permute-start.6 = (bf16[1920,128]{1,0:T(8,128)(2,1)S(1)}, bf16[1920,128]{1,0:T(8,128)(2,1)S(1)}, u32[]{:S(2)}, u32[]{:S(2)}) collective-permute-start(bf16[1920,128]{1,0:T(8,128)(2,1)S(1)} %get-tuple-element.29), channel_id=1, source_target_pairs={{0,1},{1,0},{2,3},{3,2},{4,20},{5,21},{6,22},{7,23},{8,9},{9,8},{1... | collective-permute-start | bytes 1474568 | tf_op jit(solution)/shard_map/ppermute | solution.py:44
  37.1 1.8 %shard_map.59 = (f32[768,128]{1,0:T(8,128)S(1)}, f32[768,128]{1,0:T(8,128)S(1)}) custom-call(bf16[384,4096]{1,0:T(8,128)(2,1)S(1)} %copy-done, bf16[384,4096]{1,0:T(8,128)(2,1)S(1)} %collective-permute-done.refs_3_.refs_1_, bf16[4096,128]{1,0:T(8,128)(2,1)S(1)} %collective-permute-done.2.refs_1_.refs_2_, ...), custom_call_target="tpu_custom_call" | custom-call | bytes 1024 | tf_op jit(solution)/shard_map/pallas_call | solution.py:54
  38.9 0.0 collective-permute-done.7.refs_2_
  38.9 3.4 %collective-permute-done.8.refs_3_ = bf16[2176,128]{1,0:T(8,128)(2,1)S(1)} collective-permute-done((bf16[2176,128]{1,0:T(8,128)(2,1)S(1)}, bf16[2176,128]{1,0:T(8,128)(2,1)S(1)}, u32[]{:S(2)}, u32[]{:S(2)}) %collective-permute-start.8) | collective-permute-done | bytes 557088 | tf_op jit(solution)/shard_map/ppermute | solution.py:34
  42.3 1.0 %shard_map.60.refs_4_ = f32[768,128]{1,0:T(8,128)S(1)} custom-call(bf16[384,4096]{1,0:T(8,128)(2,1)S(1)} %copy-done, bf16[384,4096]{1,0:T(8,128)(2,1)S(1)} %collective-permute-done.refs_3_.refs_1_, bf16[2176,128]{1,0:T(8,128)(2,1)S(1)} %collective-permute-done.7.refs_2_, bf16[2176,128]{1,0:T(8,128)(2,1)S(1)} %collective-permute-done.8.refs_3_, ...), custom_call_target="tpu_custom_call" | custom-call | bytes 1024 | tf_op jit(solution)/shard_map/pallas_call | solution.py:54
  43.3 0.0 collective-permute-done.3.refs_2_
  43.3 0.5 collective-permute-done.6.refs_3_
  43.8 1.1 %shard_map.61 = (f32[768,128]{1,0:T(8,128)S(1)}, bf16[768,128]{1,0:T(8,128)(2,1)S(1)}, bf16[768,128]{1,0:T(8,128)(2,1)S(1)}, bf16[768,128]{1,0:T(8,128)(2,1)S(1)}) custom-call(bf16[384,4096]{1,0:T(8,128)(2,1)S(1)} %copy-done, bf16[384,4096]{1,0:T(8,128)(2,1)S(1)} %collective-permute-done.refs_3_.refs_1_, ...), custom_call_target="tpu_custom_call" | custom-call | bytes 1024 | tf_op jit(solution)/shard_map/pallas_call | solution.py:54
  44.9 3.4 %collective-permute-start.9 = (bf16[768,128]{1,0:T(8,128)(2,1)S(1)}, bf16[768,128]{1,0:T(8,128)(2,1)S(1)}, u32[]{:S(2)}, u32[]{:S(2)}) collective-permute-start(bf16[768,128]{1,0:T(8,128)(2,1)S(1)} %get-tuple-element.35), channel_id=1, source_target_pairs={{0,3},{1,2},{2,1},{3,0},{4,7},{5,6},{6,5},{7,4},{8,11},{9,10},{10,... | collective-permute-start | bytes 589832 | tf_op jit(solution)/shard_map/ppermute | solution.py:34
  48.2 0.0 collective-permute-start.10
  48.2 0.4 collective-permute-start.11
  48.6 2.9 %collective-permute-done.9.refs_1_ = bf16[768,128]{1,0:T(8,128)(2,1)S(1)} collective-permute-done((bf16[768,128]{1,0:T(8,128)(2,1)S(1)}, bf16[768,128]{1,0:T(8,128)(2,1)S(1)}, u32[]{:S(2)}, u32[]{:S(2)}) %collective-permute-start.9) | collective-permute-done | bytes 196640 | tf_op jit(solution)/shard_map/ppermute | solution.py:34
  51.5 5.3 %collective-permute-done.10.refs_2_ = bf16[768,128]{1,0:T(8,128)(2,1)S(1)} collective-permute-done((bf16[768,128]{1,0:T(8,128)(2,1)S(1)}, bf16[768,128]{1,0:T(8,128)(2,1)S(1)}, u32[]{:S(2)}, u32[]{:S(2)}) %collective-permute-start.10) | collective-permute-done | bytes 196640 | tf_op jit(solution)/shard_map/ppermute | solution.py:34
  56.8 0.0 collective-permute-done.11.refs_3_
  56.8 0.1 shard_map.62
  56.9 0.1 collective-permute-start.12
  57.0 1.4 %collective-permute-done.12.refs_1_ = f32[384,128]{1,0:T(8,128)S(1)} collective-permute-done((f32[384,128]{1,0:T(8,128)S(1)}, f32[384,128]{1,0:T(8,128)S(1)}, u32[]{:S(2)}, u32[]{:S(2)}) %collective-permute-start.12) | collective-permute-done | bytes 196640 | tf_op jit(solution)/shard_map/ppermute | solution.py:34
  58.4 0.3 shard_map.63
  58.7 1.2 %collective-permute-start.14 = (bf16[128,384]{1,0:T(8,128)(2,1)S(1)}, bf16[128,384]{1,0:T(8,128)(2,1)S(1)}, u32[]{:S(2)}, u32[]{:S(2)}) collective-permute-start(bf16[128,384]{1,0:T(8,128)(2,1)S(1)} %get-tuple-element.46), channel_id=1, source_target_pairs={{0,4},{4,8},{8,12},{12,16},{16,20},{20,24},{24,28},{28,0},{1,5},{5... | collective-permute-start | bytes 294920 | tf_op jit(solution)/shard_map/ppermute | solution.py:226
  59.9 0.0 collective-permute-start.13
  59.9 0.4 shard_map.64
  60.4 3.5 %collective-permute-done.13.refs_4_ = bf16[128,256]{1,0:T(8,128)(2,1)S(1)} collective-permute-done((bf16[128,256]{1,0:T(8,128)(2,1)S(1)}, bf16[128,256]{1,0:T(8,128)(2,1)S(1)}, u32[]{:S(2)}, u32[]{:S(2)}) %collective-permute-start.13) | collective-permute-done | bytes 65568 | tf_op jit(solution)/shard_map/ppermute | solution.py:226
  63.9 0.0 collective-permute-done.14.refs_5_
  63.9 1.2 %shard_map.65 = f32[384,256]{1,0:T(8,128)} custom-call(f32[384,256]{1,0:T(8,128)S(1)} %get-tuple-element.42.refs_0_, bf16[128,512]{1,0:T(8,128)(2,1)S(1)} %get-tuple-element.43.refs_1_, bf16[512,512]{1,0:T(8,128)(2,1)S(1)} %get-tuple-element.26.refs_2_.refs_1_, bf16[384,128]{1,0:T(8,128)(2,1)S(1)} %get-tuple-element.44.refs_3_, ...), custom_call_target="tpu_custom_call" | custom-call | bytes 1024 | tf_op jit(solution)/shard_map/pallas_call | solution.py:54
  (1 shorter events, 0.0 us)
Async XLA Ops:
  0.0 16.4 %copy-start = (bf16[384,4096]{1,0:T(8,128)(2,1)S(1)}, bf16[384,4096]{1,0:T(8,128)(2,1)}, u32[]{:S(2)}) copy-start(bf16[384,4096]{1,0:T(8,128)(2,1)} %refs_0_.9) | copy-start | bytes 9437188
  0.0 5.9 %collective-permute-start = (bf16[384,4096]{1,0:T(8,128)(2,1)}, bf16[384,4096]{1,0:T(8,128)(2,1)S(1)}, u32[]{:S(2)}, u32[]{:S(2)}) collective-permute-start(bf16[384,4096]{1,0:T(8,128)(2,1)} %refs_0_.9), channel_id=1, source_target_pairs={{0,4},{4,0},{8,12},{12,8},{16,20},{20,16},{24,28},{28,24},{1,5},{5... | collective-permute-start | bytes 9437192 | tf_op jit(solution)/shard_map/ppermute | solution.py:34
  0.1 19.3 %collective-permute-start.2 = (bf16[4096,128]{1,0:T(8,128)(2,1)}, bf16[4096,128]{1,0:T(8,128)(2,1)S(1)}, u32[]{:S(2)}, u32[]{:S(2)}) collective-permute-start(bf16[4096,128]{1,0:T(8,128)(2,1)} %refs_3_), channel_id=1, source_target_pairs={{0,8},{1,9},{2,10},{3,11},{4,5},{5,4},{6,7},{7,6},{8,0},{9,1},{10,... | collective-permute-start | bytes 3145736 | tf_op jit(solution)/shard_map/ppermute | solution.py:44
  2.8 23.9 %collective-permute-start.1 = (bf16[4096,128]{1,0:T(8,128)(2,1)}, bf16[4096,128]{1,0:T(8,128)(2,1)S(1)}, u32[]{:S(2)}, u32[]{:S(2)}) collective-permute-start(bf16[4096,128]{1,0:T(8,128)(2,1)} %refs_3_), channel_id=1, source_target_pairs={{0,16},{1,17},{2,18},{3,19},{4,5},{5,4},{6,7},{7,6},{8,24},{9,25},... | collective-permute-start | bytes 3145736 | tf_op jit(solution)/shard_map/ppermute | solution.py:44
  5.9 1.0 %copy-start.2 = (bf16[1,512,512]{2,1,0:T(8,128)(2,1)S(1)}, bf16[1,512,512]{2,1,0:T(8,128)(2,1)}, u32[]{:S(2)}) copy-start(bf16[1,512,512]{2,1,0:T(8,128)(2,1)} %refs_0_.5) | copy-start | bytes 1572868
  6.9 0.7 %copy-start.3 = (s32[1,512]{1,0:T(1,128)S(1)}, s32[1,512]{1,0:T(1,128)}, u32[]{:S(2)}) copy-start(s32[1,512]{1,0:T(1,128)} %refs_1_.1) | copy-start | bytes 6148
  7.6 0.7 %copy-start.4 = (s32[128]{0:T(128)S(1)}, s32[128]{0:T(128)}, u32[]{:S(2)}) copy-start(s32[128]{0:T(128)} %param.9) | copy-start | bytes 1540
  9.0 21.7 %collective-permute-start.5 = (bf16[4096,128]{1,0:T(8,128)(2,1)}, bf16[4096,128]{1,0:T(8,128)(2,1)S(1)}, u32[]{:S(2)}, u32[]{:S(2)}) collective-permute-start(bf16[4096,128]{1,0:T(8,128)(2,1)} %refs_3_), channel_id=1, source_target_pairs={{4,12},{12,4},{20,28},{28,20},{5,13},{13,5},{21,29},{29,21},{6,14}... | collective-permute-start | bytes 3145736 | tf_op jit(solution)/shard_map/ppermute | solution.py:34
  13.2 17.8 %collective-permute-start.4 = (bf16[4096,128]{1,0:T(8,128)(2,1)}, bf16[4096,128]{1,0:T(8,128)(2,1)S(1)}, u32[]{:S(2)}, u32[]{:S(2)}) collective-permute-start(bf16[4096,128]{1,0:T(8,128)(2,1)} %refs_3_), channel_id=1, source_target_pairs={{4,20},{12,28},{20,4},{28,12},{5,21},{13,29},{21,5},{29,13},{6,22}... | collective-permute-start | bytes 3145736 | tf_op jit(solution)/shard_map/ppermute | solution.py:34
  16.4 1.2 %copy-start.1 = (bf16[4096,128]{1,0:T(8,128)(2,1)S(1)}, bf16[4096,128]{1,0:T(8,128)(2,1)}, u32[]{:S(2)}) copy-start(bf16[4096,128]{1,0:T(8,128)(2,1)} %refs_3_) | copy-start | bytes 3145732
  26.8 12.1 %collective-permute-start.7 = (bf16[2176,128]{1,0:T(8,128)(2,1)S(1)}, bf16[2176,128]{1,0:T(8,128)(2,1)S(1)}, u32[]{:S(2)}, u32[]{:S(2)}) collective-permute-start(bf16[2176,128]{1,0:T(8,128)(2,1)S(1)} %get-tuple-element.30), channel_id=1, source_target_pairs={{0,8},{8,0},{16,24},{24,16},{1,9},{9,1},{17,25},{25,17},{2,10},{10... | collective-permute-start | bytes 1671176 | tf_op jit(solution)/shard_map/ppermute | solution.py:34
  31.5 10.8 %collective-permute-start.8 = (bf16[2176,128]{1,0:T(8,128)(2,1)S(1)}, bf16[2176,128]{1,0:T(8,128)(2,1)S(1)}, u32[]{:S(2)}, u32[]{:S(2)}) collective-permute-start(bf16[2176,128]{1,0:T(8,128)(2,1)S(1)} %get-tuple-element.31), channel_id=1, source_target_pairs={{4,12},{12,4},{20,28},{28,20},{5,13},{13,5},{21,29},{29,21},{6,14}... | collective-permute-start | bytes 1671176 | tf_op jit(solution)/shard_map/ppermute | solution.py:34
  35.0 8.2 %collective-permute-start.3 = (bf16[1920,128]{1,0:T(8,128)(2,1)S(1)}, bf16[1920,128]{1,0:T(8,128)(2,1)S(1)}, u32[]{:S(2)}, u32[]{:S(2)}) collective-permute-start(bf16[1920,128]{1,0:T(8,128)(2,1)S(1)} %get-tuple-element.28.refs_2_), channel_id=1, source_target_pairs={{0,16},{8,24},{16,0},{24,8},{1,17},{9,25},{17,1},{25,9},{2,18},{10... | collective-permute-start | bytes 1474568 | tf_op jit(solution)/shard_map/ppermute | solution.py:34
  35.7 8.0 %collective-permute-start.6 = (bf16[1920,128]{1,0:T(8,128)(2,1)S(1)}, bf16[1920,128]{1,0:T(8,128)(2,1)S(1)}, u32[]{:S(2)}, u32[]{:S(2)}) collective-permute-start(bf16[1920,128]{1,0:T(8,128)(2,1)S(1)} %get-tuple-element.29), channel_id=1, source_target_pairs={{0,1},{1,0},{2,3},{3,2},{4,20},{5,21},{6,22},{7,23},{8,9},{9,8},{1... | collective-permute-start | bytes 1474568 | tf_op jit(solution)/shard_map/ppermute | solution.py:44
  44.9 6.6 %collective-permute-start.9 = (bf16[768,128]{1,0:T(8,128)(2,1)S(1)}, bf16[768,128]{1,0:T(8,128)(2,1)S(1)}, u32[]{:S(2)}, u32[]{:S(2)}) collective-permute-start(bf16[768,128]{1,0:T(8,128)(2,1)S(1)} %get-tuple-element.35), channel_id=1, source_target_pairs={{0,3},{1,2},{2,1},{3,0},{4,7},{5,6},{6,5},{7,4},{8,11},{9,10},{10,... | collective-permute-start | bytes 589832 | tf_op jit(solution)/shard_map/ppermute | solution.py:34
  48.2 8.6 %collective-permute-start.10 = (bf16[768,128]{1,0:T(8,128)(2,1)S(1)}, bf16[768,128]{1,0:T(8,128)(2,1)S(1)}, u32[]{:S(2)}, u32[]{:S(2)}) collective-permute-start(bf16[768,128]{1,0:T(8,128)(2,1)S(1)} %get-tuple-element.36), channel_id=1, source_target_pairs={{0,2},{1,3},{2,0},{3,1},{4,6},{5,7},{6,4},{7,5},{8,10},{9,11},{10,... | collective-permute-start | bytes 589832 | tf_op jit(solution)/shard_map/ppermute | solution.py:34
  48.2 8.6 %collective-permute-start.11 = (bf16[768,128]{1,0:T(8,128)(2,1)S(1)}, bf16[768,128]{1,0:T(8,128)(2,1)S(1)}, u32[]{:S(2)}, u32[]{:S(2)}) collective-permute-start(bf16[768,128]{1,0:T(8,128)(2,1)S(1)} %get-tuple-element.37), channel_id=1, source_target_pairs={{0,1},{1,0},{2,3},{3,2},{4,5},{5,4},{6,7},{7,6},{8,9},{9,8},{10,11... | collective-permute-start | bytes 589832 | tf_op jit(solution)/shard_map/ppermute | solution.py:34
  56.9 1.5 %collective-permute-start.12 = (f32[384,128]{1,0:T(8,128)S(1)}, f32[384,128]{1,0:T(8,128)S(1)}, u32[]{:S(2)}, u32[]{:S(2)}) collective-permute-start(f32[384,128]{1,0:T(8,128)S(1)} %get-tuple-element.39), channel_id=1, source_target_pairs={{0,4},{4,0},{8,12},{12,8},{16,20},{20,16},{24,28},{28,24},{1,5},{5... | collective-permute-start | bytes 589832 | tf_op jit(solution)/shard_map/ppermute | solution.py:34
  58.7 5.2 %collective-permute-start.14 = (bf16[128,384]{1,0:T(8,128)(2,1)S(1)}, bf16[128,384]{1,0:T(8,128)(2,1)S(1)}, u32[]{:S(2)}, u32[]{:S(2)}) collective-permute-start(bf16[128,384]{1,0:T(8,128)(2,1)S(1)} %get-tuple-element.46), channel_id=1, source_target_pairs={{0,4},{4,8},{8,12},{12,16},{16,20},{20,24},{24,28},{28,0},{1,5},{5... | collective-permute-start | bytes 294920 | tf_op jit(solution)/shard_map/ppermute | solution.py:226
  59.9 4.0 %collective-permute-start.13 = (bf16[128,256]{1,0:T(8,128)(2,1)S(1)}, bf16[128,256]{1,0:T(8,128)(2,1)S(1)}, u32[]{:S(2)}, u32[]{:S(2)}) collective-permute-start(bf16[128,256]{1,0:T(8,128)(2,1)S(1)} %get-tuple-element.45), channel_id=1, source_target_pairs={{0,28},{4,0},{8,4},{12,8},{16,12},{20,16},{24,20},{28,24},{1,29},{... | collective-permute-start | bytes 196616 | tf_op jit(solution)/shard_map/ppermute | solution.py:226
